TPU v7x, 32 devices: a whole 2x2x4 slice. The times are simulated.
32 devices in a mesh: groups: 2 (over y), ctx: 16 (over z, x, core).
Axes of the slice: x: 2, y: 2, z: 4, core: 2. Of those that a mesh axis runs over, the one named last changes fastest.
Arguments:
- queries: bfloat16 [64, 73728], P(('groups', 'ctx')), parts along dimension 0, may hold values from -10 to 10
- prefix_latents: bfloat16 [8128, 576], P(('groups', 'ctx')), parts along dimension 0, may hold values from -4 to 4
- span_latents: bfloat16 [64, 576], P(('groups', 'ctx')), parts along dimension 0, may hold values from -4 to 4
- value_up: bfloat16 [128, 512, 128], P('ctx'), may hold values from -2.109375 to 2.109375
- prefix_length: int32 [2], P('groups'), parts along dimension 0, may hold values from 2032 to 4064
- span_offset: int32 [2], P('groups'), parts along dimension 0, may hold values from 0 to 16
Outputs:
- attended: bfloat16 [64, 16384], P(('groups', 'ctx')), parts along dimension 0
There are 2 independent parts, one for each index of `groups`. A program takes and returns all parts, laid end to end along the dimension named above; an argument that names none is the same for every part. Nothing has to cross between parts.
Inputs may be any that keep to these rules, and one draw needn't show every extreme that they name: Only the first prefix_length of the 4064 cache slots hold valid latents. Block rows before span_offset belong to an earlier prompt and are no keys.
All inputs are finite; a program needn't handle non-finite values.
Results may differ from a plain program's by a relative error of at most 0.0075.
Values may be sent and summed in bfloat16 or wider, within the bound.
No kernel may reach another device: no remote copies, remote signals or barrier semaphores. Data moves between devices by JAX's collectives and lax.ppermute only.
A program may use at most 128 MiB of HBM per device.

v0:
```python
import jax
import jax.numpy as jnp
from jax import lax
from jax.sharding import PartitionSpec as P

LATENT = 512


score_scale = 192.0 ** (-0.5)
neg_large = -1e30


def attend(query_rows, row_token, prefix_latents, span_latents, prefix_length, span_offset):
    prefix_slots = prefix_latents.shape[0]
    block_slots = span_latents.shape[0]
    shard_rows = prefix_slots + block_slots
    own_latents = jnp.concatenate([prefix_latents, span_latents], axis=0)
    row_count = query_rows.shape[0]
    fragment = lax.all_gather(own_latents, "ctx", axis=0, tiled=True)
    running_max = jnp.full((row_count, 1), neg_large, jnp.float32)
    global_row = jnp.arange(fragment.shape[0], dtype=jnp.int32)
    owner_dev = global_row // shard_rows
    within = global_row % shard_rows
    cache_slot = owner_dev * prefix_slots + within
    span_row = owner_dev * block_slots + within - prefix_slots
    visible = jnp.where(
        (within < prefix_slots)[None, :],
        (cache_slot < prefix_length[0])[None, :],
        (span_row >= span_offset[0])[None, :] & (span_row[None, :] <= row_token[:, None]),
    )
    scores = jnp.dot(query_rows, fragment.T, preferred_element_type=jnp.float32) * score_scale
    masked = jnp.where(visible, scores, neg_large)
    newest_max = jnp.maximum(running_max, jnp.max(masked, axis=1, keepdims=True))
    probs = jnp.where(visible, jnp.exp(masked - newest_max), 0.0)
    running_sum = jnp.sum(probs, axis=1, keepdims=True)
    weighted = jnp.dot(
        probs.astype(jnp.bfloat16), fragment[:, :LATENT], preferred_element_type=jnp.float32
    )
    return (weighted / running_sum).astype(jnp.bfloat16)


def project_back(head_context, value_up, own_tokens, head_count):
    projected = jnp.einsum(
        "thl,hlv->thv", head_context, value_up, preferred_element_type=jnp.float32
    ).astype(jnp.bfloat16)
    returned = lax.all_to_all(projected, "ctx", split_axis=0, concat_axis=1, tiled=True)
    return returned.reshape(own_tokens, head_count * returned.shape[2])


def on_device(queries, prefix_latents, span_latents, value_up, prefix_length, span_offset):
    latent_width = prefix_latents.shape[1]
    own_tokens = queries.shape[0]
    head_count = queries.shape[1] // latent_width
    query_rows = queries.reshape(own_tokens * head_count, latent_width)
    row_token = (
        lax.axis_index("ctx") * own_tokens
        + jnp.arange(own_tokens * head_count, dtype=jnp.int32) // head_count
    )
    context = attend(
        query_rows, row_token, prefix_latents, span_latents, prefix_length, span_offset
    )
    context = context.reshape(own_tokens, head_count, LATENT)
    head_context = lax.all_to_all(context, "ctx", split_axis=1, concat_axis=0, tiled=True)
    return project_back(head_context, value_up, own_tokens, head_count)


def solution(mesh):
    return jax.shard_map(
        on_device,
        mesh=mesh,
        in_specs=(
            P(("groups", "ctx"), None),
            P(("groups", "ctx"), None),
            P(("groups", "ctx"), None),
            P("ctx", None, None),
            P("groups"),
            P("groups"),
        ),
        out_specs=P(("groups", "ctx"), None),
        check_vma=False,
    )
```

profile of v0, /device:TPU:0, one launch (start us, length us, event | category | flops | bytes accessed | tf_op | source)
XLA Modules:
  0.0 114.6 jit_solution(11372452811848152964)
XLA Ops:
  6.5 0.0 copy-start
  6.5 0.0 all-gather.2.cloned.1.call-start
  6.5 0.9 copy.13
  7.5 1.8 %pad_maximum_fusion = bf16[256,576]{0,1:T(8,128)(2,1)} fusion(bf16[2,576]{0,1:T(8,128)(2,1)S(1)} %copy.13, bf16[254,576]{0,1:T(8,128)(2,1)} %param.7), kind=kLoop, calls=%fused_computation.20 | loop fusion | flops 589824 | bytes 589824 | tf_op jit(solution)/shard_map/concatenate | solution.py:17
  9.3 0.0 all-gather.2.cloned.1.call-update
  10.6 1.3 %reshape.66 = bf16[256,576]{1,0:T(8,128)(2,1)S(1)} reshape(bf16[2,73728]{1,0:T(2,128)(2,1)} %param.6) | data formatting | bytes 589824 | tf_op jit(solution)/shard_map/reshape | solution.py:54
  12.0 56.2 %all-gather.2.cloned.1.call-done = bf16[4096,576]{0,1:T(8,128)(2,1)} async-done(((bf16[256,576]{0,1:T(8,128)(2,1)}), bf16[4096,576]{0,1:T(8,128)(2,1)}) %all-gather.2.cloned.1.call-update) | async-done | bytes 4718608 | tf_op jit(solution)/shard_map/all_gather | solution.py:19
  68.2 0.0 slice-start
  68.2 0.0 slice-start.1
  68.3 7.8 %fusion.39 = (f32[256]{0:T(256)S(1)}, f32[256,4096]{0,1:T(8,128)S(1)}) fusion(bf16[4096,576]{0,1:T(8,128)(2,1)} %all-gather.2.cloned.1.call-done, bf16[256,576]{1,0:T(8,128)(2,1)S(1)} %reshape.66, s32[256]{0:T(256)S(1)} %fusion.37, s32[4096]{0:T(1024)S(1)} %fusion.31, pred[4096]{0:T(1024)(128)(4,1)S(1)} %broadcast_compare_fusion, ...), kind=kOutput, calls=%fused_computation.49 | convolution fusion | flops 1214250752 | bytes 9238528 | tf_op jit(solution)/shard_map/dot_general | solution.py:31
  76.1 3.6 %fusion.4 = f32[256]{0:T(256)S(1)} fusion(f32[256,4096]{0,1:T(8,128)S(1)} %get-tuple-element.6, f32[256]{0:T(256)S(1)} %broadcast_maximum_fusion, s32[256]{0:T(256)S(1)} %fusion.37, s32[4096]{0:T(1024)S(1)} %fusion.31, pred[4096]{0:T(1024)(128)(4,1)S(1)} %broadcast_compare_fusion, pred[4096]{0:T(1024)(128)(4,1)S(1)} %get-tuple-element.7, ...), kind=kLoop, calls=%fused_computation.7 | loop fusion | flops 6291200 | bytes 4226048 | tf_op jit(solution)/shard_map/reduce_sum | solution.py:35
  79.7 0.0 slice-done
  79.7 0.0 slice-done.1
  79.7 3.9 %fusion.20 = bf16[256,512]{1,0:T(8,128)(2,1)S(1)} fusion(bf16[4096,576]{0,1:T(8,128)(2,1)S(1)} %bitcast.37, f32[256,4096]{0,1:T(8,128)S(1)} %get-tuple-element.6, f32[256]{0:T(256)S(1)} %broadcast_maximum_fusion, s32[256]{0:T(256)S(1)} %fusion.37, s32[4096]{0:T(1024)S(1)} %fusion.31, pred[4096]{0:T(1024)(128)(4,1)S(1)} %broadcast_compare_fusion, ...), kind=kOutput, calls=%fused_computation.19 | convolution fusion | flops 1080295424 | bytes 8682496 | tf_op jit(solution)/shard_map/dot_general | solution.py:36
  83.6 0.3 copy.14
  83.9 12.8 %all_to_all.33 = bf16[2,128,512]{2,0,1:T(2,128)(2,1)S(1)} all-to-all(bf16[2,128,512]{2,0,1:T(2,128)(2,1)S(1)} %copy.14), channel_id=1, replica_groups=mesh['groups'=2,'ctx'=16] {'ctx'}, dimensions={1} | all-to-all | bytes 524288 | tf_op jit(solution)/shard_map/all_to_all | solution.py:63
  96.7 0.2 copy.22
  96.9 0.1 all_to_all.27
  97.0 0.0 copy-done
  97.0 0.3 fusion.14
  97.4 9.7 %all_to_all.34 = bf16[32,8,128]{2,1,0:T(8,128)(2,1)S(1)} all-to-all(bf16[32,8,128]{2,1,0:T(8,128)(2,1)S(1)} %copy.16), channel_id=1, replica_groups=mesh['groups'=2,'ctx'=16] {'ctx'}, dimensions={0} | all-to-all | bytes 131072 | tf_op jit(solution)/shard_map/all_to_all | solution.py:46
  107.0 0.7 copy.23
  (8 shorter events, 0.1 us)
Async XLA Ops:
  6.5 90.5 %copy-start = (bf16[8,512,128]{2,1,0:T(8,128)(2,1)S(1)}, bf16[8,512,128]{2,1,0:T(8,128)(2,1)}, u32[]{:S(2)}) copy-start(bf16[8,512,128]{2,1,0:T(8,128)(2,1)} %param.9) | copy-start | bytes 3145732
  6.5 61.7 %all-gather.2.cloned.1.call-start = ((), (), s32[]{:S(2)}) async-start(), calls=%async_computation.2 | async-start | bytes 5013504 | tf_op jit(solution)/shard_map/all_gather | solution.py:19
  68.2 11.5 %slice-start = ((s8[4718592]{0:T(1024)(128)(4,1)}), s8[4194304]{0:T(1024)(128)(4,1)S(1)}, s32[]{:S(2)}) async-start(s8[4718592]{0:T(1024)(128)(4,1)} %bitcast.36), calls=%async_computation.3 | async-start | bytes 8388608
  68.2 11.5 %slice-start.1 = ((s8[4718592]{0:T(1024)(128)(4,1)}), s8[524288]{0:T(1024)(128)(4,1)S(1)}, s32[]{:S(2)}) async-start(s8[4718592]{0:T(1024)(128)(4,1)} %bitcast.36), calls=%async_computation.4 | async-start | bytes 1048576
Sparse Core Ops, SparseCore 0:
  9.5 58.6 all-gather.1
where the time goes:
time: 115 us
  waiting for transfers between devices  56.3 us (49%)
  blocking collectives  22.5 us (20%)
  between operations  14.8 us (13%)
  matrix products  12 us (10%)
  other arithmetic  5.49 us (5%)
  local copies, waits for them, and re-layouts  3.54 us (3%)
    all_gather x1, waiting for transfers between devices, attend(): fragment = lax.all_gather(own_latents, 'ctx', axis=0, tiled=True)  56.2 us
    all_to_all x1, blocking collectives, on_device(): lax.all_to_all(context, 'ctx', split_axis=1, concat_axis=0, tiled=True)  12.8 us
    all_to_all x1, blocking collectives, project_back(): lax.all_to_all(projected, 'ctx', split_axis=0, concat_axis=1, tiled=True)  9.67 us
    dot_general x1, matrix products, attend(): jnp.dot(query_rows, fragment.T, preferred_element_type=jnp.float32)  7.82 us
    dot_general x1, matrix products, attend(): jnp.dot(probs.astype(jnp.bfloat16), fragment[:, :LATENT], preferred_eleme...  3.88 us
    reduce_sum x1, other arithmetic, attend(): running_sum = jnp.sum(probs, axis=1, keepdims=True)  3.62 us
  transfers between devices with their start and end apart: 1, of which 1 were waited for; matrix products, arithmetic and copies ran while one was open for 1% of the time, Pallas kernels for 0%

commit v1 on v0

v1 whole, which is shorter than its diff:
```python
import functools
import math

import jax
import jax.numpy as jnp
import numpy as np
from jax import lax
from jax.experimental import pallas as pl
from jax.experimental.pallas import tpu as pltpu
from jax.sharding import PartitionSpec as P

LATENT = 512
V_HEAD = 128
CORES = 2
LANES = 128

score_scale = 192.0 ** (-0.5) * math.log2(math.e)
neg_large = -1e30
f32 = jnp.float32
bf16 = jnp.bfloat16


def chip_cycle(chips):
    wide = max(1, int(round(chips ** (1 / 3))))
    tall = chips // wide
    if wide * tall != chips or wide < 2 or tall < 2:
        return list(range(chips))
    walk = []
    for z in range(tall):
        across = range(1, wide) if z % 2 == 0 else range(wide - 1, 0, -1)
        walk += [z * wide + x for x in across]
    return walk + [z * wide for z in reversed(range(tall))]


def fold_shard(q_ref, key_ref, base, length, m_ref, l_ref, acc_ref):
    rows = q_ref.shape[0]
    block = min(256, rows)
    slots = key_ref.shape[1]
    shown = base + lax.broadcasted_iota(jnp.int32, (1, slots), 1) < length
    for start in range(0, rows, block):
        part = pl.ds(start, block)
        s = jnp.dot(q_ref[part, :], key_ref[...], preferred_element_type=f32) * score_scale
        s = jnp.where(shown, s, neg_large)
        m_old = m_ref[part, :][:, :1]
        m_new = jnp.maximum(m_old, jnp.max(s, axis=1, keepdims=True))
        probs = jnp.where(shown, jnp.exp2(s - m_new), 0.0)
        shrink = jnp.exp2(m_old - m_new)
        l_new = l_ref[part, :][:, :1] * shrink + jnp.sum(probs, axis=1, keepdims=True)
        summed = lax.dot_general(
            probs.astype(bf16), key_ref[:LATENT, :], (((1,), (1,)), ((), ())),
            preferred_element_type=f32,
        )
        acc_ref[part, :] = acc_ref[part, :] * shrink + summed
        m_ref[part, :] = jnp.broadcast_to(m_new, (block, LANES))
        l_ref[part, :] = jnp.broadcast_to(l_new, (block, LANES))


def first_kernel(tokens, heads, scal_ref, here_ref, there_ref, row_token_ref, key_token_ref,
                 key_ref, q_ref, m_ref, l_ref, acc_ref, span_ref):
    chips = here_ref.shape[0]
    rows = tokens * heads
    for core, piece_ref in enumerate((here_ref, there_ref)):
        for o in range(chips):
            at = core * chips + o
            q_ref[at * rows:(at + 1) * rows, :] = piece_ref[o, :rows, :]
            if core == 0:
                span_ref[o * tokens:(o + 1) * tokens, :] = (
                    piece_ref[o, rows:rows + tokens, :].astype(f32)
                )
    span = span_ref[...].astype(bf16)
    total = q_ref.shape[0]
    block = min(256, total)
    key_token = key_token_ref[...]
    for start in range(0, total, block):
        part = pl.ds(start, block)
        s = lax.dot_general(
            q_ref[part, :], span, (((1,), (1,)), ((), ())), preferred_element_type=f32
        ) * score_scale
        shown = (key_token >= scal_ref[1]) & (key_token <= row_token_ref[part, :])
        s = jnp.where(shown, s, neg_large)
        m_new = jnp.max(s, axis=1, keepdims=True)
        probs = jnp.where(shown, jnp.exp2(s - m_new), 0.0)
        l_new = jnp.sum(probs, axis=1, keepdims=True)
        acc_ref[part, :] = jnp.dot(
            probs.astype(bf16), span[:, :LATENT], preferred_element_type=f32
        )
        m_ref[part, :] = jnp.broadcast_to(m_new, (block, LANES))
        l_ref[part, :] = jnp.broadcast_to(l_new, (block, LANES))
    fold_shard(q_ref, key_ref, scal_ref[3], scal_ref[0], m_ref, l_ref, acc_ref)


def middle_kernel(at, count, scal_ref, q_ref, m_in, l_in, acc_in, *rest):
    keys, (m_ref, l_ref, acc_ref) = rest[:count], rest[count:]
    m_ref[...] = m_in[...]
    l_ref[...] = l_in[...]
    acc_ref[...] = acc_in[...]
    for j, key_ref in enumerate(keys):
        base = scal_ref[3 + at + j]

        @pl.when(base < scal_ref[0])
        def _():
            fold_shard(q_ref, key_ref, base, scal_ref[0], m_ref, l_ref, acc_ref)


def last_kernel(at, count, tokens, heads, scal_ref, place_ref, q_ref, m_in, l_in, acc_in, *rest):
    keys = rest[:count]
    own_up, far_up, out_ref, m_ref, l_ref, acc_ref, context_ref, flat_ref = rest[count:]
    middle_kernel(at, count, scal_ref, q_ref, m_in, l_in, acc_in, *keys, m_ref, l_ref, acc_ref)
    for k in range(LATENT // LANES):
        lanes = slice(k * LANES, (k + 1) * LANES)
        context_ref[k] = acc_ref[:, lanes] / l_ref[...]
    m_ref[...] = m_ref[...] + jnp.log2(l_ref[...])
    everyone = flat_ref.shape[0]
    core = scal_ref[2]
    per_core = heads // CORES
    tail = jnp.zeros((everyone, LANES), f32)
    lane = lax.broadcasted_iota(jnp.int32, (everyone, LANES), 1)
    for side, up_ref in enumerate((own_up, far_up)):
        for j in range(per_core):
            head = (core ^ side) * per_core + j
            rows = pl.ds(head, everyone, stride=heads)
            context = jnp.concatenate(
                [context_ref[k, rows, :] for k in range(LATENT // LANES)], axis=1
            ).astype(bf16)
            lifted = jnp.dot(context, up_ref[j], preferred_element_type=f32)
            flat_ref[:, pl.ds(pl.multiple_of(head * V_HEAD, V_HEAD), V_HEAD)] = lifted
            weight = m_ref[rows, :]
            high = weight.astype(bf16).astype(f32)
            mid = (weight - high).astype(bf16).astype(f32)
            low = weight - high - mid
            tail = jnp.where(lane == head, high, tail)
            tail = jnp.where(lane == head + heads, mid, tail)
            tail = jnp.where(lane == head + 2 * heads, low, tail)
    flat_ref[:, heads * V_HEAD:] = tail
    for i in range(everyone // tokens):
        out_ref[place_ref[i]] = flat_ref[i * tokens:(i + 1) * tokens, :].astype(bf16)


def merge_kernel(heads, parts_ref, out_ref):
    width = heads * V_HEAD
    for chip in range(parts_ref.shape[0] // CORES):
        one = parts_ref[2 * chip].astype(f32)
        two = parts_ref[2 * chip + 1].astype(f32)
        gap = one[:, width:] - two[:, width:]
        delta = gap[:, :heads] + (gap[:, heads:2 * heads] + gap[:, 2 * heads:3 * heads])
        share = 1.0 / (1.0 + jnp.exp2(-delta))
        rest = 1.0 / (1.0 + jnp.exp2(delta))
        for j in range(heads):
            lanes = slice(j * V_HEAD, (j + 1) * V_HEAD)
            mixed = one[:, lanes] * share[:, j:j + 1] + two[:, lanes] * rest[:, j:j + 1]
            out_ref[:, chip * width + j * V_HEAD:chip * width + (j + 1) * V_HEAD] = (
                mixed.astype(bf16)
            )


VMEM = pl.BlockSpec(memory_space=pltpu.VMEM)
SMEM = pl.BlockSpec(memory_space=pltpu.SMEM)
PARAMS = pltpu.CompilerParams(vmem_limit_bytes=32 * 1024 * 1024)


def shape(*dims, dtype=f32):
    return jax.ShapeDtypeStruct(dims, dtype)


def on_device(ctx, queries, prefix_latents, span_latents, value_up, prefix_length, span_offset):
    slots, width = prefix_latents.shape
    tokens = queries.shape[0]
    all_heads = queries.shape[1] // width
    chips = ctx // CORES
    heads = all_heads // chips
    rows = tokens * heads
    total = rows * ctx
    everyone = tokens * ctx
    walk = chip_cycle(chips)
    spot = np.argsort(np.array(walk))
    onward = (chips - 1 + 1) // 2
    backward = chips - 1 - onward

    me = lax.axis_index("ctx")
    chip, core = me // CORES, me % CORES

    def across(step):
        return [
            (walk[r] * CORES + c, walk[(r + step) % chips] * CORES + c)
            for r in range(chips) for c in range(CORES)
        ]

    other_core = [(d, d ^ 1) for d in range(ctx)]

    own = prefix_latents.T
    right, left = [own], [own]
    for _ in range(onward):
        right.append(lax.ppermute(right[-1], "ctx", across(1)))
    for _ in range(backward):
        left.append(lax.ppermute(left[-1], "ctx", across(-1)))

    grouped = queries.reshape(tokens, all_heads, width)
    pad = -(rows + tokens) % 8
    span_rows = jnp.concatenate([span_latents, jnp.zeros((pad, width), bf16)], axis=0)
    pieces = []
    for o in range(chips):
        piece = lax.dynamic_slice(grouped, (0, (chip ^ o) * heads, 0), (tokens, heads, width))
        piece = jnp.concatenate([piece.reshape(rows, width), span_rows], axis=0)
        if o:
            swap = [(d, d ^ (o * CORES)) for d in range(ctx)]
            piece = lax.ppermute(piece, "ctx", swap)
        pieces.append(piece)
    here = jnp.stack(pieces)
    there = lax.ppermute(here, "ctx", other_core)
    far_up = lax.ppermute(value_up, "ctx", other_core)

    turns = [0]
    for s in range(1, onward + 1):
        turns.append(-s)
        if s <= backward:
            turns.append(s)
    owner_table = np.array(
        [[walk[(spot[p] + t) % chips] for t in turns] for p in range(chips)], np.int32
    )
    owners = lax.dynamic_index_in_dim(jnp.asarray(owner_table), chip, 0, keepdims=False)
    bases = (owners * CORES + core) * slots
    scal = jnp.concatenate([prefix_length, span_offset, core[None], bases]).astype(jnp.int32)
    index = jnp.arange(ctx, dtype=jnp.int32)
    place = ((chip ^ (index % chips)) * CORES + (core ^ (index // chips))).astype(jnp.int32)
    key_token = (place[:, None] * tokens + jnp.arange(tokens, dtype=jnp.int32)[None, :]).reshape(-1)
    row_token = jnp.repeat(key_token, heads, total_repeat_length=total)[:, None]

    state_shapes = [shape(total, LANES), shape(total, LANES), shape(total, LATENT)]
    q, *state = pl.pallas_call(
        functools.partial(first_kernel, tokens, heads),
        out_shape=[shape(total, width, dtype=bf16)] + state_shapes,
        in_specs=[SMEM] + [VMEM] * 5,
        out_specs=[VMEM] * 4,
        scratch_shapes=[pltpu.VMEM((everyone // CORES, width), f32)],
        compiler_params=PARAMS,
        name="first",
    )(scal, here, there, row_token, key_token[None, :everyone // CORES], own)

    at = 1
    for s in range(1, onward):
        keys = [right[s]] + ([left[s]] if s <= backward else [])
        state = pl.pallas_call(
            functools.partial(middle_kernel, at, len(keys)),
            out_shape=state_shapes,
            in_specs=[SMEM] + [VMEM] * (4 + len(keys)),
            out_specs=[VMEM] * 3,
            compiler_params=PARAMS,
            name="middle",
        )(scal, q, *state, *keys)
        at += len(keys)
    keys = [right[onward]] + ([left[onward]] if onward <= backward else [])
    flat = heads * V_HEAD + LANES
    parts = pl.pallas_call(
        functools.partial(last_kernel, at, len(keys), tokens, heads),
        out_shape=shape(ctx, tokens, flat, dtype=bf16),
        in_specs=[SMEM, SMEM] + [VMEM] * (6 + len(keys)),
        out_specs=VMEM,
        scratch_shapes=[
            pltpu.VMEM((total, LANES), f32),
            pltpu.VMEM((total, LANES), f32),
            pltpu.VMEM((total, LATENT), f32),
            pltpu.VMEM((LATENT // LANES, total, LANES), f32),
            pltpu.VMEM((everyone, flat), f32),
        ],
        compiler_params=PARAMS,
        name="last",
    )(scal, place, q, *state, *keys, value_up, far_up)
    returned = lax.all_to_all(parts, "ctx", split_axis=0, concat_axis=0, tiled=True)
    return pl.pallas_call(
        functools.partial(merge_kernel, heads),
        out_shape=shape(tokens, all_heads * V_HEAD, dtype=bf16),
        in_specs=[VMEM],
        out_specs=VMEM,
        compiler_params=PARAMS,
        name="merge",
    )(returned)


def solution(mesh):
    return jax.shard_map(
        functools.partial(on_device, mesh.shape["ctx"]),
        mesh=mesh,
        in_specs=(
            P(("groups", "ctx"), None),
            P(("groups", "ctx"), None),
            P(("groups", "ctx"), None),
            P("ctx", None, None),
            P("groups"),
            P("groups"),
        ),
        out_specs=P(("groups", "ctx"), None),
        check_vma=False,
    )
```

time: 115 us -> 99.4 us (0.86)
  waiting for transfers between devices: 56.3 us -> 11.1 us
  starting transfers between devices: 0.01 us -> 24.1 us
  Pallas kernels: 0 us -> 19.3 us
  other arithmetic: 5.49 us -> 24.3 us
  between operations: 14.8 us -> 1.6 us
  matrix products: 12 us -> 0 us
  blocking collectives: 22.5 us -> 11.4 us
  local copies, waits for them, and re-layouts: 3.54 us -> 6.93 us
    all_gather x1 -> x0, waiting for transfers between devices: 56.2 us -> none  [attend(): fragment = lax.all_gather(own_latents, 'ctx', axis=0, tiled=True)]
    ppermute x0 -> x16, starting transfers between devices: none -> 24.1 us  [the longest x7 16.4 us: on_device(): piece = lax.ppermute(piece, 'ctx', swap)]
    gather x0 -> x3, other arithmetic: none -> 22.1 us  [on_device(): row_token = jnp.repeat(key_token, heads, total_repeat_length=total)[:, None]]
    pallas_call x0 -> x6, Pallas kernels: none -> 19.3 us  [the longest x3 11.4 us: on_device(): pl.pallas_call(functools.partial(middle_kernel, at, len(keys)), out_shape...]
    dot_general x3 -> x0, matrix products: 12 us -> none  [the longest x1 7.82 us: attend(): jnp.dot(query_rows, fragment.T, preferred_element_type=jnp.float32)]
    ppermute x0 -> x16, waiting for transfers between devices: none -> 11.1 us  [the longest x4 11.1 us: on_device(): right.append(lax.ppermute(right[-1], 'ctx', across(1)))]
    all_to_all x2 -> x1, blocking collectives: 22.5 us -> 11.4 us  [on_device(): lax.all_to_all(parts, 'ctx', split_axis=0, concat_axis=0, tiled=True)]
    reduce_sum x1 -> x0, other arithmetic: 3.62 us -> none  [attend(): running_sum = jnp.sum(probs, axis=1, keepdims=True)]
  transfers between devices with their start and end apart: 1 -> 16, of which waited for: 1 -> 2; matrix products, arithmetic and copies ran while one was open for 1% -> 29% of each run, Pallas kernels for 0% -> 14%
where the time goes in v1:
time: 99.4 us; the launch traced here: 98.8 us
  other arithmetic  24.3 us (24%)
  starting transfers between devices  24.1 us (24%)
  Pallas kernels  19.3 us (19%)
  blocking collectives  11.4 us (11%)
  waiting for transfers between devices  11.1 us (11%)
  local copies, waits for them, and re-layouts  6.93 us (7%)
  between operations  1.6 us (2%)
    gather x3, other arithmetic, on_device(): row_token = jnp.repeat(key_token, heads, total_repeat_length=total)[:, None]  22.1 us
    ppermute x7, starting transfers between devices, on_device(): piece = lax.ppermute(piece, 'ctx', swap)  16.4 us
    pallas_call x3, Pallas kernels, on_device(): pl.pallas_call(functools.partial(middle_kernel, at, len(keys)), out_shape...  11.4 us
    all_to_all x1, blocking collectives, on_device(): lax.all_to_all(parts, 'ctx', split_axis=0, concat_axis=0, tiled=True)  11.4 us
    ppermute x4, waiting for transfers between devices, on_device(): right.append(lax.ppermute(right[-1], 'ctx', across(1)))  11.1 us
    ppermute x3, starting transfers between devices, on_device(): left.append(lax.ppermute(left[-1], 'ctx', across(-1)))  3.93 us
    ppermute x4, starting transfers between devices, on_device(): right.append(lax.ppermute(right[-1], 'ctx', across(1)))  3.69 us
    pallas_call x1, Pallas kernels, on_device(): pl.pallas_call(functools.partial(last_kernel, at, len(keys), tokens, head...  3.31 us
  transfers between devices with their start and end apart: 16, of which 2 were waited for; matrix products, arithmetic and copies ran while one was open for 29% of the time, Pallas kernels for 14%

profile of v1, /device:TPU:0, one launch (start us, length us, event | category | flops | bytes accessed | tf_op | source)
XLA Modules:
  0.0 98.8 jit_solution(9099436179123820098)
XLA Ops:
  0.0 2.9 %collective-permute-start.8 = (bf16[576,254]{1,0:T(8,128)(2,1)}, bf16[576,254]{1,0:T(8,128)(2,1)S(1)}, u32[]{:S(2)}, u32[]{:S(2)}) collective-permute-start(bf16[576,254]{1,0:T(8,128)(2,1)} %bitcast.65), channel_id=1, source_target_pairs={{2,6},{3,7},{6,10},{7,11},{10,14},{11,15},{14,12},{15,13},{12,8},{... | collective-permute-start | bytes 877832 | tf_op jit(solution)/shard_map/ppermute | solution.py:193
  2.9 0.1 collective-permute-start.9
  3.0 1.3 %reshape.160 = bf16[2,128,576]{2,1,0:T(8,128)(2,1)S(1)} reshape(bf16[2,73728]{1,0:T(2,128)(2,1)} %param.9) | data formatting | bytes 589824 | tf_op jit(solution)/shard_map/reshape | solution.py:197
  4.4 0.1 pad.26.clone
  4.5 0.0 copy-start.6
  4.5 0.7 copy-done.6
  5.2 0.1 fusion.9
  5.3 2.0 %collective-permute-start = (bf16[40,576]{1,0:T(8,128)(2,1)S(1)}, bf16[40,576]{1,0:T(8,128)(2,1)S(1)}, u32[]{:S(2)}, u32[]{:S(2)}) collective-permute-start(bf16[40,576]{1,0:T(8,128)(2,1)S(1)} %get-tuple-element.81), channel_id=1, source_target_pairs={{0,2},{1,3},{2,0},{3,1},{4,6},{5,7},{6,4},{7,5},{8,10},{9,11},{10,... | collective-permute-start | bytes 138248 | tf_op jit(solution)/shard_map/ppermute | solution.py:206
  7.3 1.6 %collective-permute-start.1 = (bf16[40,576]{1,0:T(8,128)(2,1)S(1)}, bf16[40,576]{1,0:T(8,128)(2,1)S(1)}, u32[]{:S(2)}, u32[]{:S(2)}) collective-permute-start(bf16[40,576]{1,0:T(8,128)(2,1)S(1)} %get-tuple-element.82), channel_id=1, source_target_pairs={{0,4},{1,5},{2,6},{3,7},{4,0},{5,1},{6,2},{7,3},{8,12},{9,13},{10,... | collective-permute-start | bytes 138248 | tf_op jit(solution)/shard_map/ppermute | solution.py:206
  8.9 0.0 collective-permute-start.2
  8.9 0.1 iota_add_fusion
  9.0 0.1 add.150
  9.1 0.7 fusion.20
  9.8 0.7 fusion.19
  10.5 0.1 fusion.2
  10.6 0.6 copy-done.7
  11.2 0.1 add_add_fusion.1
  11.3 0.1 copy.9
  11.4 0.1 copy.8
  11.6 4.7 %select_reduce_fusion = (s32[512]{0:T(512)S(1)}, s32[512,1]{1,0:T(8,128)S(1)}) fusion(s32[]{:T(128)} %bitcast.45, s32[]{:T(128)} %bitcast.46, s32[]{:T(128)} %bitcast.47, s32[]{:T(128)} %bitcast.48, s32[]{:T(128)} %bitcast.49, s32[]{:T(128)} %bitcast.51, s32[]{:T(128)} %bitcast.50, s32[512,1]{1,0:T(8,128)S(1)} %copy.9, s32[512,1]{1,0:T(8,128)S(1)} %copy.8), kind=kLoop, calls=%fused_computation.1 | loop fusion | flops 7168 | bytes 8220 | tf_op jit(solution)/shard_map/jit(_take)/gather | solution.py:226
  16.3 0.7 copy-done.4
  17.0 1.8 %compare_reduce_fusion.24 = (pred[512]{0:T(512)(128)(4,1)S(1)}, pred[512]{0:T(512)(128)(4,1)S(1)}, pred[512]{0:T(512)(128)(4,1)S(1)}, pred[512]{0:T(512)(128)(4,...) fusion(s32[512,1]{1,0:T(8,128)S(1)} %get-tuple-element.69), kind=kLoop, calls=%fused_computation.26 | loop fusion | flops 12800 | bytes 14848 | tf_op jit(solution)/shard_map/jit(_take)/gather | solution.py:226
  18.8 15.6 %select_select_fusion = s32[512]{0:T(512)S(1)} fusion(pred[512]{0:T(512)(128)(4,1)S(1)} %get-tuple-element.66, pred[512]{0:T(512)(128)(4,1)S(1)} %get-tuple-element.65, pred[512]{0:T(512)(128)(4,1)S(1)} %get-tuple-element.60, pred[512]{0:T(512)(128)(4,1)S(1)} %get-tuple-element.61, pred[512]{0:T(512)(128)(4,1)S(1)} %get-tuple-element.62, ...), kind=kLoop, calls=%fused_computation.65 | loop fusion | flops 12800 | bytes 16996 | tf_op jit(solution)/shard_map/jit(_take)/gather | solution.py:226
  34.3 0.0 collective-permute-done
  34.3 3.1 %collective-permute-start.3 = (bf16[40,576]{1,0:T(8,128)(2,1)S(1)}, bf16[40,576]{1,0:T(8,128)(2,1)S(1)}, u32[]{:S(2)}, u32[]{:S(2)}) collective-permute-start(bf16[40,576]{1,0:T(8,128)(2,1)S(1)} %get-tuple-element.84), channel_id=1, source_target_pairs={{0,8},{1,9},{2,10},{3,11},{4,12},{5,13},{6,14},{7,15},{8,0},{9,1},... | collective-permute-start | bytes 138248 | tf_op jit(solution)/shard_map/ppermute | solution.py:206
  37.4 0.0 collective-permute-done.1
  37.4 1.3 %collective-permute-start.4 = (bf16[40,576]{1,0:T(8,128)(2,1)S(1)}, bf16[40,576]{1,0:T(8,128)(2,1)S(1)}, u32[]{:S(2)}, u32[]{:S(2)}) collective-permute-start(bf16[40,576]{1,0:T(8,128)(2,1)S(1)} %get-tuple-element.85), channel_id=1, source_target_pairs={{0,10},{1,11},{2,8},{3,9},{4,14},{5,15},{6,12},{7,13},{8,2},{9,3},... | collective-permute-start | bytes 138248 | tf_op jit(solution)/shard_map/ppermute | solution.py:206
  38.8 0.0 collective-permute-done.2
  38.8 3.7 %collective-permute-start.5 = (bf16[40,576]{1,0:T(8,128)(2,1)S(1)}, bf16[40,576]{1,0:T(8,128)(2,1)S(1)}, u32[]{:S(2)}, u32[]{:S(2)}) collective-permute-start(bf16[40,576]{1,0:T(8,128)(2,1)S(1)} %get-tuple-element.86), channel_id=1, source_target_pairs={{0,12},{1,13},{2,14},{3,15},{4,8},{5,9},{6,10},{7,11},{8,4},{9,5},... | collective-permute-start | bytes 138248 | tf_op jit(solution)/shard_map/ppermute | solution.py:206
  42.5 0.0 collective-permute-done.3
  42.5 4.7 %collective-permute-start.6 = (bf16[40,576]{1,0:T(8,128)(2,1)S(1)}, bf16[40,576]{1,0:T(8,128)(2,1)S(1)}, u32[]{:S(2)}, u32[]{:S(2)}) collective-permute-start(bf16[40,576]{1,0:T(8,128)(2,1)S(1)} %get-tuple-element.80), channel_id=1, source_target_pairs={{0,14},{1,15},{2,12},{3,13},{4,10},{5,11},{6,8},{7,9},{8,6},{9,7},... | collective-permute-start | bytes 138248 | tf_op jit(solution)/shard_map/ppermute | solution.py:206
  47.2 0.0 collective-permute-done.4
  47.2 0.1 collective-permute-start.15
  47.3 0.0 collective-permute-done.8.rest_0_
  47.3 0.1 collective-permute-start.10
  47.4 0.0 collective-permute-done.5
  47.4 0.0 collective-permute-done.9.rest_1_
  47.4 2.1 %collective-permute-start.11 = (bf16[576,254]{1,0:T(8,128)(2,1)S(1)}, bf16[576,254]{1,0:T(8,128)(2,1)}, u32[]{:S(2)}, u32[]{:S(2)}) collective-permute-start(bf16[576,254]{1,0:T(8,128)(2,1)S(1)} %collective-permute-done.9.rest_1_), channel_id=1, source_target_pairs={{2,0},{3,1},{6,2},{7,3},{10,6},{11,7},{14,10},{15,11},{12,14},{13,... | collective-permute-start | bytes 877832 | tf_op jit(solution)/shard_map/ppermute | solution.py:195
  49.5 7.2 %collective-permute-done.10.rest_0_ = bf16[576,254]{1,0:T(8,128)(2,1)S(1)} collective-permute-done((bf16[576,254]{1,0:T(8,128)(2,1)S(1)}, bf16[576,254]{1,0:T(8,128)(2,1)S(1)}, u32[]{:S(2)}, u32[]{:S(2)}) %collective-permute-start.10) | collective-permute-done | bytes 292640 | tf_op jit(solution)/shard_map/ppermute | solution.py:193
  56.7 0.3 collective-permute-start.12
  57.0 0.7 copy-done.1
  57.7 0.0 collective-permute-done.6
  57.7 0.1 collective-permute-start.7
  57.8 0.7 fusion.17
  59.8 0.0 collective-permute-done.11.rest_1_
  59.8 1.8 %collective-permute-start.13 = (bf16[576,254]{1,0:T(8,128)(2,1)}, bf16[576,254]{1,0:T(8,128)(2,1)}, u32[]{:S(2)}, u32[]{:S(2)}) collective-permute-start(bf16[576,254]{1,0:T(8,128)(2,1)} %collective-permute-done.11.rest_1_), channel_id=1, source_target_pairs={{2,0},{3,1},{6,2},{7,3},{10,6},{11,7},{14,10},{15,11},{12,14},{13,... | collective-permute-start | bytes 877832 | tf_op jit(solution)/shard_map/ppermute | solution.py:195
  61.6 3.9 %collective-permute-done.12.rest_0_ = bf16[576,254]{1,0:T(8,128)(2,1)} collective-permute-done((bf16[576,254]{1,0:T(8,128)(2,1)S(1)}, bf16[576,254]{1,0:T(8,128)(2,1)}, u32[]{:S(2)}, u32[]{:S(2)}) %collective-permute-start.12) | collective-permute-done | bytes 292640 | tf_op jit(solution)/shard_map/ppermute | solution.py:193
  65.5 0.4 collective-permute-start.14
  65.9 0.1 pad_add_fusion.scal_ref
  65.9 0.0 copy-done.5
  65.9 0.9 copy.11
  66.8 0.1 broadcast_in_dim.28.key_token_ref
  66.9 1.1 %and_select_fusion.row_token_ref = s32[512,1]{1,0:T(8,128)S(1)} fusion(s32[512,1]{1,0:T(8,128)} %copy.11, s32[512,1]{1,0:T(8,128)} %copy-done.4), kind=kLoop, calls=%fused_computation.27 | loop fusion | flops 2048 | bytes 6144 | tf_op jit(solution)/shard_map/jit(_take)/select_n | solution.py:226
  68.0 0.0 collective-permute-done.7.there_ref
  68.0 2.7 %first.1 = (bf16[512,576]{1,0:T(8,128)(2,1)S(1)}, f32[512,128]{1,0:T(8,128)S(1)}, f32[512,128]{1,0:T(8,128)S(1)}, f32[512,512]{1,0:T(8,128)S(1)}) custom-call(s32[11]{0:T(128)S(1)} %pad_add_fusion.scal_ref, bf16[8,40,576]{2,1,0:T(8,128)(2,1)S(1)} %bitcast_dynamic-update-slice_fusion.here_ref, bf16[8,40,576]{2,1,0:T(8,128)(2,1)S(1)} %collective-permute-done.7.there_ref, ...), custom_call_target="tpu_custom_call" | custom-call | tf_op jit(solution)/shard_map/first/pallas_call | solution.py:229
  70.7 3.4 %middle.3 = (f32[512,128]{1,0:T(8,128)S(1)}, f32[512,128]{1,0:T(8,128)S(1)}, f32[512,512]{1,0:T(8,128)S(1)}) custom-call(s32[11]{0:T(128)S(1)} %pad_add_fusion.scal_ref, bf16[512,576]{1,0:T(8,128)(2,1)S(1)} %get-tuple-element.30.q_ref, f32[512,128]{1,0:T(8,128)S(1)} %get-tuple-element.31.m_in, f32[512,128]{1,0:T(8,128)S(1)} %get-tuple-element.32.l_in, ...), custom_call_target="tpu_custom_call" | custom-call | tf_op jit(solution)/shard_map/middle/pallas_call | solution.py:242
  74.2 3.9 %middle.4 = (f32[512,128]{1,0:T(8,128)S(1)}, f32[512,128]{1,0:T(8,128)S(1)}, f32[512,512]{1,0:T(8,128)S(1)}) custom-call(s32[11]{0:T(128)S(1)} %pad_add_fusion.scal_ref, bf16[512,576]{1,0:T(8,128)(2,1)S(1)} %get-tuple-element.30.q_ref, f32[512,128]{1,0:T(8,128)S(1)} %get-tuple-element.34.m_in, f32[512,128]{1,0:T(8,128)S(1)} %get-tuple-element.35.l_in, ...), custom_call_target="tpu_custom_call" | custom-call | tf_op jit(solution)/shard_map/middle/pallas_call | solution.py:242
  78.1 0.0 collective-permute-done.13.rest_1_
  78.1 4.1 %middle.5 = (f32[512,128]{1,0:T(8,128)S(1)}, f32[512,128]{1,0:T(8,128)S(1)}, f32[512,512]{1,0:T(8,128)S(1)}) custom-call(s32[11]{0:T(128)S(1)} %pad_add_fusion.scal_ref, bf16[512,576]{1,0:T(8,128)(2,1)S(1)} %get-tuple-element.30.q_ref, f32[512,128]{1,0:T(8,128)S(1)} %get-tuple-element.37.m_in, f32[512,128]{1,0:T(8,128)S(1)} %get-tuple-element.38.l_in, ...), custom_call_target="tpu_custom_call" | custom-call | tf_op jit(solution)/shard_map/middle/pallas_call | solution.py:242
  82.2 0.0 collective-permute-done.15.rest_2_
  82.2 0.0 collective-permute-done.14.rest_0_
  82.2 3.3 %last.1 = bf16[16,2,2176]{2,1,0:T(2,128)(2,1)S(1)} custom-call(s32[11]{0:T(128)S(1)} %pad_add_fusion.scal_ref, s32[16]{0:T(128)S(1)} %get-tuple-element.71.place_ref, bf16[512,576]{1,0:T(8,128)(2,1)S(1)} %get-tuple-element.30.q_ref, f32[512,128]{1,0:T(8,128)S(1)} %get-tuple-element.40.m_in, f32[512,128]{1,0:T(8,128)S(1)} %get-tuple-element.41.l_in, ...), custom_call_target="tpu_custom_call" | custom-call | tf_op jit(solution)/shard_map/last/pallas_call | solution.py:253
  85.5 11.4 %all_to_all.5.parts_ref = bf16[16,2,2176]{2,1,0:T(2,128)(2,1)S(1)} all-to-all(bf16[16,2,2176]{2,1,0:T(2,128)(2,1)S(1)} %last.1), channel_id=1, replica_groups=mesh['groups'=2,'ctx'=16] {'ctx'}, dimensions={0} | all-to-all | bytes 278528 | tf_op jit(solution)/shard_map/all_to_all | solution.py:268
  96.9 1.8 %merge.1 = bf16[2,16384]{1,0:T(2,128)(2,1)} custom-call(bf16[16,2,2176]{2,1,0:T(2,128)(2,1)S(1)} %all_to_all.5.parts_ref), custom_call_target="tpu_custom_call" | custom-call | tf_op jit(solution)/shard_map/merge/pallas_call | solution.py:269
  (23 shorter events, 0.2 us)
Async XLA Ops:
  0.0 47.3 %collective-permute-start.8 = (bf16[576,254]{1,0:T(8,128)(2,1)}, bf16[576,254]{1,0:T(8,128)(2,1)S(1)}, u32[]{:S(2)}, u32[]{:S(2)}) collective-permute-start(bf16[576,254]{1,0:T(8,128)(2,1)} %bitcast.65), channel_id=1, source_target_pairs={{2,6},{3,7},{6,10},{7,11},{10,14},{11,15},{14,12},{15,13},{12,8},{... | collective-permute-start | bytes 877832 | tf_op jit(solution)/shard_map/ppermute | solution.py:193
  2.9 44.5 %collective-permute-start.9 = (bf16[576,254]{1,0:T(8,128)(2,1)}, bf16[576,254]{1,0:T(8,128)(2,1)S(1)}, u32[]{:S(2)}, u32[]{:S(2)}) collective-permute-start(bf16[576,254]{1,0:T(8,128)(2,1)} %bitcast.66), channel_id=1, source_target_pairs={{2,0},{3,1},{6,2},{7,3},{10,6},{11,7},{14,10},{15,11},{12,14},{13,... | collective-permute-start | bytes 877832 | tf_op jit(solution)/shard_map/ppermute | solution.py:195
  4.5 0.7 copy-start.6
  5.3 29.0 %collective-permute-start = (bf16[40,576]{1,0:T(8,128)(2,1)S(1)}, bf16[40,576]{1,0:T(8,128)(2,1)S(1)}, u32[]{:S(2)}, u32[]{:S(2)}) collective-permute-start(bf16[40,576]{1,0:T(8,128)(2,1)S(1)} %get-tuple-element.81), channel_id=1, source_target_pairs={{0,2},{1,3},{2,0},{3,1},{4,6},{5,7},{6,4},{7,5},{8,10},{9,11},{10,... | collective-permute-start | bytes 138248 | tf_op jit(solution)/shard_map/ppermute | solution.py:206
  7.3 30.1 %collective-permute-start.1 = (bf16[40,576]{1,0:T(8,128)(2,1)S(1)}, bf16[40,576]{1,0:T(8,128)(2,1)S(1)}, u32[]{:S(2)}, u32[]{:S(2)}) collective-permute-start(bf16[40,576]{1,0:T(8,128)(2,1)S(1)} %get-tuple-element.82), channel_id=1, source_target_pairs={{0,4},{1,5},{2,6},{3,7},{4,0},{5,1},{6,2},{7,3},{8,12},{9,13},{10,... | collective-permute-start | bytes 138248 | tf_op jit(solution)/shard_map/ppermute | solution.py:206
  8.9 29.9 %collective-permute-start.2 = (bf16[40,576]{1,0:T(8,128)(2,1)S(1)}, bf16[40,576]{1,0:T(8,128)(2,1)S(1)}, u32[]{:S(2)}, u32[]{:S(2)}) collective-permute-start(bf16[40,576]{1,0:T(8,128)(2,1)S(1)} %get-tuple-element.83), channel_id=1, source_target_pairs={{0,6},{1,7},{2,4},{3,5},{4,2},{5,3},{6,0},{7,1},{8,14},{9,15},{10,... | collective-permute-start | bytes 138248 | tf_op jit(solution)/shard_map/ppermute | solution.py:206
  9.0 57.0 %copy-start.5 = (s32[16,2]{1,0:T(8,128)}, s32[16,2]{1,0:T(8,128)S(1)}, u32[]{:S(2)}) copy-start(s32[16,2]{1,0:T(8,128)S(1)} %iota_add_fusion) | copy-start | bytes 388
  10.5 0.7 copy-start.7
  11.3 35.9 %copy-start = (bf16[8,512,128]{2,1,0:T(8,128)(2,1)S(1)}, bf16[8,512,128]{2,1,0:T(8,128)(2,1)}, u32[]{:S(2)}) copy-start(bf16[8,512,128]{2,1,0:T(8,128)(2,1)} %rest_1_.1) | copy-start | bytes 3145732
  16.3 0.7 copy-start.4
  34.3 8.1 %collective-permute-start.3 = (bf16[40,576]{1,0:T(8,128)(2,1)S(1)}, bf16[40,576]{1,0:T(8,128)(2,1)S(1)}, u32[]{:S(2)}, u32[]{:S(2)}) collective-permute-start(bf16[40,576]{1,0:T(8,128)(2,1)S(1)} %get-tuple-element.84), channel_id=1, source_target_pairs={{0,8},{1,9},{2,10},{3,11},{4,12},{5,13},{6,14},{7,15},{8,0},{9,1},... | collective-permute-start | bytes 138248 | tf_op jit(solution)/shard_map/ppermute | solution.py:206
  37.4 9.7 %collective-permute-start.4 = (bf16[40,576]{1,0:T(8,128)(2,1)S(1)}, bf16[40,576]{1,0:T(8,128)(2,1)S(1)}, u32[]{:S(2)}, u32[]{:S(2)}) collective-permute-start(bf16[40,576]{1,0:T(8,128)(2,1)S(1)} %get-tuple-element.85), channel_id=1, source_target_pairs={{0,10},{1,11},{2,8},{3,9},{4,14},{5,15},{6,12},{7,13},{8,2},{9,3},... | collective-permute-start | bytes 138248 | tf_op jit(solution)/shard_map/ppermute | solution.py:206
  38.8 8.6 %collective-permute-start.5 = (bf16[40,576]{1,0:T(8,128)(2,1)S(1)}, bf16[40,576]{1,0:T(8,128)(2,1)S(1)}, u32[]{:S(2)}, u32[]{:S(2)}) collective-permute-start(bf16[40,576]{1,0:T(8,128)(2,1)S(1)} %get-tuple-element.86), channel_id=1, source_target_pairs={{0,12},{1,13},{2,14},{3,15},{4,8},{5,9},{6,10},{7,11},{8,4},{9,5},... | collective-permute-start | bytes 138248 | tf_op jit(solution)/shard_map/ppermute | solution.py:206
  42.5 15.2 %collective-permute-start.6 = (bf16[40,576]{1,0:T(8,128)(2,1)S(1)}, bf16[40,576]{1,0:T(8,128)(2,1)S(1)}, u32[]{:S(2)}, u32[]{:S(2)}) collective-permute-start(bf16[40,576]{1,0:T(8,128)(2,1)S(1)} %get-tuple-element.80), channel_id=1, source_target_pairs={{0,14},{1,15},{2,12},{3,13},{4,10},{5,11},{6,8},{7,9},{8,6},{9,7},... | collective-permute-start | bytes 138248 | tf_op jit(solution)/shard_map/ppermute | solution.py:206
  47.2 35.0 %collective-permute-start.15 = (bf16[8,512,128]{2,1,0:T(8,128)(2,1)S(1)}, bf16[8,512,128]{2,1,0:T(8,128)(2,1)S(1)}, u32[]{:S(2)}, u32[]{:S(2)}) collective-permute-start(bf16[8,512,128]{2,1,0:T(8,128)(2,1)S(1)} %copy-done), channel_id=1, source_target_pairs={{0,1},{1,0},{2,3},{3,2},{4,5},{5,4},{6,7},{7,6},{8,9},{9,8},{10,11... | collective-permute-start | bytes 3145736 | tf_op jit(solution)/shard_map/ppermute | solution.py:210
  47.3 9.4 %collective-permute-start.10 = (bf16[576,254]{1,0:T(8,128)(2,1)S(1)}, bf16[576,254]{1,0:T(8,128)(2,1)S(1)}, u32[]{:S(2)}, u32[]{:S(2)}) collective-permute-start(bf16[576,254]{1,0:T(8,128)(2,1)S(1)} %collective-permute-done.8.rest_0_), channel_id=1, source_target_pairs={{2,6},{3,7},{6,10},{7,11},{10,14},{11,15},{14,12},{15,13},{12,8},{... | collective-permute-start | bytes 877832 | tf_op jit(solution)/shard_map/ppermute | solution.py:193
  47.4 12.4 %collective-permute-start.11 = (bf16[576,254]{1,0:T(8,128)(2,1)S(1)}, bf16[576,254]{1,0:T(8,128)(2,1)}, u32[]{:S(2)}, u32[]{:S(2)}) collective-permute-start(bf16[576,254]{1,0:T(8,128)(2,1)S(1)} %collective-permute-done.9.rest_1_), channel_id=1, source_target_pairs={{2,0},{3,1},{6,2},{7,3},{10,6},{11,7},{14,10},{15,11},{12,14},{13,... | collective-permute-start | bytes 877832 | tf_op jit(solution)/shard_map/ppermute | solution.py:195
  56.7 8.8 %collective-permute-start.12 = (bf16[576,254]{1,0:T(8,128)(2,1)S(1)}, bf16[576,254]{1,0:T(8,128)(2,1)}, u32[]{:S(2)}, u32[]{:S(2)}) collective-permute-start(bf16[576,254]{1,0:T(8,128)(2,1)S(1)} %collective-permute-done.10.rest_0_), channel_id=1, source_target_pairs={{2,6},{3,7},{6,10},{7,11},{10,14},{11,15},{14,12},{15,13},{12,8},{... | collective-permute-start | bytes 877832 | tf_op jit(solution)/shard_map/ppermute | solution.py:193
  57.0 0.7 copy-start.1
  57.7 10.3 %collective-permute-start.7 = (bf16[8,40,576]{2,1,0:T(8,128)(2,1)S(1)}, bf16[8,40,576]{2,1,0:T(8,128)(2,1)S(1)}, u32[]{:S(2)}, u32[]{:S(2)}) collective-permute-start(bf16[8,40,576]{2,1,0:T(8,128)(2,1)S(1)} %bitcast_dynamic-update-slice_fusion.here_ref), channel_id=1, source_target_pairs={{0,1},{1,0},{2,3},{3,2},{4,5},{5,4},{6,7},{7,6},{8,9},{9,8},{10,11... | collective-permute-start | bytes 1105928 | tf_op jit(solution)/shard_map/ppermute | solution.py:209
  59.8 18.3 %collective-permute-start.13 = (bf16[576,254]{1,0:T(8,128)(2,1)}, bf16[576,254]{1,0:T(8,128)(2,1)}, u32[]{:S(2)}, u32[]{:S(2)}) collective-permute-start(bf16[576,254]{1,0:T(8,128)(2,1)} %collective-permute-done.11.rest_1_), channel_id=1, source_target_pairs={{2,0},{3,1},{6,2},{7,3},{10,6},{11,7},{14,10},{15,11},{12,14},{13,... | collective-permute-start | bytes 877832 | tf_op jit(solution)/shard_map/ppermute | solution.py:195
  65.5 16.8 %collective-permute-start.14 = (bf16[576,254]{1,0:T(8,128)(2,1)}, bf16[576,254]{1,0:T(8,128)(2,1)}, u32[]{:S(2)}, u32[]{:S(2)}) collective-permute-start(bf16[576,254]{1,0:T(8,128)(2,1)} %collective-permute-done.12.rest_0_), channel_id=1, source_target_pairs={{2,6},{3,7},{6,10},{7,11},{10,14},{11,15},{14,12},{15,13},{12,8},{... | collective-permute-start | bytes 877832 | tf_op jit(solution)/shard_map/ppermute | solution.py:193
  65.9 0.9 slice-start
  66.9 1.1 %copy-start.3 = (bf16[254,576]{0,1:T(8,128)(2,1)S(1)}, bf16[254,576]{0,1:T(8,128)(2,1)}, u32[]{:S(2)}) copy-start(bf16[254,576]{0,1:T(8,128)(2,1)} %param.10) | copy-start | bytes 877828
  70.7 3.4 %copy-start.2 = (bf16[576,254]{1,0:T(8,128)(2,1)S(1)}, bf16[576,254]{1,0:T(8,128)(2,1)}, u32[]{:S(2)}) copy-start(bf16[576,254]{1,0:T(8,128)(2,1)} %copy-done.1) | copy-start | bytes 877828

commit v2 on v1

--- a/solution.py
+++ b/solution.py
@@ -55,7 +55,24 @@
         l_ref[part, :] = jnp.broadcast_to(l_new, (block, LANES))
 
 
-def first_kernel(tokens, heads, scal_ref, here_ref, there_ref, row_token_ref, key_token_ref,
+def parted(index, size):
+    return index >> (size.bit_length() - 1), index & (size - 1)
+
+
+def token_of(index, tokens, chips):
+    me = lax.axis_index("ctx")
+    device, t = parted(index, tokens)
+    core, offset = parted(device, chips)
+    return (((me // CORES) ^ offset) * CORES + ((me % CORES) ^ core)) * tokens + t
+
+
+def base_of(table_ref, at, slots):
+    me = lax.axis_index("ctx")
+    count = table_ref.shape[0] // (lax.axis_size("ctx") // CORES)
+    return (table_ref[(me // CORES) * count + at] * CORES + me % CORES) * slots
+
+
+def first_kernel(tokens, heads, length_ref, offset_ref, table_ref, here_ref, there_ref,
                  key_ref, q_ref, m_ref, l_ref, acc_ref, span_ref):
     chips = here_ref.shape[0]
     rows = tokens * heads
@@ -70,13 +87,16 @@
     span = span_ref[...].astype(bf16)
     total = q_ref.shape[0]
     block = min(256, total)
-    key_token = key_token_ref[...]
+    key_index = lax.broadcasted_iota(jnp.int32, (1, span.shape[0]), 1)
+    key_token = token_of(key_index, tokens, chips)
     for start in range(0, total, block):
         part = pl.ds(start, block)
         s = lax.dot_general(
             q_ref[part, :], span, (((1,), (1,)), ((), ())), preferred_element_type=f32
         ) * score_scale
-        shown = (key_token >= scal_ref[1]) & (key_token <= row_token_ref[part, :])
+        row_index = start + lax.broadcasted_iota(jnp.int32, (block, 1), 0)
+        row_token = token_of(row_index >> (heads.bit_length() - 1), tokens, chips)
+        shown = (key_token >= offset_ref[0]) & (key_token <= row_token)
         s = jnp.where(shown, s, neg_large)
         m_new = jnp.max(s, axis=1, keepdims=True)
         probs = jnp.where(shown, jnp.exp2(s - m_new), 0.0)
@@ -86,32 +106,34 @@
         )
         m_ref[part, :] = jnp.broadcast_to(m_new, (block, LANES))
         l_ref[part, :] = jnp.broadcast_to(l_new, (block, LANES))
-    fold_shard(q_ref, key_ref, scal_ref[3], scal_ref[0], m_ref, l_ref, acc_ref)
-
-
-def middle_kernel(at, count, scal_ref, q_ref, m_in, l_in, acc_in, *rest):
+    base = base_of(table_ref, 0, key_ref.shape[1])
+    fold_shard(q_ref, key_ref, base, length_ref[0], m_ref, l_ref, acc_ref)
+
+
+def middle_kernel(at, count, length_ref, table_ref, q_ref, m_in, l_in, acc_in, *rest):
     keys, (m_ref, l_ref, acc_ref) = rest[:count], rest[count:]
     m_ref[...] = m_in[...]
     l_ref[...] = l_in[...]
     acc_ref[...] = acc_in[...]
     for j, key_ref in enumerate(keys):
-        base = scal_ref[3 + at + j]
-
-        @pl.when(base < scal_ref[0])
+        base = base_of(table_ref, at + j, key_ref.shape[1])
+
+        @pl.when(base < length_ref[0])
         def _():
-            fold_shard(q_ref, key_ref, base, scal_ref[0], m_ref, l_ref, acc_ref)
-
-
-def last_kernel(at, count, tokens, heads, scal_ref, place_ref, q_ref, m_in, l_in, acc_in, *rest):
+            fold_shard(q_ref, key_ref, base, length_ref[0], m_ref, l_ref, acc_ref)
+
+
+def last_kernel(at, count, tokens, heads, length_ref, table_ref, q_ref, m_in, l_in, acc_in, *rest):
     keys = rest[:count]
     own_up, far_up, out_ref, m_ref, l_ref, acc_ref, context_ref, flat_ref = rest[count:]
-    middle_kernel(at, count, scal_ref, q_ref, m_in, l_in, acc_in, *keys, m_ref, l_ref, acc_ref)
+    middle_kernel(at, count, length_ref, table_ref, q_ref, m_in, l_in, acc_in, *keys, m_ref, l_ref, acc_ref)
     for k in range(LATENT // LANES):
         lanes = slice(k * LANES, (k + 1) * LANES)
         context_ref[k] = acc_ref[:, lanes] / l_ref[...]
     m_ref[...] = m_ref[...] + jnp.log2(l_ref[...])
     everyone = flat_ref.shape[0]
-    core = scal_ref[2]
+    me = lax.axis_index("ctx")
+    core = me % CORES
     per_core = heads // CORES
     tail = jnp.zeros((everyone, LANES), f32)
     lane = lax.broadcasted_iota(jnp.int32, (everyone, LANES), 1)
@@ -132,8 +154,11 @@
             tail = jnp.where(lane == head + heads, mid, tail)
             tail = jnp.where(lane == head + 2 * heads, low, tail)
     flat_ref[:, heads * V_HEAD:] = tail
-    for i in range(everyone // tokens):
-        out_ref[place_ref[i]] = flat_ref[i * tokens:(i + 1) * tokens, :].astype(bf16)
+    devices = everyone // tokens
+    for i in range(devices):
+        place = (me // CORES) ^ (i % (devices // CORES))
+        place = place * CORES + (core ^ (i // (devices // CORES)))
+        out_ref[place] = flat_ref[i * tokens:(i + 1) * tokens, :].astype(bf16)
 
 
 def merge_kernel(heads, parts_ref, out_ref):
@@ -177,7 +202,7 @@
     backward = chips - 1 - onward
 
     me = lax.axis_index("ctx")
-    chip, core = me // CORES, me % CORES
+    chip = me // CORES
 
     def across(step):
         return [
@@ -200,11 +225,15 @@
     pieces = []
     for o in range(chips):
         piece = lax.dynamic_slice(grouped, (0, (chip ^ o) * heads, 0), (tokens, heads, width))
-        piece = jnp.concatenate([piece.reshape(rows, width), span_rows], axis=0)
-        if o:
-            swap = [(d, d ^ (o * CORES)) for d in range(ctx)]
-            piece = lax.ppermute(piece, "ctx", swap)
-        pieces.append(piece)
+        pieces.append(jnp.concatenate([piece.reshape(rows, width), span_rows], axis=0))
+    bit = 1
+    while bit < chips:
+        away = [o for o in range(chips) if o & bit]
+        swap = [(d, d ^ (bit * CORES)) for d in range(ctx)]
+        moved = lax.ppermute(jnp.stack([pieces[o] for o in away]), "ctx", swap)
+        for j, o in enumerate(away):
+            pieces[o] = moved[j]
+        bit *= 2
     here = jnp.stack(pieces)
     there = lax.ppermute(here, "ctx", other_core)
     far_up = lax.ppermute(value_up, "ctx", other_core)
@@ -217,24 +246,18 @@
     owner_table = np.array(
         [[walk[(spot[p] + t) % chips] for t in turns] for p in range(chips)], np.int32
     )
-    owners = lax.dynamic_index_in_dim(jnp.asarray(owner_table), chip, 0, keepdims=False)
-    bases = (owners * CORES + core) * slots
-    scal = jnp.concatenate([prefix_length, span_offset, core[None], bases]).astype(jnp.int32)
-    index = jnp.arange(ctx, dtype=jnp.int32)
-    place = ((chip ^ (index % chips)) * CORES + (core ^ (index // chips))).astype(jnp.int32)
-    key_token = (place[:, None] * tokens + jnp.arange(tokens, dtype=jnp.int32)[None, :]).reshape(-1)
-    row_token = jnp.repeat(key_token, heads, total_repeat_length=total)[:, None]
+    table = jnp.asarray(owner_table.reshape(-1))
 
     state_shapes = [shape(total, LANES), shape(total, LANES), shape(total, LATENT)]
     q, *state = pl.pallas_call(
         functools.partial(first_kernel, tokens, heads),
         out_shape=[shape(total, width, dtype=bf16)] + state_shapes,
-        in_specs=[SMEM] + [VMEM] * 5,
+        in_specs=[SMEM] * 3 + [VMEM] * 3,
         out_specs=[VMEM] * 4,
         scratch_shapes=[pltpu.VMEM((everyone // CORES, width), f32)],
         compiler_params=PARAMS,
         name="first",
-    )(scal, here, there, row_token, key_token[None, :everyone // CORES], own)
+    )(prefix_length, span_offset, table, here, there, own)
 
     at = 1
     for s in range(1, onward):
@@ -242,11 +265,11 @@
         state = pl.pallas_call(
             functools.partial(middle_kernel, at, len(keys)),
             out_shape=state_shapes,
-            in_specs=[SMEM] + [VMEM] * (4 + len(keys)),
+            in_specs=[SMEM] * 2 + [VMEM] * (4 + len(keys)),
             out_specs=[VMEM] * 3,
             compiler_params=PARAMS,
             name="middle",
-        )(scal, q, *state, *keys)
+        )(prefix_length, table, q, *state, *keys)
         at += len(keys)
     keys = [right[onward]] + ([left[onward]] if onward <= backward else [])
     flat = heads * V_HEAD + LANES
@@ -264,7 +287,7 @@
         ],
         compiler_params=PARAMS,
         name="last",
-    )(scal, place, q, *state, *keys, value_up, far_up)
+    )(prefix_length, table, q, *state, *keys, value_up, far_up)
     returned = lax.all_to_all(parts, "ctx", split_axis=0, concat_axis=0, tiled=True)
     return pl.pallas_call(
         functools.partial(merge_kernel, heads),

time: 99.4 us -> 69.4 us (0.70)
  other arithmetic: 24.3 us -> 0.34 us
  waiting for transfers between devices: 11.1 us -> 17.1 us
  starting transfers between devices: 24.1 us -> 19.1 us
  local copies, waits for them, and re-layouts: 6.93 us -> 2.07 us
  Pallas kernels: 19.3 us -> 15.2 us
  blocking collectives: 11.4 us -> 14 us
    gather x3 -> x0, other arithmetic: 22.1 us -> none  [on_device(): row_token = jnp.repeat(key_token, heads, total_repeat_length=total)[:, None]]
    ppermute x7 -> x3, waiting for transfers between devices: 0.02 us -> 11.6 us  [on_device(): moved = lax.ppermute(jnp.stack([pieces[o] for o in away]), 'ctx', swap)]
    ppermute x7 -> x3, starting transfers between devices: 16.4 us -> 7.58 us  [on_device(): moved = lax.ppermute(jnp.stack([pieces[o] for o in away]), 'ctx', swap)]
    ppermute x4, waiting for transfers between devices: 11.1 us -> 3.01 us  [on_device(): right.append(lax.ppermute(right[-1], 'ctx', across(1)))]
    ppermute x3, starting transfers between devices: 3.93 us -> 6.94 us  [on_device(): left.append(lax.ppermute(left[-1], 'ctx', across(-1)))]
    all_to_all x1, blocking collectives: 11.4 us -> 14 us  [on_device(): lax.all_to_all(parts, 'ctx', split_axis=0, concat_axis=0, tiled=True)]
    ppermute x3, waiting for transfers between devices: 0.01 us -> 2.52 us  [on_device(): left.append(lax.ppermute(left[-1], 'ctx', across(-1)))]
    pallas_call x3, Pallas kernels: 11.4 us -> 9.07 us  [on_device(): pl.pallas_call(functools.partial(middle_kernel, at, len(keys)), out_shape...]
  transfers between devices with their start and end apart: 16 -> 12, of which waited for: 2 -> 5; matrix products, arithmetic and copies ran while one was open for 29% -> 0% of each run, Pallas kernels for 14% -> 17%
where the time goes in v2:
time: 69.4 us; the launch traced here: 69.3 us
  starting transfers between devices  19.1 us (28%)
  waiting for transfers between devices  17.1 us (25%)
  Pallas kernels  15.2 us (22%)
  blocking collectives  14 us (20%)
  local copies, waits for them, and re-layouts  2.07 us (3%)
  between operations  1.52 us (2%)
    all_to_all x1, blocking collectives, on_device(): lax.all_to_all(parts, 'ctx', split_axis=0, concat_axis=0, tiled=True)  14 us
    ppermute x3, waiting for transfers between devices, on_device(): moved = lax.ppermute(jnp.stack([pieces[o] for o in away]), 'ctx', swap)  11.6 us
    pallas_call x3, Pallas kernels, on_device(): pl.pallas_call(functools.partial(middle_kernel, at, len(keys)), out_shape...  9.07 us
    ppermute x3, starting transfers between devices, on_device(): moved = lax.ppermute(jnp.stack([pieces[o] for o in away]), 'ctx', swap)  7.58 us
    ppermute x3, starting transfers between devices, on_device(): left.append(lax.ppermute(left[-1], 'ctx', across(-1)))  6.94 us
    ppermute x4, starting transfers between devices, on_device(): right.append(lax.ppermute(right[-1], 'ctx', across(1)))  4.47 us
    ppermute x4, waiting for transfers between devices, on_device(): right.append(lax.ppermute(right[-1], 'ctx', across(1)))  3.01 us
    pallas_call x1, Pallas kernels, on_device(): pl.pallas_call(functools.partial(first_kernel, tokens, heads), out_shape=...  2.67 us
  transfers between devices with their start and end apart: 12, of which 5 were waited for; matrix products, arithmetic and copies ran while one was open for 0% of the time, Pallas kernels for 17%

profile of v2, /device:TPU:0, one launch (start us, length us, event | category | flops | bytes accessed | tf_op | source)
XLA Modules:
  0.0 69.3 jit_solution(725569017335260251)
XLA Ops:
  0.0 1.3 %reshape.27 = bf16[2,128,576]{2,1,0:T(8,128)(2,1)S(1)} reshape(bf16[2,73728]{1,0:T(2,128)(2,1)} %param.7) | data formatting | bytes 589824 | tf_op jit(solution)/shard_map/reshape | solution.py:222
  1.3 0.1 pad.38.clone
  1.4 0.0 copy-start.3
  1.4 0.0 copy-start.1
  1.5 0.0 copy-start
  1.5 0.6 copy-done.3
  2.1 0.1 fusion.1
  2.3 3.0 %collective-permute-start = (bf16[4,40,576]{2,1,0:T(8,128)(2,1)S(1)}, bf16[4,40,576]{2,1,0:T(8,128)(2,1)S(1)}, u32[]{:S(2)}, u32[]{:S(2)}) collective-permute-start(bf16[4,40,576]{2,1,0:T(8,128)(2,1)S(1)} %pad_maximum_fusion.1), channel_id=1, source_target_pairs={{0,2},{1,3},{2,0},{3,1},{4,6},{5,7},{6,4},{7,5},{8,10},{9,11},{10,... | collective-permute-start | bytes 552968 | tf_op jit(solution)/shard_map/ppermute | solution.py:233
  5.3 0.0 copy-done.1
  5.3 0.1 collective-permute-start.4
  5.4 5.4 %collective-permute-done = bf16[4,40,576]{2,1,0:T(8,128)(2,1)S(1)} collective-permute-done((bf16[4,40,576]{2,1,0:T(8,128)(2,1)S(1)}, bf16[4,40,576]{2,1,0:T(8,128)(2,1)S(1)}, u32[]{:S(2)}, u32[]{:S(2)}) %collective-permute-start) | collective-permute-done | bytes 184352 | tf_op jit(solution)/shard_map/ppermute | solution.py:233
  10.8 1.5 %collective-permute-start.1 = (bf16[4,40,576]{2,1,0:T(8,128)(2,1)S(1)}, bf16[4,40,576]{2,1,0:T(8,128)(2,1)S(1)}, u32[]{:S(2)}, u32[]{:S(2)}) collective-permute-start(bf16[4,40,576]{2,1,0:T(8,128)(2,1)S(1)} %pad_maximum_fusion.2), channel_id=1, source_target_pairs={{0,4},{1,5},{2,6},{3,7},{4,0},{5,1},{6,2},{7,3},{8,12},{9,13},{10,... | collective-permute-start | bytes 552968 | tf_op jit(solution)/shard_map/ppermute | solution.py:233
  12.3 0.0 copy-done
  12.3 0.0 collective-permute-start.11
  12.3 0.6 collective-permute-start.5
  12.9 3.0 %collective-permute-done.4.rest_0_ = bf16[576,254]{1,0:T(8,128)(2,1)S(1)} collective-permute-done((bf16[576,254]{1,0:T(8,128)(2,1)S(1)}, bf16[576,254]{1,0:T(8,128)(2,1)S(1)}, u32[]{:S(2)}, u32[]{:S(2)}) %collective-permute-start.4) | collective-permute-done | bytes 292640 | tf_op jit(solution)/shard_map/ppermute | solution.py:218
  15.9 2.5 %collective-permute-start.6 = (bf16[576,254]{1,0:T(8,128)(2,1)S(1)}, bf16[576,254]{1,0:T(8,128)(2,1)S(1)}, u32[]{:S(2)}, u32[]{:S(2)}) collective-permute-start(bf16[576,254]{1,0:T(8,128)(2,1)S(1)} %collective-permute-done.4.rest_0_), channel_id=1, source_target_pairs={{2,6},{3,7},{6,10},{7,11},{10,14},{11,15},{14,12},{15,13},{12,8},{... | collective-permute-start | bytes 877832 | tf_op jit(solution)/shard_map/ppermute | solution.py:218
  18.4 0.1 collective-permute-done.1
  18.6 3.1 %collective-permute-start.2 = (bf16[4,40,576]{2,1,0:T(8,128)(2,1)S(1)}, bf16[4,40,576]{2,1,0:T(8,128)(2,1)S(1)}, u32[]{:S(2)}, u32[]{:S(2)}) collective-permute-start(bf16[4,40,576]{2,1,0:T(8,128)(2,1)S(1)} %pad_maximum_fusion.3), channel_id=1, source_target_pairs={{0,8},{1,9},{2,10},{3,11},{4,12},{5,13},{6,14},{7,15},{8,0},{9,1},... | collective-permute-start | bytes 552968 | tf_op jit(solution)/shard_map/ppermute | solution.py:233
  21.7 2.5 %collective-permute-done.5.rest_1_ = bf16[576,254]{1,0:T(8,128)(2,1)S(1)} collective-permute-done((bf16[576,254]{1,0:T(8,128)(2,1)S(1)}, bf16[576,254]{1,0:T(8,128)(2,1)S(1)}, u32[]{:S(2)}, u32[]{:S(2)}) %collective-permute-start.5) | collective-permute-done | bytes 292640 | tf_op jit(solution)/shard_map/ppermute | solution.py:220
  24.2 2.5 %collective-permute-start.7 = (bf16[576,254]{1,0:T(8,128)(2,1)S(1)}, bf16[576,254]{1,0:T(8,128)(2,1)S(1)}, u32[]{:S(2)}, u32[]{:S(2)}) collective-permute-start(bf16[576,254]{1,0:T(8,128)(2,1)S(1)} %collective-permute-done.5.rest_1_), channel_id=1, source_target_pairs={{2,0},{3,1},{6,2},{7,3},{10,6},{11,7},{14,10},{15,11},{12,14},{13,... | collective-permute-start | bytes 877832 | tf_op jit(solution)/shard_map/ppermute | solution.py:220
  26.7 0.0 collective-permute-done.6.rest_0_
  26.7 1.9 %collective-permute-start.8 = (bf16[576,254]{1,0:T(8,128)(2,1)S(1)}, bf16[576,254]{1,0:T(8,128)(2,1)S(1)}, u32[]{:S(2)}, u32[]{:S(2)}) collective-permute-start(bf16[576,254]{1,0:T(8,128)(2,1)S(1)} %collective-permute-done.6.rest_0_), channel_id=1, source_target_pairs={{2,6},{3,7},{6,10},{7,11},{10,14},{11,15},{14,12},{15,13},{12,8},{... | collective-permute-start | bytes 877832 | tf_op jit(solution)/shard_map/ppermute | solution.py:218
  28.6 6.1 %collective-permute-done.2 = bf16[4,40,576]{2,1,0:T(8,128)(2,1)S(1)} collective-permute-done((bf16[4,40,576]{2,1,0:T(8,128)(2,1)S(1)}, bf16[4,40,576]{2,1,0:T(8,128)(2,1)S(1)}, u32[]{:S(2)}, u32[]{:S(2)}) %collective-permute-start.2) | collective-permute-done | bytes 184352 | tf_op jit(solution)/shard_map/ppermute | solution.py:233
  34.7 0.1 pad_maximum_fusion.here_ref
  34.8 0.1 collective-permute-start.3
  34.9 0.0 collective-permute-done.7.rest_1_
  34.9 3.9 %collective-permute-start.9 = (bf16[576,254]{1,0:T(8,128)(2,1)S(1)}, bf16[576,254]{1,0:T(8,128)(2,1)S(1)}, u32[]{:S(2)}, u32[]{:S(2)}) collective-permute-start(bf16[576,254]{1,0:T(8,128)(2,1)S(1)} %collective-permute-done.7.rest_1_), channel_id=1, source_target_pairs={{2,0},{3,1},{6,2},{7,3},{10,6},{11,7},{14,10},{15,11},{12,14},{13,... | collective-permute-start | bytes 877832 | tf_op jit(solution)/shard_map/ppermute | solution.py:220
  38.7 0.0 collective-permute-done.8.rest_0_
  38.7 0.0 collective-permute-start.10
  39.4 0.0 copy-start.2
  40.1 0.0 collective-permute-done.3.there_ref
  40.1 0.0 copy-done.2
  40.1 2.7 %first.1 = (bf16[512,576]{1,0:T(8,128)(2,1)S(1)}, f32[512,128]{1,0:T(8,128)S(1)}, f32[512,128]{1,0:T(8,128)S(1)}, f32[512,512]{1,0:T(8,128)S(1)}) custom-call(s32[1]{0:T(128)S(6)} %copy.8.length_ref, s32[1]{0:T(128)S(6)} %copy.9.offset_ref, s32[64]{0:T(128)S(1)} %copy-done.2, bf16[8,40,576]{2,1,0:T(8,128)(2,1)S(1)} %pad_maximum_fusion.here_ref, ...), custom_call_target="tpu_custom_call" | custom-call | tf_op jit(solution)/shard_map/first/pallas_call | solution.py:252
  42.8 3.5 %middle.3 = (f32[512,128]{1,0:T(8,128)S(1)}, f32[512,128]{1,0:T(8,128)S(1)}, f32[512,512]{1,0:T(8,128)S(1)}) custom-call(s32[1]{0:T(128)S(6)} %copy.8.length_ref, s32[64]{0:T(128)S(1)} %copy-done.2, bf16[512,576]{1,0:T(8,128)(2,1)S(1)} %get-tuple-element.18.q_ref, f32[512,128]{1,0:T(8,128)S(1)} %get-tuple-element.19.m_in, ...), custom_call_target="tpu_custom_call" | custom-call | tf_op jit(solution)/shard_map/middle/pallas_call | solution.py:265
  46.3 3.5 %middle.4 = (f32[512,128]{1,0:T(8,128)S(1)}, f32[512,128]{1,0:T(8,128)S(1)}, f32[512,512]{1,0:T(8,128)S(1)}) custom-call(s32[1]{0:T(128)S(6)} %copy.8.length_ref, s32[64]{0:T(128)S(1)} %copy-done.2, bf16[512,576]{1,0:T(8,128)(2,1)S(1)} %get-tuple-element.18.q_ref, f32[512,128]{1,0:T(8,128)S(1)} %get-tuple-element.22.m_in, ...), custom_call_target="tpu_custom_call" | custom-call | tf_op jit(solution)/shard_map/middle/pallas_call | solution.py:265
  49.8 0.0 collective-permute-done.9.rest_1_
  49.8 2.1 %middle.5 = (f32[512,128]{1,0:T(8,128)S(1)}, f32[512,128]{1,0:T(8,128)S(1)}, f32[512,512]{1,0:T(8,128)S(1)}) custom-call(s32[1]{0:T(128)S(6)} %copy.8.length_ref, s32[64]{0:T(128)S(1)} %copy-done.2, bf16[512,576]{1,0:T(8,128)(2,1)S(1)} %get-tuple-element.18.q_ref, f32[512,128]{1,0:T(8,128)S(1)} %get-tuple-element.25.m_in, ...), custom_call_target="tpu_custom_call" | custom-call | tf_op jit(solution)/shard_map/middle/pallas_call | solution.py:265
  51.8 0.0 collective-permute-done.11.rest_2_
  51.9 0.0 collective-permute-done.10.rest_0_
  51.9 1.6 %last.1 = bf16[16,2,2176]{2,1,0:T(2,128)(2,1)S(1)} custom-call(s32[1]{0:T(128)S(6)} %copy.8.length_ref, s32[64]{0:T(128)S(1)} %copy-done.2, bf16[512,576]{1,0:T(8,128)(2,1)S(1)} %get-tuple-element.18.q_ref, f32[512,128]{1,0:T(8,128)S(1)} %get-tuple-element.28.m_in, f32[512,128]{1,0:T(8,128)S(1)} %get-tuple-element.29.l_in, ...), custom_call_target="tpu_custom_call" | custom-call | tf_op jit(solution)/shard_map/last/pallas_call | solution.py:276
  53.5 14.0 %all_to_all.5.parts_ref = bf16[16,2,2176]{2,1,0:T(2,128)(2,1)S(1)} all-to-all(bf16[16,2,2176]{2,1,0:T(2,128)(2,1)S(1)} %last.1), channel_id=1, replica_groups=mesh['groups'=2,'ctx'=16] {'ctx'}, dimensions={0} | all-to-all | bytes 278528 | tf_op jit(solution)/shard_map/all_to_all | solution.py:291
  67.5 1.8 %merge.1 = bf16[2,16384]{1,0:T(2,128)(2,1)} custom-call(bf16[16,2,2176]{2,1,0:T(2,128)(2,1)S(1)} %all_to_all.5.parts_ref), custom_call_target="tpu_custom_call" | custom-call | tf_op jit(solution)/shard_map/merge/pallas_call | solution.py:292
  (7 shorter events, 0.2 us)
Async XLA Ops:
  1.4 0.7 copy-start.3
  1.4 3.9 %copy-start.1 = (bf16[254,576]{0,1:T(8,128)(2,1)S(1)}, bf16[254,576]{0,1:T(8,128)(2,1)}, u32[]{:S(2)}) copy-start(bf16[254,576]{0,1:T(8,128)(2,1)} %param.8) | copy-start | bytes 877828
  1.5 10.9 %copy-start = (bf16[8,512,128]{2,1,0:T(8,128)(2,1)S(1)}, bf16[8,512,128]{2,1,0:T(8,128)(2,1)}, u32[]{:S(2)}) copy-start(bf16[8,512,128]{2,1,0:T(8,128)(2,1)} %rest_1_.1) | copy-start | bytes 3145732
  2.3 8.5 %collective-permute-start = (bf16[4,40,576]{2,1,0:T(8,128)(2,1)S(1)}, bf16[4,40,576]{2,1,0:T(8,128)(2,1)S(1)}, u32[]{:S(2)}, u32[]{:S(2)}) collective-permute-start(bf16[4,40,576]{2,1,0:T(8,128)(2,1)S(1)} %pad_maximum_fusion.1), channel_id=1, source_target_pairs={{0,2},{1,3},{2,0},{3,1},{4,6},{5,7},{6,4},{7,5},{8,10},{9,11},{10,... | collective-permute-start | bytes 552968 | tf_op jit(solution)/shard_map/ppermute | solution.py:233
  5.3 10.7 %collective-permute-start.4 = (bf16[576,254]{1,0:T(8,128)(2,1)S(1)}, bf16[576,254]{1,0:T(8,128)(2,1)S(1)}, u32[]{:S(2)}, u32[]{:S(2)}) collective-permute-start(bf16[576,254]{1,0:T(8,128)(2,1)S(1)} %bitcast.25), channel_id=1, source_target_pairs={{2,6},{3,7},{6,10},{7,11},{10,14},{11,15},{14,12},{15,13},{12,8},{... | collective-permute-start | bytes 877832 | tf_op jit(solution)/shard_map/ppermute | solution.py:218
  10.8 7.7 %collective-permute-start.1 = (bf16[4,40,576]{2,1,0:T(8,128)(2,1)S(1)}, bf16[4,40,576]{2,1,0:T(8,128)(2,1)S(1)}, u32[]{:S(2)}, u32[]{:S(2)}) collective-permute-start(bf16[4,40,576]{2,1,0:T(8,128)(2,1)S(1)} %pad_maximum_fusion.2), channel_id=1, source_target_pairs={{0,4},{1,5},{2,6},{3,7},{4,0},{5,1},{6,2},{7,3},{8,12},{9,13},{10,... | collective-permute-start | bytes 552968 | tf_op jit(solution)/shard_map/ppermute | solution.py:233
  12.3 39.5 %collective-permute-start.11 = (bf16[8,512,128]{2,1,0:T(8,128)(2,1)S(1)}, bf16[8,512,128]{2,1,0:T(8,128)(2,1)S(1)}, u32[]{:S(2)}, u32[]{:S(2)}) collective-permute-start(bf16[8,512,128]{2,1,0:T(8,128)(2,1)S(1)} %copy-done), channel_id=1, source_target_pairs={{0,1},{1,0},{2,3},{3,2},{4,5},{5,4},{6,7},{7,6},{8,9},{9,8},{10,11... | collective-permute-start | bytes 3145736 | tf_op jit(solution)/shard_map/ppermute | solution.py:239
  12.3 11.8 %collective-permute-start.5 = (bf16[576,254]{1,0:T(8,128)(2,1)S(1)}, bf16[576,254]{1,0:T(8,128)(2,1)S(1)}, u32[]{:S(2)}, u32[]{:S(2)}) collective-permute-start(bf16[576,254]{1,0:T(8,128)(2,1)S(1)} %bitcast.26), channel_id=1, source_target_pairs={{2,0},{3,1},{6,2},{7,3},{10,6},{11,7},{14,10},{15,11},{12,14},{13,... | collective-permute-start | bytes 877832 | tf_op jit(solution)/shard_map/ppermute | solution.py:220
  15.9 10.7 %collective-permute-start.6 = (bf16[576,254]{1,0:T(8,128)(2,1)S(1)}, bf16[576,254]{1,0:T(8,128)(2,1)S(1)}, u32[]{:S(2)}, u32[]{:S(2)}) collective-permute-start(bf16[576,254]{1,0:T(8,128)(2,1)S(1)} %collective-permute-done.4.rest_0_), channel_id=1, source_target_pairs={{2,6},{3,7},{6,10},{7,11},{10,14},{11,15},{14,12},{15,13},{12,8},{... | collective-permute-start | bytes 877832 | tf_op jit(solution)/shard_map/ppermute | solution.py:218
  18.6 16.1 %collective-permute-start.2 = (bf16[4,40,576]{2,1,0:T(8,128)(2,1)S(1)}, bf16[4,40,576]{2,1,0:T(8,128)(2,1)S(1)}, u32[]{:S(2)}, u32[]{:S(2)}) collective-permute-start(bf16[4,40,576]{2,1,0:T(8,128)(2,1)S(1)} %pad_maximum_fusion.3), channel_id=1, source_target_pairs={{0,8},{1,9},{2,10},{3,11},{4,12},{5,13},{6,14},{7,15},{8,0},{9,1},... | collective-permute-start | bytes 552968 | tf_op jit(solution)/shard_map/ppermute | solution.py:233
  24.2 10.7 %collective-permute-start.7 = (bf16[576,254]{1,0:T(8,128)(2,1)S(1)}, bf16[576,254]{1,0:T(8,128)(2,1)S(1)}, u32[]{:S(2)}, u32[]{:S(2)}) collective-permute-start(bf16[576,254]{1,0:T(8,128)(2,1)S(1)} %collective-permute-done.5.rest_1_), channel_id=1, source_target_pairs={{2,0},{3,1},{6,2},{7,3},{10,6},{11,7},{14,10},{15,11},{12,14},{13,... | collective-permute-start | bytes 877832 | tf_op jit(solution)/shard_map/ppermute | solution.py:220
  26.7 12.1 %collective-permute-start.8 = (bf16[576,254]{1,0:T(8,128)(2,1)S(1)}, bf16[576,254]{1,0:T(8,128)(2,1)S(1)}, u32[]{:S(2)}, u32[]{:S(2)}) collective-permute-start(bf16[576,254]{1,0:T(8,128)(2,1)S(1)} %collective-permute-done.6.rest_0_), channel_id=1, source_target_pairs={{2,6},{3,7},{6,10},{7,11},{10,14},{11,15},{14,12},{15,13},{12,8},{... | collective-permute-start | bytes 877832 | tf_op jit(solution)/shard_map/ppermute | solution.py:218
  34.8 5.3 %collective-permute-start.3 = (bf16[8,40,576]{2,1,0:T(8,128)(2,1)S(1)}, bf16[8,40,576]{2,1,0:T(8,128)(2,1)S(1)}, u32[]{:S(2)}, u32[]{:S(2)}) collective-permute-start(bf16[8,40,576]{2,1,0:T(8,128)(2,1)S(1)} %pad_maximum_fusion.here_ref), channel_id=1, source_target_pairs={{0,1},{1,0},{2,3},{3,2},{4,5},{5,4},{6,7},{7,6},{8,9},{9,8},{10,11... | collective-permute-start | bytes 1105928 | tf_op jit(solution)/shard_map/ppermute | solution.py:238
  34.9 14.9 %collective-permute-start.9 = (bf16[576,254]{1,0:T(8,128)(2,1)S(1)}, bf16[576,254]{1,0:T(8,128)(2,1)S(1)}, u32[]{:S(2)}, u32[]{:S(2)}) collective-permute-start(bf16[576,254]{1,0:T(8,128)(2,1)S(1)} %collective-permute-done.7.rest_1_), channel_id=1, source_target_pairs={{2,0},{3,1},{6,2},{7,3},{10,6},{11,7},{14,10},{15,11},{12,14},{13,... | collective-permute-start | bytes 877832 | tf_op jit(solution)/shard_map/ppermute | solution.py:220
  38.7 13.1 %collective-permute-start.10 = (bf16[576,254]{1,0:T(8,128)(2,1)S(1)}, bf16[576,254]{1,0:T(8,128)(2,1)S(1)}, u32[]{:S(2)}, u32[]{:S(2)}) collective-permute-start(bf16[576,254]{1,0:T(8,128)(2,1)S(1)} %collective-permute-done.8.rest_0_), channel_id=1, source_target_pairs={{2,6},{3,7},{6,10},{7,11},{10,14},{11,15},{14,12},{15,13},{12,8},{... | collective-permute-start | bytes 877832 | tf_op jit(solution)/shard_map/ppermute | solution.py:218
  39.4 0.7 copy-start.2

commit v3 on v2

v3 whole, which is shorter than its diff:
```python
import functools
import math

import jax
import jax.numpy as jnp
import numpy as np
from jax import lax
from jax.experimental import pallas as pl
from jax.experimental.pallas import tpu as pltpu
from jax.sharding import PartitionSpec as P

LATENT = 512
V_HEAD = 128
CORES = 2
LANES = 128

score_scale = 192.0 ** (-0.5) * math.log2(math.e)
neg_large = -1e30
least_max = -1e29
f32 = jnp.float32
bf16 = jnp.bfloat16


def chip_cycle(chips):
    wide = max(1, int(round(chips ** (1 / 3))))
    tall = chips // wide
    if wide * tall != chips or wide < 2 or tall < 2:
        return list(range(chips))
    walk = []
    for z in range(tall):
        across = range(1, wide) if z % 2 == 0 else range(wide - 1, 0, -1)
        walk += [z * wide + x for x in across]
    return walk + [z * wide for z in reversed(range(tall))]


def fold_shards(q_ref, shards, length, m_ref, l_ref, acc_ref):
    rows = q_ref.shape[0]
    block = min(128, rows)
    for start in range(0, rows, block):
        part = pl.ds(start, block)
        m_old = m_ref[part, :][:, :1]
        m_new = m_old
        scores = []
        for base, key_ref in shards:
            slot = base + lax.broadcasted_iota(jnp.int32, (1, key_ref.shape[1]), 1)
            s = jnp.dot(q_ref[part, :], key_ref[...], preferred_element_type=f32) * score_scale
            s = jnp.where(slot < length, s, neg_large)
            m_new = jnp.maximum(m_new, jnp.max(s, axis=1, keepdims=True))
            scores.append(s)
        shrink = jnp.exp2(m_old - m_new)
        l_new = l_ref[part, :][:, :1] * shrink
        summed = acc_ref[part, :] * shrink
        for s, (_, key_ref) in zip(scores, shards):
            probs = jnp.exp2(s - m_new)
            l_new += jnp.sum(probs, axis=1, keepdims=True)
            summed += lax.dot_general(
                probs.astype(bf16), key_ref[:LATENT, :], (((1,), (1,)), ((), ())),
                preferred_element_type=f32,
            )
        acc_ref[part, :] = summed
        m_ref[part, :] = jnp.broadcast_to(m_new, (block, LANES))
        l_ref[part, :] = jnp.broadcast_to(l_new, (block, LANES))


def parted(index, size):
    return index >> (size.bit_length() - 1), index & (size - 1)


def token_of(index, tokens, chips):
    device, t = parted(index, tokens)
    core, chip = parted(device, chips)
    return (chip * CORES + ((lax.axis_index("ctx") % CORES) ^ core)) * tokens + t


def with_base(table_ref, at, key_refs):
    me = lax.axis_index("ctx")
    count = table_ref.shape[0] // (lax.axis_size("ctx") // CORES)
    shards = []
    for j, key_ref in enumerate(key_refs):
        chip = table_ref[(me // CORES) * count + at + j]
        shards.append(((chip * CORES + me % CORES) * key_ref.shape[1], key_ref))
    return shards


def first_kernel(tokens, heads, count, length_ref, offset_ref, table_ref, here_ref, there_ref, *rest):
    keys, (q_ref, m_ref, l_ref, acc_ref, span_ref) = rest[:count], rest[count:]
    chips = here_ref.shape[0]
    rows = tokens * heads
    for core, piece_ref in enumerate((here_ref, there_ref)):
        for chip in range(chips):
            at = core * chips + chip
            q_ref[at * rows:(at + 1) * rows, :] = piece_ref[chip, :rows, :]
            if core == 0:
                span_ref[chip * tokens:(chip + 1) * tokens, :] = (
                    piece_ref[chip, rows:rows + tokens, :].astype(f32)
                )
    span = span_ref[...].astype(bf16)
    total = q_ref.shape[0]
    block = min(256, total)
    key_index = lax.broadcasted_iota(jnp.int32, (1, span.shape[0]), 1)
    key_token = token_of(key_index, tokens, chips)
    for start in range(0, total, block):
        part = pl.ds(start, block)
        s = lax.dot_general(
            q_ref[part, :], span, (((1,), (1,)), ((), ())), preferred_element_type=f32
        ) * score_scale
        row_index = start + lax.broadcasted_iota(jnp.int32, (block, 1), 0)
        row_token = token_of(row_index >> (heads.bit_length() - 1), tokens, chips)
        shown = (key_token >= offset_ref[0]) & (key_token <= row_token)
        s = jnp.where(shown, s, neg_large)
        m_new = jnp.maximum(jnp.max(s, axis=1, keepdims=True), least_max)
        probs = jnp.exp2(s - m_new)
        l_new = jnp.sum(probs, axis=1, keepdims=True)
        acc_ref[part, :] = jnp.dot(
            probs.astype(bf16), span[:, :LATENT], preferred_element_type=f32
        )
        m_ref[part, :] = jnp.broadcast_to(m_new, (block, LANES))
        l_ref[part, :] = jnp.broadcast_to(l_new, (block, LANES))
    fold_shards(q_ref, with_base(table_ref, 0, keys), length_ref[0], m_ref, l_ref, acc_ref)


def middle_kernel(at, count, length_ref, table_ref, q_ref, m_in, l_in, acc_in, *rest):
    keys, (m_ref, l_ref, acc_ref) = rest[:count], rest[count:]
    m_ref[...] = m_in[...]
    l_ref[...] = l_in[...]
    acc_ref[...] = acc_in[...]
    fold_shards(q_ref, with_base(table_ref, at, keys), length_ref[0], m_ref, l_ref, acc_ref)


def last_kernel(at, tokens, heads, length_ref, table_ref, q_ref, m_in, l_in, acc_in,
                top_ref, bottom_ref, own_up, far_up, out_ref,
                key_ref, m_ref, l_ref, acc_ref, context_ref, flat_ref):
    cut = top_ref.shape[0]
    key_ref[:cut, :] = top_ref[...]
    key_ref[cut:, :] = bottom_ref[...]
    middle_kernel(at, 1, length_ref, table_ref, q_ref, m_in, l_in, acc_in,
                  key_ref, m_ref, l_ref, acc_ref)
    for k in range(LATENT // LANES):
        lanes = slice(k * LANES, (k + 1) * LANES)
        context_ref[k] = acc_ref[:, lanes] / l_ref[...]
    m_ref[...] = m_ref[...] + jnp.log2(l_ref[...])
    everyone = flat_ref.shape[0]
    core = lax.axis_index("ctx") % CORES
    per_core = heads // CORES
    tail = jnp.zeros((everyone, LANES), f32)
    lane = lax.broadcasted_iota(jnp.int32, (everyone, LANES), 1)
    for side, up_ref in enumerate((own_up, far_up)):
        for j in range(per_core):
            head = (core ^ side) * per_core + j
            rows = pl.ds(head, everyone, stride=heads)
            context = jnp.concatenate(
                [context_ref[k, rows, :] for k in range(LATENT // LANES)], axis=1
            ).astype(bf16)
            lifted = jnp.dot(context, up_ref[j], preferred_element_type=f32)
            flat_ref[:, pl.ds(pl.multiple_of(head * V_HEAD, V_HEAD), V_HEAD)] = lifted
            weight = m_ref[rows, :]
            high = weight.astype(bf16).astype(f32)
            mid = (weight - high).astype(bf16).astype(f32)
            low = weight - high - mid
            tail = jnp.where(lane == head, high, tail)
            tail = jnp.where(lane == head + heads, mid, tail)
            tail = jnp.where(lane == head + 2 * heads, low, tail)
    flat_ref[:, heads * V_HEAD:] = tail
    chips = everyone // tokens // CORES
    for i in range(chips * CORES):
        out_ref[(i % chips) * CORES + (core ^ (i // chips))] = (
            flat_ref[i * tokens:(i + 1) * tokens, :].astype(bf16)
        )


def merge_kernel(heads, parts_ref, out_ref):
    width = heads * V_HEAD
    for chip in range(parts_ref.shape[0] // CORES):
        one = parts_ref[2 * chip].astype(f32)
        two = parts_ref[2 * chip + 1].astype(f32)
        gap = one[:, width:] - two[:, width:]
        delta = gap[:, :heads] + (gap[:, heads:2 * heads] + gap[:, 2 * heads:3 * heads])
        share = 1.0 / (1.0 + jnp.exp2(-delta))
        rest = 1.0 / (1.0 + jnp.exp2(delta))
        for j in range(heads):
            lanes = slice(j * V_HEAD, (j + 1) * V_HEAD)
            mixed = one[:, lanes] * share[:, j:j + 1] + two[:, lanes] * rest[:, j:j + 1]
            out_ref[:, chip * width + j * V_HEAD:chip * width + (j + 1) * V_HEAD] = (
                mixed.astype(bf16)
            )


VMEM = pl.BlockSpec(memory_space=pltpu.VMEM)
SMEM = pl.BlockSpec(memory_space=pltpu.SMEM)
PARAMS = pltpu.CompilerParams(vmem_limit_bytes=32 * 1024 * 1024)


def shape(*dims, dtype=f32):
    return jax.ShapeDtypeStruct(dims, dtype)


def on_device(ctx, queries, prefix_latents, span_latents, value_up, prefix_length, span_offset):
    slots, width = prefix_latents.shape
    tokens = queries.shape[0]
    all_heads = queries.shape[1] // width
    chips = ctx // CORES
    heads = all_heads // chips
    rows = tokens * heads
    total = rows * ctx
    everyone = tokens * ctx
    walk = chip_cycle(chips)
    spot = np.argsort(np.array(walk))
    steps = chips // 2

    def across(step):
        return [
            (walk[r] * CORES + c, walk[(r + step) % chips] * CORES + c)
            for r in range(chips) for c in range(CORES)
        ]

    other_core = [(d, d ^ 1) for d in range(ctx)]
    same_core = [[p * CORES + c for p in range(chips)] for c in range(CORES)]

    grouped = queries.reshape(tokens, chips, heads, width).transpose(1, 0, 2, 3)
    pad = -(rows + tokens) % 8
    span_rows = jnp.pad(span_latents, ((0, pad), (0, 0)))
    span_rows = jnp.broadcast_to(span_rows[None], (chips, tokens + pad, width))
    pieces = jnp.concatenate([grouped.reshape(chips, rows, width), span_rows], axis=1)
    here = lax.all_to_all(
        pieces, "ctx", split_axis=0, concat_axis=0, axis_index_groups=same_core, tiled=True
    )

    turns = [0]
    for s in range(1, steps):
        turns += [-s, s]
    turns.append(steps)
    owner_table = np.array(
        [[walk[(spot[p] + t) % chips] for t in turns] for p in range(chips)], np.int32
    )
    table = jnp.asarray(owner_table.reshape(-1))
    state_shapes = [shape(total, LANES), shape(total, LANES), shape(total, LATENT)]

    def fold_first(keys):
        return pl.pallas_call(
            functools.partial(first_kernel, tokens, heads, len(keys)),
            out_shape=[shape(total, width, dtype=bf16)] + state_shapes,
            in_specs=[SMEM] * 3 + [VMEM] * (2 + len(keys)),
            out_specs=[VMEM] * 4,
            scratch_shapes=[pltpu.VMEM((everyone // CORES, width), f32)],
            compiler_params=PARAMS,
            name="first",
        )(prefix_length, span_offset, table, here, there, *keys)

    def fold_more(at, q, state, keys):
        return pl.pallas_call(
            functools.partial(middle_kernel, at, len(keys)),
            out_shape=state_shapes,
            in_specs=[SMEM] * 2 + [VMEM] * (4 + len(keys)),
            out_specs=[VMEM] * 3,
            compiler_params=PARAMS,
            name="middle",
        )(prefix_length, table, q, *state, *keys)

    own = prefix_latents.T
    right = lax.ppermute(own, "ctx", across(1))
    left = lax.ppermute(own, "ctx", across(-1))
    right, left, here = lax.optimization_barrier((right, left, here))
    there = lax.ppermute(here, "ctx", other_core)
    far_up = lax.ppermute(value_up, "ctx", other_core)
    cut = LATENT // 2
    for s in range(2, steps + 1):
        onward = right if s < steps else right[:cut]
        backward = left if s < steps else left[cut:]
        onward = lax.ppermute(onward, "ctx", across(1))
        backward = lax.ppermute(backward, "ctx", across(-1))
        if s == 2:
            q, *state = fold_first([own, right, left])
        else:
            state = fold_more(2 * s - 3, q, state, [right, left])
        right, left = onward, backward
        if s < steps:
            right, left, state = lax.optimization_barrier((right, left, state))
    flat = heads * V_HEAD + LANES
    parts = pl.pallas_call(
        functools.partial(last_kernel, chips - 1, tokens, heads),
        out_shape=shape(ctx, tokens, flat, dtype=bf16),
        in_specs=[SMEM] * 2 + [VMEM] * 8,
        out_specs=VMEM,
        scratch_shapes=[
            pltpu.VMEM((width, slots), bf16),
            pltpu.VMEM((total, LANES), f32),
            pltpu.VMEM((total, LANES), f32),
            pltpu.VMEM((total, LATENT), f32),
            pltpu.VMEM((LATENT // LANES, total, LANES), f32),
            pltpu.VMEM((everyone, flat), f32),
        ],
        compiler_params=PARAMS,
        name="last",
    )(prefix_length, table, q, *state, right, left, value_up, far_up)
    returned = lax.all_to_all(parts, "ctx", split_axis=0, concat_axis=0, tiled=True)
    return pl.pallas_call(
        functools.partial(merge_kernel, heads),
        out_shape=shape(tokens, all_heads * V_HEAD, dtype=bf16),
        in_specs=[VMEM],
        out_specs=VMEM,
        compiler_params=PARAMS,
        name="merge",
    )(returned)


def solution(mesh):
    return jax.shard_map(
        functools.partial(on_device, mesh.shape["ctx"]),
        mesh=mesh,
        in_specs=(
            P(("groups", "ctx"), None),
            P(("groups", "ctx"), None),
            P(("groups", "ctx"), None),
            P("ctx", None, None),
            P("groups"),
            P("groups"),
        ),
        out_specs=P(("groups", "ctx"), None),
        check_vma=False,
    )
```

time: 69.4 us -> 68.5 us (0.987)
  waiting for transfers between devices: 17.1 us -> 22 us
  blocking collectives: 14 us -> 10.8 us
  starting transfers between devices: 19.1 us -> 17.2 us
    ppermute x10 -> x8, starting transfers between devices: 19 us -> 9.79 us  [the longest x3 4.63 us: on_device(): onward = lax.ppermute(onward, 'ctx', across(1))]
    all_to_all x0 -> x1, starting transfers between devices: none -> 7.38 us  [on_device(): lax.all_to_all(pieces, 'ctx', split_axis=0, concat_axis=0, axis_index_gro...]
    ppermute x10 -> x8, waiting for transfers between devices: 17.1 us -> 22 us  [the longest x1 11.1 us: on_device(): left = lax.ppermute(own, 'ctx', across(-1))]
    all_to_all x1, blocking collectives: 14 us -> 10.8 us  [on_device(): lax.all_to_all(parts, 'ctx', split_axis=0, concat_axis=0, tiled=True)]
    concatenate x0 -> x1, other arithmetic: none -> 0.79 us  [on_device(): jnp.concatenate([grouped.reshape(chips, rows, width), span_rows], axis=1)]
    pallas_call x5 -> x4, Pallas kernels: 13.3 us -> 12.9 us  [the longest x2 5.76 us: fold_more(): pl.pallas_call(functools.partial(middle_kernel, at, len(keys)), out_shape...]
  transfers between devices with their start and end apart: 12 -> 11, of which waited for: 5 -> 7; matrix products, arithmetic and copies ran while one was open for 0% -> 0% of each run, Pallas kernels for 17% -> 15%
where the time goes in v3:
time: 68.5 us; the launch traced here: 68.3 us
  waiting for transfers between devices  22 us (32%)
  starting transfers between devices  17.2 us (25%)
  Pallas kernels  14.8 us (22%)
  blocking collectives  10.8 us (16%)
  between operations  1.41 us (2%)
  local copies, waits for them, and re-layouts  1.38 us (2%)
  other arithmetic  0.79 us (1%)
    ppermute x1, waiting for transfers between devices, on_device(): left = lax.ppermute(own, 'ctx', across(-1))  11.1 us
    all_to_all x1, blocking collectives, on_device(): lax.all_to_all(parts, 'ctx', split_axis=0, concat_axis=0, tiled=True)  10.8 us
    all_to_all x1, starting transfers between devices, on_device(): lax.all_to_all(pieces, 'ctx', split_axis=0, concat_axis=0, axis_index_gro...  7.38 us
    ppermute x3, waiting for transfers between devices, on_device(): onward = lax.ppermute(onward, 'ctx', across(1))  6.31 us
    pallas_call x2, Pallas kernels, fold_more(): pl.pallas_call(functools.partial(middle_kernel, at, len(keys)), out_shape...  5.76 us
    ppermute x3, starting transfers between devices, on_device(): onward = lax.ppermute(onward, 'ctx', across(1))  4.63 us
    pallas_call x1, Pallas kernels, fold_first(): pl.pallas_call(functools.partial(first_kernel, tokens, heads, len(keys)),...  4.29 us
    ppermute x3, starting transfers between devices, on_device(): backward = lax.ppermute(backward, 'ctx', across(-1))  3.08 us
  transfers between devices with their start and end apart: 11, of which 7 were waited for; matrix products, arithmetic and copies ran while one was open for 0% of the time, Pallas kernels for 15%

profile of v3, /device:TPU:0, one launch (start us, length us, event | category | flops | bytes accessed | tf_op | source)
XLA Modules:
  0.0 68.3 jit_solution(13995572236950455192)
XLA Ops:
  0.0 0.0 copy-start.3
  0.0 1.3 %reshape.7 = bf16[2,8,16,576]{3,2,1,0:T(8,128)(2,1)S(1)} reshape(bf16[2,73728]{1,0:T(2,128)(2,1)} %param.7) | data formatting | bytes 589824 | tf_op jit(solution)/shard_map/reshape | solution.py:219
  1.3 0.0 copy-start
  1.3 0.0 copy-done.3
  1.4 0.8 %pad_maximum_fusion = bf16[8,40,576]{2,1,0:T(8,128)(2,1)} fusion(bf16[8,8,576]{2,1,0:T(8,128)(2,1)S(1)} %broadcast_in_dim.2, bf16[8,32,576]{2,1,0:T(8,128)(2,1)S(1)} %bitcast.7), kind=kLoop, calls=%fused_computation | loop fusion | flops 737280 | bytes 737280 | tf_op jit(solution)/shard_map/concatenate | solution.py:223
  2.2 0.0 copy-start.1
  2.2 7.4 %all-to-all-start = ((bf16[8,40,576]{2,1,0:T(8,128)(2,1)}), bf16[8,40,576]{2,1,0:T(8,128)(2,1)S(1)}, u32[]{:S(2)}, u32[]{:S(2)}) async-start(bf16[8,40,576]{2,1,0:T(8,128)(2,1)} %pad_maximum_fusion), calls=%async_computation | async-start | bytes 819200 | tf_op jit(solution)/shard_map/all_to_all | solution.py:224
  9.6 0.0 copy-done.1
  9.6 2.0 %collective-permute-start.1 = (bf16[576,254]{1,0:T(8,128)(2,1)S(1)}, bf16[576,254]{1,0:T(8,128)(2,1)S(1)}, u32[]{:S(2)}, u32[]{:S(2)}) collective-permute-start(bf16[576,254]{1,0:T(8,128)(2,1)S(1)} %bitcast.4), channel_id=1, source_target_pairs={{2,0},{3,1},{6,2},{7,3},{10,6},{11,7},{14,10},{15,11},{12,14},{13,... | collective-permute-start | bytes 877832 | tf_op jit(solution)/shard_map/ppermute | solution.py:261
  11.6 0.1 collective-permute-start
  11.7 0.0 copy-done
  11.7 0.0 collective-permute-start.9
  11.7 11.1 %collective-permute-done.1.rest_2_ = bf16[576,254]{1,0:T(8,128)(2,1)S(1)} collective-permute-done((bf16[576,254]{1,0:T(8,128)(2,1)S(1)}, bf16[576,254]{1,0:T(8,128)(2,1)S(1)}, u32[]{:S(2)}, u32[]{:S(2)}) %collective-permute-start.1) | collective-permute-done | bytes 292640 | tf_op jit(solution)/shard_map/ppermute | solution.py:261
  22.7 2.3 %collective-permute-done.rest_1_ = bf16[576,254]{1,0:T(8,128)(2,1)S(1)} collective-permute-done((bf16[576,254]{1,0:T(8,128)(2,1)S(1)}, bf16[576,254]{1,0:T(8,128)(2,1)S(1)}, u32[]{:S(2)}, u32[]{:S(2)}) %collective-permute-start) | collective-permute-done | bytes 292640 | tf_op jit(solution)/shard_map/ppermute | solution.py:260
  25.0 0.0 all-to-all-done.here_ref
  25.0 0.0 collective-permute-start.2
  25.0 1.4 %collective-permute-start.3 = (bf16[576,254]{1,0:T(8,128)(2,1)S(1)}, bf16[576,254]{1,0:T(8,128)(2,1)S(1)}, u32[]{:S(2)}, u32[]{:S(2)}) collective-permute-start(bf16[576,254]{1,0:T(8,128)(2,1)S(1)} %collective-permute-done.rest_1_), channel_id=1, source_target_pairs={{2,6},{3,7},{6,10},{7,11},{10,14},{11,15},{14,12},{15,13},{12,8},{... | collective-permute-start | bytes 877832 | tf_op jit(solution)/shard_map/ppermute | solution.py:269
  26.4 2.1 %collective-permute-start.4 = (bf16[576,254]{1,0:T(8,128)(2,1)S(1)}, bf16[576,254]{1,0:T(8,128)(2,1)S(1)}, u32[]{:S(2)}, u32[]{:S(2)}) collective-permute-start(bf16[576,254]{1,0:T(8,128)(2,1)S(1)} %collective-permute-done.1.rest_2_), channel_id=1, source_target_pairs={{2,0},{3,1},{6,2},{7,3},{10,6},{11,7},{14,10},{15,11},{12,14},{13,... | collective-permute-start | bytes 877832 | tf_op jit(solution)/shard_map/ppermute | solution.py:270
  29.2 0.0 copy-start.2
  29.9 0.0 collective-permute-done.2.there_ref
  29.9 0.0 copy-done.2
  29.9 4.3 %first.1 = (bf16[512,576]{1,0:T(8,128)(2,1)S(1)}, f32[512,128]{1,0:T(8,128)S(1)}, f32[512,128]{1,0:T(8,128)S(1)}, f32[512,512]{1,0:T(8,128)S(1)}) custom-call(s32[1]{0:T(128)S(6)} %copy.9.length_ref, s32[1]{0:T(128)S(6)} %copy.10.offset_ref, s32[64]{0:T(128)S(1)} %copy-done.2, bf16[8,40,576]{2,1,0:T(8,128)(2,1)S(1)} %all-to-all-done.here_ref, ...), custom_call_target="tpu_custom_call" | custom-call | tf_op jit(solution)/shard_map/first/pallas_call | solution.py:239
  34.2 2.0 %collective-permute-done.3.rest_0_ = bf16[576,254]{1,0:T(8,128)(2,1)S(1)} collective-permute-done((bf16[576,254]{1,0:T(8,128)(2,1)S(1)}, bf16[576,254]{1,0:T(8,128)(2,1)S(1)}, u32[]{:S(2)}, u32[]{:S(2)}) %collective-permute-start.3) | collective-permute-done | bytes 292640 | tf_op jit(solution)/shard_map/ppermute | solution.py:269
  36.2 1.2 %collective-permute-done.4.rest_1_ = bf16[576,254]{1,0:T(8,128)(2,1)S(1)} collective-permute-done((bf16[576,254]{1,0:T(8,128)(2,1)S(1)}, bf16[576,254]{1,0:T(8,128)(2,1)S(1)}, u32[]{:S(2)}, u32[]{:S(2)}) %collective-permute-start.4) | collective-permute-done | bytes 292640 | tf_op jit(solution)/shard_map/ppermute | solution.py:270
  37.4 1.7 %collective-permute-start.5 = (bf16[576,254]{1,0:T(8,128)(2,1)S(1)}, bf16[576,254]{1,0:T(8,128)(2,1)S(1)}, u32[]{:S(2)}, u32[]{:S(2)}) collective-permute-start(bf16[576,254]{1,0:T(8,128)(2,1)S(1)} %collective-permute-done.3.rest_0_), channel_id=1, source_target_pairs={{2,6},{3,7},{6,10},{7,11},{10,14},{11,15},{14,12},{15,13},{12,8},{... | collective-permute-start | bytes 877832 | tf_op jit(solution)/shard_map/ppermute | solution.py:269
  39.1 0.3 collective-permute-start.6
  39.4 2.9 %middle.2 = (f32[512,128]{1,0:T(8,128)S(1)}, f32[512,128]{1,0:T(8,128)S(1)}, f32[512,512]{1,0:T(8,128)S(1)}) custom-call(s32[1]{0:T(128)S(6)} %copy.9.length_ref, s32[64]{0:T(128)S(1)} %copy-done.2, bf16[512,576]{1,0:T(8,128)(2,1)S(1)} %get-tuple-element.31.q_ref, f32[512,128]{1,0:T(8,128)S(1)} %get-tuple-element.37.m_in, ...), custom_call_target="tpu_custom_call" | custom-call | tf_op jit(solution)/shard_map/middle/pallas_call | solution.py:250
  42.3 3.7 %collective-permute-done.5.rest_0_ = bf16[576,254]{1,0:T(8,128)(2,1)S(1)} collective-permute-done((bf16[576,254]{1,0:T(8,128)(2,1)S(1)}, bf16[576,254]{1,0:T(8,128)(2,1)S(1)}, u32[]{:S(2)}, u32[]{:S(2)}) %collective-permute-start.5) | collective-permute-done | bytes 292640 | tf_op jit(solution)/shard_map/ppermute | solution.py:269
  45.9 1.1 %collective-permute-done.6.rest_1_ = bf16[576,254]{1,0:T(8,128)(2,1)S(1)} collective-permute-done((bf16[576,254]{1,0:T(8,128)(2,1)S(1)}, bf16[576,254]{1,0:T(8,128)(2,1)S(1)}, u32[]{:S(2)}, u32[]{:S(2)}) %collective-permute-start.6) | collective-permute-done | bytes 292640 | tf_op jit(solution)/shard_map/ppermute | solution.py:270
  47.1 0.7 collective-permute-start.8
  47.8 1.5 %collective-permute-start.7 = (bf16[256,254]{1,0:T(8,128)(2,1)S(1)}, bf16[256,254]{1,0:T(8,128)(2,1)S(1)}, u32[]{:S(2)}, u32[]{:S(2)}) collective-permute-start(bf16[256,254]{1,0:T(8,128)(2,1)S(1)} %slice.6), channel_id=1, source_target_pairs={{2,6},{3,7},{6,10},{7,11},{10,14},{11,15},{14,12},{15,13},{12,8},{... | collective-permute-start | bytes 390152 | tf_op jit(solution)/shard_map/ppermute | solution.py:269
  49.2 2.9 %middle.3 = (f32[512,128]{1,0:T(8,128)S(1)}, f32[512,128]{1,0:T(8,128)S(1)}, f32[512,512]{1,0:T(8,128)S(1)}) custom-call(s32[1]{0:T(128)S(6)} %copy.9.length_ref, s32[64]{0:T(128)S(1)} %copy-done.2, bf16[512,576]{1,0:T(8,128)(2,1)S(1)} %get-tuple-element.31.q_ref, f32[512,128]{1,0:T(8,128)S(1)} %get-tuple-element.43.m_in, ...), custom_call_target="tpu_custom_call" | custom-call | tf_op jit(solution)/shard_map/middle/pallas_call | solution.py:250
  52.1 0.0 collective-permute-done.9.far_up
  52.1 0.7 collective-permute-done.7.top_ref
  52.8 0.0 collective-permute-done.8.bottom_ref
  52.8 2.9 %last.1 = bf16[16,2,2176]{2,1,0:T(2,128)(2,1)S(1)} custom-call(s32[1]{0:T(128)S(6)} %copy.9.length_ref, s32[64]{0:T(128)S(1)} %copy-done.2, bf16[512,576]{1,0:T(8,128)(2,1)S(1)} %get-tuple-element.31.q_ref, f32[512,128]{1,0:T(8,128)S(1)} %get-tuple-element.48.m_in, f32[512,128]{1,0:T(8,128)S(1)} %get-tuple-element.49.l_in, ...), custom_call_target="tpu_custom_call" | custom-call | tf_op jit(solution)/shard_map/last/pallas_call | solution.py:279
  55.7 10.8 %all_to_all.10.parts_ref = bf16[16,2,2176]{2,1,0:T(2,128)(2,1)S(1)} all-to-all(bf16[16,2,2176]{2,1,0:T(2,128)(2,1)S(1)} %last.1), channel_id=1, replica_groups=mesh['groups'=2,'ctx'=16] {'ctx'}, dimensions={0} | all-to-all | bytes 278528 | tf_op jit(solution)/shard_map/all_to_all | solution.py:295
  66.4 1.8 %merge.1 = bf16[2,16384]{1,0:T(2,128)(2,1)} custom-call(bf16[16,2,2176]{2,1,0:T(2,128)(2,1)S(1)} %all_to_all.10.parts_ref), custom_call_target="tpu_custom_call" | custom-call | tf_op jit(solution)/shard_map/merge/pallas_call | solution.py:296
  (5 shorter events, 0.1 us)
Async XLA Ops:
  0.0 1.4 %copy-start.3 = (bf16[2,576]{1,0:T(2,128)(2,1)S(1)}, bf16[2,576]{1,0:T(2,128)(2,1)}, u32[]{:S(2)}) copy-start(bf16[2,576]{1,0:T(2,128)(2,1)} %param.9) | copy-start | bytes 6916
  1.3 10.4 %copy-start = (bf16[8,512,128]{2,1,0:T(8,128)(2,1)S(1)}, bf16[8,512,128]{2,1,0:T(8,128)(2,1)}, u32[]{:S(2)}) copy-start(bf16[8,512,128]{2,1,0:T(8,128)(2,1)} %own_up.1) | copy-start | bytes 3145732
  2.2 7.4 %copy-start.1 = (bf16[254,576]{0,1:T(8,128)(2,1)S(1)}, bf16[254,576]{0,1:T(8,128)(2,1)}, u32[]{:S(2)}) copy-start(bf16[254,576]{0,1:T(8,128)(2,1)} %param.8) | copy-start | bytes 877828
  2.2 22.8 %all-to-all-start = ((bf16[8,40,576]{2,1,0:T(8,128)(2,1)}), bf16[8,40,576]{2,1,0:T(8,128)(2,1)S(1)}, u32[]{:S(2)}, u32[]{:S(2)}) async-start(bf16[8,40,576]{2,1,0:T(8,128)(2,1)} %pad_maximum_fusion), calls=%async_computation | async-start | bytes 819200 | tf_op jit(solution)/shard_map/all_to_all | solution.py:224
  9.6 13.1 %collective-permute-start.1 = (bf16[576,254]{1,0:T(8,128)(2,1)S(1)}, bf16[576,254]{1,0:T(8,128)(2,1)S(1)}, u32[]{:S(2)}, u32[]{:S(2)}) collective-permute-start(bf16[576,254]{1,0:T(8,128)(2,1)S(1)} %bitcast.4), channel_id=1, source_target_pairs={{2,0},{3,1},{6,2},{7,3},{10,6},{11,7},{14,10},{15,11},{12,14},{13,... | collective-permute-start | bytes 877832 | tf_op jit(solution)/shard_map/ppermute | solution.py:261
  11.6 13.4 %collective-permute-start = (bf16[576,254]{1,0:T(8,128)(2,1)S(1)}, bf16[576,254]{1,0:T(8,128)(2,1)S(1)}, u32[]{:S(2)}, u32[]{:S(2)}) collective-permute-start(bf16[576,254]{1,0:T(8,128)(2,1)S(1)} %bitcast.5), channel_id=1, source_target_pairs={{2,6},{3,7},{6,10},{7,11},{10,14},{11,15},{14,12},{15,13},{12,8},{... | collective-permute-start | bytes 877832 | tf_op jit(solution)/shard_map/ppermute | solution.py:260
  11.7 40.5 %collective-permute-start.9 = (bf16[8,512,128]{2,1,0:T(8,128)(2,1)S(1)}, bf16[8,512,128]{2,1,0:T(8,128)(2,1)S(1)}, u32[]{:S(2)}, u32[]{:S(2)}) collective-permute-start(bf16[8,512,128]{2,1,0:T(8,128)(2,1)S(1)} %copy-done), channel_id=1, source_target_pairs={{0,1},{1,0},{2,3},{3,2},{4,5},{5,4},{6,7},{7,6},{8,9},{9,8},{10,11... | collective-permute-start | bytes 3145736 | tf_op jit(solution)/shard_map/ppermute | solution.py:264
  25.0 4.9 %collective-permute-start.2 = (bf16[8,40,576]{2,1,0:T(8,128)(2,1)S(1)}, bf16[8,40,576]{2,1,0:T(8,128)(2,1)S(1)}, u32[]{:S(2)}, u32[]{:S(2)}) collective-permute-start(bf16[8,40,576]{2,1,0:T(8,128)(2,1)S(1)} %all-to-all-done.here_ref), channel_id=1, source_target_pairs={{0,1},{1,0},{2,3},{3,2},{4,5},{5,4},{6,7},{7,6},{8,9},{9,8},{10,11... | collective-permute-start | bytes 1105928 | tf_op jit(solution)/shard_map/ppermute | solution.py:263
  25.0 11.2 %collective-permute-start.3 = (bf16[576,254]{1,0:T(8,128)(2,1)S(1)}, bf16[576,254]{1,0:T(8,128)(2,1)S(1)}, u32[]{:S(2)}, u32[]{:S(2)}) collective-permute-start(bf16[576,254]{1,0:T(8,128)(2,1)S(1)} %collective-permute-done.rest_1_), channel_id=1, source_target_pairs={{2,6},{3,7},{6,10},{7,11},{10,14},{11,15},{14,12},{15,13},{12,8},{... | collective-permute-start | bytes 877832 | tf_op jit(solution)/shard_map/ppermute | solution.py:269
  26.4 11.0 %collective-permute-start.4 = (bf16[576,254]{1,0:T(8,128)(2,1)S(1)}, bf16[576,254]{1,0:T(8,128)(2,1)S(1)}, u32[]{:S(2)}, u32[]{:S(2)}) collective-permute-start(bf16[576,254]{1,0:T(8,128)(2,1)S(1)} %collective-permute-done.1.rest_2_), channel_id=1, source_target_pairs={{2,0},{3,1},{6,2},{7,3},{10,6},{11,7},{14,10},{15,11},{12,14},{13,... | collective-permute-start | bytes 877832 | tf_op jit(solution)/shard_map/ppermute | solution.py:270
  29.2 0.7 %copy-start.2 = (s32[64]{0:T(128)S(1)}, s32[64]{0:T(128)}, u32[]{:S(2)}) copy-start(s32[64]{0:T(128)} %constant.5.clone.table_ref) | copy-start | bytes 772
  37.4 8.6 %collective-permute-start.5 = (bf16[576,254]{1,0:T(8,128)(2,1)S(1)}, bf16[576,254]{1,0:T(8,128)(2,1)S(1)}, u32[]{:S(2)}, u32[]{:S(2)}) collective-permute-start(bf16[576,254]{1,0:T(8,128)(2,1)S(1)} %collective-permute-done.3.rest_0_), channel_id=1, source_target_pairs={{2,6},{3,7},{6,10},{7,11},{10,14},{11,15},{14,12},{15,13},{12,8},{... | collective-permute-start | bytes 877832 | tf_op jit(solution)/shard_map/ppermute | solution.py:269
  39.1 8.0 %collective-permute-start.6 = (bf16[576,254]{1,0:T(8,128)(2,1)S(1)}, bf16[576,254]{1,0:T(8,128)(2,1)S(1)}, u32[]{:S(2)}, u32[]{:S(2)}) collective-permute-start(bf16[576,254]{1,0:T(8,128)(2,1)S(1)} %collective-permute-done.4.rest_1_), channel_id=1, source_target_pairs={{2,0},{3,1},{6,2},{7,3},{10,6},{11,7},{14,10},{15,11},{12,14},{13,... | collective-permute-start | bytes 877832 | tf_op jit(solution)/shard_map/ppermute | solution.py:270
  47.1 5.7 %collective-permute-start.8 = (bf16[320,254]{1,0:T(8,128)(2,1)S(1)}, bf16[320,254]{1,0:T(8,128)(2,1)S(1)}, u32[]{:S(2)}, u32[]{:S(2)}) collective-permute-start(bf16[320,254]{1,0:T(8,128)(2,1)S(1)} %slice.7), channel_id=1, source_target_pairs={{2,0},{3,1},{6,2},{7,3},{10,6},{11,7},{14,10},{15,11},{12,14},{13,... | collective-permute-start | bytes 487688 | tf_op jit(solution)/shard_map/ppermute | solution.py:270
  47.8 5.0 %collective-permute-start.7 = (bf16[256,254]{1,0:T(8,128)(2,1)S(1)}, bf16[256,254]{1,0:T(8,128)(2,1)S(1)}, u32[]{:S(2)}, u32[]{:S(2)}) collective-permute-start(bf16[256,254]{1,0:T(8,128)(2,1)S(1)} %slice.6), channel_id=1, source_target_pairs={{2,6},{3,7},{6,10},{7,11},{10,14},{11,15},{14,12},{15,13},{12,8},{... | collective-permute-start | bytes 390152 | tf_op jit(solution)/shard_map/ppermute | solution.py:269

commit v4 on v3

--- a/solution.py
+++ b/solution.py
@@ -41,23 +41,30 @@
         m_old = m_ref[part, :][:, :1]
         m_new = m_old
         scores = []
-        for base, key_ref in shards:
-            slot = base + lax.broadcasted_iota(jnp.int32, (1, key_ref.shape[1]), 1)
-            s = jnp.dot(q_ref[part, :], key_ref[...], preferred_element_type=f32) * score_scale
-            s = jnp.where(slot < length, s, neg_large)
+        for base, (top_ref, bottom_ref) in shards:
+            cut, slots = top_ref.shape
+            slot = base + lax.broadcasted_iota(jnp.int32, (1, slots), 1)
+            s = jnp.dot(q_ref[part, :cut], top_ref[...], preferred_element_type=f32)
+            s += jnp.dot(q_ref[part, cut:], bottom_ref[...], preferred_element_type=f32)
+            s = jnp.where(slot < length, s * score_scale, neg_large)
             m_new = jnp.maximum(m_new, jnp.max(s, axis=1, keepdims=True))
             scores.append(s)
         shrink = jnp.exp2(m_old - m_new)
         l_new = l_ref[part, :][:, :1] * shrink
-        summed = acc_ref[part, :] * shrink
-        for s, (_, key_ref) in zip(scores, shards):
+        weights = []
+        for s in scores:
             probs = jnp.exp2(s - m_new)
             l_new += jnp.sum(probs, axis=1, keepdims=True)
-            summed += lax.dot_general(
-                probs.astype(bf16), key_ref[:LATENT, :], (((1,), (1,)), ((), ())),
-                preferred_element_type=f32,
-            )
-        acc_ref[part, :] = summed
+            weights.append(probs.astype(bf16))
+        cut = shards[0][1][0].shape[0]
+        for half, lanes in enumerate((slice(0, cut), slice(cut, LATENT))):
+            summed = acc_ref[part, lanes] * shrink
+            for w, (_, pair) in zip(weights, shards):
+                summed += lax.dot_general(
+                    w, pair[half][:lanes.stop - lanes.start, :], (((1,), (1,)), ((), ())),
+                    preferred_element_type=f32,
+                )
+            acc_ref[part, lanes] = summed
         m_ref[part, :] = jnp.broadcast_to(m_new, (block, LANES))
         l_ref[part, :] = jnp.broadcast_to(l_new, (block, LANES))
 
@@ -76,9 +83,9 @@
     me = lax.axis_index("ctx")
     count = table_ref.shape[0] // (lax.axis_size("ctx") // CORES)
     shards = []
-    for j, key_ref in enumerate(key_refs):
+    for j, pair in enumerate(zip(key_refs[::2], key_refs[1::2])):
         chip = table_ref[(me // CORES) * count + at + j]
-        shards.append(((chip * CORES + me % CORES) * key_ref.shape[1], key_ref))
+        shards.append(((chip * CORES + me % CORES) * pair[0].shape[1], pair))
     return shards
 
 
@@ -129,12 +136,9 @@
 
 def last_kernel(at, tokens, heads, length_ref, table_ref, q_ref, m_in, l_in, acc_in,
                 top_ref, bottom_ref, own_up, far_up, out_ref,
-                key_ref, m_ref, l_ref, acc_ref, context_ref, flat_ref):
-    cut = top_ref.shape[0]
-    key_ref[:cut, :] = top_ref[...]
-    key_ref[cut:, :] = bottom_ref[...]
-    middle_kernel(at, 1, length_ref, table_ref, q_ref, m_in, l_in, acc_in,
-                  key_ref, m_ref, l_ref, acc_ref)
+                m_ref, l_ref, acc_ref, context_ref, flat_ref):
+    middle_kernel(at, 2, length_ref, table_ref, q_ref, m_in, l_in, acc_in,
+                  top_ref, bottom_ref, m_ref, l_ref, acc_ref)
     for k in range(LATENT // LANES):
         lanes = slice(k * LANES, (k + 1) * LANES)
         context_ref[k] = acc_ref[:, lanes] / l_ref[...]
@@ -216,15 +220,6 @@
     other_core = [(d, d ^ 1) for d in range(ctx)]
     same_core = [[p * CORES + c for p in range(chips)] for c in range(CORES)]
 
-    grouped = queries.reshape(tokens, chips, heads, width).transpose(1, 0, 2, 3)
-    pad = -(rows + tokens) % 8
-    span_rows = jnp.pad(span_latents, ((0, pad), (0, 0)))
-    span_rows = jnp.broadcast_to(span_rows[None], (chips, tokens + pad, width))
-    pieces = jnp.concatenate([grouped.reshape(chips, rows, width), span_rows], axis=1)
-    here = lax.all_to_all(
-        pieces, "ctx", split_axis=0, concat_axis=0, axis_index_groups=same_core, tiled=True
-    )
-
     turns = [0]
     for s in range(1, steps):
         turns += [-s, s]
@@ -256,25 +251,41 @@
             name="middle",
         )(prefix_length, table, q, *state, *keys)
 
+    cut = LATENT // 2
+    onward = functools.partial(lax.ppermute, axis_name="ctx", perm=across(1))
+    backward = functools.partial(lax.ppermute, axis_name="ctx", perm=across(-1))
     own = prefix_latents.T
-    right = lax.ppermute(own, "ctx", across(1))
-    left = lax.ppermute(own, "ctx", across(-1))
-    right, left, here = lax.optimization_barrier((right, left, here))
+    top, bottom = own[:cut], own[cut:]
+    right = [onward(top), onward(bottom)]
+    left = [backward(top), backward(bottom)]
+
+    grouped = queries.reshape(tokens, chips, heads, width).transpose(1, 0, 2, 3)
+    pad = -(rows + tokens) % 8
+    span_rows = jnp.pad(span_latents, ((0, pad), (0, 0)))
+    span_rows = jnp.broadcast_to(span_rows[None], (chips, tokens + pad, width))
+    pieces = jnp.concatenate([grouped.reshape(chips, rows, width), span_rows], axis=1)
+    pieces, right[0], left[0] = lax.optimization_barrier((pieces, right[0], left[0]))
+    here = lax.all_to_all(
+        pieces, "ctx", split_axis=0, concat_axis=0, axis_index_groups=same_core, tiled=True
+    )
+
     there = lax.ppermute(here, "ctx", other_core)
     far_up = lax.ppermute(value_up, "ctx", other_core)
-    cut = LATENT // 2
+
+    keys, state, q = [top, bottom, *right, *left], None, None
     for s in range(2, steps + 1):
-        onward = right if s < steps else right[:cut]
-        backward = left if s < steps else left[cut:]
-        onward = lax.ppermute(onward, "ctx", across(1))
-        backward = lax.ppermute(backward, "ctx", across(-1))
-        if s == 2:
-            q, *state = fold_first([own, right, left])
+        if state is not None:
+            right[1], left[1], state = lax.optimization_barrier((right[1], left[1], state))
+        if s < steps:
+            right = [onward(right[0]), onward(right[1])]
+            left = [backward(left[0]), backward(left[1])]
         else:
-            state = fold_more(2 * s - 3, q, state, [right, left])
-        right, left = onward, backward
-        if s < steps:
-            right, left, state = lax.optimization_barrier((right, left, state))
+            right, left = [onward(right[0])], [backward(left[1])]
+        if state is None:
+            q, *state = fold_first(keys)
+        else:
+            state = fold_more(2 * s - 3, q, state, keys)
+        keys = [*right, *left]
     flat = heads * V_HEAD + LANES
     parts = pl.pallas_call(
         functools.partial(last_kernel, chips - 1, tokens, heads),
@@ -282,7 +293,6 @@
         in_specs=[SMEM] * 2 + [VMEM] * 8,
         out_specs=VMEM,
         scratch_shapes=[
-            pltpu.VMEM((width, slots), bf16),
             pltpu.VMEM((total, LANES), f32),
             pltpu.VMEM((total, LANES), f32),
             pltpu.VMEM((total, LATENT), f32),
@@ -291,7 +301,7 @@
         ],
         compiler_params=PARAMS,
         name="last",
-    )(prefix_length, table, q, *state, right, left, value_up, far_up)
+    )(prefix_length, table, q, *state, *keys, value_up, far_up)
     returned = lax.all_to_all(parts, "ctx", split_axis=0, concat_axis=0, tiled=True)
     return pl.pallas_call(
         functools.partial(merge_kernel, heads),

time: 68.5 us -> 77.2 us (1.13)
  starting transfers between devices: 17.2 us -> 21.4 us
  waiting for transfers between devices: 22 us -> 25.2 us
  local copies, waits for them, and re-layouts: 1.38 us -> 2.28 us
    all_to_all x1, waiting for transfers between devices: 0.01 us -> 10.8 us  [on_device(): lax.all_to_all(pieces, 'ctx', split_axis=0, concat_axis=0, axis_index_gro...]
    ppermute x8 -> x14, waiting for transfers between devices: 22 us -> 14.4 us  [the longest x4 7.2 us: on_device(): left = [backward(left[0]), backward(left[1])]]
    ppermute x8 -> x14, starting transfers between devices: 9.79 us -> 16.4 us  [the longest x4 4.72 us: on_device(): right = [onward(right[0]), onward(right[1])]]
    all_to_all x1, starting transfers between devices: 7.38 us -> 4.88 us  [on_device(): lax.all_to_all(pieces, 'ctx', split_axis=0, concat_axis=0, axis_index_gro...]
    slice x2, local copies, waits for them, and re-layouts: 0.02 us -> 0.92 us  [on_device(): top, bottom = (own[:cut], own[cut:])]
  transfers between devices with their start and end apart: 11 -> 17, of which waited for: 7 -> 6; matrix products, arithmetic and copies ran while one was open for 0% -> 3% of each run, Pallas kernels for 15% -> 13%
where the time goes in v4:
time: 77.2 us; the launch traced here: 76.9 us
  waiting for transfers between devices  25.2 us (33%)
  starting transfers between devices  21.4 us (28%)
  Pallas kernels  14.7 us (19%)
  blocking collectives  11.1 us (14%)
  local copies, waits for them, and re-layouts  2.28 us (3%)
  between operations  1.44 us (2%)
  other arithmetic  0.79 us (1%)
    all_to_all x1, blocking collectives, on_device(): lax.all_to_all(parts, 'ctx', split_axis=0, concat_axis=0, tiled=True)  11.1 us
    all_to_all x1, waiting for transfers between devices, on_device(): lax.all_to_all(pieces, 'ctx', split_axis=0, concat_axis=0, axis_index_gro...  10.8 us
    ppermute x4, waiting for transfers between devices, on_device(): left = [backward(left[0]), backward(left[1])]  7.2 us
    ppermute x2, waiting for transfers between devices, on_device(): right = [onward(top), onward(bottom)]  5.83 us
    pallas_call x2, Pallas kernels, fold_more(): pl.pallas_call(functools.partial(middle_kernel, at, len(keys)), out_shape...  5.68 us
    all_to_all x1, starting transfers between devices, on_device(): lax.all_to_all(pieces, 'ctx', split_axis=0, concat_axis=0, axis_index_gro...  4.88 us
    ppermute x4, starting transfers between devices, on_device(): right = [onward(right[0]), onward(right[1])]  4.72 us
    ppermute x2, starting transfers between devices, on_device(): right = [onward(top), onward(bottom)]  4.51 us
  transfers between devices with their start and end apart: 17, of which 6 were waited for; matrix products, arithmetic and copies ran while one was open for 3% of the time, Pallas kernels for 13%

profile of v4, /device:TPU:0, one launch (start us, length us, event | category | flops | bytes accessed | tf_op | source)
XLA Modules:
  0.0 76.9 jit_solution(18006179266620872317)
XLA Ops:
  0.0 0.9 %slice.8.rest_0_ = bf16[256,254]{1,0:T(8,128)(2,1)S(1)} slice(bf16[576,254]{1,0:T(8,128)(2,1)} %bitcast.5), slice={[0:256], [0:254]} | slice | bytes 260096 | tf_op jit(solution)/shard_map/slice | solution.py:258
  0.9 3.0 %collective-permute-start = (bf16[256,254]{1,0:T(8,128)(2,1)S(1)}, bf16[256,254]{1,0:T(8,128)(2,1)S(1)}, u32[]{:S(2)}, u32[]{:S(2)}) collective-permute-start(bf16[256,254]{1,0:T(8,128)(2,1)S(1)} %slice.8.rest_0_), channel_id=1, source_target_pairs={{2,6},{3,7},{6,10},{7,11},{10,14},{11,15},{14,12},{15,13},{12,8},{... | collective-permute-start | bytes 390152 | tf_op jit(solution)/shard_map/ppermute | solution.py:259
  3.9 0.2 collective-permute-start.1
  4.1 0.0 copy-start.3
  4.1 1.3 %reshape.7 = bf16[2,8,16,576]{3,2,1,0:T(8,128)(2,1)S(1)} reshape(bf16[2,73728]{1,0:T(2,128)(2,1)} %param.7) | data formatting | bytes 589824 | tf_op jit(solution)/shard_map/reshape | solution.py:262
  5.4 0.0 copy-start
  5.4 0.0 copy-done.3
  5.4 0.8 %pad_maximum_fusion = bf16[8,40,576]{2,1,0:T(8,128)(2,1)} fusion(bf16[8,8,576]{2,1,0:T(8,128)(2,1)S(1)} %broadcast_in_dim.2, bf16[8,32,576]{2,1,0:T(8,128)(2,1)S(1)} %bitcast.4), kind=kLoop, calls=%fused_computation | loop fusion | flops 737280 | bytes 737280 | tf_op jit(solution)/shard_map/concatenate | solution.py:266
  6.2 0.0 copy-start.2
  6.2 1.2 %collective-permute-done.rest_2_ = bf16[256,254]{1,0:T(8,128)(2,1)S(1)} collective-permute-done((bf16[256,254]{1,0:T(8,128)(2,1)S(1)}, bf16[256,254]{1,0:T(8,128)(2,1)S(1)}, u32[]{:S(2)}, u32[]{:S(2)}) %collective-permute-start) | collective-permute-done | bytes 130080 | tf_op jit(solution)/shard_map/ppermute | solution.py:259
  7.5 1.4 %collective-permute-done.1.rest_4_ = bf16[256,254]{1,0:T(8,128)(2,1)S(1)} collective-permute-done((bf16[256,254]{1,0:T(8,128)(2,1)S(1)}, bf16[256,254]{1,0:T(8,128)(2,1)S(1)}, u32[]{:S(2)}, u32[]{:S(2)}) %collective-permute-start.1) | collective-permute-done | bytes 130080 | tf_op jit(solution)/shard_map/ppermute | solution.py:260
  8.9 4.9 %all-to-all-start = ((bf16[8,40,576]{2,1,0:T(8,128)(2,1)}), bf16[8,40,576]{2,1,0:T(8,128)(2,1)S(1)}, u32[]{:S(2)}, u32[]{:S(2)}) async-start(bf16[8,40,576]{2,1,0:T(8,128)(2,1)} %pad_maximum_fusion), calls=%async_computation | async-start | bytes 819200 | tf_op jit(solution)/shard_map/all_to_all | solution.py:268
  13.8 0.0 copy-done
  13.8 0.1 collective-permute-start.15
  13.8 10.8 %all-to-all-done.here_ref = bf16[8,40,576]{2,1,0:T(8,128)(2,1)S(1)} async-done(((bf16[8,40,576]{2,1,0:T(8,128)(2,1)}), bf16[8,40,576]{2,1,0:T(8,128)(2,1)S(1)}, u32[]{:S(2)}, u32[]{:S(2)}) %all-to-all-start) | async-done | bytes 368672 | tf_op jit(solution)/shard_map/all_to_all | solution.py:268
  24.6 0.0 collective-permute-start.2
  24.7 0.0 copy-done.2
  24.7 1.5 %collective-permute-start.3 = (bf16[320,254]{1,0:T(8,128)(2,1)S(1)}, bf16[320,254]{1,0:T(8,128)(2,1)S(1)}, u32[]{:S(2)}, u32[]{:S(2)}) collective-permute-start(bf16[320,254]{1,0:T(8,128)(2,1)S(1)} %slice.9.rest_1_), channel_id=1, source_target_pairs={{2,6},{3,7},{6,10},{7,11},{10,14},{11,15},{14,12},{15,13},{12,8},{... | collective-permute-start | bytes 487688 | tf_op jit(solution)/shard_map/ppermute | solution.py:259
  26.2 0.6 collective-permute-start.4
  26.8 4.6 %collective-permute-done.3.rest_3_ = bf16[320,254]{1,0:T(8,128)(2,1)S(1)} collective-permute-done((bf16[320,254]{1,0:T(8,128)(2,1)S(1)}, bf16[320,254]{1,0:T(8,128)(2,1)S(1)}, u32[]{:S(2)}, u32[]{:S(2)}) %collective-permute-start.3) | collective-permute-done | bytes 162592 | tf_op jit(solution)/shard_map/ppermute | solution.py:259
  31.3 1.5 %collective-permute-start.5 = (bf16[320,254]{1,0:T(8,128)(2,1)S(1)}, bf16[320,254]{1,0:T(8,128)(2,1)S(1)}, u32[]{:S(2)}, u32[]{:S(2)}) collective-permute-start(bf16[320,254]{1,0:T(8,128)(2,1)S(1)} %collective-permute-done.3.rest_3_), channel_id=1, source_target_pairs={{2,6},{3,7},{6,10},{7,11},{10,14},{11,15},{14,12},{15,13},{12,8},{... | collective-permute-start | bytes 487688 | tf_op jit(solution)/shard_map/ppermute | solution.py:280
  32.8 0.0 collective-permute-done.4.rest_5_
  32.8 0.6 collective-permute-start.6
  33.4 1.5 %collective-permute-start.9 = (bf16[256,254]{1,0:T(8,128)(2,1)S(1)}, bf16[256,254]{1,0:T(8,128)(2,1)S(1)}, u32[]{:S(2)}, u32[]{:S(2)}) collective-permute-start(bf16[256,254]{1,0:T(8,128)(2,1)S(1)} %collective-permute-done.rest_2_), channel_id=1, source_target_pairs={{2,6},{3,7},{6,10},{7,11},{10,14},{11,15},{14,12},{15,13},{12,8},{... | collective-permute-start | bytes 390152 | tf_op jit(solution)/shard_map/ppermute | solution.py:280
  35.5 0.0 copy-start.1
  36.2 0.0 collective-permute-done.2.there_ref
  36.2 0.0 copy-done.1
  36.2 4.3 %first.1 = (bf16[512,576]{1,0:T(8,128)(2,1)S(1)}, f32[512,128]{1,0:T(8,128)S(1)}, f32[512,128]{1,0:T(8,128)S(1)}, f32[512,512]{1,0:T(8,128)S(1)}) custom-call(s32[1]{0:T(128)S(6)} %copy.9.length_ref, s32[1]{0:T(128)S(6)} %copy.10.offset_ref, s32[64]{0:T(128)S(1)} %copy-done.1, bf16[8,40,576]{2,1,0:T(8,128)(2,1)S(1)} %all-to-all-done.here_ref, ...), custom_call_target="tpu_custom_call" | custom-call | tf_op jit(solution)/shard_map/first/pallas_call | solution.py:234
  40.5 0.0 collective-permute-done.5.rest_1_
  40.5 0.0 collective-permute-done.6.rest_3_
  40.5 0.3 collective-permute-start.7
  40.8 1.7 %collective-permute-start.8 = (bf16[320,254]{1,0:T(8,128)(2,1)S(1)}, bf16[320,254]{1,0:T(8,128)(2,1)S(1)}, u32[]{:S(2)}, u32[]{:S(2)}) collective-permute-start(bf16[320,254]{1,0:T(8,128)(2,1)S(1)} %collective-permute-done.6.rest_3_), channel_id=1, source_target_pairs={{2,0},{3,1},{6,2},{7,3},{10,6},{11,7},{14,10},{15,11},{12,14},{13,... | collective-permute-start | bytes 487688 | tf_op jit(solution)/shard_map/ppermute | solution.py:281
  42.6 0.6 collective-permute-start.10
  43.1 0.0 collective-permute-done.9.rest_0_
  43.1 1.5 %collective-permute-start.11 = (bf16[256,254]{1,0:T(8,128)(2,1)S(1)}, bf16[256,254]{1,0:T(8,128)(2,1)S(1)}, u32[]{:S(2)}, u32[]{:S(2)}) collective-permute-start(bf16[256,254]{1,0:T(8,128)(2,1)S(1)} %collective-permute-done.9.rest_0_), channel_id=1, source_target_pairs={{2,6},{3,7},{6,10},{7,11},{10,14},{11,15},{14,12},{15,13},{12,8},{... | collective-permute-start | bytes 390152 | tf_op jit(solution)/shard_map/ppermute | solution.py:280
  44.6 4.0 %collective-permute-done.10.rest_2_ = bf16[256,254]{1,0:T(8,128)(2,1)S(1)} collective-permute-done((bf16[256,254]{1,0:T(8,128)(2,1)S(1)}, bf16[256,254]{1,0:T(8,128)(2,1)S(1)}, u32[]{:S(2)}, u32[]{:S(2)}) %collective-permute-start.10) | collective-permute-done | bytes 130080 | tf_op jit(solution)/shard_map/ppermute | solution.py:281
  48.6 2.9 %middle.2 = (f32[512,128]{1,0:T(8,128)S(1)}, f32[512,128]{1,0:T(8,128)S(1)}, f32[512,512]{1,0:T(8,128)S(1)}) custom-call(s32[1]{0:T(128)S(6)} %copy.9.length_ref, s32[64]{0:T(128)S(1)} %copy-done.1, bf16[512,576]{1,0:T(8,128)(2,1)S(1)} %get-tuple-element.30.q_ref, f32[512,128]{1,0:T(8,128)S(1)} %get-tuple-element.36.m_in, ...), custom_call_target="tpu_custom_call" | custom-call | tf_op jit(solution)/shard_map/middle/pallas_call | solution.py:245
  51.4 0.0 collective-permute-done.7.rest_1_
  51.4 0.0 collective-permute-done.8.rest_3_
  51.4 1.6 %collective-permute-start.14 = (bf16[320,254]{1,0:T(8,128)(2,1)S(1)}, bf16[320,254]{1,0:T(8,128)(2,1)S(1)}, u32[]{:S(2)}, u32[]{:S(2)}) collective-permute-start(bf16[320,254]{1,0:T(8,128)(2,1)S(1)} %collective-permute-done.8.rest_3_), channel_id=1, source_target_pairs={{2,0},{3,1},{6,2},{7,3},{10,6},{11,7},{14,10},{15,11},{12,14},{13,... | collective-permute-start | bytes 487688 | tf_op jit(solution)/shard_map/ppermute | solution.py:283
  53.0 0.6 collective-permute-start.12
  53.6 0.0 collective-permute-done.11.rest_0_
  53.6 1.5 %collective-permute-start.13 = (bf16[256,254]{1,0:T(8,128)(2,1)S(1)}, bf16[256,254]{1,0:T(8,128)(2,1)S(1)}, u32[]{:S(2)}, u32[]{:S(2)}) collective-permute-start(bf16[256,254]{1,0:T(8,128)(2,1)S(1)} %collective-permute-done.11.rest_0_), channel_id=1, source_target_pairs={{2,6},{3,7},{6,10},{7,11},{10,14},{11,15},{14,12},{15,13},{12,8},{... | collective-permute-start | bytes 390152 | tf_op jit(solution)/shard_map/ppermute | solution.py:283
  55.0 3.2 %collective-permute-done.12.rest_2_ = bf16[256,254]{1,0:T(8,128)(2,1)S(1)} collective-permute-done((bf16[256,254]{1,0:T(8,128)(2,1)S(1)}, bf16[256,254]{1,0:T(8,128)(2,1)S(1)}, u32[]{:S(2)}, u32[]{:S(2)}) %collective-permute-start.12) | collective-permute-done | bytes 130080 | tf_op jit(solution)/shard_map/ppermute | solution.py:281
  58.3 2.8 %middle.3 = (f32[512,128]{1,0:T(8,128)S(1)}, f32[512,128]{1,0:T(8,128)S(1)}, f32[512,512]{1,0:T(8,128)S(1)}) custom-call(s32[1]{0:T(128)S(6)} %copy.9.length_ref, s32[64]{0:T(128)S(1)} %copy-done.1, bf16[512,576]{1,0:T(8,128)(2,1)S(1)} %get-tuple-element.30.q_ref, f32[512,128]{1,0:T(8,128)S(1)} %get-tuple-element.42.m_in, ...), custom_call_target="tpu_custom_call" | custom-call | tf_op jit(solution)/shard_map/middle/pallas_call | solution.py:245
  61.1 0.0 collective-permute-done.13.top_ref
  61.1 0.0 collective-permute-done.15.far_up
  61.1 0.0 collective-permute-done.14.bottom_ref
  61.1 2.9 %last.1 = bf16[16,2,2176]{2,1,0:T(2,128)(2,1)S(1)} custom-call(s32[1]{0:T(128)S(6)} %copy.9.length_ref, s32[64]{0:T(128)S(1)} %copy-done.1, bf16[512,576]{1,0:T(8,128)(2,1)S(1)} %get-tuple-element.30.q_ref, f32[512,128]{1,0:T(8,128)S(1)} %get-tuple-element.45.m_in, f32[512,128]{1,0:T(8,128)S(1)} %get-tuple-element.46.l_in, ...), custom_call_target="tpu_custom_call" | custom-call | tf_op jit(solution)/shard_map/last/pallas_call | solution.py:290
  64.0 11.1 %all_to_all.10.parts_ref = bf16[16,2,2176]{2,1,0:T(2,128)(2,1)S(1)} all-to-all(bf16[16,2,2176]{2,1,0:T(2,128)(2,1)S(1)} %last.1), channel_id=1, replica_groups=mesh['groups'=2,'ctx'=16] {'ctx'}, dimensions={0} | all-to-all | bytes 278528 | tf_op jit(solution)/shard_map/all_to_all | solution.py:305
  75.1 1.8 %merge.1 = bf16[2,16384]{1,0:T(2,128)(2,1)} custom-call(bf16[16,2,2176]{2,1,0:T(2,128)(2,1)S(1)} %all_to_all.10.parts_ref), custom_call_target="tpu_custom_call" | custom-call | tf_op jit(solution)/shard_map/merge/pallas_call | solution.py:306
  (4 shorter events, 0.1 us)
Async XLA Ops:
  0.9 6.6 %collective-permute-start = (bf16[256,254]{1,0:T(8,128)(2,1)S(1)}, bf16[256,254]{1,0:T(8,128)(2,1)S(1)}, u32[]{:S(2)}, u32[]{:S(2)}) collective-permute-start(bf16[256,254]{1,0:T(8,128)(2,1)S(1)} %slice.8.rest_0_), channel_id=1, source_target_pairs={{2,6},{3,7},{6,10},{7,11},{10,14},{11,15},{14,12},{15,13},{12,8},{... | collective-permute-start | bytes 390152 | tf_op jit(solution)/shard_map/ppermute | solution.py:259
  3.9 5.0 %collective-permute-start.1 = (bf16[256,254]{1,0:T(8,128)(2,1)S(1)}, bf16[256,254]{1,0:T(8,128)(2,1)S(1)}, u32[]{:S(2)}, u32[]{:S(2)}) collective-permute-start(bf16[256,254]{1,0:T(8,128)(2,1)S(1)} %slice.8.rest_0_), channel_id=1, source_target_pairs={{2,0},{3,1},{6,2},{7,3},{10,6},{11,7},{14,10},{15,11},{12,14},{13,... | collective-permute-start | bytes 390152 | tf_op jit(solution)/shard_map/ppermute | solution.py:260
  4.1 1.4 %copy-start.3 = (bf16[2,576]{1,0:T(2,128)(2,1)S(1)}, bf16[2,576]{1,0:T(2,128)(2,1)}, u32[]{:S(2)}) copy-start(bf16[2,576]{1,0:T(2,128)(2,1)} %param.9) | copy-start | bytes 6916
  5.4 8.4 %copy-start = (bf16[8,512,128]{2,1,0:T(8,128)(2,1)S(1)}, bf16[8,512,128]{2,1,0:T(8,128)(2,1)}, u32[]{:S(2)}) copy-start(bf16[8,512,128]{2,1,0:T(8,128)(2,1)} %own_up.1) | copy-start | bytes 3145732
  6.2 18.4 %copy-start.2 = (bf16[254,576]{0,1:T(8,128)(2,1)S(1)}, bf16[254,576]{0,1:T(8,128)(2,1)}, u32[]{:S(2)}) copy-start(bf16[254,576]{0,1:T(8,128)(2,1)} %param.8) | copy-start | bytes 877828
  8.9 15.8 %all-to-all-start = ((bf16[8,40,576]{2,1,0:T(8,128)(2,1)}), bf16[8,40,576]{2,1,0:T(8,128)(2,1)S(1)}, u32[]{:S(2)}, u32[]{:S(2)}) async-start(bf16[8,40,576]{2,1,0:T(8,128)(2,1)} %pad_maximum_fusion), calls=%async_computation | async-start | bytes 819200 | tf_op jit(solution)/shard_map/all_to_all | solution.py:268
  13.8 47.4 %collective-permute-start.15 = (bf16[8,512,128]{2,1,0:T(8,128)(2,1)S(1)}, bf16[8,512,128]{2,1,0:T(8,128)(2,1)S(1)}, u32[]{:S(2)}, u32[]{:S(2)}) collective-permute-start(bf16[8,512,128]{2,1,0:T(8,128)(2,1)S(1)} %copy-done), channel_id=1, source_target_pairs={{0,1},{1,0},{2,3},{3,2},{4,5},{5,4},{6,7},{7,6},{8,9},{9,8},{10,11... | collective-permute-start | bytes 3145736 | tf_op jit(solution)/shard_map/ppermute | solution.py:273
  24.6 11.5 %collective-permute-start.2 = (bf16[8,40,576]{2,1,0:T(8,128)(2,1)S(1)}, bf16[8,40,576]{2,1,0:T(8,128)(2,1)S(1)}, u32[]{:S(2)}, u32[]{:S(2)}) collective-permute-start(bf16[8,40,576]{2,1,0:T(8,128)(2,1)S(1)} %all-to-all-done.here_ref), channel_id=1, source_target_pairs={{0,1},{1,0},{2,3},{3,2},{4,5},{5,4},{6,7},{7,6},{8,9},{9,8},{10,11... | collective-permute-start | bytes 1105928 | tf_op jit(solution)/shard_map/ppermute | solution.py:272
  24.7 6.7 %collective-permute-start.3 = (bf16[320,254]{1,0:T(8,128)(2,1)S(1)}, bf16[320,254]{1,0:T(8,128)(2,1)S(1)}, u32[]{:S(2)}, u32[]{:S(2)}) collective-permute-start(bf16[320,254]{1,0:T(8,128)(2,1)S(1)} %slice.9.rest_1_), channel_id=1, source_target_pairs={{2,6},{3,7},{6,10},{7,11},{10,14},{11,15},{14,12},{15,13},{12,8},{... | collective-permute-start | bytes 487688 | tf_op jit(solution)/shard_map/ppermute | solution.py:259
  26.2 6.6 %collective-permute-start.4 = (bf16[320,254]{1,0:T(8,128)(2,1)S(1)}, bf16[320,254]{1,0:T(8,128)(2,1)S(1)}, u32[]{:S(2)}, u32[]{:S(2)}) collective-permute-start(bf16[320,254]{1,0:T(8,128)(2,1)S(1)} %slice.9.rest_1_), channel_id=1, source_target_pairs={{2,0},{3,1},{6,2},{7,3},{10,6},{11,7},{14,10},{15,11},{12,14},{13,... | collective-permute-start | bytes 487688 | tf_op jit(solution)/shard_map/ppermute | solution.py:260
  31.3 9.2 %collective-permute-start.5 = (bf16[320,254]{1,0:T(8,128)(2,1)S(1)}, bf16[320,254]{1,0:T(8,128)(2,1)S(1)}, u32[]{:S(2)}, u32[]{:S(2)}) collective-permute-start(bf16[320,254]{1,0:T(8,128)(2,1)S(1)} %collective-permute-done.3.rest_3_), channel_id=1, source_target_pairs={{2,6},{3,7},{6,10},{7,11},{10,14},{11,15},{14,12},{15,13},{12,8},{... | collective-permute-start | bytes 487688 | tf_op jit(solution)/shard_map/ppermute | solution.py:280
  32.8 7.7 %collective-permute-start.6 = (bf16[320,254]{1,0:T(8,128)(2,1)S(1)}, bf16[320,254]{1,0:T(8,128)(2,1)S(1)}, u32[]{:S(2)}, u32[]{:S(2)}) collective-permute-start(bf16[320,254]{1,0:T(8,128)(2,1)S(1)} %collective-permute-done.4.rest_5_), channel_id=1, source_target_pairs={{2,0},{3,1},{6,2},{7,3},{10,6},{11,7},{14,10},{15,11},{12,14},{13,... | collective-permute-start | bytes 487688 | tf_op jit(solution)/shard_map/ppermute | solution.py:281
  33.4 9.8 %collective-permute-start.9 = (bf16[256,254]{1,0:T(8,128)(2,1)S(1)}, bf16[256,254]{1,0:T(8,128)(2,1)S(1)}, u32[]{:S(2)}, u32[]{:S(2)}) collective-permute-start(bf16[256,254]{1,0:T(8,128)(2,1)S(1)} %collective-permute-done.rest_2_), channel_id=1, source_target_pairs={{2,6},{3,7},{6,10},{7,11},{10,14},{11,15},{14,12},{15,13},{12,8},{... | collective-permute-start | bytes 390152 | tf_op jit(solution)/shard_map/ppermute | solution.py:280
  35.5 0.7 copy-start.1
  40.5 10.9 %collective-permute-start.7 = (bf16[320,254]{1,0:T(8,128)(2,1)S(1)}, bf16[320,254]{1,0:T(8,128)(2,1)S(1)}, u32[]{:S(2)}, u32[]{:S(2)}) collective-permute-start(bf16[320,254]{1,0:T(8,128)(2,1)S(1)} %collective-permute-done.5.rest_1_), channel_id=1, source_target_pairs={{2,6},{3,7},{6,10},{7,11},{10,14},{11,15},{14,12},{15,13},{12,8},{... | collective-permute-start | bytes 487688 | tf_op jit(solution)/shard_map/ppermute | solution.py:280
  40.8 10.6 %collective-permute-start.8 = (bf16[320,254]{1,0:T(8,128)(2,1)S(1)}, bf16[320,254]{1,0:T(8,128)(2,1)S(1)}, u32[]{:S(2)}, u32[]{:S(2)}) collective-permute-start(bf16[320,254]{1,0:T(8,128)(2,1)S(1)} %collective-permute-done.6.rest_3_), channel_id=1, source_target_pairs={{2,0},{3,1},{6,2},{7,3},{10,6},{11,7},{14,10},{15,11},{12,14},{13,... | collective-permute-start | bytes 487688 | tf_op jit(solution)/shard_map/ppermute | solution.py:281
  42.6 6.0 %collective-permute-start.10 = (bf16[256,254]{1,0:T(8,128)(2,1)S(1)}, bf16[256,254]{1,0:T(8,128)(2,1)S(1)}, u32[]{:S(2)}, u32[]{:S(2)}) collective-permute-start(bf16[256,254]{1,0:T(8,128)(2,1)S(1)} %collective-permute-done.1.rest_4_), channel_id=1, source_target_pairs={{2,0},{3,1},{6,2},{7,3},{10,6},{11,7},{14,10},{15,11},{12,14},{13,... | collective-permute-start | bytes 390152 | tf_op jit(solution)/shard_map/ppermute | solution.py:281
  43.1 10.4 %collective-permute-start.11 = (bf16[256,254]{1,0:T(8,128)(2,1)S(1)}, bf16[256,254]{1,0:T(8,128)(2,1)S(1)}, u32[]{:S(2)}, u32[]{:S(2)}) collective-permute-start(bf16[256,254]{1,0:T(8,128)(2,1)S(1)} %collective-permute-done.9.rest_0_), channel_id=1, source_target_pairs={{2,6},{3,7},{6,10},{7,11},{10,14},{11,15},{14,12},{15,13},{12,8},{... | collective-permute-start | bytes 390152 | tf_op jit(solution)/shard_map/ppermute | solution.py:280
  51.4 9.7 %collective-permute-start.14 = (bf16[320,254]{1,0:T(8,128)(2,1)S(1)}, bf16[320,254]{1,0:T(8,128)(2,1)S(1)}, u32[]{:S(2)}, u32[]{:S(2)}) collective-permute-start(bf16[320,254]{1,0:T(8,128)(2,1)S(1)} %collective-permute-done.8.rest_3_), channel_id=1, source_target_pairs={{2,0},{3,1},{6,2},{7,3},{10,6},{11,7},{14,10},{15,11},{12,14},{13,... | collective-permute-start | bytes 487688 | tf_op jit(solution)/shard_map/ppermute | solution.py:283
  53.0 5.3 %collective-permute-start.12 = (bf16[256,254]{1,0:T(8,128)(2,1)S(1)}, bf16[256,254]{1,0:T(8,128)(2,1)S(1)}, u32[]{:S(2)}, u32[]{:S(2)}) collective-permute-start(bf16[256,254]{1,0:T(8,128)(2,1)S(1)} %collective-permute-done.10.rest_2_), channel_id=1, source_target_pairs={{2,0},{3,1},{6,2},{7,3},{10,6},{11,7},{14,10},{15,11},{12,14},{13,... | collective-permute-start | bytes 390152 | tf_op jit(solution)/shard_map/ppermute | solution.py:281
  53.6 7.5 %collective-permute-start.13 = (bf16[256,254]{1,0:T(8,128)(2,1)S(1)}, bf16[256,254]{1,0:T(8,128)(2,1)S(1)}, u32[]{:S(2)}, u32[]{:S(2)}) collective-permute-start(bf16[256,254]{1,0:T(8,128)(2,1)S(1)} %collective-permute-done.11.rest_0_), channel_id=1, source_target_pairs={{2,6},{3,7},{6,10},{7,11},{10,14},{11,15},{14,12},{15,13},{12,8},{... | collective-permute-start | bytes 390152 | tf_op jit(solution)/shard_map/ppermute | solution.py:283

commit v5 on v3

--- a/solution.py
+++ b/solution.py
@@ -33,12 +33,12 @@
     return walk + [z * wide for z in reversed(range(tall))]
 
 
-def fold_shards(q_ref, shards, length, m_ref, l_ref, acc_ref):
+def fold_shards(q_ref, shards, length, old, new):
     rows = q_ref.shape[0]
-    block = min(128, rows)
+    block = min(256, rows)
     for start in range(0, rows, block):
         part = pl.ds(start, block)
-        m_old = m_ref[part, :][:, :1]
+        m_old = old[0][part, :][:, :1]
         m_new = m_old
         scores = []
         for base, key_ref in shards:
@@ -48,8 +48,8 @@
             m_new = jnp.maximum(m_new, jnp.max(s, axis=1, keepdims=True))
             scores.append(s)
         shrink = jnp.exp2(m_old - m_new)
-        l_new = l_ref[part, :][:, :1] * shrink
-        summed = acc_ref[part, :] * shrink
+        l_new = old[1][part, :][:, :1] * shrink
+        summed = old[2][part, :] * shrink
         for s, (_, key_ref) in zip(scores, shards):
             probs = jnp.exp2(s - m_new)
             l_new += jnp.sum(probs, axis=1, keepdims=True)
@@ -57,9 +57,9 @@
                 probs.astype(bf16), key_ref[:LATENT, :], (((1,), (1,)), ((), ())),
                 preferred_element_type=f32,
             )
-        acc_ref[part, :] = summed
-        m_ref[part, :] = jnp.broadcast_to(m_new, (block, LANES))
-        l_ref[part, :] = jnp.broadcast_to(l_new, (block, LANES))
+        new[0][part, :] = jnp.broadcast_to(m_new, (block, LANES))
+        new[1][part, :] = jnp.broadcast_to(l_new, (block, LANES))
+        new[2][part, :] = summed
 
 
 def parted(index, size):
@@ -116,15 +116,13 @@
         )
         m_ref[part, :] = jnp.broadcast_to(m_new, (block, LANES))
         l_ref[part, :] = jnp.broadcast_to(l_new, (block, LANES))
-    fold_shards(q_ref, with_base(table_ref, 0, keys), length_ref[0], m_ref, l_ref, acc_ref)
+    state = (m_ref, l_ref, acc_ref)
+    fold_shards(q_ref, with_base(table_ref, 0, keys), length_ref[0], state, state)
 
 
 def middle_kernel(at, count, length_ref, table_ref, q_ref, m_in, l_in, acc_in, *rest):
-    keys, (m_ref, l_ref, acc_ref) = rest[:count], rest[count:]
-    m_ref[...] = m_in[...]
-    l_ref[...] = l_in[...]
-    acc_ref[...] = acc_in[...]
-    fold_shards(q_ref, with_base(table_ref, at, keys), length_ref[0], m_ref, l_ref, acc_ref)
+    keys, new = rest[:count], rest[count:]
+    fold_shards(q_ref, with_base(table_ref, at, keys), length_ref[0], (m_in, l_in, acc_in), new)
 
 
 def last_kernel(at, tokens, heads, length_ref, table_ref, q_ref, m_in, l_in, acc_in,
@@ -144,22 +142,33 @@
     per_core = heads // CORES
     tail = jnp.zeros((everyone, LANES), f32)
     lane = lax.broadcasted_iota(jnp.int32, (everyone, LANES), 1)
+    pair = min(2, per_core)
     for side, up_ref in enumerate((own_up, far_up)):
-        for j in range(per_core):
-            head = (core ^ side) * per_core + j
-            rows = pl.ds(head, everyone, stride=heads)
-            context = jnp.concatenate(
-                [context_ref[k, rows, :] for k in range(LATENT // LANES)], axis=1
-            ).astype(bf16)
-            lifted = jnp.dot(context, up_ref[j], preferred_element_type=f32)
-            flat_ref[:, pl.ds(pl.multiple_of(head * V_HEAD, V_HEAD), V_HEAD)] = lifted
-            weight = m_ref[rows, :]
-            high = weight.astype(bf16).astype(f32)
-            mid = (weight - high).astype(bf16).astype(f32)
-            low = weight - high - mid
-            tail = jnp.where(lane == head, high, tail)
-            tail = jnp.where(lane == head + heads, mid, tail)
-            tail = jnp.where(lane == head + 2 * heads, low, tail)
+        for j in range(0, per_core, pair):
+            first_head = (core ^ side) * per_core + j
+            contexts = []
+            for head in [first_head + i for i in range(pair)]:
+                rows = pl.ds(head, everyone, stride=heads)
+                contexts.append(jnp.concatenate(
+                    [context_ref[k, rows, :] for k in range(LATENT // LANES)], axis=1
+                ).astype(bf16))
+                weight = m_ref[rows, :]
+                high = weight.astype(bf16).astype(f32)
+                mid = (weight - high).astype(bf16).astype(f32)
+                low = weight - high - mid
+                tail = jnp.where(lane == head, high, tail)
+                tail = jnp.where(lane == head + heads, mid, tail)
+                tail = jnp.where(lane == head + 2 * heads, low, tail)
+            lifted = jnp.dot(
+                jnp.concatenate(contexts, axis=0),
+                jnp.concatenate([up_ref[j + i] for i in range(pair)], axis=1),
+                preferred_element_type=f32,
+            )
+            for i in range(pair):
+                lanes = pl.ds(pl.multiple_of((first_head + i) * V_HEAD, V_HEAD), V_HEAD)
+                flat_ref[:, lanes] = lifted[
+                    i * everyone:(i + 1) * everyone, i * V_HEAD:(i + 1) * V_HEAD
+                ]
     flat_ref[:, heads * V_HEAD:] = tail
     chips = everyone // tokens // CORES
     for i in range(chips * CORES):
@@ -216,15 +225,6 @@
     other_core = [(d, d ^ 1) for d in range(ctx)]
     same_core = [[p * CORES + c for p in range(chips)] for c in range(CORES)]
 
-    grouped = queries.reshape(tokens, chips, heads, width).transpose(1, 0, 2, 3)
-    pad = -(rows + tokens) % 8
-    span_rows = jnp.pad(span_latents, ((0, pad), (0, 0)))
-    span_rows = jnp.broadcast_to(span_rows[None], (chips, tokens + pad, width))
-    pieces = jnp.concatenate([grouped.reshape(chips, rows, width), span_rows], axis=1)
-    here = lax.all_to_all(
-        pieces, "ctx", split_axis=0, concat_axis=0, axis_index_groups=same_core, tiled=True
-    )
-
     turns = [0]
     for s in range(1, steps):
         turns += [-s, s]
@@ -256,25 +256,41 @@
             name="middle",
         )(prefix_length, table, q, *state, *keys)
 
+    onward = functools.partial(lax.ppermute, axis_name="ctx", perm=across(1))
+    backward = functools.partial(lax.ppermute, axis_name="ctx", perm=across(-1))
+    cut = LATENT // 2
     own = prefix_latents.T
-    right = lax.ppermute(own, "ctx", across(1))
-    left = lax.ppermute(own, "ctx", across(-1))
-    right, left, here = lax.optimization_barrier((right, left, here))
+    right, left = onward(own), backward(own)
+
+    grouped = queries.reshape(tokens, chips, heads, width).transpose(1, 0, 2, 3)
+    pad = -(rows + tokens) % 8
+    span_rows = jnp.pad(span_latents, ((0, pad), (0, 0)))
+    span_rows = jnp.broadcast_to(span_rows[None], (chips, tokens + pad, width))
+    pieces = jnp.concatenate([grouped.reshape(chips, rows, width), span_rows], axis=1)
+    pieces, right, left = lax.optimization_barrier((pieces, right, left))
+    here = lax.all_to_all(
+        pieces, "ctx", split_axis=0, concat_axis=0, axis_index_groups=same_core, tiled=True
+    )
+
     there = lax.ppermute(here, "ctx", other_core)
     far_up = lax.ppermute(value_up, "ctx", other_core)
-    cut = LATENT // 2
-    for s in range(2, steps + 1):
-        onward = right if s < steps else right[:cut]
-        backward = left if s < steps else left[cut:]
-        onward = lax.ppermute(onward, "ctx", across(1))
-        backward = lax.ppermute(backward, "ctx", across(-1))
+
+    keys, state, at = [own, right, left], None, 0
+    for s in range(2, steps):
+        right, left = onward(right), backward(left)
+        keys += [right, left]
         if s == 2:
-            q, *state = fold_first([own, right, left])
+            continue
+        if state is None:
+            q, *state = fold_first(keys[:-2])
         else:
-            state = fold_more(2 * s - 3, q, state, [right, left])
-        right, left = onward, backward
-        if s < steps:
-            right, left, state = lax.optimization_barrier((right, left, state))
+            state = fold_more(at, q, state, keys[:-2])
+        at += len(keys) - 2
+        keys = keys[-2:]
+    right, left, state = lax.optimization_barrier((right, left, state))
+    right, left = onward(right[:cut]), backward(left[cut:])
+    state = fold_more(at, q, state, keys)
+    keys = [right, left]
     flat = heads * V_HEAD + LANES
     parts = pl.pallas_call(
         functools.partial(last_kernel, chips - 1, tokens, heads),
@@ -291,7 +307,7 @@
         ],
         compiler_params=PARAMS,
         name="last",
-    )(prefix_length, table, q, *state, right, left, value_up, far_up)
+    )(prefix_length, table, q, *state, *keys, value_up, far_up)
     returned = lax.all_to_all(parts, "ctx", split_axis=0, concat_axis=0, tiled=True)
     return pl.pallas_call(
         functools.partial(merge_kernel, heads),

time: 68.5 us -> 64.5 us (0.942)
  Pallas kernels: 14.8 us -> 11.6 us
  starting transfers between devices: 17.2 us -> 15 us
  blocking collectives: 10.8 us -> 11.8 us
    all_to_all x1, waiting for transfers between devices: 0.01 us -> 10.8 us  [on_device(): lax.all_to_all(pieces, 'ctx', split_axis=0, concat_axis=0, axis_index_gro...]
    ppermute x8, waiting for transfers between devices: 22 us -> 11.4 us  [the longest x2 6.4 us: on_device(): right, left = (onward(own), backward(own))]
    pallas_call x2 -> x1, Pallas kernels: 5.76 us -> 2.09 us  [fold_more(): pl.pallas_call(functools.partial(middle_kernel, at, len(keys)), out_shape...]
    all_to_all x1, starting transfers between devices: 7.38 us -> 4.88 us  [on_device(): lax.all_to_all(pieces, 'ctx', split_axis=0, concat_axis=0, axis_index_gro...]
    all_to_all x1, blocking collectives: 10.8 us -> 11.8 us  [on_device(): lax.all_to_all(parts, 'ctx', split_axis=0, concat_axis=0, tiled=True)]
    pallas_call x1, Pallas kernels: 4.29 us -> 5.01 us  [fold_first(): pl.pallas_call(functools.partial(first_kernel, tokens, heads, len(keys)),...]
  transfers between devices with their start and end apart: 11 -> 11, of which waited for: 7 -> 5; matrix products, arithmetic and copies ran while one was open for 0% -> 3% of each run, Pallas kernels for 15% -> 11%
where the time goes in v5:
time: 64.5 us; the launch traced here: 64.2 us
  waiting for transfers between devices  22.2 us (34%)
  starting transfers between devices  15 us (23%)
  blocking collectives  11.8 us (18%)
  Pallas kernels  11.6 us (18%)
  between operations  1.46 us (2%)
  local copies, waits for them, and re-layouts  1.38 us (2%)
  other arithmetic  0.79 us (1%)
    all_to_all x1, blocking collectives, on_device(): lax.all_to_all(parts, 'ctx', split_axis=0, concat_axis=0, tiled=True)  11.8 us
    all_to_all x1, waiting for transfers between devices, on_device(): lax.all_to_all(pieces, 'ctx', split_axis=0, concat_axis=0, axis_index_gro...  10.8 us
    ppermute x2, waiting for transfers between devices, on_device(): right, left = (onward(own), backward(own))  6.4 us
    pallas_call x1, Pallas kernels, fold_first(): pl.pallas_call(functools.partial(first_kernel, tokens, heads, len(keys)),...  5.01 us
    ppermute x4, starting transfers between devices, on_device(): right, left = (onward(right), backward(left))  4.88 us
    all_to_all x1, starting transfers between devices, on_device(): lax.all_to_all(pieces, 'ctx', split_axis=0, concat_axis=0, axis_index_gro...  4.88 us
    ppermute x2, starting transfers between devices, on_device(): right, left = (onward(own), backward(own))  3.03 us
    ppermute x2, waiting for transfers between devices, on_device(): right, left = (onward(right[:cut]), backward(left[cut:]))  2.86 us
  transfers between devices with their start and end apart: 11, of which 5 were waited for; matrix products, arithmetic and copies ran while one was open for 3% of the time, Pallas kernels for 11%

profile of v5, /device:TPU:0, one launch (start us, length us, event | category | flops | bytes accessed | tf_op | source)
XLA Modules:
  0.0 64.2 jit_solution(3620331218615971290)
XLA Ops:
  0.0 2.9 %collective-permute-start = (bf16[576,254]{1,0:T(8,128)(2,1)}, bf16[576,254]{1,0:T(8,128)(2,1)S(1)}, u32[]{:S(2)}, u32[]{:S(2)}) collective-permute-start(bf16[576,254]{1,0:T(8,128)(2,1)} %bitcast.4), channel_id=1, source_target_pairs={{2,6},{3,7},{6,10},{7,11},{10,14},{11,15},{14,12},{15,13},{12,8},{... | collective-permute-start | bytes 877832 | tf_op jit(solution)/shard_map/ppermute | solution.py:263
  2.9 0.1 collective-permute-start.1
  3.0 0.0 copy-start.3
  3.0 1.3 %reshape.7 = bf16[2,8,16,576]{3,2,1,0:T(8,128)(2,1)S(1)} reshape(bf16[2,73728]{1,0:T(2,128)(2,1)} %param.7) | data formatting | bytes 589824 | tf_op jit(solution)/shard_map/reshape | solution.py:265
  4.3 0.0 copy-start
  4.4 0.0 copy-done.3
  4.4 0.8 %pad_maximum_fusion = bf16[8,40,576]{2,1,0:T(8,128)(2,1)} fusion(bf16[8,8,576]{2,1,0:T(8,128)(2,1)S(1)} %broadcast_in_dim.2, bf16[8,32,576]{2,1,0:T(8,128)(2,1)S(1)} %bitcast.7), kind=kLoop, calls=%fused_computation | loop fusion | flops 737280 | bytes 737280 | tf_op jit(solution)/shard_map/concatenate | solution.py:269
  5.2 0.0 copy-start.1
  5.2 5.0 %collective-permute-done.rest_1_ = bf16[576,254]{1,0:T(8,128)(2,1)S(1)} collective-permute-done((bf16[576,254]{1,0:T(8,128)(2,1)}, bf16[576,254]{1,0:T(8,128)(2,1)S(1)}, u32[]{:S(2)}, u32[]{:S(2)}) %collective-permute-start) | collective-permute-done | bytes 292640 | tf_op jit(solution)/shard_map/ppermute | solution.py:263
  10.2 1.4 %collective-permute-done.1.rest_2_ = bf16[576,254]{1,0:T(8,128)(2,1)S(1)} collective-permute-done((bf16[576,254]{1,0:T(8,128)(2,1)}, bf16[576,254]{1,0:T(8,128)(2,1)S(1)}, u32[]{:S(2)}, u32[]{:S(2)}) %collective-permute-start.1) | collective-permute-done | bytes 292640 | tf_op jit(solution)/shard_map/ppermute | solution.py:263
  11.6 4.9 %all-to-all-start = ((bf16[8,40,576]{2,1,0:T(8,128)(2,1)}), bf16[8,40,576]{2,1,0:T(8,128)(2,1)S(1)}, u32[]{:S(2)}, u32[]{:S(2)}) async-start(bf16[8,40,576]{2,1,0:T(8,128)(2,1)} %pad_maximum_fusion), calls=%async_computation | async-start | bytes 819200 | tf_op jit(solution)/shard_map/all_to_all | solution.py:271
  16.5 0.0 copy-done
  16.5 0.1 collective-permute-start.9
  16.6 2.0 %collective-permute-start.3 = (bf16[576,254]{1,0:T(8,128)(2,1)S(1)}, bf16[576,254]{1,0:T(8,128)(2,1)}, u32[]{:S(2)}, u32[]{:S(2)}) collective-permute-start(bf16[576,254]{1,0:T(8,128)(2,1)S(1)} %collective-permute-done.rest_1_), channel_id=1, source_target_pairs={{2,6},{3,7},{6,10},{7,11},{10,14},{11,15},{14,12},{15,13},{12,8},{... | collective-permute-start | bytes 877832 | tf_op jit(solution)/shard_map/ppermute | solution.py:280
  18.6 0.1 collective-permute-start.4
  18.7 10.8 %all-to-all-done.here_ref = bf16[8,40,576]{2,1,0:T(8,128)(2,1)S(1)} async-done(((bf16[8,40,576]{2,1,0:T(8,128)(2,1)}), bf16[8,40,576]{2,1,0:T(8,128)(2,1)S(1)}, u32[]{:S(2)}, u32[]{:S(2)}) %all-to-all-start) | async-done | bytes 368672 | tf_op jit(solution)/shard_map/all_to_all | solution.py:271
  29.5 0.0 collective-permute-start.2
  29.5 2.1 %collective-permute-done.3.rest_3_ = bf16[576,254]{1,0:T(8,128)(2,1)} collective-permute-done((bf16[576,254]{1,0:T(8,128)(2,1)S(1)}, bf16[576,254]{1,0:T(8,128)(2,1)}, u32[]{:S(2)}, u32[]{:S(2)}) %collective-permute-start.3) | collective-permute-done | bytes 292640 | tf_op jit(solution)/shard_map/ppermute | solution.py:280
  31.6 0.0 collective-permute-start.5
  31.6 0.0 collective-permute-done.4.rest_4_
  31.6 2.8 %collective-permute-start.6 = (bf16[576,254]{1,0:T(8,128)(2,1)}, bf16[576,254]{1,0:T(8,128)(2,1)S(1)}, u32[]{:S(2)}, u32[]{:S(2)}) collective-permute-start(bf16[576,254]{1,0:T(8,128)(2,1)} %collective-permute-done.4.rest_4_), channel_id=1, source_target_pairs={{2,0},{3,1},{6,2},{7,3},{10,6},{11,7},{14,10},{15,11},{12,14},{13,... | collective-permute-start | bytes 877832 | tf_op jit(solution)/shard_map/ppermute | solution.py:280
  35.1 0.0 copy-start.2
  35.7 0.0 collective-permute-done.2.there_ref
  35.7 0.0 copy-done.1
  35.7 0.0 copy-done.2
  35.8 5.0 %first.1 = (bf16[512,576]{1,0:T(8,128)(2,1)S(1)}, f32[512,128]{1,0:T(8,128)S(1)}, f32[512,128]{1,0:T(8,128)S(1)}, f32[512,512]{1,0:T(8,128)S(1)}) custom-call(s32[1]{0:T(128)S(6)} %copy.9.length_ref, s32[1]{0:T(128)S(6)} %copy.10.offset_ref, s32[64]{0:T(128)S(1)} %copy-done.2, bf16[8,40,576]{2,1,0:T(8,128)(2,1)S(1)} %all-to-all-done.here_ref, ...), custom_call_target="tpu_custom_call" | custom-call | tf_op jit(solution)/shard_map/first/pallas_call | solution.py:239
  40.8 0.0 collective-permute-done.5.rest_0_
  40.8 0.0 collective-permute-done.6.rest_1_
  40.8 2.1 %collective-permute-start.8 = (bf16[320,254]{1,0:T(8,128)(2,1)S(1)}, bf16[320,254]{1,0:T(8,128)(2,1)S(1)}, u32[]{:S(2)}, u32[]{:S(2)}) collective-permute-start(bf16[320,254]{1,0:T(8,128)(2,1)S(1)} %slice.7), channel_id=1, source_target_pairs={{2,0},{3,1},{6,2},{7,3},{10,6},{11,7},{14,10},{15,11},{12,14},{13,... | collective-permute-start | bytes 487688 | tf_op jit(solution)/shard_map/ppermute | solution.py:291
  42.9 0.1 collective-permute-start.7
  43.0 2.1 %middle.1 = (f32[512,128]{1,0:T(8,128)S(1)}, f32[512,128]{1,0:T(8,128)S(1)}, f32[512,512]{1,0:T(8,128)S(1)}) custom-call(s32[1]{0:T(128)S(6)} %copy.9.length_ref, s32[64]{0:T(128)S(1)} %copy-done.2, bf16[512,576]{1,0:T(8,128)(2,1)S(1)} %get-tuple-element.23.q_ref, f32[512,128]{1,0:T(8,128)S(1)} %get-tuple-element.27.m_in, ...), custom_call_target="tpu_custom_call" | custom-call | tf_op jit(solution)/shard_map/middle/pallas_call | solution.py:250
  45.1 0.0 collective-permute-done.9.far_up
  45.1 2.9 %collective-permute-done.7.top_ref = bf16[256,254]{1,0:T(8,128)(2,1)S(1)} collective-permute-done((bf16[256,254]{1,0:T(8,128)(2,1)S(1)}, bf16[256,254]{1,0:T(8,128)(2,1)S(1)}, u32[]{:S(2)}, u32[]{:S(2)}) %collective-permute-start.7) | collective-permute-done | bytes 130080 | tf_op jit(solution)/shard_map/ppermute | solution.py:291
  47.9 0.0 collective-permute-done.8.bottom_ref
  47.9 2.6 %last.1 = bf16[16,2,2176]{2,1,0:T(2,128)(2,1)S(1)} custom-call(s32[1]{0:T(128)S(6)} %copy.9.length_ref, s32[64]{0:T(128)S(1)} %copy-done.2, bf16[512,576]{1,0:T(8,128)(2,1)S(1)} %get-tuple-element.23.q_ref, f32[512,128]{1,0:T(8,128)S(1)} %get-tuple-element.30.m_in, f32[512,128]{1,0:T(8,128)S(1)} %get-tuple-element.31.l_in, ...), custom_call_target="tpu_custom_call" | custom-call | tf_op jit(solution)/shard_map/last/pallas_call | solution.py:295
  50.6 11.8 %all_to_all.10.parts_ref = bf16[16,2,2176]{2,1,0:T(2,128)(2,1)S(1)} all-to-all(bf16[16,2,2176]{2,1,0:T(2,128)(2,1)S(1)} %last.1), channel_id=1, replica_groups=mesh['groups'=2,'ctx'=16] {'ctx'}, dimensions={0} | all-to-all | bytes 278528 | tf_op jit(solution)/shard_map/all_to_all | solution.py:311
  62.4 1.8 %merge.1 = bf16[2,16384]{1,0:T(2,128)(2,1)} custom-call(bf16[16,2,2176]{2,1,0:T(2,128)(2,1)S(1)} %all_to_all.10.parts_ref), custom_call_target="tpu_custom_call" | custom-call | tf_op jit(solution)/shard_map/merge/pallas_call | solution.py:312
  (5 shorter events, 0.1 us)
Async XLA Ops:
  0.0 10.2 %collective-permute-start = (bf16[576,254]{1,0:T(8,128)(2,1)}, bf16[576,254]{1,0:T(8,128)(2,1)S(1)}, u32[]{:S(2)}, u32[]{:S(2)}) collective-permute-start(bf16[576,254]{1,0:T(8,128)(2,1)} %bitcast.4), channel_id=1, source_target_pairs={{2,6},{3,7},{6,10},{7,11},{10,14},{11,15},{14,12},{15,13},{12,8},{... | collective-permute-start | bytes 877832 | tf_op jit(solution)/shard_map/ppermute | solution.py:263
  2.9 8.7 %collective-permute-start.1 = (bf16[576,254]{1,0:T(8,128)(2,1)}, bf16[576,254]{1,0:T(8,128)(2,1)S(1)}, u32[]{:S(2)}, u32[]{:S(2)}) collective-permute-start(bf16[576,254]{1,0:T(8,128)(2,1)} %bitcast.5), channel_id=1, source_target_pairs={{2,0},{3,1},{6,2},{7,3},{10,6},{11,7},{14,10},{15,11},{12,14},{13,... | collective-permute-start | bytes 877832 | tf_op jit(solution)/shard_map/ppermute | solution.py:263
  3.0 1.4 %copy-start.3 = (bf16[2,576]{1,0:T(2,128)(2,1)S(1)}, bf16[2,576]{1,0:T(2,128)(2,1)}, u32[]{:S(2)}) copy-start(bf16[2,576]{1,0:T(2,128)(2,1)} %param.9) | copy-start | bytes 6916
  4.3 12.2 %copy-start = (bf16[8,512,128]{2,1,0:T(8,128)(2,1)S(1)}, bf16[8,512,128]{2,1,0:T(8,128)(2,1)}, u32[]{:S(2)}) copy-start(bf16[8,512,128]{2,1,0:T(8,128)(2,1)} %own_up.1) | copy-start | bytes 3145732
  5.2 30.5 %copy-start.1 = (bf16[254,576]{0,1:T(8,128)(2,1)S(1)}, bf16[254,576]{0,1:T(8,128)(2,1)}, u32[]{:S(2)}) copy-start(bf16[254,576]{0,1:T(8,128)(2,1)} %param.8) | copy-start | bytes 877828
  11.6 17.9 %all-to-all-start = ((bf16[8,40,576]{2,1,0:T(8,128)(2,1)}), bf16[8,40,576]{2,1,0:T(8,128)(2,1)S(1)}, u32[]{:S(2)}, u32[]{:S(2)}) async-start(bf16[8,40,576]{2,1,0:T(8,128)(2,1)} %pad_maximum_fusion), calls=%async_computation | async-start | bytes 819200 | tf_op jit(solution)/shard_map/all_to_all | solution.py:271
  16.5 28.6 %collective-permute-start.9 = (bf16[8,512,128]{2,1,0:T(8,128)(2,1)S(1)}, bf16[8,512,128]{2,1,0:T(8,128)(2,1)S(1)}, u32[]{:S(2)}, u32[]{:S(2)}) collective-permute-start(bf16[8,512,128]{2,1,0:T(8,128)(2,1)S(1)} %copy-done), channel_id=1, source_target_pairs={{0,1},{1,0},{2,3},{3,2},{4,5},{5,4},{6,7},{7,6},{8,9},{9,8},{10,11... | collective-permute-start | bytes 3145736 | tf_op jit(solution)/shard_map/ppermute | solution.py:276
  16.6 15.0 %collective-permute-start.3 = (bf16[576,254]{1,0:T(8,128)(2,1)S(1)}, bf16[576,254]{1,0:T(8,128)(2,1)}, u32[]{:S(2)}, u32[]{:S(2)}) collective-permute-start(bf16[576,254]{1,0:T(8,128)(2,1)S(1)} %collective-permute-done.rest_1_), channel_id=1, source_target_pairs={{2,6},{3,7},{6,10},{7,11},{10,14},{11,15},{14,12},{15,13},{12,8},{... | collective-permute-start | bytes 877832 | tf_op jit(solution)/shard_map/ppermute | solution.py:280
  18.6 13.0 %collective-permute-start.4 = (bf16[576,254]{1,0:T(8,128)(2,1)S(1)}, bf16[576,254]{1,0:T(8,128)(2,1)}, u32[]{:S(2)}, u32[]{:S(2)}) collective-permute-start(bf16[576,254]{1,0:T(8,128)(2,1)S(1)} %collective-permute-done.1.rest_2_), channel_id=1, source_target_pairs={{2,0},{3,1},{6,2},{7,3},{10,6},{11,7},{14,10},{15,11},{12,14},{13,... | collective-permute-start | bytes 877832 | tf_op jit(solution)/shard_map/ppermute | solution.py:280
  29.5 6.3 %collective-permute-start.2 = (bf16[8,40,576]{2,1,0:T(8,128)(2,1)S(1)}, bf16[8,40,576]{2,1,0:T(8,128)(2,1)S(1)}, u32[]{:S(2)}, u32[]{:S(2)}) collective-permute-start(bf16[8,40,576]{2,1,0:T(8,128)(2,1)S(1)} %all-to-all-done.here_ref), channel_id=1, source_target_pairs={{0,1},{1,0},{2,3},{3,2},{4,5},{5,4},{6,7},{7,6},{8,9},{9,8},{10,11... | collective-permute-start | bytes 1105928 | tf_op jit(solution)/shard_map/ppermute | solution.py:275
  31.6 9.2 %collective-permute-start.5 = (bf16[576,254]{1,0:T(8,128)(2,1)}, bf16[576,254]{1,0:T(8,128)(2,1)S(1)}, u32[]{:S(2)}, u32[]{:S(2)}) collective-permute-start(bf16[576,254]{1,0:T(8,128)(2,1)} %collective-permute-done.3.rest_3_), channel_id=1, source_target_pairs={{2,6},{3,7},{6,10},{7,11},{10,14},{11,15},{14,12},{15,13},{12,8},{... | collective-permute-start | bytes 877832 | tf_op jit(solution)/shard_map/ppermute | solution.py:280
  31.6 9.2 %collective-permute-start.6 = (bf16[576,254]{1,0:T(8,128)(2,1)}, bf16[576,254]{1,0:T(8,128)(2,1)S(1)}, u32[]{:S(2)}, u32[]{:S(2)}) collective-permute-start(bf16[576,254]{1,0:T(8,128)(2,1)} %collective-permute-done.4.rest_4_), channel_id=1, source_target_pairs={{2,0},{3,1},{6,2},{7,3},{10,6},{11,7},{14,10},{15,11},{12,14},{13,... | collective-permute-start | bytes 877832 | tf_op jit(solution)/shard_map/ppermute | solution.py:280
  35.1 0.7 %copy-start.2 = (s32[64]{0:T(128)S(1)}, s32[64]{0:T(128)}, u32[]{:S(2)}) copy-start(s32[64]{0:T(128)} %constant.5.clone.table_ref) | copy-start | bytes 772
  40.8 7.1 %collective-permute-start.8 = (bf16[320,254]{1,0:T(8,128)(2,1)S(1)}, bf16[320,254]{1,0:T(8,128)(2,1)S(1)}, u32[]{:S(2)}, u32[]{:S(2)}) collective-permute-start(bf16[320,254]{1,0:T(8,128)(2,1)S(1)} %slice.7), channel_id=1, source_target_pairs={{2,0},{3,1},{6,2},{7,3},{10,6},{11,7},{14,10},{15,11},{12,14},{13,... | collective-permute-start | bytes 487688 | tf_op jit(solution)/shard_map/ppermute | solution.py:291
  42.9 5.0 %collective-permute-start.7 = (bf16[256,254]{1,0:T(8,128)(2,1)S(1)}, bf16[256,254]{1,0:T(8,128)(2,1)S(1)}, u32[]{:S(2)}, u32[]{:S(2)}) collective-permute-start(bf16[256,254]{1,0:T(8,128)(2,1)S(1)} %slice.6), channel_id=1, source_target_pairs={{2,6},{3,7},{6,10},{7,11},{10,14},{11,15},{14,12},{15,13},{12,8},{... | collective-permute-start | bytes 390152 | tf_op jit(solution)/shard_map/ppermute | solution.py:291

commit v6 on v5

--- a/solution.py
+++ b/solution.py
@@ -82,19 +82,17 @@
     return shards
 
 
-def first_kernel(tokens, heads, count, length_ref, offset_ref, table_ref, here_ref, there_ref, *rest):
-    keys, (q_ref, m_ref, l_ref, acc_ref, span_ref) = rest[:count], rest[count:]
-    chips = here_ref.shape[0]
-    rows = tokens * heads
+def first_kernel(heads, count, length_ref, offset_ref, table_ref, here_ref, there_ref, *rest):
+    keys, (q_ref, m_ref, l_ref, acc_ref) = rest[:count], rest[count:]
+    chips = lax.axis_size("ctx") // CORES
+    half = here_ref.shape[0]
+    tokens = half // chips
+    width = q_ref.shape[1]
     for core, piece_ref in enumerate((here_ref, there_ref)):
-        for chip in range(chips):
-            at = core * chips + chip
-            q_ref[at * rows:(at + 1) * rows, :] = piece_ref[chip, :rows, :]
-            if core == 0:
-                span_ref[chip * tokens:(chip + 1) * tokens, :] = (
-                    piece_ref[chip, rows:rows + tokens, :].astype(f32)
-                )
-    span = span_ref[...].astype(bf16)
+        for head in range(heads):
+            row = (head * CORES + core) * half
+            q_ref[row:row + half, :] = piece_ref[:, head * width:(head + 1) * width]
+    span = here_ref[:, heads * width:]
     total = q_ref.shape[0]
     block = min(256, total)
     key_index = lax.broadcasted_iota(jnp.int32, (1, span.shape[0]), 1)
@@ -105,7 +103,7 @@
             q_ref[part, :], span, (((1,), (1,)), ((), ())), preferred_element_type=f32
         ) * score_scale
         row_index = start + lax.broadcasted_iota(jnp.int32, (block, 1), 0)
-        row_token = token_of(row_index >> (heads.bit_length() - 1), tokens, chips)
+        row_token = token_of(row_index & (half * CORES - 1), tokens, chips)
         shown = (key_token >= offset_ref[0]) & (key_token <= row_token)
         s = jnp.where(shown, s, neg_large)
         m_new = jnp.maximum(jnp.max(s, axis=1, keepdims=True), least_max)
@@ -127,15 +125,13 @@
 
 def last_kernel(at, tokens, heads, length_ref, table_ref, q_ref, m_in, l_in, acc_in,
                 top_ref, bottom_ref, own_up, far_up, out_ref,
-                key_ref, m_ref, l_ref, acc_ref, context_ref, flat_ref):
+                key_ref, m_ref, l_ref, acc_ref, flat_ref):
     cut = top_ref.shape[0]
     key_ref[:cut, :] = top_ref[...]
     key_ref[cut:, :] = bottom_ref[...]
     middle_kernel(at, 1, length_ref, table_ref, q_ref, m_in, l_in, acc_in,
                   key_ref, m_ref, l_ref, acc_ref)
-    for k in range(LATENT // LANES):
-        lanes = slice(k * LANES, (k + 1) * LANES)
-        context_ref[k] = acc_ref[:, lanes] / l_ref[...]
+    acc_ref[...] = acc_ref[...] / l_ref[:, :1]
     m_ref[...] = m_ref[...] + jnp.log2(l_ref[...])
     everyone = flat_ref.shape[0]
     core = lax.axis_index("ctx") % CORES
@@ -148,10 +144,8 @@
             first_head = (core ^ side) * per_core + j
             contexts = []
             for head in [first_head + i for i in range(pair)]:
-                rows = pl.ds(head, everyone, stride=heads)
-                contexts.append(jnp.concatenate(
-                    [context_ref[k, rows, :] for k in range(LATENT // LANES)], axis=1
-                ).astype(bf16))
+                rows = pl.ds(pl.multiple_of(head * everyone, everyone), everyone)
+                contexts.append(acc_ref[rows, :].astype(bf16))
                 weight = m_ref[rows, :]
                 high = weight.astype(bf16).astype(f32)
                 mid = (weight - high).astype(bf16).astype(f32)
@@ -237,11 +231,10 @@
 
     def fold_first(keys):
         return pl.pallas_call(
-            functools.partial(first_kernel, tokens, heads, len(keys)),
+            functools.partial(first_kernel, heads, len(keys)),
             out_shape=[shape(total, width, dtype=bf16)] + state_shapes,
             in_specs=[SMEM] * 3 + [VMEM] * (2 + len(keys)),
             out_specs=[VMEM] * 4,
-            scratch_shapes=[pltpu.VMEM((everyone // CORES, width), f32)],
             compiler_params=PARAMS,
             name="first",
         )(prefix_length, span_offset, table, here, there, *keys)
@@ -262,17 +255,12 @@
     own = prefix_latents.T
     right, left = onward(own), backward(own)
 
-    grouped = queries.reshape(tokens, chips, heads, width).transpose(1, 0, 2, 3)
-    pad = -(rows + tokens) % 8
-    span_rows = jnp.pad(span_latents, ((0, pad), (0, 0)))
-    span_rows = jnp.broadcast_to(span_rows[None], (chips, tokens + pad, width))
-    pieces = jnp.concatenate([grouped.reshape(chips, rows, width), span_rows], axis=1)
-    pieces, right, left = lax.optimization_barrier((pieces, right, left))
+    grouped = queries.reshape(tokens, chips, heads * width).transpose(1, 0, 2)
+    spans = jnp.broadcast_to(span_latents[None], (chips, tokens, width))
+    pieces = jnp.concatenate([grouped, spans], axis=2)
     here = lax.all_to_all(
         pieces, "ctx", split_axis=0, concat_axis=0, axis_index_groups=same_core, tiled=True
     )
-
-    there = lax.ppermute(here, "ctx", other_core)
     far_up = lax.ppermute(value_up, "ctx", other_core)
 
     keys, state, at = [own, right, left], None, 0
@@ -280,6 +268,10 @@
         right, left = onward(right), backward(left)
         keys += [right, left]
         if s == 2:
+            right, left, here = lax.optimization_barrier((right, left, here))
+            keys[-2:] = right, left
+            here = here.reshape(chips * tokens, (heads + 1) * width)
+            there = lax.ppermute(here, "ctx", other_core)
             continue
         if state is None:
             q, *state = fold_first(keys[:-2])
@@ -302,7 +294,6 @@
             pltpu.VMEM((total, LANES), f32),
             pltpu.VMEM((total, LANES), f32),
             pltpu.VMEM((total, LATENT), f32),
-            pltpu.VMEM((LATENT // LANES, total, LANES), f32),
             pltpu.VMEM((everyone, flat), f32),
         ],
         compiler_params=PARAMS,

time: 64.5 us -> 61.1 us (0.947)
  waiting for transfers between devices: 22.2 us -> 16.6 us
  starting transfers between devices: 15 us -> 16.9 us
  other arithmetic: 0.79 us -> 1.96 us
    ppermute x2, waiting for transfers between devices: 6.4 us -> 0.01 us  [on_device(): right, left = (onward(own), backward(own))]
    ppermute x4, waiting for transfers between devices: 2.14 us -> 5.79 us  [on_device(): right, left = (onward(right), backward(left))]
    all_to_all x1, waiting for transfers between devices: 10.8 us -> 9.23 us  [on_device(): lax.all_to_all(pieces, 'ctx', split_axis=0, concat_axis=0, axis_index_gro...]
    all_to_all x1, starting transfers between devices: 4.88 us -> 6.25 us  [on_device(): lax.all_to_all(pieces, 'ctx', split_axis=0, concat_axis=0, axis_index_gro...]
    ppermute x2, waiting for transfers between devices: 2.86 us -> 1.58 us  [on_device(): right, left = (onward(right[:cut]), backward(left[cut:]))]
    concatenate x1, other arithmetic: 0.79 us -> 1.96 us  [on_device(): pieces = jnp.concatenate([grouped, spans], axis=2)]
    reshape x2 -> x1, local copies, waits for them, and re-layouts: 1.32 us -> 0.23 us  [on_device(): here = here.reshape(chips * tokens, (heads + 1) * width)]
    broadcast_in_dim x1, local copies, waits for them, and re-layouts: 0.01 us -> 0.7 us  [on_device(): spans = jnp.broadcast_to(span_latents[None], (chips, tokens, width))]
  transfers between devices with their start and end apart: 11 -> 11, of which waited for: 5 -> 6; matrix products, arithmetic and copies ran while one was open for 3% -> 5% of each run, Pallas kernels for 11% -> 11%
where the time goes in v6:
time: 61.1 us; the launch traced here: 60.8 us
  starting transfers between devices  16.9 us (28%)
  waiting for transfers between devices  16.6 us (27%)
  blocking collectives  11.7 us (19%)
  Pallas kernels  11.2 us (18%)
  other arithmetic  1.96 us (3%)
  between operations  1.4 us (2%)
  local copies, waits for them, and re-layouts  0.96 us (2%)
    all_to_all x1, blocking collectives, on_device(): lax.all_to_all(parts, 'ctx', split_axis=0, concat_axis=0, tiled=True)  11.7 us
    all_to_all x1, waiting for transfers between devices, on_device(): lax.all_to_all(pieces, 'ctx', split_axis=0, concat_axis=0, axis_index_gro...  9.23 us
    all_to_all x1, starting transfers between devices, on_device(): lax.all_to_all(pieces, 'ctx', split_axis=0, concat_axis=0, axis_index_gro...  6.25 us
    ppermute x4, waiting for transfers between devices, on_device(): right, left = (onward(right), backward(left))  5.79 us
    ppermute x4, starting transfers between devices, on_device(): right, left = (onward(right), backward(left))  5.43 us
    pallas_call x1, Pallas kernels, fold_first(): pl.pallas_call(functools.partial(first_kernel, heads, len(keys)), out_sha...  4.59 us
    ppermute x2, starting transfers between devices, on_device(): right, left = (onward(own), backward(own))  3.03 us
    pallas_call x1, Pallas kernels, on_device(): pl.pallas_call(functools.partial(last_kernel, chips - 1, tokens, heads),...  2.68 us
  transfers between devices with their start and end apart: 11, of which 6 were waited for; matrix products, arithmetic and copies ran while one was open for 5% of the time, Pallas kernels for 11%

profile of v6, /device:TPU:0, one launch (start us, length us, event | category | flops | bytes accessed | tf_op | source)
XLA Modules:
  0.0 60.8 jit_solution(13866730619998020752)
XLA Ops:
  0.0 2.9 %collective-permute-start = (bf16[576,254]{1,0:T(8,128)(2,1)}, bf16[576,254]{1,0:T(8,128)(2,1)S(1)}, u32[]{:S(2)}, u32[]{:S(2)}) collective-permute-start(bf16[576,254]{1,0:T(8,128)(2,1)} %bitcast.4), channel_id=1, source_target_pairs={{2,6},{3,7},{6,10},{7,11},{10,14},{11,15},{14,12},{15,13},{12,8},{... | collective-permute-start | bytes 877832 | tf_op jit(solution)/shard_map/ppermute | solution.py:256
  2.9 0.1 collective-permute-start.2
  3.0 0.0 collective-permute-start.9
  3.0 0.7 %broadcast_in_dim.2 = bf16[8,2,576]{2,1,0:T(2,128)(2,1)S(1)} broadcast(bf16[2,576]{1,0:T(2,128)(2,1)} %param.9), dimensions={1,2} | broadcast | bytes 20736 | tf_op jit(solution)/shard_map/broadcast_in_dim | solution.py:259
  3.7 2.0 %pad_maximum_fusion = bf16[8,2,9792]{2,1,0:T(2,128)(2,1)} fusion(bf16[8,2,576]{2,1,0:T(2,128)(2,1)S(1)} %broadcast_in_dim.2, bf16[8,2,9216]{2,1,0:T(2,128)(2,1)} %bitcast.7), kind=kLoop, calls=%fused_computation | loop fusion | flops 626688 | bytes 626688 | tf_op jit(solution)/shard_map/concatenate | solution.py:260
  5.7 6.3 %all-to-all-start = ((bf16[8,2,9792]{2,1,0:T(2,128)(2,1)}), bf16[8,2,9792]{2,1,0:T(2,128)(2,1)S(1)}, u32[]{:S(2)}, u32[]{:S(2)}) async-start(bf16[8,2,9792]{2,1,0:T(2,128)(2,1)} %pad_maximum_fusion), calls=%async_computation | async-start | bytes 630784 | tf_op jit(solution)/shard_map/all_to_all | solution.py:261
  11.9 0.0 copy-start.1
  12.0 0.0 collective-permute-done.rest_1_
  12.0 2.1 %collective-permute-start.1 = (bf16[576,254]{1,0:T(8,128)(2,1)S(1)}, bf16[576,254]{1,0:T(8,128)(2,1)S(1)}, u32[]{:S(2)}, u32[]{:S(2)}) collective-permute-start(bf16[576,254]{1,0:T(8,128)(2,1)S(1)} %collective-permute-done.rest_1_), channel_id=1, source_target_pairs={{2,6},{3,7},{6,10},{7,11},{10,14},{11,15},{14,12},{15,13},{12,8},{... | collective-permute-start | bytes 877832 | tf_op jit(solution)/shard_map/ppermute | solution.py:268
  14.0 0.0 collective-permute-done.2.rest_2_
  14.0 0.1 collective-permute-start.3
  14.1 9.2 %all-to-all-done = bf16[8,2,9792]{2,1,0:T(2,128)(2,1)S(1)} async-done(((bf16[8,2,9792]{2,1,0:T(2,128)(2,1)}), bf16[8,2,9792]{2,1,0:T(2,128)(2,1)S(1)}, u32[]{:S(2)}, u32[]{:S(2)}) %all-to-all-start) | async-done | bytes 313376 | tf_op jit(solution)/shard_map/all_to_all | solution.py:261
  23.3 3.0 %collective-permute-done.1.rest_3_ = bf16[576,254]{1,0:T(8,128)(2,1)S(1)} collective-permute-done((bf16[576,254]{1,0:T(8,128)(2,1)S(1)}, bf16[576,254]{1,0:T(8,128)(2,1)S(1)}, u32[]{:S(2)}, u32[]{:S(2)}) %collective-permute-start.1) | collective-permute-done | bytes 292640 | tf_op jit(solution)/shard_map/ppermute | solution.py:268
  26.4 0.0 collective-permute-done.3.rest_4_
  26.4 0.2 reshape.8.here_ref
  26.6 0.1 collective-permute-start.4
  26.7 1.5 %collective-permute-start.5 = (bf16[576,254]{1,0:T(8,128)(2,1)S(1)}, bf16[576,254]{1,0:T(8,128)(2,1)S(1)}, u32[]{:S(2)}, u32[]{:S(2)}) collective-permute-start(bf16[576,254]{1,0:T(8,128)(2,1)S(1)} %collective-permute-done.1.rest_3_), channel_id=1, source_target_pairs={{2,6},{3,7},{6,10},{7,11},{10,14},{11,15},{14,12},{15,13},{12,8},{... | collective-permute-start | bytes 877832 | tf_op jit(solution)/shard_map/ppermute | solution.py:268
  28.2 1.8 %collective-permute-start.6 = (bf16[576,254]{1,0:T(8,128)(2,1)S(1)}, bf16[576,254]{1,0:T(8,128)(2,1)S(1)}, u32[]{:S(2)}, u32[]{:S(2)}) collective-permute-start(bf16[576,254]{1,0:T(8,128)(2,1)S(1)} %collective-permute-done.3.rest_4_), channel_id=1, source_target_pairs={{2,0},{3,1},{6,2},{7,3},{10,6},{11,7},{14,10},{15,11},{12,14},{13,... | collective-permute-start | bytes 877832 | tf_op jit(solution)/shard_map/ppermute | solution.py:268
  30.6 0.0 copy-start.2
  31.3 0.0 collective-permute-done.4.there_ref
  31.3 0.0 copy-done.1
  31.3 0.0 copy-done.2
  31.3 4.6 %first.1 = (bf16[512,576]{1,0:T(8,128)(2,1)S(1)}, f32[512,128]{1,0:T(8,128)S(1)}, f32[512,128]{1,0:T(8,128)S(1)}, f32[512,512]{1,0:T(8,128)S(1)}) custom-call(s32[1]{0:T(128)S(6)} %copy.9.length_ref, s32[1]{0:T(128)S(6)} %copy.10.offset_ref, s32[64]{0:T(128)S(1)} %copy-done.2, bf16[16,9792]{1,0:T(8,128)(2,1)S(1)} %reshape.8.here_ref, ...), custom_call_target="tpu_custom_call" | custom-call | tf_op jit(solution)/shard_map/first/pallas_call | solution.py:233
  35.9 1.6 %collective-permute-done.5.rest_0_ = bf16[576,254]{1,0:T(8,128)(2,1)S(1)} collective-permute-done((bf16[576,254]{1,0:T(8,128)(2,1)S(1)}, bf16[576,254]{1,0:T(8,128)(2,1)S(1)}, u32[]{:S(2)}, u32[]{:S(2)}) %collective-permute-start.5) | collective-permute-done | bytes 292640 | tf_op jit(solution)/shard_map/ppermute | solution.py:268
  37.5 1.2 %collective-permute-done.6.rest_1_ = bf16[576,254]{1,0:T(8,128)(2,1)S(1)} collective-permute-done((bf16[576,254]{1,0:T(8,128)(2,1)S(1)}, bf16[576,254]{1,0:T(8,128)(2,1)S(1)}, u32[]{:S(2)}, u32[]{:S(2)}) %collective-permute-start.6) | collective-permute-done | bytes 292640 | tf_op jit(solution)/shard_map/ppermute | solution.py:268
  38.7 0.6 %collective-permute-start.8 = (bf16[320,254]{1,0:T(8,128)(2,1)S(1)}, bf16[320,254]{1,0:T(8,128)(2,1)S(1)}, u32[]{:S(2)}, u32[]{:S(2)}) collective-permute-start(bf16[320,254]{1,0:T(8,128)(2,1)S(1)} %slice.7), channel_id=1, source_target_pairs={{2,0},{3,1},{6,2},{7,3},{10,6},{11,7},{14,10},{15,11},{12,14},{13,... | collective-permute-start | bytes 487688 | tf_op jit(solution)/shard_map/ppermute | solution.py:283
  39.3 1.5 %collective-permute-start.7 = (bf16[256,254]{1,0:T(8,128)(2,1)S(1)}, bf16[256,254]{1,0:T(8,128)(2,1)S(1)}, u32[]{:S(2)}, u32[]{:S(2)}) collective-permute-start(bf16[256,254]{1,0:T(8,128)(2,1)S(1)} %slice.6), channel_id=1, source_target_pairs={{2,6},{3,7},{6,10},{7,11},{10,14},{11,15},{14,12},{15,13},{12,8},{... | collective-permute-start | bytes 390152 | tf_op jit(solution)/shard_map/ppermute | solution.py:283
  40.8 0.0 copy-start
  40.8 2.1 %middle.1 = (f32[512,128]{1,0:T(8,128)S(1)}, f32[512,128]{1,0:T(8,128)S(1)}, f32[512,512]{1,0:T(8,128)S(1)}) custom-call(s32[1]{0:T(128)S(6)} %copy.9.length_ref, s32[64]{0:T(128)S(1)} %copy-done.2, bf16[512,576]{1,0:T(8,128)(2,1)S(1)} %get-tuple-element.23.q_ref, f32[512,128]{1,0:T(8,128)S(1)} %get-tuple-element.27.m_in, ...), custom_call_target="tpu_custom_call" | custom-call | tf_op jit(solution)/shard_map/middle/pallas_call | solution.py:243
  42.9 1.4 %collective-permute-done.7.top_ref = bf16[256,254]{1,0:T(8,128)(2,1)S(1)} collective-permute-done((bf16[256,254]{1,0:T(8,128)(2,1)S(1)}, bf16[256,254]{1,0:T(8,128)(2,1)S(1)}, u32[]{:S(2)}, u32[]{:S(2)}) %collective-permute-start.7) | collective-permute-done | bytes 130080 | tf_op jit(solution)/shard_map/ppermute | solution.py:283
  44.3 0.0 collective-permute-done.9.far_up
  44.3 0.2 collective-permute-done.8.bottom_ref
  44.5 0.0 copy-done
  44.5 2.7 %last.1 = bf16[16,2,2176]{2,1,0:T(2,128)(2,1)S(1)} custom-call(s32[1]{0:T(128)S(6)} %copy.9.length_ref, s32[64]{0:T(128)S(1)} %copy-done.2, bf16[512,576]{1,0:T(8,128)(2,1)S(1)} %get-tuple-element.23.q_ref, f32[512,128]{1,0:T(8,128)S(1)} %get-tuple-element.30.m_in, f32[512,128]{1,0:T(8,128)S(1)} %get-tuple-element.31.l_in, ...), custom_call_target="tpu_custom_call" | custom-call | tf_op jit(solution)/shard_map/last/pallas_call | solution.py:287
  47.2 11.7 %all_to_all.10.parts_ref = bf16[16,2,2176]{2,1,0:T(2,128)(2,1)S(1)} all-to-all(bf16[16,2,2176]{2,1,0:T(2,128)(2,1)S(1)} %last.1), channel_id=1, replica_groups=mesh['groups'=2,'ctx'=16] {'ctx'}, dimensions={0} | all-to-all | bytes 278528 | tf_op jit(solution)/shard_map/all_to_all | solution.py:302
  58.9 1.8 %merge.1 = bf16[2,16384]{1,0:T(2,128)(2,1)} custom-call(bf16[16,2,2176]{2,1,0:T(2,128)(2,1)S(1)} %all_to_all.10.parts_ref), custom_call_target="tpu_custom_call" | custom-call | tf_op jit(solution)/shard_map/merge/pallas_call | solution.py:303
  (2 shorter events, 0.0 us)
Async XLA Ops:
  0.0 12.0 %collective-permute-start = (bf16[576,254]{1,0:T(8,128)(2,1)}, bf16[576,254]{1,0:T(8,128)(2,1)S(1)}, u32[]{:S(2)}, u32[]{:S(2)}) collective-permute-start(bf16[576,254]{1,0:T(8,128)(2,1)} %bitcast.4), channel_id=1, source_target_pairs={{2,6},{3,7},{6,10},{7,11},{10,14},{11,15},{14,12},{15,13},{12,8},{... | collective-permute-start | bytes 877832 | tf_op jit(solution)/shard_map/ppermute | solution.py:256
  2.9 11.1 %collective-permute-start.2 = (bf16[576,254]{1,0:T(8,128)(2,1)}, bf16[576,254]{1,0:T(8,128)(2,1)S(1)}, u32[]{:S(2)}, u32[]{:S(2)}) collective-permute-start(bf16[576,254]{1,0:T(8,128)(2,1)} %bitcast.5), channel_id=1, source_target_pairs={{2,0},{3,1},{6,2},{7,3},{10,6},{11,7},{14,10},{15,11},{12,14},{13,... | collective-permute-start | bytes 877832 | tf_op jit(solution)/shard_map/ppermute | solution.py:256
  3.0 41.3 %collective-permute-start.9 = (bf16[8,512,128]{2,1,0:T(8,128)(2,1)}, bf16[8,512,128]{2,1,0:T(8,128)(2,1)S(1)}, u32[]{:S(2)}, u32[]{:S(2)}) collective-permute-start(bf16[8,512,128]{2,1,0:T(8,128)(2,1)} %own_up.1), channel_id=1, source_target_pairs={{0,1},{1,0},{2,3},{3,2},{4,5},{5,4},{6,7},{7,6},{8,9},{9,8},{10,11... | collective-permute-start | bytes 3145736 | tf_op jit(solution)/shard_map/ppermute | solution.py:264
  5.7 17.6 %all-to-all-start = ((bf16[8,2,9792]{2,1,0:T(2,128)(2,1)}), bf16[8,2,9792]{2,1,0:T(2,128)(2,1)S(1)}, u32[]{:S(2)}, u32[]{:S(2)}) async-start(bf16[8,2,9792]{2,1,0:T(2,128)(2,1)} %pad_maximum_fusion), calls=%async_computation | async-start | bytes 630784 | tf_op jit(solution)/shard_map/all_to_all | solution.py:261
  11.9 19.4 %copy-start.1 = (bf16[254,576]{0,1:T(8,128)(2,1)S(1)}, bf16[254,576]{0,1:T(8,128)(2,1)}, u32[]{:S(2)}) copy-start(bf16[254,576]{0,1:T(8,128)(2,1)} %param.8) | copy-start | bytes 877828
  12.0 14.4 %collective-permute-start.1 = (bf16[576,254]{1,0:T(8,128)(2,1)S(1)}, bf16[576,254]{1,0:T(8,128)(2,1)S(1)}, u32[]{:S(2)}, u32[]{:S(2)}) collective-permute-start(bf16[576,254]{1,0:T(8,128)(2,1)S(1)} %collective-permute-done.rest_1_), channel_id=1, source_target_pairs={{2,6},{3,7},{6,10},{7,11},{10,14},{11,15},{14,12},{15,13},{12,8},{... | collective-permute-start | bytes 877832 | tf_op jit(solution)/shard_map/ppermute | solution.py:268
  14.0 12.3 %collective-permute-start.3 = (bf16[576,254]{1,0:T(8,128)(2,1)S(1)}, bf16[576,254]{1,0:T(8,128)(2,1)S(1)}, u32[]{:S(2)}, u32[]{:S(2)}) collective-permute-start(bf16[576,254]{1,0:T(8,128)(2,1)S(1)} %collective-permute-done.2.rest_2_), channel_id=1, source_target_pairs={{2,0},{3,1},{6,2},{7,3},{10,6},{11,7},{14,10},{15,11},{12,14},{13,... | collective-permute-start | bytes 877832 | tf_op jit(solution)/shard_map/ppermute | solution.py:268
  26.6 4.7 %collective-permute-start.4 = (bf16[16,9792]{1,0:T(8,128)(2,1)S(1)}, bf16[16,9792]{1,0:T(8,128)(2,1)S(1)}, u32[]{:S(2)}, u32[]{:S(2)}) collective-permute-start(bf16[16,9792]{1,0:T(8,128)(2,1)S(1)} %reshape.8.here_ref), channel_id=1, source_target_pairs={{0,1},{1,0},{2,3},{3,2},{4,5},{5,4},{6,7},{7,6},{8,9},{9,8},{10,11... | collective-permute-start | bytes 940040 | tf_op jit(solution)/shard_map/ppermute | solution.py:274
  26.7 10.8 %collective-permute-start.5 = (bf16[576,254]{1,0:T(8,128)(2,1)S(1)}, bf16[576,254]{1,0:T(8,128)(2,1)S(1)}, u32[]{:S(2)}, u32[]{:S(2)}) collective-permute-start(bf16[576,254]{1,0:T(8,128)(2,1)S(1)} %collective-permute-done.1.rest_3_), channel_id=1, source_target_pairs={{2,6},{3,7},{6,10},{7,11},{10,14},{11,15},{14,12},{15,13},{12,8},{... | collective-permute-start | bytes 877832 | tf_op jit(solution)/shard_map/ppermute | solution.py:268
  28.2 10.5 %collective-permute-start.6 = (bf16[576,254]{1,0:T(8,128)(2,1)S(1)}, bf16[576,254]{1,0:T(8,128)(2,1)S(1)}, u32[]{:S(2)}, u32[]{:S(2)}) collective-permute-start(bf16[576,254]{1,0:T(8,128)(2,1)S(1)} %collective-permute-done.3.rest_4_), channel_id=1, source_target_pairs={{2,0},{3,1},{6,2},{7,3},{10,6},{11,7},{14,10},{15,11},{12,14},{13,... | collective-permute-start | bytes 877832 | tf_op jit(solution)/shard_map/ppermute | solution.py:268
  30.6 0.7 %copy-start.2 = (s32[64]{0:T(128)S(1)}, s32[64]{0:T(128)}, u32[]{:S(2)}) copy-start(s32[64]{0:T(128)} %constant.2.clone.table_ref) | copy-start | bytes 772
  38.7 5.8 %collective-permute-start.8 = (bf16[320,254]{1,0:T(8,128)(2,1)S(1)}, bf16[320,254]{1,0:T(8,128)(2,1)S(1)}, u32[]{:S(2)}, u32[]{:S(2)}) collective-permute-start(bf16[320,254]{1,0:T(8,128)(2,1)S(1)} %slice.7), channel_id=1, source_target_pairs={{2,0},{3,1},{6,2},{7,3},{10,6},{11,7},{14,10},{15,11},{12,14},{13,... | collective-permute-start | bytes 487688 | tf_op jit(solution)/shard_map/ppermute | solution.py:283
  39.3 5.0 %collective-permute-start.7 = (bf16[256,254]{1,0:T(8,128)(2,1)S(1)}, bf16[256,254]{1,0:T(8,128)(2,1)S(1)}, u32[]{:S(2)}, u32[]{:S(2)}) collective-permute-start(bf16[256,254]{1,0:T(8,128)(2,1)S(1)} %slice.6), channel_id=1, source_target_pairs={{2,6},{3,7},{6,10},{7,11},{10,14},{11,15},{14,12},{15,13},{12,8},{... | collective-permute-start | bytes 390152 | tf_op jit(solution)/shard_map/ppermute | solution.py:283
  40.8 3.7 %copy-start = (bf16[8,512,128]{2,1,0:T(8,128)(2,1)S(1)}, bf16[8,512,128]{2,1,0:T(8,128)(2,1)}, u32[]{:S(2)}) copy-start(bf16[8,512,128]{2,1,0:T(8,128)(2,1)} %own_up.1) | copy-start | bytes 3145732

commit v7 on v6

--- a/solution.py
+++ b/solution.py
@@ -123,8 +123,8 @@
     fold_shards(q_ref, with_base(table_ref, at, keys), length_ref[0], (m_in, l_in, acc_in), new)
 
 
-def last_kernel(at, tokens, heads, length_ref, table_ref, q_ref, m_in, l_in, acc_in,
-                top_ref, bottom_ref, own_up, far_up, out_ref,
+def last_kernel(at, heads, length_ref, table_ref, q_ref, m_in, l_in, acc_in,
+                top_ref, bottom_ref, own_up, far_up, keep_ref, give_ref,
                 key_ref, m_ref, l_ref, acc_ref, flat_ref):
     cut = top_ref.shape[0]
     key_ref[:cut, :] = top_ref[...]
@@ -164,28 +164,25 @@
                     i * everyone:(i + 1) * everyone, i * V_HEAD:(i + 1) * V_HEAD
                 ]
     flat_ref[:, heads * V_HEAD:] = tail
-    chips = everyone // tokens // CORES
-    for i in range(chips * CORES):
-        out_ref[(i % chips) * CORES + (core ^ (i // chips))] = (
-            flat_ref[i * tokens:(i + 1) * tokens, :].astype(bf16)
+    keep_ref[...] = flat_ref[:everyone // CORES, :]
+    give_ref[...] = flat_ref[everyone // CORES:, :].astype(bf16)
+
+
+def merge_kernel(heads, keep_ref, got_ref, out_ref, flat_ref):
+    width = heads * V_HEAD
+    gap = keep_ref[:, width:] - got_ref[:, width:].astype(f32)
+    delta = gap[:, :heads] + (gap[:, heads:2 * heads] + gap[:, 2 * heads:3 * heads])
+    share = 1.0 / (1.0 + jnp.exp2(-delta))
+    rest = 1.0 / (1.0 + jnp.exp2(delta))
+    for j in range(heads):
+        lanes = slice(j * V_HEAD, (j + 1) * V_HEAD)
+        flat_ref[:, lanes] = (
+            keep_ref[:, lanes] * share[:, j:j + 1]
+            + got_ref[:, lanes].astype(f32) * rest[:, j:j + 1]
         )
-
-
-def merge_kernel(heads, parts_ref, out_ref):
-    width = heads * V_HEAD
-    for chip in range(parts_ref.shape[0] // CORES):
-        one = parts_ref[2 * chip].astype(f32)
-        two = parts_ref[2 * chip + 1].astype(f32)
-        gap = one[:, width:] - two[:, width:]
-        delta = gap[:, :heads] + (gap[:, heads:2 * heads] + gap[:, 2 * heads:3 * heads])
-        share = 1.0 / (1.0 + jnp.exp2(-delta))
-        rest = 1.0 / (1.0 + jnp.exp2(delta))
-        for j in range(heads):
-            lanes = slice(j * V_HEAD, (j + 1) * V_HEAD)
-            mixed = one[:, lanes] * share[:, j:j + 1] + two[:, lanes] * rest[:, j:j + 1]
-            out_ref[:, chip * width + j * V_HEAD:chip * width + (j + 1) * V_HEAD] = (
-                mixed.astype(bf16)
-            )
+    chips, tokens, _ = out_ref.shape
+    for chip in range(chips):
+        out_ref[chip] = flat_ref[chip * tokens:(chip + 1) * tokens, :].astype(bf16)
 
 
 VMEM = pl.BlockSpec(memory_space=pltpu.VMEM)
@@ -284,11 +281,12 @@
     state = fold_more(at, q, state, keys)
     keys = [right, left]
     flat = heads * V_HEAD + LANES
-    parts = pl.pallas_call(
-        functools.partial(last_kernel, chips - 1, tokens, heads),
-        out_shape=shape(ctx, tokens, flat, dtype=bf16),
+    half = everyone // CORES
+    keep, give = pl.pallas_call(
+        functools.partial(last_kernel, chips - 1, heads),
+        out_shape=[shape(half, flat), shape(half, flat, dtype=bf16)],
         in_specs=[SMEM] * 2 + [VMEM] * 8,
-        out_specs=VMEM,
+        out_specs=[VMEM] * 2,
         scratch_shapes=[
             pltpu.VMEM((width, slots), bf16),
             pltpu.VMEM((total, LANES), f32),
@@ -299,15 +297,20 @@
         compiler_params=PARAMS,
         name="last",
     )(prefix_length, table, q, *state, *keys, value_up, far_up)
-    returned = lax.all_to_all(parts, "ctx", split_axis=0, concat_axis=0, tiled=True)
-    return pl.pallas_call(
+    got = lax.ppermute(give, "ctx", other_core)
+    merged = pl.pallas_call(
         functools.partial(merge_kernel, heads),
-        out_shape=shape(tokens, all_heads * V_HEAD, dtype=bf16),
-        in_specs=[VMEM],
+        out_shape=shape(chips, tokens, heads * V_HEAD, dtype=bf16),
+        in_specs=[VMEM] * 2,
         out_specs=VMEM,
+        scratch_shapes=[pltpu.VMEM((half, heads * V_HEAD), f32)],
         compiler_params=PARAMS,
         name="merge",
-    )(returned)
+    )(keep, got)
+    returned = lax.all_to_all(
+        merged, "ctx", split_axis=0, concat_axis=0, axis_index_groups=same_core, tiled=True
+    )
+    return returned.transpose(1, 0, 2).reshape(tokens, all_heads * V_HEAD)
 
 
 def solution(mesh):

time: 61.1 us -> 60.2 us (0.985)
  Pallas kernels: 11.2 us -> 9.56 us
  waiting for transfers between devices: 16.6 us -> 17.9 us
  blocking collectives: 11.7 us -> 10.5 us
  local copies, waits for them, and re-layouts: 0.96 us -> 1.59 us
    pallas_call x2, Pallas kernels: 4.52 us -> 2.95 us  [the longest x1 2.61 us: on_device(): pl.pallas_call(functools.partial(last_kernel, chips - 1, heads), out_shap...]
    all_to_all x1, blocking collectives: 11.7 us -> 10.5 us  [on_device(): lax.all_to_all(merged, 'ctx', split_axis=0, concat_axis=0, axis_index_gro...]
    ppermute x0 -> x1, waiting for transfers between devices: none -> 1.25 us  [on_device(): got = lax.ppermute(give, 'ctx', other_core)]
    unnamed x6 -> x7, local copies, waits for them, and re-layouts: 0.01 us -> 0.64 us
  transfers between devices with their start and end apart: 11 -> 12, of which waited for: 6 -> 7; matrix products, arithmetic and copies ran while one was open for 5% -> 5% of each run, Pallas kernels for 11% -> 11%
where the time goes in v7:
time: 60.2 us; the launch traced here: 59.9 us
  waiting for transfers between devices  17.9 us (30%)
  starting transfers between devices  17 us (28%)
  blocking collectives  10.5 us (17%)
  Pallas kernels  9.56 us (16%)
  other arithmetic  1.97 us (3%)
  local copies, waits for them, and re-layouts  1.59 us (3%)
  between operations  1.42 us (2%)
    all_to_all x1, blocking collectives, on_device(): lax.all_to_all(merged, 'ctx', split_axis=0, concat_axis=0, axis_index_gro...  10.5 us
    all_to_all x1, waiting for transfers between devices, on_device(): lax.all_to_all(pieces, 'ctx', split_axis=0, concat_axis=0, axis_index_gro...  9.23 us
    all_to_all x1, starting transfers between devices, on_device(): lax.all_to_all(pieces, 'ctx', split_axis=0, concat_axis=0, axis_index_gro...  6.25 us
    ppermute x4, waiting for transfers between devices, on_device(): right, left = (onward(right), backward(left))  5.84 us
    ppermute x4, starting transfers between devices, on_device(): right, left = (onward(right), backward(left))  5.43 us
    pallas_call x1, Pallas kernels, fold_first(): pl.pallas_call(functools.partial(first_kernel, heads, len(keys)), out_sha...  4.54 us
    ppermute x2, starting transfers between devices, on_device(): right, left = (onward(own), backward(own))  3.03 us
    pallas_call x1, Pallas kernels, on_device(): pl.pallas_call(functools.partial(last_kernel, chips - 1, heads), out_shap...  2.61 us
  transfers between devices with their start and end apart: 12, of which 7 were waited for; matrix products, arithmetic and copies ran while one was open for 5% of the time, Pallas kernels for 11%

profile of v7, /device:TPU:0, one launch (start us, length us, event | category | flops | bytes accessed | tf_op | source)
XLA Modules:
  0.0 59.9 jit_solution(3418099820544595055)
XLA Ops:
  0.0 2.9 %collective-permute-start = (bf16[576,254]{1,0:T(8,128)(2,1)}, bf16[576,254]{1,0:T(8,128)(2,1)S(1)}, u32[]{:S(2)}, u32[]{:S(2)}) collective-permute-start(bf16[576,254]{1,0:T(8,128)(2,1)} %bitcast.7), channel_id=1, source_target_pairs={{2,6},{3,7},{6,10},{7,11},{10,14},{11,15},{14,12},{15,13},{12,8},{... | collective-permute-start | bytes 877832 | tf_op jit(solution)/shard_map/ppermute | solution.py:253
  2.9 0.1 collective-permute-start.2
  3.0 0.0 collective-permute-start.9
  3.0 0.7 %broadcast_in_dim.2 = bf16[8,2,576]{2,1,0:T(2,128)(2,1)S(1)} broadcast(bf16[2,576]{1,0:T(2,128)(2,1)} %param.9), dimensions={1,2} | broadcast | bytes 20736 | tf_op jit(solution)/shard_map/broadcast_in_dim | solution.py:256
  3.7 2.0 %pad_maximum_fusion = bf16[8,2,9792]{2,1,0:T(2,128)(2,1)} fusion(bf16[8,2,576]{2,1,0:T(2,128)(2,1)S(1)} %broadcast_in_dim.2, bf16[8,2,9216]{2,1,0:T(2,128)(2,1)} %bitcast.10), kind=kLoop, calls=%fused_computation | loop fusion | flops 626688 | bytes 626688 | tf_op jit(solution)/shard_map/concatenate | solution.py:257
  5.7 6.3 %all-to-all-start = ((bf16[8,2,9792]{2,1,0:T(2,128)(2,1)}), bf16[8,2,9792]{2,1,0:T(2,128)(2,1)S(1)}, u32[]{:S(2)}, u32[]{:S(2)}) async-start(bf16[8,2,9792]{2,1,0:T(2,128)(2,1)} %pad_maximum_fusion), calls=%async_computation | async-start | bytes 630784 | tf_op jit(solution)/shard_map/all_to_all | solution.py:258
  11.9 0.0 copy-start.1
  12.0 0.0 collective-permute-done.rest_1_
  12.0 2.1 %collective-permute-start.1 = (bf16[576,254]{1,0:T(8,128)(2,1)S(1)}, bf16[576,254]{1,0:T(8,128)(2,1)S(1)}, u32[]{:S(2)}, u32[]{:S(2)}) collective-permute-start(bf16[576,254]{1,0:T(8,128)(2,1)S(1)} %collective-permute-done.rest_1_), channel_id=1, source_target_pairs={{2,6},{3,7},{6,10},{7,11},{10,14},{11,15},{14,12},{15,13},{12,8},{... | collective-permute-start | bytes 877832 | tf_op jit(solution)/shard_map/ppermute | solution.py:265
  14.0 0.0 collective-permute-done.2.rest_2_
  14.0 0.1 collective-permute-start.3
  14.1 9.2 %all-to-all-done = bf16[8,2,9792]{2,1,0:T(2,128)(2,1)S(1)} async-done(((bf16[8,2,9792]{2,1,0:T(2,128)(2,1)}), bf16[8,2,9792]{2,1,0:T(2,128)(2,1)S(1)}, u32[]{:S(2)}, u32[]{:S(2)}) %all-to-all-start) | async-done | bytes 313376 | tf_op jit(solution)/shard_map/all_to_all | solution.py:258
  23.3 3.0 %collective-permute-done.1.rest_3_ = bf16[576,254]{1,0:T(8,128)(2,1)S(1)} collective-permute-done((bf16[576,254]{1,0:T(8,128)(2,1)S(1)}, bf16[576,254]{1,0:T(8,128)(2,1)S(1)}, u32[]{:S(2)}, u32[]{:S(2)}) %collective-permute-start.1) | collective-permute-done | bytes 292640 | tf_op jit(solution)/shard_map/ppermute | solution.py:265
  26.4 0.0 collective-permute-done.3.rest_4_
  26.4 0.2 reshape.11.here_ref
  26.6 0.1 collective-permute-start.4
  26.7 1.5 %collective-permute-start.5 = (bf16[576,254]{1,0:T(8,128)(2,1)S(1)}, bf16[576,254]{1,0:T(8,128)(2,1)S(1)}, u32[]{:S(2)}, u32[]{:S(2)}) collective-permute-start(bf16[576,254]{1,0:T(8,128)(2,1)S(1)} %collective-permute-done.1.rest_3_), channel_id=1, source_target_pairs={{2,6},{3,7},{6,10},{7,11},{10,14},{11,15},{14,12},{15,13},{12,8},{... | collective-permute-start | bytes 877832 | tf_op jit(solution)/shard_map/ppermute | solution.py:265
  28.2 1.8 %collective-permute-start.6 = (bf16[576,254]{1,0:T(8,128)(2,1)S(1)}, bf16[576,254]{1,0:T(8,128)(2,1)S(1)}, u32[]{:S(2)}, u32[]{:S(2)}) collective-permute-start(bf16[576,254]{1,0:T(8,128)(2,1)S(1)} %collective-permute-done.3.rest_4_), channel_id=1, source_target_pairs={{2,0},{3,1},{6,2},{7,3},{10,6},{11,7},{14,10},{15,11},{12,14},{13,... | collective-permute-start | bytes 877832 | tf_op jit(solution)/shard_map/ppermute | solution.py:265
  30.6 0.0 copy-start.2
  31.3 0.0 collective-permute-done.4.there_ref
  31.3 0.0 copy-done.1
  31.3 0.0 copy-done.2
  31.3 4.5 %first.1 = (bf16[512,576]{1,0:T(8,128)(2,1)S(1)}, f32[512,128]{1,0:T(8,128)S(1)}, f32[512,128]{1,0:T(8,128)S(1)}, f32[512,512]{1,0:T(8,128)S(1)}) custom-call(s32[1]{0:T(128)S(6)} %copy.10.length_ref, s32[1]{0:T(128)S(6)} %copy.11.offset_ref, s32[64]{0:T(128)S(1)} %copy-done.2, bf16[16,9792]{1,0:T(8,128)(2,1)S(1)} %reshape.11.here_ref, ...), custom_call_target="tpu_custom_call" | custom-call | tf_op jit(solution)/shard_map/first/pallas_call | solution.py:230
  35.9 1.6 %collective-permute-done.5.rest_0_ = bf16[576,254]{1,0:T(8,128)(2,1)S(1)} collective-permute-done((bf16[576,254]{1,0:T(8,128)(2,1)S(1)}, bf16[576,254]{1,0:T(8,128)(2,1)S(1)}, u32[]{:S(2)}, u32[]{:S(2)}) %collective-permute-start.5) | collective-permute-done | bytes 292640 | tf_op jit(solution)/shard_map/ppermute | solution.py:265
  37.5 1.2 %collective-permute-done.6.rest_1_ = bf16[576,254]{1,0:T(8,128)(2,1)S(1)} collective-permute-done((bf16[576,254]{1,0:T(8,128)(2,1)S(1)}, bf16[576,254]{1,0:T(8,128)(2,1)S(1)}, u32[]{:S(2)}, u32[]{:S(2)}) %collective-permute-start.6) | collective-permute-done | bytes 292640 | tf_op jit(solution)/shard_map/ppermute | solution.py:265
  38.7 0.6 %collective-permute-start.8 = (bf16[320,254]{1,0:T(8,128)(2,1)S(1)}, bf16[320,254]{1,0:T(8,128)(2,1)S(1)}, u32[]{:S(2)}, u32[]{:S(2)}) collective-permute-start(bf16[320,254]{1,0:T(8,128)(2,1)S(1)} %slice.7), channel_id=1, source_target_pairs={{2,0},{3,1},{6,2},{7,3},{10,6},{11,7},{14,10},{15,11},{12,14},{13,... | collective-permute-start | bytes 487688 | tf_op jit(solution)/shard_map/ppermute | solution.py:280
  39.3 1.5 %collective-permute-start.7 = (bf16[256,254]{1,0:T(8,128)(2,1)S(1)}, bf16[256,254]{1,0:T(8,128)(2,1)S(1)}, u32[]{:S(2)}, u32[]{:S(2)}) collective-permute-start(bf16[256,254]{1,0:T(8,128)(2,1)S(1)} %slice.6), channel_id=1, source_target_pairs={{2,6},{3,7},{6,10},{7,11},{10,14},{11,15},{14,12},{15,13},{12,8},{... | collective-permute-start | bytes 390152 | tf_op jit(solution)/shard_map/ppermute | solution.py:280
  40.8 0.0 copy-start
  40.8 2.1 %middle.1 = (f32[512,128]{1,0:T(8,128)S(1)}, f32[512,128]{1,0:T(8,128)S(1)}, f32[512,512]{1,0:T(8,128)S(1)}) custom-call(s32[1]{0:T(128)S(6)} %copy.10.length_ref, s32[64]{0:T(128)S(1)} %copy-done.2, bf16[512,576]{1,0:T(8,128)(2,1)S(1)} %get-tuple-element.25.q_ref, f32[512,128]{1,0:T(8,128)S(1)} %get-tuple-element.29.m_in, ...), custom_call_target="tpu_custom_call" | custom-call | tf_op jit(solution)/shard_map/middle/pallas_call | solution.py:240
  42.9 1.4 %collective-permute-done.7.top_ref = bf16[256,254]{1,0:T(8,128)(2,1)S(1)} collective-permute-done((bf16[256,254]{1,0:T(8,128)(2,1)S(1)}, bf16[256,254]{1,0:T(8,128)(2,1)S(1)}, u32[]{:S(2)}, u32[]{:S(2)}) %collective-permute-start.7) | collective-permute-done | bytes 130080 | tf_op jit(solution)/shard_map/ppermute | solution.py:280
  44.3 0.0 collective-permute-done.9.far_up
  44.4 0.2 collective-permute-done.8.bottom_ref
  44.5 0.0 copy-done
  44.5 2.6 %last.1 = (f32[16,2176]{1,0:T(8,128)S(1)}, bf16[16,2176]{1,0:T(8,128)(2,1)S(1)}) custom-call(s32[1]{0:T(128)S(6)} %copy.10.length_ref, s32[64]{0:T(128)S(1)} %copy-done.2, bf16[512,576]{1,0:T(8,128)(2,1)S(1)} %get-tuple-element.25.q_ref, f32[512,128]{1,0:T(8,128)S(1)} %get-tuple-element.32.m_in, f32[512,128]{1,0:T(8,128)S(1)} %get-tuple-element.33.l_in, ...), custom_call_target="tpu_custom_call" | custom-call | tf_op jit(solution)/shard_map/last/pallas_call | solution.py:285
  47.1 0.1 collective-permute-start.10
  47.2 1.2 %collective-permute-done.10.got_ref = bf16[16,2176]{1,0:T(8,128)(2,1)S(1)} collective-permute-done((bf16[16,2176]{1,0:T(8,128)(2,1)S(1)}, bf16[16,2176]{1,0:T(8,128)(2,1)S(1)}, u32[]{:S(2)}, u32[]{:S(2)}) %collective-permute-start.10) | collective-permute-done | bytes 69664 | tf_op jit(solution)/shard_map/ppermute | solution.py:300
  48.5 0.3 merge.1
  48.8 10.5 %all_to_all.10 = bf16[8,2,2048]{2,1,0:T(2,128)(2,1)S(1)} all-to-all(bf16[8,2,2048]{2,1,0:T(2,128)(2,1)S(1)} %merge.1), channel_id=1, replica_groups={{0,2,4,6,8,10,12,14},{1,3,5,7,9,11,13,15},{16,18,20,22,24,26,28,30},{17..., dimensions={0} | all-to-all | bytes 131072 | tf_op jit(solution)/shard_map/all_to_all | solution.py:310
  59.3 0.6 %copy.12 = bf16[2,16384]{1,0:T(2,128)(2,1)} copy(bf16[2,16384]{1,0:T(2,128)(2,1)S(1)} %bitcast.11) | data formatting | bytes 131072
  (2 shorter events, 0.0 us)
Async XLA Ops:
  0.0 12.0 %collective-permute-start = (bf16[576,254]{1,0:T(8,128)(2,1)}, bf16[576,254]{1,0:T(8,128)(2,1)S(1)}, u32[]{:S(2)}, u32[]{:S(2)}) collective-permute-start(bf16[576,254]{1,0:T(8,128)(2,1)} %bitcast.7), channel_id=1, source_target_pairs={{2,6},{3,7},{6,10},{7,11},{10,14},{11,15},{14,12},{15,13},{12,8},{... | collective-permute-start | bytes 877832 | tf_op jit(solution)/shard_map/ppermute | solution.py:253
  2.9 11.1 %collective-permute-start.2 = (bf16[576,254]{1,0:T(8,128)(2,1)}, bf16[576,254]{1,0:T(8,128)(2,1)S(1)}, u32[]{:S(2)}, u32[]{:S(2)}) collective-permute-start(bf16[576,254]{1,0:T(8,128)(2,1)} %bitcast.8), channel_id=1, source_target_pairs={{2,0},{3,1},{6,2},{7,3},{10,6},{11,7},{14,10},{15,11},{12,14},{13,... | collective-permute-start | bytes 877832 | tf_op jit(solution)/shard_map/ppermute | solution.py:253
  3.0 41.3 %collective-permute-start.9 = (bf16[8,512,128]{2,1,0:T(8,128)(2,1)}, bf16[8,512,128]{2,1,0:T(8,128)(2,1)S(1)}, u32[]{:S(2)}, u32[]{:S(2)}) collective-permute-start(bf16[8,512,128]{2,1,0:T(8,128)(2,1)} %own_up.1), channel_id=1, source_target_pairs={{0,1},{1,0},{2,3},{3,2},{4,5},{5,4},{6,7},{7,6},{8,9},{9,8},{10,11... | collective-permute-start | bytes 3145736 | tf_op jit(solution)/shard_map/ppermute | solution.py:261
  5.7 17.6 %all-to-all-start = ((bf16[8,2,9792]{2,1,0:T(2,128)(2,1)}), bf16[8,2,9792]{2,1,0:T(2,128)(2,1)S(1)}, u32[]{:S(2)}, u32[]{:S(2)}) async-start(bf16[8,2,9792]{2,1,0:T(2,128)(2,1)} %pad_maximum_fusion), calls=%async_computation | async-start | bytes 630784 | tf_op jit(solution)/shard_map/all_to_all | solution.py:258
  11.9 19.4 %copy-start.1 = (bf16[254,576]{0,1:T(8,128)(2,1)S(1)}, bf16[254,576]{0,1:T(8,128)(2,1)}, u32[]{:S(2)}) copy-start(bf16[254,576]{0,1:T(8,128)(2,1)} %param.8) | copy-start | bytes 877828
  12.0 14.4 %collective-permute-start.1 = (bf16[576,254]{1,0:T(8,128)(2,1)S(1)}, bf16[576,254]{1,0:T(8,128)(2,1)S(1)}, u32[]{:S(2)}, u32[]{:S(2)}) collective-permute-start(bf16[576,254]{1,0:T(8,128)(2,1)S(1)} %collective-permute-done.rest_1_), channel_id=1, source_target_pairs={{2,6},{3,7},{6,10},{7,11},{10,14},{11,15},{14,12},{15,13},{12,8},{... | collective-permute-start | bytes 877832 | tf_op jit(solution)/shard_map/ppermute | solution.py:265
  14.0 12.3 %collective-permute-start.3 = (bf16[576,254]{1,0:T(8,128)(2,1)S(1)}, bf16[576,254]{1,0:T(8,128)(2,1)S(1)}, u32[]{:S(2)}, u32[]{:S(2)}) collective-permute-start(bf16[576,254]{1,0:T(8,128)(2,1)S(1)} %collective-permute-done.2.rest_2_), channel_id=1, source_target_pairs={{2,0},{3,1},{6,2},{7,3},{10,6},{11,7},{14,10},{15,11},{12,14},{13,... | collective-permute-start | bytes 877832 | tf_op jit(solution)/shard_map/ppermute | solution.py:265
  26.6 4.7 %collective-permute-start.4 = (bf16[16,9792]{1,0:T(8,128)(2,1)S(1)}, bf16[16,9792]{1,0:T(8,128)(2,1)S(1)}, u32[]{:S(2)}, u32[]{:S(2)}) collective-permute-start(bf16[16,9792]{1,0:T(8,128)(2,1)S(1)} %reshape.11.here_ref), channel_id=1, source_target_pairs={{0,1},{1,0},{2,3},{3,2},{4,5},{5,4},{6,7},{7,6},{8,9},{9,8},{10,11... | collective-permute-start | bytes 940040 | tf_op jit(solution)/shard_map/ppermute | solution.py:271
  26.7 10.8 %collective-permute-start.5 = (bf16[576,254]{1,0:T(8,128)(2,1)S(1)}, bf16[576,254]{1,0:T(8,128)(2,1)S(1)}, u32[]{:S(2)}, u32[]{:S(2)}) collective-permute-start(bf16[576,254]{1,0:T(8,128)(2,1)S(1)} %collective-permute-done.1.rest_3_), channel_id=1, source_target_pairs={{2,6},{3,7},{6,10},{7,11},{10,14},{11,15},{14,12},{15,13},{12,8},{... | collective-permute-start | bytes 877832 | tf_op jit(solution)/shard_map/ppermute | solution.py:265
  28.2 10.5 %collective-permute-start.6 = (bf16[576,254]{1,0:T(8,128)(2,1)S(1)}, bf16[576,254]{1,0:T(8,128)(2,1)S(1)}, u32[]{:S(2)}, u32[]{:S(2)}) collective-permute-start(bf16[576,254]{1,0:T(8,128)(2,1)S(1)} %collective-permute-done.3.rest_4_), channel_id=1, source_target_pairs={{2,0},{3,1},{6,2},{7,3},{10,6},{11,7},{14,10},{15,11},{12,14},{13,... | collective-permute-start | bytes 877832 | tf_op jit(solution)/shard_map/ppermute | solution.py:265
  30.6 0.7 %copy-start.2 = (s32[64]{0:T(128)S(1)}, s32[64]{0:T(128)}, u32[]{:S(2)}) copy-start(s32[64]{0:T(128)} %constant.2.clone.table_ref) | copy-start | bytes 772
  38.7 5.8 %collective-permute-start.8 = (bf16[320,254]{1,0:T(8,128)(2,1)S(1)}, bf16[320,254]{1,0:T(8,128)(2,1)S(1)}, u32[]{:S(2)}, u32[]{:S(2)}) collective-permute-start(bf16[320,254]{1,0:T(8,128)(2,1)S(1)} %slice.7), channel_id=1, source_target_pairs={{2,0},{3,1},{6,2},{7,3},{10,6},{11,7},{14,10},{15,11},{12,14},{13,... | collective-permute-start | bytes 487688 | tf_op jit(solution)/shard_map/ppermute | solution.py:280
  39.3 5.0 %collective-permute-start.7 = (bf16[256,254]{1,0:T(8,128)(2,1)S(1)}, bf16[256,254]{1,0:T(8,128)(2,1)S(1)}, u32[]{:S(2)}, u32[]{:S(2)}) collective-permute-start(bf16[256,254]{1,0:T(8,128)(2,1)S(1)} %slice.6), channel_id=1, source_target_pairs={{2,6},{3,7},{6,10},{7,11},{10,14},{11,15},{14,12},{15,13},{12,8},{... | collective-permute-start | bytes 390152 | tf_op jit(solution)/shard_map/ppermute | solution.py:280
  40.8 3.7 %copy-start = (bf16[8,512,128]{2,1,0:T(8,128)(2,1)S(1)}, bf16[8,512,128]{2,1,0:T(8,128)(2,1)}, u32[]{:S(2)}) copy-start(bf16[8,512,128]{2,1,0:T(8,128)(2,1)} %own_up.1) | copy-start | bytes 3145732
  47.1 1.3 %collective-permute-start.10 = (bf16[16,2176]{1,0:T(8,128)(2,1)S(1)}, bf16[16,2176]{1,0:T(8,128)(2,1)S(1)}, u32[]{:S(2)}, u32[]{:S(2)}) collective-permute-start(bf16[16,2176]{1,0:T(8,128)(2,1)S(1)} %get-tuple-element.38), channel_id=1, source_target_pairs={{0,1},{1,0},{2,3},{3,2},{4,5},{5,4},{6,7},{7,6},{8,9},{9,8},{10,11... | collective-permute-start | bytes 208904 | tf_op jit(solution)/shard_map/ppermute | solution.py:300

commit v8 on v7

--- a/solution.py
+++ b/solution.py
@@ -82,7 +82,7 @@
     return shards
 
 
-def first_kernel(heads, count, length_ref, offset_ref, table_ref, here_ref, there_ref, *rest):
+def first_kernel(heads, count, scal_ref, table_ref, here_ref, there_ref, *rest):
     keys, (q_ref, m_ref, l_ref, acc_ref) = rest[:count], rest[count:]
     chips = lax.axis_size("ctx") // CORES
     half = here_ref.shape[0]
@@ -104,7 +104,7 @@
         ) * score_scale
         row_index = start + lax.broadcasted_iota(jnp.int32, (block, 1), 0)
         row_token = token_of(row_index & (half * CORES - 1), tokens, chips)
-        shown = (key_token >= offset_ref[0]) & (key_token <= row_token)
+        shown = (key_token >= scal_ref[1]) & (key_token <= row_token)
         s = jnp.where(shown, s, neg_large)
         m_new = jnp.maximum(jnp.max(s, axis=1, keepdims=True), least_max)
         probs = jnp.exp2(s - m_new)
@@ -115,21 +115,32 @@
         m_ref[part, :] = jnp.broadcast_to(m_new, (block, LANES))
         l_ref[part, :] = jnp.broadcast_to(l_new, (block, LANES))
     state = (m_ref, l_ref, acc_ref)
-    fold_shards(q_ref, with_base(table_ref, 0, keys), length_ref[0], state, state)
-
-
-def middle_kernel(at, count, length_ref, table_ref, q_ref, m_in, l_in, acc_in, *rest):
+    fold_shards(q_ref, with_base(table_ref, 0, keys), scal_ref[0], state, state)
+
+
+def middle_kernel(at, count, scal_ref, table_ref, q_ref, m_in, l_in, acc_in, *rest):
     keys, new = rest[:count], rest[count:]
-    fold_shards(q_ref, with_base(table_ref, at, keys), length_ref[0], (m_in, l_in, acc_in), new)
-
-
-def last_kernel(at, heads, length_ref, table_ref, q_ref, m_in, l_in, acc_in,
+    fold_shards(q_ref, with_base(table_ref, at, keys), scal_ref[0], (m_in, l_in, acc_in), new)
+
+
+def join_halves(halves, key_refs):
+    for top_ref, bottom_ref, key_ref in zip(halves[::2], halves[1::2], key_refs):
+        cut = top_ref.shape[0]
+        key_ref[:cut, :] = top_ref[...]
+        key_ref[cut:, :] = bottom_ref[...]
+
+
+def halves_kernel(at, scal_ref, table_ref, q_ref, m_in, l_in, acc_in, *rest):
+    halves, new, keys = rest[:4], rest[4:7], rest[7:]
+    join_halves(halves, keys)
+    middle_kernel(at, 2, scal_ref, table_ref, q_ref, m_in, l_in, acc_in, *keys, *new)
+
+
+def last_kernel(at, heads, scal_ref, table_ref, q_ref, m_in, l_in, acc_in,
                 top_ref, bottom_ref, own_up, far_up, keep_ref, give_ref,
                 key_ref, m_ref, l_ref, acc_ref, flat_ref):
-    cut = top_ref.shape[0]
-    key_ref[:cut, :] = top_ref[...]
-    key_ref[cut:, :] = bottom_ref[...]
-    middle_kernel(at, 1, length_ref, table_ref, q_ref, m_in, l_in, acc_in,
+    join_halves((top_ref, bottom_ref), (key_ref,))
+    middle_kernel(at, 1, scal_ref, table_ref, q_ref, m_in, l_in, acc_in,
                   key_ref, m_ref, l_ref, acc_ref)
     acc_ref[...] = acc_ref[...] / l_ref[:, :1]
     m_ref[...] = m_ref[...] + jnp.log2(l_ref[...])
@@ -181,8 +192,18 @@
             + got_ref[:, lanes].astype(f32) * rest[:, j:j + 1]
         )
     chips, tokens, _ = out_ref.shape
+    here = lax.axis_index("ctx") // CORES
     for chip in range(chips):
-        out_ref[chip] = flat_ref[chip * tokens:(chip + 1) * tokens, :].astype(bf16)
+        out_ref[here ^ chip] = flat_ref[chip * tokens:(chip + 1) * tokens, :].astype(bf16)
+
+
+def place_kernel(kept_ref, moved_ref, out_ref):
+    here = lax.axis_index("ctx") // CORES
+    half, _, width = kept_ref.shape
+    for o in range(half):
+        for far, ref in enumerate((kept_ref, moved_ref)):
+            lanes = pl.ds(pl.multiple_of((here ^ (o + far * half)) * width, width), width)
+            out_ref[:, lanes] = ref[o]
 
 
 VMEM = pl.BlockSpec(memory_space=pltpu.VMEM)
@@ -230,11 +251,11 @@
         return pl.pallas_call(
             functools.partial(first_kernel, heads, len(keys)),
             out_shape=[shape(total, width, dtype=bf16)] + state_shapes,
-            in_specs=[SMEM] * 3 + [VMEM] * (2 + len(keys)),
+            in_specs=[SMEM] * 2 + [VMEM] * (2 + len(keys)),
             out_specs=[VMEM] * 4,
             compiler_params=PARAMS,
             name="first",
-        )(prefix_length, span_offset, table, here, there, *keys)
+        )(scal, table, here, there, *keys)
 
     def fold_more(at, q, state, keys):
         return pl.pallas_call(
@@ -244,7 +265,7 @@
             out_specs=[VMEM] * 3,
             compiler_params=PARAMS,
             name="middle",
-        )(prefix_length, table, q, *state, *keys)
+        )(scal, table, q, *state, *keys)
 
     onward = functools.partial(lax.ppermute, axis_name="ctx", perm=across(1))
     backward = functools.partial(lax.ppermute, axis_name="ctx", perm=across(-1))
@@ -255,18 +276,19 @@
     grouped = queries.reshape(tokens, chips, heads * width).transpose(1, 0, 2)
     spans = jnp.broadcast_to(span_latents[None], (chips, tokens, width))
     pieces = jnp.concatenate([grouped, spans], axis=2)
+    scal = jnp.concatenate([prefix_length, span_offset])
+    pieces, scal = lax.optimization_barrier((pieces, scal))
     here = lax.all_to_all(
         pieces, "ctx", split_axis=0, concat_axis=0, axis_index_groups=same_core, tiled=True
     )
     far_up = lax.ppermute(value_up, "ctx", other_core)
 
     keys, state, at = [own, right, left], None, 0
-    for s in range(2, steps):
+    for s in range(2, steps - 1):
         right, left = onward(right), backward(left)
         keys += [right, left]
         if s == 2:
-            right, left, here = lax.optimization_barrier((right, left, here))
-            keys[-2:] = right, left
+            here, _, _ = lax.optimization_barrier((here, right, left))
             here = here.reshape(chips * tokens, (heads + 1) * width)
             there = lax.ppermute(here, "ctx", other_core)
             continue
@@ -276,10 +298,24 @@
             state = fold_more(at, q, state, keys[:-2])
         at += len(keys) - 2
         keys = keys[-2:]
-    right, left, state = lax.optimization_barrier((right, left, state))
-    right, left = onward(right[:cut]), backward(left[cut:])
-    state = fold_more(at, q, state, keys)
-    keys = [right, left]
+    right_top, left_bottom = onward(right[:cut]), backward(left[cut:])
+    right_bottom, left_top = onward(right[cut:]), backward(left[:cut])
+    far_top, far_bottom = onward(right_top), backward(left_bottom)
+    if state is None:
+        q, *state = fold_first(keys)
+    else:
+        state = fold_more(at, q, state, keys)
+    at += len(keys)
+    state = pl.pallas_call(
+        functools.partial(halves_kernel, at),
+        out_shape=state_shapes,
+        in_specs=[SMEM] * 2 + [VMEM] * 8,
+        out_specs=[VMEM] * 3,
+        scratch_shapes=[pltpu.VMEM((width, slots), bf16)] * 2,
+        compiler_params=PARAMS,
+        name="halves",
+    )(scal, table, q, *state, right_top, right_bottom, left_top, left_bottom)
+    keys = [far_top, far_bottom]
     flat = heads * V_HEAD + LANES
     half = everyone // CORES
     keep, give = pl.pallas_call(
@@ -296,7 +332,7 @@
         ],
         compiler_params=PARAMS,
         name="last",
-    )(prefix_length, table, q, *state, *keys, value_up, far_up)
+    )(scal, table, q, *state, *keys, value_up, far_up)
     got = lax.ppermute(give, "ctx", other_core)
     merged = pl.pallas_call(
         functools.partial(merge_kernel, heads),
@@ -307,10 +343,23 @@
         compiler_params=PARAMS,
         name="merge",
     )(keep, got)
-    returned = lax.all_to_all(
-        merged, "ctx", split_axis=0, concat_axis=0, axis_index_groups=same_core, tiled=True
-    )
-    return returned.transpose(1, 0, 2).reshape(tokens, all_heads * V_HEAD)
+    slot = [merged[o] for o in range(chips)]
+    bit = 1
+    while bit < chips:
+        away = [o for o in range(chips) if o & bit]
+        swap = [(d, d ^ (bit * CORES)) for d in range(ctx)]
+        moved = lax.ppermute(jnp.stack([slot[o] for o in away]), "ctx", swap)
+        for j, o in enumerate(away):
+            slot[o] = moved[j]
+        bit *= 2
+    return pl.pallas_call(
+        place_kernel,
+        out_shape=shape(tokens, all_heads * V_HEAD, dtype=bf16),
+        in_specs=[VMEM] * 2,
+        out_specs=VMEM,
+        compiler_params=PARAMS,
+        name="place",
+    )(jnp.stack(slot[:chips // 2]), moved)
 
 
 def solution(mesh):

time: 60.2 us -> 64.5 us (1.071)
  blocking collectives: 10.5 us -> 0 us
  starting transfers between devices: 17 us -> 26.2 us
  waiting for transfers between devices: 17.9 us -> 23.6 us
  local copies, waits for them, and re-layouts: 1.59 us -> 0.41 us
  Pallas kernels: 9.56 us -> 10.3 us
    ppermute x2 -> x9, starting transfers between devices: 2.13 us -> 14.7 us  [the longest x3 5.38 us: on_device(): moved = lax.ppermute(jnp.stack([slot[o] for o in away]), 'ctx', swap)]
    all_to_all x1 -> x0, blocking collectives: 10.5 us -> none  [on_device(): lax.all_to_all(merged, 'ctx', split_axis=0, concat_axis=0, axis_index_gro...]
    ppermute x2 -> x9, waiting for transfers between devices: 1.59 us -> 10 us  [the longest x3 7.41 us: on_device(): moved = lax.ppermute(jnp.stack([slot[o] for o in away]), 'ctx', swap)]
    ppermute x4 -> x2, starting transfers between devices: 5.43 us -> 2.09 us  [on_device(): right, left = (onward(right), backward(left))]
    ppermute x4 -> x2, waiting for transfers between devices: 5.84 us -> 3.03 us  [on_device(): right, left = (onward(right), backward(left))]
    broadcast_in_dim x1, local copies, waits for them, and re-layouts: 0.7 us -> 0.01 us  [on_device(): spans = jnp.broadcast_to(span_latents[None], (chips, tokens, width))]
    pallas_call x1 -> x2, Pallas kernels: 2.07 us -> 2.73 us  [the longest x1 2.1 us: on_device(): pl.pallas_call(functools.partial(halves_kernel, at), out_shape=state_shap...]
  transfers between devices with their start and end apart: 12 -> 17, of which waited for: 7 -> 8; matrix products, arithmetic and copies ran while one was open for 5% -> 4% of each run, Pallas kernels for 11% -> 10%
where the time goes in v8:
time: 64.5 us; the launch traced here: 64.3 us
  starting transfers between devices  26.2 us (41%)
  waiting for transfers between devices  23.6 us (37%)
  Pallas kernels  10.3 us (16%)
  other arithmetic  2.27 us (4%)
  between operations  1.49 us (2%)
    all_to_all x1, waiting for transfers between devices, on_device(): lax.all_to_all(pieces, 'ctx', split_axis=0, concat_axis=0, axis_index_gro...  9.29 us
    ppermute x3, waiting for transfers between devices, on_device(): moved = lax.ppermute(jnp.stack([slot[o] for o in away]), 'ctx', swap)  7.41 us
    all_to_all x1, starting transfers between devices, on_device(): lax.all_to_all(pieces, 'ctx', split_axis=0, concat_axis=0, axis_index_gro...  6.2 us
    ppermute x3, starting transfers between devices, on_device(): moved = lax.ppermute(jnp.stack([slot[o] for o in away]), 'ctx', swap)  5.38 us
    pallas_call x1, Pallas kernels, fold_first(): pl.pallas_call(functools.partial(first_kernel, heads, len(keys)), out_sha...  4.58 us
    ppermute x2, starting transfers between devices, on_device(): far_top, far_bottom = (onward(right_top), backward(left_bottom))  4.18 us
    ppermute x2, starting transfers between devices, on_device(): right_top, left_bottom = (onward(right[:cut]), backward(left[cut:]))  3.26 us
    ppermute x2, starting transfers between devices, on_device(): right, left = (onward(own), backward(own))  3.07 us
  transfers between devices with their start and end apart: 17, of which 8 were waited for; matrix products, arithmetic and copies ran while one was open for 4% of the time, Pallas kernels for 10%

profile of v8, /device:TPU:0, one launch (start us, length us, event | category | flops | bytes accessed | tf_op | source)
XLA Modules:
  0.0 64.3 jit_solution(9093675908454818740)
XLA Ops:
  0.0 0.0 copy-start.3
  0.0 2.9 %collective-permute-start = (bf16[576,254]{1,0:T(8,128)(2,1)}, bf16[576,254]{1,0:T(8,128)(2,1)S(1)}, u32[]{:S(2)}, u32[]{:S(2)}) collective-permute-start(bf16[576,254]{1,0:T(8,128)(2,1)} %bitcast.4), channel_id=1, source_target_pairs={{2,6},{3,7},{6,10},{7,11},{10,14},{11,15},{14,12},{15,13},{12,8},{... | collective-permute-start | bytes 877832 | tf_op jit(solution)/shard_map/ppermute | solution.py:274
  2.9 0.1 collective-permute-start.2
  3.1 0.0 collective-permute-start.11
  4.4 0.0 copy-done.3
  4.4 2.0 %pad_maximum_fusion = bf16[8,2,9792]{2,1,0:T(2,128)(2,1)} fusion(bf16[8,2,576]{2,1,0:T(2,128)(2,1)S(1)} %broadcast_in_dim.2, bf16[8,2,9216]{2,1,0:T(2,128)(2,1)} %bitcast.7), kind=kLoop, calls=%fused_computation | loop fusion | flops 626688 | bytes 626688 | tf_op jit(solution)/shard_map/concatenate | solution.py:278
  6.4 0.1 pad_add_fusion.scal_ref
  6.5 6.2 %all-to-all-start = ((bf16[8,2,9792]{2,1,0:T(2,128)(2,1)}), bf16[8,2,9792]{2,1,0:T(2,128)(2,1)S(1)}, u32[]{:S(2)}, u32[]{:S(2)}) async-start(bf16[8,2,9792]{2,1,0:T(2,128)(2,1)} %pad_maximum_fusion), calls=%async_computation | async-start | bytes 630784 | tf_op jit(solution)/shard_map/all_to_all | solution.py:281
  12.7 0.0 collective-permute-done.rest_1_
  12.7 2.0 %collective-permute-start.1 = (bf16[576,254]{1,0:T(8,128)(2,1)S(1)}, bf16[576,254]{1,0:T(8,128)(2,1)S(1)}, u32[]{:S(2)}, u32[]{:S(2)}) collective-permute-start(bf16[576,254]{1,0:T(8,128)(2,1)S(1)} %collective-permute-done.rest_1_), channel_id=1, source_target_pairs={{2,6},{3,7},{6,10},{7,11},{10,14},{11,15},{14,12},{15,13},{12,8},{... | collective-permute-start | bytes 877832 | tf_op jit(solution)/shard_map/ppermute | solution.py:288
  14.7 0.0 collective-permute-done.2.rest_2_
  14.7 0.1 collective-permute-start.3
  14.8 9.3 %all-to-all-done = bf16[8,2,9792]{2,1,0:T(2,128)(2,1)S(1)} async-done(((bf16[8,2,9792]{2,1,0:T(2,128)(2,1)}), bf16[8,2,9792]{2,1,0:T(2,128)(2,1)S(1)}, u32[]{:S(2)}, u32[]{:S(2)}) %all-to-all-start) | async-done | bytes 313376 | tf_op jit(solution)/shard_map/all_to_all | solution.py:281
  24.1 3.0 %collective-permute-done.1.rest_3_ = bf16[576,254]{1,0:T(8,128)(2,1)S(1)} collective-permute-done((bf16[576,254]{1,0:T(8,128)(2,1)S(1)}, bf16[576,254]{1,0:T(8,128)(2,1)S(1)}, u32[]{:S(2)}, u32[]{:S(2)}) %collective-permute-start.1) | collective-permute-done | bytes 292640 | tf_op jit(solution)/shard_map/ppermute | solution.py:288
  27.1 0.0 collective-permute-done.3.rest_4_
  27.1 0.2 reshape.8.here_ref
  27.3 0.1 collective-permute-start.4
  27.4 3.2 %collective-permute-start.8 = (bf16[320,254]{1,0:T(8,128)(2,1)S(1)}, bf16[320,254]{1,0:T(8,128)(2,1)S(1)}, u32[]{:S(2)}, u32[]{:S(2)}) collective-permute-start(bf16[320,254]{1,0:T(8,128)(2,1)S(1)} %slice.79), channel_id=1, source_target_pairs={{2,0},{3,1},{6,2},{7,3},{10,6},{11,7},{14,10},{15,11},{12,14},{13,... | collective-permute-start | bytes 487688 | tf_op jit(solution)/shard_map/ppermute | solution.py:301
  30.6 0.0 copy-start.1
  30.7 0.1 collective-permute-start.5
  30.7 0.0 copy-start.2
  30.7 1.5 %collective-permute-start.6 = (bf16[320,254]{1,0:T(8,128)(2,1)S(1)}, bf16[320,254]{1,0:T(8,128)(2,1)S(1)}, u32[]{:S(2)}, u32[]{:S(2)}) collective-permute-start(bf16[320,254]{1,0:T(8,128)(2,1)S(1)} %slice.77), channel_id=1, source_target_pairs={{2,6},{3,7},{6,10},{7,11},{10,14},{11,15},{14,12},{15,13},{12,8},{... | collective-permute-start | bytes 487688 | tf_op jit(solution)/shard_map/ppermute | solution.py:302
  32.3 2.5 %collective-permute-done.8.rest_3_ = bf16[320,254]{1,0:T(8,128)(2,1)S(1)} collective-permute-done((bf16[320,254]{1,0:T(8,128)(2,1)S(1)}, bf16[320,254]{1,0:T(8,128)(2,1)S(1)}, u32[]{:S(2)}, u32[]{:S(2)}) %collective-permute-start.8) | collective-permute-done | bytes 162592 | tf_op jit(solution)/shard_map/ppermute | solution.py:301
  34.7 2.5 %collective-permute-start.10 = (bf16[320,254]{1,0:T(8,128)(2,1)S(1)}, bf16[320,254]{1,0:T(8,128)(2,1)S(1)}, u32[]{:S(2)}, u32[]{:S(2)}) collective-permute-start(bf16[320,254]{1,0:T(8,128)(2,1)S(1)} %collective-permute-done.8.rest_3_), channel_id=1, source_target_pairs={{2,0},{3,1},{6,2},{7,3},{10,6},{11,7},{14,10},{15,11},{12,14},{13,... | collective-permute-start | bytes 487688 | tf_op jit(solution)/shard_map/ppermute | solution.py:303
  37.2 0.0 collective-permute-done.5.rest_0_
  37.2 0.4 collective-permute-start.7
  37.6 0.0 collective-permute-done.4.there_ref
  37.6 1.7 %collective-permute-start.9 = (bf16[256,254]{1,0:T(8,128)(2,1)S(1)}, bf16[256,254]{1,0:T(8,128)(2,1)S(1)}, u32[]{:S(2)}, u32[]{:S(2)}) collective-permute-start(bf16[256,254]{1,0:T(8,128)(2,1)S(1)} %collective-permute-done.5.rest_0_), channel_id=1, source_target_pairs={{2,6},{3,7},{6,10},{7,11},{10,14},{11,15},{14,12},{15,13},{12,8},{... | collective-permute-start | bytes 390152 | tf_op jit(solution)/shard_map/ppermute | solution.py:303
  39.3 0.0 copy-done.1
  39.3 0.0 copy-done.2
  39.3 4.6 %first.1 = (bf16[512,576]{1,0:T(8,128)(2,1)S(1)}, f32[512,128]{1,0:T(8,128)S(1)}, f32[512,128]{1,0:T(8,128)S(1)}, f32[512,512]{1,0:T(8,128)S(1)}) custom-call(s32[2]{0:T(128)S(1)} %pad_add_fusion.scal_ref, s32[64]{0:T(128)S(1)} %copy-done.2, bf16[16,9792]{1,0:T(8,128)(2,1)S(1)} %reshape.8.here_ref, bf16[16,9792]{1,0:T(8,128)(2,1)S(1)} %collective-permute-done.4.there_ref, ...), custom_call_target="tpu_custom_call" | custom-call | tf_op jit(solution)/shard_map/first/pallas_call | solution.py:251
  43.9 0.1 collective-permute-done.7.rest_2_
  44.0 0.0 collective-permute-done.6.rest_1_
  44.0 0.0 copy-start
  44.0 2.1 %halves.1 = (f32[512,128]{1,0:T(8,128)S(1)}, f32[512,128]{1,0:T(8,128)S(1)}, f32[512,512]{1,0:T(8,128)S(1)}) custom-call(s32[2]{0:T(128)S(1)} %pad_add_fusion.scal_ref, s32[64]{0:T(128)S(1)} %copy-done.2, bf16[512,576]{1,0:T(8,128)(2,1)S(1)} %get-tuple-element.20.q_ref, f32[512,128]{1,0:T(8,128)S(1)} %get-tuple-element.21.m_in, ...), custom_call_target="tpu_custom_call" | custom-call | tf_op jit(solution)/shard_map/halves/pallas_call | solution.py:309
  46.1 0.0 collective-permute-done.9.top_ref
  46.1 0.0 collective-permute-done.10.bottom_ref
  46.1 0.0 collective-permute-done.11.far_up
  46.1 0.0 copy-done
  46.2 2.6 %last.1 = (f32[16,2176]{1,0:T(8,128)S(1)}, bf16[16,2176]{1,0:T(8,128)(2,1)S(1)}) custom-call(s32[2]{0:T(128)S(1)} %pad_add_fusion.scal_ref, s32[64]{0:T(128)S(1)} %copy-done.2, bf16[512,576]{1,0:T(8,128)(2,1)S(1)} %get-tuple-element.20.q_ref, f32[512,128]{1,0:T(8,128)S(1)} %get-tuple-element.24.m_in, f32[512,128]{1,0:T(8,128)S(1)} %get-tuple-element.25.l_in, ...), custom_call_target="tpu_custom_call" | custom-call | tf_op jit(solution)/shard_map/last/pallas_call | solution.py:321
  48.8 0.1 collective-permute-start.12
  48.9 1.2 %collective-permute-done.12.got_ref = bf16[16,2176]{1,0:T(8,128)(2,1)S(1)} collective-permute-done((bf16[16,2176]{1,0:T(8,128)(2,1)S(1)}, bf16[16,2176]{1,0:T(8,128)(2,1)S(1)}, u32[]{:S(2)}, u32[]{:S(2)}) %collective-permute-start.12) | collective-permute-done | bytes 69664 | tf_op jit(solution)/shard_map/ppermute | solution.py:336
  50.1 0.3 merge.1
  50.5 0.1 pad_maximum_fusion.1
  50.6 1.8 %collective-permute-start.13 = (bf16[4,2,2048]{2,1,0:T(2,128)(2,1)S(1)}, bf16[4,2,2048]{2,1,0:T(2,128)(2,1)S(1)}, u32[]{:S(2)}, u32[]{:S(2)}) collective-permute-start(bf16[4,2,2048]{2,1,0:T(2,128)(2,1)S(1)} %pad_maximum_fusion.1), channel_id=1, source_target_pairs={{0,2},{1,3},{2,0},{3,1},{4,6},{5,7},{6,4},{7,5},{8,10},{9,11},{10,... | collective-permute-start | bytes 98312 | tf_op jit(solution)/shard_map/ppermute | solution.py:351
  52.4 2.2 %collective-permute-done.13 = bf16[4,2,2048]{2,1,0:T(2,128)(2,1)S(1)} collective-permute-done((bf16[4,2,2048]{2,1,0:T(2,128)(2,1)S(1)}, bf16[4,2,2048]{2,1,0:T(2,128)(2,1)S(1)}, u32[]{:S(2)}, u32[]{:S(2)}) %collective-permute-start.13) | collective-permute-done | bytes 32800 | tf_op jit(solution)/shard_map/ppermute | solution.py:351
  54.6 0.1 pad_maximum_fusion.2
  54.7 1.9 %collective-permute-start.14 = (bf16[4,2,2048]{2,1,0:T(2,128)(2,1)S(1)}, bf16[4,2,2048]{2,1,0:T(2,128)(2,1)S(1)}, u32[]{:S(2)}, u32[]{:S(2)}) collective-permute-start(bf16[4,2,2048]{2,1,0:T(2,128)(2,1)S(1)} %pad_maximum_fusion.2), channel_id=1, source_target_pairs={{0,4},{1,5},{2,6},{3,7},{4,0},{5,1},{6,2},{7,3},{8,12},{9,13},{10,... | collective-permute-start | bytes 98312 | tf_op jit(solution)/shard_map/ppermute | solution.py:351
  56.6 2.1 %collective-permute-done.14 = bf16[4,2,2048]{2,1,0:T(2,128)(2,1)S(1)} collective-permute-done((bf16[4,2,2048]{2,1,0:T(2,128)(2,1)S(1)}, bf16[4,2,2048]{2,1,0:T(2,128)(2,1)S(1)}, u32[]{:S(2)}, u32[]{:S(2)}) %collective-permute-start.14) | collective-permute-done | bytes 32800 | tf_op jit(solution)/shard_map/ppermute | solution.py:351
  58.7 0.1 pad_maximum_fusion.4
  58.7 1.7 %collective-permute-start.15 = (bf16[4,2,2048]{2,1,0:T(2,128)(2,1)S(1)}, bf16[4,2,2048]{2,1,0:T(2,128)(2,1)S(1)}, u32[]{:S(2)}, u32[]{:S(2)}) collective-permute-start(bf16[4,2,2048]{2,1,0:T(2,128)(2,1)S(1)} %pad_maximum_fusion.4), channel_id=1, source_target_pairs={{0,8},{1,9},{2,10},{3,11},{4,12},{5,13},{6,14},{7,15},{8,0},{9,1},... | collective-permute-start | bytes 98312 | tf_op jit(solution)/shard_map/ppermute | solution.py:351
  60.4 0.1 pad_maximum_fusion.3.kept_ref
  60.5 3.2 %collective-permute-done.15.moved_ref = bf16[4,2,2048]{2,1,0:T(2,128)(2,1)S(1)} collective-permute-done((bf16[4,2,2048]{2,1,0:T(2,128)(2,1)S(1)}, bf16[4,2,2048]{2,1,0:T(2,128)(2,1)S(1)}, u32[]{:S(2)}, u32[]{:S(2)}) %collective-permute-start.15) | collective-permute-done | bytes 32800 | tf_op jit(solution)/shard_map/ppermute | solution.py:351
  63.6 0.6 place.1
  (8 shorter events, 0.2 us)
Async XLA Ops:
  0.0 4.4 %copy-start.3 = (bf16[2,576]{1,0:T(2,128)(2,1)S(1)}, bf16[2,576]{1,0:T(2,128)(2,1)}, u32[]{:S(2)}) copy-start(bf16[2,576]{1,0:T(2,128)(2,1)} %param.9) | copy-start | bytes 6916
  0.0 12.7 %collective-permute-start = (bf16[576,254]{1,0:T(8,128)(2,1)}, bf16[576,254]{1,0:T(8,128)(2,1)S(1)}, u32[]{:S(2)}, u32[]{:S(2)}) collective-permute-start(bf16[576,254]{1,0:T(8,128)(2,1)} %bitcast.4), channel_id=1, source_target_pairs={{2,6},{3,7},{6,10},{7,11},{10,14},{11,15},{14,12},{15,13},{12,8},{... | collective-permute-start | bytes 877832 | tf_op jit(solution)/shard_map/ppermute | solution.py:274
  2.9 11.8 %collective-permute-start.2 = (bf16[576,254]{1,0:T(8,128)(2,1)}, bf16[576,254]{1,0:T(8,128)(2,1)S(1)}, u32[]{:S(2)}, u32[]{:S(2)}) collective-permute-start(bf16[576,254]{1,0:T(8,128)(2,1)} %bitcast.5), channel_id=1, source_target_pairs={{2,0},{3,1},{6,2},{7,3},{10,6},{11,7},{14,10},{15,11},{12,14},{13,... | collective-permute-start | bytes 877832 | tf_op jit(solution)/shard_map/ppermute | solution.py:274
  3.1 43.1 %collective-permute-start.11 = (bf16[8,512,128]{2,1,0:T(8,128)(2,1)}, bf16[8,512,128]{2,1,0:T(8,128)(2,1)S(1)}, u32[]{:S(2)}, u32[]{:S(2)}) collective-permute-start(bf16[8,512,128]{2,1,0:T(8,128)(2,1)} %own_up.1), channel_id=1, source_target_pairs={{0,1},{1,0},{2,3},{3,2},{4,5},{5,4},{6,7},{7,6},{8,9},{9,8},{10,11... | collective-permute-start | bytes 3145736 | tf_op jit(solution)/shard_map/ppermute | solution.py:284
  6.5 17.6 %all-to-all-start = ((bf16[8,2,9792]{2,1,0:T(2,128)(2,1)}), bf16[8,2,9792]{2,1,0:T(2,128)(2,1)S(1)}, u32[]{:S(2)}, u32[]{:S(2)}) async-start(bf16[8,2,9792]{2,1,0:T(2,128)(2,1)} %pad_maximum_fusion), calls=%async_computation | async-start | bytes 630784 | tf_op jit(solution)/shard_map/all_to_all | solution.py:281
  12.7 14.4 %collective-permute-start.1 = (bf16[576,254]{1,0:T(8,128)(2,1)S(1)}, bf16[576,254]{1,0:T(8,128)(2,1)S(1)}, u32[]{:S(2)}, u32[]{:S(2)}) collective-permute-start(bf16[576,254]{1,0:T(8,128)(2,1)S(1)} %collective-permute-done.rest_1_), channel_id=1, source_target_pairs={{2,6},{3,7},{6,10},{7,11},{10,14},{11,15},{14,12},{15,13},{12,8},{... | collective-permute-start | bytes 877832 | tf_op jit(solution)/shard_map/ppermute | solution.py:288
  14.7 12.4 %collective-permute-start.3 = (bf16[576,254]{1,0:T(8,128)(2,1)S(1)}, bf16[576,254]{1,0:T(8,128)(2,1)S(1)}, u32[]{:S(2)}, u32[]{:S(2)}) collective-permute-start(bf16[576,254]{1,0:T(8,128)(2,1)S(1)} %collective-permute-done.2.rest_2_), channel_id=1, source_target_pairs={{2,0},{3,1},{6,2},{7,3},{10,6},{11,7},{14,10},{15,11},{12,14},{13,... | collective-permute-start | bytes 877832 | tf_op jit(solution)/shard_map/ppermute | solution.py:288
  27.3 10.3 %collective-permute-start.4 = (bf16[16,9792]{1,0:T(8,128)(2,1)S(1)}, bf16[16,9792]{1,0:T(8,128)(2,1)S(1)}, u32[]{:S(2)}, u32[]{:S(2)}) collective-permute-start(bf16[16,9792]{1,0:T(8,128)(2,1)S(1)} %reshape.8.here_ref), channel_id=1, source_target_pairs={{0,1},{1,0},{2,3},{3,2},{4,5},{5,4},{6,7},{7,6},{8,9},{9,8},{10,11... | collective-permute-start | bytes 940040 | tf_op jit(solution)/shard_map/ppermute | solution.py:293
  27.4 7.3 %collective-permute-start.8 = (bf16[320,254]{1,0:T(8,128)(2,1)S(1)}, bf16[320,254]{1,0:T(8,128)(2,1)S(1)}, u32[]{:S(2)}, u32[]{:S(2)}) collective-permute-start(bf16[320,254]{1,0:T(8,128)(2,1)S(1)} %slice.79), channel_id=1, source_target_pairs={{2,0},{3,1},{6,2},{7,3},{10,6},{11,7},{14,10},{15,11},{12,14},{13,... | collective-permute-start | bytes 487688 | tf_op jit(solution)/shard_map/ppermute | solution.py:301
  30.6 8.7 %copy-start.1 = (bf16[254,576]{0,1:T(8,128)(2,1)S(1)}, bf16[254,576]{0,1:T(8,128)(2,1)}, u32[]{:S(2)}) copy-start(bf16[254,576]{0,1:T(8,128)(2,1)} %param.8) | copy-start | bytes 877828
  30.7 6.6 %collective-permute-start.5 = (bf16[256,254]{1,0:T(8,128)(2,1)S(1)}, bf16[256,254]{1,0:T(8,128)(2,1)S(1)}, u32[]{:S(2)}, u32[]{:S(2)}) collective-permute-start(bf16[256,254]{1,0:T(8,128)(2,1)S(1)} %slice.76), channel_id=1, source_target_pairs={{2,6},{3,7},{6,10},{7,11},{10,14},{11,15},{14,12},{15,13},{12,8},{... | collective-permute-start | bytes 390152 | tf_op jit(solution)/shard_map/ppermute | solution.py:301
  30.7 8.6 %copy-start.2 = (s32[64]{0:T(128)S(1)}, s32[64]{0:T(128)}, u32[]{:S(2)}) copy-start(s32[64]{0:T(128)} %constant.2.clone.table_ref) | copy-start | bytes 772
  30.7 13.3 %collective-permute-start.6 = (bf16[320,254]{1,0:T(8,128)(2,1)S(1)}, bf16[320,254]{1,0:T(8,128)(2,1)S(1)}, u32[]{:S(2)}, u32[]{:S(2)}) collective-permute-start(bf16[320,254]{1,0:T(8,128)(2,1)S(1)} %slice.77), channel_id=1, source_target_pairs={{2,6},{3,7},{6,10},{7,11},{10,14},{11,15},{14,12},{15,13},{12,8},{... | collective-permute-start | bytes 487688 | tf_op jit(solution)/shard_map/ppermute | solution.py:302
  34.7 11.4 %collective-permute-start.10 = (bf16[320,254]{1,0:T(8,128)(2,1)S(1)}, bf16[320,254]{1,0:T(8,128)(2,1)S(1)}, u32[]{:S(2)}, u32[]{:S(2)}) collective-permute-start(bf16[320,254]{1,0:T(8,128)(2,1)S(1)} %collective-permute-done.8.rest_3_), channel_id=1, source_target_pairs={{2,0},{3,1},{6,2},{7,3},{10,6},{11,7},{14,10},{15,11},{12,14},{13,... | collective-permute-start | bytes 487688 | tf_op jit(solution)/shard_map/ppermute | solution.py:303
  37.2 6.8 %collective-permute-start.7 = (bf16[256,254]{1,0:T(8,128)(2,1)S(1)}, bf16[256,254]{1,0:T(8,128)(2,1)S(1)}, u32[]{:S(2)}, u32[]{:S(2)}) collective-permute-start(bf16[256,254]{1,0:T(8,128)(2,1)S(1)} %slice.78), channel_id=1, source_target_pairs={{2,0},{3,1},{6,2},{7,3},{10,6},{11,7},{14,10},{15,11},{12,14},{13,... | collective-permute-start | bytes 390152 | tf_op jit(solution)/shard_map/ppermute | solution.py:302
  37.6 8.5 %collective-permute-start.9 = (bf16[256,254]{1,0:T(8,128)(2,1)S(1)}, bf16[256,254]{1,0:T(8,128)(2,1)S(1)}, u32[]{:S(2)}, u32[]{:S(2)}) collective-permute-start(bf16[256,254]{1,0:T(8,128)(2,1)S(1)} %collective-permute-done.5.rest_0_), channel_id=1, source_target_pairs={{2,6},{3,7},{6,10},{7,11},{10,14},{11,15},{14,12},{15,13},{12,8},{... | collective-permute-start | bytes 390152 | tf_op jit(solution)/shard_map/ppermute | solution.py:303
  44.0 2.1 %copy-start = (bf16[8,512,128]{2,1,0:T(8,128)(2,1)S(1)}, bf16[8,512,128]{2,1,0:T(8,128)(2,1)}, u32[]{:S(2)}) copy-start(bf16[8,512,128]{2,1,0:T(8,128)(2,1)} %own_up.1) | copy-start | bytes 3145732
  48.8 1.3 %collective-permute-start.12 = (bf16[16,2176]{1,0:T(8,128)(2,1)S(1)}, bf16[16,2176]{1,0:T(8,128)(2,1)S(1)}, u32[]{:S(2)}, u32[]{:S(2)}) collective-permute-start(bf16[16,2176]{1,0:T(8,128)(2,1)S(1)} %get-tuple-element.28), channel_id=1, source_target_pairs={{0,1},{1,0},{2,3},{3,2},{4,5},{5,4},{6,7},{7,6},{8,9},{9,8},{10,11... | collective-permute-start | bytes 208904 | tf_op jit(solution)/shard_map/ppermute | solution.py:336
  50.6 4.0 %collective-permute-start.13 = (bf16[4,2,2048]{2,1,0:T(2,128)(2,1)S(1)}, bf16[4,2,2048]{2,1,0:T(2,128)(2,1)S(1)}, u32[]{:S(2)}, u32[]{:S(2)}) collective-permute-start(bf16[4,2,2048]{2,1,0:T(2,128)(2,1)S(1)} %pad_maximum_fusion.1), channel_id=1, source_target_pairs={{0,2},{1,3},{2,0},{3,1},{4,6},{5,7},{6,4},{7,5},{8,10},{9,11},{10,... | collective-permute-start | bytes 98312 | tf_op jit(solution)/shard_map/ppermute | solution.py:351
  54.7 4.0 %collective-permute-start.14 = (bf16[4,2,2048]{2,1,0:T(2,128)(2,1)S(1)}, bf16[4,2,2048]{2,1,0:T(2,128)(2,1)S(1)}, u32[]{:S(2)}, u32[]{:S(2)}) collective-permute-start(bf16[4,2,2048]{2,1,0:T(2,128)(2,1)S(1)} %pad_maximum_fusion.2), channel_id=1, source_target_pairs={{0,4},{1,5},{2,6},{3,7},{4,0},{5,1},{6,2},{7,3},{8,12},{9,13},{10,... | collective-permute-start | bytes 98312 | tf_op jit(solution)/shard_map/ppermute | solution.py:351
  58.7 4.9 %collective-permute-start.15 = (bf16[4,2,2048]{2,1,0:T(2,128)(2,1)S(1)}, bf16[4,2,2048]{2,1,0:T(2,128)(2,1)S(1)}, u32[]{:S(2)}, u32[]{:S(2)}) collective-permute-start(bf16[4,2,2048]{2,1,0:T(2,128)(2,1)S(1)} %pad_maximum_fusion.4), channel_id=1, source_target_pairs={{0,8},{1,9},{2,10},{3,11},{4,12},{5,13},{6,14},{7,15},{8,0},{9,1},... | collective-permute-start | bytes 98312 | tf_op jit(solution)/shard_map/ppermute | solution.py:351

commit v9 on v7

--- a/solution.py
+++ b/solution.py
@@ -74,12 +74,19 @@
 
 def with_base(table_ref, at, key_refs):
     me = lax.axis_index("ctx")
-    count = table_ref.shape[0] // (lax.axis_size("ctx") // CORES)
-    shards = []
-    for j, key_ref in enumerate(key_refs):
-        chip = table_ref[(me // CORES) * count + at + j]
-        shards.append(((chip * CORES + me % CORES) * key_ref.shape[1], key_ref))
-    return shards
+    count = table_ref.shape[0] // lax.axis_size("ctx")
+    return [
+        (table_ref[me * count + at + j] * key_ref.shape[1], key_ref)
+        for j, key_ref in enumerate(key_refs)
+    ]
+
+
+def pieces_kernel(queries_ref, span_ref, out_ref):
+    chips = out_ref.shape[0]
+    part = queries_ref.shape[1] // chips
+    for chip in range(chips):
+        out_ref[chip, :, :part] = queries_ref[:, chip * part:(chip + 1) * part]
+        out_ref[chip, :, part:] = span_ref[...]
 
 
 def first_kernel(heads, count, length_ref, offset_ref, table_ref, here_ref, there_ref, *rest):
@@ -209,7 +216,7 @@
 
     def across(step):
         return [
-            (walk[r] * CORES + c, walk[(r + step) % chips] * CORES + c)
+            (walk[r] * CORES + c, walk[(r + (-step if c else step)) % chips] * CORES + c)
             for r in range(chips) for c in range(CORES)
         ]
 
@@ -221,7 +228,11 @@
         turns += [-s, s]
     turns.append(steps)
     owner_table = np.array(
-        [[walk[(spot[p] + t) % chips] for t in turns] for p in range(chips)], np.int32
+        [
+            [walk[(spot[p] + (-t if c else t)) % chips] * CORES + c for t in turns]
+            for p in range(chips) for c in range(CORES)
+        ],
+        np.int32,
     )
     table = jnp.asarray(owner_table.reshape(-1))
     state_shapes = [shape(total, LANES), shape(total, LANES), shape(total, LATENT)]
@@ -252,9 +263,14 @@
     own = prefix_latents.T
     right, left = onward(own), backward(own)
 
-    grouped = queries.reshape(tokens, chips, heads * width).transpose(1, 0, 2)
-    spans = jnp.broadcast_to(span_latents[None], (chips, tokens, width))
-    pieces = jnp.concatenate([grouped, spans], axis=2)
+    pieces = pl.pallas_call(
+        pieces_kernel,
+        out_shape=shape(chips, tokens, (heads + 1) * width, dtype=bf16),
+        in_specs=[VMEM] * 2,
+        out_specs=VMEM,
+        compiler_params=PARAMS,
+        name="pieces",
+    )(queries, span_latents)
     here = lax.all_to_all(
         pieces, "ctx", split_axis=0, concat_axis=0, axis_index_groups=same_core, tiled=True
     )

time: 60.2 us -> 59.7 us (level)
  other arithmetic: 1.97 us -> 0 us
  local copies, waits for them, and re-layouts: 1.59 us -> 2.54 us
  Pallas kernels: 9.56 us -> 10.3 us
    concatenate x1 -> x0, other arithmetic: 1.97 us -> none  [on_device(): pieces = jnp.concatenate([grouped, spans], axis=2)]
    ppermute x4, waiting for transfers between devices: 5.84 us -> 3.91 us  [on_device(): right, left = (onward(right), backward(left))]
    unnamed x7 -> x11, local copies, waits for them, and re-layouts: 0.64 us -> 2.29 us
    ppermute x2, waiting for transfers between devices: 1.59 us -> 2.86 us  [on_device(): right, left = (onward(right[:cut]), backward(left[cut:]))]
    pallas_call x0 -> x1, Pallas kernels: none -> 0.74 us  [on_device(): pl.pallas_call(pieces_kernel, out_shape=shape(chips, tokens, (heads + 1)...]
    broadcast_in_dim x1 -> x0, local copies, waits for them, and re-layouts: 0.7 us -> none  [on_device(): spans = jnp.broadcast_to(span_latents[None], (chips, tokens, width))]
  transfers between devices with their start and end apart: 12 -> 12, of which waited for: 7 -> 6; matrix products, arithmetic and copies ran while one was open for 5% -> 0% of each run, Pallas kernels for 11% -> 12%
where the time goes in v9:
time: 59.7 us; the launch traced here: 59.3 us
  starting transfers between devices  17.5 us (29%)
  waiting for transfers between devices  17.3 us (29%)
  Pallas kernels  10.3 us (17%)
  blocking collectives  10.3 us (17%)
  local copies, waits for them, and re-layouts  2.54 us (4%)
  between operations  1.44 us (2%)
    all_to_all x1, blocking collectives, on_device(): lax.all_to_all(merged, 'ctx', split_axis=0, concat_axis=0, axis_index_gro...  10.3 us
    all_to_all x1, waiting for transfers between devices, on_device(): lax.all_to_all(pieces, 'ctx', split_axis=0, concat_axis=0, axis_index_gro...  9.23 us
    all_to_all x1, starting transfers between devices, on_device(): lax.all_to_all(pieces, 'ctx', split_axis=0, concat_axis=0, axis_index_gro...  6.25 us
    ppermute x4, starting transfers between devices, on_device(): right, left = (onward(right), backward(left))  5.43 us
    pallas_call x1, Pallas kernels, fold_first(): pl.pallas_call(functools.partial(first_kernel, heads, len(keys)), out_sha...  4.55 us
    ppermute x4, waiting for transfers between devices, on_device(): right, left = (onward(right), backward(left))  3.91 us
    ppermute x2, starting transfers between devices, on_device(): right, left = (onward(own), backward(own))  3.03 us
    ppermute x2, waiting for transfers between devices, on_device(): right, left = (onward(right[:cut]), backward(left[cut:]))  2.86 us
  transfers between devices with their start and end apart: 12, of which 6 were waited for; matrix products, arithmetic and copies ran while one was open for 0% of the time, Pallas kernels for 12%

profile of v9, /device:TPU:0, one launch (start us, length us, event | category | flops | bytes accessed | tf_op | source)
XLA Modules:
  0.0 59.3 jit_solution(12745668892925713790)
XLA Ops:
  0.0 2.9 %collective-permute-start = (bf16[576,254]{1,0:T(8,128)(2,1)}, bf16[576,254]{1,0:T(8,128)(2,1)S(1)}, u32[]{:S(2)}, u32[]{:S(2)}) collective-permute-start(bf16[576,254]{1,0:T(8,128)(2,1)} %bitcast.4), channel_id=1, source_target_pairs={{2,6},{3,1},{6,10},{7,3},{10,14},{11,7},{14,12},{15,11},{12,8},{13... | collective-permute-start | bytes 877832 | tf_op jit(solution)/shard_map/ppermute | solution.py:264
  2.9 0.1 collective-permute-start.2
  3.0 0.0 collective-permute-start.9
  3.0 0.0 copy-start.2
  3.0 1.0 %copy-done.2 = bf16[2,73728]{1,0:T(2,128)(2,1)S(1)} copy-done((bf16[2,73728]{1,0:T(2,128)(2,1)S(1)}, bf16[2,73728]{1,0:T(2,128)(2,1)}, u32[]{:S(2)}) %copy-start.2) | copy-done | bytes 294936
  4.0 0.0 copy-start.4
  4.0 0.7 %copy-done.4 = bf16[2,576]{1,0:T(2,128)(2,1)S(1)} copy-done((bf16[2,576]{1,0:T(2,128)(2,1)S(1)}, bf16[2,576]{1,0:T(2,128)(2,1)}, u32[]{:S(2)}) %copy-start.4) | copy-done | bytes 2328
  4.7 0.7 %pieces.1 = bf16[8,2,9792]{2,1,0:T(2,128)(2,1)} custom-call(bf16[2,73728]{1,0:T(2,128)(2,1)S(1)} %copy-done.2, bf16[2,576]{1,0:T(2,128)(2,1)S(1)} %copy-done.4), custom_call_target="tpu_custom_call" | custom-call | tf_op jit(solution)/shard_map/pieces/pallas_call | solution.py:266
  5.4 6.3 %all-to-all-start = ((bf16[8,2,9792]{2,1,0:T(2,128)(2,1)}), bf16[8,2,9792]{2,1,0:T(2,128)(2,1)S(1)}, u32[]{:S(2)}, u32[]{:S(2)}) async-start(bf16[8,2,9792]{2,1,0:T(2,128)(2,1)} %pieces.1), calls=%async_computation | async-start | bytes 630784 | tf_op jit(solution)/shard_map/all_to_all | solution.py:274
  11.7 0.0 copy-start.1
  11.7 0.0 collective-permute-done.rest_1_
  11.7 2.1 %collective-permute-start.1 = (bf16[576,254]{1,0:T(8,128)(2,1)S(1)}, bf16[576,254]{1,0:T(8,128)(2,1)S(1)}, u32[]{:S(2)}, u32[]{:S(2)}) collective-permute-start(bf16[576,254]{1,0:T(8,128)(2,1)S(1)} %collective-permute-done.rest_1_), channel_id=1, source_target_pairs={{2,6},{3,1},{6,10},{7,3},{10,14},{11,7},{14,12},{15,11},{12,8},{13... | collective-permute-start | bytes 877832 | tf_op jit(solution)/shard_map/ppermute | solution.py:281
  13.8 0.0 collective-permute-done.2.rest_2_
  13.8 0.1 collective-permute-start.3
  13.8 9.2 %all-to-all-done = bf16[8,2,9792]{2,1,0:T(2,128)(2,1)S(1)} async-done(((bf16[8,2,9792]{2,1,0:T(2,128)(2,1)}), bf16[8,2,9792]{2,1,0:T(2,128)(2,1)S(1)}, u32[]{:S(2)}, u32[]{:S(2)}) %all-to-all-start) | async-done | bytes 313376 | tf_op jit(solution)/shard_map/all_to_all | solution.py:274
  23.1 3.0 %collective-permute-done.1.rest_3_ = bf16[576,254]{1,0:T(8,128)(2,1)S(1)} collective-permute-done((bf16[576,254]{1,0:T(8,128)(2,1)S(1)}, bf16[576,254]{1,0:T(8,128)(2,1)S(1)}, u32[]{:S(2)}, u32[]{:S(2)}) %collective-permute-start.1) | collective-permute-done | bytes 292640 | tf_op jit(solution)/shard_map/ppermute | solution.py:281
  26.1 0.0 collective-permute-done.3.rest_4_
  26.1 0.2 reshape.6.here_ref
  26.3 0.1 collective-permute-start.4
  26.4 1.5 %collective-permute-start.5 = (bf16[576,254]{1,0:T(8,128)(2,1)S(1)}, bf16[576,254]{1,0:T(8,128)(2,1)S(1)}, u32[]{:S(2)}, u32[]{:S(2)}) collective-permute-start(bf16[576,254]{1,0:T(8,128)(2,1)S(1)} %collective-permute-done.1.rest_3_), channel_id=1, source_target_pairs={{2,6},{3,1},{6,10},{7,3},{10,14},{11,7},{14,12},{15,11},{12,8},{13... | collective-permute-start | bytes 877832 | tf_op jit(solution)/shard_map/ppermute | solution.py:281
  27.9 1.8 %collective-permute-start.6 = (bf16[576,254]{1,0:T(8,128)(2,1)S(1)}, bf16[576,254]{1,0:T(8,128)(2,1)S(1)}, u32[]{:S(2)}, u32[]{:S(2)}) collective-permute-start(bf16[576,254]{1,0:T(8,128)(2,1)S(1)} %collective-permute-done.3.rest_4_), channel_id=1, source_target_pairs={{2,0},{3,7},{6,2},{7,11},{10,6},{11,15},{14,10},{15,13},{12,14},{1... | collective-permute-start | bytes 877832 | tf_op jit(solution)/shard_map/ppermute | solution.py:281
  30.3 0.0 copy-start.3
  31.0 0.0 collective-permute-done.4.there_ref
  31.0 0.0 copy-done.1
  31.0 0.0 copy-done.3
  31.0 4.5 %first.1 = (bf16[512,576]{1,0:T(8,128)(2,1)S(1)}, f32[512,128]{1,0:T(8,128)S(1)}, f32[512,128]{1,0:T(8,128)S(1)}, f32[512,512]{1,0:T(8,128)S(1)}) custom-call(s32[1]{0:T(128)S(6)} %copy.9.length_ref, s32[1]{0:T(128)S(6)} %copy.10.offset_ref, s32[128]{0:T(128)S(1)} %copy-done.3, bf16[16,9792]{1,0:T(8,128)(2,1)S(1)} %reshape.6.here_ref, ...), custom_call_target="tpu_custom_call" | custom-call | tf_op jit(solution)/shard_map/first/pallas_call | solution.py:241
  35.6 0.6 %collective-permute-done.5.rest_0_ = bf16[576,254]{1,0:T(8,128)(2,1)S(1)} collective-permute-done((bf16[576,254]{1,0:T(8,128)(2,1)S(1)}, bf16[576,254]{1,0:T(8,128)(2,1)S(1)}, u32[]{:S(2)}, u32[]{:S(2)}) %collective-permute-start.5) | collective-permute-done | bytes 292640 | tf_op jit(solution)/shard_map/ppermute | solution.py:281
  36.2 0.3 collective-permute-done.6.rest_1_
  36.5 2.6 %collective-permute-start.8 = (bf16[320,254]{1,0:T(8,128)(2,1)S(1)}, bf16[320,254]{1,0:T(8,128)(2,1)S(1)}, u32[]{:S(2)}, u32[]{:S(2)}) collective-permute-start(bf16[320,254]{1,0:T(8,128)(2,1)S(1)} %slice.7), channel_id=1, source_target_pairs={{2,0},{3,7},{6,2},{7,11},{10,6},{11,15},{14,10},{15,13},{12,14},{1... | collective-permute-start | bytes 487688 | tf_op jit(solution)/shard_map/ppermute | solution.py:296
  39.1 0.1 collective-permute-start.7
  39.2 0.0 copy-start
  39.2 2.1 %middle.1 = (f32[512,128]{1,0:T(8,128)S(1)}, f32[512,128]{1,0:T(8,128)S(1)}, f32[512,512]{1,0:T(8,128)S(1)}) custom-call(s32[1]{0:T(128)S(6)} %copy.9.length_ref, s32[128]{0:T(128)S(1)} %copy-done.3, bf16[512,576]{1,0:T(8,128)(2,1)S(1)} %get-tuple-element.25.q_ref, f32[512,128]{1,0:T(8,128)S(1)} %get-tuple-element.29.m_in, ...), custom_call_target="tpu_custom_call" | custom-call | tf_op jit(solution)/shard_map/middle/pallas_call | solution.py:251
  41.2 2.9 %collective-permute-done.7.top_ref = bf16[256,254]{1,0:T(8,128)(2,1)S(1)} collective-permute-done((bf16[256,254]{1,0:T(8,128)(2,1)S(1)}, bf16[256,254]{1,0:T(8,128)(2,1)S(1)}, u32[]{:S(2)}, u32[]{:S(2)}) %collective-permute-start.7) | collective-permute-done | bytes 130080 | tf_op jit(solution)/shard_map/ppermute | solution.py:296
  44.1 0.0 collective-permute-done.9.far_up
  44.1 0.0 collective-permute-done.8.bottom_ref
  44.1 0.0 copy-done
  44.1 2.6 %last.1 = (f32[16,2176]{1,0:T(8,128)S(1)}, bf16[16,2176]{1,0:T(8,128)(2,1)S(1)}) custom-call(s32[1]{0:T(128)S(6)} %copy.9.length_ref, s32[128]{0:T(128)S(1)} %copy-done.3, bf16[512,576]{1,0:T(8,128)(2,1)S(1)} %get-tuple-element.25.q_ref, f32[512,128]{1,0:T(8,128)S(1)} %get-tuple-element.32.m_in, f32[512,128]{1,0:T(8,128)S(1)} %get-tuple-element.33.l_in, ...), custom_call_target="tpu_custom_call" | custom-call | tf_op jit(solution)/shard_map/last/pallas_call | solution.py:301
  46.7 0.1 collective-permute-start.10
  46.8 1.2 %collective-permute-done.10.got_ref = bf16[16,2176]{1,0:T(8,128)(2,1)S(1)} collective-permute-done((bf16[16,2176]{1,0:T(8,128)(2,1)S(1)}, bf16[16,2176]{1,0:T(8,128)(2,1)S(1)}, u32[]{:S(2)}, u32[]{:S(2)}) %collective-permute-start.10) | collective-permute-done | bytes 69664 | tf_op jit(solution)/shard_map/ppermute | solution.py:316
  48.1 0.3 merge.1
  48.4 10.3 %all_to_all.10 = bf16[8,2,2048]{2,1,0:T(2,128)(2,1)S(1)} all-to-all(bf16[8,2,2048]{2,1,0:T(2,128)(2,1)S(1)} %merge.1), channel_id=1, replica_groups={{0,2,4,6,8,10,12,14},{1,3,5,7,9,11,13,15},{16,18,20,22,24,26,28,30},{17..., dimensions={0} | all-to-all | bytes 131072 | tf_op jit(solution)/shard_map/all_to_all | solution.py:326
  58.7 0.6 %copy.11 = bf16[2,16384]{1,0:T(2,128)(2,1)} copy(bf16[2,16384]{1,0:T(2,128)(2,1)S(1)} %bitcast.7) | data formatting | bytes 131072
  (2 shorter events, 0.0 us)
Async XLA Ops:
  0.0 11.7 %collective-permute-start = (bf16[576,254]{1,0:T(8,128)(2,1)}, bf16[576,254]{1,0:T(8,128)(2,1)S(1)}, u32[]{:S(2)}, u32[]{:S(2)}) collective-permute-start(bf16[576,254]{1,0:T(8,128)(2,1)} %bitcast.4), channel_id=1, source_target_pairs={{2,6},{3,1},{6,10},{7,3},{10,14},{11,7},{14,12},{15,11},{12,8},{13... | collective-permute-start | bytes 877832 | tf_op jit(solution)/shard_map/ppermute | solution.py:264
  2.9 10.8 %collective-permute-start.2 = (bf16[576,254]{1,0:T(8,128)(2,1)}, bf16[576,254]{1,0:T(8,128)(2,1)S(1)}, u32[]{:S(2)}, u32[]{:S(2)}) collective-permute-start(bf16[576,254]{1,0:T(8,128)(2,1)} %bitcast.5), channel_id=1, source_target_pairs={{2,0},{3,7},{6,2},{7,11},{10,6},{11,15},{14,10},{15,13},{12,14},{1... | collective-permute-start | bytes 877832 | tf_op jit(solution)/shard_map/ppermute | solution.py:264
  3.0 41.1 %collective-permute-start.9 = (bf16[8,512,128]{2,1,0:T(8,128)(2,1)}, bf16[8,512,128]{2,1,0:T(8,128)(2,1)S(1)}, u32[]{:S(2)}, u32[]{:S(2)}) collective-permute-start(bf16[8,512,128]{2,1,0:T(8,128)(2,1)} %own_up.1), channel_id=1, source_target_pairs={{0,1},{1,0},{2,3},{3,2},{4,5},{5,4},{6,7},{7,6},{8,9},{9,8},{10,11... | collective-permute-start | bytes 3145736 | tf_op jit(solution)/shard_map/ppermute | solution.py:277
  3.0 1.0 %copy-start.2 = (bf16[2,73728]{1,0:T(2,128)(2,1)S(1)}, bf16[2,73728]{1,0:T(2,128)(2,1)}, u32[]{:S(2)}) copy-start(bf16[2,73728]{1,0:T(2,128)(2,1)} %queries_ref.1) | copy-start | bytes 884740
  4.0 0.7 %copy-start.4 = (bf16[2,576]{1,0:T(2,128)(2,1)S(1)}, bf16[2,576]{1,0:T(2,128)(2,1)}, u32[]{:S(2)}) copy-start(bf16[2,576]{1,0:T(2,128)(2,1)} %span_ref.1) | copy-start | bytes 6916
  5.4 17.6 %all-to-all-start = ((bf16[8,2,9792]{2,1,0:T(2,128)(2,1)}), bf16[8,2,9792]{2,1,0:T(2,128)(2,1)S(1)}, u32[]{:S(2)}, u32[]{:S(2)}) async-start(bf16[8,2,9792]{2,1,0:T(2,128)(2,1)} %pieces.1), calls=%async_computation | async-start | bytes 630784 | tf_op jit(solution)/shard_map/all_to_all | solution.py:274
  11.7 19.4 %copy-start.1 = (bf16[254,576]{0,1:T(8,128)(2,1)S(1)}, bf16[254,576]{0,1:T(8,128)(2,1)}, u32[]{:S(2)}) copy-start(bf16[254,576]{0,1:T(8,128)(2,1)} %param.8) | copy-start | bytes 877828
  11.7 14.4 %collective-permute-start.1 = (bf16[576,254]{1,0:T(8,128)(2,1)S(1)}, bf16[576,254]{1,0:T(8,128)(2,1)S(1)}, u32[]{:S(2)}, u32[]{:S(2)}) collective-permute-start(bf16[576,254]{1,0:T(8,128)(2,1)S(1)} %collective-permute-done.rest_1_), channel_id=1, source_target_pairs={{2,6},{3,1},{6,10},{7,3},{10,14},{11,7},{14,12},{15,11},{12,8},{13... | collective-permute-start | bytes 877832 | tf_op jit(solution)/shard_map/ppermute | solution.py:281
  13.8 12.3 %collective-permute-start.3 = (bf16[576,254]{1,0:T(8,128)(2,1)S(1)}, bf16[576,254]{1,0:T(8,128)(2,1)S(1)}, u32[]{:S(2)}, u32[]{:S(2)}) collective-permute-start(bf16[576,254]{1,0:T(8,128)(2,1)S(1)} %collective-permute-done.2.rest_2_), channel_id=1, source_target_pairs={{2,0},{3,7},{6,2},{7,11},{10,6},{11,15},{14,10},{15,13},{12,14},{1... | collective-permute-start | bytes 877832 | tf_op jit(solution)/shard_map/ppermute | solution.py:281
  26.3 4.7 %collective-permute-start.4 = (bf16[16,9792]{1,0:T(8,128)(2,1)S(1)}, bf16[16,9792]{1,0:T(8,128)(2,1)S(1)}, u32[]{:S(2)}, u32[]{:S(2)}) collective-permute-start(bf16[16,9792]{1,0:T(8,128)(2,1)S(1)} %reshape.6.here_ref), channel_id=1, source_target_pairs={{0,1},{1,0},{2,3},{3,2},{4,5},{5,4},{6,7},{7,6},{8,9},{9,8},{10,11... | collective-permute-start | bytes 940040 | tf_op jit(solution)/shard_map/ppermute | solution.py:287
  26.4 9.8 %collective-permute-start.5 = (bf16[576,254]{1,0:T(8,128)(2,1)S(1)}, bf16[576,254]{1,0:T(8,128)(2,1)S(1)}, u32[]{:S(2)}, u32[]{:S(2)}) collective-permute-start(bf16[576,254]{1,0:T(8,128)(2,1)S(1)} %collective-permute-done.1.rest_3_), channel_id=1, source_target_pairs={{2,6},{3,1},{6,10},{7,3},{10,14},{11,7},{14,12},{15,11},{12,8},{13... | collective-permute-start | bytes 877832 | tf_op jit(solution)/shard_map/ppermute | solution.py:281
  27.9 8.6 %collective-permute-start.6 = (bf16[576,254]{1,0:T(8,128)(2,1)S(1)}, bf16[576,254]{1,0:T(8,128)(2,1)S(1)}, u32[]{:S(2)}, u32[]{:S(2)}) collective-permute-start(bf16[576,254]{1,0:T(8,128)(2,1)S(1)} %collective-permute-done.3.rest_4_), channel_id=1, source_target_pairs={{2,0},{3,7},{6,2},{7,11},{10,6},{11,15},{14,10},{15,13},{12,14},{1... | collective-permute-start | bytes 877832 | tf_op jit(solution)/shard_map/ppermute | solution.py:281
  30.3 0.7 %copy-start.3 = (s32[128]{0:T(128)S(1)}, s32[128]{0:T(128)}, u32[]{:S(2)}) copy-start(s32[128]{0:T(128)} %constant.2.clone.table_ref) | copy-start | bytes 1540
  36.5 7.6 %collective-permute-start.8 = (bf16[320,254]{1,0:T(8,128)(2,1)S(1)}, bf16[320,254]{1,0:T(8,128)(2,1)S(1)}, u32[]{:S(2)}, u32[]{:S(2)}) collective-permute-start(bf16[320,254]{1,0:T(8,128)(2,1)S(1)} %slice.7), channel_id=1, source_target_pairs={{2,0},{3,7},{6,2},{7,11},{10,6},{11,15},{14,10},{15,13},{12,14},{1... | collective-permute-start | bytes 487688 | tf_op jit(solution)/shard_map/ppermute | solution.py:296
  39.1 5.0 %collective-permute-start.7 = (bf16[256,254]{1,0:T(8,128)(2,1)S(1)}, bf16[256,254]{1,0:T(8,128)(2,1)S(1)}, u32[]{:S(2)}, u32[]{:S(2)}) collective-permute-start(bf16[256,254]{1,0:T(8,128)(2,1)S(1)} %slice.6), channel_id=1, source_target_pairs={{2,6},{3,1},{6,10},{7,3},{10,14},{11,7},{14,12},{15,11},{12,8},{13... | collective-permute-start | bytes 390152 | tf_op jit(solution)/shard_map/ppermute | solution.py:296
  39.2 5.0 %copy-start = (bf16[8,512,128]{2,1,0:T(8,128)(2,1)S(1)}, bf16[8,512,128]{2,1,0:T(8,128)(2,1)}, u32[]{:S(2)}) copy-start(bf16[8,512,128]{2,1,0:T(8,128)(2,1)} %own_up.1) | copy-start | bytes 3145732
  46.7 1.3 %collective-permute-start.10 = (bf16[16,2176]{1,0:T(8,128)(2,1)S(1)}, bf16[16,2176]{1,0:T(8,128)(2,1)S(1)}, u32[]{:S(2)}, u32[]{:S(2)}) collective-permute-start(bf16[16,2176]{1,0:T(8,128)(2,1)S(1)} %get-tuple-element.38), channel_id=1, source_target_pairs={{0,1},{1,0},{2,3},{3,2},{4,5},{5,4},{6,7},{7,6},{8,9},{9,8},{10,11... | collective-permute-start | bytes 208904 | tf_op jit(solution)/shard_map/ppermute | solution.py:316

commit v10 on v9

--- a/solution.py
+++ b/solution.py
@@ -111,7 +111,7 @@
         ) * score_scale
         row_index = start + lax.broadcasted_iota(jnp.int32, (block, 1), 0)
         row_token = token_of(row_index & (half * CORES - 1), tokens, chips)
-        shown = (key_token >= offset_ref[0]) & (key_token <= row_token)
+        shown = (key_token >= offset_ref[...]) & (key_token <= row_token)
         s = jnp.where(shown, s, neg_large)
         m_new = jnp.maximum(jnp.max(s, axis=1, keepdims=True), least_max)
         probs = jnp.exp2(s - m_new)
@@ -122,20 +122,17 @@
         m_ref[part, :] = jnp.broadcast_to(m_new, (block, LANES))
         l_ref[part, :] = jnp.broadcast_to(l_new, (block, LANES))
     state = (m_ref, l_ref, acc_ref)
-    fold_shards(q_ref, with_base(table_ref, 0, keys), length_ref[0], state, state)
+    fold_shards(q_ref, with_base(table_ref, 0, keys), length_ref[...], state, state)
 
 
 def middle_kernel(at, count, length_ref, table_ref, q_ref, m_in, l_in, acc_in, *rest):
     keys, new = rest[:count], rest[count:]
-    fold_shards(q_ref, with_base(table_ref, at, keys), length_ref[0], (m_in, l_in, acc_in), new)
+    fold_shards(q_ref, with_base(table_ref, at, keys), length_ref[...], (m_in, l_in, acc_in), new)
 
 
 def last_kernel(at, heads, length_ref, table_ref, q_ref, m_in, l_in, acc_in,
-                top_ref, bottom_ref, own_up, far_up, keep_ref, give_ref,
-                key_ref, m_ref, l_ref, acc_ref, flat_ref):
-    cut = top_ref.shape[0]
-    key_ref[:cut, :] = top_ref[...]
-    key_ref[cut:, :] = bottom_ref[...]
+                key_ref, own_up, far_up, keep_ref, give_ref,
+                m_ref, l_ref, acc_ref, flat_ref):
     middle_kernel(at, 1, length_ref, table_ref, q_ref, m_in, l_in, acc_in,
                   key_ref, m_ref, l_ref, acc_ref)
     acc_ref[...] = acc_ref[...] / l_ref[:, :1]
@@ -235,31 +232,31 @@
         np.int32,
     )
     table = jnp.asarray(owner_table.reshape(-1))
+    length, offset = prefix_length.reshape(1, 1), span_offset.reshape(1, 1)
     state_shapes = [shape(total, LANES), shape(total, LANES), shape(total, LATENT)]
 
     def fold_first(keys):
         return pl.pallas_call(
             functools.partial(first_kernel, heads, len(keys)),
             out_shape=[shape(total, width, dtype=bf16)] + state_shapes,
-            in_specs=[SMEM] * 3 + [VMEM] * (2 + len(keys)),
+            in_specs=[VMEM, VMEM, SMEM] + [VMEM] * (2 + len(keys)),
             out_specs=[VMEM] * 4,
             compiler_params=PARAMS,
             name="first",
-        )(prefix_length, span_offset, table, here, there, *keys)
+        )(length, offset, table, here, there, *keys)
 
     def fold_more(at, q, state, keys):
         return pl.pallas_call(
             functools.partial(middle_kernel, at, len(keys)),
             out_shape=state_shapes,
-            in_specs=[SMEM] * 2 + [VMEM] * (4 + len(keys)),
+            in_specs=[VMEM, SMEM] + [VMEM] * (4 + len(keys)),
             out_specs=[VMEM] * 3,
             compiler_params=PARAMS,
             name="middle",
-        )(prefix_length, table, q, *state, *keys)
+        )(length, table, q, *state, *keys)
 
     onward = functools.partial(lax.ppermute, axis_name="ctx", perm=across(1))
     backward = functools.partial(lax.ppermute, axis_name="ctx", perm=across(-1))
-    cut = LATENT // 2
     own = prefix_latents.T
     right, left = onward(own), backward(own)
 
@@ -279,32 +276,29 @@
     keys, state, at = [own, right, left], None, 0
     for s in range(2, steps):
         right, left = onward(right), backward(left)
-        keys += [right, left]
         if s == 2:
-            right, left, here = lax.optimization_barrier((right, left, here))
-            keys[-2:] = right, left
+            here, right = lax.optimization_barrier((here, right))
             here = here.reshape(chips * tokens, (heads + 1) * width)
             there = lax.ppermute(here, "ctx", other_core)
+            keys += [right, left]
             continue
         if state is None:
-            q, *state = fold_first(keys[:-2])
+            q, *state = fold_first(keys)
         else:
-            state = fold_more(at, q, state, keys[:-2])
-        at += len(keys) - 2
-        keys = keys[-2:]
-    right, left, state = lax.optimization_barrier((right, left, state))
-    right, left = onward(right[:cut]), backward(left[cut:])
+            state = fold_more(at, q, state, keys)
+        at += len(keys)
+        keys = [right, left]
+    right, state = lax.optimization_barrier((right, state))
+    right = onward(right)
     state = fold_more(at, q, state, keys)
-    keys = [right, left]
     flat = heads * V_HEAD + LANES
     half = everyone // CORES
     keep, give = pl.pallas_call(
         functools.partial(last_kernel, chips - 1, heads),
         out_shape=[shape(half, flat), shape(half, flat, dtype=bf16)],
-        in_specs=[SMEM] * 2 + [VMEM] * 8,
+        in_specs=[VMEM, SMEM] + [VMEM] * 7,
         out_specs=[VMEM] * 2,
         scratch_shapes=[
-            pltpu.VMEM((width, slots), bf16),
             pltpu.VMEM((total, LANES), f32),
             pltpu.VMEM((total, LANES), f32),
             pltpu.VMEM((total, LATENT), f32),
@@ -312,7 +306,7 @@
         ],
         compiler_params=PARAMS,
         name="last",
-    )(prefix_length, table, q, *state, *keys, value_up, far_up)
+    )(length, table, q, *state, right, value_up, far_up)
     got = lax.ppermute(give, "ctx", other_core)
     merged = pl.pallas_call(
         functools.partial(merge_kernel, heads),

time: 59.7 us -> 65.6 us (1.099)
  waiting for transfers between devices: 17.3 us -> 23.1 us
  starting transfers between devices: 17.5 us -> 14.8 us
  local copies, waits for them, and re-layouts: 2.54 us -> 4.85 us
    ppermute x4, waiting for transfers between devices: 3.91 us -> 8.25 us  [on_device(): right, left = (onward(right), backward(left))]
    ppermute x2 -> x1, starting transfers between devices: 2.64 us -> 0.06 us  [on_device(): right = onward(right)]
    ppermute x2 -> x1, waiting for transfers between devices: 2.86 us -> 4.6 us  [on_device(): right = onward(right)]
    all_to_all x1, starting transfers between devices: 6.25 us -> 4.88 us  [on_device(): lax.all_to_all(pieces, 'ctx', split_axis=0, concat_axis=0, axis_index_gro...]
    unnamed x11 -> x13, local copies, waits for them, and re-layouts: 2.29 us -> 3.66 us
    ppermute x4, starting transfers between devices: 5.43 us -> 6.59 us  [on_device(): right, left = (onward(right), backward(left))]
    reshape x1, local copies, waits for them, and re-layouts: 0.23 us -> 1.2 us  [on_device(): here = here.reshape(chips * tokens, (heads + 1) * width)]
  transfers between devices with their start and end apart: 12 -> 11, of which waited for: 6 -> 5; matrix products, arithmetic and copies ran while one was open for 0% -> 2% of each run, Pallas kernels for 12% -> 12%
where the time goes in v10:
time: 65.6 us; the launch traced here: 65.2 us
  waiting for transfers between devices  23.1 us (35%)
  starting transfers between devices  14.8 us (23%)
  Pallas kernels  10.7 us (16%)
  blocking collectives  10.3 us (16%)
  local copies, waits for them, and re-layouts  4.85 us (7%)
  between operations  1.41 us (2%)
    all_to_all x1, blocking collectives, on_device(): lax.all_to_all(merged, 'ctx', split_axis=0, concat_axis=0, axis_index_gro...  10.3 us
    all_to_all x1, waiting for transfers between devices, on_device(): lax.all_to_all(pieces, 'ctx', split_axis=0, concat_axis=0, axis_index_gro...  9.02 us
    ppermute x4, waiting for transfers between devices, on_device(): right, left = (onward(right), backward(left))  8.25 us
    ppermute x4, starting transfers between devices, on_device(): right, left = (onward(right), backward(left))  6.59 us
    pallas_call x1, Pallas kernels, fold_first(): pl.pallas_call(functools.partial(first_kernel, heads, len(keys)), out_sha...  4.99 us
    all_to_all x1, starting transfers between devices, on_device(): lax.all_to_all(pieces, 'ctx', split_axis=0, concat_axis=0, axis_index_gro...  4.88 us
    ppermute x1, waiting for transfers between devices, on_device(): right = onward(right)  4.6 us
    unnamed x13, local copies, waits for them, and re-layouts  3.66 us
  transfers between devices with their start and end apart: 11, of which 5 were waited for; matrix products, arithmetic and copies ran while one was open for 2% of the time, Pallas kernels for 12%

profile of v10, /device:TPU:0, one launch (start us, length us, event | category | flops | bytes accessed | tf_op | source)
XLA Modules:
  0.0 65.2 jit_solution(4604171567357662583)
XLA Ops:
  0.0 0.0 copy-start
  0.0 2.9 %collective-permute-start = (bf16[576,254]{1,0:T(8,128)(2,1)}, bf16[576,254]{1,0:T(8,128)(2,1)S(1)}, u32[]{:S(2)}, u32[]{:S(2)}) collective-permute-start(bf16[576,254]{1,0:T(8,128)(2,1)} %bitcast.10), channel_id=1, source_target_pairs={{2,6},{3,1},{6,10},{7,3},{10,14},{11,7},{14,12},{15,11},{12,8},{13... | collective-permute-start | bytes 877832 | tf_op jit(solution)/shard_map/ppermute | solution.py:261
  2.9 0.0 copy-start.2
  2.9 1.0 %copy-done.2 = bf16[2,73728]{1,0:T(2,128)(2,1)S(1)} copy-done((bf16[2,73728]{1,0:T(2,128)(2,1)S(1)}, bf16[2,73728]{1,0:T(2,128)(2,1)}, u32[]{:S(2)}) %copy-start.2) | copy-done | bytes 294936
  3.9 0.0 copy-start.4
  3.9 0.7 %copy-done.4 = bf16[2,576]{1,0:T(2,128)(2,1)S(1)} copy-done((bf16[2,576]{1,0:T(2,128)(2,1)S(1)}, bf16[2,576]{1,0:T(2,128)(2,1)}, u32[]{:S(2)}) %copy-start.4) | copy-done | bytes 2328
  4.6 0.7 %pieces.1 = bf16[8,2,9792]{2,1,0:T(2,128)(2,1)} custom-call(bf16[2,73728]{1,0:T(2,128)(2,1)S(1)} %copy-done.2, bf16[2,576]{1,0:T(2,128)(2,1)S(1)} %copy-done.4), custom_call_target="tpu_custom_call" | custom-call | tf_op jit(solution)/shard_map/pieces/pallas_call | solution.py:263
  5.3 4.9 %all-to-all-start = ((bf16[8,2,9792]{2,1,0:T(2,128)(2,1)}), bf16[8,2,9792]{2,1,0:T(2,128)(2,1)S(1)}, u32[]{:S(2)}, u32[]{:S(2)}) async-start(bf16[8,2,9792]{2,1,0:T(2,128)(2,1)} %pieces.1), calls=%async_computation | async-start | bytes 630784 | tf_op jit(solution)/shard_map/all_to_all | solution.py:271
  10.2 0.0 copy-done
  10.2 0.0 copy-start.1
  10.2 0.1 collective-permute-start.8
  10.3 0.0 collective-permute-done.rest_1_
  10.3 2.1 %collective-permute-start.1 = (bf16[576,254]{1,0:T(8,128)(2,1)S(1)}, bf16[576,254]{1,0:T(8,128)(2,1)S(1)}, u32[]{:S(2)}, u32[]{:S(2)}) collective-permute-start(bf16[576,254]{1,0:T(8,128)(2,1)S(1)} %collective-permute-done.rest_1_), channel_id=1, source_target_pairs={{2,6},{3,1},{6,10},{7,3},{10,14},{11,7},{14,12},{15,11},{12,8},{13... | collective-permute-start | bytes 877832 | tf_op jit(solution)/shard_map/ppermute | solution.py:278
  12.4 0.1 collective-permute-start.3
  12.5 9.0 %all-to-all-done = bf16[8,2,9792]{2,1,0:T(2,128)(2,1)S(1)} async-done(((bf16[8,2,9792]{2,1,0:T(2,128)(2,1)}), bf16[8,2,9792]{2,1,0:T(2,128)(2,1)S(1)}, u32[]{:S(2)}, u32[]{:S(2)}) %all-to-all-start) | async-done | bytes 313376 | tf_op jit(solution)/shard_map/all_to_all | solution.py:271
  21.5 0.0 copy-start.5
  21.5 0.7 %copy-done.5 = bf16[8,2,9792]{2,1,0:T(2,128)(2,1)} copy-done((bf16[8,2,9792]{2,1,0:T(2,128)(2,1)}, bf16[8,2,9792]{2,1,0:T(2,128)(2,1)S(1)}, u32[]{:S(2)}) %copy-start.5) | copy-done | bytes 313368
  22.2 2.3 %collective-permute-done.1.rest_3_ = bf16[576,254]{1,0:T(8,128)(2,1)S(1)} collective-permute-done((bf16[576,254]{1,0:T(8,128)(2,1)S(1)}, bf16[576,254]{1,0:T(8,128)(2,1)S(1)}, u32[]{:S(2)}, u32[]{:S(2)}) %collective-permute-start.1) | collective-permute-done | bytes 292640 | tf_op jit(solution)/shard_map/ppermute | solution.py:278
  24.5 1.2 %reshape.14.here_ref = bf16[16,9792]{1,0:T(8,128)(2,1)S(1)} reshape(bf16[8,2,9792]{2,1,0:T(2,128)(2,1)} %copy-done.5) | data formatting | bytes 626688 | tf_op jit(solution)/shard_map/reshape | solution.py:281
  25.7 0.1 collective-permute-start.2
  25.8 0.0 collective-permute-done.3.rest_2_
  25.8 2.4 %collective-permute-start.4 = (bf16[576,254]{1,0:T(8,128)(2,1)}, bf16[576,254]{1,0:T(8,128)(2,1)S(1)}, u32[]{:S(2)}, u32[]{:S(2)}) collective-permute-start(bf16[576,254]{1,0:T(8,128)(2,1)} %collective-permute-done.3.rest_2_), channel_id=1, source_target_pairs={{2,0},{3,7},{6,2},{7,11},{10,6},{11,15},{14,10},{15,13},{12,14},{1... | collective-permute-start | bytes 877832 | tf_op jit(solution)/shard_map/ppermute | solution.py:278
  28.2 0.0 collective-permute-start.5
  29.5 5.9 %collective-permute-done.4.rest_4_ = bf16[576,254]{1,0:T(8,128)(2,1)S(1)} collective-permute-done((bf16[576,254]{1,0:T(8,128)(2,1)}, bf16[576,254]{1,0:T(8,128)(2,1)S(1)}, u32[]{:S(2)}, u32[]{:S(2)}) %collective-permute-start.4) | collective-permute-done | bytes 292640 | tf_op jit(solution)/shard_map/ppermute | solution.py:278
  35.4 2.1 %collective-permute-start.6 = (bf16[576,254]{1,0:T(8,128)(2,1)S(1)}, bf16[576,254]{1,0:T(8,128)(2,1)S(1)}, u32[]{:S(2)}, u32[]{:S(2)}) collective-permute-start(bf16[576,254]{1,0:T(8,128)(2,1)S(1)} %collective-permute-done.4.rest_4_), channel_id=1, source_target_pairs={{2,0},{3,7},{6,2},{7,11},{10,6},{11,15},{14,10},{15,13},{12,14},{1... | collective-permute-start | bytes 877832 | tf_op jit(solution)/shard_map/ppermute | solution.py:278
  37.6 0.0 collective-permute-done.2.there_ref
  37.6 0.0 copy-start.3
  37.6 0.0 copy-done.1
  37.6 0.7 copy-done.3
  38.2 5.0 %first.1 = (bf16[512,576]{1,0:T(8,128)(2,1)S(1)}, f32[512,128]{1,0:T(8,128)S(1)}, f32[512,128]{1,0:T(8,128)S(1)}, f32[512,512]{1,0:T(8,128)S(1)}) custom-call(s32[1,1]{1,0:T(1,128)} %bitcast.6.length_ref, s32[1,1]{1,0:T(1,128)} %bitcast.9.offset_ref, s32[128]{0:T(128)S(1)} %copy-done.3, bf16[16,9792]{1,0:T(8,128)(2,1)S(1)} %reshape.14.here_ref, ...), custom_call_target="tpu_custom_call" | custom-call | tf_op jit(solution)/shard_map/first/pallas_call | solution.py:239
  43.2 0.0 collective-permute-done.5.rest_0_
  43.2 0.1 collective-permute-start.7
  43.3 0.0 collective-permute-done.6.rest_1_
  43.3 2.1 %middle.1 = (f32[512,128]{1,0:T(8,128)S(1)}, f32[512,128]{1,0:T(8,128)S(1)}, f32[512,512]{1,0:T(8,128)S(1)}) custom-call(s32[1,1]{1,0:T(1,128)} %bitcast.7.length_ref, s32[128]{0:T(128)S(1)} %copy-done.3, bf16[512,576]{1,0:T(8,128)(2,1)S(1)} %get-tuple-element.22.q_ref, f32[512,128]{1,0:T(8,128)S(1)} %get-tuple-element.26.m_in, ...), custom_call_target="tpu_custom_call" | custom-call | tf_op jit(solution)/shard_map/middle/pallas_call | solution.py:249
  45.4 0.0 collective-permute-done.8.far_up
  45.4 4.6 %collective-permute-done.7.key_ref = bf16[576,254]{1,0:T(8,128)(2,1)S(1)} collective-permute-done((bf16[576,254]{1,0:T(8,128)(2,1)S(1)}, bf16[576,254]{1,0:T(8,128)(2,1)S(1)}, u32[]{:S(2)}, u32[]{:S(2)}) %collective-permute-start.7) | collective-permute-done | bytes 292640 | tf_op jit(solution)/shard_map/ppermute | solution.py:292
  50.0 2.6 %last.1 = (f32[16,2176]{1,0:T(8,128)S(1)}, bf16[16,2176]{1,0:T(8,128)(2,1)S(1)}) custom-call(s32[1,1]{1,0:T(1,128)} %bitcast.8.length_ref, s32[128]{0:T(128)S(1)} %copy-done.3, bf16[512,576]{1,0:T(8,128)(2,1)S(1)} %get-tuple-element.22.q_ref, f32[512,128]{1,0:T(8,128)S(1)} %get-tuple-element.29.m_in, f32[512,128]{1,0:T(8,128)S(1)} %get-tuple-element.30.l_in, ...), custom_call_target="tpu_custom_call" | custom-call | tf_op jit(solution)/shard_map/last/pallas_call | solution.py:296
  52.6 0.1 collective-permute-start.9
  52.7 1.2 %collective-permute-done.9.got_ref = bf16[16,2176]{1,0:T(8,128)(2,1)S(1)} collective-permute-done((bf16[16,2176]{1,0:T(8,128)(2,1)S(1)}, bf16[16,2176]{1,0:T(8,128)(2,1)S(1)}, u32[]{:S(2)}, u32[]{:S(2)}) %collective-permute-start.9) | collective-permute-done | bytes 69664 | tf_op jit(solution)/shard_map/ppermute | solution.py:310
  53.9 0.3 merge.1
  54.3 10.3 %all_to_all.10 = bf16[8,2,2048]{2,1,0:T(2,128)(2,1)S(1)} all-to-all(bf16[8,2,2048]{2,1,0:T(2,128)(2,1)S(1)} %merge.1), channel_id=1, replica_groups={{0,2,4,6,8,10,12,14},{1,3,5,7,9,11,13,15},{16,18,20,22,24,26,28,30},{17..., dimensions={0} | all-to-all | bytes 131072 | tf_op jit(solution)/shard_map/all_to_all | solution.py:320
  64.5 0.6 copy.11
Async XLA Ops:
  0.0 10.2 %copy-start = (bf16[8,512,128]{2,1,0:T(8,128)(2,1)S(1)}, bf16[8,512,128]{2,1,0:T(8,128)(2,1)}, u32[]{:S(2)}) copy-start(bf16[8,512,128]{2,1,0:T(8,128)(2,1)} %own_up.1) | copy-start | bytes 3145732
  0.0 10.3 %collective-permute-start = (bf16[576,254]{1,0:T(8,128)(2,1)}, bf16[576,254]{1,0:T(8,128)(2,1)S(1)}, u32[]{:S(2)}, u32[]{:S(2)}) collective-permute-start(bf16[576,254]{1,0:T(8,128)(2,1)} %bitcast.10), channel_id=1, source_target_pairs={{2,6},{3,1},{6,10},{7,3},{10,14},{11,7},{14,12},{15,11},{12,8},{13... | collective-permute-start | bytes 877832 | tf_op jit(solution)/shard_map/ppermute | solution.py:261
  2.9 1.0 %copy-start.2 = (bf16[2,73728]{1,0:T(2,128)(2,1)S(1)}, bf16[2,73728]{1,0:T(2,128)(2,1)}, u32[]{:S(2)}) copy-start(bf16[2,73728]{1,0:T(2,128)(2,1)} %queries_ref.1) | copy-start | bytes 884740
  3.9 0.7 %copy-start.4 = (bf16[2,576]{1,0:T(2,128)(2,1)S(1)}, bf16[2,576]{1,0:T(2,128)(2,1)}, u32[]{:S(2)}) copy-start(bf16[2,576]{1,0:T(2,128)(2,1)} %span_ref.1) | copy-start | bytes 6916
  5.3 16.1 %all-to-all-start = ((bf16[8,2,9792]{2,1,0:T(2,128)(2,1)}), bf16[8,2,9792]{2,1,0:T(2,128)(2,1)S(1)}, u32[]{:S(2)}, u32[]{:S(2)}) async-start(bf16[8,2,9792]{2,1,0:T(2,128)(2,1)} %pieces.1), calls=%async_computation | async-start | bytes 630784 | tf_op jit(solution)/shard_map/all_to_all | solution.py:271
  10.2 27.4 %copy-start.1 = (bf16[254,576]{0,1:T(8,128)(2,1)S(1)}, bf16[254,576]{0,1:T(8,128)(2,1)}, u32[]{:S(2)}) copy-start(bf16[254,576]{0,1:T(8,128)(2,1)} %param.8) | copy-start | bytes 877828
  10.2 35.2 %collective-permute-start.8 = (bf16[8,512,128]{2,1,0:T(8,128)(2,1)S(1)}, bf16[8,512,128]{2,1,0:T(8,128)(2,1)S(1)}, u32[]{:S(2)}, u32[]{:S(2)}) collective-permute-start(bf16[8,512,128]{2,1,0:T(8,128)(2,1)S(1)} %copy-done), channel_id=1, source_target_pairs={{0,1},{1,0},{2,3},{3,2},{4,5},{5,4},{6,7},{7,6},{8,9},{9,8},{10,11... | collective-permute-start | bytes 3145736 | tf_op jit(solution)/shard_map/ppermute | solution.py:274
  10.3 14.2 %collective-permute-start.1 = (bf16[576,254]{1,0:T(8,128)(2,1)S(1)}, bf16[576,254]{1,0:T(8,128)(2,1)S(1)}, u32[]{:S(2)}, u32[]{:S(2)}) collective-permute-start(bf16[576,254]{1,0:T(8,128)(2,1)S(1)} %collective-permute-done.rest_1_), channel_id=1, source_target_pairs={{2,6},{3,1},{6,10},{7,3},{10,14},{11,7},{14,12},{15,11},{12,8},{13... | collective-permute-start | bytes 877832 | tf_op jit(solution)/shard_map/ppermute | solution.py:278
  12.4 13.4 %collective-permute-start.3 = (bf16[576,254]{1,0:T(8,128)(2,1)}, bf16[576,254]{1,0:T(8,128)(2,1)}, u32[]{:S(2)}, u32[]{:S(2)}) collective-permute-start(bf16[576,254]{1,0:T(8,128)(2,1)} %bitcast.11), channel_id=1, source_target_pairs={{2,0},{3,7},{6,2},{7,11},{10,6},{11,15},{14,10},{15,13},{12,14},{1... | collective-permute-start | bytes 877832 | tf_op jit(solution)/shard_map/ppermute | solution.py:261
  21.5 0.7 %copy-start.5 = (bf16[8,2,9792]{2,1,0:T(2,128)(2,1)}, bf16[8,2,9792]{2,1,0:T(2,128)(2,1)S(1)}, u32[]{:S(2)}) copy-start(bf16[8,2,9792]{2,1,0:T(2,128)(2,1)S(1)} %all-to-all-done) | copy-start | bytes 940036
  25.7 11.9 %collective-permute-start.2 = (bf16[16,9792]{1,0:T(8,128)(2,1)S(1)}, bf16[16,9792]{1,0:T(8,128)(2,1)S(1)}, u32[]{:S(2)}, u32[]{:S(2)}) collective-permute-start(bf16[16,9792]{1,0:T(8,128)(2,1)S(1)} %reshape.14.here_ref), channel_id=1, source_target_pairs={{0,1},{1,0},{2,3},{3,2},{4,5},{5,4},{6,7},{7,6},{8,9},{9,8},{10,11... | collective-permute-start | bytes 940040 | tf_op jit(solution)/shard_map/ppermute | solution.py:282
  25.8 9.6 %collective-permute-start.4 = (bf16[576,254]{1,0:T(8,128)(2,1)}, bf16[576,254]{1,0:T(8,128)(2,1)S(1)}, u32[]{:S(2)}, u32[]{:S(2)}) collective-permute-start(bf16[576,254]{1,0:T(8,128)(2,1)} %collective-permute-done.3.rest_2_), channel_id=1, source_target_pairs={{2,0},{3,7},{6,2},{7,11},{10,6},{11,15},{14,10},{15,13},{12,14},{1... | collective-permute-start | bytes 877832 | tf_op jit(solution)/shard_map/ppermute | solution.py:278
  28.2 15.0 %collective-permute-start.5 = (bf16[576,254]{1,0:T(8,128)(2,1)S(1)}, bf16[576,254]{1,0:T(8,128)(2,1)S(1)}, u32[]{:S(2)}, u32[]{:S(2)}) collective-permute-start(bf16[576,254]{1,0:T(8,128)(2,1)S(1)} %collective-permute-done.1.rest_3_), channel_id=1, source_target_pairs={{2,6},{3,1},{6,10},{7,3},{10,14},{11,7},{14,12},{15,11},{12,8},{13... | collective-permute-start | bytes 877832 | tf_op jit(solution)/shard_map/ppermute | solution.py:278
  35.4 7.9 %collective-permute-start.6 = (bf16[576,254]{1,0:T(8,128)(2,1)S(1)}, bf16[576,254]{1,0:T(8,128)(2,1)S(1)}, u32[]{:S(2)}, u32[]{:S(2)}) collective-permute-start(bf16[576,254]{1,0:T(8,128)(2,1)S(1)} %collective-permute-done.4.rest_4_), channel_id=1, source_target_pairs={{2,0},{3,7},{6,2},{7,11},{10,6},{11,15},{14,10},{15,13},{12,14},{1... | collective-permute-start | bytes 877832 | tf_op jit(solution)/shard_map/ppermute | solution.py:278
  37.6 0.7 %copy-start.3 = (s32[128]{0:T(128)S(1)}, s32[128]{0:T(128)}, u32[]{:S(2)}) copy-start(s32[128]{0:T(128)} %constant.2.clone.table_ref) | copy-start | bytes 1540
  43.2 6.8 %collective-permute-start.7 = (bf16[576,254]{1,0:T(8,128)(2,1)S(1)}, bf16[576,254]{1,0:T(8,128)(2,1)S(1)}, u32[]{:S(2)}, u32[]{:S(2)}) collective-permute-start(bf16[576,254]{1,0:T(8,128)(2,1)S(1)} %collective-permute-done.5.rest_0_), channel_id=1, source_target_pairs={{2,6},{3,1},{6,10},{7,3},{10,14},{11,7},{14,12},{15,11},{12,8},{13... | collective-permute-start | bytes 877832 | tf_op jit(solution)/shard_map/ppermute | solution.py:292
  52.6 1.3 %collective-permute-start.9 = (bf16[16,2176]{1,0:T(8,128)(2,1)S(1)}, bf16[16,2176]{1,0:T(8,128)(2,1)S(1)}, u32[]{:S(2)}, u32[]{:S(2)}) collective-permute-start(bf16[16,2176]{1,0:T(8,128)(2,1)S(1)} %get-tuple-element.34), channel_id=1, source_target_pairs={{0,1},{1,0},{2,3},{3,2},{4,5},{5,4},{6,7},{7,6},{8,9},{9,8},{10,11... | collective-permute-start | bytes 208904 | tf_op jit(solution)/shard_map/ppermute | solution.py:310

commit v11 on v9

--- a/solution.py
+++ b/solution.py
@@ -33,30 +33,35 @@
     return walk + [z * wide for z in reversed(range(tall))]
 
 
+def fold_block(part, q_ref, shards, length, old):
+    m_old = old[0][part, :][:, :1]
+    m_new = m_old
+    scores = []
+    for base, key_ref in shards:
+        slot = base + lax.broadcasted_iota(jnp.int32, (1, key_ref.shape[1]), 1)
+        s = jnp.dot(q_ref[part, :], key_ref[...], preferred_element_type=f32) * score_scale
+        s = jnp.where(slot < length, s, neg_large)
+        m_new = jnp.maximum(m_new, jnp.max(s, axis=1, keepdims=True))
+        scores.append(s)
+    shrink = jnp.exp2(m_old - m_new)
+    l_new = old[1][part, :][:, :1] * shrink
+    summed = old[2][part, :] * shrink
+    for s, (_, key_ref) in zip(scores, shards):
+        probs = jnp.exp2(s - m_new)
+        l_new += jnp.sum(probs, axis=1, keepdims=True)
+        summed += lax.dot_general(
+            probs.astype(bf16), key_ref[:LATENT, :], (((1,), (1,)), ((), ())),
+            preferred_element_type=f32,
+        )
+    return m_new, l_new, summed
+
+
 def fold_shards(q_ref, shards, length, old, new):
     rows = q_ref.shape[0]
     block = min(256, rows)
     for start in range(0, rows, block):
         part = pl.ds(start, block)
-        m_old = old[0][part, :][:, :1]
-        m_new = m_old
-        scores = []
-        for base, key_ref in shards:
-            slot = base + lax.broadcasted_iota(jnp.int32, (1, key_ref.shape[1]), 1)
-            s = jnp.dot(q_ref[part, :], key_ref[...], preferred_element_type=f32) * score_scale
-            s = jnp.where(slot < length, s, neg_large)
-            m_new = jnp.maximum(m_new, jnp.max(s, axis=1, keepdims=True))
-            scores.append(s)
-        shrink = jnp.exp2(m_old - m_new)
-        l_new = old[1][part, :][:, :1] * shrink
-        summed = old[2][part, :] * shrink
-        for s, (_, key_ref) in zip(scores, shards):
-            probs = jnp.exp2(s - m_new)
-            l_new += jnp.sum(probs, axis=1, keepdims=True)
-            summed += lax.dot_general(
-                probs.astype(bf16), key_ref[:LATENT, :], (((1,), (1,)), ((), ())),
-                preferred_element_type=f32,
-            )
+        m_new, l_new, summed = fold_block(part, q_ref, shards, length, old)
         new[0][part, :] = jnp.broadcast_to(m_new, (block, LANES))
         new[1][part, :] = jnp.broadcast_to(l_new, (block, LANES))
         new[2][part, :] = summed
@@ -81,7 +86,15 @@
     ]
 
 
-def pieces_kernel(queries_ref, span_ref, out_ref):
+def pieces_kernel(queries_hbm, span_hbm, out_ref, queries_ref, span_ref, sems):
+    copies = [
+        pltpu.make_async_copy(queries_hbm, queries_ref, sems.at[0]),
+        pltpu.make_async_copy(span_hbm, span_ref, sems.at[1]),
+    ]
+    for copy in copies:
+        copy.start()
+    for copy in copies:
+        copy.wait()
     chips = out_ref.shape[0]
     part = queries_ref.shape[1] // chips
     for chip in range(chips):
@@ -130,43 +143,39 @@
     fold_shards(q_ref, with_base(table_ref, at, keys), length_ref[0], (m_in, l_in, acc_in), new)
 
 
-def last_kernel(at, heads, length_ref, table_ref, q_ref, m_in, l_in, acc_in,
-                top_ref, bottom_ref, own_up, far_up, keep_ref, give_ref,
-                key_ref, m_ref, l_ref, acc_ref, flat_ref):
-    cut = top_ref.shape[0]
-    key_ref[:cut, :] = top_ref[...]
-    key_ref[cut:, :] = bottom_ref[...]
-    middle_kernel(at, 1, length_ref, table_ref, q_ref, m_in, l_in, acc_in,
-                  key_ref, m_ref, l_ref, acc_ref)
-    acc_ref[...] = acc_ref[...] / l_ref[:, :1]
-    m_ref[...] = m_ref[...] + jnp.log2(l_ref[...])
+def last_kernel(at, heads, length_ref, table_ref, q_ref, m_ref, l_ref, acc_ref,
+                key_ref, own_up, far_up, keep_ref, give_ref, flat_ref):
+    core = lax.axis_index("ctx") % CORES
+    shards = with_base(table_ref, at, (key_ref,))
     everyone = flat_ref.shape[0]
-    core = lax.axis_index("ctx") % CORES
     per_core = heads // CORES
+    rows = per_core * everyone
+    pair = min(2, per_core)
     tail = jnp.zeros((everyone, LANES), f32)
     lane = lax.broadcasted_iota(jnp.int32, (everyone, LANES), 1)
-    pair = min(2, per_core)
     for side, up_ref in enumerate((own_up, far_up)):
+        part = pl.ds(pl.multiple_of((core ^ side) * rows, rows), rows)
+        m_new, l_new, summed = fold_block(
+            part, q_ref, shards, length_ref[0], (m_ref, l_ref, acc_ref)
+        )
+        context = (summed * (1.0 / l_new)).astype(bf16)
+        weight = m_new + jnp.log2(l_new)
+        high = weight.astype(bf16).astype(f32)
+        mid = (weight - high).astype(bf16).astype(f32)
+        low = weight - high - mid
         for j in range(0, per_core, pair):
-            first_head = (core ^ side) * per_core + j
-            contexts = []
-            for head in [first_head + i for i in range(pair)]:
-                rows = pl.ds(pl.multiple_of(head * everyone, everyone), everyone)
-                contexts.append(acc_ref[rows, :].astype(bf16))
-                weight = m_ref[rows, :]
-                high = weight.astype(bf16).astype(f32)
-                mid = (weight - high).astype(bf16).astype(f32)
-                low = weight - high - mid
-                tail = jnp.where(lane == head, high, tail)
-                tail = jnp.where(lane == head + heads, mid, tail)
-                tail = jnp.where(lane == head + 2 * heads, low, tail)
             lifted = jnp.dot(
-                jnp.concatenate(contexts, axis=0),
+                context[j * everyone:(j + pair) * everyone, :],
                 jnp.concatenate([up_ref[j + i] for i in range(pair)], axis=1),
                 preferred_element_type=f32,
             )
             for i in range(pair):
-                lanes = pl.ds(pl.multiple_of((first_head + i) * V_HEAD, V_HEAD), V_HEAD)
+                head = (core ^ side) * per_core + j + i
+                here = slice((j + i) * everyone, (j + i + 1) * everyone)
+                tail = jnp.where(lane == head, high[here], tail)
+                tail = jnp.where(lane == head + heads, mid[here], tail)
+                tail = jnp.where(lane == head + 2 * heads, low[here], tail)
+                lanes = pl.ds(pl.multiple_of(head * V_HEAD, V_HEAD), V_HEAD)
                 flat_ref[:, lanes] = lifted[
                     i * everyone:(i + 1) * everyone, i * V_HEAD:(i + 1) * V_HEAD
                 ]
@@ -259,16 +268,21 @@
 
     onward = functools.partial(lax.ppermute, axis_name="ctx", perm=across(1))
     backward = functools.partial(lax.ppermute, axis_name="ctx", perm=across(-1))
-    cut = LATENT // 2
     own = prefix_latents.T
     right, left = onward(own), backward(own)
 
+    anywhere = pl.BlockSpec(memory_space=pl.ANY)
     pieces = pl.pallas_call(
         pieces_kernel,
         out_shape=shape(chips, tokens, (heads + 1) * width, dtype=bf16),
-        in_specs=[VMEM] * 2,
+        in_specs=[anywhere] * 2,
         out_specs=VMEM,
-        compiler_params=PARAMS,
+        scratch_shapes=[
+            pltpu.VMEM(queries.shape, bf16),
+            pltpu.VMEM(span_latents.shape, bf16),
+            pltpu.SemaphoreType.DMA((2,)),
+        ],
+        compiler_params=pltpu.CompilerParams(vmem_limit_bytes=56 * 1024 * 1024),
         name="pieces",
     )(queries, span_latents)
     here = lax.all_to_all(
@@ -293,26 +307,19 @@
         at += len(keys) - 2
         keys = keys[-2:]
     right, left, state = lax.optimization_barrier((right, left, state))
-    right, left = onward(right[:cut]), backward(left[cut:])
+    right = onward(right)
     state = fold_more(at, q, state, keys)
-    keys = [right, left]
     flat = heads * V_HEAD + LANES
     half = everyone // CORES
     keep, give = pl.pallas_call(
         functools.partial(last_kernel, chips - 1, heads),
         out_shape=[shape(half, flat), shape(half, flat, dtype=bf16)],
-        in_specs=[SMEM] * 2 + [VMEM] * 8,
+        in_specs=[SMEM] * 2 + [VMEM] * 7,
         out_specs=[VMEM] * 2,
-        scratch_shapes=[
-            pltpu.VMEM((width, slots), bf16),
-            pltpu.VMEM((total, LANES), f32),
-            pltpu.VMEM((total, LANES), f32),
-            pltpu.VMEM((total, LATENT), f32),
-            pltpu.VMEM((everyone, flat), f32),
-        ],
+        scratch_shapes=[pltpu.VMEM((everyone, flat), f32)],
         compiler_params=PARAMS,
         name="last",
-    )(prefix_length, table, q, *state, *keys, value_up, far_up)
+    )(prefix_length, table, q, *state, right, value_up, far_up)
     got = lax.ppermute(give, "ctx", other_core)
     merged = pl.pallas_call(
         functools.partial(merge_kernel, heads),

time: 59.7 us -> 60.1 us (level)
  starting transfers between devices: 17.5 us -> 15.4 us
  Pallas kernels: 10.3 us -> 11.5 us
  blocking collectives: 10.3 us -> 11.3 us
  local copies, waits for them, and re-layouts: 2.54 us -> 3.51 us
  waiting for transfers between devices: 17.3 us -> 16.6 us
    ppermute x2 -> x1, starting transfers between devices: 2.64 us -> 1.32 us  [on_device(): right = onward(right)]
    all_to_all x1, blocking collectives: 10.3 us -> 11.3 us  [on_device(): lax.all_to_all(merged, 'ctx', split_axis=0, concat_axis=0, axis_index_gro...]
    pallas_call x1, Pallas kernels: 0.74 us -> 1.73 us  [on_device(): pl.pallas_call(pieces_kernel, out_shape=shape(chips, tokens, (heads + 1)...]
    reshape x1, local copies, waits for them, and re-layouts: 0.23 us -> 1.2 us  [on_device(): here = here.reshape(chips * tokens, (heads + 1) * width)]
    ppermute x4, waiting for transfers between devices: 3.91 us -> 3 us  [on_device(): right, left = (onward(right), backward(left))]
    ppermute x4, starting transfers between devices: 5.43 us -> 4.53 us  [on_device(): right, left = (onward(right), backward(left))]
    ppermute x2 -> x1, waiting for transfers between devices: 2.86 us -> 3.48 us  [on_device(): right = onward(right)]
  transfers between devices with their start and end apart: 12 -> 11, of which waited for: 6 -> 4; matrix products, arithmetic and copies ran while one was open for 0% -> 2% of each run, Pallas kernels for 12% -> 15%
where the time goes in v11:
time: 60.1 us; the launch traced here: 59.7 us
  waiting for transfers between devices  16.6 us (28%)
  starting transfers between devices  15.4 us (26%)
  Pallas kernels  11.5 us (19%)
  blocking collectives  11.3 us (19%)
  local copies, waits for them, and re-layouts  3.51 us (6%)
  between operations  1.45 us (2%)
    all_to_all x1, blocking collectives, on_device(): lax.all_to_all(merged, 'ctx', split_axis=0, concat_axis=0, axis_index_gro...  11.3 us
    all_to_all x1, waiting for transfers between devices, on_device(): lax.all_to_all(pieces, 'ctx', split_axis=0, concat_axis=0, axis_index_gro...  8.84 us
    all_to_all x1, starting transfers between devices, on_device(): lax.all_to_all(pieces, 'ctx', split_axis=0, concat_axis=0, axis_index_gro...  6.22 us
    pallas_call x1, Pallas kernels, fold_first(): pl.pallas_call(functools.partial(first_kernel, heads, len(keys)), out_sha...  4.98 us
    ppermute x4, starting transfers between devices, on_device(): right, left = (onward(right), backward(left))  4.53 us
    ppermute x1, waiting for transfers between devices, on_device(): right = onward(right)  3.48 us
    ppermute x2, starting transfers between devices, on_device(): right, left = (onward(own), backward(own))  3.07 us
    ppermute x4, waiting for transfers between devices, on_device(): right, left = (onward(right), backward(left))  3 us
  transfers between devices with their start and end apart: 11, of which 4 were waited for; matrix products, arithmetic and copies ran while one was open for 2% of the time, Pallas kernels for 15%

profile of v11, /device:TPU:0, one launch (start us, length us, event | category | flops | bytes accessed | tf_op | source)
XLA Modules:
  0.0 59.7 jit_solution(17295958312546657103)
XLA Ops:
  0.0 0.0 copy-start
  0.0 2.9 %collective-permute-start = (bf16[576,254]{1,0:T(8,128)(2,1)}, bf16[576,254]{1,0:T(8,128)(2,1)S(1)}, u32[]{:S(2)}, u32[]{:S(2)}) collective-permute-start(bf16[576,254]{1,0:T(8,128)(2,1)} %bitcast.4), channel_id=1, source_target_pairs={{2,6},{3,1},{6,10},{7,3},{10,14},{11,7},{14,12},{15,11},{12,8},{13... | collective-permute-start | bytes 877832 | tf_op jit(solution)/shard_map/ppermute | solution.py:272
  2.9 0.1 collective-permute-start.2
  3.1 1.7 %pieces.1 = bf16[8,2,9792]{2,1,0:T(2,128)(2,1)} custom-call(bf16[2,73728]{1,0:T(2,128)(2,1)} %queries_hbm.1, bf16[2,576]{1,0:T(2,128)(2,1)} %span_hbm.1), custom_call_target="tpu_custom_call" | custom-call | tf_op jit(solution)/shard_map/pieces/pallas_call | solution.py:275
  4.8 6.2 %all-to-all-start = ((bf16[8,2,9792]{2,1,0:T(2,128)(2,1)}), bf16[8,2,9792]{2,1,0:T(2,128)(2,1)}, u32[]{:S(2)}, u32[]{:S(2)}) async-start(bf16[8,2,9792]{2,1,0:T(2,128)(2,1)} %pieces.1), calls=%async_computation | async-start | bytes 630784 | tf_op jit(solution)/shard_map/all_to_all | solution.py:288
  11.0 0.0 copy-done
  11.0 0.0 copy-start.1
  11.0 0.1 collective-permute-start.8
  11.1 0.0 collective-permute-done.rest_1_
  11.1 2.1 %collective-permute-start.1 = (bf16[576,254]{1,0:T(8,128)(2,1)S(1)}, bf16[576,254]{1,0:T(8,128)(2,1)S(1)}, u32[]{:S(2)}, u32[]{:S(2)}) collective-permute-start(bf16[576,254]{1,0:T(8,128)(2,1)S(1)} %collective-permute-done.rest_1_), channel_id=1, source_target_pairs={{2,6},{3,1},{6,10},{7,3},{10,14},{11,7},{14,12},{15,11},{12,8},{13... | collective-permute-start | bytes 877832 | tf_op jit(solution)/shard_map/ppermute | solution.py:295
  13.2 0.0 collective-permute-done.2.rest_2_
  13.2 0.1 collective-permute-start.3
  13.3 8.8 %all-to-all-done = bf16[8,2,9792]{2,1,0:T(2,128)(2,1)} async-done(((bf16[8,2,9792]{2,1,0:T(2,128)(2,1)}), bf16[8,2,9792]{2,1,0:T(2,128)(2,1)}, u32[]{:S(2)}, u32[]{:S(2)}) %all-to-all-start) | async-done | bytes 313376 | tf_op jit(solution)/shard_map/all_to_all | solution.py:288
  22.1 3.0 %collective-permute-done.1.rest_3_ = bf16[576,254]{1,0:T(8,128)(2,1)S(1)} collective-permute-done((bf16[576,254]{1,0:T(8,128)(2,1)S(1)}, bf16[576,254]{1,0:T(8,128)(2,1)S(1)}, u32[]{:S(2)}, u32[]{:S(2)}) %collective-permute-start.1) | collective-permute-done | bytes 292640 | tf_op jit(solution)/shard_map/ppermute | solution.py:295
  25.1 0.0 copy-start.2
  25.1 0.7 %copy-done.2 = bf16[576,254]{1,0:T(8,128)(2,1)} copy-done((bf16[576,254]{1,0:T(8,128)(2,1)}, bf16[576,254]{1,0:T(8,128)(2,1)S(1)}, u32[]{:S(2)}) %copy-start.2) | copy-done | bytes 292632
  25.8 0.0 collective-permute-done.3.rest_4_
  25.8 1.2 %reshape.6.here_ref = bf16[16,9792]{1,0:T(8,128)(2,1)S(1)} reshape(bf16[8,2,9792]{2,1,0:T(2,128)(2,1)} %all-to-all-done) | data formatting | bytes 626688 | tf_op jit(solution)/shard_map/reshape | solution.py:300
  27.0 0.1 collective-permute-start.4
  27.1 0.7 %collective-permute-start.5 = (bf16[576,254]{1,0:T(8,128)(2,1)}, bf16[576,254]{1,0:T(8,128)(2,1)S(1)}, u32[]{:S(2)}, u32[]{:S(2)}) collective-permute-start(bf16[576,254]{1,0:T(8,128)(2,1)} %copy-done.2), channel_id=1, source_target_pairs={{2,6},{3,1},{6,10},{7,3},{10,14},{11,7},{14,12},{15,11},{12,8},{13... | collective-permute-start | bytes 877832 | tf_op jit(solution)/shard_map/ppermute | solution.py:295
  27.8 1.7 %collective-permute-start.6 = (bf16[576,254]{1,0:T(8,128)(2,1)}, bf16[576,254]{1,0:T(8,128)(2,1)S(1)}, u32[]{:S(2)}, u32[]{:S(2)}) collective-permute-start(bf16[576,254]{1,0:T(8,128)(2,1)} %collective-permute-done.3.rest_4_), channel_id=1, source_target_pairs={{2,0},{3,7},{6,2},{7,11},{10,6},{11,15},{14,10},{15,13},{12,14},{1... | collective-permute-start | bytes 877832 | tf_op jit(solution)/shard_map/ppermute | solution.py:295
  30.1 0.0 copy-start.4
  30.8 0.0 collective-permute-done.4.there_ref
  30.8 0.0 copy-done.1
  30.8 0.0 copy-done.4
  30.8 0.0 copy-start.3
  30.9 1.0 %copy-done.3 = bf16[576,254]{1,0:T(8,128)(2,1)S(1)} copy-done((bf16[576,254]{1,0:T(8,128)(2,1)S(1)}, bf16[576,254]{1,0:T(8,128)(2,1)}, u32[]{:S(2)}) %copy-start.3) | copy-done | bytes 292632
  31.8 5.0 %first.1 = (bf16[512,576]{1,0:T(8,128)(2,1)S(1)}, f32[512,128]{1,0:T(8,128)S(1)}, f32[512,128]{1,0:T(8,128)S(1)}, f32[512,512]{1,0:T(8,128)S(1)}) custom-call(s32[1]{0:T(128)S(6)} %copy.9.length_ref, s32[1]{0:T(128)S(6)} %copy.10.offset_ref, s32[128]{0:T(128)S(1)} %copy-done.4, bf16[16,9792]{1,0:T(8,128)(2,1)S(1)} %reshape.6.here_ref, ...), custom_call_target="tpu_custom_call" | custom-call | tf_op jit(solution)/shard_map/first/pallas_call | solution.py:250
  36.8 0.0 collective-permute-done.5.rest_0_
  36.8 0.0 collective-permute-done.6.rest_1_
  36.8 1.3 %collective-permute-start.7 = (bf16[576,254]{1,0:T(8,128)(2,1)S(1)}, bf16[576,254]{1,0:T(8,128)(2,1)S(1)}, u32[]{:S(2)}, u32[]{:S(2)}) collective-permute-start(bf16[576,254]{1,0:T(8,128)(2,1)S(1)} %collective-permute-done.5.rest_0_), channel_id=1, source_target_pairs={{2,6},{3,1},{6,10},{7,3},{10,14},{11,7},{14,12},{15,11},{12,8},{13... | collective-permute-start | bytes 877832 | tf_op jit(solution)/shard_map/ppermute | solution.py:310
  38.1 2.1 %middle.1 = (f32[512,128]{1,0:T(8,128)S(1)}, f32[512,128]{1,0:T(8,128)S(1)}, f32[512,512]{1,0:T(8,128)S(1)}) custom-call(s32[1]{0:T(128)S(6)} %copy.9.length_ref, s32[128]{0:T(128)S(1)} %copy-done.4, bf16[512,576]{1,0:T(8,128)(2,1)S(1)} %get-tuple-element.24.q_ref, f32[512,128]{1,0:T(8,128)S(1)} %get-tuple-element.28.m_in, ...), custom_call_target="tpu_custom_call" | custom-call | tf_op jit(solution)/shard_map/middle/pallas_call | solution.py:260
  40.2 0.0 collective-permute-done.8.far_up
  40.2 3.5 %collective-permute-done.7.key_ref = bf16[576,254]{1,0:T(8,128)(2,1)S(1)} collective-permute-done((bf16[576,254]{1,0:T(8,128)(2,1)S(1)}, bf16[576,254]{1,0:T(8,128)(2,1)S(1)}, u32[]{:S(2)}, u32[]{:S(2)}) %collective-permute-start.7) | collective-permute-done | bytes 292640 | tf_op jit(solution)/shard_map/ppermute | solution.py:310
  43.7 2.4 %last.1 = (f32[16,2176]{1,0:T(8,128)S(1)}, bf16[16,2176]{1,0:T(8,128)(2,1)S(1)}) custom-call(s32[1]{0:T(128)S(6)} %copy.9.length_ref, s32[128]{0:T(128)S(1)} %copy-done.4, bf16[512,576]{1,0:T(8,128)(2,1)S(1)} %get-tuple-element.24.q_ref, f32[512,128]{1,0:T(8,128)S(1)} %get-tuple-element.31.m_ref, f32[512,128]{1,0:T(8,128)S(1)} %get-tuple-element.32.l_ref, ...), custom_call_target="tpu_custom_call" | custom-call | tf_op jit(solution)/shard_map/last/pallas_call | solution.py:314
  46.1 0.1 collective-permute-start.9
  46.2 1.2 %collective-permute-done.9.got_ref = bf16[16,2176]{1,0:T(8,128)(2,1)S(1)} collective-permute-done((bf16[16,2176]{1,0:T(8,128)(2,1)S(1)}, bf16[16,2176]{1,0:T(8,128)(2,1)S(1)}, u32[]{:S(2)}, u32[]{:S(2)}) %collective-permute-start.9) | collective-permute-done | bytes 69664 | tf_op jit(solution)/shard_map/ppermute | solution.py:323
  47.4 0.3 merge.1
  47.8 11.3 %all_to_all.10 = bf16[8,2,2048]{2,1,0:T(2,128)(2,1)S(1)} all-to-all(bf16[8,2,2048]{2,1,0:T(2,128)(2,1)S(1)} %merge.1), channel_id=1, replica_groups={{0,2,4,6,8,10,12,14},{1,3,5,7,9,11,13,15},{16,18,20,22,24,26,28,30},{17..., dimensions={0} | all-to-all | bytes 131072 | tf_op jit(solution)/shard_map/all_to_all | solution.py:333
  59.1 0.6 %copy.11 = bf16[2,16384]{1,0:T(2,128)(2,1)} copy(bf16[2,16384]{1,0:T(2,128)(2,1)S(1)} %bitcast.7) | data formatting | bytes 131072
Async XLA Ops:
  0.0 11.0 %copy-start = (bf16[8,512,128]{2,1,0:T(8,128)(2,1)S(1)}, bf16[8,512,128]{2,1,0:T(8,128)(2,1)}, u32[]{:S(2)}) copy-start(bf16[8,512,128]{2,1,0:T(8,128)(2,1)} %own_up.1) | copy-start | bytes 3145732
  0.0 11.1 %collective-permute-start = (bf16[576,254]{1,0:T(8,128)(2,1)}, bf16[576,254]{1,0:T(8,128)(2,1)S(1)}, u32[]{:S(2)}, u32[]{:S(2)}) collective-permute-start(bf16[576,254]{1,0:T(8,128)(2,1)} %bitcast.4), channel_id=1, source_target_pairs={{2,6},{3,1},{6,10},{7,3},{10,14},{11,7},{14,12},{15,11},{12,8},{13... | collective-permute-start | bytes 877832 | tf_op jit(solution)/shard_map/ppermute | solution.py:272
  2.9 10.3 %collective-permute-start.2 = (bf16[576,254]{1,0:T(8,128)(2,1)}, bf16[576,254]{1,0:T(8,128)(2,1)S(1)}, u32[]{:S(2)}, u32[]{:S(2)}) collective-permute-start(bf16[576,254]{1,0:T(8,128)(2,1)} %bitcast.5), channel_id=1, source_target_pairs={{2,0},{3,7},{6,2},{7,11},{10,6},{11,15},{14,10},{15,13},{12,14},{1... | collective-permute-start | bytes 877832 | tf_op jit(solution)/shard_map/ppermute | solution.py:272
  4.8 17.3 %all-to-all-start = ((bf16[8,2,9792]{2,1,0:T(2,128)(2,1)}), bf16[8,2,9792]{2,1,0:T(2,128)(2,1)}, u32[]{:S(2)}, u32[]{:S(2)}) async-start(bf16[8,2,9792]{2,1,0:T(2,128)(2,1)} %pieces.1), calls=%async_computation | async-start | bytes 630784 | tf_op jit(solution)/shard_map/all_to_all | solution.py:288
  11.0 19.8 %copy-start.1 = (bf16[254,576]{0,1:T(8,128)(2,1)S(1)}, bf16[254,576]{0,1:T(8,128)(2,1)}, u32[]{:S(2)}) copy-start(bf16[254,576]{0,1:T(8,128)(2,1)} %param.8) | copy-start | bytes 877828
  11.0 29.2 %collective-permute-start.8 = (bf16[8,512,128]{2,1,0:T(8,128)(2,1)S(1)}, bf16[8,512,128]{2,1,0:T(8,128)(2,1)S(1)}, u32[]{:S(2)}, u32[]{:S(2)}) collective-permute-start(bf16[8,512,128]{2,1,0:T(8,128)(2,1)S(1)} %copy-done), channel_id=1, source_target_pairs={{0,1},{1,0},{2,3},{3,2},{4,5},{5,4},{6,7},{7,6},{8,9},{9,8},{10,11... | collective-permute-start | bytes 3145736 | tf_op jit(solution)/shard_map/ppermute | solution.py:291
  11.1 14.0 %collective-permute-start.1 = (bf16[576,254]{1,0:T(8,128)(2,1)S(1)}, bf16[576,254]{1,0:T(8,128)(2,1)S(1)}, u32[]{:S(2)}, u32[]{:S(2)}) collective-permute-start(bf16[576,254]{1,0:T(8,128)(2,1)S(1)} %collective-permute-done.rest_1_), channel_id=1, source_target_pairs={{2,6},{3,1},{6,10},{7,3},{10,14},{11,7},{14,12},{15,11},{12,8},{13... | collective-permute-start | bytes 877832 | tf_op jit(solution)/shard_map/ppermute | solution.py:295
  13.2 12.6 %collective-permute-start.3 = (bf16[576,254]{1,0:T(8,128)(2,1)S(1)}, bf16[576,254]{1,0:T(8,128)(2,1)}, u32[]{:S(2)}, u32[]{:S(2)}) collective-permute-start(bf16[576,254]{1,0:T(8,128)(2,1)S(1)} %collective-permute-done.2.rest_2_), channel_id=1, source_target_pairs={{2,0},{3,7},{6,2},{7,11},{10,6},{11,15},{14,10},{15,13},{12,14},{1... | collective-permute-start | bytes 877832 | tf_op jit(solution)/shard_map/ppermute | solution.py:295
  25.1 0.7 %copy-start.2 = (bf16[576,254]{1,0:T(8,128)(2,1)}, bf16[576,254]{1,0:T(8,128)(2,1)S(1)}, u32[]{:S(2)}) copy-start(bf16[576,254]{1,0:T(8,128)(2,1)S(1)} %collective-permute-done.1.rest_3_) | copy-start | bytes 877828
  27.0 3.8 %collective-permute-start.4 = (bf16[16,9792]{1,0:T(8,128)(2,1)S(1)}, bf16[16,9792]{1,0:T(8,128)(2,1)S(1)}, u32[]{:S(2)}, u32[]{:S(2)}) collective-permute-start(bf16[16,9792]{1,0:T(8,128)(2,1)S(1)} %reshape.6.here_ref), channel_id=1, source_target_pairs={{0,1},{1,0},{2,3},{3,2},{4,5},{5,4},{6,7},{7,6},{8,9},{9,8},{10,11... | collective-permute-start | bytes 940040 | tf_op jit(solution)/shard_map/ppermute | solution.py:301
  27.1 9.7 %collective-permute-start.5 = (bf16[576,254]{1,0:T(8,128)(2,1)}, bf16[576,254]{1,0:T(8,128)(2,1)S(1)}, u32[]{:S(2)}, u32[]{:S(2)}) collective-permute-start(bf16[576,254]{1,0:T(8,128)(2,1)} %copy-done.2), channel_id=1, source_target_pairs={{2,6},{3,1},{6,10},{7,3},{10,14},{11,7},{14,12},{15,11},{12,8},{13... | collective-permute-start | bytes 877832 | tf_op jit(solution)/shard_map/ppermute | solution.py:295
  27.8 9.0 %collective-permute-start.6 = (bf16[576,254]{1,0:T(8,128)(2,1)}, bf16[576,254]{1,0:T(8,128)(2,1)S(1)}, u32[]{:S(2)}, u32[]{:S(2)}) collective-permute-start(bf16[576,254]{1,0:T(8,128)(2,1)} %collective-permute-done.3.rest_4_), channel_id=1, source_target_pairs={{2,0},{3,7},{6,2},{7,11},{10,6},{11,15},{14,10},{15,13},{12,14},{1... | collective-permute-start | bytes 877832 | tf_op jit(solution)/shard_map/ppermute | solution.py:295
  30.1 0.7 %copy-start.4 = (s32[128]{0:T(128)S(1)}, s32[128]{0:T(128)}, u32[]{:S(2)}) copy-start(s32[128]{0:T(128)} %constant.2.clone.table_ref) | copy-start | bytes 1540
  30.8 1.0 %copy-start.3 = (bf16[576,254]{1,0:T(8,128)(2,1)S(1)}, bf16[576,254]{1,0:T(8,128)(2,1)}, u32[]{:S(2)}) copy-start(bf16[576,254]{1,0:T(8,128)(2,1)} %copy-done.2) | copy-start | bytes 877828
  36.8 6.9 %collective-permute-start.7 = (bf16[576,254]{1,0:T(8,128)(2,1)S(1)}, bf16[576,254]{1,0:T(8,128)(2,1)S(1)}, u32[]{:S(2)}, u32[]{:S(2)}) collective-permute-start(bf16[576,254]{1,0:T(8,128)(2,1)S(1)} %collective-permute-done.5.rest_0_), channel_id=1, source_target_pairs={{2,6},{3,1},{6,10},{7,3},{10,14},{11,7},{14,12},{15,11},{12,8},{13... | collective-permute-start | bytes 877832 | tf_op jit(solution)/shard_map/ppermute | solution.py:310
  46.1 1.3 %collective-permute-start.9 = (bf16[16,2176]{1,0:T(8,128)(2,1)S(1)}, bf16[16,2176]{1,0:T(8,128)(2,1)S(1)}, u32[]{:S(2)}, u32[]{:S(2)}) collective-permute-start(bf16[16,2176]{1,0:T(8,128)(2,1)S(1)} %get-tuple-element.36), channel_id=1, source_target_pairs={{0,1},{1,0},{2,3},{3,2},{4,5},{5,4},{6,7},{7,6},{8,9},{9,8},{10,11... | collective-permute-start | bytes 208904 | tf_op jit(solution)/shard_map/ppermute | solution.py:323

commit v12 on v11

--- a/solution.py
+++ b/solution.py
@@ -33,8 +33,8 @@
     return walk + [z * wide for z in reversed(range(tall))]
 
 
-def fold_block(part, q_ref, shards, length, old):
-    m_old = old[0][part, :][:, :1]
+def fold_block(part, q_ref, shards, length, old=None, span=None):
+    m_old = least_max if old is None else old[0][part, :][:, :1]
     m_new = m_old
     scores = []
     for base, key_ref in shards:
@@ -43,9 +43,18 @@
         s = jnp.where(slot < length, s, neg_large)
         m_new = jnp.maximum(m_new, jnp.max(s, axis=1, keepdims=True))
         scores.append(s)
-    shrink = jnp.exp2(m_old - m_new)
-    l_new = old[1][part, :][:, :1] * shrink
-    summed = old[2][part, :] * shrink
+    if span is not None:
+        keys, shown = span
+        s = lax.dot_general(
+            q_ref[part, :], keys, (((1,), (1,)), ((), ())), preferred_element_type=f32
+        )
+        span_s = jnp.where(shown, s * score_scale, neg_large)
+        m_new = jnp.maximum(m_new, jnp.max(span_s, axis=1, keepdims=True))
+    l_new, summed = 0.0, 0.0
+    if old is not None:
+        shrink = jnp.exp2(m_old - m_new)
+        l_new = old[1][part, :][:, :1] * shrink
+        summed = old[2][part, :] * shrink
     for s, (_, key_ref) in zip(scores, shards):
         probs = jnp.exp2(s - m_new)
         l_new += jnp.sum(probs, axis=1, keepdims=True)
@@ -53,15 +62,22 @@
             probs.astype(bf16), key_ref[:LATENT, :], (((1,), (1,)), ((), ())),
             preferred_element_type=f32,
         )
+    if span is not None:
+        probs = jnp.exp2(span_s - m_new)
+        l_new += jnp.sum(probs, axis=1, keepdims=True)
+        summed += jnp.dot(
+            probs.astype(bf16), keys[:, :LATENT], preferred_element_type=f32
+        )
     return m_new, l_new, summed
 
 
-def fold_shards(q_ref, shards, length, old, new):
+def fold_shards(q_ref, shards, length, old, new, span=None):
     rows = q_ref.shape[0]
     block = min(256, rows)
     for start in range(0, rows, block):
         part = pl.ds(start, block)
-        m_new, l_new, summed = fold_block(part, q_ref, shards, length, old)
+        shown = None if span is None else (span[0], span[1](start, block))
+        m_new, l_new, summed = fold_block(part, q_ref, shards, length, old, shown)
         new[0][part, :] = jnp.broadcast_to(m_new, (block, LANES))
         new[1][part, :] = jnp.broadcast_to(l_new, (block, LANES))
         new[2][part, :] = summed
@@ -86,15 +102,7 @@
     ]
 
 
-def pieces_kernel(queries_hbm, span_hbm, out_ref, queries_ref, span_ref, sems):
-    copies = [
-        pltpu.make_async_copy(queries_hbm, queries_ref, sems.at[0]),
-        pltpu.make_async_copy(span_hbm, span_ref, sems.at[1]),
-    ]
-    for copy in copies:
-        copy.start()
-    for copy in copies:
-        copy.wait()
+def pieces_kernel(queries_ref, span_ref, out_ref):
     chips = out_ref.shape[0]
     part = queries_ref.shape[1] // chips
     for chip in range(chips):
@@ -102,40 +110,16 @@
         out_ref[chip, :, part:] = span_ref[...]
 
 
-def first_kernel(heads, count, length_ref, offset_ref, table_ref, here_ref, there_ref, *rest):
+def first_kernel(heads, count, length_ref, table_ref, here_ref, there_ref, *rest):
     keys, (q_ref, m_ref, l_ref, acc_ref) = rest[:count], rest[count:]
-    chips = lax.axis_size("ctx") // CORES
     half = here_ref.shape[0]
-    tokens = half // chips
     width = q_ref.shape[1]
     for core, piece_ref in enumerate((here_ref, there_ref)):
         for head in range(heads):
             row = (head * CORES + core) * half
             q_ref[row:row + half, :] = piece_ref[:, head * width:(head + 1) * width]
-    span = here_ref[:, heads * width:]
-    total = q_ref.shape[0]
-    block = min(256, total)
-    key_index = lax.broadcasted_iota(jnp.int32, (1, span.shape[0]), 1)
-    key_token = token_of(key_index, tokens, chips)
-    for start in range(0, total, block):
-        part = pl.ds(start, block)
-        s = lax.dot_general(
-            q_ref[part, :], span, (((1,), (1,)), ((), ())), preferred_element_type=f32
-        ) * score_scale
-        row_index = start + lax.broadcasted_iota(jnp.int32, (block, 1), 0)
-        row_token = token_of(row_index & (half * CORES - 1), tokens, chips)
-        shown = (key_token >= offset_ref[0]) & (key_token <= row_token)
-        s = jnp.where(shown, s, neg_large)
-        m_new = jnp.maximum(jnp.max(s, axis=1, keepdims=True), least_max)
-        probs = jnp.exp2(s - m_new)
-        l_new = jnp.sum(probs, axis=1, keepdims=True)
-        acc_ref[part, :] = jnp.dot(
-            probs.astype(bf16), span[:, :LATENT], preferred_element_type=f32
-        )
-        m_ref[part, :] = jnp.broadcast_to(m_new, (block, LANES))
-        l_ref[part, :] = jnp.broadcast_to(l_new, (block, LANES))
-    state = (m_ref, l_ref, acc_ref)
-    fold_shards(q_ref, with_base(table_ref, 0, keys), length_ref[0], state, state)
+    shards = with_base(table_ref, 0, keys)
+    fold_shards(q_ref, shards, length_ref[0], None, (m_ref, l_ref, acc_ref))
 
 
 def middle_kernel(at, count, length_ref, table_ref, q_ref, m_in, l_in, acc_in, *rest):
@@ -143,8 +127,36 @@
     fold_shards(q_ref, with_base(table_ref, at, keys), length_ref[0], (m_in, l_in, acc_in), new)
 
 
+def span_kernel(at, count, length_ref, offset_ref, table_ref, q_ref, m_in, l_in, acc_in,
+                here_ref, *rest):
+    keys, new = rest[:count], rest[count:]
+    chips = lax.axis_size("ctx") // CORES
+    half = here_ref.shape[0]
+    tokens = half // chips
+    width = q_ref.shape[1]
+    key_index = lax.broadcasted_iota(jnp.int32, (1, half), 1)
+    key_token = token_of(key_index, tokens, chips)
+
+    def shown(start, block):
+        row_index = start + lax.broadcasted_iota(jnp.int32, (block, 1), 0)
+        row_token = token_of(row_index & (half * CORES - 1), tokens, chips)
+        return (key_token >= offset_ref[0]) & (key_token <= row_token)
+
+    fold_shards(
+        q_ref, with_base(table_ref, at, keys), length_ref[0], (m_in, l_in, acc_in), new,
+        (here_ref[:, here_ref.shape[1] - width:], shown),
+    )
+
+
+def join_halves(top_ref, bottom_ref, key_ref):
+    cut = top_ref.shape[0]
+    key_ref[:cut, :] = top_ref[...]
+    key_ref[cut:, :] = bottom_ref[...]
+
+
 def last_kernel(at, heads, length_ref, table_ref, q_ref, m_ref, l_ref, acc_ref,
-                key_ref, own_up, far_up, keep_ref, give_ref, flat_ref):
+                top_ref, bottom_ref, own_up, far_up, keep_ref, give_ref, key_ref, flat_ref):
+    join_halves(top_ref, bottom_ref, key_ref)
     core = lax.axis_index("ctx") % CORES
     shards = with_base(table_ref, at, (key_ref,))
     everyone = flat_ref.shape[0]
@@ -250,11 +262,11 @@
         return pl.pallas_call(
             functools.partial(first_kernel, heads, len(keys)),
             out_shape=[shape(total, width, dtype=bf16)] + state_shapes,
-            in_specs=[SMEM] * 3 + [VMEM] * (2 + len(keys)),
+            in_specs=[SMEM] * 2 + [VMEM] * (2 + len(keys)),
             out_specs=[VMEM] * 4,
             compiler_params=PARAMS,
             name="first",
-        )(prefix_length, span_offset, table, here, there, *keys)
+        )(prefix_length, table, here, there, *keys)
 
     def fold_more(at, q, state, keys):
         return pl.pallas_call(
@@ -268,21 +280,16 @@
 
     onward = functools.partial(lax.ppermute, axis_name="ctx", perm=across(1))
     backward = functools.partial(lax.ppermute, axis_name="ctx", perm=across(-1))
+    cut = LATENT // 2
     own = prefix_latents.T
     right, left = onward(own), backward(own)
 
-    anywhere = pl.BlockSpec(memory_space=pl.ANY)
     pieces = pl.pallas_call(
         pieces_kernel,
         out_shape=shape(chips, tokens, (heads + 1) * width, dtype=bf16),
-        in_specs=[anywhere] * 2,
+        in_specs=[VMEM] * 2,
         out_specs=VMEM,
-        scratch_shapes=[
-            pltpu.VMEM(queries.shape, bf16),
-            pltpu.VMEM(span_latents.shape, bf16),
-            pltpu.SemaphoreType.DMA((2,)),
-        ],
-        compiler_params=pltpu.CompilerParams(vmem_limit_bytes=56 * 1024 * 1024),
+        compiler_params=PARAMS,
         name="pieces",
     )(queries, span_latents)
     here = lax.all_to_all(
@@ -293,33 +300,40 @@
     keys, state, at = [own, right, left], None, 0
     for s in range(2, steps):
         right, left = onward(right), backward(left)
-        keys += [right, left]
         if s == 2:
-            right, left, here = lax.optimization_barrier((right, left, here))
-            keys[-2:] = right, left
+            here, right = lax.optimization_barrier((here, right))
             here = here.reshape(chips * tokens, (heads + 1) * width)
             there = lax.ppermute(here, "ctx", other_core)
+            keys += [right, left]
             continue
         if state is None:
-            q, *state = fold_first(keys[:-2])
+            q, *state = fold_first(keys)
         else:
-            state = fold_more(at, q, state, keys[:-2])
-        at += len(keys) - 2
-        keys = keys[-2:]
-    right, left, state = lax.optimization_barrier((right, left, state))
-    right = onward(right)
-    state = fold_more(at, q, state, keys)
+            state = fold_more(at, q, state, keys)
+        at += len(keys)
+        keys = [right, left]
+    top = onward(right[:cut])
+    left, state = lax.optimization_barrier((left, state))
+    bottom = backward(left[cut:])
+    state = pl.pallas_call(
+        functools.partial(span_kernel, at, len(keys)),
+        out_shape=state_shapes,
+        in_specs=[SMEM] * 3 + [VMEM] * (5 + len(keys)),
+        out_specs=[VMEM] * 3,
+        compiler_params=PARAMS,
+        name="middle",
+    )(prefix_length, span_offset, table, q, *state, here, *keys)
     flat = heads * V_HEAD + LANES
     half = everyone // CORES
     keep, give = pl.pallas_call(
         functools.partial(last_kernel, chips - 1, heads),
         out_shape=[shape(half, flat), shape(half, flat, dtype=bf16)],
-        in_specs=[SMEM] * 2 + [VMEM] * 7,
+        in_specs=[SMEM] * 2 + [VMEM] * 8,
         out_specs=[VMEM] * 2,
-        scratch_shapes=[pltpu.VMEM((everyone, flat), f32)],
+        scratch_shapes=[pltpu.VMEM((width, slots), bf16), pltpu.VMEM((everyone, flat), f32)],
         compiler_params=PARAMS,
         name="last",
-    )(prefix_length, table, q, *state, right, value_up, far_up)
+    )(prefix_length, table, q, *state, top, bottom, value_up, far_up)
     got = lax.ppermute(give, "ctx", other_core)
     merged = pl.pallas_call(
         functools.partial(merge_kernel, heads),

time: 60.1 us -> 58.4 us (0.972)
  Pallas kernels: 11.5 us -> 9.54 us
  starting transfers between devices: 15.4 us -> 16.7 us
  local copies, waits for them, and re-layouts: 3.51 us -> 2.54 us
  blocking collectives: 11.3 us -> 10.4 us
  waiting for transfers between devices: 16.6 us -> 17.4 us
    ppermute x4, waiting for transfers between devices: 3 us -> 5.45 us  [on_device(): right, left = (onward(right), backward(left))]
    ppermute x1 -> x2, waiting for transfers between devices: 3.48 us -> 1.82 us  [the longest x1 1.81 us: on_device(): top = onward(right[:cut])]
    pallas_call x1, Pallas kernels: 4.98 us -> 3.59 us  [fold_first(): pl.pallas_call(functools.partial(first_kernel, heads, len(keys)), out_sha...]
    all_to_all x1, starting transfers between devices: 6.22 us -> 5.13 us  [on_device(): lax.all_to_all(pieces, 'ctx', split_axis=0, concat_axis=0, axis_index_gro...]
    ppermute x2, starting transfers between devices: 3.07 us -> 4.15 us  [on_device(): right, left = (onward(own), backward(own))]
    ppermute x1 -> x2, starting transfers between devices: 1.32 us -> 2.39 us  [the longest x1 2.33 us: on_device(): bottom = backward(left[cut:])]
    pallas_call x1, Pallas kernels: 1.73 us -> 0.74 us  [on_device(): pl.pallas_call(pieces_kernel, out_shape=shape(chips, tokens, (heads + 1)...]
    reshape x1, local copies, waits for them, and re-layouts: 1.2 us -> 0.23 us  [on_device(): here = here.reshape(chips * tokens, (heads + 1) * width)]
  transfers between devices with their start and end apart: 11 -> 12, of which waited for: 4 -> 5; matrix products, arithmetic and copies ran while one was open for 2% -> 0% of each run, Pallas kernels for 15% -> 12%
where the time goes in v12:
time: 58.4 us; the launch traced here: 58.1 us
  waiting for transfers between devices  17.4 us (30%)
  starting transfers between devices  16.7 us (29%)
  blocking collectives  10.4 us (18%)
  Pallas kernels  9.54 us (16%)
  local copies, waits for them, and re-layouts  2.54 us (4%)
  between operations  1.44 us (2%)
    all_to_all x1, blocking collectives, on_device(): lax.all_to_all(merged, 'ctx', split_axis=0, concat_axis=0, axis_index_gro...  10.4 us
    all_to_all x1, waiting for transfers between devices, on_device(): lax.all_to_all(pieces, 'ctx', split_axis=0, concat_axis=0, axis_index_gro...  8.91 us
    ppermute x4, waiting for transfers between devices, on_device(): right, left = (onward(right), backward(left))  5.45 us
    all_to_all x1, starting transfers between devices, on_device(): lax.all_to_all(pieces, 'ctx', split_axis=0, concat_axis=0, axis_index_gro...  5.13 us
    ppermute x4, starting transfers between devices, on_device(): right, left = (onward(right), backward(left))  4.91 us
    ppermute x2, starting transfers between devices, on_device(): right, left = (onward(own), backward(own))  4.15 us
    pallas_call x1, Pallas kernels, fold_first(): pl.pallas_call(functools.partial(first_kernel, heads, len(keys)), out_sha...  3.59 us
    pallas_call x1, Pallas kernels, on_device(): pl.pallas_call(functools.partial(span_kernel, at, len(keys)), out_shape=s...  2.47 us
  transfers between devices with their start and end apart: 12, of which 5 were waited for; matrix products, arithmetic and copies ran while one was open for 0% of the time, Pallas kernels for 12%

profile of v12, /device:TPU:0, one launch (start us, length us, event | category | flops | bytes accessed | tf_op | source)
XLA Modules:
  0.0 58.1 jit_solution(13859103142194739243)
XLA Ops:
  0.0 2.9 %collective-permute-start = (bf16[576,254]{1,0:T(8,128)(2,1)}, bf16[576,254]{1,0:T(8,128)(2,1)S(1)}, u32[]{:S(2)}, u32[]{:S(2)}) collective-permute-start(bf16[576,254]{1,0:T(8,128)(2,1)} %bitcast.4), channel_id=1, source_target_pairs={{2,6},{3,1},{6,10},{7,3},{10,14},{11,7},{14,12},{15,11},{12,8},{13... | collective-permute-start | bytes 877832 | tf_op jit(solution)/shard_map/ppermute | solution.py:285
  2.9 0.0 collective-permute-start.9
  2.9 1.2 %collective-permute-start.3 = (bf16[576,254]{1,0:T(8,128)(2,1)}, bf16[576,254]{1,0:T(8,128)(2,1)S(1)}, u32[]{:S(2)}, u32[]{:S(2)}) collective-permute-start(bf16[576,254]{1,0:T(8,128)(2,1)} %bitcast.5), channel_id=1, source_target_pairs={{2,0},{3,7},{6,2},{7,11},{10,6},{11,15},{14,10},{15,13},{12,14},{1... | collective-permute-start | bytes 877832 | tf_op jit(solution)/shard_map/ppermute | solution.py:285
  4.2 0.0 copy-start.1
  4.2 1.0 %copy-done.1 = bf16[2,73728]{1,0:T(2,128)(2,1)S(1)} copy-done((bf16[2,73728]{1,0:T(2,128)(2,1)S(1)}, bf16[2,73728]{1,0:T(2,128)(2,1)}, u32[]{:S(2)}) %copy-start.1) | copy-done | bytes 294936
  5.1 0.0 copy-start.4
  5.1 0.7 %copy-done.4 = bf16[2,576]{1,0:T(2,128)(2,1)S(1)} copy-done((bf16[2,576]{1,0:T(2,128)(2,1)S(1)}, bf16[2,576]{1,0:T(2,128)(2,1)}, u32[]{:S(2)}) %copy-start.4) | copy-done | bytes 2328
  5.8 0.7 %pieces.1 = bf16[8,2,9792]{2,1,0:T(2,128)(2,1)} custom-call(bf16[2,73728]{1,0:T(2,128)(2,1)S(1)} %copy-done.1, bf16[2,576]{1,0:T(2,128)(2,1)S(1)} %copy-done.4), custom_call_target="tpu_custom_call" | custom-call | tf_op jit(solution)/shard_map/pieces/pallas_call | solution.py:287
  6.5 5.1 %all-to-all-start = ((bf16[8,2,9792]{2,1,0:T(2,128)(2,1)}), bf16[8,2,9792]{2,1,0:T(2,128)(2,1)S(1)}, u32[]{:S(2)}, u32[]{:S(2)}) async-start(bf16[8,2,9792]{2,1,0:T(2,128)(2,1)} %pieces.1), calls=%async_computation | async-start | bytes 630784 | tf_op jit(solution)/shard_map/all_to_all | solution.py:295
  11.7 0.0 copy-start.2
  11.7 0.0 collective-permute-done.rest_1_
  11.7 2.1 %collective-permute-start.1 = (bf16[576,254]{1,0:T(8,128)(2,1)S(1)}, bf16[576,254]{1,0:T(8,128)(2,1)S(1)}, u32[]{:S(2)}, u32[]{:S(2)}) collective-permute-start(bf16[576,254]{1,0:T(8,128)(2,1)S(1)} %collective-permute-done.rest_1_), channel_id=1, source_target_pairs={{2,6},{3,1},{6,10},{7,3},{10,14},{11,7},{14,12},{15,11},{12,8},{13... | collective-permute-start | bytes 877832 | tf_op jit(solution)/shard_map/ppermute | solution.py:302
  13.8 0.0 collective-permute-done.3.rest_2_
  13.8 0.1 collective-permute-start.4
  13.8 8.9 %all-to-all-done = bf16[8,2,9792]{2,1,0:T(2,128)(2,1)S(1)} async-done(((bf16[8,2,9792]{2,1,0:T(2,128)(2,1)}), bf16[8,2,9792]{2,1,0:T(2,128)(2,1)S(1)}, u32[]{:S(2)}, u32[]{:S(2)}) %all-to-all-start) | async-done | bytes 313376 | tf_op jit(solution)/shard_map/all_to_all | solution.py:295
  22.7 2.6 %collective-permute-done.1.rest_3_ = bf16[576,254]{1,0:T(8,128)(2,1)S(1)} collective-permute-done((bf16[576,254]{1,0:T(8,128)(2,1)S(1)}, bf16[576,254]{1,0:T(8,128)(2,1)S(1)}, u32[]{:S(2)}, u32[]{:S(2)}) %collective-permute-start.1) | collective-permute-done | bytes 292640 | tf_op jit(solution)/shard_map/ppermute | solution.py:302
  25.4 0.2 reshape.6.here_ref
  25.6 0.0 copy-start.3
  25.6 0.1 collective-permute-start.2
  25.7 0.0 collective-permute-done.4.rest_4_
  25.7 2.8 %collective-permute-start.5 = (bf16[576,254]{1,0:T(8,128)(2,1)S(1)}, bf16[576,254]{1,0:T(8,128)(2,1)S(1)}, u32[]{:S(2)}, u32[]{:S(2)}) collective-permute-start(bf16[576,254]{1,0:T(8,128)(2,1)S(1)} %collective-permute-done.4.rest_4_), channel_id=1, source_target_pairs={{2,0},{3,7},{6,2},{7,11},{10,6},{11,15},{14,10},{15,13},{12,14},{1... | collective-permute-start | bytes 877832 | tf_op jit(solution)/shard_map/ppermute | solution.py:302
  28.5 0.0 collective-permute-start.6
  29.1 0.0 collective-permute-done.2.there_ref
  29.2 0.0 copy-done.2
  29.2 0.0 copy-done.3
  29.2 3.6 %first.1 = (bf16[512,576]{1,0:T(8,128)(2,1)S(1)}, f32[512,128]{1,0:T(8,128)S(1)}, f32[512,128]{1,0:T(8,128)S(1)}, f32[512,512]{1,0:T(8,128)S(1)}) custom-call(s32[1]{0:T(128)S(6)} %copy.9.length_ref, s32[128]{0:T(128)S(1)} %copy-done.3, bf16[16,9792]{1,0:T(8,128)(2,1)S(1)} %reshape.6.here_ref, bf16[16,9792]{1,0:T(8,128)(2,1)S(1)} %collective-permute-done.2.there_ref, ...), custom_call_target="tpu_custom_call" | custom-call | tf_op jit(solution)/shard_map/first/pallas_call | solution.py:262
  32.8 2.8 %collective-permute-done.5.rest_1_ = bf16[576,254]{1,0:T(8,128)(2,1)S(1)} collective-permute-done((bf16[576,254]{1,0:T(8,128)(2,1)S(1)}, bf16[576,254]{1,0:T(8,128)(2,1)S(1)}, u32[]{:S(2)}, u32[]{:S(2)}) %collective-permute-start.5) | collective-permute-done | bytes 292640 | tf_op jit(solution)/shard_map/ppermute | solution.py:302
  35.6 2.3 %collective-permute-start.8 = (bf16[320,254]{1,0:T(8,128)(2,1)S(1)}, bf16[320,254]{1,0:T(8,128)(2,1)S(1)}, u32[]{:S(2)}, u32[]{:S(2)}) collective-permute-start(bf16[320,254]{1,0:T(8,128)(2,1)S(1)} %slice.7), channel_id=1, source_target_pairs={{2,0},{3,7},{6,2},{7,11},{10,6},{11,15},{14,10},{15,13},{12,14},{1... | collective-permute-start | bytes 487688 | tf_op jit(solution)/shard_map/ppermute | solution.py:317
  37.9 0.0 collective-permute-done.6.rest_0_
  37.9 0.1 collective-permute-start.7
  38.6 0.0 copy-start
  38.7 2.5 %middle.1 = (f32[512,128]{1,0:T(8,128)S(1)}, f32[512,128]{1,0:T(8,128)S(1)}, f32[512,512]{1,0:T(8,128)S(1)}) custom-call(s32[1]{0:T(128)S(6)} %copy.9.length_ref, s32[1]{0:T(128)S(6)} %copy.10.offset_ref, s32[128]{0:T(128)S(1)} %copy-done.3, bf16[512,576]{1,0:T(8,128)(2,1)S(1)} %get-tuple-element.22.q_ref, f32[512,128]{1,0:T(8,128)S(1)} %get-tuple-element.26.m_in, ...), custom_call_target="tpu_custom_call" | custom-call | tf_op jit(solution)/shard_map/middle/pallas_call | solution.py:318
  41.1 1.8 %collective-permute-done.7.top_ref = bf16[256,254]{1,0:T(8,128)(2,1)S(1)} collective-permute-done((bf16[256,254]{1,0:T(8,128)(2,1)S(1)}, bf16[256,254]{1,0:T(8,128)(2,1)S(1)}, u32[]{:S(2)}, u32[]{:S(2)}) %collective-permute-start.7) | collective-permute-done | bytes 130080 | tf_op jit(solution)/shard_map/ppermute | solution.py:315
  42.9 0.0 collective-permute-done.9.far_up
  43.0 0.0 collective-permute-done.8.bottom_ref
  43.0 0.0 copy-done
  43.0 2.4 %last.1 = (f32[16,2176]{1,0:T(8,128)S(1)}, bf16[16,2176]{1,0:T(8,128)(2,1)S(1)}) custom-call(s32[1]{0:T(128)S(6)} %copy.9.length_ref, s32[128]{0:T(128)S(1)} %copy-done.3, bf16[512,576]{1,0:T(8,128)(2,1)S(1)} %get-tuple-element.22.q_ref, f32[512,128]{1,0:T(8,128)S(1)} %get-tuple-element.29.m_ref, f32[512,128]{1,0:T(8,128)S(1)} %get-tuple-element.30.l_ref, ...), custom_call_target="tpu_custom_call" | custom-call | tf_op jit(solution)/shard_map/last/pallas_call | solution.py:328
  45.4 0.1 collective-permute-start.10
  45.4 1.2 %collective-permute-done.10.got_ref = bf16[16,2176]{1,0:T(8,128)(2,1)S(1)} collective-permute-done((bf16[16,2176]{1,0:T(8,128)(2,1)S(1)}, bf16[16,2176]{1,0:T(8,128)(2,1)S(1)}, u32[]{:S(2)}, u32[]{:S(2)}) %collective-permute-start.10) | collective-permute-done | bytes 69664 | tf_op jit(solution)/shard_map/ppermute | solution.py:337
  46.7 0.3 merge.1
  47.0 10.4 %all_to_all.10 = bf16[8,2,2048]{2,1,0:T(2,128)(2,1)S(1)} all-to-all(bf16[8,2,2048]{2,1,0:T(2,128)(2,1)S(1)} %merge.1), channel_id=1, replica_groups={{0,2,4,6,8,10,12,14},{1,3,5,7,9,11,13,15},{16,18,20,22,24,26,28,30},{17..., dimensions={0} | all-to-all | bytes 131072 | tf_op jit(solution)/shard_map/all_to_all | solution.py:347
  57.4 0.6 %copy.11 = bf16[2,16384]{1,0:T(2,128)(2,1)} copy(bf16[2,16384]{1,0:T(2,128)(2,1)S(1)} %bitcast.7) | data formatting | bytes 131072
  (2 shorter events, 0.0 us)
Async XLA Ops:
  0.0 11.7 %collective-permute-start = (bf16[576,254]{1,0:T(8,128)(2,1)}, bf16[576,254]{1,0:T(8,128)(2,1)S(1)}, u32[]{:S(2)}, u32[]{:S(2)}) collective-permute-start(bf16[576,254]{1,0:T(8,128)(2,1)} %bitcast.4), channel_id=1, source_target_pairs={{2,6},{3,1},{6,10},{7,3},{10,14},{11,7},{14,12},{15,11},{12,8},{13... | collective-permute-start | bytes 877832 | tf_op jit(solution)/shard_map/ppermute | solution.py:285
  2.9 40.0 %collective-permute-start.9 = (bf16[8,512,128]{2,1,0:T(8,128)(2,1)}, bf16[8,512,128]{2,1,0:T(8,128)(2,1)S(1)}, u32[]{:S(2)}, u32[]{:S(2)}) collective-permute-start(bf16[8,512,128]{2,1,0:T(8,128)(2,1)} %own_up.1), channel_id=1, source_target_pairs={{0,1},{1,0},{2,3},{3,2},{4,5},{5,4},{6,7},{7,6},{8,9},{9,8},{10,11... | collective-permute-start | bytes 3145736 | tf_op jit(solution)/shard_map/ppermute | solution.py:298
  2.9 10.8 %collective-permute-start.3 = (bf16[576,254]{1,0:T(8,128)(2,1)}, bf16[576,254]{1,0:T(8,128)(2,1)S(1)}, u32[]{:S(2)}, u32[]{:S(2)}) collective-permute-start(bf16[576,254]{1,0:T(8,128)(2,1)} %bitcast.5), channel_id=1, source_target_pairs={{2,0},{3,7},{6,2},{7,11},{10,6},{11,15},{14,10},{15,13},{12,14},{1... | collective-permute-start | bytes 877832 | tf_op jit(solution)/shard_map/ppermute | solution.py:285
  4.2 1.0 %copy-start.1 = (bf16[2,73728]{1,0:T(2,128)(2,1)S(1)}, bf16[2,73728]{1,0:T(2,128)(2,1)}, u32[]{:S(2)}) copy-start(bf16[2,73728]{1,0:T(2,128)(2,1)} %queries_ref.1) | copy-start | bytes 884740
  5.1 0.7 %copy-start.4 = (bf16[2,576]{1,0:T(2,128)(2,1)S(1)}, bf16[2,576]{1,0:T(2,128)(2,1)}, u32[]{:S(2)}) copy-start(bf16[2,576]{1,0:T(2,128)(2,1)} %span_ref.1) | copy-start | bytes 6916
  6.5 16.2 %all-to-all-start = ((bf16[8,2,9792]{2,1,0:T(2,128)(2,1)}), bf16[8,2,9792]{2,1,0:T(2,128)(2,1)S(1)}, u32[]{:S(2)}, u32[]{:S(2)}) async-start(bf16[8,2,9792]{2,1,0:T(2,128)(2,1)} %pieces.1), calls=%async_computation | async-start | bytes 630784 | tf_op jit(solution)/shard_map/all_to_all | solution.py:295
  11.7 17.5 %copy-start.2 = (bf16[254,576]{0,1:T(8,128)(2,1)S(1)}, bf16[254,576]{0,1:T(8,128)(2,1)}, u32[]{:S(2)}) copy-start(bf16[254,576]{0,1:T(8,128)(2,1)} %param.8) | copy-start | bytes 877828
  11.7 13.7 %collective-permute-start.1 = (bf16[576,254]{1,0:T(8,128)(2,1)S(1)}, bf16[576,254]{1,0:T(8,128)(2,1)S(1)}, u32[]{:S(2)}, u32[]{:S(2)}) collective-permute-start(bf16[576,254]{1,0:T(8,128)(2,1)S(1)} %collective-permute-done.rest_1_), channel_id=1, source_target_pairs={{2,6},{3,1},{6,10},{7,3},{10,14},{11,7},{14,12},{15,11},{12,8},{13... | collective-permute-start | bytes 877832 | tf_op jit(solution)/shard_map/ppermute | solution.py:302
  13.8 12.0 %collective-permute-start.4 = (bf16[576,254]{1,0:T(8,128)(2,1)S(1)}, bf16[576,254]{1,0:T(8,128)(2,1)S(1)}, u32[]{:S(2)}, u32[]{:S(2)}) collective-permute-start(bf16[576,254]{1,0:T(8,128)(2,1)S(1)} %collective-permute-done.3.rest_2_), channel_id=1, source_target_pairs={{2,0},{3,7},{6,2},{7,11},{10,6},{11,15},{14,10},{15,13},{12,14},{1... | collective-permute-start | bytes 877832 | tf_op jit(solution)/shard_map/ppermute | solution.py:302
  25.6 3.6 %copy-start.3 = (s32[128]{0:T(128)S(1)}, s32[128]{0:T(128)}, u32[]{:S(2)}) copy-start(s32[128]{0:T(128)} %constant.2.clone.table_ref) | copy-start | bytes 1540
  25.6 3.5 %collective-permute-start.2 = (bf16[16,9792]{1,0:T(8,128)(2,1)S(1)}, bf16[16,9792]{1,0:T(8,128)(2,1)S(1)}, u32[]{:S(2)}, u32[]{:S(2)}) collective-permute-start(bf16[16,9792]{1,0:T(8,128)(2,1)S(1)} %reshape.6.here_ref), channel_id=1, source_target_pairs={{0,1},{1,0},{2,3},{3,2},{4,5},{5,4},{6,7},{7,6},{8,9},{9,8},{10,11... | collective-permute-start | bytes 940040 | tf_op jit(solution)/shard_map/ppermute | solution.py:306
  25.7 9.8 %collective-permute-start.5 = (bf16[576,254]{1,0:T(8,128)(2,1)S(1)}, bf16[576,254]{1,0:T(8,128)(2,1)S(1)}, u32[]{:S(2)}, u32[]{:S(2)}) collective-permute-start(bf16[576,254]{1,0:T(8,128)(2,1)S(1)} %collective-permute-done.4.rest_4_), channel_id=1, source_target_pairs={{2,0},{3,7},{6,2},{7,11},{10,6},{11,15},{14,10},{15,13},{12,14},{1... | collective-permute-start | bytes 877832 | tf_op jit(solution)/shard_map/ppermute | solution.py:302
  28.5 9.4 %collective-permute-start.6 = (bf16[576,254]{1,0:T(8,128)(2,1)S(1)}, bf16[576,254]{1,0:T(8,128)(2,1)S(1)}, u32[]{:S(2)}, u32[]{:S(2)}) collective-permute-start(bf16[576,254]{1,0:T(8,128)(2,1)S(1)} %collective-permute-done.1.rest_3_), channel_id=1, source_target_pairs={{2,6},{3,1},{6,10},{7,3},{10,14},{11,7},{14,12},{15,11},{12,8},{13... | collective-permute-start | bytes 877832 | tf_op jit(solution)/shard_map/ppermute | solution.py:302
  35.6 7.4 %collective-permute-start.8 = (bf16[320,254]{1,0:T(8,128)(2,1)S(1)}, bf16[320,254]{1,0:T(8,128)(2,1)S(1)}, u32[]{:S(2)}, u32[]{:S(2)}) collective-permute-start(bf16[320,254]{1,0:T(8,128)(2,1)S(1)} %slice.7), channel_id=1, source_target_pairs={{2,0},{3,7},{6,2},{7,11},{10,6},{11,15},{14,10},{15,13},{12,14},{1... | collective-permute-start | bytes 487688 | tf_op jit(solution)/shard_map/ppermute | solution.py:317
  37.9 5.0 %collective-permute-start.7 = (bf16[256,254]{1,0:T(8,128)(2,1)S(1)}, bf16[256,254]{1,0:T(8,128)(2,1)S(1)}, u32[]{:S(2)}, u32[]{:S(2)}) collective-permute-start(bf16[256,254]{1,0:T(8,128)(2,1)S(1)} %slice.8), channel_id=1, source_target_pairs={{2,6},{3,1},{6,10},{7,3},{10,14},{11,7},{14,12},{15,11},{12,8},{13... | collective-permute-start | bytes 390152 | tf_op jit(solution)/shard_map/ppermute | solution.py:315
  38.6 4.3 %copy-start = (bf16[8,512,128]{2,1,0:T(8,128)(2,1)S(1)}, bf16[8,512,128]{2,1,0:T(8,128)(2,1)}, u32[]{:S(2)}) copy-start(bf16[8,512,128]{2,1,0:T(8,128)(2,1)} %own_up.1) | copy-start | bytes 3145732
  45.4 1.3 %collective-permute-start.10 = (bf16[16,2176]{1,0:T(8,128)(2,1)S(1)}, bf16[16,2176]{1,0:T(8,128)(2,1)S(1)}, u32[]{:S(2)}, u32[]{:S(2)}) collective-permute-start(bf16[16,2176]{1,0:T(8,128)(2,1)S(1)} %get-tuple-element.34), channel_id=1, source_target_pairs={{0,1},{1,0},{2,3},{3,2},{4,5},{5,4},{6,7},{7,6},{8,9},{9,8},{10,11... | collective-permute-start | bytes 208904 | tf_op jit(solution)/shard_map/ppermute | solution.py:337

commit v13 on v12

--- a/solution.py
+++ b/solution.py
@@ -301,7 +301,6 @@
     for s in range(2, steps):
         right, left = onward(right), backward(left)
         if s == 2:
-            here, right = lax.optimization_barrier((here, right))
             here = here.reshape(chips * tokens, (heads + 1) * width)
             there = lax.ppermute(here, "ctx", other_core)
             keys += [right, left]

time: 58.4 us -> 64.8 us (1.11)
  waiting for transfers between devices: 17.4 us -> 23.7 us
  blocking collectives: 10.4 us -> 11.4 us
  starting transfers between devices: 16.7 us -> 15.9 us
    ppermute x2, waiting for transfers between devices: 0.01 us -> 12.2 us  [on_device(): right, left = (onward(own), backward(own))]
    all_to_all x1, waiting for transfers between devices: 8.91 us -> 0.01 us  [on_device(): lax.all_to_all(pieces, 'ctx', split_axis=0, concat_axis=0, axis_index_gro...]
    ppermute x4, waiting for transfers between devices: 5.45 us -> 8.92 us  [on_device(): right, left = (onward(right), backward(left))]
    ppermute x4, starting transfers between devices: 4.91 us -> 2.96 us  [on_device(): right, left = (onward(right), backward(left))]
    all_to_all x1, blocking collectives: 10.4 us -> 11.4 us  [on_device(): lax.all_to_all(merged, 'ctx', split_axis=0, concat_axis=0, axis_index_gro...]
  transfers between devices with their start and end apart: 12 -> 12, of which waited for: 5 -> 5; matrix products, arithmetic and copies ran while one was open for 0% -> 0% of each run, Pallas kernels for 12% -> 11%
where the time goes in v13:
time: 64.8 us; the launch traced here: 64.5 us
  waiting for transfers between devices  23.7 us (37%)
  starting transfers between devices  15.9 us (25%)
  blocking collectives  11.4 us (18%)
  Pallas kernels  9.55 us (15%)
  local copies, waits for them, and re-layouts  2.54 us (4%)
  between operations  1.42 us (2%)
    ppermute x2, waiting for transfers between devices, on_device(): right, left = (onward(own), backward(own))  12.2 us
    all_to_all x1, blocking collectives, on_device(): lax.all_to_all(merged, 'ctx', split_axis=0, concat_axis=0, axis_index_gro...  11.4 us
    ppermute x4, waiting for transfers between devices, on_device(): right, left = (onward(right), backward(left))  8.92 us
    all_to_all x1, starting transfers between devices, on_device(): lax.all_to_all(pieces, 'ctx', split_axis=0, concat_axis=0, axis_index_gro...  4.92 us
    ppermute x2, starting transfers between devices, on_device(): right, left = (onward(own), backward(own))  4.59 us
    pallas_call x1, Pallas kernels, fold_first(): pl.pallas_call(functools.partial(first_kernel, heads, len(keys)), out_sha...  3.59 us
    ppermute x4, starting transfers between devices, on_device(): right, left = (onward(right), backward(left))  2.96 us
    pallas_call x1, Pallas kernels, on_device(): pl.pallas_call(functools.partial(span_kernel, at, len(keys)), out_shape=s...  2.48 us
  transfers between devices with their start and end apart: 12, of which 5 were waited for; matrix products, arithmetic and copies ran while one was open for 0% of the time, Pallas kernels for 11%

profile of v13, /device:TPU:0, one launch (start us, length us, event | category | flops | bytes accessed | tf_op | source)
XLA Modules:
  0.0 64.5 jit_solution(16738803336890050046)
XLA Ops:
  0.0 0.5 collective-permute-start.9
  0.5 2.6 %collective-permute-start.2 = (bf16[576,254]{1,0:T(8,128)(2,1)}, bf16[576,254]{1,0:T(8,128)(2,1)S(1)}, u32[]{:S(2)}, u32[]{:S(2)}) collective-permute-start(bf16[576,254]{1,0:T(8,128)(2,1)} %bitcast.4), channel_id=1, source_target_pairs={{2,0},{3,7},{6,2},{7,11},{10,6},{11,15},{14,10},{15,13},{12,14},{1... | collective-permute-start | bytes 877832 | tf_op jit(solution)/shard_map/ppermute | solution.py:285
  3.0 0.0 copy-start.1
  3.0 1.0 %copy-done.1 = bf16[2,73728]{1,0:T(2,128)(2,1)S(1)} copy-done((bf16[2,73728]{1,0:T(2,128)(2,1)S(1)}, bf16[2,73728]{1,0:T(2,128)(2,1)}, u32[]{:S(2)}) %copy-start.1) | copy-done | bytes 294936
  4.0 0.0 copy-start.4
  4.0 0.7 %copy-done.4 = bf16[2,576]{1,0:T(2,128)(2,1)S(1)} copy-done((bf16[2,576]{1,0:T(2,128)(2,1)S(1)}, bf16[2,576]{1,0:T(2,128)(2,1)}, u32[]{:S(2)}) %copy-start.4) | copy-done | bytes 2328
  4.7 0.7 %pieces.1 = bf16[8,2,9792]{2,1,0:T(2,128)(2,1)} custom-call(bf16[2,73728]{1,0:T(2,128)(2,1)S(1)} %copy-done.1, bf16[2,576]{1,0:T(2,128)(2,1)S(1)} %copy-done.4), custom_call_target="tpu_custom_call" | custom-call | tf_op jit(solution)/shard_map/pieces/pallas_call | solution.py:287
  5.4 0.0 copy-start.2
  5.4 4.9 %all-to-all-start = ((bf16[8,2,9792]{2,1,0:T(2,128)(2,1)}), bf16[8,2,9792]{2,1,0:T(2,128)(2,1)S(1)}, u32[]{:S(2)}, u32[]{:S(2)}) async-start(bf16[8,2,9792]{2,1,0:T(2,128)(2,1)} %pieces.1), calls=%async_computation | async-start | bytes 630784 | tf_op jit(solution)/shard_map/all_to_all | solution.py:295
  10.3 0.0 copy-done.2
  10.3 2.0 %collective-permute-start.1 = (bf16[576,254]{1,0:T(8,128)(2,1)S(1)}, bf16[576,254]{1,0:T(8,128)(2,1)S(1)}, u32[]{:S(2)}, u32[]{:S(2)}) collective-permute-start(bf16[576,254]{1,0:T(8,128)(2,1)S(1)} %bitcast.5), channel_id=1, source_target_pairs={{2,6},{3,1},{6,10},{7,3},{10,14},{11,7},{14,12},{15,11},{12,8},{13... | collective-permute-start | bytes 877832 | tf_op jit(solution)/shard_map/ppermute | solution.py:285
  12.4 0.0 collective-permute-done.2.rest_2_
  12.4 0.1 collective-permute-start.4
  12.4 12.2 %collective-permute-done.1.rest_1_ = bf16[576,254]{1,0:T(8,128)(2,1)S(1)} collective-permute-done((bf16[576,254]{1,0:T(8,128)(2,1)S(1)}, bf16[576,254]{1,0:T(8,128)(2,1)S(1)}, u32[]{:S(2)}, u32[]{:S(2)}) %collective-permute-start.1) | collective-permute-done | bytes 292640 | tf_op jit(solution)/shard_map/ppermute | solution.py:285
  24.7 0.0 collective-permute-start.3
  24.7 0.0 all-to-all-done
  24.7 0.2 reshape.6.here_ref
  24.9 0.0 copy-start.3
  24.9 0.2 collective-permute-start
  25.1 0.0 collective-permute-done.4.rest_4_
  25.1 2.9 %collective-permute-start.5 = (bf16[576,254]{1,0:T(8,128)(2,1)S(1)}, bf16[576,254]{1,0:T(8,128)(2,1)S(1)}, u32[]{:S(2)}, u32[]{:S(2)}) collective-permute-start(bf16[576,254]{1,0:T(8,128)(2,1)S(1)} %collective-permute-done.4.rest_4_), channel_id=1, source_target_pairs={{2,0},{3,7},{6,2},{7,11},{10,6},{11,15},{14,10},{15,13},{12,14},{1... | collective-permute-start | bytes 877832 | tf_op jit(solution)/shard_map/ppermute | solution.py:302
  28.0 7.3 %collective-permute-done.3.rest_3_ = bf16[576,254]{1,0:T(8,128)(2,1)S(1)} collective-permute-done((bf16[576,254]{1,0:T(8,128)(2,1)S(1)}, bf16[576,254]{1,0:T(8,128)(2,1)S(1)}, u32[]{:S(2)}, u32[]{:S(2)}) %collective-permute-start.3) | collective-permute-done | bytes 292640 | tf_op jit(solution)/shard_map/ppermute | solution.py:302
  35.3 0.0 collective-permute-start.6
  36.0 0.0 collective-permute-done.there_ref
  36.0 0.0 copy-done.3
  36.0 3.6 %first.1 = (bf16[512,576]{1,0:T(8,128)(2,1)S(1)}, f32[512,128]{1,0:T(8,128)S(1)}, f32[512,128]{1,0:T(8,128)S(1)}, f32[512,512]{1,0:T(8,128)S(1)}) custom-call(s32[1]{0:T(128)S(6)} %copy.9.length_ref, s32[128]{0:T(128)S(1)} %copy-done.3, bf16[16,9792]{1,0:T(8,128)(2,1)S(1)} %reshape.6.here_ref, bf16[16,9792]{1,0:T(8,128)(2,1)S(1)} %collective-permute-done.there_ref, ...), custom_call_target="tpu_custom_call" | custom-call | tf_op jit(solution)/shard_map/first/pallas_call | solution.py:262
  39.6 0.0 collective-permute-done.5.rest_1_
  39.6 2.1 %collective-permute-start.8 = (bf16[320,254]{1,0:T(8,128)(2,1)S(1)}, bf16[320,254]{1,0:T(8,128)(2,1)S(1)}, u32[]{:S(2)}, u32[]{:S(2)}) collective-permute-start(bf16[320,254]{1,0:T(8,128)(2,1)S(1)} %slice.7), channel_id=1, source_target_pairs={{2,0},{3,7},{6,2},{7,11},{10,6},{11,15},{14,10},{15,13},{12,14},{1... | collective-permute-start | bytes 487688 | tf_op jit(solution)/shard_map/ppermute | solution.py:316
  41.7 1.6 %collective-permute-done.6.rest_0_ = bf16[576,254]{1,0:T(8,128)(2,1)S(1)} collective-permute-done((bf16[576,254]{1,0:T(8,128)(2,1)S(1)}, bf16[576,254]{1,0:T(8,128)(2,1)S(1)}, u32[]{:S(2)}, u32[]{:S(2)}) %collective-permute-start.6) | collective-permute-done | bytes 292640 | tf_op jit(solution)/shard_map/ppermute | solution.py:302
  43.3 0.6 collective-permute-start.7
  44.5 0.0 copy-start
  44.6 2.5 %middle.1 = (f32[512,128]{1,0:T(8,128)S(1)}, f32[512,128]{1,0:T(8,128)S(1)}, f32[512,512]{1,0:T(8,128)S(1)}) custom-call(s32[1]{0:T(128)S(6)} %copy.9.length_ref, s32[1]{0:T(128)S(6)} %copy.10.offset_ref, s32[128]{0:T(128)S(1)} %copy-done.3, bf16[512,576]{1,0:T(8,128)(2,1)S(1)} %get-tuple-element.18.q_ref, f32[512,128]{1,0:T(8,128)S(1)} %get-tuple-element.22.m_in, ...), custom_call_target="tpu_custom_call" | custom-call | tf_op jit(solution)/shard_map/middle/pallas_call | solution.py:317
  47.0 1.3 %collective-permute-done.7.top_ref = bf16[256,254]{1,0:T(8,128)(2,1)S(1)} collective-permute-done((bf16[256,254]{1,0:T(8,128)(2,1)S(1)}, bf16[256,254]{1,0:T(8,128)(2,1)S(1)}, u32[]{:S(2)}, u32[]{:S(2)}) %collective-permute-start.7) | collective-permute-done | bytes 130080 | tf_op jit(solution)/shard_map/ppermute | solution.py:314
  48.3 0.0 collective-permute-done.8.bottom_ref
  48.4 0.0 collective-permute-done.9.far_up
  48.4 0.0 copy-done
  48.4 2.4 %last.1 = (f32[16,2176]{1,0:T(8,128)S(1)}, bf16[16,2176]{1,0:T(8,128)(2,1)S(1)}) custom-call(s32[1]{0:T(128)S(6)} %copy.9.length_ref, s32[128]{0:T(128)S(1)} %copy-done.3, bf16[512,576]{1,0:T(8,128)(2,1)S(1)} %get-tuple-element.18.q_ref, f32[512,128]{1,0:T(8,128)S(1)} %get-tuple-element.25.m_ref, f32[512,128]{1,0:T(8,128)S(1)} %get-tuple-element.26.l_ref, ...), custom_call_target="tpu_custom_call" | custom-call | tf_op jit(solution)/shard_map/last/pallas_call | solution.py:327
  50.8 0.1 collective-permute-start.10
  50.8 1.2 %collective-permute-done.10.got_ref = bf16[16,2176]{1,0:T(8,128)(2,1)S(1)} collective-permute-done((bf16[16,2176]{1,0:T(8,128)(2,1)S(1)}, bf16[16,2176]{1,0:T(8,128)(2,1)S(1)}, u32[]{:S(2)}, u32[]{:S(2)}) %collective-permute-start.10) | collective-permute-done | bytes 69664 | tf_op jit(solution)/shard_map/ppermute | solution.py:336
  52.1 0.3 merge.1
  52.4 11.4 %all_to_all.10 = bf16[8,2,2048]{2,1,0:T(2,128)(2,1)S(1)} all-to-all(bf16[8,2,2048]{2,1,0:T(2,128)(2,1)S(1)} %merge.1), channel_id=1, replica_groups={{0,2,4,6,8,10,12,14},{1,3,5,7,9,11,13,15},{16,18,20,22,24,26,28,30},{17..., dimensions={0} | all-to-all | bytes 131072 | tf_op jit(solution)/shard_map/all_to_all | solution.py:346
  63.8 0.6 copy.11
  (2 shorter events, 0.0 us)
Async XLA Ops:
  0.0 48.4 %collective-permute-start.9 = (bf16[8,512,128]{2,1,0:T(8,128)(2,1)}, bf16[8,512,128]{2,1,0:T(8,128)(2,1)S(1)}, u32[]{:S(2)}, u32[]{:S(2)}) collective-permute-start(bf16[8,512,128]{2,1,0:T(8,128)(2,1)} %own_up.1), channel_id=1, source_target_pairs={{0,1},{1,0},{2,3},{3,2},{4,5},{5,4},{6,7},{7,6},{8,9},{9,8},{10,11... | collective-permute-start | bytes 3145736 | tf_op jit(solution)/shard_map/ppermute | solution.py:298
  0.5 11.9 %collective-permute-start.2 = (bf16[576,254]{1,0:T(8,128)(2,1)}, bf16[576,254]{1,0:T(8,128)(2,1)S(1)}, u32[]{:S(2)}, u32[]{:S(2)}) collective-permute-start(bf16[576,254]{1,0:T(8,128)(2,1)} %bitcast.4), channel_id=1, source_target_pairs={{2,0},{3,7},{6,2},{7,11},{10,6},{11,15},{14,10},{15,13},{12,14},{1... | collective-permute-start | bytes 877832 | tf_op jit(solution)/shard_map/ppermute | solution.py:285
  3.0 1.0 %copy-start.1 = (bf16[2,73728]{1,0:T(2,128)(2,1)S(1)}, bf16[2,73728]{1,0:T(2,128)(2,1)}, u32[]{:S(2)}) copy-start(bf16[2,73728]{1,0:T(2,128)(2,1)} %queries_ref.1) | copy-start | bytes 884740
  4.0 0.7 %copy-start.4 = (bf16[2,576]{1,0:T(2,128)(2,1)S(1)}, bf16[2,576]{1,0:T(2,128)(2,1)}, u32[]{:S(2)}) copy-start(bf16[2,576]{1,0:T(2,128)(2,1)} %span_ref.1) | copy-start | bytes 6916
  5.4 4.9 %copy-start.2 = (bf16[254,576]{0,1:T(8,128)(2,1)S(1)}, bf16[254,576]{0,1:T(8,128)(2,1)}, u32[]{:S(2)}) copy-start(bf16[254,576]{0,1:T(8,128)(2,1)} %param.8) | copy-start | bytes 877828
  5.4 19.2 %all-to-all-start = ((bf16[8,2,9792]{2,1,0:T(2,128)(2,1)}), bf16[8,2,9792]{2,1,0:T(2,128)(2,1)S(1)}, u32[]{:S(2)}, u32[]{:S(2)}) async-start(bf16[8,2,9792]{2,1,0:T(2,128)(2,1)} %pieces.1), calls=%async_computation | async-start | bytes 630784 | tf_op jit(solution)/shard_map/all_to_all | solution.py:295
  10.3 14.3 %collective-permute-start.1 = (bf16[576,254]{1,0:T(8,128)(2,1)S(1)}, bf16[576,254]{1,0:T(8,128)(2,1)S(1)}, u32[]{:S(2)}, u32[]{:S(2)}) collective-permute-start(bf16[576,254]{1,0:T(8,128)(2,1)S(1)} %bitcast.5), channel_id=1, source_target_pairs={{2,6},{3,1},{6,10},{7,3},{10,14},{11,7},{14,12},{15,11},{12,8},{13... | collective-permute-start | bytes 877832 | tf_op jit(solution)/shard_map/ppermute | solution.py:285
  12.4 12.8 %collective-permute-start.4 = (bf16[576,254]{1,0:T(8,128)(2,1)S(1)}, bf16[576,254]{1,0:T(8,128)(2,1)S(1)}, u32[]{:S(2)}, u32[]{:S(2)}) collective-permute-start(bf16[576,254]{1,0:T(8,128)(2,1)S(1)} %collective-permute-done.2.rest_2_), channel_id=1, source_target_pairs={{2,0},{3,7},{6,2},{7,11},{10,6},{11,15},{14,10},{15,13},{12,14},{1... | collective-permute-start | bytes 877832 | tf_op jit(solution)/shard_map/ppermute | solution.py:302
  24.7 10.7 %collective-permute-start.3 = (bf16[576,254]{1,0:T(8,128)(2,1)S(1)}, bf16[576,254]{1,0:T(8,128)(2,1)S(1)}, u32[]{:S(2)}, u32[]{:S(2)}) collective-permute-start(bf16[576,254]{1,0:T(8,128)(2,1)S(1)} %collective-permute-done.1.rest_1_), channel_id=1, source_target_pairs={{2,6},{3,1},{6,10},{7,3},{10,14},{11,7},{14,12},{15,11},{12,8},{13... | collective-permute-start | bytes 877832 | tf_op jit(solution)/shard_map/ppermute | solution.py:302
  24.9 11.1 %copy-start.3 = (s32[128]{0:T(128)S(1)}, s32[128]{0:T(128)}, u32[]{:S(2)}) copy-start(s32[128]{0:T(128)} %constant.2.clone.table_ref) | copy-start | bytes 1540
  24.9 11.1 %collective-permute-start = (bf16[16,9792]{1,0:T(8,128)(2,1)S(1)}, bf16[16,9792]{1,0:T(8,128)(2,1)S(1)}, u32[]{:S(2)}, u32[]{:S(2)}) collective-permute-start(bf16[16,9792]{1,0:T(8,128)(2,1)S(1)} %reshape.6.here_ref), channel_id=1, source_target_pairs={{0,1},{1,0},{2,3},{3,2},{4,5},{5,4},{6,7},{7,6},{8,9},{9,8},{10,11... | collective-permute-start | bytes 940040 | tf_op jit(solution)/shard_map/ppermute | solution.py:305
  25.1 14.5 %collective-permute-start.5 = (bf16[576,254]{1,0:T(8,128)(2,1)S(1)}, bf16[576,254]{1,0:T(8,128)(2,1)S(1)}, u32[]{:S(2)}, u32[]{:S(2)}) collective-permute-start(bf16[576,254]{1,0:T(8,128)(2,1)S(1)} %collective-permute-done.4.rest_4_), channel_id=1, source_target_pairs={{2,0},{3,7},{6,2},{7,11},{10,6},{11,15},{14,10},{15,13},{12,14},{1... | collective-permute-start | bytes 877832 | tf_op jit(solution)/shard_map/ppermute | solution.py:302
  35.3 8.0 %collective-permute-start.6 = (bf16[576,254]{1,0:T(8,128)(2,1)S(1)}, bf16[576,254]{1,0:T(8,128)(2,1)S(1)}, u32[]{:S(2)}, u32[]{:S(2)}) collective-permute-start(bf16[576,254]{1,0:T(8,128)(2,1)S(1)} %collective-permute-done.3.rest_3_), channel_id=1, source_target_pairs={{2,6},{3,1},{6,10},{7,3},{10,14},{11,7},{14,12},{15,11},{12,8},{13... | collective-permute-start | bytes 877832 | tf_op jit(solution)/shard_map/ppermute | solution.py:302
  39.6 8.7 %collective-permute-start.8 = (bf16[320,254]{1,0:T(8,128)(2,1)S(1)}, bf16[320,254]{1,0:T(8,128)(2,1)S(1)}, u32[]{:S(2)}, u32[]{:S(2)}) collective-permute-start(bf16[320,254]{1,0:T(8,128)(2,1)S(1)} %slice.7), channel_id=1, source_target_pairs={{2,0},{3,7},{6,2},{7,11},{10,6},{11,15},{14,10},{15,13},{12,14},{1... | collective-permute-start | bytes 487688 | tf_op jit(solution)/shard_map/ppermute | solution.py:316
  43.3 5.0 %collective-permute-start.7 = (bf16[256,254]{1,0:T(8,128)(2,1)S(1)}, bf16[256,254]{1,0:T(8,128)(2,1)S(1)}, u32[]{:S(2)}, u32[]{:S(2)}) collective-permute-start(bf16[256,254]{1,0:T(8,128)(2,1)S(1)} %slice.8), channel_id=1, source_target_pairs={{2,6},{3,1},{6,10},{7,3},{10,14},{11,7},{14,12},{15,11},{12,8},{13... | collective-permute-start | bytes 390152 | tf_op jit(solution)/shard_map/ppermute | solution.py:314
  44.5 3.8 %copy-start = (bf16[8,512,128]{2,1,0:T(8,128)(2,1)S(1)}, bf16[8,512,128]{2,1,0:T(8,128)(2,1)}, u32[]{:S(2)}) copy-start(bf16[8,512,128]{2,1,0:T(8,128)(2,1)} %own_up.1) | copy-start | bytes 3145732
  50.8 1.3 %collective-permute-start.10 = (bf16[16,2176]{1,0:T(8,128)(2,1)S(1)}, bf16[16,2176]{1,0:T(8,128)(2,1)S(1)}, u32[]{:S(2)}, u32[]{:S(2)}) collective-permute-start(bf16[16,2176]{1,0:T(8,128)(2,1)S(1)} %get-tuple-element.30), channel_id=1, source_target_pairs={{0,1},{1,0},{2,3},{3,2},{4,5},{5,4},{6,7},{7,6},{8,9},{9,8},{10,11... | collective-permute-start | bytes 208904 | tf_op jit(solution)/shard_map/ppermute | solution.py:336

commit v14 on v13

--- a/solution.py
+++ b/solution.py
@@ -297,6 +297,7 @@
     )
     far_up = lax.ppermute(value_up, "ctx", other_core)
 
+    right, left = lax.optimization_barrier((right, left))
     keys, state, at = [own, right, left], None, 0
     for s in range(2, steps):
         right, left = onward(right), backward(left)

time: 64.8 us -> 58 us (0.90)
  waiting for transfers between devices: 23.7 us -> 16.2 us
    ppermute x2, waiting for transfers between devices: 12.2 us -> 0.01 us  [on_device(): right, left = (onward(own), backward(own))]
    all_to_all x1, waiting for transfers between devices: 0.01 us -> 9.31 us  [on_device(): lax.all_to_all(pieces, 'ctx', split_axis=0, concat_axis=0, axis_index_gro...]
    ppermute x4, waiting for transfers between devices: 8.92 us -> 4.7 us  [on_device(): right, left = (onward(right), backward(left))]
    ppermute x2, starting transfers between devices: 4.59 us -> 2.63 us  [on_device(): right, left = (onward(own), backward(own))]
    ppermute x4, starting transfers between devices: 2.96 us -> 4.46 us  [on_device(): right, left = (onward(right), backward(left))]
    all_to_all x1, starting transfers between devices: 4.92 us -> 6.2 us  [on_device(): lax.all_to_all(pieces, 'ctx', split_axis=0, concat_axis=0, axis_index_gro...]
  transfers between devices with their start and end apart: 12 -> 12, of which waited for: 5 -> 5; matrix products, arithmetic and copies ran while one was open for 0% -> 0% of each run, Pallas kernels for 11% -> 12%
where the time goes in v14:
time: 58 us; the launch traced here: 57.7 us
  starting transfers between devices  16.5 us (28%)
  waiting for transfers between devices  16.2 us (28%)
  blocking collectives  11.5 us (20%)
  Pallas kernels  9.54 us (16%)
  local copies, waits for them, and re-layouts  2.54 us (4%)
  between operations  1.43 us (2%)
    all_to_all x1, blocking collectives, on_device(): lax.all_to_all(merged, 'ctx', split_axis=0, concat_axis=0, axis_index_gro...  11.5 us
    all_to_all x1, waiting for transfers between devices, on_device(): lax.all_to_all(pieces, 'ctx', split_axis=0, concat_axis=0, axis_index_gro...  9.31 us
    all_to_all x1, starting transfers between devices, on_device(): lax.all_to_all(pieces, 'ctx', split_axis=0, concat_axis=0, axis_index_gro...  6.2 us
    ppermute x4, waiting for transfers between devices, on_device(): right, left = (onward(right), backward(left))  4.7 us
    ppermute x4, starting transfers between devices, on_device(): right, left = (onward(right), backward(left))  4.46 us
    pallas_call x1, Pallas kernels, fold_first(): pl.pallas_call(functools.partial(first_kernel, heads, len(keys)), out_sha...  3.59 us
    ppermute x2, starting transfers between devices, on_device(): right, left = (onward(own), backward(own))  2.63 us
    pallas_call x1, Pallas kernels, on_device(): pl.pallas_call(functools.partial(span_kernel, at, len(keys)), out_shape=s...  2.48 us
  transfers between devices with their start and end apart: 12, of which 5 were waited for; matrix products, arithmetic and copies ran while one was open for 0% of the time, Pallas kernels for 12%

profile of v14, /device:TPU:0, one launch (start us, length us, event | category | flops | bytes accessed | tf_op | source)
XLA Modules:
  0.0 57.7 jit_solution(17231142462472142263)
XLA Ops:
  0.0 0.5 collective-permute-start.9
  0.5 2.5 %collective-permute-start.1 = (bf16[576,254]{1,0:T(8,128)(2,1)}, bf16[576,254]{1,0:T(8,128)(2,1)S(1)}, u32[]{:S(2)}, u32[]{:S(2)}) collective-permute-start(bf16[576,254]{1,0:T(8,128)(2,1)} %bitcast.4), channel_id=1, source_target_pairs={{2,6},{3,1},{6,10},{7,3},{10,14},{11,7},{14,12},{15,11},{12,8},{13... | collective-permute-start | bytes 877832 | tf_op jit(solution)/shard_map/ppermute | solution.py:285
  2.9 0.1 collective-permute-start.2
  3.1 0.0 copy-start.1
  3.1 1.0 %copy-done.1 = bf16[2,73728]{1,0:T(2,128)(2,1)S(1)} copy-done((bf16[2,73728]{1,0:T(2,128)(2,1)S(1)}, bf16[2,73728]{1,0:T(2,128)(2,1)}, u32[]{:S(2)}) %copy-start.1) | copy-done | bytes 294936
  4.0 0.0 copy-start.4
  4.0 0.7 %copy-done.4 = bf16[2,576]{1,0:T(2,128)(2,1)S(1)} copy-done((bf16[2,576]{1,0:T(2,128)(2,1)S(1)}, bf16[2,576]{1,0:T(2,128)(2,1)}, u32[]{:S(2)}) %copy-start.4) | copy-done | bytes 2328
  4.7 0.7 %pieces.1 = bf16[8,2,9792]{2,1,0:T(2,128)(2,1)} custom-call(bf16[2,73728]{1,0:T(2,128)(2,1)S(1)} %copy-done.1, bf16[2,576]{1,0:T(2,128)(2,1)S(1)} %copy-done.4), custom_call_target="tpu_custom_call" | custom-call | tf_op jit(solution)/shard_map/pieces/pallas_call | solution.py:287
  5.5 6.2 %all-to-all-start = ((bf16[8,2,9792]{2,1,0:T(2,128)(2,1)}), bf16[8,2,9792]{2,1,0:T(2,128)(2,1)S(1)}, u32[]{:S(2)}, u32[]{:S(2)}) async-start(bf16[8,2,9792]{2,1,0:T(2,128)(2,1)} %pieces.1), calls=%async_computation | async-start | bytes 630784 | tf_op jit(solution)/shard_map/all_to_all | solution.py:295
  11.7 0.0 copy-start.2
  11.7 0.0 collective-permute-done.1.rest_1_
  11.7 0.0 collective-permute-done.2.rest_2_
  11.7 2.1 %collective-permute-start.4 = (bf16[576,254]{1,0:T(8,128)(2,1)S(1)}, bf16[576,254]{1,0:T(8,128)(2,1)S(1)}, u32[]{:S(2)}, u32[]{:S(2)}) collective-permute-start(bf16[576,254]{1,0:T(8,128)(2,1)S(1)} %collective-permute-done.2.rest_2_), channel_id=1, source_target_pairs={{2,0},{3,7},{6,2},{7,11},{10,6},{11,15},{14,10},{15,13},{12,14},{1... | collective-permute-start | bytes 877832 | tf_op jit(solution)/shard_map/ppermute | solution.py:303
  13.8 0.1 collective-permute-start.3
  13.8 9.3 %all-to-all-done = bf16[8,2,9792]{2,1,0:T(2,128)(2,1)S(1)} async-done(((bf16[8,2,9792]{2,1,0:T(2,128)(2,1)}), bf16[8,2,9792]{2,1,0:T(2,128)(2,1)S(1)}, u32[]{:S(2)}, u32[]{:S(2)}) %all-to-all-start) | async-done | bytes 313376 | tf_op jit(solution)/shard_map/all_to_all | solution.py:295
  23.1 0.2 reshape.6.here_ref
  23.4 0.0 copy-start.3
  23.4 0.1 collective-permute-start
  23.5 1.3 %collective-permute-done.4.rest_4_ = bf16[576,254]{1,0:T(8,128)(2,1)S(1)} collective-permute-done((bf16[576,254]{1,0:T(8,128)(2,1)S(1)}, bf16[576,254]{1,0:T(8,128)(2,1)S(1)}, u32[]{:S(2)}, u32[]{:S(2)}) %collective-permute-start.4) | collective-permute-done | bytes 292640 | tf_op jit(solution)/shard_map/ppermute | solution.py:303
  24.7 1.8 %collective-permute-start.5 = (bf16[576,254]{1,0:T(8,128)(2,1)S(1)}, bf16[576,254]{1,0:T(8,128)(2,1)S(1)}, u32[]{:S(2)}, u32[]{:S(2)}) collective-permute-start(bf16[576,254]{1,0:T(8,128)(2,1)S(1)} %collective-permute-done.4.rest_4_), channel_id=1, source_target_pairs={{2,0},{3,7},{6,2},{7,11},{10,6},{11,15},{14,10},{15,13},{12,14},{1... | collective-permute-start | bytes 877832 | tf_op jit(solution)/shard_map/ppermute | solution.py:303
  26.5 0.0 collective-permute-done.3.rest_3_
  26.5 0.6 collective-permute-start.6
  27.7 0.0 collective-permute-done.there_ref
  27.7 0.0 copy-done.2
  27.7 0.0 copy-done.3
  27.7 3.6 %first.1 = (bf16[512,576]{1,0:T(8,128)(2,1)S(1)}, f32[512,128]{1,0:T(8,128)S(1)}, f32[512,128]{1,0:T(8,128)S(1)}, f32[512,512]{1,0:T(8,128)S(1)}) custom-call(s32[1]{0:T(128)S(6)} %copy.9.length_ref, s32[128]{0:T(128)S(1)} %copy-done.3, bf16[16,9792]{1,0:T(8,128)(2,1)S(1)} %reshape.6.here_ref, bf16[16,9792]{1,0:T(8,128)(2,1)S(1)} %collective-permute-done.there_ref, ...), custom_call_target="tpu_custom_call" | custom-call | tf_op jit(solution)/shard_map/first/pallas_call | solution.py:262
  31.3 3.4 %collective-permute-done.5.rest_1_ = bf16[576,254]{1,0:T(8,128)(2,1)S(1)} collective-permute-done((bf16[576,254]{1,0:T(8,128)(2,1)S(1)}, bf16[576,254]{1,0:T(8,128)(2,1)S(1)}, u32[]{:S(2)}, u32[]{:S(2)}) %collective-permute-start.5) | collective-permute-done | bytes 292640 | tf_op jit(solution)/shard_map/ppermute | solution.py:303
  34.8 1.6 %collective-permute-start.8 = (bf16[320,254]{1,0:T(8,128)(2,1)S(1)}, bf16[320,254]{1,0:T(8,128)(2,1)S(1)}, u32[]{:S(2)}, u32[]{:S(2)}) collective-permute-start(bf16[320,254]{1,0:T(8,128)(2,1)S(1)} %slice.7), channel_id=1, source_target_pairs={{2,0},{3,7},{6,2},{7,11},{10,6},{11,15},{14,10},{15,13},{12,14},{1... | collective-permute-start | bytes 487688 | tf_op jit(solution)/shard_map/ppermute | solution.py:317
  36.4 0.0 collective-permute-done.6.rest_0_
  36.4 1.0 %collective-permute-start.7 = (bf16[256,254]{1,0:T(8,128)(2,1)S(1)}, bf16[256,254]{1,0:T(8,128)(2,1)S(1)}, u32[]{:S(2)}, u32[]{:S(2)}) collective-permute-start(bf16[256,254]{1,0:T(8,128)(2,1)S(1)} %slice.8), channel_id=1, source_target_pairs={{2,6},{3,1},{6,10},{7,3},{10,14},{11,7},{14,12},{15,11},{12,8},{13... | collective-permute-start | bytes 390152 | tf_op jit(solution)/shard_map/ppermute | solution.py:315
  38.1 0.0 copy-start
  38.1 2.5 %middle.1 = (f32[512,128]{1,0:T(8,128)S(1)}, f32[512,128]{1,0:T(8,128)S(1)}, f32[512,512]{1,0:T(8,128)S(1)}) custom-call(s32[1]{0:T(128)S(6)} %copy.9.length_ref, s32[1]{0:T(128)S(6)} %copy.10.offset_ref, s32[128]{0:T(128)S(1)} %copy-done.3, bf16[512,576]{1,0:T(8,128)(2,1)S(1)} %get-tuple-element.22.q_ref, f32[512,128]{1,0:T(8,128)S(1)} %get-tuple-element.26.m_in, ...), custom_call_target="tpu_custom_call" | custom-call | tf_op jit(solution)/shard_map/middle/pallas_call | solution.py:318
  40.6 0.9 %collective-permute-done.7.top_ref = bf16[256,254]{1,0:T(8,128)(2,1)S(1)} collective-permute-done((bf16[256,254]{1,0:T(8,128)(2,1)S(1)}, bf16[256,254]{1,0:T(8,128)(2,1)S(1)}, u32[]{:S(2)}, u32[]{:S(2)}) %collective-permute-start.7) | collective-permute-done | bytes 130080 | tf_op jit(solution)/shard_map/ppermute | solution.py:315
  41.5 0.0 collective-permute-done.8.bottom_ref
  41.5 0.0 collective-permute-done.9.far_up
  41.5 0.0 copy-done
  41.5 2.4 %last.1 = (f32[16,2176]{1,0:T(8,128)S(1)}, bf16[16,2176]{1,0:T(8,128)(2,1)S(1)}) custom-call(s32[1]{0:T(128)S(6)} %copy.9.length_ref, s32[128]{0:T(128)S(1)} %copy-done.3, bf16[512,576]{1,0:T(8,128)(2,1)S(1)} %get-tuple-element.22.q_ref, f32[512,128]{1,0:T(8,128)S(1)} %get-tuple-element.29.m_ref, f32[512,128]{1,0:T(8,128)S(1)} %get-tuple-element.30.l_ref, ...), custom_call_target="tpu_custom_call" | custom-call | tf_op jit(solution)/shard_map/last/pallas_call | solution.py:328
  43.9 0.1 collective-permute-start.10
  44.0 1.2 %collective-permute-done.10.got_ref = bf16[16,2176]{1,0:T(8,128)(2,1)S(1)} collective-permute-done((bf16[16,2176]{1,0:T(8,128)(2,1)S(1)}, bf16[16,2176]{1,0:T(8,128)(2,1)S(1)}, u32[]{:S(2)}, u32[]{:S(2)}) %collective-permute-start.10) | collective-permute-done | bytes 69664 | tf_op jit(solution)/shard_map/ppermute | solution.py:337
  45.2 0.3 merge.1
  45.5 11.5 %all_to_all.10 = bf16[8,2,2048]{2,1,0:T(2,128)(2,1)S(1)} all-to-all(bf16[8,2,2048]{2,1,0:T(2,128)(2,1)S(1)} %merge.1), channel_id=1, replica_groups={{0,2,4,6,8,10,12,14},{1,3,5,7,9,11,13,15},{16,18,20,22,24,26,28,30},{17..., dimensions={0} | all-to-all | bytes 131072 | tf_op jit(solution)/shard_map/all_to_all | solution.py:347
  57.1 0.6 %copy.11 = bf16[2,16384]{1,0:T(2,128)(2,1)} copy(bf16[2,16384]{1,0:T(2,128)(2,1)S(1)} %bitcast.7) | data formatting | bytes 131072
  (2 shorter events, 0.0 us)
Async XLA Ops:
  0.0 41.5 %collective-permute-start.9 = (bf16[8,512,128]{2,1,0:T(8,128)(2,1)}, bf16[8,512,128]{2,1,0:T(8,128)(2,1)S(1)}, u32[]{:S(2)}, u32[]{:S(2)}) collective-permute-start(bf16[8,512,128]{2,1,0:T(8,128)(2,1)} %own_up.1), channel_id=1, source_target_pairs={{0,1},{1,0},{2,3},{3,2},{4,5},{5,4},{6,7},{7,6},{8,9},{9,8},{10,11... | collective-permute-start | bytes 3145736 | tf_op jit(solution)/shard_map/ppermute | solution.py:298
  0.5 11.2 %collective-permute-start.1 = (bf16[576,254]{1,0:T(8,128)(2,1)}, bf16[576,254]{1,0:T(8,128)(2,1)S(1)}, u32[]{:S(2)}, u32[]{:S(2)}) collective-permute-start(bf16[576,254]{1,0:T(8,128)(2,1)} %bitcast.4), channel_id=1, source_target_pairs={{2,6},{3,1},{6,10},{7,3},{10,14},{11,7},{14,12},{15,11},{12,8},{13... | collective-permute-start | bytes 877832 | tf_op jit(solution)/shard_map/ppermute | solution.py:285
  2.9 8.7 %collective-permute-start.2 = (bf16[576,254]{1,0:T(8,128)(2,1)}, bf16[576,254]{1,0:T(8,128)(2,1)S(1)}, u32[]{:S(2)}, u32[]{:S(2)}) collective-permute-start(bf16[576,254]{1,0:T(8,128)(2,1)} %bitcast.5), channel_id=1, source_target_pairs={{2,0},{3,7},{6,2},{7,11},{10,6},{11,15},{14,10},{15,13},{12,14},{1... | collective-permute-start | bytes 877832 | tf_op jit(solution)/shard_map/ppermute | solution.py:285
  3.1 1.0 %copy-start.1 = (bf16[2,73728]{1,0:T(2,128)(2,1)S(1)}, bf16[2,73728]{1,0:T(2,128)(2,1)}, u32[]{:S(2)}) copy-start(bf16[2,73728]{1,0:T(2,128)(2,1)} %queries_ref.1) | copy-start | bytes 884740
  4.0 0.7 %copy-start.4 = (bf16[2,576]{1,0:T(2,128)(2,1)S(1)}, bf16[2,576]{1,0:T(2,128)(2,1)}, u32[]{:S(2)}) copy-start(bf16[2,576]{1,0:T(2,128)(2,1)} %span_ref.1) | copy-start | bytes 6916
  5.5 17.7 %all-to-all-start = ((bf16[8,2,9792]{2,1,0:T(2,128)(2,1)}), bf16[8,2,9792]{2,1,0:T(2,128)(2,1)S(1)}, u32[]{:S(2)}, u32[]{:S(2)}) async-start(bf16[8,2,9792]{2,1,0:T(2,128)(2,1)} %pieces.1), calls=%async_computation | async-start | bytes 630784 | tf_op jit(solution)/shard_map/all_to_all | solution.py:295
  11.7 16.0 %copy-start.2 = (bf16[254,576]{0,1:T(8,128)(2,1)S(1)}, bf16[254,576]{0,1:T(8,128)(2,1)}, u32[]{:S(2)}) copy-start(bf16[254,576]{0,1:T(8,128)(2,1)} %param.8) | copy-start | bytes 877828
  11.7 13.0 %collective-permute-start.4 = (bf16[576,254]{1,0:T(8,128)(2,1)S(1)}, bf16[576,254]{1,0:T(8,128)(2,1)S(1)}, u32[]{:S(2)}, u32[]{:S(2)}) collective-permute-start(bf16[576,254]{1,0:T(8,128)(2,1)S(1)} %collective-permute-done.2.rest_2_), channel_id=1, source_target_pairs={{2,0},{3,7},{6,2},{7,11},{10,6},{11,15},{14,10},{15,13},{12,14},{1... | collective-permute-start | bytes 877832 | tf_op jit(solution)/shard_map/ppermute | solution.py:303
  13.8 12.7 %collective-permute-start.3 = (bf16[576,254]{1,0:T(8,128)(2,1)S(1)}, bf16[576,254]{1,0:T(8,128)(2,1)S(1)}, u32[]{:S(2)}, u32[]{:S(2)}) collective-permute-start(bf16[576,254]{1,0:T(8,128)(2,1)S(1)} %collective-permute-done.1.rest_1_), channel_id=1, source_target_pairs={{2,6},{3,1},{6,10},{7,3},{10,14},{11,7},{14,12},{15,11},{12,8},{13... | collective-permute-start | bytes 877832 | tf_op jit(solution)/shard_map/ppermute | solution.py:303
  23.4 4.4 %copy-start.3 = (s32[128]{0:T(128)S(1)}, s32[128]{0:T(128)}, u32[]{:S(2)}) copy-start(s32[128]{0:T(128)} %constant.2.clone.table_ref) | copy-start | bytes 1540
  23.4 4.3 %collective-permute-start = (bf16[16,9792]{1,0:T(8,128)(2,1)S(1)}, bf16[16,9792]{1,0:T(8,128)(2,1)S(1)}, u32[]{:S(2)}, u32[]{:S(2)}) collective-permute-start(bf16[16,9792]{1,0:T(8,128)(2,1)S(1)} %reshape.6.here_ref), channel_id=1, source_target_pairs={{0,1},{1,0},{2,3},{3,2},{4,5},{5,4},{6,7},{7,6},{8,9},{9,8},{10,11... | collective-permute-start | bytes 940040 | tf_op jit(solution)/shard_map/ppermute | solution.py:306
  24.7 10.1 %collective-permute-start.5 = (bf16[576,254]{1,0:T(8,128)(2,1)S(1)}, bf16[576,254]{1,0:T(8,128)(2,1)S(1)}, u32[]{:S(2)}, u32[]{:S(2)}) collective-permute-start(bf16[576,254]{1,0:T(8,128)(2,1)S(1)} %collective-permute-done.4.rest_4_), channel_id=1, source_target_pairs={{2,0},{3,7},{6,2},{7,11},{10,6},{11,15},{14,10},{15,13},{12,14},{1... | collective-permute-start | bytes 877832 | tf_op jit(solution)/shard_map/ppermute | solution.py:303
  26.5 9.9 %collective-permute-start.6 = (bf16[576,254]{1,0:T(8,128)(2,1)S(1)}, bf16[576,254]{1,0:T(8,128)(2,1)S(1)}, u32[]{:S(2)}, u32[]{:S(2)}) collective-permute-start(bf16[576,254]{1,0:T(8,128)(2,1)S(1)} %collective-permute-done.3.rest_3_), channel_id=1, source_target_pairs={{2,6},{3,1},{6,10},{7,3},{10,14},{11,7},{14,12},{15,11},{12,8},{13... | collective-permute-start | bytes 877832 | tf_op jit(solution)/shard_map/ppermute | solution.py:303
  34.8 6.7 %collective-permute-start.8 = (bf16[320,254]{1,0:T(8,128)(2,1)S(1)}, bf16[320,254]{1,0:T(8,128)(2,1)S(1)}, u32[]{:S(2)}, u32[]{:S(2)}) collective-permute-start(bf16[320,254]{1,0:T(8,128)(2,1)S(1)} %slice.7), channel_id=1, source_target_pairs={{2,0},{3,7},{6,2},{7,11},{10,6},{11,15},{14,10},{15,13},{12,14},{1... | collective-permute-start | bytes 487688 | tf_op jit(solution)/shard_map/ppermute | solution.py:317
  36.4 5.0 %collective-permute-start.7 = (bf16[256,254]{1,0:T(8,128)(2,1)S(1)}, bf16[256,254]{1,0:T(8,128)(2,1)S(1)}, u32[]{:S(2)}, u32[]{:S(2)}) collective-permute-start(bf16[256,254]{1,0:T(8,128)(2,1)S(1)} %slice.8), channel_id=1, source_target_pairs={{2,6},{3,1},{6,10},{7,3},{10,14},{11,7},{14,12},{15,11},{12,8},{13... | collective-permute-start | bytes 390152 | tf_op jit(solution)/shard_map/ppermute | solution.py:315
  38.1 3.4 %copy-start = (bf16[8,512,128]{2,1,0:T(8,128)(2,1)S(1)}, bf16[8,512,128]{2,1,0:T(8,128)(2,1)}, u32[]{:S(2)}) copy-start(bf16[8,512,128]{2,1,0:T(8,128)(2,1)} %own_up.1) | copy-start | bytes 3145732
  43.9 1.3 %collective-permute-start.10 = (bf16[16,2176]{1,0:T(8,128)(2,1)S(1)}, bf16[16,2176]{1,0:T(8,128)(2,1)S(1)}, u32[]{:S(2)}, u32[]{:S(2)}) collective-permute-start(bf16[16,2176]{1,0:T(8,128)(2,1)S(1)} %get-tuple-element.34), channel_id=1, source_target_pairs={{0,1},{1,0},{2,3},{3,2},{4,5},{5,4},{6,7},{7,6},{8,9},{9,8},{10,11... | collective-permute-start | bytes 208904 | tf_op jit(solution)/shard_map/ppermute | solution.py:337

commit v15 on v13

--- a/solution.py
+++ b/solution.py
@@ -33,13 +33,34 @@
     return walk + [z * wide for z in reversed(range(tall))]
 
 
+def scores_of(q_ref, part, pieces):
+    total, at = None, 0
+    for piece in pieces:
+        s = jnp.dot(
+            q_ref[part, at:at + piece.shape[0]], piece[...], preferred_element_type=f32
+        )
+        total, at = s if total is None else total + s, at + piece.shape[0]
+    return total
+
+
+def values_of(weights, pieces):
+    summed, at = [], 0
+    for piece in pieces:
+        wide = min(piece.shape[0], LATENT - at)
+        summed.append(lax.dot_general(
+            weights, piece[:wide, :], (((1,), (1,)), ((), ())), preferred_element_type=f32
+        ))
+        at += wide
+    return summed[0] if len(summed) == 1 else jnp.concatenate(summed, axis=1)
+
+
 def fold_block(part, q_ref, shards, length, old=None, span=None):
     m_old = least_max if old is None else old[0][part, :][:, :1]
     m_new = m_old
     scores = []
     for base, key_ref in shards:
-        slot = base + lax.broadcasted_iota(jnp.int32, (1, key_ref.shape[1]), 1)
-        s = jnp.dot(q_ref[part, :], key_ref[...], preferred_element_type=f32) * score_scale
+        slot = base + lax.broadcasted_iota(jnp.int32, (1, key_ref[0].shape[1]), 1)
+        s = scores_of(q_ref, part, key_ref) * score_scale
         s = jnp.where(slot < length, s, neg_large)
         m_new = jnp.maximum(m_new, jnp.max(s, axis=1, keepdims=True))
         scores.append(s)
@@ -58,10 +79,7 @@
     for s, (_, key_ref) in zip(scores, shards):
         probs = jnp.exp2(s - m_new)
         l_new += jnp.sum(probs, axis=1, keepdims=True)
-        summed += lax.dot_general(
-            probs.astype(bf16), key_ref[:LATENT, :], (((1,), (1,)), ((), ())),
-            preferred_element_type=f32,
-        )
+        summed += values_of(probs.astype(bf16), key_ref)
     if span is not None:
         probs = jnp.exp2(span_s - m_new)
         l_new += jnp.sum(probs, axis=1, keepdims=True)
@@ -97,7 +115,7 @@
     me = lax.axis_index("ctx")
     count = table_ref.shape[0] // lax.axis_size("ctx")
     return [
-        (table_ref[me * count + at + j] * key_ref.shape[1], key_ref)
+        (table_ref[me * count + at + j] * key_ref.shape[1], (key_ref,))
         for j, key_ref in enumerate(key_refs)
     ]
 
@@ -148,17 +166,10 @@
     )
 
 
-def join_halves(top_ref, bottom_ref, key_ref):
-    cut = top_ref.shape[0]
-    key_ref[:cut, :] = top_ref[...]
-    key_ref[cut:, :] = bottom_ref[...]
-
-
 def last_kernel(at, heads, length_ref, table_ref, q_ref, m_ref, l_ref, acc_ref,
-                top_ref, bottom_ref, own_up, far_up, keep_ref, give_ref, key_ref, flat_ref):
-    join_halves(top_ref, bottom_ref, key_ref)
+                top_ref, bottom_ref, own_up, far_up, keep_ref, give_ref, flat_ref):
     core = lax.axis_index("ctx") % CORES
-    shards = with_base(table_ref, at, (key_ref,))
+    shards = [(with_base(table_ref, at, (top_ref,))[0][0], (top_ref, bottom_ref))]
     everyone = flat_ref.shape[0]
     per_core = heads // CORES
     rows = per_core * everyone
@@ -172,9 +183,6 @@
         )
         context = (summed * (1.0 / l_new)).astype(bf16)
         weight = m_new + jnp.log2(l_new)
-        high = weight.astype(bf16).astype(f32)
-        mid = (weight - high).astype(bf16).astype(f32)
-        low = weight - high - mid
         for j in range(0, per_core, pair):
             lifted = jnp.dot(
                 context[j * everyone:(j + pair) * everyone, :],
@@ -184,14 +192,17 @@
             for i in range(pair):
                 head = (core ^ side) * per_core + j + i
                 here = slice((j + i) * everyone, (j + i + 1) * everyone)
-                tail = jnp.where(lane == head, high[here], tail)
-                tail = jnp.where(lane == head + heads, mid[here], tail)
-                tail = jnp.where(lane == head + 2 * heads, low[here], tail)
+                tail = jnp.where(lane == head, weight[here], tail)
                 lanes = pl.ds(pl.multiple_of(head * V_HEAD, V_HEAD), V_HEAD)
                 flat_ref[:, lanes] = lifted[
                     i * everyone:(i + 1) * everyone, i * V_HEAD:(i + 1) * V_HEAD
                 ]
-    flat_ref[:, heads * V_HEAD:] = tail
+    high = tail.astype(bf16).astype(f32)
+    mid = (tail - high).astype(bf16).astype(f32)
+    low = tail - high - mid
+    flat_ref[:, heads * V_HEAD:] = (
+        high + pltpu.roll(mid, heads, 1) + pltpu.roll(low, 2 * heads, 1)
+    )
     keep_ref[...] = flat_ref[:everyone // CORES, :]
     give_ref[...] = flat_ref[everyone // CORES:, :].astype(bf16)
 
@@ -295,8 +306,9 @@
     here = lax.all_to_all(
         pieces, "ctx", split_axis=0, concat_axis=0, axis_index_groups=same_core, tiled=True
     )
-    far_up = lax.ppermute(value_up, "ctx", other_core)
-
+
+    right, left, up = lax.optimization_barrier((right, left, value_up))
+    far_up = lax.ppermute(up, "ctx", other_core)
     keys, state, at = [own, right, left], None, 0
     for s in range(2, steps):
         right, left = onward(right), backward(left)
@@ -329,7 +341,7 @@
         out_shape=[shape(half, flat), shape(half, flat, dtype=bf16)],
         in_specs=[SMEM] * 2 + [VMEM] * 8,
         out_specs=[VMEM] * 2,
-        scratch_shapes=[pltpu.VMEM((width, slots), bf16), pltpu.VMEM((everyone, flat), f32)],
+        scratch_shapes=[pltpu.VMEM((everyone, flat), f32)],
         compiler_params=PARAMS,
         name="last",
     )(prefix_length, table, q, *state, top, bottom, value_up, far_up)

time: 64.8 us -> 66.1 us (1.020)
  starting transfers between devices: 15.9 us -> 17.2 us
    all_to_all x1, waiting for transfers between devices: 0.01 us -> 9.32 us  [on_device(): lax.all_to_all(pieces, 'ctx', split_axis=0, concat_axis=0, axis_index_gro...]
    ppermute x2, waiting for transfers between devices: 12.2 us -> 7.52 us  [on_device(): right, left = (onward(own), backward(own))]
    ppermute x4, waiting for transfers between devices: 8.92 us -> 4.59 us  [on_device(): right, left = (onward(right), backward(left))]
    ppermute x4, starting transfers between devices: 2.96 us -> 4.85 us  [on_device(): right, left = (onward(right), backward(left))]
    ppermute x2, starting transfers between devices: 4.59 us -> 3.03 us  [on_device(): right, left = (onward(own), backward(own))]
    ppermute x1, starting transfers between devices: 0.56 us -> 1.53 us  [on_device(): top = onward(right[:cut])]
  transfers between devices with their start and end apart: 12 -> 12, of which waited for: 5 -> 6; matrix products, arithmetic and copies ran while one was open for 0% -> 0% of each run, Pallas kernels for 11% -> 10%
where the time goes in v15:
time: 66.1 us; the launch traced here: 65.7 us
  waiting for transfers between devices  23.5 us (36%)
  starting transfers between devices  17.2 us (26%)
  blocking collectives  11.6 us (18%)
  Pallas kernels  9.53 us (14%)
  local copies, waits for them, and re-layouts  2.54 us (4%)
  between operations  1.42 us (2%)
    all_to_all x1, blocking collectives, on_device(): lax.all_to_all(merged, 'ctx', split_axis=0, concat_axis=0, axis_index_gro...  11.6 us
    all_to_all x1, waiting for transfers between devices, on_device(): lax.all_to_all(pieces, 'ctx', split_axis=0, concat_axis=0, axis_index_gro...  9.32 us
    ppermute x2, waiting for transfers between devices, on_device(): right, left = (onward(own), backward(own))  7.52 us
    all_to_all x1, starting transfers between devices, on_device(): lax.all_to_all(pieces, 'ctx', split_axis=0, concat_axis=0, axis_index_gro...  5.54 us
    ppermute x4, starting transfers between devices, on_device(): right, left = (onward(right), backward(left))  4.85 us
    ppermute x4, waiting for transfers between devices, on_device(): right, left = (onward(right), backward(left))  4.59 us
    pallas_call x1, Pallas kernels, fold_first(): pl.pallas_call(functools.partial(first_kernel, heads, len(keys)), out_sha...  3.59 us
    ppermute x2, starting transfers between devices, on_device(): right, left = (onward(own), backward(own))  3.03 us
  transfers between devices with their start and end apart: 12, of which 6 were waited for; matrix products, arithmetic and copies ran while one was open for 0% of the time, Pallas kernels for 10%

profile of v15, /device:TPU:0, one launch (start us, length us, event | category | flops | bytes accessed | tf_op | source)
XLA Modules:
  0.0 65.7 jit_solution(4751289681909835149)
XLA Ops:
  0.0 2.9 %collective-permute-start.1 = (bf16[576,254]{1,0:T(8,128)(2,1)}, bf16[576,254]{1,0:T(8,128)(2,1)S(1)}, u32[]{:S(2)}, u32[]{:S(2)}) collective-permute-start(bf16[576,254]{1,0:T(8,128)(2,1)} %bitcast.4), channel_id=1, source_target_pairs={{2,6},{3,1},{6,10},{7,3},{10,14},{11,7},{14,12},{15,11},{12,8},{13... | collective-permute-start | bytes 877832 | tf_op jit(solution)/shard_map/ppermute | solution.py:296
  2.9 0.1 collective-permute-start.2
  3.0 7.5 %collective-permute-done.1.rest_1_ = bf16[576,254]{1,0:T(8,128)(2,1)S(1)} collective-permute-done((bf16[576,254]{1,0:T(8,128)(2,1)}, bf16[576,254]{1,0:T(8,128)(2,1)S(1)}, u32[]{:S(2)}, u32[]{:S(2)}) %collective-permute-start.1) | collective-permute-done | bytes 292640 | tf_op jit(solution)/shard_map/ppermute | solution.py:296
  10.5 0.0 collective-permute-done.2.rest_2_
  10.5 0.4 collective-permute-start.9
  10.9 0.0 copy-start.1
  10.9 1.0 %copy-done.1 = bf16[2,73728]{1,0:T(2,128)(2,1)S(1)} copy-done((bf16[2,73728]{1,0:T(2,128)(2,1)S(1)}, bf16[2,73728]{1,0:T(2,128)(2,1)}, u32[]{:S(2)}) %copy-start.1) | copy-done | bytes 294936
  11.9 0.0 copy-start.4
  11.9 0.7 %copy-done.4 = bf16[2,576]{1,0:T(2,128)(2,1)S(1)} copy-done((bf16[2,576]{1,0:T(2,128)(2,1)S(1)}, bf16[2,576]{1,0:T(2,128)(2,1)}, u32[]{:S(2)}) %copy-start.4) | copy-done | bytes 2328
  12.6 0.7 %pieces.1 = bf16[8,2,9792]{2,1,0:T(2,128)(2,1)} custom-call(bf16[2,73728]{1,0:T(2,128)(2,1)S(1)} %copy-done.1, bf16[2,576]{1,0:T(2,128)(2,1)S(1)} %copy-done.4), custom_call_target="tpu_custom_call" | custom-call | tf_op jit(solution)/shard_map/pieces/pallas_call | solution.py:298
  13.3 5.5 %all-to-all-start = ((bf16[8,2,9792]{2,1,0:T(2,128)(2,1)}), bf16[8,2,9792]{2,1,0:T(2,128)(2,1)S(1)}, u32[]{:S(2)}, u32[]{:S(2)}) async-start(bf16[8,2,9792]{2,1,0:T(2,128)(2,1)} %pieces.1), calls=%async_computation | async-start | bytes 630784 | tf_op jit(solution)/shard_map/all_to_all | solution.py:306
  18.8 0.0 copy-start.2
  18.8 2.0 %collective-permute-start.4 = (bf16[576,254]{1,0:T(8,128)(2,1)S(1)}, bf16[576,254]{1,0:T(8,128)(2,1)S(1)}, u32[]{:S(2)}, u32[]{:S(2)}) collective-permute-start(bf16[576,254]{1,0:T(8,128)(2,1)S(1)} %collective-permute-done.2.rest_2_), channel_id=1, source_target_pairs={{2,0},{3,7},{6,2},{7,11},{10,6},{11,15},{14,10},{15,13},{12,14},{1... | collective-permute-start | bytes 877832 | tf_op jit(solution)/shard_map/ppermute | solution.py:314
  20.9 0.1 collective-permute-start.3
  20.9 9.3 %all-to-all-done = bf16[8,2,9792]{2,1,0:T(2,128)(2,1)S(1)} async-done(((bf16[8,2,9792]{2,1,0:T(2,128)(2,1)}), bf16[8,2,9792]{2,1,0:T(2,128)(2,1)S(1)}, u32[]{:S(2)}, u32[]{:S(2)}) %all-to-all-start) | async-done | bytes 313376 | tf_op jit(solution)/shard_map/all_to_all | solution.py:306
  30.2 0.2 reshape.6.here_ref
  30.5 0.0 copy-start.3
  30.5 0.1 collective-permute-start
  30.6 1.3 %collective-permute-done.4.rest_4_ = bf16[576,254]{1,0:T(8,128)(2,1)S(1)} collective-permute-done((bf16[576,254]{1,0:T(8,128)(2,1)S(1)}, bf16[576,254]{1,0:T(8,128)(2,1)S(1)}, u32[]{:S(2)}, u32[]{:S(2)}) %collective-permute-start.4) | collective-permute-done | bytes 292640 | tf_op jit(solution)/shard_map/ppermute | solution.py:314
  31.9 2.3 %collective-permute-start.5 = (bf16[576,254]{1,0:T(8,128)(2,1)S(1)}, bf16[576,254]{1,0:T(8,128)(2,1)S(1)}, u32[]{:S(2)}, u32[]{:S(2)}) collective-permute-start(bf16[576,254]{1,0:T(8,128)(2,1)S(1)} %collective-permute-done.4.rest_4_), channel_id=1, source_target_pairs={{2,0},{3,7},{6,2},{7,11},{10,6},{11,15},{14,10},{15,13},{12,14},{1... | collective-permute-start | bytes 877832 | tf_op jit(solution)/shard_map/ppermute | solution.py:314
  34.1 0.0 collective-permute-done.3.rest_3_
  34.1 0.5 collective-permute-start.6
  35.3 0.0 collective-permute-done.there_ref
  35.3 0.0 copy-done.2
  35.3 0.0 copy-done.3
  35.3 3.6 %first.1 = (bf16[512,576]{1,0:T(8,128)(2,1)S(1)}, f32[512,128]{1,0:T(8,128)S(1)}, f32[512,128]{1,0:T(8,128)S(1)}, f32[512,512]{1,0:T(8,128)S(1)}) custom-call(s32[1]{0:T(128)S(6)} %copy.9.length_ref, s32[128]{0:T(128)S(1)} %copy-done.3, bf16[16,9792]{1,0:T(8,128)(2,1)S(1)} %reshape.6.here_ref, bf16[16,9792]{1,0:T(8,128)(2,1)S(1)} %collective-permute-done.there_ref, ...), custom_call_target="tpu_custom_call" | custom-call | tf_op jit(solution)/shard_map/first/pallas_call | solution.py:273
  38.9 3.3 %collective-permute-done.5.rest_1_ = bf16[576,254]{1,0:T(8,128)(2,1)S(1)} collective-permute-done((bf16[576,254]{1,0:T(8,128)(2,1)S(1)}, bf16[576,254]{1,0:T(8,128)(2,1)S(1)}, u32[]{:S(2)}, u32[]{:S(2)}) %collective-permute-start.5) | collective-permute-done | bytes 292640 | tf_op jit(solution)/shard_map/ppermute | solution.py:314
  42.2 1.7 %collective-permute-start.8 = (bf16[320,254]{1,0:T(8,128)(2,1)S(1)}, bf16[320,254]{1,0:T(8,128)(2,1)S(1)}, u32[]{:S(2)}, u32[]{:S(2)}) collective-permute-start(bf16[320,254]{1,0:T(8,128)(2,1)S(1)} %slice.7), channel_id=1, source_target_pairs={{2,0},{3,7},{6,2},{7,11},{10,6},{11,15},{14,10},{15,13},{12,14},{1... | collective-permute-start | bytes 487688 | tf_op jit(solution)/shard_map/ppermute | solution.py:328
  43.9 0.0 collective-permute-done.6.rest_0_
  43.9 1.5 %collective-permute-start.7 = (bf16[256,254]{1,0:T(8,128)(2,1)S(1)}, bf16[256,254]{1,0:T(8,128)(2,1)S(1)}, u32[]{:S(2)}, u32[]{:S(2)}) collective-permute-start(bf16[256,254]{1,0:T(8,128)(2,1)S(1)} %slice.8), channel_id=1, source_target_pairs={{2,6},{3,1},{6,10},{7,3},{10,14},{11,7},{14,12},{15,11},{12,8},{13... | collective-permute-start | bytes 390152 | tf_op jit(solution)/shard_map/ppermute | solution.py:326
  46.1 0.0 copy-start
  46.1 2.5 %middle.1 = (f32[512,128]{1,0:T(8,128)S(1)}, f32[512,128]{1,0:T(8,128)S(1)}, f32[512,512]{1,0:T(8,128)S(1)}) custom-call(s32[1]{0:T(128)S(6)} %copy.9.length_ref, s32[1]{0:T(128)S(6)} %copy.10.offset_ref, s32[128]{0:T(128)S(1)} %copy-done.3, bf16[512,576]{1,0:T(8,128)(2,1)S(1)} %get-tuple-element.23.q_ref, f32[512,128]{1,0:T(8,128)S(1)} %get-tuple-element.27.m_in, ...), custom_call_target="tpu_custom_call" | custom-call | tf_op jit(solution)/shard_map/middle/pallas_call | solution.py:329
  48.6 0.8 %collective-permute-done.7.top_ref = bf16[256,254]{1,0:T(8,128)(2,1)S(1)} collective-permute-done((bf16[256,254]{1,0:T(8,128)(2,1)S(1)}, bf16[256,254]{1,0:T(8,128)(2,1)S(1)}, u32[]{:S(2)}, u32[]{:S(2)}) %collective-permute-start.7) | collective-permute-done | bytes 130080 | tf_op jit(solution)/shard_map/ppermute | solution.py:326
  49.4 0.0 collective-permute-done.8.bottom_ref
  49.4 0.0 collective-permute-done.9.far_up
  49.4 0.0 copy-done
  49.4 2.4 %last.1 = (f32[16,2176]{1,0:T(8,128)S(1)}, bf16[16,2176]{1,0:T(8,128)(2,1)S(1)}) custom-call(s32[1]{0:T(128)S(6)} %copy.9.length_ref, s32[128]{0:T(128)S(1)} %copy-done.3, bf16[512,576]{1,0:T(8,128)(2,1)S(1)} %get-tuple-element.23.q_ref, f32[512,128]{1,0:T(8,128)S(1)} %get-tuple-element.30.m_ref, f32[512,128]{1,0:T(8,128)S(1)} %get-tuple-element.31.l_ref, ...), custom_call_target="tpu_custom_call" | custom-call | tf_op jit(solution)/shard_map/last/pallas_call | solution.py:339
  51.8 0.1 collective-permute-start.10
  51.9 1.2 %collective-permute-done.10.got_ref = bf16[16,2176]{1,0:T(8,128)(2,1)S(1)} collective-permute-done((bf16[16,2176]{1,0:T(8,128)(2,1)S(1)}, bf16[16,2176]{1,0:T(8,128)(2,1)S(1)}, u32[]{:S(2)}, u32[]{:S(2)}) %collective-permute-start.10) | collective-permute-done | bytes 69664 | tf_op jit(solution)/shard_map/ppermute | solution.py:348
  53.2 0.3 merge.1
  53.5 11.6 %all_to_all.10 = bf16[8,2,2048]{2,1,0:T(2,128)(2,1)S(1)} all-to-all(bf16[8,2,2048]{2,1,0:T(2,128)(2,1)S(1)} %merge.1), channel_id=1, replica_groups={{0,2,4,6,8,10,12,14},{1,3,5,7,9,11,13,15},{16,18,20,22,24,26,28,30},{17..., dimensions={0} | all-to-all | bytes 131072 | tf_op jit(solution)/shard_map/all_to_all | solution.py:358
  65.1 0.6 copy.11
  (2 shorter events, 0.0 us)
Async XLA Ops:
  0.0 10.5 %collective-permute-start.1 = (bf16[576,254]{1,0:T(8,128)(2,1)}, bf16[576,254]{1,0:T(8,128)(2,1)S(1)}, u32[]{:S(2)}, u32[]{:S(2)}) collective-permute-start(bf16[576,254]{1,0:T(8,128)(2,1)} %bitcast.4), channel_id=1, source_target_pairs={{2,6},{3,1},{6,10},{7,3},{10,14},{11,7},{14,12},{15,11},{12,8},{13... | collective-permute-start | bytes 877832 | tf_op jit(solution)/shard_map/ppermute | solution.py:296
  2.9 7.6 %collective-permute-start.2 = (bf16[576,254]{1,0:T(8,128)(2,1)}, bf16[576,254]{1,0:T(8,128)(2,1)S(1)}, u32[]{:S(2)}, u32[]{:S(2)}) collective-permute-start(bf16[576,254]{1,0:T(8,128)(2,1)} %bitcast.5), channel_id=1, source_target_pairs={{2,0},{3,7},{6,2},{7,11},{10,6},{11,15},{14,10},{15,13},{12,14},{1... | collective-permute-start | bytes 877832 | tf_op jit(solution)/shard_map/ppermute | solution.py:296
  10.5 38.9 %collective-permute-start.9 = (bf16[8,512,128]{2,1,0:T(8,128)(2,1)}, bf16[8,512,128]{2,1,0:T(8,128)(2,1)S(1)}, u32[]{:S(2)}, u32[]{:S(2)}) collective-permute-start(bf16[8,512,128]{2,1,0:T(8,128)(2,1)} %own_up.1), channel_id=1, source_target_pairs={{0,1},{1,0},{2,3},{3,2},{4,5},{5,4},{6,7},{7,6},{8,9},{9,8},{10,11... | collective-permute-start | bytes 3145736 | tf_op jit(solution)/shard_map/ppermute | solution.py:311
  10.9 1.0 %copy-start.1 = (bf16[2,73728]{1,0:T(2,128)(2,1)S(1)}, bf16[2,73728]{1,0:T(2,128)(2,1)}, u32[]{:S(2)}) copy-start(bf16[2,73728]{1,0:T(2,128)(2,1)} %queries_ref.1) | copy-start | bytes 884740
  11.9 0.7 %copy-start.4 = (bf16[2,576]{1,0:T(2,128)(2,1)S(1)}, bf16[2,576]{1,0:T(2,128)(2,1)}, u32[]{:S(2)}) copy-start(bf16[2,576]{1,0:T(2,128)(2,1)} %span_ref.1) | copy-start | bytes 6916
  13.3 16.9 %all-to-all-start = ((bf16[8,2,9792]{2,1,0:T(2,128)(2,1)}), bf16[8,2,9792]{2,1,0:T(2,128)(2,1)S(1)}, u32[]{:S(2)}, u32[]{:S(2)}) async-start(bf16[8,2,9792]{2,1,0:T(2,128)(2,1)} %pieces.1), calls=%async_computation | async-start | bytes 630784 | tf_op jit(solution)/shard_map/all_to_all | solution.py:306
  18.8 16.5 %copy-start.2 = (bf16[254,576]{0,1:T(8,128)(2,1)S(1)}, bf16[254,576]{0,1:T(8,128)(2,1)}, u32[]{:S(2)}) copy-start(bf16[254,576]{0,1:T(8,128)(2,1)} %param.8) | copy-start | bytes 877828
  18.8 13.0 %collective-permute-start.4 = (bf16[576,254]{1,0:T(8,128)(2,1)S(1)}, bf16[576,254]{1,0:T(8,128)(2,1)S(1)}, u32[]{:S(2)}, u32[]{:S(2)}) collective-permute-start(bf16[576,254]{1,0:T(8,128)(2,1)S(1)} %collective-permute-done.2.rest_2_), channel_id=1, source_target_pairs={{2,0},{3,7},{6,2},{7,11},{10,6},{11,15},{14,10},{15,13},{12,14},{1... | collective-permute-start | bytes 877832 | tf_op jit(solution)/shard_map/ppermute | solution.py:314
  20.9 13.3 %collective-permute-start.3 = (bf16[576,254]{1,0:T(8,128)(2,1)S(1)}, bf16[576,254]{1,0:T(8,128)(2,1)S(1)}, u32[]{:S(2)}, u32[]{:S(2)}) collective-permute-start(bf16[576,254]{1,0:T(8,128)(2,1)S(1)} %collective-permute-done.1.rest_1_), channel_id=1, source_target_pairs={{2,6},{3,1},{6,10},{7,3},{10,14},{11,7},{14,12},{15,11},{12,8},{13... | collective-permute-start | bytes 877832 | tf_op jit(solution)/shard_map/ppermute | solution.py:314
  30.5 4.9 %copy-start.3 = (s32[128]{0:T(128)S(1)}, s32[128]{0:T(128)}, u32[]{:S(2)}) copy-start(s32[128]{0:T(128)} %constant.2.clone.table_ref) | copy-start | bytes 1540
  30.5 4.8 %collective-permute-start = (bf16[16,9792]{1,0:T(8,128)(2,1)S(1)}, bf16[16,9792]{1,0:T(8,128)(2,1)S(1)}, u32[]{:S(2)}, u32[]{:S(2)}) collective-permute-start(bf16[16,9792]{1,0:T(8,128)(2,1)S(1)} %reshape.6.here_ref), channel_id=1, source_target_pairs={{0,1},{1,0},{2,3},{3,2},{4,5},{5,4},{6,7},{7,6},{8,9},{9,8},{10,11... | collective-permute-start | bytes 940040 | tf_op jit(solution)/shard_map/ppermute | solution.py:317
  31.9 10.3 %collective-permute-start.5 = (bf16[576,254]{1,0:T(8,128)(2,1)S(1)}, bf16[576,254]{1,0:T(8,128)(2,1)S(1)}, u32[]{:S(2)}, u32[]{:S(2)}) collective-permute-start(bf16[576,254]{1,0:T(8,128)(2,1)S(1)} %collective-permute-done.4.rest_4_), channel_id=1, source_target_pairs={{2,0},{3,7},{6,2},{7,11},{10,6},{11,15},{14,10},{15,13},{12,14},{1... | collective-permute-start | bytes 877832 | tf_op jit(solution)/shard_map/ppermute | solution.py:314
  34.1 9.8 %collective-permute-start.6 = (bf16[576,254]{1,0:T(8,128)(2,1)S(1)}, bf16[576,254]{1,0:T(8,128)(2,1)S(1)}, u32[]{:S(2)}, u32[]{:S(2)}) collective-permute-start(bf16[576,254]{1,0:T(8,128)(2,1)S(1)} %collective-permute-done.3.rest_3_), channel_id=1, source_target_pairs={{2,6},{3,1},{6,10},{7,3},{10,14},{11,7},{14,12},{15,11},{12,8},{13... | collective-permute-start | bytes 877832 | tf_op jit(solution)/shard_map/ppermute | solution.py:314
  42.2 7.2 %collective-permute-start.8 = (bf16[320,254]{1,0:T(8,128)(2,1)S(1)}, bf16[320,254]{1,0:T(8,128)(2,1)S(1)}, u32[]{:S(2)}, u32[]{:S(2)}) collective-permute-start(bf16[320,254]{1,0:T(8,128)(2,1)S(1)} %slice.7), channel_id=1, source_target_pairs={{2,0},{3,7},{6,2},{7,11},{10,6},{11,15},{14,10},{15,13},{12,14},{1... | collective-permute-start | bytes 487688 | tf_op jit(solution)/shard_map/ppermute | solution.py:328
  43.9 5.5 %collective-permute-start.7 = (bf16[256,254]{1,0:T(8,128)(2,1)S(1)}, bf16[256,254]{1,0:T(8,128)(2,1)S(1)}, u32[]{:S(2)}, u32[]{:S(2)}) collective-permute-start(bf16[256,254]{1,0:T(8,128)(2,1)S(1)} %slice.8), channel_id=1, source_target_pairs={{2,6},{3,1},{6,10},{7,3},{10,14},{11,7},{14,12},{15,11},{12,8},{13... | collective-permute-start | bytes 390152 | tf_op jit(solution)/shard_map/ppermute | solution.py:326
  46.1 3.3 %copy-start = (bf16[8,512,128]{2,1,0:T(8,128)(2,1)S(1)}, bf16[8,512,128]{2,1,0:T(8,128)(2,1)}, u32[]{:S(2)}) copy-start(bf16[8,512,128]{2,1,0:T(8,128)(2,1)} %own_up.1) | copy-start | bytes 3145732
  51.8 1.3 %collective-permute-start.10 = (bf16[16,2176]{1,0:T(8,128)(2,1)S(1)}, bf16[16,2176]{1,0:T(8,128)(2,1)S(1)}, u32[]{:S(2)}, u32[]{:S(2)}) collective-permute-start(bf16[16,2176]{1,0:T(8,128)(2,1)S(1)} %get-tuple-element.36), channel_id=1, source_target_pairs={{0,1},{1,0},{2,3},{3,2},{4,5},{5,4},{6,7},{7,6},{8,9},{9,8},{10,11... | collective-permute-start | bytes 208904 | tf_op jit(solution)/shard_map/ppermute | solution.py:348

commit v16 on v15

--- a/solution.py
+++ b/solution.py
@@ -167,61 +167,65 @@
 
 
 def last_kernel(at, heads, length_ref, table_ref, q_ref, m_ref, l_ref, acc_ref,
-                top_ref, bottom_ref, own_up, far_up, keep_ref, give_ref, flat_ref):
+                top_ref, bottom_ref, keep_ref, give_ref):
     core = lax.axis_index("ctx") % CORES
     shards = [(with_base(table_ref, at, (top_ref,))[0][0], (top_ref, bottom_ref))]
-    everyone = flat_ref.shape[0]
-    per_core = heads // CORES
-    rows = per_core * everyone
-    pair = min(2, per_core)
-    tail = jnp.zeros((everyone, LANES), f32)
-    lane = lax.broadcasted_iota(jnp.int32, (everyone, LANES), 1)
-    for side, up_ref in enumerate((own_up, far_up)):
+    rows = keep_ref.shape[0]
+    lane = lax.broadcasted_iota(jnp.int32, (rows, LANES), 1)
+    for side in (1, 0):
         part = pl.ds(pl.multiple_of((core ^ side) * rows, rows), rows)
         m_new, l_new, summed = fold_block(
             part, q_ref, shards, length_ref[0], (m_ref, l_ref, acc_ref)
         )
-        context = (summed * (1.0 / l_new)).astype(bf16)
-        weight = m_new + jnp.log2(l_new)
-        for j in range(0, per_core, pair):
-            lifted = jnp.dot(
-                context[j * everyone:(j + pair) * everyone, :],
-                jnp.concatenate([up_ref[j + i] for i in range(pair)], axis=1),
-                preferred_element_type=f32,
+        context = summed * (1.0 / l_new)
+        weight = jnp.broadcast_to(m_new + jnp.log2(l_new), (rows, LANES))
+        if side:
+            high = weight.astype(bf16).astype(f32)
+            mid = (weight - high).astype(bf16).astype(f32)
+            terms = jnp.where(lane == 0, high, jnp.where(lane == 1, mid, weight - high - mid))
+            give_ref[:, :LATENT] = context.astype(bf16)
+            give_ref[:, LATENT:] = terms.astype(bf16)
+        else:
+            keep_ref[:, :LATENT] = context
+            keep_ref[:, LATENT:] = weight
+
+
+def merge_kernel(keep_ref, got_ref, up_ref, out_ref, flat_ref):
+    core = lax.axis_index("ctx") % CORES
+    heads = up_ref.shape[0]
+    everyone = flat_ref.shape[0]
+    half = everyone // CORES
+    pair = min(2, heads)
+    for j in range(0, heads, pair):
+        contexts = []
+        for head in range(j, j + pair):
+            row = head * everyone
+            got = jnp.concatenate(
+                [got_ref[row + half:row + everyone, :], got_ref[row:row + half, :]], axis=0
+            ).astype(f32)
+            keep = keep_ref[row:row + everyone, :]
+            gap = keep[:, LATENT:LATENT + 1] - got[:, LATENT:LATENT + 1]
+            gap = gap - got[:, LATENT + 1:LATENT + 2] - got[:, LATENT + 2:LATENT + 3]
+            share = 1.0 / (1.0 + jnp.exp2(-gap))
+            rest = 1.0 / (1.0 + jnp.exp2(gap))
+            contexts.append(
+                (keep[:, :LATENT] * share + got[:, :LATENT] * rest).astype(bf16)
             )
-            for i in range(pair):
-                head = (core ^ side) * per_core + j + i
-                here = slice((j + i) * everyone, (j + i + 1) * everyone)
-                tail = jnp.where(lane == head, weight[here], tail)
-                lanes = pl.ds(pl.multiple_of(head * V_HEAD, V_HEAD), V_HEAD)
-                flat_ref[:, lanes] = lifted[
-                    i * everyone:(i + 1) * everyone, i * V_HEAD:(i + 1) * V_HEAD
-                ]
-    high = tail.astype(bf16).astype(f32)
-    mid = (tail - high).astype(bf16).astype(f32)
-    low = tail - high - mid
-    flat_ref[:, heads * V_HEAD:] = (
-        high + pltpu.roll(mid, heads, 1) + pltpu.roll(low, 2 * heads, 1)
-    )
-    keep_ref[...] = flat_ref[:everyone // CORES, :]
-    give_ref[...] = flat_ref[everyone // CORES:, :].astype(bf16)
-
-
-def merge_kernel(heads, keep_ref, got_ref, out_ref, flat_ref):
-    width = heads * V_HEAD
-    gap = keep_ref[:, width:] - got_ref[:, width:].astype(f32)
-    delta = gap[:, :heads] + (gap[:, heads:2 * heads] + gap[:, 2 * heads:3 * heads])
-    share = 1.0 / (1.0 + jnp.exp2(-delta))
-    rest = 1.0 / (1.0 + jnp.exp2(delta))
-    for j in range(heads):
-        lanes = slice(j * V_HEAD, (j + 1) * V_HEAD)
-        flat_ref[:, lanes] = (
-            keep_ref[:, lanes] * share[:, j:j + 1]
-            + got_ref[:, lanes].astype(f32) * rest[:, j:j + 1]
-        )
-    chips, tokens, _ = out_ref.shape
-    for chip in range(chips):
-        out_ref[chip] = flat_ref[chip * tokens:(chip + 1) * tokens, :].astype(bf16)
+        lifted = jnp.dot(
+            jnp.concatenate(contexts, axis=0),
+            jnp.concatenate([up_ref[j + i] for i in range(pair)], axis=1),
+            preferred_element_type=f32,
+        )
+        for i in range(pair):
+            flat_ref[:, (j + i) * V_HEAD:(j + i + 1) * V_HEAD] = lifted[
+                i * everyone:(i + 1) * everyone, i * V_HEAD:(i + 1) * V_HEAD
+            ]
+    devices, tokens, _ = out_ref.shape
+    chips = devices // CORES
+    for i in range(devices):
+        out_ref[(i % chips) * CORES + (core ^ (i // chips))] = (
+            flat_ref[i * tokens:(i + 1) * tokens, :].astype(bf16)
+        )
 
 
 VMEM = pl.BlockSpec(memory_space=pltpu.VMEM)
@@ -307,8 +311,7 @@
         pieces, "ctx", split_axis=0, concat_axis=0, axis_index_groups=same_core, tiled=True
     )
 
-    right, left, up = lax.optimization_barrier((right, left, value_up))
-    far_up = lax.ppermute(up, "ctx", other_core)
+    right, left = lax.optimization_barrier((right, left))
     keys, state, at = [own, right, left], None, 0
     for s in range(2, steps):
         right, left = onward(right), backward(left)
@@ -334,30 +337,27 @@
         compiler_params=PARAMS,
         name="middle",
     )(prefix_length, span_offset, table, q, *state, here, *keys)
-    flat = heads * V_HEAD + LANES
-    half = everyone // CORES
+    per_core = heads // CORES
+    part = per_core * everyone
     keep, give = pl.pallas_call(
         functools.partial(last_kernel, chips - 1, heads),
-        out_shape=[shape(half, flat), shape(half, flat, dtype=bf16)],
-        in_specs=[SMEM] * 2 + [VMEM] * 8,
+        out_shape=[shape(part, LATENT + LANES), shape(part, LATENT + LANES, dtype=bf16)],
+        in_specs=[SMEM] * 2 + [VMEM] * 6,
         out_specs=[VMEM] * 2,
-        scratch_shapes=[pltpu.VMEM((everyone, flat), f32)],
         compiler_params=PARAMS,
         name="last",
-    )(prefix_length, table, q, *state, top, bottom, value_up, far_up)
+    )(prefix_length, table, q, *state, top, bottom)
     got = lax.ppermute(give, "ctx", other_core)
     merged = pl.pallas_call(
-        functools.partial(merge_kernel, heads),
-        out_shape=shape(chips, tokens, heads * V_HEAD, dtype=bf16),
-        in_specs=[VMEM] * 2,
+        merge_kernel,
+        out_shape=shape(ctx, tokens, per_core * V_HEAD, dtype=bf16),
+        in_specs=[VMEM] * 3,
         out_specs=VMEM,
-        scratch_shapes=[pltpu.VMEM((half, heads * V_HEAD), f32)],
+        scratch_shapes=[pltpu.VMEM((everyone, per_core * V_HEAD), f32)],
         compiler_params=PARAMS,
         name="merge",
-    )(keep, got)
-    returned = lax.all_to_all(
-        merged, "ctx", split_axis=0, concat_axis=0, axis_index_groups=same_core, tiled=True
-    )
+    )(keep, got, value_up)
+    returned = lax.all_to_all(merged, "ctx", split_axis=0, concat_axis=0, tiled=True)
     return returned.transpose(1, 0, 2).reshape(tokens, all_heads * V_HEAD)
 
 

time: 66.1 us -> 57.2 us (0.87)
  waiting for transfers between devices: 23.5 us -> 15.7 us
  starting transfers between devices: 17.2 us -> 16.5 us
    ppermute x2, waiting for transfers between devices: 7.52 us -> 0.01 us  [on_device(): right, left = (onward(own), backward(own))]
    all_to_all x1, starting transfers between devices: 5.54 us -> 6.25 us  [on_device(): lax.all_to_all(pieces, 'ctx', split_axis=0, concat_axis=0, axis_index_gro...]
    ppermute x1, starting transfers between devices: 1.53 us -> 0.82 us  [on_device(): top = onward(right[:cut])]
  transfers between devices with their start and end apart: 12 -> 11, of which waited for: 6 -> 5; matrix products, arithmetic and copies ran while one was open for 0% -> 0% of each run, Pallas kernels for 10% -> 12%
where the time goes in v16:
time: 57.2 us; the launch traced here: 56.9 us
  starting transfers between devices  16.5 us (29%)
  waiting for transfers between devices  15.7 us (27%)
  blocking collectives  11.5 us (20%)
  Pallas kernels  9.31 us (16%)
  local copies, waits for them, and re-layouts  2.54 us (4%)
  between operations  1.42 us (2%)
    all_to_all x1, blocking collectives, on_device(): lax.all_to_all(merged, 'ctx', split_axis=0, concat_axis=0, tiled=True)  11.5 us
    all_to_all x1, waiting for transfers between devices, on_device(): lax.all_to_all(pieces, 'ctx', split_axis=0, concat_axis=0, axis_index_gro...  8.91 us
    all_to_all x1, starting transfers between devices, on_device(): lax.all_to_all(pieces, 'ctx', split_axis=0, concat_axis=0, axis_index_gro...  6.25 us
    ppermute x4, starting transfers between devices, on_device(): right, left = (onward(right), backward(left))  4.45 us
    ppermute x4, waiting for transfers between devices, on_device(): right, left = (onward(right), backward(left))  4.12 us
    pallas_call x1, Pallas kernels, fold_first(): pl.pallas_call(functools.partial(first_kernel, heads, len(keys)), out_sha...  3.59 us
    ppermute x2, starting transfers between devices, on_device(): right, left = (onward(own), backward(own))  3.03 us
    pallas_call x1, Pallas kernels, on_device(): pl.pallas_call(functools.partial(span_kernel, at, len(keys)), out_shape=s...  2.52 us
  transfers between devices with their start and end apart: 11, of which 5 were waited for; matrix products, arithmetic and copies ran while one was open for 0% of the time, Pallas kernels for 12%

profile of v16, /device:TPU:0, one launch (start us, length us, event | category | flops | bytes accessed | tf_op | source)
XLA Modules:
  0.0 56.9 jit_solution(5201927951915460868)
XLA Ops:
  0.0 2.9 %collective-permute-start.1 = (bf16[576,254]{1,0:T(8,128)(2,1)}, bf16[576,254]{1,0:T(8,128)(2,1)S(1)}, u32[]{:S(2)}, u32[]{:S(2)}) collective-permute-start(bf16[576,254]{1,0:T(8,128)(2,1)} %bitcast.4), channel_id=1, source_target_pairs={{2,6},{3,1},{6,10},{7,3},{10,14},{11,7},{14,12},{15,11},{12,8},{13... | collective-permute-start | bytes 877832 | tf_op jit(solution)/shard_map/ppermute | solution.py:300
  2.9 0.1 collective-permute-start.2
  3.0 0.0 copy-start.1
  3.0 1.0 %copy-done.1 = bf16[2,73728]{1,0:T(2,128)(2,1)S(1)} copy-done((bf16[2,73728]{1,0:T(2,128)(2,1)S(1)}, bf16[2,73728]{1,0:T(2,128)(2,1)}, u32[]{:S(2)}) %copy-start.1) | copy-done | bytes 294936
  4.0 0.0 copy-start.4
  4.0 0.7 %copy-done.4 = bf16[2,576]{1,0:T(2,128)(2,1)S(1)} copy-done((bf16[2,576]{1,0:T(2,128)(2,1)S(1)}, bf16[2,576]{1,0:T(2,128)(2,1)}, u32[]{:S(2)}) %copy-start.4) | copy-done | bytes 2328
  4.7 0.7 %pieces.1 = bf16[8,2,9792]{2,1,0:T(2,128)(2,1)} custom-call(bf16[2,73728]{1,0:T(2,128)(2,1)S(1)} %copy-done.1, bf16[2,576]{1,0:T(2,128)(2,1)S(1)} %copy-done.4), custom_call_target="tpu_custom_call" | custom-call | tf_op jit(solution)/shard_map/pieces/pallas_call | solution.py:302
  5.4 6.3 %all-to-all-start = ((bf16[8,2,9792]{2,1,0:T(2,128)(2,1)}), bf16[8,2,9792]{2,1,0:T(2,128)(2,1)S(1)}, u32[]{:S(2)}, u32[]{:S(2)}) async-start(bf16[8,2,9792]{2,1,0:T(2,128)(2,1)} %pieces.1), calls=%async_computation | async-start | bytes 630784 | tf_op jit(solution)/shard_map/all_to_all | solution.py:310
  11.7 0.0 copy-start.2
  11.7 0.0 collective-permute-done.1.rest_1_
  11.7 0.0 collective-permute-done.2.rest_2_
  11.7 2.1 %collective-permute-start.4 = (bf16[576,254]{1,0:T(8,128)(2,1)S(1)}, bf16[576,254]{1,0:T(8,128)(2,1)S(1)}, u32[]{:S(2)}, u32[]{:S(2)}) collective-permute-start(bf16[576,254]{1,0:T(8,128)(2,1)S(1)} %collective-permute-done.2.rest_2_), channel_id=1, source_target_pairs={{2,0},{3,7},{6,2},{7,11},{10,6},{11,15},{14,10},{15,13},{12,14},{1... | collective-permute-start | bytes 877832 | tf_op jit(solution)/shard_map/ppermute | solution.py:317
  13.8 0.1 collective-permute-start.3
  13.8 8.9 %all-to-all-done = bf16[8,2,9792]{2,1,0:T(2,128)(2,1)S(1)} async-done(((bf16[8,2,9792]{2,1,0:T(2,128)(2,1)}), bf16[8,2,9792]{2,1,0:T(2,128)(2,1)S(1)}, u32[]{:S(2)}, u32[]{:S(2)}) %all-to-all-start) | async-done | bytes 313376 | tf_op jit(solution)/shard_map/all_to_all | solution.py:310
  22.7 0.2 reshape.6.here_ref
  23.0 0.0 copy-start.3
  23.0 0.1 collective-permute-start
  23.1 1.0 %collective-permute-done.4.rest_4_ = bf16[576,254]{1,0:T(8,128)(2,1)S(1)} collective-permute-done((bf16[576,254]{1,0:T(8,128)(2,1)S(1)}, bf16[576,254]{1,0:T(8,128)(2,1)S(1)}, u32[]{:S(2)}, u32[]{:S(2)}) %collective-permute-start.4) | collective-permute-done | bytes 292640 | tf_op jit(solution)/shard_map/ppermute | solution.py:317
  24.1 1.7 %collective-permute-start.5 = (bf16[576,254]{1,0:T(8,128)(2,1)S(1)}, bf16[576,254]{1,0:T(8,128)(2,1)S(1)}, u32[]{:S(2)}, u32[]{:S(2)}) collective-permute-start(bf16[576,254]{1,0:T(8,128)(2,1)S(1)} %collective-permute-done.4.rest_4_), channel_id=1, source_target_pairs={{2,0},{3,7},{6,2},{7,11},{10,6},{11,15},{14,10},{15,13},{12,14},{1... | collective-permute-start | bytes 877832 | tf_op jit(solution)/shard_map/ppermute | solution.py:317
  25.8 0.0 collective-permute-done.3.rest_3_
  25.8 0.6 %collective-permute-start.6 = (bf16[576,254]{1,0:T(8,128)(2,1)S(1)}, bf16[576,254]{1,0:T(8,128)(2,1)S(1)}, u32[]{:S(2)}, u32[]{:S(2)}) collective-permute-start(bf16[576,254]{1,0:T(8,128)(2,1)S(1)} %collective-permute-done.3.rest_3_), channel_id=1, source_target_pairs={{2,6},{3,1},{6,10},{7,3},{10,14},{11,7},{14,12},{15,11},{12,8},{13... | collective-permute-start | bytes 877832 | tf_op jit(solution)/shard_map/ppermute | solution.py:317
  27.0 0.0 collective-permute-done.there_ref
  27.0 0.0 copy-done.2
  27.0 0.0 copy-done.3
  27.1 3.6 %first.1 = (bf16[512,576]{1,0:T(8,128)(2,1)S(1)}, f32[512,128]{1,0:T(8,128)S(1)}, f32[512,128]{1,0:T(8,128)S(1)}, f32[512,512]{1,0:T(8,128)S(1)}) custom-call(s32[1]{0:T(128)S(6)} %copy.9.length_ref, s32[128]{0:T(128)S(1)} %copy-done.3, bf16[16,9792]{1,0:T(8,128)(2,1)S(1)} %reshape.6.here_ref, bf16[16,9792]{1,0:T(8,128)(2,1)S(1)} %collective-permute-done.there_ref, ...), custom_call_target="tpu_custom_call" | custom-call | tf_op jit(solution)/shard_map/first/pallas_call | solution.py:277
  30.7 3.1 %collective-permute-done.5.rest_1_ = bf16[576,254]{1,0:T(8,128)(2,1)S(1)} collective-permute-done((bf16[576,254]{1,0:T(8,128)(2,1)S(1)}, bf16[576,254]{1,0:T(8,128)(2,1)S(1)}, u32[]{:S(2)}, u32[]{:S(2)}) %collective-permute-start.5) | collective-permute-done | bytes 292640 | tf_op jit(solution)/shard_map/ppermute | solution.py:317
  33.8 1.8 %collective-permute-start.8 = (bf16[320,254]{1,0:T(8,128)(2,1)S(1)}, bf16[320,254]{1,0:T(8,128)(2,1)S(1)}, u32[]{:S(2)}, u32[]{:S(2)}) collective-permute-start(bf16[320,254]{1,0:T(8,128)(2,1)S(1)} %slice.7), channel_id=1, source_target_pairs={{2,0},{3,7},{6,2},{7,11},{10,6},{11,15},{14,10},{15,13},{12,14},{1... | collective-permute-start | bytes 487688 | tf_op jit(solution)/shard_map/ppermute | solution.py:331
  35.6 0.0 collective-permute-done.6.rest_0_
  35.6 0.8 %collective-permute-start.7 = (bf16[256,254]{1,0:T(8,128)(2,1)S(1)}, bf16[256,254]{1,0:T(8,128)(2,1)S(1)}, u32[]{:S(2)}, u32[]{:S(2)}) collective-permute-start(bf16[256,254]{1,0:T(8,128)(2,1)S(1)} %slice.8), channel_id=1, source_target_pairs={{2,6},{3,1},{6,10},{7,3},{10,14},{11,7},{14,12},{15,11},{12,8},{13... | collective-permute-start | bytes 390152 | tf_op jit(solution)/shard_map/ppermute | solution.py:329
  37.1 2.5 %middle.1 = (f32[512,128]{1,0:T(8,128)S(1)}, f32[512,128]{1,0:T(8,128)S(1)}, f32[512,512]{1,0:T(8,128)S(1)}) custom-call(s32[1]{0:T(128)S(6)} %copy.9.length_ref, s32[1]{0:T(128)S(6)} %copy.10.offset_ref, s32[128]{0:T(128)S(1)} %copy-done.3, bf16[512,576]{1,0:T(8,128)(2,1)S(1)} %get-tuple-element.22.q_ref, f32[512,128]{1,0:T(8,128)S(1)} %get-tuple-element.26.m_in, ...), custom_call_target="tpu_custom_call" | custom-call | tf_op jit(solution)/shard_map/middle/pallas_call | solution.py:332
  39.6 1.0 %collective-permute-done.7.top_ref = bf16[256,254]{1,0:T(8,128)(2,1)S(1)} collective-permute-done((bf16[256,254]{1,0:T(8,128)(2,1)S(1)}, bf16[256,254]{1,0:T(8,128)(2,1)S(1)}, u32[]{:S(2)}, u32[]{:S(2)}) %collective-permute-start.7) | collective-permute-done | bytes 130080 | tf_op jit(solution)/shard_map/ppermute | solution.py:329
  40.6 0.0 collective-permute-done.8.bottom_ref
  40.6 0.0 copy-start
  40.6 2.0 %last.1 = (f32[256,640]{1,0:T(8,128)S(1)}, bf16[256,640]{1,0:T(8,128)(2,1)S(1)}) custom-call(s32[1]{0:T(128)S(6)} %copy.9.length_ref, s32[128]{0:T(128)S(1)} %copy-done.3, bf16[512,576]{1,0:T(8,128)(2,1)S(1)} %get-tuple-element.22.q_ref, f32[512,128]{1,0:T(8,128)S(1)} %get-tuple-element.29.m_ref, f32[512,128]{1,0:T(8,128)S(1)} %get-tuple-element.30.l_ref, ...), custom_call_target="tpu_custom_call" | custom-call | tf_op jit(solution)/shard_map/last/pallas_call | solution.py:342
  42.6 0.1 collective-permute-start.9
  42.7 1.6 %collective-permute-done.9.got_ref = bf16[256,640]{1,0:T(8,128)(2,1)S(1)} collective-permute-done((bf16[256,640]{1,0:T(8,128)(2,1)S(1)}, bf16[256,640]{1,0:T(8,128)(2,1)S(1)}, u32[]{:S(2)}, u32[]{:S(2)}) %collective-permute-start.9) | collective-permute-done | bytes 327712 | tf_op jit(solution)/shard_map/ppermute | solution.py:350
  44.3 0.0 copy-done
  44.3 0.5 merge.1
  44.8 11.5 %all_to_all.10 = bf16[16,2,1024]{2,1,0:T(2,128)(2,1)S(1)} all-to-all(bf16[16,2,1024]{2,1,0:T(2,128)(2,1)S(1)} %merge.1), channel_id=1, replica_groups=mesh['groups'=2,'ctx'=16] {'ctx'}, dimensions={0} | all-to-all | bytes 131072 | tf_op jit(solution)/shard_map/all_to_all | solution.py:360
  56.3 0.6 %copy.11 = bf16[2,16384]{1,0:T(2,128)(2,1)} copy(bf16[2,16384]{1,0:T(2,128)(2,1)S(1)} %bitcast.7) | data formatting | bytes 131072
  (2 shorter events, 0.0 us)
Async XLA Ops:
  0.0 11.7 %collective-permute-start.1 = (bf16[576,254]{1,0:T(8,128)(2,1)}, bf16[576,254]{1,0:T(8,128)(2,1)S(1)}, u32[]{:S(2)}, u32[]{:S(2)}) collective-permute-start(bf16[576,254]{1,0:T(8,128)(2,1)} %bitcast.4), channel_id=1, source_target_pairs={{2,6},{3,1},{6,10},{7,3},{10,14},{11,7},{14,12},{15,11},{12,8},{13... | collective-permute-start | bytes 877832 | tf_op jit(solution)/shard_map/ppermute | solution.py:300
  2.9 8.7 %collective-permute-start.2 = (bf16[576,254]{1,0:T(8,128)(2,1)}, bf16[576,254]{1,0:T(8,128)(2,1)S(1)}, u32[]{:S(2)}, u32[]{:S(2)}) collective-permute-start(bf16[576,254]{1,0:T(8,128)(2,1)} %bitcast.5), channel_id=1, source_target_pairs={{2,0},{3,7},{6,2},{7,11},{10,6},{11,15},{14,10},{15,13},{12,14},{1... | collective-permute-start | bytes 877832 | tf_op jit(solution)/shard_map/ppermute | solution.py:300
  3.0 1.0 %copy-start.1 = (bf16[2,73728]{1,0:T(2,128)(2,1)S(1)}, bf16[2,73728]{1,0:T(2,128)(2,1)}, u32[]{:S(2)}) copy-start(bf16[2,73728]{1,0:T(2,128)(2,1)} %queries_ref.1) | copy-start | bytes 884740
  4.0 0.7 %copy-start.4 = (bf16[2,576]{1,0:T(2,128)(2,1)S(1)}, bf16[2,576]{1,0:T(2,128)(2,1)}, u32[]{:S(2)}) copy-start(bf16[2,576]{1,0:T(2,128)(2,1)} %span_ref.1) | copy-start | bytes 6916
  5.4 17.3 %all-to-all-start = ((bf16[8,2,9792]{2,1,0:T(2,128)(2,1)}), bf16[8,2,9792]{2,1,0:T(2,128)(2,1)S(1)}, u32[]{:S(2)}, u32[]{:S(2)}) async-start(bf16[8,2,9792]{2,1,0:T(2,128)(2,1)} %pieces.1), calls=%async_computation | async-start | bytes 630784 | tf_op jit(solution)/shard_map/all_to_all | solution.py:310
  11.7 15.4 %copy-start.2 = (bf16[254,576]{0,1:T(8,128)(2,1)S(1)}, bf16[254,576]{0,1:T(8,128)(2,1)}, u32[]{:S(2)}) copy-start(bf16[254,576]{0,1:T(8,128)(2,1)} %param.8) | copy-start | bytes 877828
  11.7 12.4 %collective-permute-start.4 = (bf16[576,254]{1,0:T(8,128)(2,1)S(1)}, bf16[576,254]{1,0:T(8,128)(2,1)S(1)}, u32[]{:S(2)}, u32[]{:S(2)}) collective-permute-start(bf16[576,254]{1,0:T(8,128)(2,1)S(1)} %collective-permute-done.2.rest_2_), channel_id=1, source_target_pairs={{2,0},{3,7},{6,2},{7,11},{10,6},{11,15},{14,10},{15,13},{12,14},{1... | collective-permute-start | bytes 877832 | tf_op jit(solution)/shard_map/ppermute | solution.py:317
  13.8 12.0 %collective-permute-start.3 = (bf16[576,254]{1,0:T(8,128)(2,1)S(1)}, bf16[576,254]{1,0:T(8,128)(2,1)S(1)}, u32[]{:S(2)}, u32[]{:S(2)}) collective-permute-start(bf16[576,254]{1,0:T(8,128)(2,1)S(1)} %collective-permute-done.1.rest_1_), channel_id=1, source_target_pairs={{2,6},{3,1},{6,10},{7,3},{10,14},{11,7},{14,12},{15,11},{12,8},{13... | collective-permute-start | bytes 877832 | tf_op jit(solution)/shard_map/ppermute | solution.py:317
  23.0 4.1 %copy-start.3 = (s32[128]{0:T(128)S(1)}, s32[128]{0:T(128)}, u32[]{:S(2)}) copy-start(s32[128]{0:T(128)} %constant.2.clone.table_ref) | copy-start | bytes 1540
  23.0 4.1 %collective-permute-start = (bf16[16,9792]{1,0:T(8,128)(2,1)S(1)}, bf16[16,9792]{1,0:T(8,128)(2,1)S(1)}, u32[]{:S(2)}, u32[]{:S(2)}) collective-permute-start(bf16[16,9792]{1,0:T(8,128)(2,1)S(1)} %reshape.6.here_ref), channel_id=1, source_target_pairs={{0,1},{1,0},{2,3},{3,2},{4,5},{5,4},{6,7},{7,6},{8,9},{9,8},{10,11... | collective-permute-start | bytes 940040 | tf_op jit(solution)/shard_map/ppermute | solution.py:320
  24.1 9.7 %collective-permute-start.5 = (bf16[576,254]{1,0:T(8,128)(2,1)S(1)}, bf16[576,254]{1,0:T(8,128)(2,1)S(1)}, u32[]{:S(2)}, u32[]{:S(2)}) collective-permute-start(bf16[576,254]{1,0:T(8,128)(2,1)S(1)} %collective-permute-done.4.rest_4_), channel_id=1, source_target_pairs={{2,0},{3,7},{6,2},{7,11},{10,6},{11,15},{14,10},{15,13},{12,14},{1... | collective-permute-start | bytes 877832 | tf_op jit(solution)/shard_map/ppermute | solution.py:317
  25.8 9.8 %collective-permute-start.6 = (bf16[576,254]{1,0:T(8,128)(2,1)S(1)}, bf16[576,254]{1,0:T(8,128)(2,1)S(1)}, u32[]{:S(2)}, u32[]{:S(2)}) collective-permute-start(bf16[576,254]{1,0:T(8,128)(2,1)S(1)} %collective-permute-done.3.rest_3_), channel_id=1, source_target_pairs={{2,6},{3,1},{6,10},{7,3},{10,14},{11,7},{14,12},{15,11},{12,8},{13... | collective-permute-start | bytes 877832 | tf_op jit(solution)/shard_map/ppermute | solution.py:317
  33.8 6.8 %collective-permute-start.8 = (bf16[320,254]{1,0:T(8,128)(2,1)S(1)}, bf16[320,254]{1,0:T(8,128)(2,1)S(1)}, u32[]{:S(2)}, u32[]{:S(2)}) collective-permute-start(bf16[320,254]{1,0:T(8,128)(2,1)S(1)} %slice.7), channel_id=1, source_target_pairs={{2,0},{3,7},{6,2},{7,11},{10,6},{11,15},{14,10},{15,13},{12,14},{1... | collective-permute-start | bytes 487688 | tf_op jit(solution)/shard_map/ppermute | solution.py:331
  35.6 5.0 %collective-permute-start.7 = (bf16[256,254]{1,0:T(8,128)(2,1)S(1)}, bf16[256,254]{1,0:T(8,128)(2,1)S(1)}, u32[]{:S(2)}, u32[]{:S(2)}) collective-permute-start(bf16[256,254]{1,0:T(8,128)(2,1)S(1)} %slice.8), channel_id=1, source_target_pairs={{2,6},{3,1},{6,10},{7,3},{10,14},{11,7},{14,12},{15,11},{12,8},{13... | collective-permute-start | bytes 390152 | tf_op jit(solution)/shard_map/ppermute | solution.py:329
  40.6 3.7 %copy-start = (bf16[8,512,128]{2,1,0:T(8,128)(2,1)S(1)}, bf16[8,512,128]{2,1,0:T(8,128)(2,1)}, u32[]{:S(2)}) copy-start(bf16[8,512,128]{2,1,0:T(8,128)(2,1)} %up_ref.1) | copy-start | bytes 3145732
  42.6 1.7 %collective-permute-start.9 = (bf16[256,640]{1,0:T(8,128)(2,1)S(1)}, bf16[256,640]{1,0:T(8,128)(2,1)S(1)}, u32[]{:S(2)}, u32[]{:S(2)}) collective-permute-start(bf16[256,640]{1,0:T(8,128)(2,1)S(1)} %get-tuple-element.34), channel_id=1, source_target_pairs={{0,1},{1,0},{2,3},{3,2},{4,5},{5,4},{6,7},{7,6},{8,9},{9,8},{10,11... | collective-permute-start | bytes 983048 | tf_op jit(solution)/shard_map/ppermute | solution.py:350

commit v17 on v16

--- a/solution.py
+++ b/solution.py
@@ -166,28 +166,23 @@
     )
 
 
-def last_kernel(at, heads, length_ref, table_ref, q_ref, m_ref, l_ref, acc_ref,
-                top_ref, bottom_ref, keep_ref, give_ref):
+def last_kernel(at, side, length_ref, table_ref, q_ref, m_ref, l_ref, acc_ref,
+                top_ref, bottom_ref, out_ref):
     core = lax.axis_index("ctx") % CORES
     shards = [(with_base(table_ref, at, (top_ref,))[0][0], (top_ref, bottom_ref))]
-    rows = keep_ref.shape[0]
-    lane = lax.broadcasted_iota(jnp.int32, (rows, LANES), 1)
-    for side in (1, 0):
-        part = pl.ds(pl.multiple_of((core ^ side) * rows, rows), rows)
-        m_new, l_new, summed = fold_block(
-            part, q_ref, shards, length_ref[0], (m_ref, l_ref, acc_ref)
-        )
-        context = summed * (1.0 / l_new)
-        weight = jnp.broadcast_to(m_new + jnp.log2(l_new), (rows, LANES))
-        if side:
-            high = weight.astype(bf16).astype(f32)
-            mid = (weight - high).astype(bf16).astype(f32)
-            terms = jnp.where(lane == 0, high, jnp.where(lane == 1, mid, weight - high - mid))
-            give_ref[:, :LATENT] = context.astype(bf16)
-            give_ref[:, LATENT:] = terms.astype(bf16)
-        else:
-            keep_ref[:, :LATENT] = context
-            keep_ref[:, LATENT:] = weight
+    rows = out_ref.shape[0]
+    part = pl.ds(pl.multiple_of((core ^ side) * rows, rows), rows)
+    m_new, l_new, summed = fold_block(
+        part, q_ref, shards, length_ref[0], (m_ref, l_ref, acc_ref)
+    )
+    out_ref[:, :LATENT] = (summed * (1.0 / l_new)).astype(out_ref.dtype)
+    weight = jnp.broadcast_to(m_new + jnp.log2(l_new), (rows, LANES))
+    if side:
+        lane = lax.broadcasted_iota(jnp.int32, (rows, LANES), 1)
+        high = weight.astype(bf16).astype(f32)
+        mid = (weight - high).astype(bf16).astype(f32)
+        weight = jnp.where(lane == 0, high, jnp.where(lane == 1, mid, weight - high - mid))
+    out_ref[:, LATENT:] = weight.astype(out_ref.dtype)
 
 
 def merge_kernel(keep_ref, got_ref, up_ref, out_ref, flat_ref):
@@ -339,15 +334,19 @@
     )(prefix_length, span_offset, table, q, *state, here, *keys)
     per_core = heads // CORES
     part = per_core * everyone
-    keep, give = pl.pallas_call(
-        functools.partial(last_kernel, chips - 1, heads),
-        out_shape=[shape(part, LATENT + LANES), shape(part, LATENT + LANES, dtype=bf16)],
-        in_specs=[SMEM] * 2 + [VMEM] * 6,
-        out_specs=[VMEM] * 2,
-        compiler_params=PARAMS,
-        name="last",
-    )(prefix_length, table, q, *state, top, bottom)
-    got = lax.ppermute(give, "ctx", other_core)
+
+    def fold_last(side, dtype):
+        return pl.pallas_call(
+            functools.partial(last_kernel, chips - 1, side),
+            out_shape=shape(part, LATENT + LANES, dtype=dtype),
+            in_specs=[SMEM] * 2 + [VMEM] * 6,
+            out_specs=VMEM,
+            compiler_params=PARAMS,
+            name="keep" if side == 0 else "give",
+        )(prefix_length, table, q, *state, top, bottom)
+
+    got = lax.ppermute(fold_last(1, bf16), "ctx", other_core)
+    keep = fold_last(0, f32)
     merged = pl.pallas_call(
         merge_kernel,
         out_shape=shape(ctx, tokens, per_core * V_HEAD, dtype=bf16),

time: 57.2 us -> 56.5 us (0.988)
  waiting for transfers between devices: 15.7 us -> 14.5 us
    ppermute x1, waiting for transfers between devices: 1.62 us -> 0.43 us  [on_device(): got = lax.ppermute(fold_last(1, bf16), 'ctx', other_core)]
    pallas_call x1 -> x2, Pallas kernels: 1.98 us -> 2.37 us  [fold_last(): pl.pallas_call(functools.partial(last_kernel, chips - 1, side), out_shape...]
  transfers between devices with their start and end apart: 11 -> 11, of which waited for: 5 -> 5; matrix products, arithmetic and copies ran while one was open for 0% -> 0% of each run, Pallas kernels for 12% -> 14%
where the time goes in v17:
time: 56.5 us; the launch traced here: 56.1 us
  starting transfers between devices  16.5 us (29%)
  waiting for transfers between devices  14.5 us (26%)
  blocking collectives  11.5 us (20%)
  Pallas kernels  9.7 us (17%)
  local copies, waits for them, and re-layouts  2.54 us (4%)
  between operations  1.44 us (3%)
    all_to_all x1, blocking collectives, on_device(): lax.all_to_all(merged, 'ctx', split_axis=0, concat_axis=0, tiled=True)  11.5 us
    all_to_all x1, waiting for transfers between devices, on_device(): lax.all_to_all(pieces, 'ctx', split_axis=0, concat_axis=0, axis_index_gro...  8.91 us
    all_to_all x1, starting transfers between devices, on_device(): lax.all_to_all(pieces, 'ctx', split_axis=0, concat_axis=0, axis_index_gro...  6.25 us
    ppermute x4, starting transfers between devices, on_device(): right, left = (onward(right), backward(left))  4.45 us
    ppermute x4, waiting for transfers between devices, on_device(): right, left = (onward(right), backward(left))  4.11 us
    pallas_call x1, Pallas kernels, fold_first(): pl.pallas_call(functools.partial(first_kernel, heads, len(keys)), out_sha...  3.6 us
    ppermute x2, starting transfers between devices, on_device(): right, left = (onward(own), backward(own))  3.03 us
    pallas_call x1, Pallas kernels, on_device(): pl.pallas_call(functools.partial(span_kernel, at, len(keys)), out_shape=s...  2.48 us
  transfers between devices with their start and end apart: 11, of which 5 were waited for; matrix products, arithmetic and copies ran while one was open for 0% of the time, Pallas kernels for 14%

profile of v17, /device:TPU:0, one launch (start us, length us, event | category | flops | bytes accessed | tf_op | source)
XLA Modules:
  0.0 56.1 jit_solution(9785185287065798443)
XLA Ops:
  0.0 2.9 %collective-permute-start.1 = (bf16[576,254]{1,0:T(8,128)(2,1)}, bf16[576,254]{1,0:T(8,128)(2,1)S(1)}, u32[]{:S(2)}, u32[]{:S(2)}) collective-permute-start(bf16[576,254]{1,0:T(8,128)(2,1)} %bitcast.4), channel_id=1, source_target_pairs={{2,6},{3,1},{6,10},{7,3},{10,14},{11,7},{14,12},{15,11},{12,8},{13... | collective-permute-start | bytes 877832 | tf_op jit(solution)/shard_map/ppermute | solution.py:295
  2.9 0.1 collective-permute-start.2
  3.0 0.0 copy-start.1
  3.0 1.0 %copy-done.1 = bf16[2,73728]{1,0:T(2,128)(2,1)S(1)} copy-done((bf16[2,73728]{1,0:T(2,128)(2,1)S(1)}, bf16[2,73728]{1,0:T(2,128)(2,1)}, u32[]{:S(2)}) %copy-start.1) | copy-done | bytes 294936
  4.0 0.0 copy-start.4
  4.0 0.7 %copy-done.4 = bf16[2,576]{1,0:T(2,128)(2,1)S(1)} copy-done((bf16[2,576]{1,0:T(2,128)(2,1)S(1)}, bf16[2,576]{1,0:T(2,128)(2,1)}, u32[]{:S(2)}) %copy-start.4) | copy-done | bytes 2328
  4.7 0.7 %pieces.1 = bf16[8,2,9792]{2,1,0:T(2,128)(2,1)} custom-call(bf16[2,73728]{1,0:T(2,128)(2,1)S(1)} %copy-done.1, bf16[2,576]{1,0:T(2,128)(2,1)S(1)} %copy-done.4), custom_call_target="tpu_custom_call" | custom-call | tf_op jit(solution)/shard_map/pieces/pallas_call | solution.py:297
  5.4 6.3 %all-to-all-start = ((bf16[8,2,9792]{2,1,0:T(2,128)(2,1)}), bf16[8,2,9792]{2,1,0:T(2,128)(2,1)S(1)}, u32[]{:S(2)}, u32[]{:S(2)}) async-start(bf16[8,2,9792]{2,1,0:T(2,128)(2,1)} %pieces.1), calls=%async_computation | async-start | bytes 630784 | tf_op jit(solution)/shard_map/all_to_all | solution.py:305
  11.7 0.0 copy-start.2
  11.7 0.0 collective-permute-done.1.rest_1_
  11.7 0.0 collective-permute-done.2.rest_2_
  11.7 2.1 %collective-permute-start.4 = (bf16[576,254]{1,0:T(8,128)(2,1)S(1)}, bf16[576,254]{1,0:T(8,128)(2,1)S(1)}, u32[]{:S(2)}, u32[]{:S(2)}) collective-permute-start(bf16[576,254]{1,0:T(8,128)(2,1)S(1)} %collective-permute-done.2.rest_2_), channel_id=1, source_target_pairs={{2,0},{3,7},{6,2},{7,11},{10,6},{11,15},{14,10},{15,13},{12,14},{1... | collective-permute-start | bytes 877832 | tf_op jit(solution)/shard_map/ppermute | solution.py:312
  13.8 0.1 collective-permute-start.3
  13.8 8.9 %all-to-all-done = bf16[8,2,9792]{2,1,0:T(2,128)(2,1)S(1)} async-done(((bf16[8,2,9792]{2,1,0:T(2,128)(2,1)}), bf16[8,2,9792]{2,1,0:T(2,128)(2,1)S(1)}, u32[]{:S(2)}, u32[]{:S(2)}) %all-to-all-start) | async-done | bytes 313376 | tf_op jit(solution)/shard_map/all_to_all | solution.py:305
  22.7 0.2 reshape.6.here_ref
  23.0 0.0 copy-start.3
  23.0 0.1 collective-permute-start
  23.1 1.0 %collective-permute-done.4.rest_4_ = bf16[576,254]{1,0:T(8,128)(2,1)S(1)} collective-permute-done((bf16[576,254]{1,0:T(8,128)(2,1)S(1)}, bf16[576,254]{1,0:T(8,128)(2,1)S(1)}, u32[]{:S(2)}, u32[]{:S(2)}) %collective-permute-start.4) | collective-permute-done | bytes 292640 | tf_op jit(solution)/shard_map/ppermute | solution.py:312
  24.1 1.7 %collective-permute-start.5 = (bf16[576,254]{1,0:T(8,128)(2,1)S(1)}, bf16[576,254]{1,0:T(8,128)(2,1)S(1)}, u32[]{:S(2)}, u32[]{:S(2)}) collective-permute-start(bf16[576,254]{1,0:T(8,128)(2,1)S(1)} %collective-permute-done.4.rest_4_), channel_id=1, source_target_pairs={{2,0},{3,7},{6,2},{7,11},{10,6},{11,15},{14,10},{15,13},{12,14},{1... | collective-permute-start | bytes 877832 | tf_op jit(solution)/shard_map/ppermute | solution.py:312
  25.8 0.0 collective-permute-done.3.rest_3_
  25.8 0.6 %collective-permute-start.6 = (bf16[576,254]{1,0:T(8,128)(2,1)S(1)}, bf16[576,254]{1,0:T(8,128)(2,1)S(1)}, u32[]{:S(2)}, u32[]{:S(2)}) collective-permute-start(bf16[576,254]{1,0:T(8,128)(2,1)S(1)} %collective-permute-done.3.rest_3_), channel_id=1, source_target_pairs={{2,6},{3,1},{6,10},{7,3},{10,14},{11,7},{14,12},{15,11},{12,8},{13... | collective-permute-start | bytes 877832 | tf_op jit(solution)/shard_map/ppermute | solution.py:312
  27.0 0.0 collective-permute-done.there_ref
  27.0 0.0 copy-done.2
  27.1 0.0 copy-done.3
  27.1 3.6 %first.1 = (bf16[512,576]{1,0:T(8,128)(2,1)S(1)}, f32[512,128]{1,0:T(8,128)S(1)}, f32[512,128]{1,0:T(8,128)S(1)}, f32[512,512]{1,0:T(8,128)S(1)}) custom-call(s32[1]{0:T(128)S(6)} %copy.9.length_ref, s32[128]{0:T(128)S(1)} %copy-done.3, bf16[16,9792]{1,0:T(8,128)(2,1)S(1)} %reshape.6.here_ref, bf16[16,9792]{1,0:T(8,128)(2,1)S(1)} %collective-permute-done.there_ref, ...), custom_call_target="tpu_custom_call" | custom-call | tf_op jit(solution)/shard_map/first/pallas_call | solution.py:272
  30.7 3.1 %collective-permute-done.5.rest_1_ = bf16[576,254]{1,0:T(8,128)(2,1)S(1)} collective-permute-done((bf16[576,254]{1,0:T(8,128)(2,1)S(1)}, bf16[576,254]{1,0:T(8,128)(2,1)S(1)}, u32[]{:S(2)}, u32[]{:S(2)}) %collective-permute-start.5) | collective-permute-done | bytes 292640 | tf_op jit(solution)/shard_map/ppermute | solution.py:312
  33.8 1.8 %collective-permute-start.8 = (bf16[320,254]{1,0:T(8,128)(2,1)S(1)}, bf16[320,254]{1,0:T(8,128)(2,1)S(1)}, u32[]{:S(2)}, u32[]{:S(2)}) collective-permute-start(bf16[320,254]{1,0:T(8,128)(2,1)S(1)} %slice.7), channel_id=1, source_target_pairs={{2,0},{3,7},{6,2},{7,11},{10,6},{11,15},{14,10},{15,13},{12,14},{1... | collective-permute-start | bytes 487688 | tf_op jit(solution)/shard_map/ppermute | solution.py:326
  35.6 0.0 collective-permute-done.6.rest_0_
  35.6 0.8 %collective-permute-start.7 = (bf16[256,254]{1,0:T(8,128)(2,1)S(1)}, bf16[256,254]{1,0:T(8,128)(2,1)S(1)}, u32[]{:S(2)}, u32[]{:S(2)}) collective-permute-start(bf16[256,254]{1,0:T(8,128)(2,1)S(1)} %slice.8), channel_id=1, source_target_pairs={{2,6},{3,1},{6,10},{7,3},{10,14},{11,7},{14,12},{15,11},{12,8},{13... | collective-permute-start | bytes 390152 | tf_op jit(solution)/shard_map/ppermute | solution.py:324
  37.1 2.5 %middle.1 = (f32[512,128]{1,0:T(8,128)S(1)}, f32[512,128]{1,0:T(8,128)S(1)}, f32[512,512]{1,0:T(8,128)S(1)}) custom-call(s32[1]{0:T(128)S(6)} %copy.9.length_ref, s32[1]{0:T(128)S(6)} %copy.10.offset_ref, s32[128]{0:T(128)S(1)} %copy-done.3, bf16[512,576]{1,0:T(8,128)(2,1)S(1)} %get-tuple-element.20.q_ref, f32[512,128]{1,0:T(8,128)S(1)} %get-tuple-element.24.m_in, ...), custom_call_target="tpu_custom_call" | custom-call | tf_op jit(solution)/shard_map/middle/pallas_call | solution.py:327
  39.6 1.1 %collective-permute-done.7.top_ref = bf16[256,254]{1,0:T(8,128)(2,1)S(1)} collective-permute-done((bf16[256,254]{1,0:T(8,128)(2,1)S(1)}, bf16[256,254]{1,0:T(8,128)(2,1)S(1)}, u32[]{:S(2)}, u32[]{:S(2)}) %collective-permute-start.7) | collective-permute-done | bytes 130080 | tf_op jit(solution)/shard_map/ppermute | solution.py:324
  40.6 0.0 collective-permute-done.8.bottom_ref
  40.6 1.2 %give.1 = bf16[256,640]{1,0:T(8,128)(2,1)S(1)} custom-call(s32[1]{0:T(128)S(6)} %copy.9.length_ref, s32[128]{0:T(128)S(1)} %copy-done.3, bf16[512,576]{1,0:T(8,128)(2,1)S(1)} %get-tuple-element.20.q_ref, f32[512,128]{1,0:T(8,128)S(1)} %get-tuple-element.27.m_ref, f32[512,128]{1,0:T(8,128)S(1)} %get-tuple-element.28.l_ref, ...), custom_call_target="tpu_custom_call" | custom-call | tf_op jit(solution)/shard_map/give/pallas_call | solution.py:339
  41.8 0.0 copy-start
  41.8 0.1 collective-permute-start.9
  41.9 1.2 %keep.1.keep_ref = f32[256,640]{1,0:T(8,128)S(1)} custom-call(s32[1]{0:T(128)S(6)} %copy.9.length_ref, s32[128]{0:T(128)S(1)} %copy-done.3, bf16[512,576]{1,0:T(8,128)(2,1)S(1)} %get-tuple-element.20.q_ref, f32[512,128]{1,0:T(8,128)S(1)} %get-tuple-element.27.m_ref, f32[512,128]{1,0:T(8,128)S(1)} %get-tuple-element.28.l_ref, ...), custom_call_target="tpu_custom_call" | custom-call | tf_op jit(solution)/shard_map/keep/pallas_call | solution.py:339
  43.1 0.4 collective-permute-done.9.got_ref
  43.5 0.0 copy-done
  43.5 0.5 merge.1
  44.0 11.5 %all_to_all.10 = bf16[16,2,1024]{2,1,0:T(2,128)(2,1)S(1)} all-to-all(bf16[16,2,1024]{2,1,0:T(2,128)(2,1)S(1)} %merge.1), channel_id=1, replica_groups=mesh['groups'=2,'ctx'=16] {'ctx'}, dimensions={0} | all-to-all | bytes 131072 | tf_op jit(solution)/shard_map/all_to_all | solution.py:359
  55.5 0.6 %copy.11 = bf16[2,16384]{1,0:T(2,128)(2,1)} copy(bf16[2,16384]{1,0:T(2,128)(2,1)S(1)} %bitcast.7) | data formatting | bytes 131072
  (2 shorter events, 0.0 us)
Async XLA Ops:
  0.0 11.7 %collective-permute-start.1 = (bf16[576,254]{1,0:T(8,128)(2,1)}, bf16[576,254]{1,0:T(8,128)(2,1)S(1)}, u32[]{:S(2)}, u32[]{:S(2)}) collective-permute-start(bf16[576,254]{1,0:T(8,128)(2,1)} %bitcast.4), channel_id=1, source_target_pairs={{2,6},{3,1},{6,10},{7,3},{10,14},{11,7},{14,12},{15,11},{12,8},{13... | collective-permute-start | bytes 877832 | tf_op jit(solution)/shard_map/ppermute | solution.py:295
  2.9 8.7 %collective-permute-start.2 = (bf16[576,254]{1,0:T(8,128)(2,1)}, bf16[576,254]{1,0:T(8,128)(2,1)S(1)}, u32[]{:S(2)}, u32[]{:S(2)}) collective-permute-start(bf16[576,254]{1,0:T(8,128)(2,1)} %bitcast.5), channel_id=1, source_target_pairs={{2,0},{3,7},{6,2},{7,11},{10,6},{11,15},{14,10},{15,13},{12,14},{1... | collective-permute-start | bytes 877832 | tf_op jit(solution)/shard_map/ppermute | solution.py:295
  3.0 1.0 %copy-start.1 = (bf16[2,73728]{1,0:T(2,128)(2,1)S(1)}, bf16[2,73728]{1,0:T(2,128)(2,1)}, u32[]{:S(2)}) copy-start(bf16[2,73728]{1,0:T(2,128)(2,1)} %queries_ref.1) | copy-start | bytes 884740
  4.0 0.7 %copy-start.4 = (bf16[2,576]{1,0:T(2,128)(2,1)S(1)}, bf16[2,576]{1,0:T(2,128)(2,1)}, u32[]{:S(2)}) copy-start(bf16[2,576]{1,0:T(2,128)(2,1)} %span_ref.1) | copy-start | bytes 6916
  5.4 17.3 %all-to-all-start = ((bf16[8,2,9792]{2,1,0:T(2,128)(2,1)}), bf16[8,2,9792]{2,1,0:T(2,128)(2,1)S(1)}, u32[]{:S(2)}, u32[]{:S(2)}) async-start(bf16[8,2,9792]{2,1,0:T(2,128)(2,1)} %pieces.1), calls=%async_computation | async-start | bytes 630784 | tf_op jit(solution)/shard_map/all_to_all | solution.py:305
  11.7 15.4 %copy-start.2 = (bf16[254,576]{0,1:T(8,128)(2,1)S(1)}, bf16[254,576]{0,1:T(8,128)(2,1)}, u32[]{:S(2)}) copy-start(bf16[254,576]{0,1:T(8,128)(2,1)} %param.8) | copy-start | bytes 877828
  11.7 12.4 %collective-permute-start.4 = (bf16[576,254]{1,0:T(8,128)(2,1)S(1)}, bf16[576,254]{1,0:T(8,128)(2,1)S(1)}, u32[]{:S(2)}, u32[]{:S(2)}) collective-permute-start(bf16[576,254]{1,0:T(8,128)(2,1)S(1)} %collective-permute-done.2.rest_2_), channel_id=1, source_target_pairs={{2,0},{3,7},{6,2},{7,11},{10,6},{11,15},{14,10},{15,13},{12,14},{1... | collective-permute-start | bytes 877832 | tf_op jit(solution)/shard_map/ppermute | solution.py:312
  13.8 12.0 %collective-permute-start.3 = (bf16[576,254]{1,0:T(8,128)(2,1)S(1)}, bf16[576,254]{1,0:T(8,128)(2,1)S(1)}, u32[]{:S(2)}, u32[]{:S(2)}) collective-permute-start(bf16[576,254]{1,0:T(8,128)(2,1)S(1)} %collective-permute-done.1.rest_1_), channel_id=1, source_target_pairs={{2,6},{3,1},{6,10},{7,3},{10,14},{11,7},{14,12},{15,11},{12,8},{13... | collective-permute-start | bytes 877832 | tf_op jit(solution)/shard_map/ppermute | solution.py:312
  23.0 4.1 %copy-start.3 = (s32[128]{0:T(128)S(1)}, s32[128]{0:T(128)}, u32[]{:S(2)}) copy-start(s32[128]{0:T(128)} %constant.2.clone.table_ref) | copy-start | bytes 1540
  23.0 4.1 %collective-permute-start = (bf16[16,9792]{1,0:T(8,128)(2,1)S(1)}, bf16[16,9792]{1,0:T(8,128)(2,1)S(1)}, u32[]{:S(2)}, u32[]{:S(2)}) collective-permute-start(bf16[16,9792]{1,0:T(8,128)(2,1)S(1)} %reshape.6.here_ref), channel_id=1, source_target_pairs={{0,1},{1,0},{2,3},{3,2},{4,5},{5,4},{6,7},{7,6},{8,9},{9,8},{10,11... | collective-permute-start | bytes 940040 | tf_op jit(solution)/shard_map/ppermute | solution.py:315
  24.1 9.7 %collective-permute-start.5 = (bf16[576,254]{1,0:T(8,128)(2,1)S(1)}, bf16[576,254]{1,0:T(8,128)(2,1)S(1)}, u32[]{:S(2)}, u32[]{:S(2)}) collective-permute-start(bf16[576,254]{1,0:T(8,128)(2,1)S(1)} %collective-permute-done.4.rest_4_), channel_id=1, source_target_pairs={{2,0},{3,7},{6,2},{7,11},{10,6},{11,15},{14,10},{15,13},{12,14},{1... | collective-permute-start | bytes 877832 | tf_op jit(solution)/shard_map/ppermute | solution.py:312
  25.8 9.8 %collective-permute-start.6 = (bf16[576,254]{1,0:T(8,128)(2,1)S(1)}, bf16[576,254]{1,0:T(8,128)(2,1)S(1)}, u32[]{:S(2)}, u32[]{:S(2)}) collective-permute-start(bf16[576,254]{1,0:T(8,128)(2,1)S(1)} %collective-permute-done.3.rest_3_), channel_id=1, source_target_pairs={{2,6},{3,1},{6,10},{7,3},{10,14},{11,7},{14,12},{15,11},{12,8},{13... | collective-permute-start | bytes 877832 | tf_op jit(solution)/shard_map/ppermute | solution.py:312
  33.8 6.8 %collective-permute-start.8 = (bf16[320,254]{1,0:T(8,128)(2,1)S(1)}, bf16[320,254]{1,0:T(8,128)(2,1)S(1)}, u32[]{:S(2)}, u32[]{:S(2)}) collective-permute-start(bf16[320,254]{1,0:T(8,128)(2,1)S(1)} %slice.7), channel_id=1, source_target_pairs={{2,0},{3,7},{6,2},{7,11},{10,6},{11,15},{14,10},{15,13},{12,14},{1... | collective-permute-start | bytes 487688 | tf_op jit(solution)/shard_map/ppermute | solution.py:326
  35.6 5.0 %collective-permute-start.7 = (bf16[256,254]{1,0:T(8,128)(2,1)S(1)}, bf16[256,254]{1,0:T(8,128)(2,1)S(1)}, u32[]{:S(2)}, u32[]{:S(2)}) collective-permute-start(bf16[256,254]{1,0:T(8,128)(2,1)S(1)} %slice.8), channel_id=1, source_target_pairs={{2,6},{3,1},{6,10},{7,3},{10,14},{11,7},{14,12},{15,11},{12,8},{13... | collective-permute-start | bytes 390152 | tf_op jit(solution)/shard_map/ppermute | solution.py:324
  41.8 1.7 %copy-start = (bf16[8,512,128]{2,1,0:T(8,128)(2,1)S(1)}, bf16[8,512,128]{2,1,0:T(8,128)(2,1)}, u32[]{:S(2)}) copy-start(bf16[8,512,128]{2,1,0:T(8,128)(2,1)} %up_ref.1) | copy-start | bytes 3145732
  41.8 1.7 %collective-permute-start.9 = (bf16[256,640]{1,0:T(8,128)(2,1)S(1)}, bf16[256,640]{1,0:T(8,128)(2,1)S(1)}, u32[]{:S(2)}, u32[]{:S(2)}) collective-permute-start(bf16[256,640]{1,0:T(8,128)(2,1)S(1)} %give.1), channel_id=1, source_target_pairs={{0,1},{1,0},{2,3},{3,2},{4,5},{5,4},{6,7},{7,6},{8,9},{9,8},{10,11... | collective-permute-start | bytes 983048 | tf_op jit(solution)/shard_map/ppermute | solution.py:348

commit v18 on v17

--- a/solution.py
+++ b/solution.py
@@ -120,14 +120,6 @@
     ]
 
 
-def pieces_kernel(queries_ref, span_ref, out_ref):
-    chips = out_ref.shape[0]
-    part = queries_ref.shape[1] // chips
-    for chip in range(chips):
-        out_ref[chip, :, :part] = queries_ref[:, chip * part:(chip + 1) * part]
-        out_ref[chip, :, part:] = span_ref[...]
-
-
 def first_kernel(heads, count, length_ref, table_ref, here_ref, there_ref, *rest):
     keys, (q_ref, m_ref, l_ref, acc_ref) = rest[:count], rest[count:]
     half = here_ref.shape[0]
@@ -146,14 +138,14 @@
 
 
 def span_kernel(at, count, length_ref, offset_ref, table_ref, q_ref, m_in, l_in, acc_in,
-                here_ref, *rest):
+                span_ref, *rest):
     keys, new = rest[:count], rest[count:]
     chips = lax.axis_size("ctx") // CORES
-    half = here_ref.shape[0]
+    half = span_ref.shape[0]
     tokens = half // chips
-    width = q_ref.shape[1]
-    key_index = lax.broadcasted_iota(jnp.int32, (1, half), 1)
-    key_token = token_of(key_index, tokens, chips)
+    slot, t = parted(lax.broadcasted_iota(jnp.int32, (1, half), 1), tokens)
+    me = lax.axis_index("ctx")
+    key_token = (((me // CORES) ^ slot) * CORES + me % CORES) * tokens + t
 
     def shown(start, block):
         row_index = start + lax.broadcasted_iota(jnp.int32, (block, 1), 0)
@@ -162,7 +154,7 @@
 
     fold_shards(
         q_ref, with_base(table_ref, at, keys), length_ref[0], (m_in, l_in, acc_in), new,
-        (here_ref[:, here_ref.shape[1] - width:], shown),
+        (span_ref[...], shown),
     )
 
 
@@ -294,24 +286,23 @@
     own = prefix_latents.T
     right, left = onward(own), backward(own)
 
-    pieces = pl.pallas_call(
-        pieces_kernel,
-        out_shape=shape(chips, tokens, (heads + 1) * width, dtype=bf16),
-        in_specs=[VMEM] * 2,
-        out_specs=VMEM,
-        compiler_params=PARAMS,
-        name="pieces",
-    )(queries, span_latents)
+    pieces = queries.reshape(tokens, chips, heads * width).transpose(1, 0, 2)
     here = lax.all_to_all(
         pieces, "ctx", split_axis=0, concat_axis=0, axis_index_groups=same_core, tiled=True
     )
 
     right, left = lax.optimization_barrier((right, left))
+    spans, bit = span_latents, 1
+    while bit < chips:
+        swap = [(d, d ^ (bit * CORES)) for d in range(ctx)]
+        spans = jnp.concatenate([spans, lax.ppermute(spans, "ctx", swap)], axis=0)
+        bit *= 2
     keys, state, at = [own, right, left], None, 0
     for s in range(2, steps):
         right, left = onward(right), backward(left)
         if s == 2:
-            here = here.reshape(chips * tokens, (heads + 1) * width)
+            here, spans = lax.optimization_barrier((here, spans))
+            here = here.reshape(chips * tokens, heads * width)
             there = lax.ppermute(here, "ctx", other_core)
             keys += [right, left]
             continue
@@ -331,7 +322,7 @@
         out_specs=[VMEM] * 3,
         compiler_params=PARAMS,
         name="middle",
-    )(prefix_length, span_offset, table, q, *state, here, *keys)
+    )(prefix_length, span_offset, table, q, *state, spans, *keys)
     per_core = heads // CORES
     part = per_core * everyone
 

time: 56.5 us -> 59.4 us (1.051)
  starting transfers between devices: 16.5 us -> 21.5 us
  local copies, waits for them, and re-layouts: 2.54 us -> 0.79 us
  Pallas kernels: 9.7 us -> 8.91 us
    ppermute x0 -> x3, waiting for transfers between devices: none -> 11 us  [on_device(): spans = jnp.concatenate([spans, lax.ppermute(spans, 'ctx', swap)], axis=0)]
    all_to_all x1, waiting for transfers between devices: 8.91 us -> 0.01 us  [on_device(): lax.all_to_all(pieces, 'ctx', split_axis=0, concat_axis=0, axis_index_gro...]
    ppermute x0 -> x3, starting transfers between devices: none -> 5.72 us  [on_device(): spans = jnp.concatenate([spans, lax.ppermute(spans, 'ctx', swap)], axis=0)]
    ppermute x1, starting transfers between devices: 1.79 us -> 0.06 us  [on_device(): bottom = backward(left[cut:])]
    unnamed x11 -> x9, local copies, waits for them, and re-layouts: 2.29 us -> 0.65 us
    ppermute x1, starting transfers between devices: 0.82 us -> 2.05 us  [on_device(): top = onward(right[:cut])]
    ppermute x1, waiting for transfers between devices: 1.06 us -> 0.05 us  [on_device(): top = onward(right[:cut])]
    ppermute x4, waiting for transfers between devices: 4.11 us -> 3.18 us  [on_device(): right, left = (onward(right), backward(left))]
  transfers between devices with their start and end apart: 11 -> 14, of which waited for: 5 -> 6; matrix products, arithmetic and copies ran while one was open for 0% -> 0% of each run, Pallas kernels for 14% -> 12%
where the time goes in v18:
time: 59.4 us; the launch traced here: 59.2 us
  starting transfers between devices  21.5 us (36%)
  waiting for transfers between devices  14.9 us (25%)
  blocking collectives  11.5 us (19%)
  Pallas kernels  8.91 us (15%)
  between operations  1.49 us (3%)
  local copies, waits for them, and re-layouts  0.79 us (1%)
    all_to_all x1, blocking collectives, on_device(): lax.all_to_all(merged, 'ctx', split_axis=0, concat_axis=0, tiled=True)  11.5 us
    ppermute x3, waiting for transfers between devices, on_device(): spans = jnp.concatenate([spans, lax.ppermute(spans, 'ctx', swap)], axis=0)  11 us
    all_to_all x1, starting transfers between devices, on_device(): lax.all_to_all(pieces, 'ctx', split_axis=0, concat_axis=0, axis_index_gro...  6.38 us
    ppermute x3, starting transfers between devices, on_device(): spans = jnp.concatenate([spans, lax.ppermute(spans, 'ctx', swap)], axis=0)  5.72 us
    ppermute x4, starting transfers between devices, on_device(): right, left = (onward(right), backward(left))  4.09 us
    pallas_call x1, Pallas kernels, fold_first(): pl.pallas_call(functools.partial(first_kernel, heads, len(keys)), out_sha...  3.58 us
    ppermute x4, waiting for transfers between devices, on_device(): right, left = (onward(right), backward(left))  3.18 us
    ppermute x2, starting transfers between devices, on_device(): right, left = (onward(own), backward(own))  3.03 us
  transfers between devices with their start and end apart: 14, of which 6 were waited for; matrix products, arithmetic and copies ran while one was open for 0% of the time, Pallas kernels for 12%

profile of v18, /device:TPU:0, one launch (start us, length us, event | category | flops | bytes accessed | tf_op | source)
XLA Modules:
  0.0 59.2 jit_solution(1437515522952897487)
XLA Ops:
  0.0 2.9 %collective-permute-start.4 = (bf16[576,254]{1,0:T(8,128)(2,1)}, bf16[576,254]{1,0:T(8,128)(2,1)S(1)}, u32[]{:S(2)}, u32[]{:S(2)}) collective-permute-start(bf16[576,254]{1,0:T(8,128)(2,1)} %bitcast.7), channel_id=1, source_target_pairs={{2,6},{3,1},{6,10},{7,3},{10,14},{11,7},{14,12},{15,11},{12,8},{13... | collective-permute-start | bytes 877832 | tf_op jit(solution)/shard_map/ppermute | solution.py:287
  2.9 0.1 collective-permute-start.5
  3.0 0.0 copy-start.3
  3.0 6.4 %all-to-all-start = ((bf16[8,2,9216]{2,1,0:T(2,128)(2,1)}), bf16[8,2,9216]{2,1,0:T(2,128)(2,1)S(1)}, u32[]{:S(2)}, u32[]{:S(2)}) async-start(bf16[8,2,9216]{2,1,0:T(2,128)(2,1)} %bitcast.10), calls=%async_computation | async-start | bytes 589824 | tf_op jit(solution)/shard_map/all_to_all | solution.py:290
  9.4 0.0 copy-done.3
  9.4 2.0 %collective-permute-start = (bf16[2,576]{1,0:T(2,128)(2,1)S(1)}, bf16[2,576]{1,0:T(2,128)(2,1)S(1)}, u32[]{:S(2)}, u32[]{:S(2)}) collective-permute-start(bf16[2,576]{1,0:T(2,128)(2,1)S(1)} %copy-done.3), channel_id=1, source_target_pairs={{0,2},{1,3},{2,0},{3,1},{4,6},{5,7},{6,4},{7,5},{8,10},{9,11},{10,... | collective-permute-start | bytes 6920 | tf_op jit(solution)/shard_map/ppermute | solution.py:298
  11.4 0.0 collective-permute-done.4.rest_1_
  11.4 0.0 collective-permute-done.5.rest_2_
  11.4 1.0 %collective-permute-start.6 = (bf16[576,254]{1,0:T(8,128)(2,1)S(1)}, bf16[576,254]{1,0:T(8,128)(2,1)S(1)}, u32[]{:S(2)}, u32[]{:S(2)}) collective-permute-start(bf16[576,254]{1,0:T(8,128)(2,1)S(1)} %collective-permute-done.4.rest_1_), channel_id=1, source_target_pairs={{2,6},{3,1},{6,10},{7,3},{10,14},{11,7},{14,12},{15,11},{12,8},{13... | collective-permute-start | bytes 877832 | tf_op jit(solution)/shard_map/ppermute | solution.py:302
  12.4 1.1 %collective-permute-start.7 = (bf16[576,254]{1,0:T(8,128)(2,1)S(1)}, bf16[576,254]{1,0:T(8,128)(2,1)S(1)}, u32[]{:S(2)}, u32[]{:S(2)}) collective-permute-start(bf16[576,254]{1,0:T(8,128)(2,1)S(1)} %collective-permute-done.5.rest_2_), channel_id=1, source_target_pairs={{2,0},{3,7},{6,2},{7,11},{10,6},{11,15},{14,10},{15,13},{12,14},{1... | collective-permute-start | bytes 877832 | tf_op jit(solution)/shard_map/ppermute | solution.py:302
  13.5 0.7 %collective-permute-done = bf16[2,576]{1,0:T(2,128)(2,1)S(1)} collective-permute-done((bf16[2,576]{1,0:T(2,128)(2,1)S(1)}, bf16[2,576]{1,0:T(2,128)(2,1)S(1)}, u32[]{:S(2)}, u32[]{:S(2)}) %collective-permute-start) | collective-permute-done | bytes 2336 | tf_op jit(solution)/shard_map/ppermute | solution.py:298
  14.2 1.9 %collective-permute-start.1 = (bf16[4,576]{1,0:T(4,128)(2,1)S(1)}, bf16[4,576]{1,0:T(4,128)(2,1)S(1)}, u32[]{:S(2)}, u32[]{:S(2)}) collective-permute-start(bf16[4,576]{1,0:T(4,128)(2,1)S(1)} %pad_maximum_fusion.2), channel_id=1, source_target_pairs={{0,4},{1,5},{2,6},{3,7},{4,0},{5,1},{6,2},{7,3},{8,12},{9,13},{10,... | collective-permute-start | bytes 13832 | tf_op jit(solution)/shard_map/ppermute | solution.py:298
  16.0 7.5 %collective-permute-done.1 = bf16[4,576]{1,0:T(4,128)(2,1)S(1)} collective-permute-done((bf16[4,576]{1,0:T(4,128)(2,1)S(1)}, bf16[4,576]{1,0:T(4,128)(2,1)S(1)}, u32[]{:S(2)}, u32[]{:S(2)}) %collective-permute-start.1) | collective-permute-done | bytes 4640 | tf_op jit(solution)/shard_map/ppermute | solution.py:298
  23.6 1.8 %collective-permute-start.2 = (bf16[8,576]{1,0:T(8,128)(2,1)S(1)}, bf16[8,576]{1,0:T(8,128)(2,1)S(1)}, u32[]{:S(2)}, u32[]{:S(2)}) collective-permute-start(bf16[8,576]{1,0:T(8,128)(2,1)S(1)} %pad_maximum_fusion.1), channel_id=1, source_target_pairs={{0,8},{1,9},{2,10},{3,11},{4,12},{5,13},{6,14},{7,15},{8,0},{9,1},... | collective-permute-start | bytes 27656 | tf_op jit(solution)/shard_map/ppermute | solution.py:298
  25.4 2.8 %collective-permute-done.2 = bf16[8,576]{1,0:T(8,128)(2,1)S(1)} collective-permute-done((bf16[8,576]{1,0:T(8,128)(2,1)S(1)}, bf16[8,576]{1,0:T(8,128)(2,1)S(1)}, u32[]{:S(2)}, u32[]{:S(2)}) %collective-permute-start.2) | collective-permute-done | bytes 9248 | tf_op jit(solution)/shard_map/ppermute | solution.py:298
  28.2 0.0 copy-start.1
  28.3 0.0 all-to-all-done
  28.3 0.1 reshape.10.here_ref
  28.4 0.0 copy-start.2
  28.4 0.1 collective-permute-start.3
  28.5 0.0 collective-permute-done.7.rest_4_
  28.5 0.1 collective-permute-start.8
  28.6 0.0 collective-permute-done.6.rest_3_
  28.6 2.0 %collective-permute-start.9 = (bf16[576,254]{1,0:T(8,128)(2,1)S(1)}, bf16[576,254]{1,0:T(8,128)(2,1)S(1)}, u32[]{:S(2)}, u32[]{:S(2)}) collective-permute-start(bf16[576,254]{1,0:T(8,128)(2,1)S(1)} %collective-permute-done.6.rest_3_), channel_id=1, source_target_pairs={{2,6},{3,1},{6,10},{7,3},{10,14},{11,7},{14,12},{15,11},{12,8},{13... | collective-permute-start | bytes 877832 | tf_op jit(solution)/shard_map/ppermute | solution.py:302
  31.2 0.0 collective-permute-done.3.there_ref
  31.2 0.0 copy-done.1
  31.2 0.0 copy-done.2
  31.2 3.6 %first.1 = (bf16[512,576]{1,0:T(8,128)(2,1)S(1)}, f32[512,128]{1,0:T(8,128)S(1)}, f32[512,128]{1,0:T(8,128)S(1)}, f32[512,512]{1,0:T(8,128)S(1)}) custom-call(s32[1]{0:T(128)S(6)} %copy.10.length_ref, s32[128]{0:T(128)S(1)} %copy-done.2, bf16[16,9216]{1,0:T(8,128)(2,1)S(1)} %reshape.10.here_ref, bf16[16,9216]{1,0:T(8,128)(2,1)S(1)} %collective-permute-done.3.there_ref, ...), custom_call_target="tpu_custom_call" | custom-call | tf_op jit(solution)/shard_map/first/pallas_call | solution.py:264
  34.8 3.2 %collective-permute-done.8.rest_1_ = bf16[576,254]{1,0:T(8,128)(2,1)S(1)} collective-permute-done((bf16[576,254]{1,0:T(8,128)(2,1)S(1)}, bf16[576,254]{1,0:T(8,128)(2,1)S(1)}, u32[]{:S(2)}, u32[]{:S(2)}) %collective-permute-start.8) | collective-permute-done | bytes 292640 | tf_op jit(solution)/shard_map/ppermute | solution.py:302
  38.0 0.1 collective-permute-start.11
  38.1 0.0 collective-permute-done.9.rest_0_
  38.1 2.1 %collective-permute-start.10 = (bf16[256,254]{1,0:T(8,128)(2,1)S(1)}, bf16[256,254]{1,0:T(8,128)(2,1)S(1)}, u32[]{:S(2)}, u32[]{:S(2)}) collective-permute-start(bf16[256,254]{1,0:T(8,128)(2,1)S(1)} %slice.8), channel_id=1, source_target_pairs={{2,6},{3,1},{6,10},{7,3},{10,14},{11,7},{14,12},{15,11},{12,8},{13... | collective-permute-start | bytes 390152 | tf_op jit(solution)/shard_map/ppermute | solution.py:315
  40.8 2.5 %middle.1 = (f32[512,128]{1,0:T(8,128)S(1)}, f32[512,128]{1,0:T(8,128)S(1)}, f32[512,512]{1,0:T(8,128)S(1)}) custom-call(s32[1]{0:T(128)S(6)} %copy.10.length_ref, s32[1]{0:T(128)S(6)} %copy.11.offset_ref, s32[128]{0:T(128)S(1)} %copy-done.2, bf16[512,576]{1,0:T(8,128)(2,1)S(1)} %get-tuple-element.23.q_ref, f32[512,128]{1,0:T(8,128)S(1)} %get-tuple-element.27.m_in, ...), custom_call_target="tpu_custom_call" | custom-call | tf_op jit(solution)/shard_map/middle/pallas_call | solution.py:318
  43.3 0.0 collective-permute-done.10.top_ref
  43.3 0.3 collective-permute-done.11.bottom_ref
  43.6 1.2 %give.1 = bf16[256,640]{1,0:T(8,128)(2,1)S(1)} custom-call(s32[1]{0:T(128)S(6)} %copy.10.length_ref, s32[128]{0:T(128)S(1)} %copy-done.2, bf16[512,576]{1,0:T(8,128)(2,1)S(1)} %get-tuple-element.23.q_ref, f32[512,128]{1,0:T(8,128)S(1)} %get-tuple-element.31.m_ref, f32[512,128]{1,0:T(8,128)S(1)} %get-tuple-element.32.l_ref, ...), custom_call_target="tpu_custom_call" | custom-call | tf_op jit(solution)/shard_map/give/pallas_call | solution.py:330
  44.8 0.0 copy-start
  44.8 0.1 collective-permute-start.12
  44.9 1.2 %keep.1.keep_ref = f32[256,640]{1,0:T(8,128)S(1)} custom-call(s32[1]{0:T(128)S(6)} %copy.10.length_ref, s32[128]{0:T(128)S(1)} %copy-done.2, bf16[512,576]{1,0:T(8,128)(2,1)S(1)} %get-tuple-element.23.q_ref, f32[512,128]{1,0:T(8,128)S(1)} %get-tuple-element.31.m_ref, f32[512,128]{1,0:T(8,128)S(1)} %get-tuple-element.32.l_ref, ...), custom_call_target="tpu_custom_call" | custom-call | tf_op jit(solution)/shard_map/keep/pallas_call | solution.py:330
  46.1 0.4 collective-permute-done.12.got_ref
  46.5 0.0 copy-done
  46.5 0.5 merge.1
  47.0 11.5 %all_to_all.10 = bf16[16,2,1024]{2,1,0:T(2,128)(2,1)S(1)} all-to-all(bf16[16,2,1024]{2,1,0:T(2,128)(2,1)S(1)} %merge.1), channel_id=1, replica_groups=mesh['groups'=2,'ctx'=16] {'ctx'}, dimensions={0} | all-to-all | bytes 131072 | tf_op jit(solution)/shard_map/all_to_all | solution.py:350
  58.5 0.6 %copy.12 = bf16[2,16384]{1,0:T(2,128)(2,1)} copy(bf16[2,16384]{1,0:T(2,128)(2,1)S(1)} %bitcast.11) | data formatting | bytes 131072
  (5 shorter events, 0.1 us)
Async XLA Ops:
  0.0 11.4 %collective-permute-start.4 = (bf16[576,254]{1,0:T(8,128)(2,1)}, bf16[576,254]{1,0:T(8,128)(2,1)S(1)}, u32[]{:S(2)}, u32[]{:S(2)}) collective-permute-start(bf16[576,254]{1,0:T(8,128)(2,1)} %bitcast.7), channel_id=1, source_target_pairs={{2,6},{3,1},{6,10},{7,3},{10,14},{11,7},{14,12},{15,11},{12,8},{13... | collective-permute-start | bytes 877832 | tf_op jit(solution)/shard_map/ppermute | solution.py:287
  2.9 8.5 %collective-permute-start.5 = (bf16[576,254]{1,0:T(8,128)(2,1)}, bf16[576,254]{1,0:T(8,128)(2,1)S(1)}, u32[]{:S(2)}, u32[]{:S(2)}) collective-permute-start(bf16[576,254]{1,0:T(8,128)(2,1)} %bitcast.8), channel_id=1, source_target_pairs={{2,0},{3,7},{6,2},{7,11},{10,6},{11,15},{14,10},{15,13},{12,14},{1... | collective-permute-start | bytes 877832 | tf_op jit(solution)/shard_map/ppermute | solution.py:287
  3.0 6.4 %copy-start.3 = (bf16[2,576]{1,0:T(2,128)(2,1)S(1)}, bf16[2,576]{1,0:T(2,128)(2,1)}, u32[]{:S(2)}) copy-start(bf16[2,576]{1,0:T(2,128)(2,1)} %param.9) | copy-start | bytes 6916
  3.0 25.2 %all-to-all-start = ((bf16[8,2,9216]{2,1,0:T(2,128)(2,1)}), bf16[8,2,9216]{2,1,0:T(2,128)(2,1)S(1)}, u32[]{:S(2)}, u32[]{:S(2)}) async-start(bf16[8,2,9216]{2,1,0:T(2,128)(2,1)} %bitcast.10), calls=%async_computation | async-start | bytes 589824 | tf_op jit(solution)/shard_map/all_to_all | solution.py:290
  9.4 4.7 %collective-permute-start = (bf16[2,576]{1,0:T(2,128)(2,1)S(1)}, bf16[2,576]{1,0:T(2,128)(2,1)S(1)}, u32[]{:S(2)}, u32[]{:S(2)}) collective-permute-start(bf16[2,576]{1,0:T(2,128)(2,1)S(1)} %copy-done.3), channel_id=1, source_target_pairs={{0,2},{1,3},{2,0},{3,1},{4,6},{5,7},{6,4},{7,5},{8,10},{9,11},{10,... | collective-permute-start | bytes 6920 | tf_op jit(solution)/shard_map/ppermute | solution.py:298
  11.4 17.1 %collective-permute-start.6 = (bf16[576,254]{1,0:T(8,128)(2,1)S(1)}, bf16[576,254]{1,0:T(8,128)(2,1)S(1)}, u32[]{:S(2)}, u32[]{:S(2)}) collective-permute-start(bf16[576,254]{1,0:T(8,128)(2,1)S(1)} %collective-permute-done.4.rest_1_), channel_id=1, source_target_pairs={{2,6},{3,1},{6,10},{7,3},{10,14},{11,7},{14,12},{15,11},{12,8},{13... | collective-permute-start | bytes 877832 | tf_op jit(solution)/shard_map/ppermute | solution.py:302
  12.4 16.1 %collective-permute-start.7 = (bf16[576,254]{1,0:T(8,128)(2,1)S(1)}, bf16[576,254]{1,0:T(8,128)(2,1)S(1)}, u32[]{:S(2)}, u32[]{:S(2)}) collective-permute-start(bf16[576,254]{1,0:T(8,128)(2,1)S(1)} %collective-permute-done.5.rest_2_), channel_id=1, source_target_pairs={{2,0},{3,7},{6,2},{7,11},{10,6},{11,15},{14,10},{15,13},{12,14},{1... | collective-permute-start | bytes 877832 | tf_op jit(solution)/shard_map/ppermute | solution.py:302
  14.2 9.4 %collective-permute-start.1 = (bf16[4,576]{1,0:T(4,128)(2,1)S(1)}, bf16[4,576]{1,0:T(4,128)(2,1)S(1)}, u32[]{:S(2)}, u32[]{:S(2)}) collective-permute-start(bf16[4,576]{1,0:T(4,128)(2,1)S(1)} %pad_maximum_fusion.2), channel_id=1, source_target_pairs={{0,4},{1,5},{2,6},{3,7},{4,0},{5,1},{6,2},{7,3},{8,12},{9,13},{10,... | collective-permute-start | bytes 13832 | tf_op jit(solution)/shard_map/ppermute | solution.py:298
  23.6 4.6 %collective-permute-start.2 = (bf16[8,576]{1,0:T(8,128)(2,1)S(1)}, bf16[8,576]{1,0:T(8,128)(2,1)S(1)}, u32[]{:S(2)}, u32[]{:S(2)}) collective-permute-start(bf16[8,576]{1,0:T(8,128)(2,1)S(1)} %pad_maximum_fusion.1), channel_id=1, source_target_pairs={{0,8},{1,9},{2,10},{3,11},{4,12},{5,13},{6,14},{7,15},{8,0},{9,1},... | collective-permute-start | bytes 27656 | tf_op jit(solution)/shard_map/ppermute | solution.py:298
  28.2 3.0 %copy-start.1 = (bf16[254,576]{0,1:T(8,128)(2,1)S(1)}, bf16[254,576]{0,1:T(8,128)(2,1)}, u32[]{:S(2)}) copy-start(bf16[254,576]{0,1:T(8,128)(2,1)} %param.8) | copy-start | bytes 877828
  28.4 2.9 %copy-start.2 = (s32[128]{0:T(128)S(1)}, s32[128]{0:T(128)}, u32[]{:S(2)}) copy-start(s32[128]{0:T(128)} %constant.2.clone.table_ref) | copy-start | bytes 1540
  28.4 2.8 %collective-permute-start.3 = (bf16[16,9216]{1,0:T(8,128)(2,1)S(1)}, bf16[16,9216]{1,0:T(8,128)(2,1)S(1)}, u32[]{:S(2)}, u32[]{:S(2)}) collective-permute-start(bf16[16,9216]{1,0:T(8,128)(2,1)S(1)} %reshape.10.here_ref), channel_id=1, source_target_pairs={{0,1},{1,0},{2,3},{3,2},{4,5},{5,4},{6,7},{7,6},{8,9},{9,8},{10,11... | collective-permute-start | bytes 884744 | tf_op jit(solution)/shard_map/ppermute | solution.py:306
  28.5 9.5 %collective-permute-start.8 = (bf16[576,254]{1,0:T(8,128)(2,1)S(1)}, bf16[576,254]{1,0:T(8,128)(2,1)S(1)}, u32[]{:S(2)}, u32[]{:S(2)}) collective-permute-start(bf16[576,254]{1,0:T(8,128)(2,1)S(1)} %collective-permute-done.7.rest_4_), channel_id=1, source_target_pairs={{2,0},{3,7},{6,2},{7,11},{10,6},{11,15},{14,10},{15,13},{12,14},{1... | collective-permute-start | bytes 877832 | tf_op jit(solution)/shard_map/ppermute | solution.py:302
  28.6 9.5 %collective-permute-start.9 = (bf16[576,254]{1,0:T(8,128)(2,1)S(1)}, bf16[576,254]{1,0:T(8,128)(2,1)S(1)}, u32[]{:S(2)}, u32[]{:S(2)}) collective-permute-start(bf16[576,254]{1,0:T(8,128)(2,1)S(1)} %collective-permute-done.6.rest_3_), channel_id=1, source_target_pairs={{2,6},{3,1},{6,10},{7,3},{10,14},{11,7},{14,12},{15,11},{12,8},{13... | collective-permute-start | bytes 877832 | tf_op jit(solution)/shard_map/ppermute | solution.py:302
  38.0 5.6 %collective-permute-start.11 = (bf16[320,254]{1,0:T(8,128)(2,1)S(1)}, bf16[320,254]{1,0:T(8,128)(2,1)S(1)}, u32[]{:S(2)}, u32[]{:S(2)}) collective-permute-start(bf16[320,254]{1,0:T(8,128)(2,1)S(1)} %slice.7), channel_id=1, source_target_pairs={{2,0},{3,7},{6,2},{7,11},{10,6},{11,15},{14,10},{15,13},{12,14},{1... | collective-permute-start | bytes 487688 | tf_op jit(solution)/shard_map/ppermute | solution.py:317
  38.1 5.2 %collective-permute-start.10 = (bf16[256,254]{1,0:T(8,128)(2,1)S(1)}, bf16[256,254]{1,0:T(8,128)(2,1)S(1)}, u32[]{:S(2)}, u32[]{:S(2)}) collective-permute-start(bf16[256,254]{1,0:T(8,128)(2,1)S(1)} %slice.8), channel_id=1, source_target_pairs={{2,6},{3,1},{6,10},{7,3},{10,14},{11,7},{14,12},{15,11},{12,8},{13... | collective-permute-start | bytes 390152 | tf_op jit(solution)/shard_map/ppermute | solution.py:315
  44.8 1.7 %copy-start = (bf16[8,512,128]{2,1,0:T(8,128)(2,1)S(1)}, bf16[8,512,128]{2,1,0:T(8,128)(2,1)}, u32[]{:S(2)}) copy-start(bf16[8,512,128]{2,1,0:T(8,128)(2,1)} %up_ref.1) | copy-start | bytes 3145732
  44.8 1.7 %collective-permute-start.12 = (bf16[256,640]{1,0:T(8,128)(2,1)S(1)}, bf16[256,640]{1,0:T(8,128)(2,1)S(1)}, u32[]{:S(2)}, u32[]{:S(2)}) collective-permute-start(bf16[256,640]{1,0:T(8,128)(2,1)S(1)} %give.1), channel_id=1, source_target_pairs={{0,1},{1,0},{2,3},{3,2},{4,5},{5,4},{6,7},{7,6},{8,9},{9,8},{10,11... | collective-permute-start | bytes 983048 | tf_op jit(solution)/shard_map/ppermute | solution.py:339

commit v19 on v17

--- a/solution.py
+++ b/solution.py
@@ -120,7 +120,15 @@
     ]
 
 
-def pieces_kernel(queries_ref, span_ref, out_ref):
+def pieces_kernel(queries_hbm, span_hbm, out_ref, queries_ref, span_ref, sems):
+    copies = [
+        pltpu.make_async_copy(queries_hbm, queries_ref, sems.at[0]),
+        pltpu.make_async_copy(span_hbm, span_ref, sems.at[1]),
+    ]
+    for copy in copies:
+        copy.start()
+    for copy in copies:
+        copy.wait()
     chips = out_ref.shape[0]
     part = queries_ref.shape[1] // chips
     for chip in range(chips):
@@ -294,12 +302,18 @@
     own = prefix_latents.T
     right, left = onward(own), backward(own)
 
+    anywhere = pl.BlockSpec(memory_space=pl.ANY)
     pieces = pl.pallas_call(
         pieces_kernel,
         out_shape=shape(chips, tokens, (heads + 1) * width, dtype=bf16),
-        in_specs=[VMEM] * 2,
+        in_specs=[anywhere] * 2,
         out_specs=VMEM,
-        compiler_params=PARAMS,
+        scratch_shapes=[
+            pltpu.VMEM(queries.shape, bf16),
+            pltpu.VMEM(span_latents.shape, bf16),
+            pltpu.SemaphoreType.DMA((2,)),
+        ],
+        compiler_params=pltpu.CompilerParams(vmem_limit_bytes=56 * 1024 * 1024),
         name="pieces",
     )(queries, span_latents)
     here = lax.all_to_all(

time: 56.5 us -> 55.8 us (0.988)
  local copies, waits for them, and re-layouts: 2.54 us -> 0.9 us
  Pallas kernels: 9.7 us -> 10.7 us
    unnamed x11 -> x7, local copies, waits for them, and re-layouts: 2.29 us -> 0.65 us
    pallas_call x1, Pallas kernels: 0.74 us -> 1.71 us  [on_device(): pl.pallas_call(pieces_kernel, out_shape=shape(chips, tokens, (heads + 1)...]
  transfers between devices with their start and end apart: 11 -> 11, of which waited for: 5 -> 5; matrix products, arithmetic and copies ran while one was open for 0% -> 0% of each run, Pallas kernels for 14% -> 16%
where the time goes in v19:
time: 55.8 us; the launch traced here: 55.5 us
  starting transfers between devices  16.5 us (30%)
  waiting for transfers between devices  14.5 us (26%)
  blocking collectives  11.5 us (21%)
  Pallas kernels  10.7 us (19%)
  between operations  1.44 us (3%)
  local copies, waits for them, and re-layouts  0.9 us (2%)
    all_to_all x1, blocking collectives, on_device(): lax.all_to_all(merged, 'ctx', split_axis=0, concat_axis=0, tiled=True)  11.5 us
    all_to_all x1, waiting for transfers between devices, on_device(): lax.all_to_all(pieces, 'ctx', split_axis=0, concat_axis=0, axis_index_gro...  8.91 us
    all_to_all x1, starting transfers between devices, on_device(): lax.all_to_all(pieces, 'ctx', split_axis=0, concat_axis=0, axis_index_gro...  6.26 us
    ppermute x4, starting transfers between devices, on_device(): right, left = (onward(right), backward(left))  4.45 us
    ppermute x4, waiting for transfers between devices, on_device(): right, left = (onward(right), backward(left))  4.06 us
    pallas_call x1, Pallas kernels, fold_first(): pl.pallas_call(functools.partial(first_kernel, heads, len(keys)), out_sha...  3.65 us
    ppermute x2, starting transfers between devices, on_device(): right, left = (onward(own), backward(own))  3.03 us
    pallas_call x1, Pallas kernels, on_device(): pl.pallas_call(functools.partial(span_kernel, at, len(keys)), out_shape=s...  2.48 us
  transfers between devices with their start and end apart: 11, of which 5 were waited for; matrix products, arithmetic and copies ran while one was open for 0% of the time, Pallas kernels for 16%

profile of v19, /device:TPU:0, one launch (start us, length us, event | category | flops | bytes accessed | tf_op | source)
XLA Modules:
  0.0 55.5 jit_solution(14179660515414898496)
XLA Ops:
  0.0 2.9 %collective-permute-start.1 = (bf16[576,254]{1,0:T(8,128)(2,1)}, bf16[576,254]{1,0:T(8,128)(2,1)S(1)}, u32[]{:S(2)}, u32[]{:S(2)}) collective-permute-start(bf16[576,254]{1,0:T(8,128)(2,1)} %bitcast.4), channel_id=1, source_target_pairs={{2,6},{3,1},{6,10},{7,3},{10,14},{11,7},{14,12},{15,11},{12,8},{13... | collective-permute-start | bytes 877832 | tf_op jit(solution)/shard_map/ppermute | solution.py:303
  2.9 0.1 collective-permute-start.2
  3.0 1.7 %pieces.1 = bf16[8,2,9792]{2,1,0:T(2,128)(2,1)} custom-call(bf16[2,73728]{1,0:T(2,128)(2,1)} %queries_hbm.1, bf16[2,576]{1,0:T(2,128)(2,1)} %span_hbm.1), custom_call_target="tpu_custom_call" | custom-call | tf_op jit(solution)/shard_map/pieces/pallas_call | solution.py:306
  4.8 6.3 %all-to-all-start = ((bf16[8,2,9792]{2,1,0:T(2,128)(2,1)}), bf16[8,2,9792]{2,1,0:T(2,128)(2,1)S(1)}, u32[]{:S(2)}, u32[]{:S(2)}) async-start(bf16[8,2,9792]{2,1,0:T(2,128)(2,1)} %pieces.1), calls=%async_computation | async-start | bytes 630784 | tf_op jit(solution)/shard_map/all_to_all | solution.py:319
  11.0 0.0 copy-start.1
  11.0 0.0 collective-permute-done.1.rest_1_
  11.0 0.0 collective-permute-done.2.rest_2_
  11.0 2.1 %collective-permute-start.4 = (bf16[576,254]{1,0:T(8,128)(2,1)S(1)}, bf16[576,254]{1,0:T(8,128)(2,1)S(1)}, u32[]{:S(2)}, u32[]{:S(2)}) collective-permute-start(bf16[576,254]{1,0:T(8,128)(2,1)S(1)} %collective-permute-done.2.rest_2_), channel_id=1, source_target_pairs={{2,0},{3,7},{6,2},{7,11},{10,6},{11,15},{14,10},{15,13},{12,14},{1... | collective-permute-start | bytes 877832 | tf_op jit(solution)/shard_map/ppermute | solution.py:326
  13.1 0.1 collective-permute-start.3
  13.2 8.9 %all-to-all-done = bf16[8,2,9792]{2,1,0:T(2,128)(2,1)S(1)} async-done(((bf16[8,2,9792]{2,1,0:T(2,128)(2,1)}), bf16[8,2,9792]{2,1,0:T(2,128)(2,1)S(1)}, u32[]{:S(2)}, u32[]{:S(2)}) %all-to-all-start) | async-done | bytes 313376 | tf_op jit(solution)/shard_map/all_to_all | solution.py:319
  22.1 0.2 reshape.6.here_ref
  22.3 0.0 copy-start.2
  22.3 0.1 collective-permute-start
  22.4 1.0 %collective-permute-done.4.rest_4_ = bf16[576,254]{1,0:T(8,128)(2,1)S(1)} collective-permute-done((bf16[576,254]{1,0:T(8,128)(2,1)S(1)}, bf16[576,254]{1,0:T(8,128)(2,1)S(1)}, u32[]{:S(2)}, u32[]{:S(2)}) %collective-permute-start.4) | collective-permute-done | bytes 292640 | tf_op jit(solution)/shard_map/ppermute | solution.py:326
  23.4 1.7 %collective-permute-start.5 = (bf16[576,254]{1,0:T(8,128)(2,1)S(1)}, bf16[576,254]{1,0:T(8,128)(2,1)S(1)}, u32[]{:S(2)}, u32[]{:S(2)}) collective-permute-start(bf16[576,254]{1,0:T(8,128)(2,1)S(1)} %collective-permute-done.4.rest_4_), channel_id=1, source_target_pairs={{2,0},{3,7},{6,2},{7,11},{10,6},{11,15},{14,10},{15,13},{12,14},{1... | collective-permute-start | bytes 877832 | tf_op jit(solution)/shard_map/ppermute | solution.py:326
  25.2 0.0 collective-permute-done.3.rest_3_
  25.2 0.6 %collective-permute-start.6 = (bf16[576,254]{1,0:T(8,128)(2,1)S(1)}, bf16[576,254]{1,0:T(8,128)(2,1)S(1)}, u32[]{:S(2)}, u32[]{:S(2)}) collective-permute-start(bf16[576,254]{1,0:T(8,128)(2,1)S(1)} %collective-permute-done.3.rest_3_), channel_id=1, source_target_pairs={{2,6},{3,1},{6,10},{7,3},{10,14},{11,7},{14,12},{15,11},{12,8},{13... | collective-permute-start | bytes 877832 | tf_op jit(solution)/shard_map/ppermute | solution.py:326
  26.4 0.0 collective-permute-done.there_ref
  26.4 0.0 copy-done.1
  26.4 0.0 copy-done.2
  26.4 3.7 %first.1 = (bf16[512,576]{1,0:T(8,128)(2,1)S(1)}, f32[512,128]{1,0:T(8,128)S(1)}, f32[512,128]{1,0:T(8,128)S(1)}, f32[512,512]{1,0:T(8,128)S(1)}) custom-call(s32[1]{0:T(128)S(6)} %copy.9.length_ref, s32[128]{0:T(128)S(1)} %copy-done.2, bf16[16,9792]{1,0:T(8,128)(2,1)S(1)} %reshape.6.here_ref, bf16[16,9792]{1,0:T(8,128)(2,1)S(1)} %collective-permute-done.there_ref, ...), custom_call_target="tpu_custom_call" | custom-call | tf_op jit(solution)/shard_map/first/pallas_call | solution.py:280
  30.1 3.1 %collective-permute-done.5.rest_1_ = bf16[576,254]{1,0:T(8,128)(2,1)S(1)} collective-permute-done((bf16[576,254]{1,0:T(8,128)(2,1)S(1)}, bf16[576,254]{1,0:T(8,128)(2,1)S(1)}, u32[]{:S(2)}, u32[]{:S(2)}) %collective-permute-start.5) | collective-permute-done | bytes 292640 | tf_op jit(solution)/shard_map/ppermute | solution.py:326
  33.1 1.8 %collective-permute-start.8 = (bf16[320,254]{1,0:T(8,128)(2,1)S(1)}, bf16[320,254]{1,0:T(8,128)(2,1)S(1)}, u32[]{:S(2)}, u32[]{:S(2)}) collective-permute-start(bf16[320,254]{1,0:T(8,128)(2,1)S(1)} %slice.7), channel_id=1, source_target_pairs={{2,0},{3,7},{6,2},{7,11},{10,6},{11,15},{14,10},{15,13},{12,14},{1... | collective-permute-start | bytes 487688 | tf_op jit(solution)/shard_map/ppermute | solution.py:340
  34.9 0.0 collective-permute-done.6.rest_0_
  34.9 0.8 %collective-permute-start.7 = (bf16[256,254]{1,0:T(8,128)(2,1)S(1)}, bf16[256,254]{1,0:T(8,128)(2,1)S(1)}, u32[]{:S(2)}, u32[]{:S(2)}) collective-permute-start(bf16[256,254]{1,0:T(8,128)(2,1)S(1)} %slice.8), channel_id=1, source_target_pairs={{2,6},{3,1},{6,10},{7,3},{10,14},{11,7},{14,12},{15,11},{12,8},{13... | collective-permute-start | bytes 390152 | tf_op jit(solution)/shard_map/ppermute | solution.py:338
  36.4 2.5 %middle.1 = (f32[512,128]{1,0:T(8,128)S(1)}, f32[512,128]{1,0:T(8,128)S(1)}, f32[512,512]{1,0:T(8,128)S(1)}) custom-call(s32[1]{0:T(128)S(6)} %copy.9.length_ref, s32[1]{0:T(128)S(6)} %copy.10.offset_ref, s32[128]{0:T(128)S(1)} %copy-done.2, bf16[512,576]{1,0:T(8,128)(2,1)S(1)} %get-tuple-element.20.q_ref, f32[512,128]{1,0:T(8,128)S(1)} %get-tuple-element.24.m_in, ...), custom_call_target="tpu_custom_call" | custom-call | tf_op jit(solution)/shard_map/middle/pallas_call | solution.py:341
  38.9 1.1 %collective-permute-done.7.top_ref = bf16[256,254]{1,0:T(8,128)(2,1)S(1)} collective-permute-done((bf16[256,254]{1,0:T(8,128)(2,1)S(1)}, bf16[256,254]{1,0:T(8,128)(2,1)S(1)}, u32[]{:S(2)}, u32[]{:S(2)}) %collective-permute-start.7) | collective-permute-done | bytes 130080 | tf_op jit(solution)/shard_map/ppermute | solution.py:338
  40.0 0.0 collective-permute-done.8.bottom_ref
  40.0 1.2 %give.1 = bf16[256,640]{1,0:T(8,128)(2,1)S(1)} custom-call(s32[1]{0:T(128)S(6)} %copy.9.length_ref, s32[128]{0:T(128)S(1)} %copy-done.2, bf16[512,576]{1,0:T(8,128)(2,1)S(1)} %get-tuple-element.20.q_ref, f32[512,128]{1,0:T(8,128)S(1)} %get-tuple-element.27.m_ref, f32[512,128]{1,0:T(8,128)S(1)} %get-tuple-element.28.l_ref, ...), custom_call_target="tpu_custom_call" | custom-call | tf_op jit(solution)/shard_map/give/pallas_call | solution.py:353
  41.2 0.0 copy-start
  41.2 0.1 collective-permute-start.9
  41.3 1.2 %keep.1.keep_ref = f32[256,640]{1,0:T(8,128)S(1)} custom-call(s32[1]{0:T(128)S(6)} %copy.9.length_ref, s32[128]{0:T(128)S(1)} %copy-done.2, bf16[512,576]{1,0:T(8,128)(2,1)S(1)} %get-tuple-element.20.q_ref, f32[512,128]{1,0:T(8,128)S(1)} %get-tuple-element.27.m_ref, f32[512,128]{1,0:T(8,128)S(1)} %get-tuple-element.28.l_ref, ...), custom_call_target="tpu_custom_call" | custom-call | tf_op jit(solution)/shard_map/keep/pallas_call | solution.py:353
  42.4 0.4 collective-permute-done.9.got_ref
  42.9 0.0 copy-done
  42.9 0.5 merge.1
  43.4 11.5 %all_to_all.10 = bf16[16,2,1024]{2,1,0:T(2,128)(2,1)S(1)} all-to-all(bf16[16,2,1024]{2,1,0:T(2,128)(2,1)S(1)} %merge.1), channel_id=1, replica_groups=mesh['groups'=2,'ctx'=16] {'ctx'}, dimensions={0} | all-to-all | bytes 131072 | tf_op jit(solution)/shard_map/all_to_all | solution.py:373
  54.9 0.6 %copy.11 = bf16[2,16384]{1,0:T(2,128)(2,1)} copy(bf16[2,16384]{1,0:T(2,128)(2,1)S(1)} %bitcast.7) | data formatting | bytes 131072
  (2 shorter events, 0.0 us)
Async XLA Ops:
  0.0 11.0 %collective-permute-start.1 = (bf16[576,254]{1,0:T(8,128)(2,1)}, bf16[576,254]{1,0:T(8,128)(2,1)S(1)}, u32[]{:S(2)}, u32[]{:S(2)}) collective-permute-start(bf16[576,254]{1,0:T(8,128)(2,1)} %bitcast.4), channel_id=1, source_target_pairs={{2,6},{3,1},{6,10},{7,3},{10,14},{11,7},{14,12},{15,11},{12,8},{13... | collective-permute-start | bytes 877832 | tf_op jit(solution)/shard_map/ppermute | solution.py:303
  2.9 8.1 %collective-permute-start.2 = (bf16[576,254]{1,0:T(8,128)(2,1)}, bf16[576,254]{1,0:T(8,128)(2,1)S(1)}, u32[]{:S(2)}, u32[]{:S(2)}) collective-permute-start(bf16[576,254]{1,0:T(8,128)(2,1)} %bitcast.5), channel_id=1, source_target_pairs={{2,0},{3,7},{6,2},{7,11},{10,6},{11,15},{14,10},{15,13},{12,14},{1... | collective-permute-start | bytes 877832 | tf_op jit(solution)/shard_map/ppermute | solution.py:303
  4.8 17.3 %all-to-all-start = ((bf16[8,2,9792]{2,1,0:T(2,128)(2,1)}), bf16[8,2,9792]{2,1,0:T(2,128)(2,1)S(1)}, u32[]{:S(2)}, u32[]{:S(2)}) async-start(bf16[8,2,9792]{2,1,0:T(2,128)(2,1)} %pieces.1), calls=%async_computation | async-start | bytes 630784 | tf_op jit(solution)/shard_map/all_to_all | solution.py:319
  11.0 15.4 %copy-start.1 = (bf16[254,576]{0,1:T(8,128)(2,1)S(1)}, bf16[254,576]{0,1:T(8,128)(2,1)}, u32[]{:S(2)}) copy-start(bf16[254,576]{0,1:T(8,128)(2,1)} %param.8) | copy-start | bytes 877828
  11.0 12.4 %collective-permute-start.4 = (bf16[576,254]{1,0:T(8,128)(2,1)S(1)}, bf16[576,254]{1,0:T(8,128)(2,1)S(1)}, u32[]{:S(2)}, u32[]{:S(2)}) collective-permute-start(bf16[576,254]{1,0:T(8,128)(2,1)S(1)} %collective-permute-done.2.rest_2_), channel_id=1, source_target_pairs={{2,0},{3,7},{6,2},{7,11},{10,6},{11,15},{14,10},{15,13},{12,14},{1... | collective-permute-start | bytes 877832 | tf_op jit(solution)/shard_map/ppermute | solution.py:326
  13.1 12.0 %collective-permute-start.3 = (bf16[576,254]{1,0:T(8,128)(2,1)S(1)}, bf16[576,254]{1,0:T(8,128)(2,1)S(1)}, u32[]{:S(2)}, u32[]{:S(2)}) collective-permute-start(bf16[576,254]{1,0:T(8,128)(2,1)S(1)} %collective-permute-done.1.rest_1_), channel_id=1, source_target_pairs={{2,6},{3,1},{6,10},{7,3},{10,14},{11,7},{14,12},{15,11},{12,8},{13... | collective-permute-start | bytes 877832 | tf_op jit(solution)/shard_map/ppermute | solution.py:326
  22.3 4.1 %copy-start.2 = (s32[128]{0:T(128)S(1)}, s32[128]{0:T(128)}, u32[]{:S(2)}) copy-start(s32[128]{0:T(128)} %constant.2.clone.table_ref) | copy-start | bytes 1540
  22.3 4.1 %collective-permute-start = (bf16[16,9792]{1,0:T(8,128)(2,1)S(1)}, bf16[16,9792]{1,0:T(8,128)(2,1)S(1)}, u32[]{:S(2)}, u32[]{:S(2)}) collective-permute-start(bf16[16,9792]{1,0:T(8,128)(2,1)S(1)} %reshape.6.here_ref), channel_id=1, source_target_pairs={{0,1},{1,0},{2,3},{3,2},{4,5},{5,4},{6,7},{7,6},{8,9},{9,8},{10,11... | collective-permute-start | bytes 940040 | tf_op jit(solution)/shard_map/ppermute | solution.py:329
  23.4 9.7 %collective-permute-start.5 = (bf16[576,254]{1,0:T(8,128)(2,1)S(1)}, bf16[576,254]{1,0:T(8,128)(2,1)S(1)}, u32[]{:S(2)}, u32[]{:S(2)}) collective-permute-start(bf16[576,254]{1,0:T(8,128)(2,1)S(1)} %collective-permute-done.4.rest_4_), channel_id=1, source_target_pairs={{2,0},{3,7},{6,2},{7,11},{10,6},{11,15},{14,10},{15,13},{12,14},{1... | collective-permute-start | bytes 877832 | tf_op jit(solution)/shard_map/ppermute | solution.py:326
  25.2 9.8 %collective-permute-start.6 = (bf16[576,254]{1,0:T(8,128)(2,1)S(1)}, bf16[576,254]{1,0:T(8,128)(2,1)S(1)}, u32[]{:S(2)}, u32[]{:S(2)}) collective-permute-start(bf16[576,254]{1,0:T(8,128)(2,1)S(1)} %collective-permute-done.3.rest_3_), channel_id=1, source_target_pairs={{2,6},{3,1},{6,10},{7,3},{10,14},{11,7},{14,12},{15,11},{12,8},{13... | collective-permute-start | bytes 877832 | tf_op jit(solution)/shard_map/ppermute | solution.py:326
  33.1 6.8 %collective-permute-start.8 = (bf16[320,254]{1,0:T(8,128)(2,1)S(1)}, bf16[320,254]{1,0:T(8,128)(2,1)S(1)}, u32[]{:S(2)}, u32[]{:S(2)}) collective-permute-start(bf16[320,254]{1,0:T(8,128)(2,1)S(1)} %slice.7), channel_id=1, source_target_pairs={{2,0},{3,7},{6,2},{7,11},{10,6},{11,15},{14,10},{15,13},{12,14},{1... | collective-permute-start | bytes 487688 | tf_op jit(solution)/shard_map/ppermute | solution.py:340
  34.9 5.0 %collective-permute-start.7 = (bf16[256,254]{1,0:T(8,128)(2,1)S(1)}, bf16[256,254]{1,0:T(8,128)(2,1)S(1)}, u32[]{:S(2)}, u32[]{:S(2)}) collective-permute-start(bf16[256,254]{1,0:T(8,128)(2,1)S(1)} %slice.8), channel_id=1, source_target_pairs={{2,6},{3,1},{6,10},{7,3},{10,14},{11,7},{14,12},{15,11},{12,8},{13... | collective-permute-start | bytes 390152 | tf_op jit(solution)/shard_map/ppermute | solution.py:338
  41.2 1.7 %copy-start = (bf16[8,512,128]{2,1,0:T(8,128)(2,1)S(1)}, bf16[8,512,128]{2,1,0:T(8,128)(2,1)}, u32[]{:S(2)}) copy-start(bf16[8,512,128]{2,1,0:T(8,128)(2,1)} %up_ref.1) | copy-start | bytes 3145732
  41.2 1.7 %collective-permute-start.9 = (bf16[256,640]{1,0:T(8,128)(2,1)S(1)}, bf16[256,640]{1,0:T(8,128)(2,1)S(1)}, u32[]{:S(2)}, u32[]{:S(2)}) collective-permute-start(bf16[256,640]{1,0:T(8,128)(2,1)S(1)} %give.1), channel_id=1, source_target_pairs={{0,1},{1,0},{2,3},{3,2},{4,5},{5,4},{6,7},{7,6},{8,9},{9,8},{10,11... | collective-permute-start | bytes 983048 | tf_op jit(solution)/shard_map/ppermute | solution.py:362

commit v20 on v17

--- a/solution.py
+++ b/solution.py
@@ -120,12 +120,22 @@
     ]
 
 
-def pieces_kernel(queries_ref, span_ref, out_ref):
+def pieces_kernel(queries_hbm, span_hbm, out_ref, sems):
     chips = out_ref.shape[0]
-    part = queries_ref.shape[1] // chips
+    part = queries_hbm.shape[1] // chips
+    copies = []
     for chip in range(chips):
-        out_ref[chip, :, :part] = queries_ref[:, chip * part:(chip + 1) * part]
-        out_ref[chip, :, part:] = span_ref[...]
+        copies.append(pltpu.make_async_copy(
+            queries_hbm.at[:, chip * part:(chip + 1) * part],
+            out_ref.at[chip, :, :part], sems.at[2 * chip],
+        ))
+        copies.append(pltpu.make_async_copy(
+            span_hbm, out_ref.at[chip, :, part:], sems.at[2 * chip + 1],
+        ))
+    for copy in copies:
+        copy.start()
+    for copy in copies:
+        copy.wait()
 
 
 def first_kernel(heads, count, length_ref, table_ref, here_ref, there_ref, *rest):
@@ -294,12 +304,14 @@
     own = prefix_latents.T
     right, left = onward(own), backward(own)
 
+    anywhere = pl.BlockSpec(memory_space=pl.ANY)
     pieces = pl.pallas_call(
         pieces_kernel,
         out_shape=shape(chips, tokens, (heads + 1) * width, dtype=bf16),
-        in_specs=[VMEM] * 2,
+        in_specs=[anywhere] * 2,
         out_specs=VMEM,
-        compiler_params=PARAMS,
+        scratch_shapes=[pltpu.SemaphoreType.DMA((2 * chips,))],
+        compiler_params=pltpu.CompilerParams(vmem_limit_bytes=56 * 1024 * 1024),
         name="pieces",
     )(queries, span_latents)
     here = lax.all_to_all(

time: 56.5 us -> 56 us (level)
  local copies, waits for them, and re-layouts: 2.54 us -> 0.9 us
  Pallas kernels: 9.7 us -> 10.8 us
    unnamed x11 -> x7, local copies, waits for them, and re-layouts: 2.29 us -> 0.65 us
    pallas_call x1, Pallas kernels: 0.74 us -> 1.85 us  [on_device(): pl.pallas_call(pieces_kernel, out_shape=shape(chips, tokens, (heads + 1)...]
  transfers between devices with their start and end apart: 11 -> 11, of which waited for: 5 -> 5; matrix products, arithmetic and copies ran while one was open for 0% -> 0% of each run, Pallas kernels for 14% -> 16%
where the time goes in v20:
time: 56 us; the launch traced here: 55.6 us
  starting transfers between devices  16.5 us (29%)
  waiting for transfers between devices  14.5 us (26%)
  blocking collectives  11.5 us (21%)
  Pallas kernels  10.8 us (19%)
  between operations  1.44 us (3%)
  local copies, waits for them, and re-layouts  0.9 us (2%)
    all_to_all x1, blocking collectives, on_device(): lax.all_to_all(merged, 'ctx', split_axis=0, concat_axis=0, tiled=True)  11.5 us
    all_to_all x1, waiting for transfers between devices, on_device(): lax.all_to_all(pieces, 'ctx', split_axis=0, concat_axis=0, axis_index_gro...  8.91 us
    all_to_all x1, starting transfers between devices, on_device(): lax.all_to_all(pieces, 'ctx', split_axis=0, concat_axis=0, axis_index_gro...  6.26 us
    ppermute x4, starting transfers between devices, on_device(): right, left = (onward(right), backward(left))  4.45 us
    ppermute x4, waiting for transfers between devices, on_device(): right, left = (onward(right), backward(left))  4.06 us
    pallas_call x1, Pallas kernels, fold_first(): pl.pallas_call(functools.partial(first_kernel, heads, len(keys)), out_sha...  3.65 us
    ppermute x2, starting transfers between devices, on_device(): right, left = (onward(own), backward(own))  3.03 us
    pallas_call x1, Pallas kernels, on_device(): pl.pallas_call(functools.partial(span_kernel, at, len(keys)), out_shape=s...  2.46 us
  transfers between devices with their start and end apart: 11, of which 5 were waited for; matrix products, arithmetic and copies ran while one was open for 0% of the time, Pallas kernels for 16%

profile of v20, /device:TPU:0, one launch (start us, length us, event | category | flops | bytes accessed | tf_op | source)
XLA Modules:
  0.0 55.6 jit_solution(1149079146924705485)
XLA Ops:
  0.0 2.9 %collective-permute-start.1 = (bf16[576,254]{1,0:T(8,128)(2,1)}, bf16[576,254]{1,0:T(8,128)(2,1)S(1)}, u32[]{:S(2)}, u32[]{:S(2)}) collective-permute-start(bf16[576,254]{1,0:T(8,128)(2,1)} %bitcast.4), channel_id=1, source_target_pairs={{2,6},{3,1},{6,10},{7,3},{10,14},{11,7},{14,12},{15,11},{12,8},{13... | collective-permute-start | bytes 877832 | tf_op jit(solution)/shard_map/ppermute | solution.py:305
  2.9 0.1 collective-permute-start.2
  3.0 1.9 %pieces.1 = bf16[8,2,9792]{2,1,0:T(2,128)(2,1)} custom-call(bf16[2,73728]{1,0:T(2,128)(2,1)} %queries_hbm.1, bf16[2,576]{1,0:T(2,128)(2,1)} %span_hbm.1), custom_call_target="tpu_custom_call" | custom-call | tf_op jit(solution)/shard_map/pieces/pallas_call | solution.py:308
  4.9 6.3 %all-to-all-start = ((bf16[8,2,9792]{2,1,0:T(2,128)(2,1)}), bf16[8,2,9792]{2,1,0:T(2,128)(2,1)S(1)}, u32[]{:S(2)}, u32[]{:S(2)}) async-start(bf16[8,2,9792]{2,1,0:T(2,128)(2,1)} %pieces.1), calls=%async_computation | async-start | bytes 630784 | tf_op jit(solution)/shard_map/all_to_all | solution.py:317
  11.2 0.0 copy-start.1
  11.2 0.0 collective-permute-done.1.rest_1_
  11.2 0.0 collective-permute-done.2.rest_2_
  11.2 2.1 %collective-permute-start.4 = (bf16[576,254]{1,0:T(8,128)(2,1)S(1)}, bf16[576,254]{1,0:T(8,128)(2,1)S(1)}, u32[]{:S(2)}, u32[]{:S(2)}) collective-permute-start(bf16[576,254]{1,0:T(8,128)(2,1)S(1)} %collective-permute-done.2.rest_2_), channel_id=1, source_target_pairs={{2,0},{3,7},{6,2},{7,11},{10,6},{11,15},{14,10},{15,13},{12,14},{1... | collective-permute-start | bytes 877832 | tf_op jit(solution)/shard_map/ppermute | solution.py:324
  13.2 0.1 collective-permute-start.3
  13.3 8.9 %all-to-all-done = bf16[8,2,9792]{2,1,0:T(2,128)(2,1)S(1)} async-done(((bf16[8,2,9792]{2,1,0:T(2,128)(2,1)}), bf16[8,2,9792]{2,1,0:T(2,128)(2,1)S(1)}, u32[]{:S(2)}, u32[]{:S(2)}) %all-to-all-start) | async-done | bytes 313376 | tf_op jit(solution)/shard_map/all_to_all | solution.py:317
  22.2 0.2 reshape.6.here_ref
  22.4 0.0 copy-start.2
  22.5 0.1 collective-permute-start
  22.5 1.0 %collective-permute-done.4.rest_4_ = bf16[576,254]{1,0:T(8,128)(2,1)S(1)} collective-permute-done((bf16[576,254]{1,0:T(8,128)(2,1)S(1)}, bf16[576,254]{1,0:T(8,128)(2,1)S(1)}, u32[]{:S(2)}, u32[]{:S(2)}) %collective-permute-start.4) | collective-permute-done | bytes 292640 | tf_op jit(solution)/shard_map/ppermute | solution.py:324
  23.5 1.7 %collective-permute-start.5 = (bf16[576,254]{1,0:T(8,128)(2,1)S(1)}, bf16[576,254]{1,0:T(8,128)(2,1)S(1)}, u32[]{:S(2)}, u32[]{:S(2)}) collective-permute-start(bf16[576,254]{1,0:T(8,128)(2,1)S(1)} %collective-permute-done.4.rest_4_), channel_id=1, source_target_pairs={{2,0},{3,7},{6,2},{7,11},{10,6},{11,15},{14,10},{15,13},{12,14},{1... | collective-permute-start | bytes 877832 | tf_op jit(solution)/shard_map/ppermute | solution.py:324
  25.3 0.0 collective-permute-done.3.rest_3_
  25.3 0.6 %collective-permute-start.6 = (bf16[576,254]{1,0:T(8,128)(2,1)S(1)}, bf16[576,254]{1,0:T(8,128)(2,1)S(1)}, u32[]{:S(2)}, u32[]{:S(2)}) collective-permute-start(bf16[576,254]{1,0:T(8,128)(2,1)S(1)} %collective-permute-done.3.rest_3_), channel_id=1, source_target_pairs={{2,6},{3,1},{6,10},{7,3},{10,14},{11,7},{14,12},{15,11},{12,8},{13... | collective-permute-start | bytes 877832 | tf_op jit(solution)/shard_map/ppermute | solution.py:324
  26.5 0.0 collective-permute-done.there_ref
  26.5 0.0 copy-done.1
  26.5 0.0 copy-done.2
  26.5 3.7 %first.1 = (bf16[512,576]{1,0:T(8,128)(2,1)S(1)}, f32[512,128]{1,0:T(8,128)S(1)}, f32[512,128]{1,0:T(8,128)S(1)}, f32[512,512]{1,0:T(8,128)S(1)}) custom-call(s32[1]{0:T(128)S(6)} %copy.9.length_ref, s32[128]{0:T(128)S(1)} %copy-done.2, bf16[16,9792]{1,0:T(8,128)(2,1)S(1)} %reshape.6.here_ref, bf16[16,9792]{1,0:T(8,128)(2,1)S(1)} %collective-permute-done.there_ref, ...), custom_call_target="tpu_custom_call" | custom-call | tf_op jit(solution)/shard_map/first/pallas_call | solution.py:282
  30.2 3.1 %collective-permute-done.5.rest_1_ = bf16[576,254]{1,0:T(8,128)(2,1)S(1)} collective-permute-done((bf16[576,254]{1,0:T(8,128)(2,1)S(1)}, bf16[576,254]{1,0:T(8,128)(2,1)S(1)}, u32[]{:S(2)}, u32[]{:S(2)}) %collective-permute-start.5) | collective-permute-done | bytes 292640 | tf_op jit(solution)/shard_map/ppermute | solution.py:324
  33.3 1.8 %collective-permute-start.8 = (bf16[320,254]{1,0:T(8,128)(2,1)S(1)}, bf16[320,254]{1,0:T(8,128)(2,1)S(1)}, u32[]{:S(2)}, u32[]{:S(2)}) collective-permute-start(bf16[320,254]{1,0:T(8,128)(2,1)S(1)} %slice.7), channel_id=1, source_target_pairs={{2,0},{3,7},{6,2},{7,11},{10,6},{11,15},{14,10},{15,13},{12,14},{1... | collective-permute-start | bytes 487688 | tf_op jit(solution)/shard_map/ppermute | solution.py:338
  35.1 0.0 collective-permute-done.6.rest_0_
  35.1 0.8 %collective-permute-start.7 = (bf16[256,254]{1,0:T(8,128)(2,1)S(1)}, bf16[256,254]{1,0:T(8,128)(2,1)S(1)}, u32[]{:S(2)}, u32[]{:S(2)}) collective-permute-start(bf16[256,254]{1,0:T(8,128)(2,1)S(1)} %slice.8), channel_id=1, source_target_pairs={{2,6},{3,1},{6,10},{7,3},{10,14},{11,7},{14,12},{15,11},{12,8},{13... | collective-permute-start | bytes 390152 | tf_op jit(solution)/shard_map/ppermute | solution.py:336
  36.6 2.5 %middle.1 = (f32[512,128]{1,0:T(8,128)S(1)}, f32[512,128]{1,0:T(8,128)S(1)}, f32[512,512]{1,0:T(8,128)S(1)}) custom-call(s32[1]{0:T(128)S(6)} %copy.9.length_ref, s32[1]{0:T(128)S(6)} %copy.10.offset_ref, s32[128]{0:T(128)S(1)} %copy-done.2, bf16[512,576]{1,0:T(8,128)(2,1)S(1)} %get-tuple-element.20.q_ref, f32[512,128]{1,0:T(8,128)S(1)} %get-tuple-element.24.m_in, ...), custom_call_target="tpu_custom_call" | custom-call | tf_op jit(solution)/shard_map/middle/pallas_call | solution.py:339
  39.0 1.1 %collective-permute-done.7.top_ref = bf16[256,254]{1,0:T(8,128)(2,1)S(1)} collective-permute-done((bf16[256,254]{1,0:T(8,128)(2,1)S(1)}, bf16[256,254]{1,0:T(8,128)(2,1)S(1)}, u32[]{:S(2)}, u32[]{:S(2)}) %collective-permute-start.7) | collective-permute-done | bytes 130080 | tf_op jit(solution)/shard_map/ppermute | solution.py:336
  40.1 0.0 collective-permute-done.8.bottom_ref
  40.1 1.2 %give.1 = bf16[256,640]{1,0:T(8,128)(2,1)S(1)} custom-call(s32[1]{0:T(128)S(6)} %copy.9.length_ref, s32[128]{0:T(128)S(1)} %copy-done.2, bf16[512,576]{1,0:T(8,128)(2,1)S(1)} %get-tuple-element.20.q_ref, f32[512,128]{1,0:T(8,128)S(1)} %get-tuple-element.27.m_ref, f32[512,128]{1,0:T(8,128)S(1)} %get-tuple-element.28.l_ref, ...), custom_call_target="tpu_custom_call" | custom-call | tf_op jit(solution)/shard_map/give/pallas_call | solution.py:351
  41.3 0.0 copy-start
  41.3 0.1 collective-permute-start.9
  41.4 1.2 %keep.1.keep_ref = f32[256,640]{1,0:T(8,128)S(1)} custom-call(s32[1]{0:T(128)S(6)} %copy.9.length_ref, s32[128]{0:T(128)S(1)} %copy-done.2, bf16[512,576]{1,0:T(8,128)(2,1)S(1)} %get-tuple-element.20.q_ref, f32[512,128]{1,0:T(8,128)S(1)} %get-tuple-element.27.m_ref, f32[512,128]{1,0:T(8,128)S(1)} %get-tuple-element.28.l_ref, ...), custom_call_target="tpu_custom_call" | custom-call | tf_op jit(solution)/shard_map/keep/pallas_call | solution.py:351
  42.6 0.4 collective-permute-done.9.got_ref
  43.0 0.0 copy-done
  43.0 0.5 merge.1
  43.5 11.5 %all_to_all.10 = bf16[16,2,1024]{2,1,0:T(2,128)(2,1)S(1)} all-to-all(bf16[16,2,1024]{2,1,0:T(2,128)(2,1)S(1)} %merge.1), channel_id=1, replica_groups=mesh['groups'=2,'ctx'=16] {'ctx'}, dimensions={0} | all-to-all | bytes 131072 | tf_op jit(solution)/shard_map/all_to_all | solution.py:371
  55.0 0.6 %copy.11 = bf16[2,16384]{1,0:T(2,128)(2,1)} copy(bf16[2,16384]{1,0:T(2,128)(2,1)S(1)} %bitcast.7) | data formatting | bytes 131072
  (2 shorter events, 0.0 us)
Async XLA Ops:
  0.0 11.2 %collective-permute-start.1 = (bf16[576,254]{1,0:T(8,128)(2,1)}, bf16[576,254]{1,0:T(8,128)(2,1)S(1)}, u32[]{:S(2)}, u32[]{:S(2)}) collective-permute-start(bf16[576,254]{1,0:T(8,128)(2,1)} %bitcast.4), channel_id=1, source_target_pairs={{2,6},{3,1},{6,10},{7,3},{10,14},{11,7},{14,12},{15,11},{12,8},{13... | collective-permute-start | bytes 877832 | tf_op jit(solution)/shard_map/ppermute | solution.py:305
  2.9 8.2 %collective-permute-start.2 = (bf16[576,254]{1,0:T(8,128)(2,1)}, bf16[576,254]{1,0:T(8,128)(2,1)S(1)}, u32[]{:S(2)}, u32[]{:S(2)}) collective-permute-start(bf16[576,254]{1,0:T(8,128)(2,1)} %bitcast.5), channel_id=1, source_target_pairs={{2,0},{3,7},{6,2},{7,11},{10,6},{11,15},{14,10},{15,13},{12,14},{1... | collective-permute-start | bytes 877832 | tf_op jit(solution)/shard_map/ppermute | solution.py:305
  4.9 17.3 %all-to-all-start = ((bf16[8,2,9792]{2,1,0:T(2,128)(2,1)}), bf16[8,2,9792]{2,1,0:T(2,128)(2,1)S(1)}, u32[]{:S(2)}, u32[]{:S(2)}) async-start(bf16[8,2,9792]{2,1,0:T(2,128)(2,1)} %pieces.1), calls=%async_computation | async-start | bytes 630784 | tf_op jit(solution)/shard_map/all_to_all | solution.py:317
  11.2 15.4 %copy-start.1 = (bf16[254,576]{0,1:T(8,128)(2,1)S(1)}, bf16[254,576]{0,1:T(8,128)(2,1)}, u32[]{:S(2)}) copy-start(bf16[254,576]{0,1:T(8,128)(2,1)} %param.8) | copy-start | bytes 877828
  11.2 12.4 %collective-permute-start.4 = (bf16[576,254]{1,0:T(8,128)(2,1)S(1)}, bf16[576,254]{1,0:T(8,128)(2,1)S(1)}, u32[]{:S(2)}, u32[]{:S(2)}) collective-permute-start(bf16[576,254]{1,0:T(8,128)(2,1)S(1)} %collective-permute-done.2.rest_2_), channel_id=1, source_target_pairs={{2,0},{3,7},{6,2},{7,11},{10,6},{11,15},{14,10},{15,13},{12,14},{1... | collective-permute-start | bytes 877832 | tf_op jit(solution)/shard_map/ppermute | solution.py:324
  13.2 12.0 %collective-permute-start.3 = (bf16[576,254]{1,0:T(8,128)(2,1)S(1)}, bf16[576,254]{1,0:T(8,128)(2,1)S(1)}, u32[]{:S(2)}, u32[]{:S(2)}) collective-permute-start(bf16[576,254]{1,0:T(8,128)(2,1)S(1)} %collective-permute-done.1.rest_1_), channel_id=1, source_target_pairs={{2,6},{3,1},{6,10},{7,3},{10,14},{11,7},{14,12},{15,11},{12,8},{13... | collective-permute-start | bytes 877832 | tf_op jit(solution)/shard_map/ppermute | solution.py:324
  22.4 4.1 %copy-start.2 = (s32[128]{0:T(128)S(1)}, s32[128]{0:T(128)}, u32[]{:S(2)}) copy-start(s32[128]{0:T(128)} %constant.2.clone.table_ref) | copy-start | bytes 1540
  22.5 4.1 %collective-permute-start = (bf16[16,9792]{1,0:T(8,128)(2,1)S(1)}, bf16[16,9792]{1,0:T(8,128)(2,1)S(1)}, u32[]{:S(2)}, u32[]{:S(2)}) collective-permute-start(bf16[16,9792]{1,0:T(8,128)(2,1)S(1)} %reshape.6.here_ref), channel_id=1, source_target_pairs={{0,1},{1,0},{2,3},{3,2},{4,5},{5,4},{6,7},{7,6},{8,9},{9,8},{10,11... | collective-permute-start | bytes 940040 | tf_op jit(solution)/shard_map/ppermute | solution.py:327
  23.5 9.7 %collective-permute-start.5 = (bf16[576,254]{1,0:T(8,128)(2,1)S(1)}, bf16[576,254]{1,0:T(8,128)(2,1)S(1)}, u32[]{:S(2)}, u32[]{:S(2)}) collective-permute-start(bf16[576,254]{1,0:T(8,128)(2,1)S(1)} %collective-permute-done.4.rest_4_), channel_id=1, source_target_pairs={{2,0},{3,7},{6,2},{7,11},{10,6},{11,15},{14,10},{15,13},{12,14},{1... | collective-permute-start | bytes 877832 | tf_op jit(solution)/shard_map/ppermute | solution.py:324
  25.3 9.8 %collective-permute-start.6 = (bf16[576,254]{1,0:T(8,128)(2,1)S(1)}, bf16[576,254]{1,0:T(8,128)(2,1)S(1)}, u32[]{:S(2)}, u32[]{:S(2)}) collective-permute-start(bf16[576,254]{1,0:T(8,128)(2,1)S(1)} %collective-permute-done.3.rest_3_), channel_id=1, source_target_pairs={{2,6},{3,1},{6,10},{7,3},{10,14},{11,7},{14,12},{15,11},{12,8},{13... | collective-permute-start | bytes 877832 | tf_op jit(solution)/shard_map/ppermute | solution.py:324
  33.3 6.8 %collective-permute-start.8 = (bf16[320,254]{1,0:T(8,128)(2,1)S(1)}, bf16[320,254]{1,0:T(8,128)(2,1)S(1)}, u32[]{:S(2)}, u32[]{:S(2)}) collective-permute-start(bf16[320,254]{1,0:T(8,128)(2,1)S(1)} %slice.7), channel_id=1, source_target_pairs={{2,0},{3,7},{6,2},{7,11},{10,6},{11,15},{14,10},{15,13},{12,14},{1... | collective-permute-start | bytes 487688 | tf_op jit(solution)/shard_map/ppermute | solution.py:338
  35.1 5.0 %collective-permute-start.7 = (bf16[256,254]{1,0:T(8,128)(2,1)S(1)}, bf16[256,254]{1,0:T(8,128)(2,1)S(1)}, u32[]{:S(2)}, u32[]{:S(2)}) collective-permute-start(bf16[256,254]{1,0:T(8,128)(2,1)S(1)} %slice.8), channel_id=1, source_target_pairs={{2,6},{3,1},{6,10},{7,3},{10,14},{11,7},{14,12},{15,11},{12,8},{13... | collective-permute-start | bytes 390152 | tf_op jit(solution)/shard_map/ppermute | solution.py:336
  41.3 1.7 %copy-start = (bf16[8,512,128]{2,1,0:T(8,128)(2,1)S(1)}, bf16[8,512,128]{2,1,0:T(8,128)(2,1)}, u32[]{:S(2)}) copy-start(bf16[8,512,128]{2,1,0:T(8,128)(2,1)} %up_ref.1) | copy-start | bytes 3145732
  41.3 1.7 %collective-permute-start.9 = (bf16[256,640]{1,0:T(8,128)(2,1)S(1)}, bf16[256,640]{1,0:T(8,128)(2,1)S(1)}, u32[]{:S(2)}, u32[]{:S(2)}) collective-permute-start(bf16[256,640]{1,0:T(8,128)(2,1)S(1)} %give.1), channel_id=1, source_target_pairs={{0,1},{1,0},{2,3},{3,2},{4,5},{5,4},{6,7},{7,6},{8,9},{9,8},{10,11... | collective-permute-start | bytes 983048 | tf_op jit(solution)/shard_map/ppermute | solution.py:360

commit v21 on v19

--- a/solution.py
+++ b/solution.py
@@ -121,19 +121,23 @@
 
 
 def pieces_kernel(queries_hbm, span_hbm, out_ref, queries_ref, span_ref, sems):
-    copies = [
-        pltpu.make_async_copy(queries_hbm, queries_ref, sems.at[0]),
-        pltpu.make_async_copy(span_hbm, span_ref, sems.at[1]),
-    ]
-    for copy in copies:
-        copy.start()
-    for copy in copies:
-        copy.wait()
     chips = out_ref.shape[0]
     part = queries_ref.shape[1] // chips
-    for chip in range(chips):
-        out_ref[chip, :, :part] = queries_ref[:, chip * part:(chip + 1) * part]
-        out_ref[chip, :, part:] = span_ref[...]
+    span_copy = pltpu.make_async_copy(span_hbm, span_ref, sems.at[0])
+    span_copy.start()
+    copies = []
+    for i, first in enumerate((0, chips // 2)):
+        lanes = slice(first * part, (first + chips // 2) * part)
+        copies.append(pltpu.make_async_copy(
+            queries_hbm.at[:, lanes], queries_ref.at[:, lanes], sems.at[1 + i]
+        ))
+        copies[-1].start()
+    span_copy.wait()
+    for i, first in enumerate((0, chips // 2)):
+        copies[i].wait()
+        for chip in range(first, first + chips // 2):
+            out_ref[chip, :, :part] = queries_ref[:, chip * part:(chip + 1) * part]
+            out_ref[chip, :, part:] = span_ref[...]
 
 
 def first_kernel(heads, count, length_ref, table_ref, here_ref, there_ref, *rest):
@@ -179,18 +183,21 @@
     core = lax.axis_index("ctx") % CORES
     shards = [(with_base(table_ref, at, (top_ref,))[0][0], (top_ref, bottom_ref))]
     rows = out_ref.shape[0]
-    part = pl.ds(pl.multiple_of((core ^ side) * rows, rows), rows)
-    m_new, l_new, summed = fold_block(
-        part, q_ref, shards, length_ref[0], (m_ref, l_ref, acc_ref)
-    )
-    out_ref[:, :LATENT] = (summed * (1.0 / l_new)).astype(out_ref.dtype)
-    weight = jnp.broadcast_to(m_new + jnp.log2(l_new), (rows, LANES))
-    if side:
-        lane = lax.broadcasted_iota(jnp.int32, (rows, LANES), 1)
-        high = weight.astype(bf16).astype(f32)
-        mid = (weight - high).astype(bf16).astype(f32)
-        weight = jnp.where(lane == 0, high, jnp.where(lane == 1, mid, weight - high - mid))
-    out_ref[:, LATENT:] = weight.astype(out_ref.dtype)
+    block = min(128, rows)
+    for start in range(0, rows, block):
+        part = pl.ds(pl.multiple_of((core ^ side) * rows + start, block), block)
+        m_new, l_new, summed = fold_block(
+            part, q_ref, shards, length_ref[0], (m_ref, l_ref, acc_ref)
+        )
+        here = slice(start, start + block)
+        out_ref[here, :LATENT] = (summed * (1.0 / l_new)).astype(out_ref.dtype)
+        weight = jnp.broadcast_to(m_new + jnp.log2(l_new), (block, LANES))
+        if side:
+            lane = lax.broadcasted_iota(jnp.int32, (block, LANES), 1)
+            high = weight.astype(bf16).astype(f32)
+            mid = (weight - high).astype(bf16).astype(f32)
+            weight = jnp.where(lane == 0, high, jnp.where(lane == 1, mid, weight - high - mid))
+        out_ref[here, LATENT:] = weight.astype(out_ref.dtype)
 
 
 def merge_kernel(keep_ref, got_ref, up_ref, out_ref, flat_ref):
@@ -311,7 +318,7 @@
         scratch_shapes=[
             pltpu.VMEM(queries.shape, bf16),
             pltpu.VMEM(span_latents.shape, bf16),
-            pltpu.SemaphoreType.DMA((2,)),
+            pltpu.SemaphoreType.DMA((3,)),
         ],
         compiler_params=pltpu.CompilerParams(vmem_limit_bytes=56 * 1024 * 1024),
         name="pieces",

time: 55.8 us -> 56 us (level)
  transfers between devices with their start and end apart: 11 -> 11, of which waited for: 5 -> 5; matrix products, arithmetic and copies ran while one was open for 0% -> 0% of each run, Pallas kernels for 16% -> 17%
where the time goes in v21:
time: 56 us; the launch traced here: 55.7 us
  starting transfers between devices  16.5 us (29%)
  waiting for transfers between devices  14.2 us (25%)
  blocking collectives  11.5 us (21%)
  Pallas kernels  11.2 us (20%)
  between operations  1.44 us (3%)
  local copies, waits for them, and re-layouts  0.9 us (2%)
    all_to_all x1, blocking collectives, on_device(): lax.all_to_all(merged, 'ctx', split_axis=0, concat_axis=0, tiled=True)  11.5 us
    all_to_all x1, waiting for transfers between devices, on_device(): lax.all_to_all(pieces, 'ctx', split_axis=0, concat_axis=0, axis_index_gro...  8.91 us
    all_to_all x1, starting transfers between devices, on_device(): lax.all_to_all(pieces, 'ctx', split_axis=0, concat_axis=0, axis_index_gro...  6.26 us
    ppermute x4, starting transfers between devices, on_device(): right, left = (onward(right), backward(left))  4.45 us
    ppermute x4, waiting for transfers between devices, on_device(): right, left = (onward(right), backward(left))  4.06 us
    pallas_call x1, Pallas kernels, fold_first(): pl.pallas_call(functools.partial(first_kernel, heads, len(keys)), out_sha...  3.65 us
    ppermute x2, starting transfers between devices, on_device(): right, left = (onward(own), backward(own))  3.03 us
    pallas_call x2, Pallas kernels, fold_last(): pl.pallas_call(functools.partial(last_kernel, chips - 1, side), out_shape...  2.79 us
  transfers between devices with their start and end apart: 11, of which 5 were waited for; matrix products, arithmetic and copies ran while one was open for 0% of the time, Pallas kernels for 17%

profile of v21, /device:TPU:0, one launch (start us, length us, event | category | flops | bytes accessed | tf_op | source)
XLA Modules:
  0.0 55.7 jit_solution(10763047366057529112)
XLA Ops:
  0.0 2.9 %collective-permute-start.1 = (bf16[576,254]{1,0:T(8,128)(2,1)}, bf16[576,254]{1,0:T(8,128)(2,1)S(1)}, u32[]{:S(2)}, u32[]{:S(2)}) collective-permute-start(bf16[576,254]{1,0:T(8,128)(2,1)} %bitcast.4), channel_id=1, source_target_pairs={{2,6},{3,1},{6,10},{7,3},{10,14},{11,7},{14,12},{15,11},{12,8},{13... | collective-permute-start | bytes 877832 | tf_op jit(solution)/shard_map/ppermute | solution.py:310
  2.9 0.1 collective-permute-start.2
  3.0 1.7 %pieces.1 = bf16[8,2,9792]{2,1,0:T(2,128)(2,1)} custom-call(bf16[2,73728]{1,0:T(2,128)(2,1)} %queries_hbm.1, bf16[2,576]{1,0:T(2,128)(2,1)} %span_hbm.1), custom_call_target="tpu_custom_call" | custom-call | tf_op jit(solution)/shard_map/pieces/pallas_call | solution.py:313
  4.8 6.3 %all-to-all-start = ((bf16[8,2,9792]{2,1,0:T(2,128)(2,1)}), bf16[8,2,9792]{2,1,0:T(2,128)(2,1)S(1)}, u32[]{:S(2)}, u32[]{:S(2)}) async-start(bf16[8,2,9792]{2,1,0:T(2,128)(2,1)} %pieces.1), calls=%async_computation | async-start | bytes 630784 | tf_op jit(solution)/shard_map/all_to_all | solution.py:326
  11.0 0.0 copy-start.1
  11.0 0.0 collective-permute-done.1.rest_1_
  11.1 0.0 collective-permute-done.2.rest_2_
  11.1 2.1 %collective-permute-start.4 = (bf16[576,254]{1,0:T(8,128)(2,1)S(1)}, bf16[576,254]{1,0:T(8,128)(2,1)S(1)}, u32[]{:S(2)}, u32[]{:S(2)}) collective-permute-start(bf16[576,254]{1,0:T(8,128)(2,1)S(1)} %collective-permute-done.2.rest_2_), channel_id=1, source_target_pairs={{2,0},{3,7},{6,2},{7,11},{10,6},{11,15},{14,10},{15,13},{12,14},{1... | collective-permute-start | bytes 877832 | tf_op jit(solution)/shard_map/ppermute | solution.py:333
  13.1 0.1 collective-permute-start.3
  13.2 8.9 %all-to-all-done = bf16[8,2,9792]{2,1,0:T(2,128)(2,1)S(1)} async-done(((bf16[8,2,9792]{2,1,0:T(2,128)(2,1)}), bf16[8,2,9792]{2,1,0:T(2,128)(2,1)S(1)}, u32[]{:S(2)}, u32[]{:S(2)}) %all-to-all-start) | async-done | bytes 313376 | tf_op jit(solution)/shard_map/all_to_all | solution.py:326
  22.1 0.2 reshape.6.here_ref
  22.3 0.0 copy-start.2
  22.4 0.1 collective-permute-start
  22.4 1.0 %collective-permute-done.4.rest_4_ = bf16[576,254]{1,0:T(8,128)(2,1)S(1)} collective-permute-done((bf16[576,254]{1,0:T(8,128)(2,1)S(1)}, bf16[576,254]{1,0:T(8,128)(2,1)S(1)}, u32[]{:S(2)}, u32[]{:S(2)}) %collective-permute-start.4) | collective-permute-done | bytes 292640 | tf_op jit(solution)/shard_map/ppermute | solution.py:333
  23.4 1.7 %collective-permute-start.5 = (bf16[576,254]{1,0:T(8,128)(2,1)S(1)}, bf16[576,254]{1,0:T(8,128)(2,1)S(1)}, u32[]{:S(2)}, u32[]{:S(2)}) collective-permute-start(bf16[576,254]{1,0:T(8,128)(2,1)S(1)} %collective-permute-done.4.rest_4_), channel_id=1, source_target_pairs={{2,0},{3,7},{6,2},{7,11},{10,6},{11,15},{14,10},{15,13},{12,14},{1... | collective-permute-start | bytes 877832 | tf_op jit(solution)/shard_map/ppermute | solution.py:333
  25.2 0.0 collective-permute-done.3.rest_3_
  25.2 0.6 %collective-permute-start.6 = (bf16[576,254]{1,0:T(8,128)(2,1)S(1)}, bf16[576,254]{1,0:T(8,128)(2,1)S(1)}, u32[]{:S(2)}, u32[]{:S(2)}) collective-permute-start(bf16[576,254]{1,0:T(8,128)(2,1)S(1)} %collective-permute-done.3.rest_3_), channel_id=1, source_target_pairs={{2,6},{3,1},{6,10},{7,3},{10,14},{11,7},{14,12},{15,11},{12,8},{13... | collective-permute-start | bytes 877832 | tf_op jit(solution)/shard_map/ppermute | solution.py:333
  26.4 0.0 collective-permute-done.there_ref
  26.4 0.0 copy-done.1
  26.4 0.0 copy-done.2
  26.4 3.7 %first.1 = (bf16[512,576]{1,0:T(8,128)(2,1)S(1)}, f32[512,128]{1,0:T(8,128)S(1)}, f32[512,128]{1,0:T(8,128)S(1)}, f32[512,512]{1,0:T(8,128)S(1)}) custom-call(s32[1]{0:T(128)S(6)} %copy.9.length_ref, s32[128]{0:T(128)S(1)} %copy-done.2, bf16[16,9792]{1,0:T(8,128)(2,1)S(1)} %reshape.6.here_ref, bf16[16,9792]{1,0:T(8,128)(2,1)S(1)} %collective-permute-done.there_ref, ...), custom_call_target="tpu_custom_call" | custom-call | tf_op jit(solution)/shard_map/first/pallas_call | solution.py:287
  30.1 3.1 %collective-permute-done.5.rest_1_ = bf16[576,254]{1,0:T(8,128)(2,1)S(1)} collective-permute-done((bf16[576,254]{1,0:T(8,128)(2,1)S(1)}, bf16[576,254]{1,0:T(8,128)(2,1)S(1)}, u32[]{:S(2)}, u32[]{:S(2)}) %collective-permute-start.5) | collective-permute-done | bytes 292640 | tf_op jit(solution)/shard_map/ppermute | solution.py:333
  33.2 1.8 %collective-permute-start.8 = (bf16[320,254]{1,0:T(8,128)(2,1)S(1)}, bf16[320,254]{1,0:T(8,128)(2,1)S(1)}, u32[]{:S(2)}, u32[]{:S(2)}) collective-permute-start(bf16[320,254]{1,0:T(8,128)(2,1)S(1)} %slice.7), channel_id=1, source_target_pairs={{2,0},{3,7},{6,2},{7,11},{10,6},{11,15},{14,10},{15,13},{12,14},{1... | collective-permute-start | bytes 487688 | tf_op jit(solution)/shard_map/ppermute | solution.py:347
  35.0 0.0 collective-permute-done.6.rest_0_
  35.0 0.8 %collective-permute-start.7 = (bf16[256,254]{1,0:T(8,128)(2,1)S(1)}, bf16[256,254]{1,0:T(8,128)(2,1)S(1)}, u32[]{:S(2)}, u32[]{:S(2)}) collective-permute-start(bf16[256,254]{1,0:T(8,128)(2,1)S(1)} %slice.8), channel_id=1, source_target_pairs={{2,6},{3,1},{6,10},{7,3},{10,14},{11,7},{14,12},{15,11},{12,8},{13... | collective-permute-start | bytes 390152 | tf_op jit(solution)/shard_map/ppermute | solution.py:345
  36.4 2.5 %middle.1 = (f32[512,128]{1,0:T(8,128)S(1)}, f32[512,128]{1,0:T(8,128)S(1)}, f32[512,512]{1,0:T(8,128)S(1)}) custom-call(s32[1]{0:T(128)S(6)} %copy.9.length_ref, s32[1]{0:T(128)S(6)} %copy.10.offset_ref, s32[128]{0:T(128)S(1)} %copy-done.2, bf16[512,576]{1,0:T(8,128)(2,1)S(1)} %get-tuple-element.20.q_ref, f32[512,128]{1,0:T(8,128)S(1)} %get-tuple-element.24.m_in, ...), custom_call_target="tpu_custom_call" | custom-call | tf_op jit(solution)/shard_map/middle/pallas_call | solution.py:348
  38.9 1.1 %collective-permute-done.7.top_ref = bf16[256,254]{1,0:T(8,128)(2,1)S(1)} collective-permute-done((bf16[256,254]{1,0:T(8,128)(2,1)S(1)}, bf16[256,254]{1,0:T(8,128)(2,1)S(1)}, u32[]{:S(2)}, u32[]{:S(2)}) %collective-permute-start.7) | collective-permute-done | bytes 130080 | tf_op jit(solution)/shard_map/ppermute | solution.py:345
  40.0 0.0 collective-permute-done.8.bottom_ref
  40.0 1.4 %give.1 = bf16[256,640]{1,0:T(8,128)(2,1)S(1)} custom-call(s32[1]{0:T(128)S(6)} %copy.9.length_ref, s32[128]{0:T(128)S(1)} %copy-done.2, bf16[512,576]{1,0:T(8,128)(2,1)S(1)} %get-tuple-element.20.q_ref, f32[512,128]{1,0:T(8,128)S(1)} %get-tuple-element.27.m_ref, f32[512,128]{1,0:T(8,128)S(1)} %get-tuple-element.28.l_ref, ...), custom_call_target="tpu_custom_call" | custom-call | tf_op jit(solution)/shard_map/give/pallas_call | solution.py:360
  41.4 0.0 copy-start
  41.4 0.1 collective-permute-start.9
  41.5 1.4 %keep.1.keep_ref = f32[256,640]{1,0:T(8,128)S(1)} custom-call(s32[1]{0:T(128)S(6)} %copy.9.length_ref, s32[128]{0:T(128)S(1)} %copy-done.2, bf16[512,576]{1,0:T(8,128)(2,1)S(1)} %get-tuple-element.20.q_ref, f32[512,128]{1,0:T(8,128)S(1)} %get-tuple-element.27.m_ref, f32[512,128]{1,0:T(8,128)S(1)} %get-tuple-element.28.l_ref, ...), custom_call_target="tpu_custom_call" | custom-call | tf_op jit(solution)/shard_map/keep/pallas_call | solution.py:360
  42.9 0.2 collective-permute-done.9.got_ref
  43.1 0.0 copy-done
  43.1 0.5 merge.1
  43.6 11.5 %all_to_all.10 = bf16[16,2,1024]{2,1,0:T(2,128)(2,1)S(1)} all-to-all(bf16[16,2,1024]{2,1,0:T(2,128)(2,1)S(1)} %merge.1), channel_id=1, replica_groups=mesh['groups'=2,'ctx'=16] {'ctx'}, dimensions={0} | all-to-all | bytes 131072 | tf_op jit(solution)/shard_map/all_to_all | solution.py:380
  55.1 0.6 %copy.11 = bf16[2,16384]{1,0:T(2,128)(2,1)} copy(bf16[2,16384]{1,0:T(2,128)(2,1)S(1)} %bitcast.7) | data formatting | bytes 131072
  (2 shorter events, 0.0 us)
Async XLA Ops:
  0.0 11.1 %collective-permute-start.1 = (bf16[576,254]{1,0:T(8,128)(2,1)}, bf16[576,254]{1,0:T(8,128)(2,1)S(1)}, u32[]{:S(2)}, u32[]{:S(2)}) collective-permute-start(bf16[576,254]{1,0:T(8,128)(2,1)} %bitcast.4), channel_id=1, source_target_pairs={{2,6},{3,1},{6,10},{7,3},{10,14},{11,7},{14,12},{15,11},{12,8},{13... | collective-permute-start | bytes 877832 | tf_op jit(solution)/shard_map/ppermute | solution.py:310
  2.9 8.1 %collective-permute-start.2 = (bf16[576,254]{1,0:T(8,128)(2,1)}, bf16[576,254]{1,0:T(8,128)(2,1)S(1)}, u32[]{:S(2)}, u32[]{:S(2)}) collective-permute-start(bf16[576,254]{1,0:T(8,128)(2,1)} %bitcast.5), channel_id=1, source_target_pairs={{2,0},{3,7},{6,2},{7,11},{10,6},{11,15},{14,10},{15,13},{12,14},{1... | collective-permute-start | bytes 877832 | tf_op jit(solution)/shard_map/ppermute | solution.py:310
  4.8 17.3 %all-to-all-start = ((bf16[8,2,9792]{2,1,0:T(2,128)(2,1)}), bf16[8,2,9792]{2,1,0:T(2,128)(2,1)S(1)}, u32[]{:S(2)}, u32[]{:S(2)}) async-start(bf16[8,2,9792]{2,1,0:T(2,128)(2,1)} %pieces.1), calls=%async_computation | async-start | bytes 630784 | tf_op jit(solution)/shard_map/all_to_all | solution.py:326
  11.0 15.4 %copy-start.1 = (bf16[254,576]{0,1:T(8,128)(2,1)S(1)}, bf16[254,576]{0,1:T(8,128)(2,1)}, u32[]{:S(2)}) copy-start(bf16[254,576]{0,1:T(8,128)(2,1)} %param.8) | copy-start | bytes 877828
  11.1 12.4 %collective-permute-start.4 = (bf16[576,254]{1,0:T(8,128)(2,1)S(1)}, bf16[576,254]{1,0:T(8,128)(2,1)S(1)}, u32[]{:S(2)}, u32[]{:S(2)}) collective-permute-start(bf16[576,254]{1,0:T(8,128)(2,1)S(1)} %collective-permute-done.2.rest_2_), channel_id=1, source_target_pairs={{2,0},{3,7},{6,2},{7,11},{10,6},{11,15},{14,10},{15,13},{12,14},{1... | collective-permute-start | bytes 877832 | tf_op jit(solution)/shard_map/ppermute | solution.py:333
  13.1 12.0 %collective-permute-start.3 = (bf16[576,254]{1,0:T(8,128)(2,1)S(1)}, bf16[576,254]{1,0:T(8,128)(2,1)S(1)}, u32[]{:S(2)}, u32[]{:S(2)}) collective-permute-start(bf16[576,254]{1,0:T(8,128)(2,1)S(1)} %collective-permute-done.1.rest_1_), channel_id=1, source_target_pairs={{2,6},{3,1},{6,10},{7,3},{10,14},{11,7},{14,12},{15,11},{12,8},{13... | collective-permute-start | bytes 877832 | tf_op jit(solution)/shard_map/ppermute | solution.py:333
  22.3 4.1 %copy-start.2 = (s32[128]{0:T(128)S(1)}, s32[128]{0:T(128)}, u32[]{:S(2)}) copy-start(s32[128]{0:T(128)} %constant.2.clone.table_ref) | copy-start | bytes 1540
  22.4 4.1 %collective-permute-start = (bf16[16,9792]{1,0:T(8,128)(2,1)S(1)}, bf16[16,9792]{1,0:T(8,128)(2,1)S(1)}, u32[]{:S(2)}, u32[]{:S(2)}) collective-permute-start(bf16[16,9792]{1,0:T(8,128)(2,1)S(1)} %reshape.6.here_ref), channel_id=1, source_target_pairs={{0,1},{1,0},{2,3},{3,2},{4,5},{5,4},{6,7},{7,6},{8,9},{9,8},{10,11... | collective-permute-start | bytes 940040 | tf_op jit(solution)/shard_map/ppermute | solution.py:336
  23.4 9.7 %collective-permute-start.5 = (bf16[576,254]{1,0:T(8,128)(2,1)S(1)}, bf16[576,254]{1,0:T(8,128)(2,1)S(1)}, u32[]{:S(2)}, u32[]{:S(2)}) collective-permute-start(bf16[576,254]{1,0:T(8,128)(2,1)S(1)} %collective-permute-done.4.rest_4_), channel_id=1, source_target_pairs={{2,0},{3,7},{6,2},{7,11},{10,6},{11,15},{14,10},{15,13},{12,14},{1... | collective-permute-start | bytes 877832 | tf_op jit(solution)/shard_map/ppermute | solution.py:333
  25.2 9.8 %collective-permute-start.6 = (bf16[576,254]{1,0:T(8,128)(2,1)S(1)}, bf16[576,254]{1,0:T(8,128)(2,1)S(1)}, u32[]{:S(2)}, u32[]{:S(2)}) collective-permute-start(bf16[576,254]{1,0:T(8,128)(2,1)S(1)} %collective-permute-done.3.rest_3_), channel_id=1, source_target_pairs={{2,6},{3,1},{6,10},{7,3},{10,14},{11,7},{14,12},{15,11},{12,8},{13... | collective-permute-start | bytes 877832 | tf_op jit(solution)/shard_map/ppermute | solution.py:333
  33.2 6.8 %collective-permute-start.8 = (bf16[320,254]{1,0:T(8,128)(2,1)S(1)}, bf16[320,254]{1,0:T(8,128)(2,1)S(1)}, u32[]{:S(2)}, u32[]{:S(2)}) collective-permute-start(bf16[320,254]{1,0:T(8,128)(2,1)S(1)} %slice.7), channel_id=1, source_target_pairs={{2,0},{3,7},{6,2},{7,11},{10,6},{11,15},{14,10},{15,13},{12,14},{1... | collective-permute-start | bytes 487688 | tf_op jit(solution)/shard_map/ppermute | solution.py:347
  35.0 5.0 %collective-permute-start.7 = (bf16[256,254]{1,0:T(8,128)(2,1)S(1)}, bf16[256,254]{1,0:T(8,128)(2,1)S(1)}, u32[]{:S(2)}, u32[]{:S(2)}) collective-permute-start(bf16[256,254]{1,0:T(8,128)(2,1)S(1)} %slice.8), channel_id=1, source_target_pairs={{2,6},{3,1},{6,10},{7,3},{10,14},{11,7},{14,12},{15,11},{12,8},{13... | collective-permute-start | bytes 390152 | tf_op jit(solution)/shard_map/ppermute | solution.py:345
  41.4 1.7 %copy-start = (bf16[8,512,128]{2,1,0:T(8,128)(2,1)S(1)}, bf16[8,512,128]{2,1,0:T(8,128)(2,1)}, u32[]{:S(2)}) copy-start(bf16[8,512,128]{2,1,0:T(8,128)(2,1)} %up_ref.1) | copy-start | bytes 3145732
  41.4 1.7 %collective-permute-start.9 = (bf16[256,640]{1,0:T(8,128)(2,1)S(1)}, bf16[256,640]{1,0:T(8,128)(2,1)S(1)}, u32[]{:S(2)}, u32[]{:S(2)}) collective-permute-start(bf16[256,640]{1,0:T(8,128)(2,1)S(1)} %give.1), channel_id=1, source_target_pairs={{0,1},{1,0},{2,3},{3,2},{4,5},{5,4},{6,7},{7,6},{8,9},{9,8},{10,11... | collective-permute-start | bytes 983048 | tf_op jit(solution)/shard_map/ppermute | solution.py:369

commit v22 on v19

--- a/solution.py
+++ b/solution.py
@@ -120,19 +120,17 @@
     ]
 
 
-def pieces_kernel(queries_hbm, span_hbm, out_ref, queries_ref, span_ref, sems):
+def pieces_kernel(queries_hbm, span_hbm, out_ref, span_ref, sems):
+    part = queries_hbm.shape[2]
     copies = [
-        pltpu.make_async_copy(queries_hbm, queries_ref, sems.at[0]),
+        pltpu.make_async_copy(queries_hbm, out_ref.at[:, :, :part], sems.at[0]),
         pltpu.make_async_copy(span_hbm, span_ref, sems.at[1]),
     ]
     for copy in copies:
         copy.start()
     for copy in copies:
         copy.wait()
-    chips = out_ref.shape[0]
-    part = queries_ref.shape[1] // chips
-    for chip in range(chips):
-        out_ref[chip, :, :part] = queries_ref[:, chip * part:(chip + 1) * part]
+    for chip in range(out_ref.shape[0]):
         out_ref[chip, :, part:] = span_ref[...]
 
 
@@ -309,13 +307,12 @@
         in_specs=[anywhere] * 2,
         out_specs=VMEM,
         scratch_shapes=[
-            pltpu.VMEM(queries.shape, bf16),
             pltpu.VMEM(span_latents.shape, bf16),
             pltpu.SemaphoreType.DMA((2,)),
         ],
         compiler_params=pltpu.CompilerParams(vmem_limit_bytes=56 * 1024 * 1024),
         name="pieces",
-    )(queries, span_latents)
+    )(queries.reshape(tokens, chips, heads * width).transpose(1, 0, 2), span_latents)
     here = lax.all_to_all(
         pieces, "ctx", split_axis=0, concat_axis=0, axis_index_groups=same_core, tiled=True
     )

time: 55.8 us -> 55.7 us (level)
  no operation moved by 1% of the time
where the time goes in v22:
time: 55.7 us; the launch traced here: 55.5 us
  starting transfers between devices  16.5 us (30%)
  waiting for transfers between devices  14.5 us (26%)
  blocking collectives  11.5 us (21%)
  Pallas kernels  10.7 us (19%)
  between operations  1.44 us (3%)
  local copies, waits for them, and re-layouts  0.9 us (2%)
    all_to_all x1, blocking collectives, on_device(): lax.all_to_all(merged, 'ctx', split_axis=0, concat_axis=0, tiled=True)  11.5 us
    all_to_all x1, waiting for transfers between devices, on_device(): lax.all_to_all(pieces, 'ctx', split_axis=0, concat_axis=0, axis_index_gro...  8.91 us
    all_to_all x1, starting transfers between devices, on_device(): lax.all_to_all(pieces, 'ctx', split_axis=0, concat_axis=0, axis_index_gro...  6.26 us
    ppermute x4, starting transfers between devices, on_device(): right, left = (onward(right), backward(left))  4.45 us
    ppermute x4, waiting for transfers between devices, on_device(): right, left = (onward(right), backward(left))  4.06 us
    pallas_call x1, Pallas kernels, fold_first(): pl.pallas_call(functools.partial(first_kernel, heads, len(keys)), out_sha...  3.65 us
    ppermute x2, starting transfers between devices, on_device(): right, left = (onward(own), backward(own))  3.03 us
    pallas_call x1, Pallas kernels, on_device(): pl.pallas_call(functools.partial(span_kernel, at, len(keys)), out_shape=s...  2.47 us
  transfers between devices with their start and end apart: 11, of which 5 were waited for; matrix products, arithmetic and copies ran while one was open for 0% of the time, Pallas kernels for 16%

profile of v22, /device:TPU:0, one launch (start us, length us, event | category | flops | bytes accessed | tf_op | source)
XLA Modules:
  0.0 55.5 jit_solution(1959509750969614449)
XLA Ops:
  0.0 2.9 %collective-permute-start.1 = (bf16[576,254]{1,0:T(8,128)(2,1)}, bf16[576,254]{1,0:T(8,128)(2,1)S(1)}, u32[]{:S(2)}, u32[]{:S(2)}) collective-permute-start(bf16[576,254]{1,0:T(8,128)(2,1)} %bitcast.7), channel_id=1, source_target_pairs={{2,6},{3,1},{6,10},{7,3},{10,14},{11,7},{14,12},{15,11},{12,8},{13... | collective-permute-start | bytes 877832 | tf_op jit(solution)/shard_map/ppermute | solution.py:301
  2.9 0.1 collective-permute-start.2
  3.0 1.7 %pieces.1 = bf16[8,2,9792]{2,1,0:T(2,128)(2,1)} custom-call(bf16[8,2,9216]{2,1,0:T(2,128)(2,1)} %bitcast.10, bf16[2,576]{1,0:T(2,128)(2,1)} %span_hbm.1), custom_call_target="tpu_custom_call" | custom-call | tf_op jit(solution)/shard_map/pieces/pallas_call | solution.py:304
  4.7 6.3 %all-to-all-start = ((bf16[8,2,9792]{2,1,0:T(2,128)(2,1)}), bf16[8,2,9792]{2,1,0:T(2,128)(2,1)S(1)}, u32[]{:S(2)}, u32[]{:S(2)}) async-start(bf16[8,2,9792]{2,1,0:T(2,128)(2,1)} %pieces.1), calls=%async_computation | async-start | bytes 630784 | tf_op jit(solution)/shard_map/all_to_all | solution.py:316
  11.0 0.0 copy-start.1
  11.0 0.0 collective-permute-done.1.rest_1_
  11.0 0.0 collective-permute-done.2.rest_2_
  11.0 2.1 %collective-permute-start.4 = (bf16[576,254]{1,0:T(8,128)(2,1)S(1)}, bf16[576,254]{1,0:T(8,128)(2,1)S(1)}, u32[]{:S(2)}, u32[]{:S(2)}) collective-permute-start(bf16[576,254]{1,0:T(8,128)(2,1)S(1)} %collective-permute-done.2.rest_2_), channel_id=1, source_target_pairs={{2,0},{3,7},{6,2},{7,11},{10,6},{11,15},{14,10},{15,13},{12,14},{1... | collective-permute-start | bytes 877832 | tf_op jit(solution)/shard_map/ppermute | solution.py:323
  13.1 0.1 collective-permute-start.3
  13.2 8.9 %all-to-all-done = bf16[8,2,9792]{2,1,0:T(2,128)(2,1)S(1)} async-done(((bf16[8,2,9792]{2,1,0:T(2,128)(2,1)}), bf16[8,2,9792]{2,1,0:T(2,128)(2,1)S(1)}, u32[]{:S(2)}, u32[]{:S(2)}) %all-to-all-start) | async-done | bytes 313376 | tf_op jit(solution)/shard_map/all_to_all | solution.py:316
  22.1 0.2 reshape.10.here_ref
  22.3 0.0 copy-start.2
  22.3 0.1 collective-permute-start
  22.4 1.0 %collective-permute-done.4.rest_4_ = bf16[576,254]{1,0:T(8,128)(2,1)S(1)} collective-permute-done((bf16[576,254]{1,0:T(8,128)(2,1)S(1)}, bf16[576,254]{1,0:T(8,128)(2,1)S(1)}, u32[]{:S(2)}, u32[]{:S(2)}) %collective-permute-start.4) | collective-permute-done | bytes 292640 | tf_op jit(solution)/shard_map/ppermute | solution.py:323
  23.4 1.7 %collective-permute-start.5 = (bf16[576,254]{1,0:T(8,128)(2,1)S(1)}, bf16[576,254]{1,0:T(8,128)(2,1)S(1)}, u32[]{:S(2)}, u32[]{:S(2)}) collective-permute-start(bf16[576,254]{1,0:T(8,128)(2,1)S(1)} %collective-permute-done.4.rest_4_), channel_id=1, source_target_pairs={{2,0},{3,7},{6,2},{7,11},{10,6},{11,15},{14,10},{15,13},{12,14},{1... | collective-permute-start | bytes 877832 | tf_op jit(solution)/shard_map/ppermute | solution.py:323
  25.1 0.0 collective-permute-done.3.rest_3_
  25.1 0.6 %collective-permute-start.6 = (bf16[576,254]{1,0:T(8,128)(2,1)S(1)}, bf16[576,254]{1,0:T(8,128)(2,1)S(1)}, u32[]{:S(2)}, u32[]{:S(2)}) collective-permute-start(bf16[576,254]{1,0:T(8,128)(2,1)S(1)} %collective-permute-done.3.rest_3_), channel_id=1, source_target_pairs={{2,6},{3,1},{6,10},{7,3},{10,14},{11,7},{14,12},{15,11},{12,8},{13... | collective-permute-start | bytes 877832 | tf_op jit(solution)/shard_map/ppermute | solution.py:323
  26.4 0.0 collective-permute-done.there_ref
  26.4 0.0 copy-done.1
  26.4 0.0 copy-done.2
  26.4 3.7 %first.1 = (bf16[512,576]{1,0:T(8,128)(2,1)S(1)}, f32[512,128]{1,0:T(8,128)S(1)}, f32[512,128]{1,0:T(8,128)S(1)}, f32[512,512]{1,0:T(8,128)S(1)}) custom-call(s32[1]{0:T(128)S(6)} %copy.9.length_ref, s32[128]{0:T(128)S(1)} %copy-done.2, bf16[16,9792]{1,0:T(8,128)(2,1)S(1)} %reshape.10.here_ref, bf16[16,9792]{1,0:T(8,128)(2,1)S(1)} %collective-permute-done.there_ref, ...), custom_call_target="tpu_custom_call" | custom-call | tf_op jit(solution)/shard_map/first/pallas_call | solution.py:278
  30.0 3.1 %collective-permute-done.5.rest_1_ = bf16[576,254]{1,0:T(8,128)(2,1)S(1)} collective-permute-done((bf16[576,254]{1,0:T(8,128)(2,1)S(1)}, bf16[576,254]{1,0:T(8,128)(2,1)S(1)}, u32[]{:S(2)}, u32[]{:S(2)}) %collective-permute-start.5) | collective-permute-done | bytes 292640 | tf_op jit(solution)/shard_map/ppermute | solution.py:323
  33.1 1.8 %collective-permute-start.8 = (bf16[320,254]{1,0:T(8,128)(2,1)S(1)}, bf16[320,254]{1,0:T(8,128)(2,1)S(1)}, u32[]{:S(2)}, u32[]{:S(2)}) collective-permute-start(bf16[320,254]{1,0:T(8,128)(2,1)S(1)} %slice.7), channel_id=1, source_target_pairs={{2,0},{3,7},{6,2},{7,11},{10,6},{11,15},{14,10},{15,13},{12,14},{1... | collective-permute-start | bytes 487688 | tf_op jit(solution)/shard_map/ppermute | solution.py:337
  34.9 0.0 collective-permute-done.6.rest_0_
  34.9 0.8 %collective-permute-start.7 = (bf16[256,254]{1,0:T(8,128)(2,1)S(1)}, bf16[256,254]{1,0:T(8,128)(2,1)S(1)}, u32[]{:S(2)}, u32[]{:S(2)}) collective-permute-start(bf16[256,254]{1,0:T(8,128)(2,1)S(1)} %slice.8), channel_id=1, source_target_pairs={{2,6},{3,1},{6,10},{7,3},{10,14},{11,7},{14,12},{15,11},{12,8},{13... | collective-permute-start | bytes 390152 | tf_op jit(solution)/shard_map/ppermute | solution.py:335
  36.4 2.5 %middle.1 = (f32[512,128]{1,0:T(8,128)S(1)}, f32[512,128]{1,0:T(8,128)S(1)}, f32[512,512]{1,0:T(8,128)S(1)}) custom-call(s32[1]{0:T(128)S(6)} %copy.9.length_ref, s32[1]{0:T(128)S(6)} %copy.10.offset_ref, s32[128]{0:T(128)S(1)} %copy-done.2, bf16[512,576]{1,0:T(8,128)(2,1)S(1)} %get-tuple-element.20.q_ref, f32[512,128]{1,0:T(8,128)S(1)} %get-tuple-element.24.m_in, ...), custom_call_target="tpu_custom_call" | custom-call | tf_op jit(solution)/shard_map/middle/pallas_call | solution.py:338
  38.9 1.1 %collective-permute-done.7.top_ref = bf16[256,254]{1,0:T(8,128)(2,1)S(1)} collective-permute-done((bf16[256,254]{1,0:T(8,128)(2,1)S(1)}, bf16[256,254]{1,0:T(8,128)(2,1)S(1)}, u32[]{:S(2)}, u32[]{:S(2)}) %collective-permute-start.7) | collective-permute-done | bytes 130080 | tf_op jit(solution)/shard_map/ppermute | solution.py:335
  39.9 0.0 collective-permute-done.8.bottom_ref
  39.9 1.2 %give.1 = bf16[256,640]{1,0:T(8,128)(2,1)S(1)} custom-call(s32[1]{0:T(128)S(6)} %copy.9.length_ref, s32[128]{0:T(128)S(1)} %copy-done.2, bf16[512,576]{1,0:T(8,128)(2,1)S(1)} %get-tuple-element.20.q_ref, f32[512,128]{1,0:T(8,128)S(1)} %get-tuple-element.27.m_ref, f32[512,128]{1,0:T(8,128)S(1)} %get-tuple-element.28.l_ref, ...), custom_call_target="tpu_custom_call" | custom-call | tf_op jit(solution)/shard_map/give/pallas_call | solution.py:350
  41.2 0.0 copy-start
  41.2 0.1 collective-permute-start.9
  41.2 1.2 %keep.1.keep_ref = f32[256,640]{1,0:T(8,128)S(1)} custom-call(s32[1]{0:T(128)S(6)} %copy.9.length_ref, s32[128]{0:T(128)S(1)} %copy-done.2, bf16[512,576]{1,0:T(8,128)(2,1)S(1)} %get-tuple-element.20.q_ref, f32[512,128]{1,0:T(8,128)S(1)} %get-tuple-element.27.m_ref, f32[512,128]{1,0:T(8,128)S(1)} %get-tuple-element.28.l_ref, ...), custom_call_target="tpu_custom_call" | custom-call | tf_op jit(solution)/shard_map/keep/pallas_call | solution.py:350
  42.4 0.4 collective-permute-done.9.got_ref
  42.9 0.0 copy-done
  42.9 0.5 merge.1
  43.4 11.5 %all_to_all.10 = bf16[16,2,1024]{2,1,0:T(2,128)(2,1)S(1)} all-to-all(bf16[16,2,1024]{2,1,0:T(2,128)(2,1)S(1)} %merge.1), channel_id=1, replica_groups=mesh['groups'=2,'ctx'=16] {'ctx'}, dimensions={0} | all-to-all | bytes 131072 | tf_op jit(solution)/shard_map/all_to_all | solution.py:370
  54.8 0.6 %copy.11 = bf16[2,16384]{1,0:T(2,128)(2,1)} copy(bf16[2,16384]{1,0:T(2,128)(2,1)S(1)} %bitcast.11) | data formatting | bytes 131072
  (2 shorter events, 0.0 us)
Async XLA Ops:
  0.0 11.0 %collective-permute-start.1 = (bf16[576,254]{1,0:T(8,128)(2,1)}, bf16[576,254]{1,0:T(8,128)(2,1)S(1)}, u32[]{:S(2)}, u32[]{:S(2)}) collective-permute-start(bf16[576,254]{1,0:T(8,128)(2,1)} %bitcast.7), channel_id=1, source_target_pairs={{2,6},{3,1},{6,10},{7,3},{10,14},{11,7},{14,12},{15,11},{12,8},{13... | collective-permute-start | bytes 877832 | tf_op jit(solution)/shard_map/ppermute | solution.py:301
  2.9 8.1 %collective-permute-start.2 = (bf16[576,254]{1,0:T(8,128)(2,1)}, bf16[576,254]{1,0:T(8,128)(2,1)S(1)}, u32[]{:S(2)}, u32[]{:S(2)}) collective-permute-start(bf16[576,254]{1,0:T(8,128)(2,1)} %bitcast.8), channel_id=1, source_target_pairs={{2,0},{3,7},{6,2},{7,11},{10,6},{11,15},{14,10},{15,13},{12,14},{1... | collective-permute-start | bytes 877832 | tf_op jit(solution)/shard_map/ppermute | solution.py:301
  4.7 17.3 %all-to-all-start = ((bf16[8,2,9792]{2,1,0:T(2,128)(2,1)}), bf16[8,2,9792]{2,1,0:T(2,128)(2,1)S(1)}, u32[]{:S(2)}, u32[]{:S(2)}) async-start(bf16[8,2,9792]{2,1,0:T(2,128)(2,1)} %pieces.1), calls=%async_computation | async-start | bytes 630784 | tf_op jit(solution)/shard_map/all_to_all | solution.py:316
  11.0 15.4 %copy-start.1 = (bf16[254,576]{0,1:T(8,128)(2,1)S(1)}, bf16[254,576]{0,1:T(8,128)(2,1)}, u32[]{:S(2)}) copy-start(bf16[254,576]{0,1:T(8,128)(2,1)} %param.8) | copy-start | bytes 877828
  11.0 12.4 %collective-permute-start.4 = (bf16[576,254]{1,0:T(8,128)(2,1)S(1)}, bf16[576,254]{1,0:T(8,128)(2,1)S(1)}, u32[]{:S(2)}, u32[]{:S(2)}) collective-permute-start(bf16[576,254]{1,0:T(8,128)(2,1)S(1)} %collective-permute-done.2.rest_2_), channel_id=1, source_target_pairs={{2,0},{3,7},{6,2},{7,11},{10,6},{11,15},{14,10},{15,13},{12,14},{1... | collective-permute-start | bytes 877832 | tf_op jit(solution)/shard_map/ppermute | solution.py:323
  13.1 12.0 %collective-permute-start.3 = (bf16[576,254]{1,0:T(8,128)(2,1)S(1)}, bf16[576,254]{1,0:T(8,128)(2,1)S(1)}, u32[]{:S(2)}, u32[]{:S(2)}) collective-permute-start(bf16[576,254]{1,0:T(8,128)(2,1)S(1)} %collective-permute-done.1.rest_1_), channel_id=1, source_target_pairs={{2,6},{3,1},{6,10},{7,3},{10,14},{11,7},{14,12},{15,11},{12,8},{13... | collective-permute-start | bytes 877832 | tf_op jit(solution)/shard_map/ppermute | solution.py:323
  22.3 4.1 %copy-start.2 = (s32[128]{0:T(128)S(1)}, s32[128]{0:T(128)}, u32[]{:S(2)}) copy-start(s32[128]{0:T(128)} %constant.2.clone.table_ref) | copy-start | bytes 1540
  22.3 4.1 %collective-permute-start = (bf16[16,9792]{1,0:T(8,128)(2,1)S(1)}, bf16[16,9792]{1,0:T(8,128)(2,1)S(1)}, u32[]{:S(2)}, u32[]{:S(2)}) collective-permute-start(bf16[16,9792]{1,0:T(8,128)(2,1)S(1)} %reshape.10.here_ref), channel_id=1, source_target_pairs={{0,1},{1,0},{2,3},{3,2},{4,5},{5,4},{6,7},{7,6},{8,9},{9,8},{10,11... | collective-permute-start | bytes 940040 | tf_op jit(solution)/shard_map/ppermute | solution.py:326
  23.4 9.7 %collective-permute-start.5 = (bf16[576,254]{1,0:T(8,128)(2,1)S(1)}, bf16[576,254]{1,0:T(8,128)(2,1)S(1)}, u32[]{:S(2)}, u32[]{:S(2)}) collective-permute-start(bf16[576,254]{1,0:T(8,128)(2,1)S(1)} %collective-permute-done.4.rest_4_), channel_id=1, source_target_pairs={{2,0},{3,7},{6,2},{7,11},{10,6},{11,15},{14,10},{15,13},{12,14},{1... | collective-permute-start | bytes 877832 | tf_op jit(solution)/shard_map/ppermute | solution.py:323
  25.1 9.8 %collective-permute-start.6 = (bf16[576,254]{1,0:T(8,128)(2,1)S(1)}, bf16[576,254]{1,0:T(8,128)(2,1)S(1)}, u32[]{:S(2)}, u32[]{:S(2)}) collective-permute-start(bf16[576,254]{1,0:T(8,128)(2,1)S(1)} %collective-permute-done.3.rest_3_), channel_id=1, source_target_pairs={{2,6},{3,1},{6,10},{7,3},{10,14},{11,7},{14,12},{15,11},{12,8},{13... | collective-permute-start | bytes 877832 | tf_op jit(solution)/shard_map/ppermute | solution.py:323
  33.1 6.8 %collective-permute-start.8 = (bf16[320,254]{1,0:T(8,128)(2,1)S(1)}, bf16[320,254]{1,0:T(8,128)(2,1)S(1)}, u32[]{:S(2)}, u32[]{:S(2)}) collective-permute-start(bf16[320,254]{1,0:T(8,128)(2,1)S(1)} %slice.7), channel_id=1, source_target_pairs={{2,0},{3,7},{6,2},{7,11},{10,6},{11,15},{14,10},{15,13},{12,14},{1... | collective-permute-start | bytes 487688 | tf_op jit(solution)/shard_map/ppermute | solution.py:337
  34.9 5.0 %collective-permute-start.7 = (bf16[256,254]{1,0:T(8,128)(2,1)S(1)}, bf16[256,254]{1,0:T(8,128)(2,1)S(1)}, u32[]{:S(2)}, u32[]{:S(2)}) collective-permute-start(bf16[256,254]{1,0:T(8,128)(2,1)S(1)} %slice.8), channel_id=1, source_target_pairs={{2,6},{3,1},{6,10},{7,3},{10,14},{11,7},{14,12},{15,11},{12,8},{13... | collective-permute-start | bytes 390152 | tf_op jit(solution)/shard_map/ppermute | solution.py:335
  41.2 1.7 %copy-start = (bf16[8,512,128]{2,1,0:T(8,128)(2,1)S(1)}, bf16[8,512,128]{2,1,0:T(8,128)(2,1)}, u32[]{:S(2)}) copy-start(bf16[8,512,128]{2,1,0:T(8,128)(2,1)} %up_ref.1) | copy-start | bytes 3145732
  41.2 1.7 %collective-permute-start.9 = (bf16[256,640]{1,0:T(8,128)(2,1)S(1)}, bf16[256,640]{1,0:T(8,128)(2,1)S(1)}, u32[]{:S(2)}, u32[]{:S(2)}) collective-permute-start(bf16[256,640]{1,0:T(8,128)(2,1)S(1)} %give.1), channel_id=1, source_target_pairs={{0,1},{1,0},{2,3},{3,2},{4,5},{5,4},{6,7},{7,6},{8,9},{9,8},{10,11... | collective-permute-start | bytes 983048 | tf_op jit(solution)/shard_map/ppermute | solution.py:359

commit v23 on v22

--- a/solution.py
+++ b/solution.py
@@ -120,18 +120,17 @@
     ]
 
 
-def pieces_kernel(queries_hbm, span_hbm, out_ref, span_ref, sems):
+def pieces_kernel(queries_hbm, span_hbm, out_hbm, sems):
     part = queries_hbm.shape[2]
-    copies = [
-        pltpu.make_async_copy(queries_hbm, out_ref.at[:, :, :part], sems.at[0]),
-        pltpu.make_async_copy(span_hbm, span_ref, sems.at[1]),
-    ]
+    copies = [pltpu.make_async_copy(queries_hbm, out_hbm.at[:, :, :part], sems.at[0])]
+    for chip in range(out_hbm.shape[0]):
+        copies.append(pltpu.make_async_copy(
+            span_hbm, out_hbm.at[chip, :, part:], sems.at[1 + chip]
+        ))
     for copy in copies:
         copy.start()
     for copy in copies:
         copy.wait()
-    for chip in range(out_ref.shape[0]):
-        out_ref[chip, :, part:] = span_ref[...]
 
 
 def first_kernel(heads, count, length_ref, table_ref, here_ref, there_ref, *rest):
@@ -305,11 +304,8 @@
         pieces_kernel,
         out_shape=shape(chips, tokens, (heads + 1) * width, dtype=bf16),
         in_specs=[anywhere] * 2,
-        out_specs=VMEM,
-        scratch_shapes=[
-            pltpu.VMEM(span_latents.shape, bf16),
-            pltpu.SemaphoreType.DMA((2,)),
-        ],
+        out_specs=anywhere,
+        scratch_shapes=[pltpu.SemaphoreType.DMA((1 + chips,))],
         compiler_params=pltpu.CompilerParams(vmem_limit_bytes=56 * 1024 * 1024),
         name="pieces",
     )(queries.reshape(tokens, chips, heads * width).transpose(1, 0, 2), span_latents)

time: 55.7 us -> 64.8 us (1.16)
  Pallas kernels: 10.7 us -> 19.7 us
    pallas_call x1, Pallas kernels: 1.7 us -> 10.7 us  [on_device(): pl.pallas_call(pieces_kernel, out_shape=shape(chips, tokens, (heads + 1)...]
  transfers between devices with their start and end apart: 11 -> 11, of which waited for: 5 -> 5; matrix products, arithmetic and copies ran while one was open for 0% -> 0% of each run, Pallas kernels for 16% -> 28%
where the time goes in v23:
time: 64.8 us; the launch traced here: 64.5 us
  Pallas kernels  19.7 us (30%)
  starting transfers between devices  16.5 us (25%)
  waiting for transfers between devices  14.5 us (22%)
  blocking collectives  11.5 us (18%)
  between operations  1.44 us (2%)
  local copies, waits for them, and re-layouts  0.9 us (1%)
    all_to_all x1, blocking collectives, on_device(): lax.all_to_all(merged, 'ctx', split_axis=0, concat_axis=0, tiled=True)  11.5 us
    pallas_call x1, Pallas kernels, on_device(): pl.pallas_call(pieces_kernel, out_shape=shape(chips, tokens, (heads + 1)...  10.7 us
    all_to_all x1, waiting for transfers between devices, on_device(): lax.all_to_all(pieces, 'ctx', split_axis=0, concat_axis=0, axis_index_gro...  8.91 us
    all_to_all x1, starting transfers between devices, on_device(): lax.all_to_all(pieces, 'ctx', split_axis=0, concat_axis=0, axis_index_gro...  6.26 us
    ppermute x4, starting transfers between devices, on_device(): right, left = (onward(right), backward(left))  4.45 us
    ppermute x4, waiting for transfers between devices, on_device(): right, left = (onward(right), backward(left))  4.06 us
    pallas_call x1, Pallas kernels, fold_first(): pl.pallas_call(functools.partial(first_kernel, heads, len(keys)), out_sha...  3.65 us
    ppermute x2, starting transfers between devices, on_device(): right, left = (onward(own), backward(own))  3.03 us
  transfers between devices with their start and end apart: 11, of which 5 were waited for; matrix products, arithmetic and copies ran while one was open for 0% of the time, Pallas kernels for 28%

profile of v23, /device:TPU:0, one launch (start us, length us, event | category | flops | bytes accessed | tf_op | source)
XLA Modules:
  0.0 64.5 jit_solution(2477693999666537462)
XLA Ops:
  0.0 2.9 %collective-permute-start.1 = (bf16[576,254]{1,0:T(8,128)(2,1)}, bf16[576,254]{1,0:T(8,128)(2,1)S(1)}, u32[]{:S(2)}, u32[]{:S(2)}) collective-permute-start(bf16[576,254]{1,0:T(8,128)(2,1)} %bitcast.7), channel_id=1, source_target_pairs={{2,6},{3,1},{6,10},{7,3},{10,14},{11,7},{14,12},{15,11},{12,8},{13... | collective-permute-start | bytes 877832 | tf_op jit(solution)/shard_map/ppermute | solution.py:300
  2.9 0.1 collective-permute-start.2
  3.0 10.7 %pieces.1 = bf16[8,2,9792]{2,1,0:T(2,128)(2,1)} custom-call(bf16[8,2,9216]{2,1,0:T(2,128)(2,1)} %bitcast.10, bf16[2,576]{1,0:T(2,128)(2,1)} %span_hbm.1), custom_call_target="tpu_custom_call" | custom-call | tf_op jit(solution)/shard_map/pieces/pallas_call | solution.py:303
  13.8 6.3 %all-to-all-start = ((bf16[8,2,9792]{2,1,0:T(2,128)(2,1)}), bf16[8,2,9792]{2,1,0:T(2,128)(2,1)S(1)}, u32[]{:S(2)}, u32[]{:S(2)}) async-start(bf16[8,2,9792]{2,1,0:T(2,128)(2,1)} %pieces.1), calls=%async_computation | async-start | bytes 630784 | tf_op jit(solution)/shard_map/all_to_all | solution.py:312
  20.0 0.0 copy-start.1
  20.0 0.0 collective-permute-done.1.rest_1_
  20.1 0.0 collective-permute-done.2.rest_2_
  20.1 2.1 %collective-permute-start.4 = (bf16[576,254]{1,0:T(8,128)(2,1)S(1)}, bf16[576,254]{1,0:T(8,128)(2,1)S(1)}, u32[]{:S(2)}, u32[]{:S(2)}) collective-permute-start(bf16[576,254]{1,0:T(8,128)(2,1)S(1)} %collective-permute-done.2.rest_2_), channel_id=1, source_target_pairs={{2,0},{3,7},{6,2},{7,11},{10,6},{11,15},{14,10},{15,13},{12,14},{1... | collective-permute-start | bytes 877832 | tf_op jit(solution)/shard_map/ppermute | solution.py:319
  22.1 0.1 collective-permute-start.3
  22.2 8.9 %all-to-all-done = bf16[8,2,9792]{2,1,0:T(2,128)(2,1)S(1)} async-done(((bf16[8,2,9792]{2,1,0:T(2,128)(2,1)}), bf16[8,2,9792]{2,1,0:T(2,128)(2,1)S(1)}, u32[]{:S(2)}, u32[]{:S(2)}) %all-to-all-start) | async-done | bytes 313376 | tf_op jit(solution)/shard_map/all_to_all | solution.py:312
  31.1 0.2 reshape.10.here_ref
  31.3 0.0 copy-start.2
  31.4 0.1 collective-permute-start
  31.4 1.0 %collective-permute-done.4.rest_4_ = bf16[576,254]{1,0:T(8,128)(2,1)S(1)} collective-permute-done((bf16[576,254]{1,0:T(8,128)(2,1)S(1)}, bf16[576,254]{1,0:T(8,128)(2,1)S(1)}, u32[]{:S(2)}, u32[]{:S(2)}) %collective-permute-start.4) | collective-permute-done | bytes 292640 | tf_op jit(solution)/shard_map/ppermute | solution.py:319
  32.4 1.7 %collective-permute-start.5 = (bf16[576,254]{1,0:T(8,128)(2,1)S(1)}, bf16[576,254]{1,0:T(8,128)(2,1)S(1)}, u32[]{:S(2)}, u32[]{:S(2)}) collective-permute-start(bf16[576,254]{1,0:T(8,128)(2,1)S(1)} %collective-permute-done.4.rest_4_), channel_id=1, source_target_pairs={{2,0},{3,7},{6,2},{7,11},{10,6},{11,15},{14,10},{15,13},{12,14},{1... | collective-permute-start | bytes 877832 | tf_op jit(solution)/shard_map/ppermute | solution.py:319
  34.2 0.0 collective-permute-done.3.rest_3_
  34.2 0.6 collective-permute-start.6
  35.4 0.0 collective-permute-done.there_ref
  35.4 0.0 copy-done.1
  35.4 0.0 copy-done.2
  35.4 3.7 %first.1 = (bf16[512,576]{1,0:T(8,128)(2,1)S(1)}, f32[512,128]{1,0:T(8,128)S(1)}, f32[512,128]{1,0:T(8,128)S(1)}, f32[512,512]{1,0:T(8,128)S(1)}) custom-call(s32[1]{0:T(128)S(6)} %copy.9.length_ref, s32[128]{0:T(128)S(1)} %copy-done.2, bf16[16,9792]{1,0:T(8,128)(2,1)S(1)} %reshape.10.here_ref, bf16[16,9792]{1,0:T(8,128)(2,1)S(1)} %collective-permute-done.there_ref, ...), custom_call_target="tpu_custom_call" | custom-call | tf_op jit(solution)/shard_map/first/pallas_call | solution.py:277
  39.1 3.1 %collective-permute-done.5.rest_1_ = bf16[576,254]{1,0:T(8,128)(2,1)S(1)} collective-permute-done((bf16[576,254]{1,0:T(8,128)(2,1)S(1)}, bf16[576,254]{1,0:T(8,128)(2,1)S(1)}, u32[]{:S(2)}, u32[]{:S(2)}) %collective-permute-start.5) | collective-permute-done | bytes 292640 | tf_op jit(solution)/shard_map/ppermute | solution.py:319
  42.2 1.8 %collective-permute-start.8 = (bf16[320,254]{1,0:T(8,128)(2,1)S(1)}, bf16[320,254]{1,0:T(8,128)(2,1)S(1)}, u32[]{:S(2)}, u32[]{:S(2)}) collective-permute-start(bf16[320,254]{1,0:T(8,128)(2,1)S(1)} %slice.7), channel_id=1, source_target_pairs={{2,0},{3,7},{6,2},{7,11},{10,6},{11,15},{14,10},{15,13},{12,14},{1... | collective-permute-start | bytes 487688 | tf_op jit(solution)/shard_map/ppermute | solution.py:333
  43.9 0.0 collective-permute-done.6.rest_0_
  44.0 0.8 %collective-permute-start.7 = (bf16[256,254]{1,0:T(8,128)(2,1)S(1)}, bf16[256,254]{1,0:T(8,128)(2,1)S(1)}, u32[]{:S(2)}, u32[]{:S(2)}) collective-permute-start(bf16[256,254]{1,0:T(8,128)(2,1)S(1)} %slice.8), channel_id=1, source_target_pairs={{2,6},{3,1},{6,10},{7,3},{10,14},{11,7},{14,12},{15,11},{12,8},{13... | collective-permute-start | bytes 390152 | tf_op jit(solution)/shard_map/ppermute | solution.py:331
  45.4 2.5 %middle.1 = (f32[512,128]{1,0:T(8,128)S(1)}, f32[512,128]{1,0:T(8,128)S(1)}, f32[512,512]{1,0:T(8,128)S(1)}) custom-call(s32[1]{0:T(128)S(6)} %copy.9.length_ref, s32[1]{0:T(128)S(6)} %copy.10.offset_ref, s32[128]{0:T(128)S(1)} %copy-done.2, bf16[512,576]{1,0:T(8,128)(2,1)S(1)} %get-tuple-element.20.q_ref, f32[512,128]{1,0:T(8,128)S(1)} %get-tuple-element.24.m_in, ...), custom_call_target="tpu_custom_call" | custom-call | tf_op jit(solution)/shard_map/middle/pallas_call | solution.py:334
  47.9 1.1 %collective-permute-done.7.top_ref = bf16[256,254]{1,0:T(8,128)(2,1)S(1)} collective-permute-done((bf16[256,254]{1,0:T(8,128)(2,1)S(1)}, bf16[256,254]{1,0:T(8,128)(2,1)S(1)}, u32[]{:S(2)}, u32[]{:S(2)}) %collective-permute-start.7) | collective-permute-done | bytes 130080 | tf_op jit(solution)/shard_map/ppermute | solution.py:331
  49.0 0.0 collective-permute-done.8.bottom_ref
  49.0 1.2 %give.1 = bf16[256,640]{1,0:T(8,128)(2,1)S(1)} custom-call(s32[1]{0:T(128)S(6)} %copy.9.length_ref, s32[128]{0:T(128)S(1)} %copy-done.2, bf16[512,576]{1,0:T(8,128)(2,1)S(1)} %get-tuple-element.20.q_ref, f32[512,128]{1,0:T(8,128)S(1)} %get-tuple-element.27.m_ref, f32[512,128]{1,0:T(8,128)S(1)} %get-tuple-element.28.l_ref, ...), custom_call_target="tpu_custom_call" | custom-call | tf_op jit(solution)/shard_map/give/pallas_call | solution.py:346
  50.2 0.0 copy-start
  50.2 0.1 collective-permute-start.9
  50.3 1.2 %keep.1.keep_ref = f32[256,640]{1,0:T(8,128)S(1)} custom-call(s32[1]{0:T(128)S(6)} %copy.9.length_ref, s32[128]{0:T(128)S(1)} %copy-done.2, bf16[512,576]{1,0:T(8,128)(2,1)S(1)} %get-tuple-element.20.q_ref, f32[512,128]{1,0:T(8,128)S(1)} %get-tuple-element.27.m_ref, f32[512,128]{1,0:T(8,128)S(1)} %get-tuple-element.28.l_ref, ...), custom_call_target="tpu_custom_call" | custom-call | tf_op jit(solution)/shard_map/keep/pallas_call | solution.py:346
  51.5 0.4 collective-permute-done.9.got_ref
  51.9 0.0 copy-done
  51.9 0.5 merge.1
  52.4 11.5 %all_to_all.10 = bf16[16,2,1024]{2,1,0:T(2,128)(2,1)S(1)} all-to-all(bf16[16,2,1024]{2,1,0:T(2,128)(2,1)S(1)} %merge.1), channel_id=1, replica_groups=mesh['groups'=2,'ctx'=16] {'ctx'}, dimensions={0} | all-to-all | bytes 131072 | tf_op jit(solution)/shard_map/all_to_all | solution.py:366
  63.9 0.6 copy.11
  (2 shorter events, 0.0 us)
Async XLA Ops:
  0.0 20.0 %collective-permute-start.1 = (bf16[576,254]{1,0:T(8,128)(2,1)}, bf16[576,254]{1,0:T(8,128)(2,1)S(1)}, u32[]{:S(2)}, u32[]{:S(2)}) collective-permute-start(bf16[576,254]{1,0:T(8,128)(2,1)} %bitcast.7), channel_id=1, source_target_pairs={{2,6},{3,1},{6,10},{7,3},{10,14},{11,7},{14,12},{15,11},{12,8},{13... | collective-permute-start | bytes 877832 | tf_op jit(solution)/shard_map/ppermute | solution.py:300
  2.9 17.1 %collective-permute-start.2 = (bf16[576,254]{1,0:T(8,128)(2,1)}, bf16[576,254]{1,0:T(8,128)(2,1)S(1)}, u32[]{:S(2)}, u32[]{:S(2)}) collective-permute-start(bf16[576,254]{1,0:T(8,128)(2,1)} %bitcast.8), channel_id=1, source_target_pairs={{2,0},{3,7},{6,2},{7,11},{10,6},{11,15},{14,10},{15,13},{12,14},{1... | collective-permute-start | bytes 877832 | tf_op jit(solution)/shard_map/ppermute | solution.py:300
  13.8 17.3 %all-to-all-start = ((bf16[8,2,9792]{2,1,0:T(2,128)(2,1)}), bf16[8,2,9792]{2,1,0:T(2,128)(2,1)S(1)}, u32[]{:S(2)}, u32[]{:S(2)}) async-start(bf16[8,2,9792]{2,1,0:T(2,128)(2,1)} %pieces.1), calls=%async_computation | async-start | bytes 630784 | tf_op jit(solution)/shard_map/all_to_all | solution.py:312
  20.0 15.4 %copy-start.1 = (bf16[254,576]{0,1:T(8,128)(2,1)S(1)}, bf16[254,576]{0,1:T(8,128)(2,1)}, u32[]{:S(2)}) copy-start(bf16[254,576]{0,1:T(8,128)(2,1)} %param.8) | copy-start | bytes 877828
  20.1 12.4 %collective-permute-start.4 = (bf16[576,254]{1,0:T(8,128)(2,1)S(1)}, bf16[576,254]{1,0:T(8,128)(2,1)S(1)}, u32[]{:S(2)}, u32[]{:S(2)}) collective-permute-start(bf16[576,254]{1,0:T(8,128)(2,1)S(1)} %collective-permute-done.2.rest_2_), channel_id=1, source_target_pairs={{2,0},{3,7},{6,2},{7,11},{10,6},{11,15},{14,10},{15,13},{12,14},{1... | collective-permute-start | bytes 877832 | tf_op jit(solution)/shard_map/ppermute | solution.py:319
  22.1 12.0 %collective-permute-start.3 = (bf16[576,254]{1,0:T(8,128)(2,1)S(1)}, bf16[576,254]{1,0:T(8,128)(2,1)S(1)}, u32[]{:S(2)}, u32[]{:S(2)}) collective-permute-start(bf16[576,254]{1,0:T(8,128)(2,1)S(1)} %collective-permute-done.1.rest_1_), channel_id=1, source_target_pairs={{2,6},{3,1},{6,10},{7,3},{10,14},{11,7},{14,12},{15,11},{12,8},{13... | collective-permute-start | bytes 877832 | tf_op jit(solution)/shard_map/ppermute | solution.py:319
  31.3 4.1 %copy-start.2 = (s32[128]{0:T(128)S(1)}, s32[128]{0:T(128)}, u32[]{:S(2)}) copy-start(s32[128]{0:T(128)} %constant.2.clone.table_ref) | copy-start | bytes 1540
  31.4 4.1 %collective-permute-start = (bf16[16,9792]{1,0:T(8,128)(2,1)S(1)}, bf16[16,9792]{1,0:T(8,128)(2,1)S(1)}, u32[]{:S(2)}, u32[]{:S(2)}) collective-permute-start(bf16[16,9792]{1,0:T(8,128)(2,1)S(1)} %reshape.10.here_ref), channel_id=1, source_target_pairs={{0,1},{1,0},{2,3},{3,2},{4,5},{5,4},{6,7},{7,6},{8,9},{9,8},{10,11... | collective-permute-start | bytes 940040 | tf_op jit(solution)/shard_map/ppermute | solution.py:322
  32.4 9.7 %collective-permute-start.5 = (bf16[576,254]{1,0:T(8,128)(2,1)S(1)}, bf16[576,254]{1,0:T(8,128)(2,1)S(1)}, u32[]{:S(2)}, u32[]{:S(2)}) collective-permute-start(bf16[576,254]{1,0:T(8,128)(2,1)S(1)} %collective-permute-done.4.rest_4_), channel_id=1, source_target_pairs={{2,0},{3,7},{6,2},{7,11},{10,6},{11,15},{14,10},{15,13},{12,14},{1... | collective-permute-start | bytes 877832 | tf_op jit(solution)/shard_map/ppermute | solution.py:319
  34.2 9.8 %collective-permute-start.6 = (bf16[576,254]{1,0:T(8,128)(2,1)S(1)}, bf16[576,254]{1,0:T(8,128)(2,1)S(1)}, u32[]{:S(2)}, u32[]{:S(2)}) collective-permute-start(bf16[576,254]{1,0:T(8,128)(2,1)S(1)} %collective-permute-done.3.rest_3_), channel_id=1, source_target_pairs={{2,6},{3,1},{6,10},{7,3},{10,14},{11,7},{14,12},{15,11},{12,8},{13... | collective-permute-start | bytes 877832 | tf_op jit(solution)/shard_map/ppermute | solution.py:319
  42.2 6.8 %collective-permute-start.8 = (bf16[320,254]{1,0:T(8,128)(2,1)S(1)}, bf16[320,254]{1,0:T(8,128)(2,1)S(1)}, u32[]{:S(2)}, u32[]{:S(2)}) collective-permute-start(bf16[320,254]{1,0:T(8,128)(2,1)S(1)} %slice.7), channel_id=1, source_target_pairs={{2,0},{3,7},{6,2},{7,11},{10,6},{11,15},{14,10},{15,13},{12,14},{1... | collective-permute-start | bytes 487688 | tf_op jit(solution)/shard_map/ppermute | solution.py:333
  44.0 5.0 %collective-permute-start.7 = (bf16[256,254]{1,0:T(8,128)(2,1)S(1)}, bf16[256,254]{1,0:T(8,128)(2,1)S(1)}, u32[]{:S(2)}, u32[]{:S(2)}) collective-permute-start(bf16[256,254]{1,0:T(8,128)(2,1)S(1)} %slice.8), channel_id=1, source_target_pairs={{2,6},{3,1},{6,10},{7,3},{10,14},{11,7},{14,12},{15,11},{12,8},{13... | collective-permute-start | bytes 390152 | tf_op jit(solution)/shard_map/ppermute | solution.py:331
  50.2 1.7 %copy-start = (bf16[8,512,128]{2,1,0:T(8,128)(2,1)S(1)}, bf16[8,512,128]{2,1,0:T(8,128)(2,1)}, u32[]{:S(2)}) copy-start(bf16[8,512,128]{2,1,0:T(8,128)(2,1)} %up_ref.1) | copy-start | bytes 3145732
  50.2 1.7 %collective-permute-start.9 = (bf16[256,640]{1,0:T(8,128)(2,1)S(1)}, bf16[256,640]{1,0:T(8,128)(2,1)S(1)}, u32[]{:S(2)}, u32[]{:S(2)}) collective-permute-start(bf16[256,640]{1,0:T(8,128)(2,1)S(1)} %give.1), channel_id=1, source_target_pairs={{0,1},{1,0},{2,3},{3,2},{4,5},{5,4},{6,7},{7,6},{8,9},{9,8},{10,11... | collective-permute-start | bytes 983048 | tf_op jit(solution)/shard_map/ppermute | solution.py:355

commit v24 on v22

--- a/solution.py
+++ b/solution.py
@@ -224,7 +224,7 @@
     devices, tokens, _ = out_ref.shape
     chips = devices // CORES
     for i in range(devices):
-        out_ref[(i % chips) * CORES + (core ^ (i // chips))] = (
+        out_ref[devices - 1 - (i % chips) * CORES - (core ^ (i // chips))] = (
             flat_ref[i * tokens:(i + 1) * tokens, :].astype(bf16)
         )
 
@@ -367,8 +367,11 @@
         compiler_params=PARAMS,
         name="merge",
     )(keep, got, value_up)
-    returned = lax.all_to_all(merged, "ctx", split_axis=0, concat_axis=0, tiled=True)
-    return returned.transpose(1, 0, 2).reshape(tokens, all_heads * V_HEAD)
+    returned = lax.all_to_all(
+        merged, "ctx", split_axis=0, concat_axis=0, tiled=True,
+        axis_index_groups=[list(range(ctx))[::-1]],
+    )
+    return returned[::-1].transpose(1, 0, 2).reshape(tokens, all_heads * V_HEAD)
 
 
 def solution(mesh):

time: 55.7 us -> 53 us (0.952)
  blocking collectives: 11.5 us -> 8.72 us
    all_to_all x1, blocking collectives: 11.5 us -> 8.72 us  [on_device(): lax.all_to_all(merged, 'ctx', split_axis=0, concat_axis=0, tiled=True, ax...]
    rev x0 -> x1, local copies, waits for them, and re-layouts: none -> 0.68 us  [on_device(): return returned[::-1].transpose(1, 0, 2).reshape(tokens, all_heads * V_HEAD)]
    unnamed x7 -> x6, local copies, waits for them, and re-layouts: 0.65 us -> 0.02 us
  transfers between devices with their start and end apart: 11 -> 11, of which waited for: 5 -> 5; matrix products, arithmetic and copies ran while one was open for 0% -> 0% of each run, Pallas kernels for 16% -> 17%
where the time goes in v24:
time: 53 us; the launch traced here: 52.8 us
  starting transfers between devices  16.5 us (31%)
  waiting for transfers between devices  14.5 us (27%)
  Pallas kernels  10.7 us (20%)
  blocking collectives  8.72 us (16%)
  between operations  1.44 us (3%)
  local copies, waits for them, and re-layouts  0.94 us (2%)
    all_to_all x1, waiting for transfers between devices, on_device(): lax.all_to_all(pieces, 'ctx', split_axis=0, concat_axis=0, axis_index_gro...  8.91 us
    all_to_all x1, blocking collectives, on_device(): lax.all_to_all(merged, 'ctx', split_axis=0, concat_axis=0, tiled=True, ax...  8.72 us
    all_to_all x1, starting transfers between devices, on_device(): lax.all_to_all(pieces, 'ctx', split_axis=0, concat_axis=0, axis_index_gro...  6.26 us
    ppermute x4, starting transfers between devices, on_device(): right, left = (onward(right), backward(left))  4.45 us
    ppermute x4, waiting for transfers between devices, on_device(): right, left = (onward(right), backward(left))  4.06 us
    pallas_call x1, Pallas kernels, fold_first(): pl.pallas_call(functools.partial(first_kernel, heads, len(keys)), out_sha...  3.65 us
    ppermute x2, starting transfers between devices, on_device(): right, left = (onward(own), backward(own))  3.03 us
    pallas_call x1, Pallas kernels, on_device(): pl.pallas_call(functools.partial(span_kernel, at, len(keys)), out_shape=s...  2.47 us
  transfers between devices with their start and end apart: 11, of which 5 were waited for; matrix products, arithmetic and copies ran while one was open for 0% of the time, Pallas kernels for 17%

profile of v24, /device:TPU:0, one launch (start us, length us, event | category | flops | bytes accessed | tf_op | source)
XLA Modules:
  0.0 52.8 jit_solution(17744771084541002903)
XLA Ops:
  0.0 2.9 %collective-permute-start.1 = (bf16[576,254]{1,0:T(8,128)(2,1)}, bf16[576,254]{1,0:T(8,128)(2,1)S(1)}, u32[]{:S(2)}, u32[]{:S(2)}) collective-permute-start(bf16[576,254]{1,0:T(8,128)(2,1)} %bitcast.7), channel_id=1, source_target_pairs={{2,6},{3,1},{6,10},{7,3},{10,14},{11,7},{14,12},{15,11},{12,8},{13... | collective-permute-start | bytes 877832 | tf_op jit(solution)/shard_map/ppermute | solution.py:301
  2.9 0.1 collective-permute-start.2
  3.0 1.7 %pieces.1 = bf16[8,2,9792]{2,1,0:T(2,128)(2,1)} custom-call(bf16[8,2,9216]{2,1,0:T(2,128)(2,1)} %bitcast.10, bf16[2,576]{1,0:T(2,128)(2,1)} %span_hbm.1), custom_call_target="tpu_custom_call" | custom-call | tf_op jit(solution)/shard_map/pieces/pallas_call | solution.py:304
  4.7 6.3 %all-to-all-start = ((bf16[8,2,9792]{2,1,0:T(2,128)(2,1)}), bf16[8,2,9792]{2,1,0:T(2,128)(2,1)S(1)}, u32[]{:S(2)}, u32[]{:S(2)}) async-start(bf16[8,2,9792]{2,1,0:T(2,128)(2,1)} %pieces.1), calls=%async_computation | async-start | bytes 630784 | tf_op jit(solution)/shard_map/all_to_all | solution.py:316
  11.0 0.0 copy-start.1
  11.0 0.0 collective-permute-done.1.rest_1_
  11.0 0.0 collective-permute-done.2.rest_2_
  11.0 2.1 %collective-permute-start.4 = (bf16[576,254]{1,0:T(8,128)(2,1)S(1)}, bf16[576,254]{1,0:T(8,128)(2,1)S(1)}, u32[]{:S(2)}, u32[]{:S(2)}) collective-permute-start(bf16[576,254]{1,0:T(8,128)(2,1)S(1)} %collective-permute-done.2.rest_2_), channel_id=1, source_target_pairs={{2,0},{3,7},{6,2},{7,11},{10,6},{11,15},{14,10},{15,13},{12,14},{1... | collective-permute-start | bytes 877832 | tf_op jit(solution)/shard_map/ppermute | solution.py:323
  13.1 0.1 collective-permute-start.3
  13.2 8.9 %all-to-all-done = bf16[8,2,9792]{2,1,0:T(2,128)(2,1)S(1)} async-done(((bf16[8,2,9792]{2,1,0:T(2,128)(2,1)}), bf16[8,2,9792]{2,1,0:T(2,128)(2,1)S(1)}, u32[]{:S(2)}, u32[]{:S(2)}) %all-to-all-start) | async-done | bytes 313376 | tf_op jit(solution)/shard_map/all_to_all | solution.py:316
  22.1 0.2 reshape.10.here_ref
  22.3 0.0 copy-start.2
  22.3 0.1 collective-permute-start
  22.4 1.0 %collective-permute-done.4.rest_4_ = bf16[576,254]{1,0:T(8,128)(2,1)S(1)} collective-permute-done((bf16[576,254]{1,0:T(8,128)(2,1)S(1)}, bf16[576,254]{1,0:T(8,128)(2,1)S(1)}, u32[]{:S(2)}, u32[]{:S(2)}) %collective-permute-start.4) | collective-permute-done | bytes 292640 | tf_op jit(solution)/shard_map/ppermute | solution.py:323
  23.4 1.7 %collective-permute-start.5 = (bf16[576,254]{1,0:T(8,128)(2,1)S(1)}, bf16[576,254]{1,0:T(8,128)(2,1)S(1)}, u32[]{:S(2)}, u32[]{:S(2)}) collective-permute-start(bf16[576,254]{1,0:T(8,128)(2,1)S(1)} %collective-permute-done.4.rest_4_), channel_id=1, source_target_pairs={{2,0},{3,7},{6,2},{7,11},{10,6},{11,15},{14,10},{15,13},{12,14},{1... | collective-permute-start | bytes 877832 | tf_op jit(solution)/shard_map/ppermute | solution.py:323
  25.1 0.0 collective-permute-done.3.rest_3_
  25.1 0.6 %collective-permute-start.6 = (bf16[576,254]{1,0:T(8,128)(2,1)S(1)}, bf16[576,254]{1,0:T(8,128)(2,1)S(1)}, u32[]{:S(2)}, u32[]{:S(2)}) collective-permute-start(bf16[576,254]{1,0:T(8,128)(2,1)S(1)} %collective-permute-done.3.rest_3_), channel_id=1, source_target_pairs={{2,6},{3,1},{6,10},{7,3},{10,14},{11,7},{14,12},{15,11},{12,8},{13... | collective-permute-start | bytes 877832 | tf_op jit(solution)/shard_map/ppermute | solution.py:323
  26.4 0.0 collective-permute-done.there_ref
  26.4 0.0 copy-done.1
  26.4 0.0 copy-done.2
  26.4 3.7 %first.1 = (bf16[512,576]{1,0:T(8,128)(2,1)S(1)}, f32[512,128]{1,0:T(8,128)S(1)}, f32[512,128]{1,0:T(8,128)S(1)}, f32[512,512]{1,0:T(8,128)S(1)}) custom-call(s32[1]{0:T(128)S(6)} %copy.8.length_ref, s32[128]{0:T(128)S(1)} %copy-done.2, bf16[16,9792]{1,0:T(8,128)(2,1)S(1)} %reshape.10.here_ref, bf16[16,9792]{1,0:T(8,128)(2,1)S(1)} %collective-permute-done.there_ref, ...), custom_call_target="tpu_custom_call" | custom-call | tf_op jit(solution)/shard_map/first/pallas_call | solution.py:278
  30.0 3.1 %collective-permute-done.5.rest_1_ = bf16[576,254]{1,0:T(8,128)(2,1)S(1)} collective-permute-done((bf16[576,254]{1,0:T(8,128)(2,1)S(1)}, bf16[576,254]{1,0:T(8,128)(2,1)S(1)}, u32[]{:S(2)}, u32[]{:S(2)}) %collective-permute-start.5) | collective-permute-done | bytes 292640 | tf_op jit(solution)/shard_map/ppermute | solution.py:323
  33.1 1.8 %collective-permute-start.8 = (bf16[320,254]{1,0:T(8,128)(2,1)S(1)}, bf16[320,254]{1,0:T(8,128)(2,1)S(1)}, u32[]{:S(2)}, u32[]{:S(2)}) collective-permute-start(bf16[320,254]{1,0:T(8,128)(2,1)S(1)} %slice.7), channel_id=1, source_target_pairs={{2,0},{3,7},{6,2},{7,11},{10,6},{11,15},{14,10},{15,13},{12,14},{1... | collective-permute-start | bytes 487688 | tf_op jit(solution)/shard_map/ppermute | solution.py:337
  34.9 0.0 collective-permute-done.6.rest_0_
  34.9 0.8 %collective-permute-start.7 = (bf16[256,254]{1,0:T(8,128)(2,1)S(1)}, bf16[256,254]{1,0:T(8,128)(2,1)S(1)}, u32[]{:S(2)}, u32[]{:S(2)}) collective-permute-start(bf16[256,254]{1,0:T(8,128)(2,1)S(1)} %slice.8), channel_id=1, source_target_pairs={{2,6},{3,1},{6,10},{7,3},{10,14},{11,7},{14,12},{15,11},{12,8},{13... | collective-permute-start | bytes 390152 | tf_op jit(solution)/shard_map/ppermute | solution.py:335
  36.4 2.5 %middle.1 = (f32[512,128]{1,0:T(8,128)S(1)}, f32[512,128]{1,0:T(8,128)S(1)}, f32[512,512]{1,0:T(8,128)S(1)}) custom-call(s32[1]{0:T(128)S(6)} %copy.8.length_ref, s32[1]{0:T(128)S(6)} %copy.9.offset_ref, s32[128]{0:T(128)S(1)} %copy-done.2, bf16[512,576]{1,0:T(8,128)(2,1)S(1)} %get-tuple-element.20.q_ref, f32[512,128]{1,0:T(8,128)S(1)} %get-tuple-element.24.m_in, ...), custom_call_target="tpu_custom_call" | custom-call | tf_op jit(solution)/shard_map/middle/pallas_call | solution.py:338
  38.9 1.1 %collective-permute-done.7.top_ref = bf16[256,254]{1,0:T(8,128)(2,1)S(1)} collective-permute-done((bf16[256,254]{1,0:T(8,128)(2,1)S(1)}, bf16[256,254]{1,0:T(8,128)(2,1)S(1)}, u32[]{:S(2)}, u32[]{:S(2)}) %collective-permute-start.7) | collective-permute-done | bytes 130080 | tf_op jit(solution)/shard_map/ppermute | solution.py:335
  39.9 0.0 collective-permute-done.8.bottom_ref
  39.9 1.2 %give.1 = bf16[256,640]{1,0:T(8,128)(2,1)S(1)} custom-call(s32[1]{0:T(128)S(6)} %copy.8.length_ref, s32[128]{0:T(128)S(1)} %copy-done.2, bf16[512,576]{1,0:T(8,128)(2,1)S(1)} %get-tuple-element.20.q_ref, f32[512,128]{1,0:T(8,128)S(1)} %get-tuple-element.27.m_ref, f32[512,128]{1,0:T(8,128)S(1)} %get-tuple-element.28.l_ref, ...), custom_call_target="tpu_custom_call" | custom-call | tf_op jit(solution)/shard_map/give/pallas_call | solution.py:350
  41.2 0.0 copy-start
  41.2 0.1 collective-permute-start.9
  41.2 1.2 %keep.1.keep_ref = f32[256,640]{1,0:T(8,128)S(1)} custom-call(s32[1]{0:T(128)S(6)} %copy.8.length_ref, s32[128]{0:T(128)S(1)} %copy-done.2, bf16[512,576]{1,0:T(8,128)(2,1)S(1)} %get-tuple-element.20.q_ref, f32[512,128]{1,0:T(8,128)S(1)} %get-tuple-element.27.m_ref, f32[512,128]{1,0:T(8,128)S(1)} %get-tuple-element.28.l_ref, ...), custom_call_target="tpu_custom_call" | custom-call | tf_op jit(solution)/shard_map/keep/pallas_call | solution.py:350
  42.4 0.4 collective-permute-done.9.got_ref
  42.9 0.0 copy-done
  42.9 0.5 merge.1
  43.4 8.7 %all_to_all.10 = bf16[16,2,1024]{2,1,0:T(2,128)(2,1)S(1)} all-to-all(bf16[16,2,1024]{2,1,0:T(2,128)(2,1)S(1)} %merge.1), channel_id=1, replica_groups={{15,14,13,12,11,10,9,8,7,6,5,4,3,2,1,0},{31,30,29,28,27,26,25,24,23,22,..., dimensions={0} | all-to-all | bytes 131072 | tf_op jit(solution)/shard_map/all_to_all | solution.py:370
  52.1 0.7 %rev.3 = bf16[16,2,1024]{2,1,0:T(2,128)(2,1)} reverse(bf16[16,2,1024]{2,1,0:T(2,128)(2,1)S(1)} %all_to_all.10), dimensions={0} | reverse | bytes 131072 | tf_op jit(solution)/shard_map/rev | solution.py:374
  (2 shorter events, 0.0 us)
Async XLA Ops:
  0.0 11.0 %collective-permute-start.1 = (bf16[576,254]{1,0:T(8,128)(2,1)}, bf16[576,254]{1,0:T(8,128)(2,1)S(1)}, u32[]{:S(2)}, u32[]{:S(2)}) collective-permute-start(bf16[576,254]{1,0:T(8,128)(2,1)} %bitcast.7), channel_id=1, source_target_pairs={{2,6},{3,1},{6,10},{7,3},{10,14},{11,7},{14,12},{15,11},{12,8},{13... | collective-permute-start | bytes 877832 | tf_op jit(solution)/shard_map/ppermute | solution.py:301
  2.9 8.1 %collective-permute-start.2 = (bf16[576,254]{1,0:T(8,128)(2,1)}, bf16[576,254]{1,0:T(8,128)(2,1)S(1)}, u32[]{:S(2)}, u32[]{:S(2)}) collective-permute-start(bf16[576,254]{1,0:T(8,128)(2,1)} %bitcast.8), channel_id=1, source_target_pairs={{2,0},{3,7},{6,2},{7,11},{10,6},{11,15},{14,10},{15,13},{12,14},{1... | collective-permute-start | bytes 877832 | tf_op jit(solution)/shard_map/ppermute | solution.py:301
  4.7 17.3 %all-to-all-start = ((bf16[8,2,9792]{2,1,0:T(2,128)(2,1)}), bf16[8,2,9792]{2,1,0:T(2,128)(2,1)S(1)}, u32[]{:S(2)}, u32[]{:S(2)}) async-start(bf16[8,2,9792]{2,1,0:T(2,128)(2,1)} %pieces.1), calls=%async_computation | async-start | bytes 630784 | tf_op jit(solution)/shard_map/all_to_all | solution.py:316
  11.0 15.4 %copy-start.1 = (bf16[254,576]{0,1:T(8,128)(2,1)S(1)}, bf16[254,576]{0,1:T(8,128)(2,1)}, u32[]{:S(2)}) copy-start(bf16[254,576]{0,1:T(8,128)(2,1)} %param.8) | copy-start | bytes 877828
  11.0 12.4 %collective-permute-start.4 = (bf16[576,254]{1,0:T(8,128)(2,1)S(1)}, bf16[576,254]{1,0:T(8,128)(2,1)S(1)}, u32[]{:S(2)}, u32[]{:S(2)}) collective-permute-start(bf16[576,254]{1,0:T(8,128)(2,1)S(1)} %collective-permute-done.2.rest_2_), channel_id=1, source_target_pairs={{2,0},{3,7},{6,2},{7,11},{10,6},{11,15},{14,10},{15,13},{12,14},{1... | collective-permute-start | bytes 877832 | tf_op jit(solution)/shard_map/ppermute | solution.py:323
  13.1 12.0 %collective-permute-start.3 = (bf16[576,254]{1,0:T(8,128)(2,1)S(1)}, bf16[576,254]{1,0:T(8,128)(2,1)S(1)}, u32[]{:S(2)}, u32[]{:S(2)}) collective-permute-start(bf16[576,254]{1,0:T(8,128)(2,1)S(1)} %collective-permute-done.1.rest_1_), channel_id=1, source_target_pairs={{2,6},{3,1},{6,10},{7,3},{10,14},{11,7},{14,12},{15,11},{12,8},{13... | collective-permute-start | bytes 877832 | tf_op jit(solution)/shard_map/ppermute | solution.py:323
  22.3 4.1 %copy-start.2 = (s32[128]{0:T(128)S(1)}, s32[128]{0:T(128)}, u32[]{:S(2)}) copy-start(s32[128]{0:T(128)} %constant.2.clone.table_ref) | copy-start | bytes 1540
  22.3 4.1 %collective-permute-start = (bf16[16,9792]{1,0:T(8,128)(2,1)S(1)}, bf16[16,9792]{1,0:T(8,128)(2,1)S(1)}, u32[]{:S(2)}, u32[]{:S(2)}) collective-permute-start(bf16[16,9792]{1,0:T(8,128)(2,1)S(1)} %reshape.10.here_ref), channel_id=1, source_target_pairs={{0,1},{1,0},{2,3},{3,2},{4,5},{5,4},{6,7},{7,6},{8,9},{9,8},{10,11... | collective-permute-start | bytes 940040 | tf_op jit(solution)/shard_map/ppermute | solution.py:326
  23.4 9.7 %collective-permute-start.5 = (bf16[576,254]{1,0:T(8,128)(2,1)S(1)}, bf16[576,254]{1,0:T(8,128)(2,1)S(1)}, u32[]{:S(2)}, u32[]{:S(2)}) collective-permute-start(bf16[576,254]{1,0:T(8,128)(2,1)S(1)} %collective-permute-done.4.rest_4_), channel_id=1, source_target_pairs={{2,0},{3,7},{6,2},{7,11},{10,6},{11,15},{14,10},{15,13},{12,14},{1... | collective-permute-start | bytes 877832 | tf_op jit(solution)/shard_map/ppermute | solution.py:323
  25.1 9.8 %collective-permute-start.6 = (bf16[576,254]{1,0:T(8,128)(2,1)S(1)}, bf16[576,254]{1,0:T(8,128)(2,1)S(1)}, u32[]{:S(2)}, u32[]{:S(2)}) collective-permute-start(bf16[576,254]{1,0:T(8,128)(2,1)S(1)} %collective-permute-done.3.rest_3_), channel_id=1, source_target_pairs={{2,6},{3,1},{6,10},{7,3},{10,14},{11,7},{14,12},{15,11},{12,8},{13... | collective-permute-start | bytes 877832 | tf_op jit(solution)/shard_map/ppermute | solution.py:323
  33.1 6.8 %collective-permute-start.8 = (bf16[320,254]{1,0:T(8,128)(2,1)S(1)}, bf16[320,254]{1,0:T(8,128)(2,1)S(1)}, u32[]{:S(2)}, u32[]{:S(2)}) collective-permute-start(bf16[320,254]{1,0:T(8,128)(2,1)S(1)} %slice.7), channel_id=1, source_target_pairs={{2,0},{3,7},{6,2},{7,11},{10,6},{11,15},{14,10},{15,13},{12,14},{1... | collective-permute-start | bytes 487688 | tf_op jit(solution)/shard_map/ppermute | solution.py:337
  34.9 5.0 %collective-permute-start.7 = (bf16[256,254]{1,0:T(8,128)(2,1)S(1)}, bf16[256,254]{1,0:T(8,128)(2,1)S(1)}, u32[]{:S(2)}, u32[]{:S(2)}) collective-permute-start(bf16[256,254]{1,0:T(8,128)(2,1)S(1)} %slice.8), channel_id=1, source_target_pairs={{2,6},{3,1},{6,10},{7,3},{10,14},{11,7},{14,12},{15,11},{12,8},{13... | collective-permute-start | bytes 390152 | tf_op jit(solution)/shard_map/ppermute | solution.py:335
  41.2 1.7 %copy-start = (bf16[8,512,128]{2,1,0:T(8,128)(2,1)S(1)}, bf16[8,512,128]{2,1,0:T(8,128)(2,1)}, u32[]{:S(2)}) copy-start(bf16[8,512,128]{2,1,0:T(8,128)(2,1)} %up_ref.1) | copy-start | bytes 3145732
  41.2 1.7 %collective-permute-start.9 = (bf16[256,640]{1,0:T(8,128)(2,1)S(1)}, bf16[256,640]{1,0:T(8,128)(2,1)S(1)}, u32[]{:S(2)}, u32[]{:S(2)}) collective-permute-start(bf16[256,640]{1,0:T(8,128)(2,1)S(1)} %give.1), channel_id=1, source_target_pairs={{0,1},{1,0},{2,3},{3,2},{4,5},{5,4},{6,7},{7,6},{8,9},{9,8},{10,11... | collective-permute-start | bytes 983048 | tf_op jit(solution)/shard_map/ppermute | solution.py:359

commit v25 on v19

--- a/solution.py
+++ b/solution.py
@@ -108,7 +108,7 @@
 def token_of(index, tokens, chips):
     device, t = parted(index, tokens)
     core, chip = parted(device, chips)
-    return (chip * CORES + ((lax.axis_index("ctx") % CORES) ^ core)) * tokens + t
+    return ((chips - 1 - chip) * CORES + ((lax.axis_index("ctx") % CORES) ^ core)) * tokens + t
 
 
 def with_base(table_ref, at, key_refs):
@@ -132,7 +132,7 @@
     chips = out_ref.shape[0]
     part = queries_ref.shape[1] // chips
     for chip in range(chips):
-        out_ref[chip, :, :part] = queries_ref[:, chip * part:(chip + 1) * part]
+        out_ref[chips - 1 - chip, :, :part] = queries_ref[:, chip * part:(chip + 1) * part]
         out_ref[chip, :, part:] = span_ref[...]
 
 
@@ -226,7 +226,7 @@
     devices, tokens, _ = out_ref.shape
     chips = devices // CORES
     for i in range(devices):
-        out_ref[(i % chips) * CORES + (core ^ (i // chips))] = (
+        out_ref[1 + (i % chips) * CORES - (core ^ (i // chips))] = (
             flat_ref[i * tokens:(i + 1) * tokens, :].astype(bf16)
         )
 
@@ -260,7 +260,7 @@
         ]
 
     other_core = [(d, d ^ 1) for d in range(ctx)]
-    same_core = [[p * CORES + c for p in range(chips)] for c in range(CORES)]
+    same_core = [[p * CORES + c for p in reversed(range(chips))] for c in range(CORES)]
 
     turns = [0]
     for s in range(1, steps):
@@ -370,8 +370,11 @@
         compiler_params=PARAMS,
         name="merge",
     )(keep, got, value_up)
-    returned = lax.all_to_all(merged, "ctx", split_axis=0, concat_axis=0, tiled=True)
-    return returned.transpose(1, 0, 2).reshape(tokens, all_heads * V_HEAD)
+    returned = lax.all_to_all(
+        merged, "ctx", split_axis=0, concat_axis=0, tiled=True,
+        axis_index_groups=[list(range(ctx))[::-1]],
+    )
+    return returned[::-1].transpose(1, 0, 2).reshape(tokens, all_heads * V_HEAD)
 
 
 def solution(mesh):

time: 55.8 us -> 54 us (0.968)
  blocking collectives: 11.5 us -> 8.73 us
  starting transfers between devices: 16.5 us -> 18.4 us
  waiting for transfers between devices: 14.5 us -> 13.5 us
    all_to_all x1, waiting for transfers between devices: 8.91 us -> 5.77 us  [on_device(): lax.all_to_all(pieces, 'ctx', split_axis=0, concat_axis=0, axis_index_gro...]
    all_to_all x1, blocking collectives: 11.5 us -> 8.73 us  [on_device(): lax.all_to_all(merged, 'ctx', split_axis=0, concat_axis=0, tiled=True, ax...]
    all_to_all x1, starting transfers between devices: 6.26 us -> 8.36 us  [on_device(): lax.all_to_all(pieces, 'ctx', split_axis=0, concat_axis=0, axis_index_gro...]
    ppermute x4, waiting for transfers between devices: 4.06 us -> 5.45 us  [on_device(): right, left = (onward(right), backward(left))]
    ppermute x1, waiting for transfers between devices: 1.05 us -> 1.83 us  [on_device(): top = onward(right[:cut])]
    ppermute x1, starting transfers between devices: 0.83 us -> 0.06 us  [on_device(): top = onward(right[:cut])]
    rev x0 -> x1, local copies, waits for them, and re-layouts: none -> 0.68 us  [on_device(): return returned[::-1].transpose(1, 0, 2).reshape(tokens, all_heads * V_HEAD)]
    unnamed x7 -> x6, local copies, waits for them, and re-layouts: 0.65 us -> 0.02 us
  transfers between devices with their start and end apart: 11 -> 11, of which waited for: 5 -> 5; matrix products, arithmetic and copies ran while one was open for 0% -> 0% of each run, Pallas kernels for 16% -> 17%
where the time goes in v25:
time: 54 us; the launch traced here: 53.7 us
  starting transfers between devices  18.4 us (34%)
  waiting for transfers between devices  13.5 us (25%)
  Pallas kernels  10.7 us (20%)
  blocking collectives  8.73 us (16%)
  between operations  1.44 us (3%)
  local copies, waits for them, and re-layouts  0.94 us (2%)
    all_to_all x1, blocking collectives, on_device(): lax.all_to_all(merged, 'ctx', split_axis=0, concat_axis=0, tiled=True, ax...  8.73 us
    all_to_all x1, starting transfers between devices, on_device(): lax.all_to_all(pieces, 'ctx', split_axis=0, concat_axis=0, axis_index_gro...  8.36 us
    all_to_all x1, waiting for transfers between devices, on_device(): lax.all_to_all(pieces, 'ctx', split_axis=0, concat_axis=0, axis_index_gro...  5.77 us
    ppermute x4, waiting for transfers between devices, on_device(): right, left = (onward(right), backward(left))  5.45 us
    ppermute x4, starting transfers between devices, on_device(): right, left = (onward(right), backward(left))  4.56 us
    pallas_call x1, Pallas kernels, fold_first(): pl.pallas_call(functools.partial(first_kernel, heads, len(keys)), out_sha...  3.65 us
    ppermute x2, starting transfers between devices, on_device(): right, left = (onward(own), backward(own))  3.03 us
    pallas_call x1, Pallas kernels, on_device(): pl.pallas_call(functools.partial(span_kernel, at, len(keys)), out_shape=s...  2.47 us
  transfers between devices with their start and end apart: 11, of which 5 were waited for; matrix products, arithmetic and copies ran while one was open for 0% of the time, Pallas kernels for 17%

profile of v25, /device:TPU:0, one launch (start us, length us, event | category | flops | bytes accessed | tf_op | source)
XLA Modules:
  0.0 53.7 jit_solution(17122710474335630807)
XLA Ops:
  0.0 2.9 %collective-permute-start.1 = (bf16[576,254]{1,0:T(8,128)(2,1)}, bf16[576,254]{1,0:T(8,128)(2,1)S(1)}, u32[]{:S(2)}, u32[]{:S(2)}) collective-permute-start(bf16[576,254]{1,0:T(8,128)(2,1)} %bitcast.4), channel_id=1, source_target_pairs={{2,6},{3,1},{6,10},{7,3},{10,14},{11,7},{14,12},{15,11},{12,8},{13... | collective-permute-start | bytes 877832 | tf_op jit(solution)/shard_map/ppermute | solution.py:303
  2.9 0.1 collective-permute-start.2
  3.0 1.7 %pieces.1 = bf16[8,2,9792]{2,1,0:T(2,128)(2,1)} custom-call(bf16[2,73728]{1,0:T(2,128)(2,1)} %queries_hbm.1, bf16[2,576]{1,0:T(2,128)(2,1)} %span_hbm.1), custom_call_target="tpu_custom_call" | custom-call | tf_op jit(solution)/shard_map/pieces/pallas_call | solution.py:306
  4.8 8.4 %all-to-all-start = ((bf16[8,2,9792]{2,1,0:T(2,128)(2,1)}), bf16[8,2,9792]{2,1,0:T(2,128)(2,1)S(1)}, u32[]{:S(2)}, u32[]{:S(2)}) async-start(bf16[8,2,9792]{2,1,0:T(2,128)(2,1)} %pieces.1), calls=%async_computation | async-start | bytes 630784 | tf_op jit(solution)/shard_map/all_to_all | solution.py:319
  13.1 0.0 copy-start.1
  13.1 0.0 collective-permute-done.1.rest_1_
  13.1 0.0 collective-permute-done.2.rest_2_
  13.1 0.6 %collective-permute-start.4 = (bf16[576,254]{1,0:T(8,128)(2,1)S(1)}, bf16[576,254]{1,0:T(8,128)(2,1)S(1)}, u32[]{:S(2)}, u32[]{:S(2)}) collective-permute-start(bf16[576,254]{1,0:T(8,128)(2,1)S(1)} %collective-permute-done.2.rest_2_), channel_id=1, source_target_pairs={{2,0},{3,7},{6,2},{7,11},{10,6},{11,15},{14,10},{15,13},{12,14},{1... | collective-permute-start | bytes 877832 | tf_op jit(solution)/shard_map/ppermute | solution.py:326
  13.7 1.5 %collective-permute-start.3 = (bf16[576,254]{1,0:T(8,128)(2,1)S(1)}, bf16[576,254]{1,0:T(8,128)(2,1)S(1)}, u32[]{:S(2)}, u32[]{:S(2)}) collective-permute-start(bf16[576,254]{1,0:T(8,128)(2,1)S(1)} %collective-permute-done.1.rest_1_), channel_id=1, source_target_pairs={{2,6},{3,1},{6,10},{7,3},{10,14},{11,7},{14,12},{15,11},{12,8},{13... | collective-permute-start | bytes 877832 | tf_op jit(solution)/shard_map/ppermute | solution.py:326
  15.2 5.8 %all-to-all-done = bf16[8,2,9792]{2,1,0:T(2,128)(2,1)S(1)} async-done(((bf16[8,2,9792]{2,1,0:T(2,128)(2,1)}), bf16[8,2,9792]{2,1,0:T(2,128)(2,1)S(1)}, u32[]{:S(2)}, u32[]{:S(2)}) %all-to-all-start) | async-done | bytes 313376 | tf_op jit(solution)/shard_map/all_to_all | solution.py:319
  21.0 0.2 reshape.6.here_ref
  21.2 0.0 copy-start.2
  21.2 0.1 collective-permute-start
  21.3 2.8 %collective-permute-done.4.rest_4_ = bf16[576,254]{1,0:T(8,128)(2,1)S(1)} collective-permute-done((bf16[576,254]{1,0:T(8,128)(2,1)S(1)}, bf16[576,254]{1,0:T(8,128)(2,1)S(1)}, u32[]{:S(2)}, u32[]{:S(2)}) %collective-permute-start.4) | collective-permute-done | bytes 292640 | tf_op jit(solution)/shard_map/ppermute | solution.py:326
  24.1 2.5 %collective-permute-start.5 = (bf16[576,254]{1,0:T(8,128)(2,1)S(1)}, bf16[576,254]{1,0:T(8,128)(2,1)S(1)}, u32[]{:S(2)}, u32[]{:S(2)}) collective-permute-start(bf16[576,254]{1,0:T(8,128)(2,1)S(1)} %collective-permute-done.4.rest_4_), channel_id=1, source_target_pairs={{2,0},{3,7},{6,2},{7,11},{10,6},{11,15},{14,10},{15,13},{12,14},{1... | collective-permute-start | bytes 877832 | tf_op jit(solution)/shard_map/ppermute | solution.py:326
  26.6 0.0 collective-permute-done.3.rest_3_
  26.6 0.0 collective-permute-start.6
  27.2 0.0 collective-permute-done.there_ref
  27.2 0.0 copy-done.1
  27.3 0.0 copy-done.2
  27.3 3.7 %first.1 = (bf16[512,576]{1,0:T(8,128)(2,1)S(1)}, f32[512,128]{1,0:T(8,128)S(1)}, f32[512,128]{1,0:T(8,128)S(1)}, f32[512,512]{1,0:T(8,128)S(1)}) custom-call(s32[1]{0:T(128)S(6)} %copy.8.length_ref, s32[128]{0:T(128)S(1)} %copy-done.2, bf16[16,9792]{1,0:T(8,128)(2,1)S(1)} %reshape.6.here_ref, bf16[16,9792]{1,0:T(8,128)(2,1)S(1)} %collective-permute-done.there_ref, ...), custom_call_target="tpu_custom_call" | custom-call | tf_op jit(solution)/shard_map/first/pallas_call | solution.py:280
  30.9 2.7 %collective-permute-done.5.rest_1_ = bf16[576,254]{1,0:T(8,128)(2,1)S(1)} collective-permute-done((bf16[576,254]{1,0:T(8,128)(2,1)S(1)}, bf16[576,254]{1,0:T(8,128)(2,1)S(1)}, u32[]{:S(2)}, u32[]{:S(2)}) %collective-permute-start.5) | collective-permute-done | bytes 292640 | tf_op jit(solution)/shard_map/ppermute | solution.py:326
  33.6 2.3 %collective-permute-start.8 = (bf16[320,254]{1,0:T(8,128)(2,1)S(1)}, bf16[320,254]{1,0:T(8,128)(2,1)S(1)}, u32[]{:S(2)}, u32[]{:S(2)}) collective-permute-start(bf16[320,254]{1,0:T(8,128)(2,1)S(1)} %slice.7), channel_id=1, source_target_pairs={{2,0},{3,7},{6,2},{7,11},{10,6},{11,15},{14,10},{15,13},{12,14},{1... | collective-permute-start | bytes 487688 | tf_op jit(solution)/shard_map/ppermute | solution.py:340
  35.9 0.0 collective-permute-done.6.rest_0_
  35.9 0.1 collective-permute-start.7
  36.6 2.5 %middle.1 = (f32[512,128]{1,0:T(8,128)S(1)}, f32[512,128]{1,0:T(8,128)S(1)}, f32[512,512]{1,0:T(8,128)S(1)}) custom-call(s32[1]{0:T(128)S(6)} %copy.8.length_ref, s32[1]{0:T(128)S(6)} %copy.9.offset_ref, s32[128]{0:T(128)S(1)} %copy-done.2, bf16[512,576]{1,0:T(8,128)(2,1)S(1)} %get-tuple-element.20.q_ref, f32[512,128]{1,0:T(8,128)S(1)} %get-tuple-element.24.m_in, ...), custom_call_target="tpu_custom_call" | custom-call | tf_op jit(solution)/shard_map/middle/pallas_call | solution.py:341
  39.1 1.8 %collective-permute-done.7.top_ref = bf16[256,254]{1,0:T(8,128)(2,1)S(1)} collective-permute-done((bf16[256,254]{1,0:T(8,128)(2,1)S(1)}, bf16[256,254]{1,0:T(8,128)(2,1)S(1)}, u32[]{:S(2)}, u32[]{:S(2)}) %collective-permute-start.7) | collective-permute-done | bytes 130080 | tf_op jit(solution)/shard_map/ppermute | solution.py:338
  40.9 0.0 collective-permute-done.8.bottom_ref
  40.9 1.2 %give.1 = bf16[256,640]{1,0:T(8,128)(2,1)S(1)} custom-call(s32[1]{0:T(128)S(6)} %copy.8.length_ref, s32[128]{0:T(128)S(1)} %copy-done.2, bf16[512,576]{1,0:T(8,128)(2,1)S(1)} %get-tuple-element.20.q_ref, f32[512,128]{1,0:T(8,128)S(1)} %get-tuple-element.27.m_ref, f32[512,128]{1,0:T(8,128)S(1)} %get-tuple-element.28.l_ref, ...), custom_call_target="tpu_custom_call" | custom-call | tf_op jit(solution)/shard_map/give/pallas_call | solution.py:353
  42.1 0.0 copy-start
  42.1 0.1 collective-permute-start.9
  42.2 1.2 %keep.1.keep_ref = f32[256,640]{1,0:T(8,128)S(1)} custom-call(s32[1]{0:T(128)S(6)} %copy.8.length_ref, s32[128]{0:T(128)S(1)} %copy-done.2, bf16[512,576]{1,0:T(8,128)(2,1)S(1)} %get-tuple-element.20.q_ref, f32[512,128]{1,0:T(8,128)S(1)} %get-tuple-element.27.m_ref, f32[512,128]{1,0:T(8,128)S(1)} %get-tuple-element.28.l_ref, ...), custom_call_target="tpu_custom_call" | custom-call | tf_op jit(solution)/shard_map/keep/pallas_call | solution.py:353
  43.4 0.4 collective-permute-done.9.got_ref
  43.8 0.0 copy-done
  43.8 0.5 merge.1
  44.3 8.7 %all_to_all.10 = bf16[16,2,1024]{2,1,0:T(2,128)(2,1)S(1)} all-to-all(bf16[16,2,1024]{2,1,0:T(2,128)(2,1)S(1)} %merge.1), channel_id=1, replica_groups={{15,14,13,12,11,10,9,8,7,6,5,4,3,2,1,0},{31,30,29,28,27,26,25,24,23,22,..., dimensions={0} | all-to-all | bytes 131072 | tf_op jit(solution)/shard_map/all_to_all | solution.py:373
  53.1 0.7 %rev.3 = bf16[16,2,1024]{2,1,0:T(2,128)(2,1)} reverse(bf16[16,2,1024]{2,1,0:T(2,128)(2,1)S(1)} %all_to_all.10), dimensions={0} | reverse | bytes 131072 | tf_op jit(solution)/shard_map/rev | solution.py:377
  (2 shorter events, 0.0 us)
Async XLA Ops:
  0.0 13.1 %collective-permute-start.1 = (bf16[576,254]{1,0:T(8,128)(2,1)}, bf16[576,254]{1,0:T(8,128)(2,1)S(1)}, u32[]{:S(2)}, u32[]{:S(2)}) collective-permute-start(bf16[576,254]{1,0:T(8,128)(2,1)} %bitcast.4), channel_id=1, source_target_pairs={{2,6},{3,1},{6,10},{7,3},{10,14},{11,7},{14,12},{15,11},{12,8},{13... | collective-permute-start | bytes 877832 | tf_op jit(solution)/shard_map/ppermute | solution.py:303
  2.9 10.2 %collective-permute-start.2 = (bf16[576,254]{1,0:T(8,128)(2,1)}, bf16[576,254]{1,0:T(8,128)(2,1)S(1)}, u32[]{:S(2)}, u32[]{:S(2)}) collective-permute-start(bf16[576,254]{1,0:T(8,128)(2,1)} %bitcast.5), channel_id=1, source_target_pairs={{2,0},{3,7},{6,2},{7,11},{10,6},{11,15},{14,10},{15,13},{12,14},{1... | collective-permute-start | bytes 877832 | tf_op jit(solution)/shard_map/ppermute | solution.py:303
  4.8 16.2 %all-to-all-start = ((bf16[8,2,9792]{2,1,0:T(2,128)(2,1)}), bf16[8,2,9792]{2,1,0:T(2,128)(2,1)S(1)}, u32[]{:S(2)}, u32[]{:S(2)}) async-start(bf16[8,2,9792]{2,1,0:T(2,128)(2,1)} %pieces.1), calls=%async_computation | async-start | bytes 630784 | tf_op jit(solution)/shard_map/all_to_all | solution.py:319
  13.1 14.1 %copy-start.1 = (bf16[254,576]{0,1:T(8,128)(2,1)S(1)}, bf16[254,576]{0,1:T(8,128)(2,1)}, u32[]{:S(2)}) copy-start(bf16[254,576]{0,1:T(8,128)(2,1)} %param.8) | copy-start | bytes 877828
  13.1 11.0 %collective-permute-start.4 = (bf16[576,254]{1,0:T(8,128)(2,1)S(1)}, bf16[576,254]{1,0:T(8,128)(2,1)S(1)}, u32[]{:S(2)}, u32[]{:S(2)}) collective-permute-start(bf16[576,254]{1,0:T(8,128)(2,1)S(1)} %collective-permute-done.2.rest_2_), channel_id=1, source_target_pairs={{2,0},{3,7},{6,2},{7,11},{10,6},{11,15},{14,10},{15,13},{12,14},{1... | collective-permute-start | bytes 877832 | tf_op jit(solution)/shard_map/ppermute | solution.py:326
  13.7 12.8 %collective-permute-start.3 = (bf16[576,254]{1,0:T(8,128)(2,1)S(1)}, bf16[576,254]{1,0:T(8,128)(2,1)S(1)}, u32[]{:S(2)}, u32[]{:S(2)}) collective-permute-start(bf16[576,254]{1,0:T(8,128)(2,1)S(1)} %collective-permute-done.1.rest_1_), channel_id=1, source_target_pairs={{2,6},{3,1},{6,10},{7,3},{10,14},{11,7},{14,12},{15,11},{12,8},{13... | collective-permute-start | bytes 877832 | tf_op jit(solution)/shard_map/ppermute | solution.py:326
  21.2 6.0 %copy-start.2 = (s32[128]{0:T(128)S(1)}, s32[128]{0:T(128)}, u32[]{:S(2)}) copy-start(s32[128]{0:T(128)} %constant.2.clone.table_ref) | copy-start | bytes 1540
  21.2 6.0 %collective-permute-start = (bf16[16,9792]{1,0:T(8,128)(2,1)S(1)}, bf16[16,9792]{1,0:T(8,128)(2,1)S(1)}, u32[]{:S(2)}, u32[]{:S(2)}) collective-permute-start(bf16[16,9792]{1,0:T(8,128)(2,1)S(1)} %reshape.6.here_ref), channel_id=1, source_target_pairs={{0,1},{1,0},{2,3},{3,2},{4,5},{5,4},{6,7},{7,6},{8,9},{9,8},{10,11... | collective-permute-start | bytes 940040 | tf_op jit(solution)/shard_map/ppermute | solution.py:329
  24.1 9.5 %collective-permute-start.5 = (bf16[576,254]{1,0:T(8,128)(2,1)S(1)}, bf16[576,254]{1,0:T(8,128)(2,1)S(1)}, u32[]{:S(2)}, u32[]{:S(2)}) collective-permute-start(bf16[576,254]{1,0:T(8,128)(2,1)S(1)} %collective-permute-done.4.rest_4_), channel_id=1, source_target_pairs={{2,0},{3,7},{6,2},{7,11},{10,6},{11,15},{14,10},{15,13},{12,14},{1... | collective-permute-start | bytes 877832 | tf_op jit(solution)/shard_map/ppermute | solution.py:326
  26.6 9.3 %collective-permute-start.6 = (bf16[576,254]{1,0:T(8,128)(2,1)S(1)}, bf16[576,254]{1,0:T(8,128)(2,1)S(1)}, u32[]{:S(2)}, u32[]{:S(2)}) collective-permute-start(bf16[576,254]{1,0:T(8,128)(2,1)S(1)} %collective-permute-done.3.rest_3_), channel_id=1, source_target_pairs={{2,6},{3,1},{6,10},{7,3},{10,14},{11,7},{14,12},{15,11},{12,8},{13... | collective-permute-start | bytes 877832 | tf_op jit(solution)/shard_map/ppermute | solution.py:326
  33.6 7.3 %collective-permute-start.8 = (bf16[320,254]{1,0:T(8,128)(2,1)S(1)}, bf16[320,254]{1,0:T(8,128)(2,1)S(1)}, u32[]{:S(2)}, u32[]{:S(2)}) collective-permute-start(bf16[320,254]{1,0:T(8,128)(2,1)S(1)} %slice.7), channel_id=1, source_target_pairs={{2,0},{3,7},{6,2},{7,11},{10,6},{11,15},{14,10},{15,13},{12,14},{1... | collective-permute-start | bytes 487688 | tf_op jit(solution)/shard_map/ppermute | solution.py:340
  35.9 5.0 %collective-permute-start.7 = (bf16[256,254]{1,0:T(8,128)(2,1)S(1)}, bf16[256,254]{1,0:T(8,128)(2,1)S(1)}, u32[]{:S(2)}, u32[]{:S(2)}) collective-permute-start(bf16[256,254]{1,0:T(8,128)(2,1)S(1)} %slice.8), channel_id=1, source_target_pairs={{2,6},{3,1},{6,10},{7,3},{10,14},{11,7},{14,12},{15,11},{12,8},{13... | collective-permute-start | bytes 390152 | tf_op jit(solution)/shard_map/ppermute | solution.py:338
  42.1 1.7 %copy-start = (bf16[8,512,128]{2,1,0:T(8,128)(2,1)S(1)}, bf16[8,512,128]{2,1,0:T(8,128)(2,1)}, u32[]{:S(2)}) copy-start(bf16[8,512,128]{2,1,0:T(8,128)(2,1)} %up_ref.1) | copy-start | bytes 3145732
  42.1 1.7 %collective-permute-start.9 = (bf16[256,640]{1,0:T(8,128)(2,1)S(1)}, bf16[256,640]{1,0:T(8,128)(2,1)S(1)}, u32[]{:S(2)}, u32[]{:S(2)}) collective-permute-start(bf16[256,640]{1,0:T(8,128)(2,1)S(1)} %give.1), channel_id=1, source_target_pairs={{0,1},{1,0},{2,3},{3,2},{4,5},{5,4},{6,7},{7,6},{8,9},{9,8},{10,11... | collective-permute-start | bytes 983048 | tf_op jit(solution)/shard_map/ppermute | solution.py:362

commit v26 on v24

--- a/solution.py
+++ b/solution.py
@@ -224,9 +224,18 @@
     devices, tokens, _ = out_ref.shape
     chips = devices // CORES
     for i in range(devices):
-        out_ref[devices - 1 - (i % chips) * CORES - (core ^ (i // chips))] = (
+        out_ref[(1 - (core ^ (i // chips))) * chips + chips - 1 - i % chips] = (
             flat_ref[i * tokens:(i + 1) * tokens, :].astype(bf16)
         )
+
+
+def place_kernel(parts_ref, out_ref):
+    devices, _, width = parts_ref.shape
+    chips = devices // CORES
+    for i in range(devices):
+        core, chip = 1 - i // chips, chips - 1 - i % chips
+        at = (chip * CORES + core) * width
+        out_ref[:, at:at + width] = parts_ref[i]
 
 
 VMEM = pl.BlockSpec(memory_space=pltpu.VMEM)
@@ -369,9 +378,18 @@
     )(keep, got, value_up)
     returned = lax.all_to_all(
         merged, "ctx", split_axis=0, concat_axis=0, tiled=True,
-        axis_index_groups=[list(range(ctx))[::-1]],
-    )
-    return returned[::-1].transpose(1, 0, 2).reshape(tokens, all_heads * V_HEAD)
+        axis_index_groups=[
+            [p * CORES + c for c in reversed(range(CORES)) for p in reversed(range(chips))]
+        ],
+    )
+    return pl.pallas_call(
+        place_kernel,
+        out_shape=shape(tokens, all_heads * V_HEAD, dtype=bf16),
+        in_specs=[VMEM],
+        out_specs=VMEM,
+        compiler_params=PARAMS,
+        name="place",
+    )(returned)
 
 
 def solution(mesh):

time: 53 us -> 52.9 us (level)
  local copies, waits for them, and re-layouts: 0.94 us -> 0.27 us
  Pallas kernels: 10.7 us -> 11.3 us
    rev x1 -> x0, local copies, waits for them, and re-layouts: 0.68 us -> none  [on_device(): return returned[::-1].transpose(1, 0, 2).reshape(tokens, all_heads * V_HEAD)]
    pallas_call x0 -> x1, Pallas kernels: none -> 0.63 us  [on_device(): pl.pallas_call(place_kernel, out_shape=shape(tokens, all_heads * V_HEAD,...]
where the time goes in v26:
time: 52.9 us; the launch traced here: 52.6 us
  starting transfers between devices  16.5 us (31%)
  waiting for transfers between devices  14.5 us (27%)
  Pallas kernels  11.3 us (21%)
  blocking collectives  8.62 us (16%)
  between operations  1.44 us (3%)
    all_to_all x1, waiting for transfers between devices, on_device(): lax.all_to_all(pieces, 'ctx', split_axis=0, concat_axis=0, axis_index_gro...  8.91 us
    all_to_all x1, blocking collectives, on_device(): lax.all_to_all(merged, 'ctx', split_axis=0, concat_axis=0, tiled=True, ax...  8.62 us
    all_to_all x1, starting transfers between devices, on_device(): lax.all_to_all(pieces, 'ctx', split_axis=0, concat_axis=0, axis_index_gro...  6.26 us
    ppermute x4, starting transfers between devices, on_device(): right, left = (onward(right), backward(left))  4.45 us
    ppermute x4, waiting for transfers between devices, on_device(): right, left = (onward(right), backward(left))  4.06 us
    pallas_call x1, Pallas kernels, fold_first(): pl.pallas_call(functools.partial(first_kernel, heads, len(keys)), out_sha...  3.65 us
    ppermute x2, starting transfers between devices, on_device(): right, left = (onward(own), backward(own))  3.03 us
    pallas_call x1, Pallas kernels, on_device(): pl.pallas_call(functools.partial(span_kernel, at, len(keys)), out_shape=s...  2.47 us
  transfers between devices with their start and end apart: 11, of which 5 were waited for; matrix products, arithmetic and copies ran while one was open for 0% of the time, Pallas kernels for 17%

profile of v26, /device:TPU:0, one launch (start us, length us, event | category | flops | bytes accessed | tf_op | source)
XLA Modules:
  0.0 52.6 jit_solution(4016305552309622002)
XLA Ops:
  0.0 2.9 %collective-permute-start.1 = (bf16[576,254]{1,0:T(8,128)(2,1)}, bf16[576,254]{1,0:T(8,128)(2,1)S(1)}, u32[]{:S(2)}, u32[]{:S(2)}) collective-permute-start(bf16[576,254]{1,0:T(8,128)(2,1)} %bitcast.4), channel_id=1, source_target_pairs={{2,6},{3,1},{6,10},{7,3},{10,14},{11,7},{14,12},{15,11},{12,8},{13... | collective-permute-start | bytes 877832 | tf_op jit(solution)/shard_map/ppermute | solution.py:310
  2.9 0.1 collective-permute-start.2
  3.0 1.7 %pieces.1 = bf16[8,2,9792]{2,1,0:T(2,128)(2,1)} custom-call(bf16[8,2,9216]{2,1,0:T(2,128)(2,1)} %bitcast.7, bf16[2,576]{1,0:T(2,128)(2,1)} %span_hbm.1), custom_call_target="tpu_custom_call" | custom-call | tf_op jit(solution)/shard_map/pieces/pallas_call | solution.py:313
  4.7 6.3 %all-to-all-start = ((bf16[8,2,9792]{2,1,0:T(2,128)(2,1)}), bf16[8,2,9792]{2,1,0:T(2,128)(2,1)S(1)}, u32[]{:S(2)}, u32[]{:S(2)}) async-start(bf16[8,2,9792]{2,1,0:T(2,128)(2,1)} %pieces.1), calls=%async_computation | async-start | bytes 630784 | tf_op jit(solution)/shard_map/all_to_all | solution.py:325
  11.0 0.0 copy-start.1
  11.0 0.0 collective-permute-done.1.rest_1_
  11.0 0.0 collective-permute-done.2.rest_2_
  11.0 2.1 %collective-permute-start.4 = (bf16[576,254]{1,0:T(8,128)(2,1)S(1)}, bf16[576,254]{1,0:T(8,128)(2,1)S(1)}, u32[]{:S(2)}, u32[]{:S(2)}) collective-permute-start(bf16[576,254]{1,0:T(8,128)(2,1)S(1)} %collective-permute-done.2.rest_2_), channel_id=1, source_target_pairs={{2,0},{3,7},{6,2},{7,11},{10,6},{11,15},{14,10},{15,13},{12,14},{1... | collective-permute-start | bytes 877832 | tf_op jit(solution)/shard_map/ppermute | solution.py:332
  13.1 0.1 collective-permute-start.3
  13.2 8.9 %all-to-all-done = bf16[8,2,9792]{2,1,0:T(2,128)(2,1)S(1)} async-done(((bf16[8,2,9792]{2,1,0:T(2,128)(2,1)}), bf16[8,2,9792]{2,1,0:T(2,128)(2,1)S(1)}, u32[]{:S(2)}, u32[]{:S(2)}) %all-to-all-start) | async-done | bytes 313376 | tf_op jit(solution)/shard_map/all_to_all | solution.py:325
  22.1 0.2 reshape.7.here_ref
  22.3 0.0 copy-start.2
  22.3 0.1 collective-permute-start
  22.4 1.0 %collective-permute-done.4.rest_4_ = bf16[576,254]{1,0:T(8,128)(2,1)S(1)} collective-permute-done((bf16[576,254]{1,0:T(8,128)(2,1)S(1)}, bf16[576,254]{1,0:T(8,128)(2,1)S(1)}, u32[]{:S(2)}, u32[]{:S(2)}) %collective-permute-start.4) | collective-permute-done | bytes 292640 | tf_op jit(solution)/shard_map/ppermute | solution.py:332
  23.4 1.7 %collective-permute-start.5 = (bf16[576,254]{1,0:T(8,128)(2,1)S(1)}, bf16[576,254]{1,0:T(8,128)(2,1)S(1)}, u32[]{:S(2)}, u32[]{:S(2)}) collective-permute-start(bf16[576,254]{1,0:T(8,128)(2,1)S(1)} %collective-permute-done.4.rest_4_), channel_id=1, source_target_pairs={{2,0},{3,7},{6,2},{7,11},{10,6},{11,15},{14,10},{15,13},{12,14},{1... | collective-permute-start | bytes 877832 | tf_op jit(solution)/shard_map/ppermute | solution.py:332
  25.1 0.0 collective-permute-done.3.rest_3_
  25.1 0.6 %collective-permute-start.6 = (bf16[576,254]{1,0:T(8,128)(2,1)S(1)}, bf16[576,254]{1,0:T(8,128)(2,1)S(1)}, u32[]{:S(2)}, u32[]{:S(2)}) collective-permute-start(bf16[576,254]{1,0:T(8,128)(2,1)S(1)} %collective-permute-done.3.rest_3_), channel_id=1, source_target_pairs={{2,6},{3,1},{6,10},{7,3},{10,14},{11,7},{14,12},{15,11},{12,8},{13... | collective-permute-start | bytes 877832 | tf_op jit(solution)/shard_map/ppermute | solution.py:332
  26.4 0.0 collective-permute-done.there_ref
  26.4 0.0 copy-done.1
  26.4 0.0 copy-done.2
  26.4 3.7 %first.1 = (bf16[512,576]{1,0:T(8,128)(2,1)S(1)}, f32[512,128]{1,0:T(8,128)S(1)}, f32[512,128]{1,0:T(8,128)S(1)}, f32[512,512]{1,0:T(8,128)S(1)}) custom-call(s32[1]{0:T(128)S(6)} %copy.8.length_ref, s32[128]{0:T(128)S(1)} %copy-done.2, bf16[16,9792]{1,0:T(8,128)(2,1)S(1)} %reshape.7.here_ref, bf16[16,9792]{1,0:T(8,128)(2,1)S(1)} %collective-permute-done.there_ref, ...), custom_call_target="tpu_custom_call" | custom-call | tf_op jit(solution)/shard_map/first/pallas_call | solution.py:287
  30.0 3.1 %collective-permute-done.5.rest_1_ = bf16[576,254]{1,0:T(8,128)(2,1)S(1)} collective-permute-done((bf16[576,254]{1,0:T(8,128)(2,1)S(1)}, bf16[576,254]{1,0:T(8,128)(2,1)S(1)}, u32[]{:S(2)}, u32[]{:S(2)}) %collective-permute-start.5) | collective-permute-done | bytes 292640 | tf_op jit(solution)/shard_map/ppermute | solution.py:332
  33.1 1.8 %collective-permute-start.8 = (bf16[320,254]{1,0:T(8,128)(2,1)S(1)}, bf16[320,254]{1,0:T(8,128)(2,1)S(1)}, u32[]{:S(2)}, u32[]{:S(2)}) collective-permute-start(bf16[320,254]{1,0:T(8,128)(2,1)S(1)} %slice.7), channel_id=1, source_target_pairs={{2,0},{3,7},{6,2},{7,11},{10,6},{11,15},{14,10},{15,13},{12,14},{1... | collective-permute-start | bytes 487688 | tf_op jit(solution)/shard_map/ppermute | solution.py:346
  34.9 0.0 collective-permute-done.6.rest_0_
  34.9 0.8 %collective-permute-start.7 = (bf16[256,254]{1,0:T(8,128)(2,1)S(1)}, bf16[256,254]{1,0:T(8,128)(2,1)S(1)}, u32[]{:S(2)}, u32[]{:S(2)}) collective-permute-start(bf16[256,254]{1,0:T(8,128)(2,1)S(1)} %slice.8), channel_id=1, source_target_pairs={{2,6},{3,1},{6,10},{7,3},{10,14},{11,7},{14,12},{15,11},{12,8},{13... | collective-permute-start | bytes 390152 | tf_op jit(solution)/shard_map/ppermute | solution.py:344
  36.4 2.5 %middle.1 = (f32[512,128]{1,0:T(8,128)S(1)}, f32[512,128]{1,0:T(8,128)S(1)}, f32[512,512]{1,0:T(8,128)S(1)}) custom-call(s32[1]{0:T(128)S(6)} %copy.8.length_ref, s32[1]{0:T(128)S(6)} %copy.9.offset_ref, s32[128]{0:T(128)S(1)} %copy-done.2, bf16[512,576]{1,0:T(8,128)(2,1)S(1)} %get-tuple-element.20.q_ref, f32[512,128]{1,0:T(8,128)S(1)} %get-tuple-element.24.m_in, ...), custom_call_target="tpu_custom_call" | custom-call | tf_op jit(solution)/shard_map/middle/pallas_call | solution.py:347
  38.9 1.1 %collective-permute-done.7.top_ref = bf16[256,254]{1,0:T(8,128)(2,1)S(1)} collective-permute-done((bf16[256,254]{1,0:T(8,128)(2,1)S(1)}, bf16[256,254]{1,0:T(8,128)(2,1)S(1)}, u32[]{:S(2)}, u32[]{:S(2)}) %collective-permute-start.7) | collective-permute-done | bytes 130080 | tf_op jit(solution)/shard_map/ppermute | solution.py:344
  39.9 0.0 collective-permute-done.8.bottom_ref
  39.9 1.2 %give.1 = bf16[256,640]{1,0:T(8,128)(2,1)S(1)} custom-call(s32[1]{0:T(128)S(6)} %copy.8.length_ref, s32[128]{0:T(128)S(1)} %copy-done.2, bf16[512,576]{1,0:T(8,128)(2,1)S(1)} %get-tuple-element.20.q_ref, f32[512,128]{1,0:T(8,128)S(1)} %get-tuple-element.27.m_ref, f32[512,128]{1,0:T(8,128)S(1)} %get-tuple-element.28.l_ref, ...), custom_call_target="tpu_custom_call" | custom-call | tf_op jit(solution)/shard_map/give/pallas_call | solution.py:359
  41.2 0.0 copy-start
  41.2 0.1 collective-permute-start.9
  41.2 1.2 %keep.1.keep_ref = f32[256,640]{1,0:T(8,128)S(1)} custom-call(s32[1]{0:T(128)S(6)} %copy.8.length_ref, s32[128]{0:T(128)S(1)} %copy-done.2, bf16[512,576]{1,0:T(8,128)(2,1)S(1)} %get-tuple-element.20.q_ref, f32[512,128]{1,0:T(8,128)S(1)} %get-tuple-element.27.m_ref, f32[512,128]{1,0:T(8,128)S(1)} %get-tuple-element.28.l_ref, ...), custom_call_target="tpu_custom_call" | custom-call | tf_op jit(solution)/shard_map/keep/pallas_call | solution.py:359
  42.4 0.4 collective-permute-done.9.got_ref
  42.9 0.0 copy-done
  42.9 0.5 merge.1
  43.4 8.6 %all_to_all.10.parts_ref = bf16[16,2,1024]{2,1,0:T(2,128)(2,1)S(1)} all-to-all(bf16[16,2,1024]{2,1,0:T(2,128)(2,1)S(1)} %merge.1), channel_id=1, replica_groups={{15,13,11,9,7,5,3,1,14,12,10,8,6,4,2,0},{31,29,27,25,23,21,19,17,30,28,..., dimensions={0} | all-to-all | bytes 131072 | tf_op jit(solution)/shard_map/all_to_all | solution.py:379
  52.0 0.6 %place.1 = bf16[2,16384]{1,0:T(2,128)(2,1)} custom-call(bf16[16,2,1024]{2,1,0:T(2,128)(2,1)S(1)} %all_to_all.10.parts_ref), custom_call_target="tpu_custom_call" | custom-call | tf_op jit(solution)/shard_map/place/pallas_call | solution.py:385
  (2 shorter events, 0.0 us)
Async XLA Ops:
  0.0 11.0 %collective-permute-start.1 = (bf16[576,254]{1,0:T(8,128)(2,1)}, bf16[576,254]{1,0:T(8,128)(2,1)S(1)}, u32[]{:S(2)}, u32[]{:S(2)}) collective-permute-start(bf16[576,254]{1,0:T(8,128)(2,1)} %bitcast.4), channel_id=1, source_target_pairs={{2,6},{3,1},{6,10},{7,3},{10,14},{11,7},{14,12},{15,11},{12,8},{13... | collective-permute-start | bytes 877832 | tf_op jit(solution)/shard_map/ppermute | solution.py:310
  2.9 8.1 %collective-permute-start.2 = (bf16[576,254]{1,0:T(8,128)(2,1)}, bf16[576,254]{1,0:T(8,128)(2,1)S(1)}, u32[]{:S(2)}, u32[]{:S(2)}) collective-permute-start(bf16[576,254]{1,0:T(8,128)(2,1)} %bitcast.5), channel_id=1, source_target_pairs={{2,0},{3,7},{6,2},{7,11},{10,6},{11,15},{14,10},{15,13},{12,14},{1... | collective-permute-start | bytes 877832 | tf_op jit(solution)/shard_map/ppermute | solution.py:310
  4.7 17.3 %all-to-all-start = ((bf16[8,2,9792]{2,1,0:T(2,128)(2,1)}), bf16[8,2,9792]{2,1,0:T(2,128)(2,1)S(1)}, u32[]{:S(2)}, u32[]{:S(2)}) async-start(bf16[8,2,9792]{2,1,0:T(2,128)(2,1)} %pieces.1), calls=%async_computation | async-start | bytes 630784 | tf_op jit(solution)/shard_map/all_to_all | solution.py:325
  11.0 15.4 %copy-start.1 = (bf16[254,576]{0,1:T(8,128)(2,1)S(1)}, bf16[254,576]{0,1:T(8,128)(2,1)}, u32[]{:S(2)}) copy-start(bf16[254,576]{0,1:T(8,128)(2,1)} %param.8) | copy-start | bytes 877828
  11.0 12.4 %collective-permute-start.4 = (bf16[576,254]{1,0:T(8,128)(2,1)S(1)}, bf16[576,254]{1,0:T(8,128)(2,1)S(1)}, u32[]{:S(2)}, u32[]{:S(2)}) collective-permute-start(bf16[576,254]{1,0:T(8,128)(2,1)S(1)} %collective-permute-done.2.rest_2_), channel_id=1, source_target_pairs={{2,0},{3,7},{6,2},{7,11},{10,6},{11,15},{14,10},{15,13},{12,14},{1... | collective-permute-start | bytes 877832 | tf_op jit(solution)/shard_map/ppermute | solution.py:332
  13.1 12.0 %collective-permute-start.3 = (bf16[576,254]{1,0:T(8,128)(2,1)S(1)}, bf16[576,254]{1,0:T(8,128)(2,1)S(1)}, u32[]{:S(2)}, u32[]{:S(2)}) collective-permute-start(bf16[576,254]{1,0:T(8,128)(2,1)S(1)} %collective-permute-done.1.rest_1_), channel_id=1, source_target_pairs={{2,6},{3,1},{6,10},{7,3},{10,14},{11,7},{14,12},{15,11},{12,8},{13... | collective-permute-start | bytes 877832 | tf_op jit(solution)/shard_map/ppermute | solution.py:332
  22.3 4.1 %copy-start.2 = (s32[128]{0:T(128)S(1)}, s32[128]{0:T(128)}, u32[]{:S(2)}) copy-start(s32[128]{0:T(128)} %constant.2.clone.table_ref) | copy-start | bytes 1540
  22.3 4.1 %collective-permute-start = (bf16[16,9792]{1,0:T(8,128)(2,1)S(1)}, bf16[16,9792]{1,0:T(8,128)(2,1)S(1)}, u32[]{:S(2)}, u32[]{:S(2)}) collective-permute-start(bf16[16,9792]{1,0:T(8,128)(2,1)S(1)} %reshape.7.here_ref), channel_id=1, source_target_pairs={{0,1},{1,0},{2,3},{3,2},{4,5},{5,4},{6,7},{7,6},{8,9},{9,8},{10,11... | collective-permute-start | bytes 940040 | tf_op jit(solution)/shard_map/ppermute | solution.py:335
  23.4 9.7 %collective-permute-start.5 = (bf16[576,254]{1,0:T(8,128)(2,1)S(1)}, bf16[576,254]{1,0:T(8,128)(2,1)S(1)}, u32[]{:S(2)}, u32[]{:S(2)}) collective-permute-start(bf16[576,254]{1,0:T(8,128)(2,1)S(1)} %collective-permute-done.4.rest_4_), channel_id=1, source_target_pairs={{2,0},{3,7},{6,2},{7,11},{10,6},{11,15},{14,10},{15,13},{12,14},{1... | collective-permute-start | bytes 877832 | tf_op jit(solution)/shard_map/ppermute | solution.py:332
  25.1 9.8 %collective-permute-start.6 = (bf16[576,254]{1,0:T(8,128)(2,1)S(1)}, bf16[576,254]{1,0:T(8,128)(2,1)S(1)}, u32[]{:S(2)}, u32[]{:S(2)}) collective-permute-start(bf16[576,254]{1,0:T(8,128)(2,1)S(1)} %collective-permute-done.3.rest_3_), channel_id=1, source_target_pairs={{2,6},{3,1},{6,10},{7,3},{10,14},{11,7},{14,12},{15,11},{12,8},{13... | collective-permute-start | bytes 877832 | tf_op jit(solution)/shard_map/ppermute | solution.py:332
  33.1 6.8 %collective-permute-start.8 = (bf16[320,254]{1,0:T(8,128)(2,1)S(1)}, bf16[320,254]{1,0:T(8,128)(2,1)S(1)}, u32[]{:S(2)}, u32[]{:S(2)}) collective-permute-start(bf16[320,254]{1,0:T(8,128)(2,1)S(1)} %slice.7), channel_id=1, source_target_pairs={{2,0},{3,7},{6,2},{7,11},{10,6},{11,15},{14,10},{15,13},{12,14},{1... | collective-permute-start | bytes 487688 | tf_op jit(solution)/shard_map/ppermute | solution.py:346
  34.9 5.0 %collective-permute-start.7 = (bf16[256,254]{1,0:T(8,128)(2,1)S(1)}, bf16[256,254]{1,0:T(8,128)(2,1)S(1)}, u32[]{:S(2)}, u32[]{:S(2)}) collective-permute-start(bf16[256,254]{1,0:T(8,128)(2,1)S(1)} %slice.8), channel_id=1, source_target_pairs={{2,6},{3,1},{6,10},{7,3},{10,14},{11,7},{14,12},{15,11},{12,8},{13... | collective-permute-start | bytes 390152 | tf_op jit(solution)/shard_map/ppermute | solution.py:344
  41.2 1.7 %copy-start = (bf16[8,512,128]{2,1,0:T(8,128)(2,1)S(1)}, bf16[8,512,128]{2,1,0:T(8,128)(2,1)}, u32[]{:S(2)}) copy-start(bf16[8,512,128]{2,1,0:T(8,128)(2,1)} %up_ref.1) | copy-start | bytes 3145732
  41.2 1.7 %collective-permute-start.9 = (bf16[256,640]{1,0:T(8,128)(2,1)S(1)}, bf16[256,640]{1,0:T(8,128)(2,1)S(1)}, u32[]{:S(2)}, u32[]{:S(2)}) collective-permute-start(bf16[256,640]{1,0:T(8,128)(2,1)S(1)} %give.1), channel_id=1, source_target_pairs={{0,1},{1,0},{2,3},{3,2},{4,5},{5,4},{6,7},{7,6},{8,9},{9,8},{10,11... | collective-permute-start | bytes 983048 | tf_op jit(solution)/shard_map/ppermute | solution.py:368

commit v27 on v24

--- a/solution.py
+++ b/solution.py
@@ -253,7 +253,7 @@
 
     def across(step):
         return [
-            (walk[r] * CORES + c, walk[(r + (-step if c else step)) % chips] * CORES + c)
+            (walk[r] * CORES + c, walk[(r + (step if c else -step)) % chips] * CORES + c)
             for r in range(chips) for c in range(CORES)
         ]
 
@@ -266,7 +266,7 @@
     turns.append(steps)
     owner_table = np.array(
         [
-            [walk[(spot[p] + (-t if c else t)) % chips] * CORES + c for t in turns]
+            [walk[(spot[p] + (t if c else -t)) % chips] * CORES + c for t in turns]
             for p in range(chips) for c in range(CORES)
         ],
         np.int32,

time: 53 us -> 53.2 us (level)
  blocking collectives: 8.72 us -> 9.27 us
    ppermute x1, starting transfers between devices: 1.78 us -> 0.34 us  [on_device(): bottom = backward(left[cut:])]
    ppermute x1, starting transfers between devices: 0.83 us -> 1.79 us  [on_device(): top = onward(right[:cut])]
    all_to_all x1, blocking collectives: 8.72 us -> 9.27 us  [on_device(): lax.all_to_all(merged, 'ctx', split_axis=0, concat_axis=0, tiled=True, ax...]
where the time goes in v27:
time: 53.2 us; the launch traced here: 52.9 us
  starting transfers between devices  16.4 us (31%)
  waiting for transfers between devices  14.2 us (27%)
  Pallas kernels  10.7 us (20%)
  blocking collectives  9.27 us (17%)
  between operations  1.44 us (3%)
  local copies, waits for them, and re-layouts  0.94 us (2%)
    all_to_all x1, blocking collectives, on_device(): lax.all_to_all(merged, 'ctx', split_axis=0, concat_axis=0, tiled=True, ax...  9.27 us
    all_to_all x1, waiting for transfers between devices, on_device(): lax.all_to_all(pieces, 'ctx', split_axis=0, concat_axis=0, axis_index_gro...  8.91 us
    all_to_all x1, starting transfers between devices, on_device(): lax.all_to_all(pieces, 'ctx', split_axis=0, concat_axis=0, axis_index_gro...  6.26 us
    ppermute x4, starting transfers between devices, on_device(): right, left = (onward(right), backward(left))  4.85 us
    ppermute x4, waiting for transfers between devices, on_device(): right, left = (onward(right), backward(left))  4.27 us
    pallas_call x1, Pallas kernels, fold_first(): pl.pallas_call(functools.partial(first_kernel, heads, len(keys)), out_sha...  3.65 us
    ppermute x2, starting transfers between devices, on_device(): right, left = (onward(own), backward(own))  3.03 us
    pallas_call x1, Pallas kernels, on_device(): pl.pallas_call(functools.partial(span_kernel, at, len(keys)), out_shape=s...  2.48 us
  transfers between devices with their start and end apart: 11, of which 5 were waited for; matrix products, arithmetic and copies ran while one was open for 0% of the time, Pallas kernels for 17%

profile of v27, /device:TPU:0, one launch (start us, length us, event | category | flops | bytes accessed | tf_op | source)
XLA Modules:
  0.0 52.9 jit_solution(8287837706922457834)
XLA Ops:
  0.0 3.0 %collective-permute-start.1 = (bf16[576,254]{1,0:T(8,128)(2,1)}, bf16[576,254]{1,0:T(8,128)(2,1)S(1)}, u32[]{:S(2)}, u32[]{:S(2)}) collective-permute-start(bf16[576,254]{1,0:T(8,128)(2,1)} %bitcast.7), channel_id=1, source_target_pairs={{2,0},{3,7},{6,2},{7,11},{10,6},{11,15},{14,10},{15,13},{12,14},{1... | collective-permute-start | bytes 877832 | tf_op jit(solution)/shard_map/ppermute | solution.py:301
  3.0 0.0 collective-permute-start.2
  3.0 1.7 %pieces.1 = bf16[8,2,9792]{2,1,0:T(2,128)(2,1)} custom-call(bf16[8,2,9216]{2,1,0:T(2,128)(2,1)} %bitcast.10, bf16[2,576]{1,0:T(2,128)(2,1)} %span_hbm.1), custom_call_target="tpu_custom_call" | custom-call | tf_op jit(solution)/shard_map/pieces/pallas_call | solution.py:304
  4.7 6.3 %all-to-all-start = ((bf16[8,2,9792]{2,1,0:T(2,128)(2,1)}), bf16[8,2,9792]{2,1,0:T(2,128)(2,1)S(1)}, u32[]{:S(2)}, u32[]{:S(2)}) async-start(bf16[8,2,9792]{2,1,0:T(2,128)(2,1)} %pieces.1), calls=%async_computation | async-start | bytes 630784 | tf_op jit(solution)/shard_map/all_to_all | solution.py:316
  11.0 0.0 copy-start.1
  11.0 0.0 collective-permute-done.1.rest_1_
  11.0 0.0 collective-permute-done.2.rest_2_
  11.0 2.1 %collective-permute-start.4 = (bf16[576,254]{1,0:T(8,128)(2,1)S(1)}, bf16[576,254]{1,0:T(8,128)(2,1)S(1)}, u32[]{:S(2)}, u32[]{:S(2)}) collective-permute-start(bf16[576,254]{1,0:T(8,128)(2,1)S(1)} %collective-permute-done.2.rest_2_), channel_id=1, source_target_pairs={{2,6},{3,1},{6,10},{7,3},{10,14},{11,7},{14,12},{15,11},{12,8},{13... | collective-permute-start | bytes 877832 | tf_op jit(solution)/shard_map/ppermute | solution.py:323
  13.1 0.1 collective-permute-start.3
  13.2 8.9 %all-to-all-done = bf16[8,2,9792]{2,1,0:T(2,128)(2,1)S(1)} async-done(((bf16[8,2,9792]{2,1,0:T(2,128)(2,1)}), bf16[8,2,9792]{2,1,0:T(2,128)(2,1)S(1)}, u32[]{:S(2)}, u32[]{:S(2)}) %all-to-all-start) | async-done | bytes 313376 | tf_op jit(solution)/shard_map/all_to_all | solution.py:316
  22.1 0.2 reshape.10.here_ref
  22.3 0.0 copy-start.2
  22.3 0.1 collective-permute-start
  22.4 2.3 %collective-permute-done.4.rest_4_ = bf16[576,254]{1,0:T(8,128)(2,1)S(1)} collective-permute-done((bf16[576,254]{1,0:T(8,128)(2,1)S(1)}, bf16[576,254]{1,0:T(8,128)(2,1)S(1)}, u32[]{:S(2)}, u32[]{:S(2)}) %collective-permute-start.4) | collective-permute-done | bytes 292640 | tf_op jit(solution)/shard_map/ppermute | solution.py:323
  24.7 0.0 collective-permute-start.5
  24.7 0.0 collective-permute-done.3.rest_3_
  24.7 2.7 %collective-permute-start.6 = (bf16[576,254]{1,0:T(8,128)(2,1)S(1)}, bf16[576,254]{1,0:T(8,128)(2,1)S(1)}, u32[]{:S(2)}, u32[]{:S(2)}) collective-permute-start(bf16[576,254]{1,0:T(8,128)(2,1)S(1)} %collective-permute-done.3.rest_3_), channel_id=1, source_target_pairs={{2,0},{3,7},{6,2},{7,11},{10,6},{11,15},{14,10},{15,13},{12,14},{1... | collective-permute-start | bytes 877832 | tf_op jit(solution)/shard_map/ppermute | solution.py:323
  28.0 0.0 collective-permute-done.there_ref
  28.0 0.0 copy-done.1
  28.1 0.0 copy-done.2
  28.1 3.7 %first.1 = (bf16[512,576]{1,0:T(8,128)(2,1)S(1)}, f32[512,128]{1,0:T(8,128)S(1)}, f32[512,128]{1,0:T(8,128)S(1)}, f32[512,512]{1,0:T(8,128)S(1)}) custom-call(s32[1]{0:T(128)S(6)} %copy.8.length_ref, s32[128]{0:T(128)S(1)} %copy-done.2, bf16[16,9792]{1,0:T(8,128)(2,1)S(1)} %reshape.10.here_ref, bf16[16,9792]{1,0:T(8,128)(2,1)S(1)} %collective-permute-done.there_ref, ...), custom_call_target="tpu_custom_call" | custom-call | tf_op jit(solution)/shard_map/first/pallas_call | solution.py:278
  31.7 2.0 %collective-permute-done.5.rest_1_ = bf16[576,254]{1,0:T(8,128)(2,1)S(1)} collective-permute-done((bf16[576,254]{1,0:T(8,128)(2,1)S(1)}, bf16[576,254]{1,0:T(8,128)(2,1)S(1)}, u32[]{:S(2)}, u32[]{:S(2)}) %collective-permute-start.5) | collective-permute-done | bytes 292640 | tf_op jit(solution)/shard_map/ppermute | solution.py:323
  33.7 0.3 collective-permute-start.8
  34.1 0.0 collective-permute-done.6.rest_0_
  34.1 1.8 %collective-permute-start.7 = (bf16[256,254]{1,0:T(8,128)(2,1)S(1)}, bf16[256,254]{1,0:T(8,128)(2,1)S(1)}, u32[]{:S(2)}, u32[]{:S(2)}) collective-permute-start(bf16[256,254]{1,0:T(8,128)(2,1)S(1)} %slice.8), channel_id=1, source_target_pairs={{2,0},{3,7},{6,2},{7,11},{10,6},{11,15},{14,10},{15,13},{12,14},{1... | collective-permute-start | bytes 390152 | tf_op jit(solution)/shard_map/ppermute | solution.py:335
  36.5 2.5 %middle.1 = (f32[512,128]{1,0:T(8,128)S(1)}, f32[512,128]{1,0:T(8,128)S(1)}, f32[512,512]{1,0:T(8,128)S(1)}) custom-call(s32[1]{0:T(128)S(6)} %copy.8.length_ref, s32[1]{0:T(128)S(6)} %copy.9.offset_ref, s32[128]{0:T(128)S(1)} %copy-done.2, bf16[512,576]{1,0:T(8,128)(2,1)S(1)} %get-tuple-element.20.q_ref, f32[512,128]{1,0:T(8,128)S(1)} %get-tuple-element.24.m_in, ...), custom_call_target="tpu_custom_call" | custom-call | tf_op jit(solution)/shard_map/middle/pallas_call | solution.py:338
  39.0 0.6 %collective-permute-done.7.top_ref = bf16[256,254]{1,0:T(8,128)(2,1)S(1)} collective-permute-done((bf16[256,254]{1,0:T(8,128)(2,1)S(1)}, bf16[256,254]{1,0:T(8,128)(2,1)S(1)}, u32[]{:S(2)}, u32[]{:S(2)}) %collective-permute-start.7) | collective-permute-done | bytes 130080 | tf_op jit(solution)/shard_map/ppermute | solution.py:335
  39.6 0.0 collective-permute-done.8.bottom_ref
  39.6 1.2 %give.1 = bf16[256,640]{1,0:T(8,128)(2,1)S(1)} custom-call(s32[1]{0:T(128)S(6)} %copy.8.length_ref, s32[128]{0:T(128)S(1)} %copy-done.2, bf16[512,576]{1,0:T(8,128)(2,1)S(1)} %get-tuple-element.20.q_ref, f32[512,128]{1,0:T(8,128)S(1)} %get-tuple-element.27.m_ref, f32[512,128]{1,0:T(8,128)S(1)} %get-tuple-element.28.l_ref, ...), custom_call_target="tpu_custom_call" | custom-call | tf_op jit(solution)/shard_map/give/pallas_call | solution.py:350
  40.8 0.0 copy-start
  40.8 0.1 collective-permute-start.9
  40.9 1.2 %keep.1.keep_ref = f32[256,640]{1,0:T(8,128)S(1)} custom-call(s32[1]{0:T(128)S(6)} %copy.8.length_ref, s32[128]{0:T(128)S(1)} %copy-done.2, bf16[512,576]{1,0:T(8,128)(2,1)S(1)} %get-tuple-element.20.q_ref, f32[512,128]{1,0:T(8,128)S(1)} %get-tuple-element.27.m_ref, f32[512,128]{1,0:T(8,128)S(1)} %get-tuple-element.28.l_ref, ...), custom_call_target="tpu_custom_call" | custom-call | tf_op jit(solution)/shard_map/keep/pallas_call | solution.py:350
  42.1 0.4 collective-permute-done.9.got_ref
  42.5 0.0 copy-done
  42.5 0.5 merge.1
  43.0 9.3 %all_to_all.10 = bf16[16,2,1024]{2,1,0:T(2,128)(2,1)S(1)} all-to-all(bf16[16,2,1024]{2,1,0:T(2,128)(2,1)S(1)} %merge.1), channel_id=1, replica_groups={{15,14,13,12,11,10,9,8,7,6,5,4,3,2,1,0},{31,30,29,28,27,26,25,24,23,22,..., dimensions={0} | all-to-all | bytes 131072 | tf_op jit(solution)/shard_map/all_to_all | solution.py:370
  52.3 0.7 %rev.3 = bf16[16,2,1024]{2,1,0:T(2,128)(2,1)} reverse(bf16[16,2,1024]{2,1,0:T(2,128)(2,1)S(1)} %all_to_all.10), dimensions={0} | reverse | bytes 131072 | tf_op jit(solution)/shard_map/rev | solution.py:374
  (2 shorter events, 0.0 us)
Async XLA Ops:
  0.0 11.0 %collective-permute-start.1 = (bf16[576,254]{1,0:T(8,128)(2,1)}, bf16[576,254]{1,0:T(8,128)(2,1)S(1)}, u32[]{:S(2)}, u32[]{:S(2)}) collective-permute-start(bf16[576,254]{1,0:T(8,128)(2,1)} %bitcast.7), channel_id=1, source_target_pairs={{2,0},{3,7},{6,2},{7,11},{10,6},{11,15},{14,10},{15,13},{12,14},{1... | collective-permute-start | bytes 877832 | tf_op jit(solution)/shard_map/ppermute | solution.py:301
  3.0 8.0 %collective-permute-start.2 = (bf16[576,254]{1,0:T(8,128)(2,1)}, bf16[576,254]{1,0:T(8,128)(2,1)S(1)}, u32[]{:S(2)}, u32[]{:S(2)}) collective-permute-start(bf16[576,254]{1,0:T(8,128)(2,1)} %bitcast.8), channel_id=1, source_target_pairs={{2,6},{3,1},{6,10},{7,3},{10,14},{11,7},{14,12},{15,11},{12,8},{13... | collective-permute-start | bytes 877832 | tf_op jit(solution)/shard_map/ppermute | solution.py:301
  4.7 17.3 %all-to-all-start = ((bf16[8,2,9792]{2,1,0:T(2,128)(2,1)}), bf16[8,2,9792]{2,1,0:T(2,128)(2,1)S(1)}, u32[]{:S(2)}, u32[]{:S(2)}) async-start(bf16[8,2,9792]{2,1,0:T(2,128)(2,1)} %pieces.1), calls=%async_computation | async-start | bytes 630784 | tf_op jit(solution)/shard_map/all_to_all | solution.py:316
  11.0 17.1 %copy-start.1 = (bf16[254,576]{0,1:T(8,128)(2,1)S(1)}, bf16[254,576]{0,1:T(8,128)(2,1)}, u32[]{:S(2)}) copy-start(bf16[254,576]{0,1:T(8,128)(2,1)} %param.8) | copy-start | bytes 877828
  11.0 13.6 %collective-permute-start.4 = (bf16[576,254]{1,0:T(8,128)(2,1)S(1)}, bf16[576,254]{1,0:T(8,128)(2,1)S(1)}, u32[]{:S(2)}, u32[]{:S(2)}) collective-permute-start(bf16[576,254]{1,0:T(8,128)(2,1)S(1)} %collective-permute-done.2.rest_2_), channel_id=1, source_target_pairs={{2,6},{3,1},{6,10},{7,3},{10,14},{11,7},{14,12},{15,11},{12,8},{13... | collective-permute-start | bytes 877832 | tf_op jit(solution)/shard_map/ppermute | solution.py:323
  13.1 11.6 %collective-permute-start.3 = (bf16[576,254]{1,0:T(8,128)(2,1)S(1)}, bf16[576,254]{1,0:T(8,128)(2,1)S(1)}, u32[]{:S(2)}, u32[]{:S(2)}) collective-permute-start(bf16[576,254]{1,0:T(8,128)(2,1)S(1)} %collective-permute-done.1.rest_1_), channel_id=1, source_target_pairs={{2,0},{3,7},{6,2},{7,11},{10,6},{11,15},{14,10},{15,13},{12,14},{1... | collective-permute-start | bytes 877832 | tf_op jit(solution)/shard_map/ppermute | solution.py:323
  22.3 5.8 %copy-start.2 = (s32[128]{0:T(128)S(1)}, s32[128]{0:T(128)}, u32[]{:S(2)}) copy-start(s32[128]{0:T(128)} %constant.2.clone.table_ref) | copy-start | bytes 1540
  22.3 5.7 %collective-permute-start = (bf16[16,9792]{1,0:T(8,128)(2,1)S(1)}, bf16[16,9792]{1,0:T(8,128)(2,1)S(1)}, u32[]{:S(2)}, u32[]{:S(2)}) collective-permute-start(bf16[16,9792]{1,0:T(8,128)(2,1)S(1)} %reshape.10.here_ref), channel_id=1, source_target_pairs={{0,1},{1,0},{2,3},{3,2},{4,5},{5,4},{6,7},{7,6},{8,9},{9,8},{10,11... | collective-permute-start | bytes 940040 | tf_op jit(solution)/shard_map/ppermute | solution.py:326
  24.7 9.1 %collective-permute-start.5 = (bf16[576,254]{1,0:T(8,128)(2,1)S(1)}, bf16[576,254]{1,0:T(8,128)(2,1)S(1)}, u32[]{:S(2)}, u32[]{:S(2)}) collective-permute-start(bf16[576,254]{1,0:T(8,128)(2,1)S(1)} %collective-permute-done.4.rest_4_), channel_id=1, source_target_pairs={{2,6},{3,1},{6,10},{7,3},{10,14},{11,7},{14,12},{15,11},{12,8},{13... | collective-permute-start | bytes 877832 | tf_op jit(solution)/shard_map/ppermute | solution.py:323
  24.7 9.4 %collective-permute-start.6 = (bf16[576,254]{1,0:T(8,128)(2,1)S(1)}, bf16[576,254]{1,0:T(8,128)(2,1)S(1)}, u32[]{:S(2)}, u32[]{:S(2)}) collective-permute-start(bf16[576,254]{1,0:T(8,128)(2,1)S(1)} %collective-permute-done.3.rest_3_), channel_id=1, source_target_pairs={{2,0},{3,7},{6,2},{7,11},{10,6},{11,15},{14,10},{15,13},{12,14},{1... | collective-permute-start | bytes 877832 | tf_op jit(solution)/shard_map/ppermute | solution.py:323
  33.7 5.8 %collective-permute-start.8 = (bf16[320,254]{1,0:T(8,128)(2,1)S(1)}, bf16[320,254]{1,0:T(8,128)(2,1)S(1)}, u32[]{:S(2)}, u32[]{:S(2)}) collective-permute-start(bf16[320,254]{1,0:T(8,128)(2,1)S(1)} %slice.7), channel_id=1, source_target_pairs={{2,6},{3,1},{6,10},{7,3},{10,14},{11,7},{14,12},{15,11},{12,8},{13... | collective-permute-start | bytes 487688 | tf_op jit(solution)/shard_map/ppermute | solution.py:337
  34.1 5.5 %collective-permute-start.7 = (bf16[256,254]{1,0:T(8,128)(2,1)S(1)}, bf16[256,254]{1,0:T(8,128)(2,1)S(1)}, u32[]{:S(2)}, u32[]{:S(2)}) collective-permute-start(bf16[256,254]{1,0:T(8,128)(2,1)S(1)} %slice.8), channel_id=1, source_target_pairs={{2,0},{3,7},{6,2},{7,11},{10,6},{11,15},{14,10},{15,13},{12,14},{1... | collective-permute-start | bytes 390152 | tf_op jit(solution)/shard_map/ppermute | solution.py:335
  40.8 1.7 %copy-start = (bf16[8,512,128]{2,1,0:T(8,128)(2,1)S(1)}, bf16[8,512,128]{2,1,0:T(8,128)(2,1)}, u32[]{:S(2)}) copy-start(bf16[8,512,128]{2,1,0:T(8,128)(2,1)} %up_ref.1) | copy-start | bytes 3145732
  40.8 1.7 %collective-permute-start.9 = (bf16[256,640]{1,0:T(8,128)(2,1)S(1)}, bf16[256,640]{1,0:T(8,128)(2,1)S(1)}, u32[]{:S(2)}, u32[]{:S(2)}) collective-permute-start(bf16[256,640]{1,0:T(8,128)(2,1)S(1)} %give.1), channel_id=1, source_target_pairs={{0,1},{1,0},{2,3},{3,2},{4,5},{5,4},{6,7},{7,6},{8,9},{9,8},{10,11... | collective-permute-start | bytes 983048 | tf_op jit(solution)/shard_map/ppermute | solution.py:359

commit v28 on v26

--- a/solution.py
+++ b/solution.py
@@ -224,16 +224,15 @@
     devices, tokens, _ = out_ref.shape
     chips = devices // CORES
     for i in range(devices):
-        out_ref[(1 - (core ^ (i // chips))) * chips + chips - 1 - i % chips] = (
+        out_ref[(i % chips) * CORES + 1 - (core ^ (i // chips))] = (
             flat_ref[i * tokens:(i + 1) * tokens, :].astype(bf16)
         )
 
 
 def place_kernel(parts_ref, out_ref):
     devices, _, width = parts_ref.shape
-    chips = devices // CORES
     for i in range(devices):
-        core, chip = 1 - i // chips, chips - 1 - i % chips
+        core, chip = 1 - i % CORES, i // CORES
         at = (chip * CORES + core) * width
         out_ref[:, at:at + width] = parts_ref[i]
 
@@ -379,7 +378,7 @@
     returned = lax.all_to_all(
         merged, "ctx", split_axis=0, concat_axis=0, tiled=True,
         axis_index_groups=[
-            [p * CORES + c for c in reversed(range(CORES)) for p in reversed(range(chips))]
+            [p * CORES + c for p in range(chips) for c in reversed(range(CORES))]
         ],
     )
     return pl.pallas_call(

time: 52.9 us -> 55.5 us (1.049)
  blocking collectives: 8.62 us -> 11.2 us
    all_to_all x1, blocking collectives: 8.62 us -> 11.2 us  [on_device(): lax.all_to_all(merged, 'ctx', split_axis=0, concat_axis=0, tiled=True, ax...]
  transfers between devices with their start and end apart: 11 -> 11, of which waited for: 5 -> 5; matrix products, arithmetic and copies ran while one was open for 0% -> 0% of each run, Pallas kernels for 17% -> 16%
where the time goes in v28:
time: 55.5 us; the launch traced here: 55.2 us
  starting transfers between devices  16.5 us (30%)
  waiting for transfers between devices  14.5 us (26%)
  Pallas kernels  11.3 us (20%)
  blocking collectives  11.2 us (20%)
  between operations  1.44 us (3%)
    all_to_all x1, blocking collectives, on_device(): lax.all_to_all(merged, 'ctx', split_axis=0, concat_axis=0, tiled=True, ax...  11.2 us
    all_to_all x1, waiting for transfers between devices, on_device(): lax.all_to_all(pieces, 'ctx', split_axis=0, concat_axis=0, axis_index_gro...  8.91 us
    all_to_all x1, starting transfers between devices, on_device(): lax.all_to_all(pieces, 'ctx', split_axis=0, concat_axis=0, axis_index_gro...  6.26 us
    ppermute x4, starting transfers between devices, on_device(): right, left = (onward(right), backward(left))  4.45 us
    ppermute x4, waiting for transfers between devices, on_device(): right, left = (onward(right), backward(left))  4.06 us
    pallas_call x1, Pallas kernels, fold_first(): pl.pallas_call(functools.partial(first_kernel, heads, len(keys)), out_sha...  3.65 us
    ppermute x2, starting transfers between devices, on_device(): right, left = (onward(own), backward(own))  3.03 us
    pallas_call x1, Pallas kernels, on_device(): pl.pallas_call(functools.partial(span_kernel, at, len(keys)), out_shape=s...  2.47 us
  transfers between devices with their start and end apart: 11, of which 5 were waited for; matrix products, arithmetic and copies ran while one was open for 0% of the time, Pallas kernels for 16%

profile of v28, /device:TPU:0, one launch (start us, length us, event | category | flops | bytes accessed | tf_op | source)
XLA Modules:
  0.0 55.2 jit_solution(14455764508472626995)
XLA Ops:
  0.0 2.9 %collective-permute-start.1 = (bf16[576,254]{1,0:T(8,128)(2,1)}, bf16[576,254]{1,0:T(8,128)(2,1)S(1)}, u32[]{:S(2)}, u32[]{:S(2)}) collective-permute-start(bf16[576,254]{1,0:T(8,128)(2,1)} %bitcast.4), channel_id=1, source_target_pairs={{2,6},{3,1},{6,10},{7,3},{10,14},{11,7},{14,12},{15,11},{12,8},{13... | collective-permute-start | bytes 877832 | tf_op jit(solution)/shard_map/ppermute | solution.py:309
  2.9 0.1 collective-permute-start.2
  3.0 1.7 %pieces.1 = bf16[8,2,9792]{2,1,0:T(2,128)(2,1)} custom-call(bf16[8,2,9216]{2,1,0:T(2,128)(2,1)} %bitcast.7, bf16[2,576]{1,0:T(2,128)(2,1)} %span_hbm.1), custom_call_target="tpu_custom_call" | custom-call | tf_op jit(solution)/shard_map/pieces/pallas_call | solution.py:312
  4.7 6.3 %all-to-all-start = ((bf16[8,2,9792]{2,1,0:T(2,128)(2,1)}), bf16[8,2,9792]{2,1,0:T(2,128)(2,1)S(1)}, u32[]{:S(2)}, u32[]{:S(2)}) async-start(bf16[8,2,9792]{2,1,0:T(2,128)(2,1)} %pieces.1), calls=%async_computation | async-start | bytes 630784 | tf_op jit(solution)/shard_map/all_to_all | solution.py:324
  11.0 0.0 copy-start.1
  11.0 0.0 collective-permute-done.1.rest_1_
  11.0 0.0 collective-permute-done.2.rest_2_
  11.0 2.1 %collective-permute-start.4 = (bf16[576,254]{1,0:T(8,128)(2,1)S(1)}, bf16[576,254]{1,0:T(8,128)(2,1)S(1)}, u32[]{:S(2)}, u32[]{:S(2)}) collective-permute-start(bf16[576,254]{1,0:T(8,128)(2,1)S(1)} %collective-permute-done.2.rest_2_), channel_id=1, source_target_pairs={{2,0},{3,7},{6,2},{7,11},{10,6},{11,15},{14,10},{15,13},{12,14},{1... | collective-permute-start | bytes 877832 | tf_op jit(solution)/shard_map/ppermute | solution.py:331
  13.1 0.1 collective-permute-start.3
  13.2 8.9 %all-to-all-done = bf16[8,2,9792]{2,1,0:T(2,128)(2,1)S(1)} async-done(((bf16[8,2,9792]{2,1,0:T(2,128)(2,1)}), bf16[8,2,9792]{2,1,0:T(2,128)(2,1)S(1)}, u32[]{:S(2)}, u32[]{:S(2)}) %all-to-all-start) | async-done | bytes 313376 | tf_op jit(solution)/shard_map/all_to_all | solution.py:324
  22.1 0.2 reshape.7.here_ref
  22.3 0.0 copy-start.2
  22.3 0.1 collective-permute-start
  22.4 1.0 %collective-permute-done.4.rest_4_ = bf16[576,254]{1,0:T(8,128)(2,1)S(1)} collective-permute-done((bf16[576,254]{1,0:T(8,128)(2,1)S(1)}, bf16[576,254]{1,0:T(8,128)(2,1)S(1)}, u32[]{:S(2)}, u32[]{:S(2)}) %collective-permute-start.4) | collective-permute-done | bytes 292640 | tf_op jit(solution)/shard_map/ppermute | solution.py:331
  23.4 1.7 %collective-permute-start.5 = (bf16[576,254]{1,0:T(8,128)(2,1)S(1)}, bf16[576,254]{1,0:T(8,128)(2,1)S(1)}, u32[]{:S(2)}, u32[]{:S(2)}) collective-permute-start(bf16[576,254]{1,0:T(8,128)(2,1)S(1)} %collective-permute-done.4.rest_4_), channel_id=1, source_target_pairs={{2,0},{3,7},{6,2},{7,11},{10,6},{11,15},{14,10},{15,13},{12,14},{1... | collective-permute-start | bytes 877832 | tf_op jit(solution)/shard_map/ppermute | solution.py:331
  25.1 0.0 collective-permute-done.3.rest_3_
  25.1 0.6 %collective-permute-start.6 = (bf16[576,254]{1,0:T(8,128)(2,1)S(1)}, bf16[576,254]{1,0:T(8,128)(2,1)S(1)}, u32[]{:S(2)}, u32[]{:S(2)}) collective-permute-start(bf16[576,254]{1,0:T(8,128)(2,1)S(1)} %collective-permute-done.3.rest_3_), channel_id=1, source_target_pairs={{2,6},{3,1},{6,10},{7,3},{10,14},{11,7},{14,12},{15,11},{12,8},{13... | collective-permute-start | bytes 877832 | tf_op jit(solution)/shard_map/ppermute | solution.py:331
  26.4 0.0 collective-permute-done.there_ref
  26.4 0.0 copy-done.1
  26.4 0.0 copy-done.2
  26.4 3.7 %first.1 = (bf16[512,576]{1,0:T(8,128)(2,1)S(1)}, f32[512,128]{1,0:T(8,128)S(1)}, f32[512,128]{1,0:T(8,128)S(1)}, f32[512,512]{1,0:T(8,128)S(1)}) custom-call(s32[1]{0:T(128)S(6)} %copy.8.length_ref, s32[128]{0:T(128)S(1)} %copy-done.2, bf16[16,9792]{1,0:T(8,128)(2,1)S(1)} %reshape.7.here_ref, bf16[16,9792]{1,0:T(8,128)(2,1)S(1)} %collective-permute-done.there_ref, ...), custom_call_target="tpu_custom_call" | custom-call | tf_op jit(solution)/shard_map/first/pallas_call | solution.py:286
  30.0 3.1 %collective-permute-done.5.rest_1_ = bf16[576,254]{1,0:T(8,128)(2,1)S(1)} collective-permute-done((bf16[576,254]{1,0:T(8,128)(2,1)S(1)}, bf16[576,254]{1,0:T(8,128)(2,1)S(1)}, u32[]{:S(2)}, u32[]{:S(2)}) %collective-permute-start.5) | collective-permute-done | bytes 292640 | tf_op jit(solution)/shard_map/ppermute | solution.py:331
  33.1 1.8 %collective-permute-start.8 = (bf16[320,254]{1,0:T(8,128)(2,1)S(1)}, bf16[320,254]{1,0:T(8,128)(2,1)S(1)}, u32[]{:S(2)}, u32[]{:S(2)}) collective-permute-start(bf16[320,254]{1,0:T(8,128)(2,1)S(1)} %slice.7), channel_id=1, source_target_pairs={{2,0},{3,7},{6,2},{7,11},{10,6},{11,15},{14,10},{15,13},{12,14},{1... | collective-permute-start | bytes 487688 | tf_op jit(solution)/shard_map/ppermute | solution.py:345
  34.9 0.0 collective-permute-done.6.rest_0_
  34.9 0.8 %collective-permute-start.7 = (bf16[256,254]{1,0:T(8,128)(2,1)S(1)}, bf16[256,254]{1,0:T(8,128)(2,1)S(1)}, u32[]{:S(2)}, u32[]{:S(2)}) collective-permute-start(bf16[256,254]{1,0:T(8,128)(2,1)S(1)} %slice.8), channel_id=1, source_target_pairs={{2,6},{3,1},{6,10},{7,3},{10,14},{11,7},{14,12},{15,11},{12,8},{13... | collective-permute-start | bytes 390152 | tf_op jit(solution)/shard_map/ppermute | solution.py:343
  36.4 2.5 %middle.1 = (f32[512,128]{1,0:T(8,128)S(1)}, f32[512,128]{1,0:T(8,128)S(1)}, f32[512,512]{1,0:T(8,128)S(1)}) custom-call(s32[1]{0:T(128)S(6)} %copy.8.length_ref, s32[1]{0:T(128)S(6)} %copy.9.offset_ref, s32[128]{0:T(128)S(1)} %copy-done.2, bf16[512,576]{1,0:T(8,128)(2,1)S(1)} %get-tuple-element.20.q_ref, f32[512,128]{1,0:T(8,128)S(1)} %get-tuple-element.24.m_in, ...), custom_call_target="tpu_custom_call" | custom-call | tf_op jit(solution)/shard_map/middle/pallas_call | solution.py:346
  38.9 1.1 %collective-permute-done.7.top_ref = bf16[256,254]{1,0:T(8,128)(2,1)S(1)} collective-permute-done((bf16[256,254]{1,0:T(8,128)(2,1)S(1)}, bf16[256,254]{1,0:T(8,128)(2,1)S(1)}, u32[]{:S(2)}, u32[]{:S(2)}) %collective-permute-start.7) | collective-permute-done | bytes 130080 | tf_op jit(solution)/shard_map/ppermute | solution.py:343
  39.9 0.0 collective-permute-done.8.bottom_ref
  39.9 1.2 %give.1 = bf16[256,640]{1,0:T(8,128)(2,1)S(1)} custom-call(s32[1]{0:T(128)S(6)} %copy.8.length_ref, s32[128]{0:T(128)S(1)} %copy-done.2, bf16[512,576]{1,0:T(8,128)(2,1)S(1)} %get-tuple-element.20.q_ref, f32[512,128]{1,0:T(8,128)S(1)} %get-tuple-element.27.m_ref, f32[512,128]{1,0:T(8,128)S(1)} %get-tuple-element.28.l_ref, ...), custom_call_target="tpu_custom_call" | custom-call | tf_op jit(solution)/shard_map/give/pallas_call | solution.py:358
  41.2 0.0 copy-start
  41.2 0.1 collective-permute-start.9
  41.2 1.2 %keep.1.keep_ref = f32[256,640]{1,0:T(8,128)S(1)} custom-call(s32[1]{0:T(128)S(6)} %copy.8.length_ref, s32[128]{0:T(128)S(1)} %copy-done.2, bf16[512,576]{1,0:T(8,128)(2,1)S(1)} %get-tuple-element.20.q_ref, f32[512,128]{1,0:T(8,128)S(1)} %get-tuple-element.27.m_ref, f32[512,128]{1,0:T(8,128)S(1)} %get-tuple-element.28.l_ref, ...), custom_call_target="tpu_custom_call" | custom-call | tf_op jit(solution)/shard_map/keep/pallas_call | solution.py:358
  42.4 0.4 collective-permute-done.9.got_ref
  42.9 0.0 copy-done
  42.9 0.5 merge.1
  43.4 11.2 %all_to_all.10.parts_ref = bf16[16,2,1024]{2,1,0:T(2,128)(2,1)S(1)} all-to-all(bf16[16,2,1024]{2,1,0:T(2,128)(2,1)S(1)} %merge.1), channel_id=1, replica_groups={{1,0,3,2,5,4,7,6,9,8,11,10,13,12,15,14},{17,16,19,18,21,20,23,22,25,24,..., dimensions={0} | all-to-all | bytes 131072 | tf_op jit(solution)/shard_map/all_to_all | solution.py:378
  54.6 0.6 %place.1 = bf16[2,16384]{1,0:T(2,128)(2,1)} custom-call(bf16[16,2,1024]{2,1,0:T(2,128)(2,1)S(1)} %all_to_all.10.parts_ref), custom_call_target="tpu_custom_call" | custom-call | tf_op jit(solution)/shard_map/place/pallas_call | solution.py:384
  (2 shorter events, 0.0 us)
Async XLA Ops:
  0.0 11.0 %collective-permute-start.1 = (bf16[576,254]{1,0:T(8,128)(2,1)}, bf16[576,254]{1,0:T(8,128)(2,1)S(1)}, u32[]{:S(2)}, u32[]{:S(2)}) collective-permute-start(bf16[576,254]{1,0:T(8,128)(2,1)} %bitcast.4), channel_id=1, source_target_pairs={{2,6},{3,1},{6,10},{7,3},{10,14},{11,7},{14,12},{15,11},{12,8},{13... | collective-permute-start | bytes 877832 | tf_op jit(solution)/shard_map/ppermute | solution.py:309
  2.9 8.1 %collective-permute-start.2 = (bf16[576,254]{1,0:T(8,128)(2,1)}, bf16[576,254]{1,0:T(8,128)(2,1)S(1)}, u32[]{:S(2)}, u32[]{:S(2)}) collective-permute-start(bf16[576,254]{1,0:T(8,128)(2,1)} %bitcast.5), channel_id=1, source_target_pairs={{2,0},{3,7},{6,2},{7,11},{10,6},{11,15},{14,10},{15,13},{12,14},{1... | collective-permute-start | bytes 877832 | tf_op jit(solution)/shard_map/ppermute | solution.py:309
  4.7 17.3 %all-to-all-start = ((bf16[8,2,9792]{2,1,0:T(2,128)(2,1)}), bf16[8,2,9792]{2,1,0:T(2,128)(2,1)S(1)}, u32[]{:S(2)}, u32[]{:S(2)}) async-start(bf16[8,2,9792]{2,1,0:T(2,128)(2,1)} %pieces.1), calls=%async_computation | async-start | bytes 630784 | tf_op jit(solution)/shard_map/all_to_all | solution.py:324
  11.0 15.4 %copy-start.1 = (bf16[254,576]{0,1:T(8,128)(2,1)S(1)}, bf16[254,576]{0,1:T(8,128)(2,1)}, u32[]{:S(2)}) copy-start(bf16[254,576]{0,1:T(8,128)(2,1)} %param.8) | copy-start | bytes 877828
  11.0 12.4 %collective-permute-start.4 = (bf16[576,254]{1,0:T(8,128)(2,1)S(1)}, bf16[576,254]{1,0:T(8,128)(2,1)S(1)}, u32[]{:S(2)}, u32[]{:S(2)}) collective-permute-start(bf16[576,254]{1,0:T(8,128)(2,1)S(1)} %collective-permute-done.2.rest_2_), channel_id=1, source_target_pairs={{2,0},{3,7},{6,2},{7,11},{10,6},{11,15},{14,10},{15,13},{12,14},{1... | collective-permute-start | bytes 877832 | tf_op jit(solution)/shard_map/ppermute | solution.py:331
  13.1 12.0 %collective-permute-start.3 = (bf16[576,254]{1,0:T(8,128)(2,1)S(1)}, bf16[576,254]{1,0:T(8,128)(2,1)S(1)}, u32[]{:S(2)}, u32[]{:S(2)}) collective-permute-start(bf16[576,254]{1,0:T(8,128)(2,1)S(1)} %collective-permute-done.1.rest_1_), channel_id=1, source_target_pairs={{2,6},{3,1},{6,10},{7,3},{10,14},{11,7},{14,12},{15,11},{12,8},{13... | collective-permute-start | bytes 877832 | tf_op jit(solution)/shard_map/ppermute | solution.py:331
  22.3 4.1 %copy-start.2 = (s32[128]{0:T(128)S(1)}, s32[128]{0:T(128)}, u32[]{:S(2)}) copy-start(s32[128]{0:T(128)} %constant.2.clone.table_ref) | copy-start | bytes 1540
  22.3 4.1 %collective-permute-start = (bf16[16,9792]{1,0:T(8,128)(2,1)S(1)}, bf16[16,9792]{1,0:T(8,128)(2,1)S(1)}, u32[]{:S(2)}, u32[]{:S(2)}) collective-permute-start(bf16[16,9792]{1,0:T(8,128)(2,1)S(1)} %reshape.7.here_ref), channel_id=1, source_target_pairs={{0,1},{1,0},{2,3},{3,2},{4,5},{5,4},{6,7},{7,6},{8,9},{9,8},{10,11... | collective-permute-start | bytes 940040 | tf_op jit(solution)/shard_map/ppermute | solution.py:334
  23.4 9.7 %collective-permute-start.5 = (bf16[576,254]{1,0:T(8,128)(2,1)S(1)}, bf16[576,254]{1,0:T(8,128)(2,1)S(1)}, u32[]{:S(2)}, u32[]{:S(2)}) collective-permute-start(bf16[576,254]{1,0:T(8,128)(2,1)S(1)} %collective-permute-done.4.rest_4_), channel_id=1, source_target_pairs={{2,0},{3,7},{6,2},{7,11},{10,6},{11,15},{14,10},{15,13},{12,14},{1... | collective-permute-start | bytes 877832 | tf_op jit(solution)/shard_map/ppermute | solution.py:331
  25.1 9.8 %collective-permute-start.6 = (bf16[576,254]{1,0:T(8,128)(2,1)S(1)}, bf16[576,254]{1,0:T(8,128)(2,1)S(1)}, u32[]{:S(2)}, u32[]{:S(2)}) collective-permute-start(bf16[576,254]{1,0:T(8,128)(2,1)S(1)} %collective-permute-done.3.rest_3_), channel_id=1, source_target_pairs={{2,6},{3,1},{6,10},{7,3},{10,14},{11,7},{14,12},{15,11},{12,8},{13... | collective-permute-start | bytes 877832 | tf_op jit(solution)/shard_map/ppermute | solution.py:331
  33.1 6.8 %collective-permute-start.8 = (bf16[320,254]{1,0:T(8,128)(2,1)S(1)}, bf16[320,254]{1,0:T(8,128)(2,1)S(1)}, u32[]{:S(2)}, u32[]{:S(2)}) collective-permute-start(bf16[320,254]{1,0:T(8,128)(2,1)S(1)} %slice.7), channel_id=1, source_target_pairs={{2,0},{3,7},{6,2},{7,11},{10,6},{11,15},{14,10},{15,13},{12,14},{1... | collective-permute-start | bytes 487688 | tf_op jit(solution)/shard_map/ppermute | solution.py:345
  34.9 5.0 %collective-permute-start.7 = (bf16[256,254]{1,0:T(8,128)(2,1)S(1)}, bf16[256,254]{1,0:T(8,128)(2,1)S(1)}, u32[]{:S(2)}, u32[]{:S(2)}) collective-permute-start(bf16[256,254]{1,0:T(8,128)(2,1)S(1)} %slice.8), channel_id=1, source_target_pairs={{2,6},{3,1},{6,10},{7,3},{10,14},{11,7},{14,12},{15,11},{12,8},{13... | collective-permute-start | bytes 390152 | tf_op jit(solution)/shard_map/ppermute | solution.py:343
  41.2 1.7 %copy-start = (bf16[8,512,128]{2,1,0:T(8,128)(2,1)S(1)}, bf16[8,512,128]{2,1,0:T(8,128)(2,1)}, u32[]{:S(2)}) copy-start(bf16[8,512,128]{2,1,0:T(8,128)(2,1)} %up_ref.1) | copy-start | bytes 3145732
  41.2 1.7 %collective-permute-start.9 = (bf16[256,640]{1,0:T(8,128)(2,1)S(1)}, bf16[256,640]{1,0:T(8,128)(2,1)S(1)}, u32[]{:S(2)}, u32[]{:S(2)}) collective-permute-start(bf16[256,640]{1,0:T(8,128)(2,1)S(1)} %give.1), channel_id=1, source_target_pairs={{0,1},{1,0},{2,3},{3,2},{4,5},{5,4},{6,7},{7,6},{8,9},{9,8},{10,11... | collective-permute-start | bytes 983048 | tf_op jit(solution)/shard_map/ppermute | solution.py:367
